TPU v7x, 32 devices: a whole 2x2x4 slice. The times are simulated.
32 devices in a mesh: group: 2 (over y), expert: 8 (over z, x), dp: 2 (over core).
Axes of the slice: x: 2, y: 2, z: 4, core: 2. Of those that a mesh axis runs over, the one named last changes fastest.
Arguments:
- tokens: bfloat16 [2048, 2048], P(('group', 'expert', 'dp')), parts along dimension 0, may hold values from -6 to 6
- out_grad: bfloat16 [2048, 2048], P(('group', 'expert', 'dp')), parts along dimension 0, may hold values from -6 to 6
- expert_ids: int32 [2048, 8], P(('group', 'expert', 'dp')), parts along dimension 0, may hold values from 0 to 15, all different within a row; in each aligned block of 64 rows (0 to 63, 64 to 127, ...) at most 40 rows name the same one
- route_weight: bfloat16 [2048, 8], P(('group', 'expert', 'dp')), parts along dimension 0, may hold values from 0.019897461 to 0.3984375
- gate_weight: bfloat16 [16, 2048, 384], P('expert', 'dp'), may hold values from -0.125 to 0.125
- up_weight: bfloat16 [16, 2048, 384], P('expert', 'dp'), may hold values from -0.125 to 0.125
- down_weight: bfloat16 [16, 2048, 384], P('expert', 'dp'), may hold values from -0.3125 to 0.3125
- adapter_in: bfloat16 [16, 16, 384], P('expert'), may hold values from -0.3125 to 0.3125
- adapter_out: bfloat16 [16, 16, 2048], P('expert'), may hold values from -0.125 to 0.125
Outputs:
- grad_tokens: bfloat16 [2048, 2048], P(('group', 'expert', 'dp')), parts along dimension 0
- grad_adapter_in: float32 [32, 16, 384], P(('group', 'expert'), None, 'dp'), parts along dimension 0
- grad_adapter_out: float32 [32, 16, 2048], P(('group', 'expert'), None, 'dp'), parts along dimension 0
There are 2 independent parts, one for each index of `group`. A program takes and returns all parts, laid end to end along the dimension named above; an argument that names none is the same for every part. Nothing has to cross between parts.
Inputs may be any that keep to these rules, and one draw needn't show every extreme that they name: `expert_ids`: each token names 8 different experts. Within each aligned block of 64 tokens (the tokens of one device) no expert is named more than 40 times, and some block reaches 40.
All inputs are finite; a program needn't handle non-finite values.
Results may differ from a plain program's by a relative error of at most 0.006.
Values may be sent and summed in bfloat16 or wider, within the bound.
No kernel may reach another device: no remote copies, remote signals or barrier semaphores. Data moves between devices by JAX's collectives and lax.ppermute only.
A program may use at most 128 MiB of HBM per device.

v0:
```python
import jax
import jax.numpy as jnp
from jax import lax
from jax.sharding import PartitionSpec as P

adapter_scale = 2.0


def silu_parts(gate_pre):
    logistic = jax.nn.sigmoid(gate_pre)
    return (gate_pre * logistic, logistic * (1.0 + gate_pre * (1.0 - logistic)))


def recompute(tokens_in, w_gate, w_up):
    gate_pre = jnp.dot(tokens_in, w_gate, preferred_element_type=jnp.float32)
    up_pre = jnp.dot(tokens_in, w_up, preferred_element_type=jnp.float32)
    return (gate_pre, up_pre)


def backward_rows(
    gate_pre, up_pre, grad_in, weight_in, w_gate, w_up, w_down, factor_in, factor_out
):
    activation, derivative = silu_parts(gate_pre)
    hidden = (activation * up_pre).astype(jnp.bfloat16)
    route_scale = weight_in.astype(jnp.float32)[:, None]
    low_rank = jnp.dot(hidden, factor_in.T, preferred_element_type=jnp.float32)
    low_scaled = (route_scale * low_rank).astype(jnp.bfloat16)
    adapter_back = jnp.dot(grad_in, factor_out.T, preferred_element_type=jnp.float32).astype(
        jnp.bfloat16
    )
    back_scaled = (route_scale * adapter_back.astype(jnp.float32)).astype(jnp.bfloat16)
    grad_hidden = route_scale * (
        jnp.dot(grad_in, w_down, preferred_element_type=jnp.float32)
        + adapter_scale * jnp.dot(adapter_back, factor_in, preferred_element_type=jnp.float32)
    )
    grad_gate = (grad_hidden * up_pre * derivative).astype(jnp.bfloat16)
    grad_up = (grad_hidden * activation).astype(jnp.bfloat16)
    rows_out = (
        jnp.dot(grad_gate, w_gate.T, preferred_element_type=jnp.float32)
        + jnp.dot(grad_up, w_up.T, preferred_element_type=jnp.float32)
    ).astype(jnp.bfloat16)
    grad_factor_in = adapter_scale * jnp.dot(
        back_scaled.T, hidden, preferred_element_type=jnp.float32
    )
    grad_factor_out = adapter_scale * jnp.dot(
        low_scaled.T, grad_in, preferred_element_type=jnp.float32
    )
    return (rows_out, grad_factor_in, grad_factor_out)


def expert_rows(bundle, weights):
    w_gate, w_up, w_down, factor_in, factor_out = weights
    tokens_in, grad_in, weight_in = bundle
    gate_pre, up_pre = recompute(tokens_in, w_gate, w_up)
    return backward_rows(
        gate_pre, up_pre, grad_in, weight_in, w_gate, w_up, w_down, factor_in, factor_out
    )


def per_device(
    tokens,
    out_grad,
    expert_ids,
    route_weight,
    gate_weight,
    up_weight,
    down_weight,
    adapter_in,
    adapter_out,
):
    peer_count = lax.axis_size("expert")
    token_count, model_width = tokens.shape
    route_count = expert_ids.shape[1]
    local_count = gate_weight.shape[0]
    expert_total = local_count * peer_count
    capacity = max(3, min(token_count, 5 * token_count * route_count // (4 * expert_total)))
    slot_total = expert_total * capacity
    flat_ids = expert_ids.reshape(-1)
    one_hot = (flat_ids[:, None] == jnp.arange(expert_total, dtype=jnp.int32)[None, :]).astype(
        jnp.int32
    )
    before = jnp.cumsum(one_hot, axis=0) - one_hot
    position = jnp.sum(before * one_hot, axis=1)
    slot_index = flat_ids * capacity + position
    route_owner = jnp.arange(token_count * route_count, dtype=jnp.int32) // route_count
    slot_owner = jnp.full((slot_total,), -1, jnp.int32).at[slot_index].set(route_owner)
    filled = (slot_owner >= 0)[:, None]
    source = jnp.maximum(slot_owner, 0)
    zero_value = jnp.zeros((), jnp.bfloat16)
    send_tokens = jnp.where(filled, tokens[source], zero_value).reshape(
        peer_count, local_count, capacity, model_width
    )
    send_grads = jnp.where(filled, out_grad[source], zero_value).reshape(
        peer_count, local_count, capacity, model_width
    )
    send_weight = (
        jnp.zeros((slot_total,), jnp.bfloat16).at[slot_index].set(route_weight.reshape(-1))
    )
    send_weight = send_weight.reshape(peer_count, local_count, capacity)
    w_gate_all, w_up_all, w_down_all = (
        lax.all_gather(gate_weight, "dp", axis=1, tiled=True),
        lax.all_gather(up_weight, "dp", axis=1, tiled=True),
        lax.all_gather(down_weight, "dp", axis=1, tiled=True),
    )
    recv_tokens, recv_grads, recv_weight = (
        lax.all_to_all(send_tokens, "expert", split_axis=0, concat_axis=2, tiled=True),
        lax.all_to_all(send_grads, "expert", split_axis=0, concat_axis=2, tiled=True),
        lax.all_to_all(send_weight, "expert", split_axis=0, concat_axis=2, tiled=True),
    )
    bundles = [
        (recv_tokens[0, expert], recv_grads[0, expert], recv_weight[0, expert])
        for expert in range(local_count)
    ]
    results_rows = []
    results_in = []
    results_out = []
    for expert in range(local_count):
        weights = (
            w_gate_all[expert],
            w_up_all[expert],
            w_down_all[expert],
            adapter_in[expert],
            adapter_out[expert],
        )
        rows_out, grad_factor_in, grad_factor_out = expert_rows(bundles[expert], weights)
        results_rows.append(rows_out)
        results_in.append(grad_factor_in)
        results_out.append(grad_factor_out)
    back_rows = jnp.stack(results_rows)[None]
    returned = lax.all_to_all(back_rows, "expert", split_axis=2, concat_axis=0, tiled=True)
    route_rows = returned.reshape(slot_total, model_width)[slot_index]
    grad_tokens = jnp.sum(
        route_rows.reshape(token_count, route_count, model_width).astype(jnp.float32), axis=1
    )
    grad_in_all, grad_out_all = (
        lax.psum_scatter(jnp.stack(results_in), "dp", scatter_dimension=2, tiled=True),
        lax.psum_scatter(jnp.stack(results_out), "dp", scatter_dimension=2, tiled=True),
    )
    return (grad_tokens.astype(jnp.bfloat16), grad_in_all, grad_out_all)


def solution(mesh):
    return jax.shard_map(
        per_device,
        mesh=mesh,
        in_specs=(
            P(("group", "expert", "dp"), None),
            P(("group", "expert", "dp"), None),
            P(("group", "expert", "dp"), None),
            P(("group", "expert", "dp"), None),
            P("expert", "dp", None),
            P("expert", "dp", None),
            P("expert", "dp", None),
            P("expert", None, None),
            P("expert", None, None),
        ),
        out_specs=(
            P(("group", "expert", "dp"), None),
            P(("group", "expert"), None, "dp"),
            P(("group", "expert"), None, "dp"),
        ),
        check_vma=False,
    )
```

profile of v0, /device:TPU:0, one launch (start us, length us, event | category | flops | bytes accessed | tf_op | source)
XLA Modules:
  0.0 277.4 jit_solution(6579244968035068298)
XLA Ops:
  7.2 0.8 copy.33
  8.2 0.7 broadcast_multiply_fusion
  8.9 1.1 reduce-window.6
  10.5 0.8 copy.36
  11.5 3.8 %scatter_custom_fusion = bf16[640]{0:T(1024)(128)(2,1)S(1)} fusion(s32[512]{0:T(512)S(1)} %bitcast.157, bf16[512]{0:T(512)(128)(2,1)S(1)} %reshape.128, bf16[]{:T(256)} %constant.15.clone.1), kind=kCustom, calls=%fused_computation.113 | custom fusion | bytes 1282 | tf_op jit(solution)/shard_map/scatter | solution.py:97
  15.2 0.7 reshape.95
  15.9 7.3 %all-to-all-start = ((bf16[8,2,40]{2,1,0:T(2,128)(2,1)}), bf16[8,2,40]{2,1,0:T(2,128)(2,1)S(1)}, u32[]{:S(2)}, u32[]{:S(2)}) async-start(bf16[8,2,40]{2,1,0:T(2,128)(2,1)} %reshape.95), calls=%async_computation | async-start | bytes 8192 | tf_op jit(solution)/shard_map/all_to_all | solution.py:108
  23.2 2.4 scatter_custom_fusion.1
  25.7 3.4 %gather_fusion.1 = bf16[640,2048]{1,0:T(8,128)(2,1)S(1)} fusion(bf16[64,2048]{1,0:T(8,128)(2,1)S(1)} %copy-done, s32[1024]{0:T(1024)S(1)} %pad_clamp_fusion.1), kind=kCustom, calls=%fused_computation.1 | custom fusion | bytes 5245440 | tf_op jit(solution)/shard_map/gather | solution.py:90
  29.1 4.1 %gather_fusion = bf16[640,2048]{1,0:T(8,128)(2,1)} fusion(bf16[64,2048]{1,0:T(8,128)(2,1)S(1)} %copy-done.1, s32[1024]{0:T(1024)S(1)} %pad_clamp_fusion.1), kind=kCustom, calls=%fused_computation | custom fusion | bytes 5245440 | tf_op jit(solution)/shard_map/gather | solution.py:93
  33.3 4.5 %broadcast_select_fusion.1 = (bf16[8,2,40,2048]{3,2,1,0:T(8,128)(2,1)}, bf16[8,2,40,2048]{3,2,1,0:T(8,128)(2,1)}) fusion(bf16[8,2,40,2048]{3,2,1,0:T(8,128)(2,1)} %bitcast.143, pred[8,2,40]{2,1,0:T(4,128)(4,1)S(1)} %broadcast_in_dim.40, bf16[8,2,40,2048]{3,2,1,0:T(8,128)(2,1)S(1)} %bitcast.142), kind=kLoop, calls=%fused_computation.11 | loop fusion | flops 2621440 | bytes 10486400 | tf_op jit(solution)/shard_map/jit(_where)/select_n | solution.py:93
  37.8 6.0 %all-to-all-start.2 = ((bf16[8,2,40,2048]{3,2,1,0:T(8,128)(2,1)}), bf16[8,2,40,2048]{3,2,1,0:T(8,128)(2,1)S(1)}, u32[]{:S(2)}, u32[]{:S(2)}) async-start(bf16[8,2,40,2048]{3,2,1,0:T(8,128)(2,1)} %get-tuple-element.6), calls=%async_computation.2 | async-start | bytes 5242880 | tf_op jit(solution)/shard_map/all_to_all | solution.py:106
  44.5 58.2 %all-to-all-done.2 = bf16[8,2,40,2048]{3,2,1,0:T(8,128)(2,1)S(1)} async-done(((bf16[8,2,40,2048]{3,2,1,0:T(8,128)(2,1)}), bf16[8,2,40,2048]{3,2,1,0:T(8,128)(2,1)S(1)}, u32[]{:S(2)}, u32[]{:S(2)}) %all-to-all-start.2) | async-done | bytes 2621472 | tf_op jit(solution)/shard_map/all_to_all | solution.py:106
  102.7 4.4 %all-to-all-start.1 = ((bf16[8,2,40,2048]{3,2,1,0:T(8,128)(2,1)}), bf16[8,2,40,2048]{3,2,1,0:T(8,128)(2,1)}, u32[]{:S(2)}, u32[]{:S(2)}) async-start(bf16[8,2,40,2048]{3,2,1,0:T(8,128)(2,1)} %get-tuple-element.5), calls=%async_computation.1 | async-start | bytes 5242880 | tf_op jit(solution)/shard_map/all_to_all | solution.py:107
  107.2 0.7 all-gather.6.cloned.1.call-update
  108.7 1.7 copy.39
  110.5 55.7 %all-to-all-done.1 = bf16[8,2,40,2048]{3,2,1,0:T(8,128)(2,1)} async-done(((bf16[8,2,40,2048]{3,2,1,0:T(8,128)(2,1)}), bf16[8,2,40,2048]{3,2,1,0:T(8,128)(2,1)}, u32[]{:S(2)}, u32[]{:S(2)}) %all-to-all-start.1) | async-done | bytes 2621472 | tf_op jit(solution)/shard_map/all_to_all | solution.py:107
  166.1 1.9 copy.38
  168.5 1.0 copy-done.19
  169.5 1.1 convolution_multiply_fusion.3
  171.0 1.1 convolution_multiply_fusion.2
  172.1 3.6 %fusion.10 = f32[320,384]{1,0:T(8,128)} fusion(bf16[2,2048,384]{2,1,0:T(8,128)(2,1)} %all-gather.8.cloned.1.call-done, bf16[1,2,320,2048]{3,2,1,0:T(8,128)(2,1)} %bitcast.150), kind=kOutput, calls=%fused_computation.29 | convolution fusion | flops 503316480 | bytes 3375104 | tf_op jit(solution)/shard_map/dot_general | solution.py:15
  175.7 0.8 fusion.13
  176.6 3.8 %multiply_convert_fusion.1 = (bf16[320,384]{1,0:T(8,128)(2,1)}, f32[320,384]{1,0:T(8,128)}) fusion(f32[320,384]{1,0:T(8,128)} %fusion.10, bf16[2,2048,384]{2,1,0:T(8,128)(2,1)} %all-gather.6.cloned.1.call-done, bf16[1,2,320,2048]{3,2,1,0:T(8,128)(2,1)} %bitcast.151), kind=kOutput, calls=%fused_computation.54 | convolution fusion | flops 504053760 | bytes 4112384 | tf_op jit(solution)/shard_map/dot_general | solution.py:16
  180.4 1.7 multiply_convert_fusion
  182.1 2.5 fusion.15
  184.8 0.9 fusion.9
  185.8 1.0 copy-done.7
  186.7 0.9 fusion.3
  187.8 1.0 copy-done.22
  188.8 0.9 fusion.17
  189.8 0.9 fusion.12
  190.8 0.9 fusion.2
  191.9 4.2 %copy.40 = bf16[1,2,320,2048]{3,1,0,2:T(2,128)(2,1)} copy(bf16[1,2,320,2048]{3,2,1,0:T(8,128)(2,1)S(1)} %maximum_bitcast_fusion) | data formatting | bytes 5242880 | tf_op jit(solution)/shard_map/broadcast_in_dim | solution.py:129
  196.1 3.8 %all-to-all-start.3 = ((bf16[1,2,320,2048]{3,1,0,2:T(2,128)(2,1)}), bf16[1,2,320,2048]{3,1,0,2:T(2,128)(2,1)S(1)}, u32[]{:S(2)}, u32[]{:S(2)}) async-start(bf16[1,2,320,2048]{3,1,0,2:T(2,128)(2,1)} %copy.40), calls=%async_computation.3 | async-start | bytes 5242880 | tf_op jit(solution)/shard_map/all_to_all | solution.py:130
  200.9 1.0 copy.42
  201.9 0.9 reshape.142
  203.1 2.0 fusion.5
  205.1 1.8 fusion.4
  206.9 0.8 pad_maximum_fusion
  208.4 3.9 %reduce-scatter.7.cloned.1.call-done = f32[192,32]{1,0:T(8,128)} async-done(((f32[384,32]{1,0:T(8,128)}), f32[192,32]{1,0:T(8,128)}) %reduce-scatter.7.cloned.1.call-update) | async-done | bytes 24592
  212.3 1.0 reshape.143
  213.3 0.7 copy.43
  214.1 45.5 %all-to-all-done.3 = bf16[1,2,320,2048]{3,1,0,2:T(2,128)(2,1)S(1)} async-done(((bf16[1,2,320,2048]{3,1,0,2:T(2,128)(2,1)}), bf16[1,2,320,2048]{3,1,0,2:T(2,128)(2,1)S(1)}, u32[]{:S(2)}, u32[]{:S(2)}) %all-to-all-start.3) | async-done | bytes 2621472 | tf_op jit(solution)/shard_map/all_to_all | solution.py:130
  259.5 1.5 copy-done.2
  261.0 2.9 %copy.41 = bf16[1,2,8,40,2048]{4,3,1,2,0:T(8,128)(2,1)S(1)} copy(bf16[1,2,8,40,2048]{4,1,3,2,0:T(2,128)(2,1)} %bitcast.141) | data formatting | bytes 5242880 | tf_op jit(solution)/shard_map/all_to_all | solution.py:130
  263.9 3.3 %gather_fusion.2 = bf16[512,2048]{1,0:T(8,128)(2,1)} fusion(bf16[640,2048]{1,0:T(8,128)(2,1)S(1)} %bitcast.140, s32[1024]{0:T(1024)S(1)} %pad_clamp_fusion), kind=kCustom, calls=%fused_computation.2 | custom fusion | bytes 4196352 | tf_op jit(solution)/shard_map/gather | solution.py:131
  267.2 3.7 %bitcast_reduce_fusion = bf16[64,2048]{1,0:T(8,128)(2,1)} fusion(bf16[512,2048]{1,0:T(8,128)(2,1)} %gather_fusion.2), kind=kLoop, calls=%fused_computation.18 | loop fusion | flops 917504 | bytes 2359296 | tf_op jit(solution)/shard_map/reduce_sum | solution.py:132
  (84 shorter events, 6.1 us)
Async XLA Ops:
  7.2 18.5 %copy-start = (bf16[64,2048]{1,0:T(8,128)(2,1)S(1)}, bf16[64,2048]{1,0:T(8,128)(2,1)}, u32[]{:S(2)}) copy-start(bf16[64,2048]{1,0:T(8,128)(2,1)} %param.9) | copy-start | bytes 786436
  11.5 11.7 %copy-start.21 = (s32[512,1]{0,1:T(1,128)}, s32[512,1]{0,1:T(1,128)S(1)}, u32[]{:S(2)}) copy-start(s32[512,1]{0,1:T(1,128)S(1)} %compare_select_fusion) | copy-start | bytes 6148
  15.9 21.9 %all-to-all-start = ((bf16[8,2,40]{2,1,0:T(2,128)(2,1)}), bf16[8,2,40]{2,1,0:T(2,128)(2,1)S(1)}, u32[]{:S(2)}, u32[]{:S(2)}) async-start(bf16[8,2,40]{2,1,0:T(2,128)(2,1)} %reshape.95), calls=%async_computation | async-start | bytes 8192 | tf_op jit(solution)/shard_map/all_to_all | solution.py:108
  25.7 3.4 %copy-start.1 = (bf16[64,2048]{1,0:T(8,128)(2,1)S(1)}, bf16[64,2048]{1,0:T(8,128)(2,1)}, u32[]{:S(2)}) copy-start(bf16[64,2048]{1,0:T(8,128)(2,1)} %param.10) | copy-start | bytes 786436
  37.8 64.9 %all-to-all-start.2 = ((bf16[8,2,40,2048]{3,2,1,0:T(8,128)(2,1)}), bf16[8,2,40,2048]{3,2,1,0:T(8,128)(2,1)S(1)}, u32[]{:S(2)}, u32[]{:S(2)}) async-start(bf16[8,2,40,2048]{3,2,1,0:T(8,128)(2,1)} %get-tuple-element.6), calls=%async_computation.2 | async-start | bytes 5242880 | tf_op jit(solution)/shard_map/all_to_all | solution.py:106
  43.8 128.3 %all-gather.8.cloned.1.call-start = ((), (), s32[]{:S(2)}) async-start(), calls=%async_computation.8 | async-start | bytes 4718592 | tf_op jit(solution)/shard_map/all_gather | solution.py:101
  102.7 63.4 %all-to-all-start.1 = ((bf16[8,2,40,2048]{3,2,1,0:T(8,128)(2,1)}), bf16[8,2,40,2048]{3,2,1,0:T(8,128)(2,1)}, u32[]{:S(2)}, u32[]{:S(2)}) async-start(bf16[8,2,40,2048]{3,2,1,0:T(8,128)(2,1)} %get-tuple-element.5), calls=%async_computation.1 | async-start | bytes 5242880 | tf_op jit(solution)/shard_map/all_to_all | solution.py:107
  107.1 69.5 %all-gather.6.cloned.1.call-start = ((), (), s32[]{:S(2)}) async-start(), calls=%async_computation.7 | async-start | bytes 4718592 | tf_op jit(solution)/shard_map/all_gather | solution.py:102
  107.9 74.2 %all-gather.4.cloned.1.call-start = ((), (), s32[]{:S(2)}) async-start(), calls=%async_computation.6 | async-start | bytes 4718592 | tf_op jit(solution)/shard_map/all_gather | solution.py:103
  110.4 57.6 %copy-start.23 = (bf16[2,16,2048]{2,1,0:T(8,128)(2,1)S(1)}, bf16[2,16,2048]{2,1,0:T(8,128)(2,1)}, u32[]{:S(2)}) copy-start(bf16[2,16,2048]{2,1,0:T(8,128)(2,1)} %param.17) | copy-start | bytes 393220
  110.5 59.1 %copy-start.16 = (bf16[2,16,384]{2,1,0:T(8,128)(2,1)S(1)}, bf16[2,16,384]{2,1,0:T(8,128)(2,1)}, u32[]{:S(2)}) copy-start(bf16[2,16,384]{2,1,0:T(8,128)(2,1)} %param.16) | copy-start | bytes 73732
  168.0 19.6 %copy-start.3 = (bf16[8,2,40,2048]{3,2,0,1:T(8,128)(2,1)}, bf16[8,2,40,2048]{3,2,0,1:T(8,128)(2,1)S(1)}, u32[]{:S(2)}) copy-start(bf16[8,2,40,2048]{3,2,0,1:T(8,128)(2,1)S(1)} %copy.38) | copy-start | bytes 7864324
  168.5 1.0 copy-start.19
  171.0 1.1 copy-start.17
  172.1 3.6 %copy-start.4 = (bf16[2,2048,384]{2,1,0:T(8,128)(2,1)S(1)}, bf16[2,2048,384]{2,1,0:T(8,128)(2,1)}, u32[]{:S(2)}) copy-start(bf16[2,2048,384]{2,1,0:T(8,128)(2,1)} %all-gather.8.cloned.1.call-done) | copy-start | bytes 9437188
  172.1 3.6 %copy-start.8 = (bf16[8,2,40,2048]{3,2,0,1:T(8,128)(2,1)S(1)}, bf16[8,2,40,2048]{3,2,0,1:T(8,128)(2,1)}, u32[]{:S(2)}) copy-start(bf16[8,2,40,2048]{3,2,0,1:T(8,128)(2,1)} %copy.39) | copy-start | bytes 7864324
  176.6 3.8 %copy-start.6 = (bf16[2,2048,384]{2,1,0:T(8,128)(2,1)S(1)}, bf16[2,2048,384]{2,1,0:T(8,128)(2,1)}, u32[]{:S(2)}) copy-start(bf16[2,2048,384]{2,1,0:T(8,128)(2,1)} %all-gather.6.cloned.1.call-done) | copy-start | bytes 9437188
  176.6 3.8 %copy-start.9 = (bf16[8,2,40,2048]{3,2,0,1:T(8,128)(2,1)S(1)}, bf16[8,2,40,2048]{3,2,0,1:T(8,128)(2,1)}, u32[]{:S(2)}) copy-start(bf16[8,2,40,2048]{3,2,0,1:T(8,128)(2,1)} %copy.39) | copy-start | bytes 7864324
  182.1 2.5 copy-start.5
  182.1 2.6 copy-start.10
  182.1 2.7 copy-start.15
  184.8 1.9 copy-start.7
  186.7 1.0 copy-start.13
  186.7 2.1 copy-start.22
  188.8 1.0 copy-start.14
  196.1 3.8 %copy-start.12 = (bf16[320,384]{1,0:T(8,128)(2,1)S(1)}, bf16[320,384]{1,0:T(8,128)(2,1)}, u32[]{:S(2)}) copy-start(bf16[320,384]{1,0:T(8,128)(2,1)} %get-tuple-element.9) | copy-start | bytes 737284
  196.1 3.8 %copy-start.20 = (bf16[320,16]{0,1:T(8,128)(2,1)S(1)}, bf16[320,16]{0,1:T(8,128)(2,1)}, u32[]{:S(2)}) copy-start(bf16[320,16]{0,1:T(8,128)(2,1)} %copy-done.19) | copy-start | bytes 30724
  196.1 4.0 %copy-start.11 = (bf16[320,384]{1,0:T(8,128)(2,1)S(1)}, bf16[320,384]{1,0:T(8,128)(2,1)}, u32[]{:S(2)}) copy-start(bf16[320,384]{1,0:T(8,128)(2,1)} %get-tuple-element.7) | copy-start | bytes 737284
  196.1 4.0 %copy-start.18 = (bf16[320,16]{0,1:T(8,128)(2,1)S(1)}, bf16[320,16]{0,1:T(8,128)(2,1)}, u32[]{:S(2)}) copy-start(bf16[320,16]{0,1:T(8,128)(2,1)} %copy-done.17) | copy-start | bytes 30724
  196.1 63.4 %all-to-all-start.3 = ((bf16[1,2,320,2048]{3,1,0,2:T(2,128)(2,1)}), bf16[1,2,320,2048]{3,1,0,2:T(2,128)(2,1)S(1)}, u32[]{:S(2)}, u32[]{:S(2)}) async-start(bf16[1,2,320,2048]{3,1,0,2:T(2,128)(2,1)} %copy.40), calls=%async_computation.3 | async-start | bytes 5242880 | tf_op jit(solution)/shard_map/all_to_all | solution.py:130
  199.9 12.4 %reduce-scatter.7.cloned.1.call-start = ((), (), s32[]{:S(2)}) async-start(), calls=%async_computation.10 | async-start | bytes 294912
  202.9 68.0 %reduce-scatter.5.cloned.1.call-start = ((), (), s32[]{:S(2)}) async-start(), calls=%async_computation.9 | async-start | bytes 393216 | tf_op jit(solution)/shard_map/reduce_scatter | solution.py:137
  259.5 1.5 copy-start.2
Sparse Core Ops, SparseCore 0:
  46.2 13.5 all-gather.7
  109.5 13.4 all-gather.5
  124.6 13.2 all-gather.3
  203.2 8.9 reduce-scatter.6
  214.9 8.7 reduce-scatter.4
where the time goes:
time: 278 us; the launch traced here: 277 us
  waiting for transfers between devices  165 us (59%)
  local copies, waits for them, and re-layouts  39.5 us (14%)
  matrix products  24.1 us (9%)
  starting transfers between devices  22 us (8%)
  between operations  14.1 us (5%)
  other arithmetic  12.5 us (4%)
    all_to_all x1, waiting for transfers between devices, per_device(): lax.all_to_all(send_tokens, 'expert', split_axis=0, concat_axis=2, tiled=...  58.2 us
    all_to_all x1, waiting for transfers between devices, per_device(): lax.all_to_all(send_grads, 'expert', split_axis=0, concat_axis=2, tiled=T...  55.7 us
    all_to_all x1, waiting for transfers between devices, per_device(): lax.all_to_all(back_rows, 'expert', split_axis=2, concat_axis=0, tiled=True)  45.5 us
    unnamed x54, local copies, waits for them, and re-layouts  10.3 us
    all_to_all x1, starting transfers between devices, per_device(): lax.all_to_all(send_weight, 'expert', split_axis=0, concat_axis=2, tiled=...  7.25 us
    all_to_all x1, starting transfers between devices, per_device(): lax.all_to_all(send_tokens, 'expert', split_axis=0, concat_axis=2, tiled=...  5.99 us
    unnamed x6, waiting for transfers between devices  5.81 us
  transfers between devices with their start and end apart: 9, of which 4 were waited for; matrix products, arithmetic and copies ran while one was open for 18% of the time, Pallas kernels for 0%

commit v1 on v0

v1 whole, which is shorter than its diff:
```python
import jax
import jax.numpy as jnp
from jax import lax
from jax.sharding import PartitionSpec as P

adapter_scale = 2.0


def silu_parts(gate_pre):
    logistic = jax.nn.sigmoid(gate_pre)
    return (gate_pre * logistic, logistic * (1.0 + gate_pre * (1.0 - logistic)))


def expert_grads(tokens_in, grad_in, route_scale, weights):
    w_gate, w_up, w_down, factor_in, factor_out = weights
    gate_pre = jnp.dot(tokens_in, w_gate, preferred_element_type=jnp.float32)
    up_pre = jnp.dot(tokens_in, w_up, preferred_element_type=jnp.float32)
    activation, derivative = silu_parts(gate_pre)
    hidden = (activation * up_pre).astype(jnp.bfloat16)
    low_rank = jnp.dot(hidden, factor_in.T, preferred_element_type=jnp.float32)
    low_scaled = (route_scale * low_rank).astype(jnp.bfloat16)
    adapter_back = jnp.dot(grad_in, factor_out.T, preferred_element_type=jnp.float32).astype(
        jnp.bfloat16
    )
    back_scaled = (route_scale * adapter_back.astype(jnp.float32)).astype(jnp.bfloat16)
    grad_hidden = route_scale * (
        jnp.dot(grad_in, w_down, preferred_element_type=jnp.float32)
        + adapter_scale * jnp.dot(adapter_back, factor_in, preferred_element_type=jnp.float32)
    )
    grad_gate = (grad_hidden * up_pre * derivative).astype(jnp.bfloat16)
    grad_up = (grad_hidden * activation).astype(jnp.bfloat16)
    rows_out = jnp.dot(grad_gate, w_gate.T, preferred_element_type=jnp.float32) + jnp.dot(
        grad_up, w_up.T, preferred_element_type=jnp.float32
    )
    grad_factor_in = adapter_scale * jnp.dot(
        back_scaled.T, hidden, preferred_element_type=jnp.float32
    )
    grad_factor_out = adapter_scale * jnp.dot(
        low_scaled.T, grad_in, preferred_element_type=jnp.float32
    )
    return (rows_out, grad_factor_in, grad_factor_out)


def per_device(
    tokens,
    out_grad,
    expert_ids,
    route_weight,
    gate_weight,
    up_weight,
    down_weight,
    adapter_in,
    adapter_out,
):
    peer_count = lax.axis_size("expert")
    local_count = gate_weight.shape[0]
    expert_total = local_count * peer_count
    named = expert_ids[:, :, None] == jnp.arange(expert_total, dtype=jnp.int32)[None, None, :]
    dense_weight = jnp.sum(
        jnp.where(named, route_weight.astype(jnp.float32)[:, :, None], 0.0), axis=1
    ).astype(jnp.bfloat16)
    all_weight = lax.all_gather(dense_weight, "expert", axis=0, tiled=True)
    all_tokens = lax.all_gather(tokens, "expert", axis=0, tiled=True)
    all_grads = lax.all_gather(out_grad, "expert", axis=0, tiled=True)
    w_gate_all, w_up_all, w_down_all = (
        lax.all_gather(gate_weight, "dp", axis=1, tiled=True),
        lax.all_gather(up_weight, "dp", axis=1, tiled=True),
        lax.all_gather(down_weight, "dp", axis=1, tiled=True),
    )
    first = lax.axis_index("expert") * local_count
    own_weight = lax.dynamic_slice_in_dim(all_weight, first, local_count, axis=1).astype(
        jnp.float32
    )
    rows = 0.0
    results_in = []
    results_out = []
    for expert in range(local_count):
        weights = (
            w_gate_all[expert],
            w_up_all[expert],
            w_down_all[expert],
            adapter_in[expert],
            adapter_out[expert],
        )
        rows_out, grad_factor_in, grad_factor_out = expert_grads(
            all_tokens, all_grads, own_weight[:, expert : expert + 1], weights
        )
        rows = rows + rows_out
        results_in.append(grad_factor_in)
        results_out.append(grad_factor_out)
    grad_tokens = lax.psum_scatter(
        rows.astype(jnp.bfloat16), "expert", scatter_dimension=0, tiled=True
    )
    grad_in_all, grad_out_all = (
        lax.psum_scatter(jnp.stack(results_in), "dp", scatter_dimension=2, tiled=True),
        lax.psum_scatter(jnp.stack(results_out), "dp", scatter_dimension=2, tiled=True),
    )
    return (grad_tokens, grad_in_all, grad_out_all)


def solution(mesh):
    return jax.shard_map(
        per_device,
        mesh=mesh,
        in_specs=(
            P(("group", "expert", "dp"), None),
            P(("group", "expert", "dp"), None),
            P(("group", "expert", "dp"), None),
            P(("group", "expert", "dp"), None),
            P("expert", "dp", None),
            P("expert", "dp", None),
            P("expert", "dp", None),
            P("expert", None, None),
            P("expert", None, None),
        ),
        out_specs=(
            P(("group", "expert", "dp"), None),
            P(("group", "expert"), None, "dp"),
            P(("group", "expert"), None, "dp"),
        ),
        check_vma=False,
    )
```

time: 278 us -> 268 us (0.964)
  local copies, waits for them, and re-layouts: 39.5 us -> 6.66 us
  blocking collectives: 0 us -> 32.3 us
  starting transfers between devices: 22 us -> 0.49 us
  waiting for transfers between devices: 165 us -> 182 us
  other arithmetic: 12.5 us -> 0.76 us
  matrix products: 24.1 us -> 31 us
    all_to_all x4 -> x0, waiting for transfers between devices: 159 us -> none  [the longest x1 58.2 us: per_device(): lax.all_to_all(send_tokens, 'expert', split_axis=0, concat_axis=2, tiled=...]
    reduce_scatter x0 -> x1, waiting for transfers between devices: none -> 73.3 us  [per_device(): lax.psum_scatter(rows.astype(jnp.bfloat16), 'expert', scatter_dimension=0...]
    all_gather x0 -> x2, waiting for transfers between devices: none -> 72 us  [the longest x1 52.6 us: per_device(): all_tokens = lax.all_gather(tokens, 'expert', axis=0, tiled=True)]
    all_gather x0 -> x1, blocking collectives: none -> 32.3 us  [per_device(): all_weight = lax.all_gather(dense_weight, 'expert', axis=0, tiled=True)]
    all_to_all x4 -> x0, starting transfers between devices: 21.4 us -> none  [the longest x1 7.25 us: per_device(): lax.all_to_all(send_weight, 'expert', split_axis=0, concat_axis=2, tiled=...]
    gather x3 -> x0, local copies, waits for them, and re-layouts: 10.8 us -> none  [the longest x1 4.07 us: per_device(): out_grad[source]]
    all_gather x1, waiting for transfers between devices: 0.01 us -> 9.95 us  [per_device(): lax.all_gather(gate_weight, 'dp', axis=1, tiled=True)]
    all_gather x1, waiting for transfers between devices: 0.01 us -> 9.6 us  [per_device(): lax.all_gather(down_weight, 'dp', axis=1, tiled=True)]
  transfers between devices with their start and end apart: 9 -> 8, of which waited for: 4 -> 7; matrix products, arithmetic and copies ran while one was open for 18% -> 9% of each run, Pallas kernels for 0% -> 0%
where the time goes in v1:
time: 268 us
  waiting for transfers between devices  182 us (68%)
  blocking collectives  32.3 us (12%)
  matrix products  31 us (12%)
  between operations  14.4 us (5%)
  local copies, waits for them, and re-layouts  6.66 us (2%)
    reduce_scatter x1, waiting for transfers between devices, per_device(): lax.psum_scatter(rows.astype(jnp.bfloat16), 'expert', scatter_dimension=0...  73.3 us
    all_gather x1, waiting for transfers between devices, per_device(): all_tokens = lax.all_gather(tokens, 'expert', axis=0, tiled=True)  52.6 us
    all_gather x1, blocking collectives, per_device(): all_weight = lax.all_gather(dense_weight, 'expert', axis=0, tiled=True)  32.3 us
    all_gather x1, waiting for transfers between devices, per_device(): all_grads = lax.all_gather(out_grad, 'expert', axis=0, tiled=True)  19.3 us
    all_gather x1, waiting for transfers between devices, per_device(): lax.all_gather(gate_weight, 'dp', axis=1, tiled=True)  9.95 us
    all_gather x1, waiting for transfers between devices, per_device(): lax.all_gather(down_weight, 'dp', axis=1, tiled=True)  9.6 us
    all_gather x1, waiting for transfers between devices, per_device(): lax.all_gather(up_weight, 'dp', axis=1, tiled=True)  8.74 us
    unnamed x47, local copies, waits for them, and re-layouts  6.64 us
  transfers between devices with their start and end apart: 8, of which 7 were waited for; matrix products, arithmetic and copies ran while one was open for 9% of the time, Pallas kernels for 0%

profile of v1, /device:TPU:0, one launch (start us, length us, event | category | flops | bytes accessed | tf_op | source)
XLA Modules:
  0.0 267.7 jit_solution(8619494146216281395)
XLA Ops:
  7.2 0.7 all-gather.7.cloned.1.call-update
  7.9 0.0 all-gather.15.cloned.1.call-start
  7.9 0.7 all-gather.15.cloned.1.call-update
  8.7 0.7 all-gather.11.cloned.1.call-update
  9.5 0.5 all-gather.13.cloned.1.call-update
  10.0 0.5 all-gather.9.cloned.1.call-update
  10.6 0.0 reduce-scatter.10.cloned.1.call-start
  10.7 32.3 %all-gather = bf16[8,64,16]{1,2,0:T(8,128)(2,1)S(1)} all-gather(bf16[1,64,16]{1,2,0:T(8,128)(2,1)S(1)} %bitcast.85), channel_id=1, replica_groups=mesh['group'=2,'expert'=8,'dp'=2] {'expert'}, dimensions={0}, use_global_device_ids=true | all-gather | bytes 18432 | tf_op jit(solution)/shard_map/all_gather | solution.py:62
  43.0 0.1 reshape.9
  43.1 19.3 %all-gather.7.cloned.1.call-done = bf16[512,2048]{1,0:T(8,128)(2,1)} async-done(((bf16[64,2048]{1,0:T(8,128)(2,1)}), bf16[512,2048]{1,0:T(8,128)(2,1)}) %all-gather.7.cloned.1.call-update) | async-done | bytes 2097168 | tf_op jit(solution)/shard_map/all_gather | solution.py:64
  62.5 2.2 convolution_convert_fusion.1
  64.7 10.0 %all-gather.15.cloned.1.call-done = bf16[2,2048,384]{2,1,0:T(8,128)(2,1)} async-done(((bf16[2,1024,384]{2,1,0:T(8,128)(2,1)}), bf16[2,2048,384]{2,1,0:T(8,128)(2,1)}) %all-gather.15.cloned.1.call-update) | async-done | bytes 3145744 | tf_op jit(solution)/shard_map/all_gather | solution.py:66
  74.7 52.6 %all-gather.11.cloned.1.call-done = bf16[512,2048]{1,0:T(8,128)(2,1)} async-done(((bf16[64,2048]{1,0:T(8,128)(2,1)}), bf16[512,2048]{1,0:T(8,128)(2,1)}) %all-gather.11.cloned.1.call-update) | async-done | bytes 2097168 | tf_op jit(solution)/shard_map/all_gather | solution.py:63
  127.3 3.3 %fusion.7 = f32[512,384]{1,0:T(8,128)S(1)} fusion(bf16[512,2048]{1,0:T(8,128)(2,1)} %all-gather.11.cloned.1.call-done, bf16[2,2048,384]{2,1,0:T(8,128)(2,1)} %all-gather.15.cloned.1.call-done), kind=kOutput, calls=%fused_computation.16 | convolution fusion | flops 805306368 | bytes 4456448 | tf_op jit(solution)/shard_map/dot_general | solution.py:16
  130.6 8.7 %all-gather.13.cloned.1.call-done = bf16[2,2048,384]{2,1,0:T(8,128)(2,1)} async-done(((bf16[2,1024,384]{2,1,0:T(8,128)(2,1)}), bf16[2,2048,384]{2,1,0:T(8,128)(2,1)}) %all-gather.13.cloned.1.call-update) | async-done | bytes 3145744 | tf_op jit(solution)/shard_map/all_gather | solution.py:67
  139.3 4.2 %multiply_convert_fusion.1 = (bf16[512,384]{1,0:T(8,128)(2,1)S(1)}, f32[512,384]{1,0:T(8,128)}) fusion(f32[512,384]{1,0:T(8,128)S(1)} %fusion.7, bf16[512,2048]{1,0:T(8,128)(2,1)} %all-gather.11.cloned.1.call-done, bf16[2,2048,384]{2,1,0:T(8,128)(2,1)} %all-gather.13.cloned.1.call-done), kind=kOutput, calls=%fused_computation.37 | convolution fusion | flops 806486016 | bytes 5636096 | tf_op jit(solution)/shard_map/dot_general | solution.py:17
  143.5 0.7 copy-done.10
  144.3 0.2 fusion.18
  144.4 9.6 %all-gather.9.cloned.1.call-done = bf16[2,2048,384]{2,1,0:T(8,128)(2,1)} async-done(((bf16[2,1024,384]{2,1,0:T(8,128)(2,1)}), bf16[2,2048,384]{2,1,0:T(8,128)(2,1)}) %all-gather.9.cloned.1.call-update) | async-done | bytes 3145744 | tf_op jit(solution)/shard_map/all_gather | solution.py:68
  154.0 2.6 fusion.3
  156.7 0.3 fusion.13
  157.0 0.6 convolution_convert_fusion
  157.7 0.9 copy-done.19
  158.6 1.3 fusion.2
  159.9 1.2 fusion.14
  161.1 0.1 copy-done.20
  161.1 1.2 fusion.10
  162.4 0.6 copy-done.4
  163.0 2.1 multiply_convert_fusion
  165.2 0.2 fusion.17
  165.3 0.6 copy-done.11
  165.9 0.2 copy.25
  166.1 0.9 reshape.10
  167.1 0.0 reduce-scatter.8.cloned.1.call-start
  167.1 1.6 fusion.1
  168.7 1.3 fusion
  170.0 0.7 pad_maximum_fusion
  170.8 0.2 reduce-scatter.6.cloned.1.call-start
  171.0 3.1 %fusion.4 = f32[512,2048]{1,0:T(8,128)S(1)} fusion(bf16[2,2048,384]{2,1,0:T(8,128)(2,1)} %all-gather.13.cloned.1.call-done, f32[512,384]{1,0:T(8,128)S(1)} %fusion.13, f32[512,384]{1,0:T(8,128)} %copy-done.2), kind=kOutput, calls=%fused_computation.13 | convolution fusion | flops 806486016 | bytes 7340032 | tf_op jit(solution)/shard_map/dot_general | solution.py:32
  174.2 1.4 fusion.6
  175.6 0.2 copy-done.14
  175.8 1.4 fusion.9
  177.1 0.5 copy-done.5
  177.6 2.7 %add_convert_fusion = bf16[512,2048]{1,0:T(8,128)(2,1)} fusion(f32[512,2048]{1,0:T(8,128)S(1)} %fusion.9, f32[512,2048]{1,0:T(8,128)S(1)} %fusion.6, f32[512,2048]{1,0:T(8,128)S(1)} %fusion.4, bf16[2,2048,384]{2,1,0:T(8,128)(2,1)S(1)} %copy-done.5, f32[512,384]{1,0:T(8,128)S(1)} %copy-done.1, f32[512,384]{1,0:T(8,128)S(1)} %copy-done.7), kind=kOutput, calls=%fused_computation | convolution fusion | flops 810680320 | bytes 17825792 | tf_op jit(solution)/shard_map/dot_general | solution.py:32
  180.4 1.1 reshape.11
  181.5 0.7 copy.26
  182.2 5.4 %reduce-scatter.8.cloned.1.call-done = f32[2,16,1024]{2,1,0:T(8,128)} async-done(((f32[2,16,2048]{2,1,0:T(8,128)}), f32[2,16,1024]{2,1,0:T(8,128)}) %reduce-scatter.8.cloned.1.call-update) | async-done | bytes 131088 | tf_op jit(solution)/shard_map/reduce_scatter | solution.py:96
  187.6 73.3 %reduce-scatter.6.cloned.1.call-done = bf16[64,2048]{1,0:T(8,128)(2,1)} async-done(((bf16[512,2048]{1,0:T(8,128)(2,1)}), bf16[64,2048]{1,0:T(8,128)(2,1)}) %reduce-scatter.6.cloned.1.call-update) | async-done | bytes 262160 | tf_op jit(solution)/shard_map/reduce_scatter | solution.py:91
  (49 shorter events, 0.3 us)
Async XLA Ops:
  7.2 55.3 %all-gather.7.cloned.1.call-start = ((), (), s32[]{:S(2)}) async-start(), calls=%async_computation.3 | async-start | bytes 2359296 | tf_op jit(solution)/shard_map/all_gather | solution.py:64
  7.9 66.8 %all-gather.15.cloned.1.call-start = ((), (), s32[]{:S(2)}) async-start(), calls=%async_computation.7 | async-start | bytes 4718592 | tf_op jit(solution)/shard_map/all_gather | solution.py:66
  8.6 2.0 copy-start.18
  8.7 2.0 copy-start.17
  8.7 53.8 %copy-start.15 = (bf16[2,16,2048]{2,1,0:T(8,128)(2,1)S(1)}, bf16[2,16,2048]{2,1,0:T(8,128)(2,1)}, u32[]{:S(2)}) copy-start(bf16[2,16,2048]{2,1,0:T(8,128)(2,1)} %param.17) | copy-start | bytes 393220
  8.7 118.6 %all-gather.11.cloned.1.call-start = ((), (), s32[]{:S(2)}) async-start(), calls=%async_computation.5 | async-start | bytes 2359296 | tf_op jit(solution)/shard_map/all_gather | solution.py:63
  9.4 129.9 %all-gather.13.cloned.1.call-start = ((), (), s32[]{:S(2)}) async-start(), calls=%async_computation.6 | async-start | bytes 4718592 | tf_op jit(solution)/shard_map/all_gather | solution.py:67
  10.0 144.1 %all-gather.9.cloned.1.call-start = ((), (), s32[]{:S(2)}) async-start(), calls=%async_computation.4 | async-start | bytes 4718592 | tf_op jit(solution)/shard_map/all_gather | solution.py:68
  10.6 169.8 %reduce-scatter.10.cloned.1.call-start = ((), (), s32[]{:S(2)}) async-start(), calls=%async_computation.10 | async-start | bytes 294912
  130.6 13.0 %copy-start.2 = (f32[512,384]{1,0:T(8,128)}, f32[512,384]{1,0:T(8,128)S(1)}, u32[]{:S(2)}) copy-start(f32[512,384]{1,0:T(8,128)S(1)} %fusion.7) | copy-start | bytes 2359300
  130.6 23.5 %copy-start = (bf16[512,2048]{1,0:T(8,128)(2,1)S(1)}, bf16[512,2048]{1,0:T(8,128)(2,1)}, u32[]{:S(2)}) copy-start(bf16[512,2048]{1,0:T(8,128)(2,1)} %all-gather.7.cloned.1.call-done) | copy-start | bytes 6291460
  143.5 0.7 copy-start.10
  144.4 12.3 %copy-start.16 = (bf16[2,16,384]{2,1,0:T(8,128)(2,1)S(1)}, bf16[2,16,384]{2,1,0:T(8,128)(2,1)}, u32[]{:S(2)}) copy-start(bf16[2,16,384]{2,1,0:T(8,128)(2,1)} %param.16) | copy-start | bytes 73732
  156.7 1.9 copy-start.19
  158.6 2.5 copy-start.8
  158.6 2.5 copy-start.20
  161.1 1.9 copy-start.4
  163.0 2.1 copy-start.6
  165.2 0.7 copy-start.11
  167.0 1.7 copy-start.12
  167.1 20.6 %reduce-scatter.8.cloned.1.call-start = ((), (), s32[]{:S(2)}) async-start(), calls=%async_computation.9 | async-start | bytes 393216 | tf_op jit(solution)/shard_map/reduce_scatter | solution.py:96
  170.7 3.4 %copy-start.3 = (f32[512,384]{1,0:T(8,128)S(1)}, f32[512,384]{1,0:T(8,128)}, u32[]{:S(2)}) copy-start(f32[512,384]{1,0:T(8,128)} %copy-done.2) | copy-start | bytes 2359300
  170.8 3.4 %copy-start.13 = (f32[512,384]{1,0:T(8,128)S(1)}, f32[512,384]{1,0:T(8,128)}, u32[]{:S(2)}) copy-start(f32[512,384]{1,0:T(8,128)} %get-tuple-element.8) | copy-start | bytes 2359300
  170.8 90.1 %reduce-scatter.6.cloned.1.call-start = ((), (), s32[]{:S(2)}) async-start(), calls=%async_computation.8 | async-start | bytes 2359296 | tf_op jit(solution)/shard_map/reduce_scatter | solution.py:91
  171.0 3.1 %copy-start.9 = (bf16[2,2048,384]{2,1,0:T(8,128)(2,1)S(1)}, bf16[2,2048,384]{2,1,0:T(8,128)(2,1)}, u32[]{:S(2)}) copy-start(bf16[2,2048,384]{2,1,0:T(8,128)(2,1)} %all-gather.15.cloned.1.call-done) | copy-start | bytes 9437188
  174.1 1.4 copy-start.1
  174.1 1.4 copy-start.7
  174.2 1.6 copy-start.14
  175.7 1.9 copy-start.5
Sparse Core Ops, SparseCore 0:
  10.1 52.2 all-gather.6
  64.0 10.6 all-gather.14
  76.8 50.4 all-gather.10
  128.7 10.6 all-gather.12
  140.7 13.2 all-gather.8
  167.2 8.7 reduce-scatter.9
  178.8 8.8 reduce-scatter.7
  192.1 68.7 reduce-scatter.5

commit v2 on v1

v2 whole, which is shorter than its diff:
```python
import functools

import jax
import jax.numpy as jnp
from jax import lax
from jax.experimental import pallas as pl
from jax.experimental.pallas import tpu as pltpu
from jax.sharding import PartitionSpec as P

adapter_scale = 2.0
f32 = jnp.float32
bf16 = jnp.bfloat16


def ring_order(count, snake):
    if snake and count % 2 == 0:
        return list(range(0, count, 2)) + list(range(count - 1, 0, -2))
    return list(range(count))


def matmul(a, b):
    return jnp.dot(a, b, preferred_element_type=f32)


def matmul_bt(a, b):
    return lax.dot_general(a, b, (((1,), (1,)), ((), ())), preferred_element_type=f32)


def matmul_at(a, b):
    return lax.dot_general(a, b, (((0,), (0,)), ((), ())), preferred_element_type=f32)


def stage_kernel(pieces, parts, hidden_width, rank, *refs):
    offset_ref, refs = refs[0], refs[1:]
    token_refs, refs = refs[:pieces], refs[pieces:]
    grad_refs, refs = refs[:pieces], refs[pieces:]
    scale_ref, factor_in_ref, factor_out_ref, refs = refs[0], refs[1], refs[2], refs[3:]
    weight_refs, refs = refs[:parts], refs[parts:]
    rows_ref, grad_in_ref, grad_out_ref = refs
    depth = weight_refs[0].shape[0]
    wide = weight_refs[0].shape[1] // 3
    spans = [
        pl.ds(pl.multiple_of(offset_ref[part], depth), depth) if parts > 1 else slice(None)
        for part in range(parts)
    ]

    def columns(piece_refs, span):
        return jnp.concatenate([ref[:, span] for ref in piece_refs], axis=0)

    gate_pre, up_pre, grad_down = 0.0, 0.0, 0.0
    for span, weight in zip(spans, weight_refs):
        tokens_in = columns(token_refs, span)
        gate_pre += matmul(tokens_in, weight[:, :wide])
        up_pre += matmul(tokens_in, weight[:, wide : 2 * wide])
    for span, weight in zip(spans, weight_refs):
        grad_down += matmul(columns(grad_refs, span), weight[:, 2 * wide :])
    grad_all = columns(grad_refs, slice(None))
    logistic = 1.0 / (1.0 + jnp.exp(-gate_pre))
    activation = gate_pre * logistic
    derivative = logistic * (1.0 + gate_pre * (1.0 - logistic))
    hidden = (activation * up_pre).astype(bf16)
    rows = hidden.shape[0]
    experts = wide // hidden_width
    scale = scale_ref[...]

    def spread(width):
        return jnp.concatenate(
            [jnp.broadcast_to(scale[:, j : j + 1], (rows, width)) for j in range(experts)], axis=1
        )

    rank_at = lax.broadcasted_iota(jnp.int32, (rows, experts * rank), 1) // rank
    rank_scale = jnp.zeros((rows, experts * rank), f32)
    for j in range(experts):
        rank_scale = jnp.where(rank_at == j, scale[:, j : j + 1], rank_scale)
    low_rank = matmul_bt(hidden, factor_in_ref[...])
    low_scaled = (rank_scale * low_rank).astype(bf16)
    adapter_back = matmul_bt(grad_all, factor_out_ref[...]).astype(bf16)
    back_scaled = (rank_scale * adapter_back.astype(f32)).astype(bf16)
    grad_hidden = spread(hidden_width) * (
        grad_down + adapter_scale * matmul(adapter_back, factor_in_ref[...])
    )
    grad_gate = (grad_hidden * up_pre * derivative).astype(bf16)
    grad_up = (grad_hidden * activation).astype(bf16)
    for span, weight in zip(spans, weight_refs):
        rows_ref[:, span] = matmul_bt(grad_gate, weight[:, :wide]) + matmul_bt(
            grad_up, weight[:, wide : 2 * wide]
        )
    grad_in_ref[...] = adapter_scale * matmul_at(back_scaled, hidden)
    grad_out_ref[...] = adapter_scale * matmul_at(low_scaled, grad_all)


def stage(offsets, token_pieces, grad_pieces, scale, factor_in, factor_out, weights, hidden_width, rank):
    rows = sum(piece.shape[0] for piece in token_pieces)
    model_width = token_pieces[0].shape[1]
    wide = weights[0].shape[1] // 3
    ranks = factor_in.shape[0]
    operands = [*token_pieces, *grad_pieces, scale, factor_in, factor_out, *weights]
    return pl.pallas_call(
        functools.partial(stage_kernel, len(token_pieces), len(weights), hidden_width, rank),
        out_shape=(
            jax.ShapeDtypeStruct((rows, model_width), f32),
            jax.ShapeDtypeStruct((ranks, wide), f32),
            jax.ShapeDtypeStruct((ranks, model_width), f32),
        ),
        in_specs=[pl.BlockSpec(memory_space=pltpu.SMEM)]
        + [pl.BlockSpec(memory_space=pltpu.VMEM)] * len(operands),
        out_specs=(pl.BlockSpec(memory_space=pltpu.VMEM),) * 3,
        compiler_params=pltpu.CompilerParams(vmem_limit_bytes=40 * 1024 * 1024),
        cost_estimate=pl.CostEstimate(
            flops=10 * rows * model_width * wide,
            bytes_accessed=sum(op.size * op.dtype.itemsize for op in operands)
            + 4 * rows * model_width,
            transcendentals=rows * wide,
        ),
    )(offsets, *operands)


def per_device(
    snake,
    tokens,
    out_grad,
    expert_ids,
    route_weight,
    gate_weight,
    up_weight,
    down_weight,
    adapter_in,
    adapter_out,
):
    peer_count = lax.axis_size("expert")
    dp_count = lax.axis_size("dp")
    token_count, model_width = tokens.shape
    local_count, depth, hidden_width = gate_weight.shape
    rank = adapter_in.shape[1]
    ranks = local_count * rank
    wide = local_count * hidden_width
    expert_total = local_count * peer_count
    order = ring_order(peer_count, snake)
    forward = [(order[i], order[(i + 1) % peer_count]) for i in range(peer_count)]
    backward = [(b, a) for a, b in forward]
    me = lax.axis_index("expert")
    dp_me = lax.axis_index("dp")

    mine = jnp.concatenate(
        [w.transpose(1, 0, 2).reshape(depth, wide) for w in (gate_weight, up_weight, down_weight)],
        axis=1,
    )
    if dp_count == 2:
        weights = (mine, lax.ppermute(mine, "dp", [(0, 1), (1, 0)]))
        offsets = jnp.stack([dp_me, 1 - dp_me]).astype(jnp.int32) * depth
    else:
        weights = (lax.all_gather(mine, "dp", axis=0, tiled=True),)
        offsets = jnp.zeros((1,), jnp.int32)

    named = expert_ids[:, :, None] == jnp.arange(expert_total, dtype=jnp.int32)[None, None, :]
    dense_weight = jnp.sum(
        jnp.where(named, route_weight.astype(f32)[:, :, None], 0.0), axis=1
    ).astype(bf16)
    all_weight = lax.all_gather(dense_weight, "expert", axis=0, tiled=False)
    order_array = jnp.asarray(order, jnp.int32)
    place = jnp.argmax(order_array == me).astype(jnp.int32)
    own_weight = lax.dynamic_slice_in_dim(all_weight, me * local_count, local_count, axis=2)
    behind = order_array[(place - jnp.arange(peer_count)) % peer_count]
    scales = own_weight[behind].astype(f32)

    eye = jnp.eye(local_count, dtype=bf16)
    factor_in = (adapter_in[:, :, None, :] * eye[:, None, :, None]).reshape(ranks, wide)
    factor_out = adapter_out.reshape(ranks, model_width)

    full = (peer_count - 1) // 2
    split = peer_count % 2 == 0
    half = token_count // 2
    tokens_behind, tokens_ahead, grads_behind, grads_ahead = [tokens], [tokens], [out_grad], [out_grad]
    for _ in range(full):
        tokens_behind.append(lax.ppermute(tokens_behind[-1], "expert", forward))
        tokens_ahead.append(lax.ppermute(tokens_ahead[-1], "expert", backward))
        grads_behind.append(lax.ppermute(grads_behind[-1], "expert", forward))
        grads_ahead.append(lax.ppermute(grads_ahead[-1], "expert", backward))
    if split:
        tokens_far = (
            lax.ppermute(tokens_behind[-1][:half], "expert", forward),
            lax.ppermute(tokens_ahead[-1][half:], "expert", backward),
        )
        grads_far = (
            lax.ppermute(grads_behind[-1][:half], "expert", forward),
            lax.ppermute(grads_ahead[-1][half:], "expert", backward),
        )

    run = functools.partial(
        stage,
        offsets,
        factor_in=factor_in,
        factor_out=factor_out,
        weights=weights,
        hidden_width=hidden_width,
        rank=rank,
    )
    total_in, total_out = [], []
    rows_own, grad_in, grad_out = run([tokens], [out_grad], scales[0])
    total_in.append(grad_in)
    total_out.append(grad_out)
    rows_at = [None]
    for d in range(1, full + 1):
        rows_d, grad_in, grad_out = run(
            [tokens_behind[d], tokens_ahead[d]],
            [grads_behind[d], grads_ahead[d]],
            jnp.concatenate([scales[d], scales[peer_count - d]]),
        )
        rows_at.append(rows_d)
        total_in.append(grad_in)
        total_out.append(grad_out)
    if split:
        rows_far, grad_in, grad_out = run(tokens_far, grads_far, scales[peer_count // 2])
        total_in.append(grad_in)
        total_out.append(grad_out)
        moving_back = lax.ppermute(rows_far[:half].astype(bf16), "expert", backward)
        moving_ahead = lax.ppermute(rows_far[half:].astype(bf16), "expert", forward)

    for d in range(full, 0, -1):
        back = rows_at[d][:token_count]
        ahead = rows_at[d][token_count:]
        if d < full:
            back = back + moving_back.astype(f32)
            ahead = ahead + moving_ahead.astype(f32)
        elif split:
            back = jnp.concatenate([back[:half] + moving_back.astype(f32), back[half:]])
            ahead = jnp.concatenate([ahead[:half], ahead[half:] + moving_ahead.astype(f32)])
        moving_back = lax.ppermute(back.astype(bf16), "expert", backward)
        moving_ahead = lax.ppermute(ahead.astype(bf16), "expert", forward)
    grad_tokens = (rows_own + moving_back.astype(f32) + moving_ahead.astype(f32)).astype(bf16)

    sum_in = sum(total_in)
    grad_in = jnp.stack(
        [
            sum_in[j * rank : (j + 1) * rank, j * hidden_width : (j + 1) * hidden_width]
            for j in range(local_count)
        ]
    )
    grad_out = sum(total_out).reshape(local_count, rank, model_width)
    grad_in_all = lax.psum_scatter(grad_in, "dp", scatter_dimension=2, tiled=True)
    grad_out_all = lax.psum_scatter(grad_out, "dp", scatter_dimension=2, tiled=True)
    return (grad_tokens, grad_in_all, grad_out_all)


def solution(mesh):
    snake = mesh.shape["dp"] == 2
    return jax.shard_map(
        functools.partial(per_device, snake),
        mesh=mesh,
        in_specs=(
            P(("group", "expert", "dp"), None),
            P(("group", "expert", "dp"), None),
            P(("group", "expert", "dp"), None),
            P(("group", "expert", "dp"), None),
            P("expert", "dp", None),
            P("expert", "dp", None),
            P("expert", "dp", None),
            P("expert", None, None),
            P("expert", None, None),
        ),
        out_specs=(
            P(("group", "expert", "dp"), None),
            P(("group", "expert"), None, "dp"),
            P(("group", "expert"), None, "dp"),
        ),
        check_vma=False,
    )
```

time: 268 us -> 153 us (0.57)
  waiting for transfers between devices: 182 us -> 21.7 us
  Pallas kernels: 0 us -> 38.3 us
  matrix products: 31 us -> 0 us
  starting transfers between devices: 0.49 us -> 25.6 us
  other arithmetic: 0.76 us -> 6.28 us
  local copies, waits for them, and re-layouts: 6.66 us -> 11 us
  blocking collectives: 32.3 us -> 35.3 us
    all_gather x5 -> x0, waiting for transfers between devices: 100 us -> none  [the longest x1 52.6 us: per_device(): all_tokens = lax.all_gather(tokens, 'expert', axis=0, tiled=True)]
    reduce_scatter x2 -> x1, waiting for transfers between devices: 78.7 us -> 3.46 us  [per_device(): lax.psum_scatter(grad_out, 'dp', scatter_dimension=2, tiled=True)]
    pallas_call x0 -> x5, Pallas kernels: none -> 38.3 us  [stage(): pl.pallas_call(functools.partial(stage_kernel, len(token_pieces), len(wei...]
    dot_general x18 -> x0, matrix products: 31 us -> none  [the longest x2 6.33 us: expert_grads(): up_pre = jnp.dot(tokens_in, w_up, preferred_element_type=jnp.float32)]
    ppermute x0 -> x25, starting transfers between devices: none -> 25.5 us  [the longest x3 4.85 us: per_device(): moving_ahead = lax.ppermute(ahead.astype(bf16), 'expert', forward)]
    ppermute x0 -> x25, waiting for transfers between devices: none -> 18.2 us  [the longest x3 6.52 us: per_device(): tokens_behind.append(lax.ppermute(tokens_behind[-1], 'expert', forward))]
    convert_element_type x2 -> x6, other arithmetic: 0.01 us -> 3.54 us  [the longest x2 2.74 us: per_device(): moving_back = lax.ppermute(back.astype(bf16), 'expert', backward)]
    unnamed x9 -> x3, waiting for transfers between devices: 3.18 us -> 0.05 us
  transfers between devices with their start and end apart: 8 -> 27, of which waited for: 7 -> 10; matrix products, arithmetic and copies ran while one was open for 9% -> 7% of each run, Pallas kernels for 0% -> 20%
where the time goes in v2:
time: 153 us
  Pallas kernels  38.3 us (25%)
  blocking collectives  35.3 us (23%)
  starting transfers between devices  25.6 us (17%)
  waiting for transfers between devices  21.7 us (14%)
  between operations  14.5 us (9%)
  local copies, waits for them, and re-layouts  11 us (7%)
  other arithmetic  6.28 us (4%)
    pallas_call x5, Pallas kernels, stage(): pl.pallas_call(functools.partial(stage_kernel, len(token_pieces), len(wei...  38.3 us
    all_gather x1, blocking collectives, per_device(): all_weight = lax.all_gather(dense_weight, 'expert', axis=0, tiled=False)  35.3 us
    ppermute x3, waiting for transfers between devices, per_device(): tokens_behind.append(lax.ppermute(tokens_behind[-1], 'expert', forward))  6.52 us
    unnamed x37, local copies, waits for them, and re-layouts  5.75 us
    ppermute x3, waiting for transfers between devices, per_device(): moving_back = lax.ppermute(back.astype(bf16), 'expert', backward)  5.26 us
    ppermute x3, starting transfers between devices, per_device(): moving_ahead = lax.ppermute(ahead.astype(bf16), 'expert', forward)  4.85 us
    ppermute x3, waiting for transfers between devices, per_device(): grads_behind.append(lax.ppermute(grads_behind[-1], 'expert', forward))  4.24 us
    ppermute x3, starting transfers between devices, per_device(): tokens_ahead.append(lax.ppermute(tokens_ahead[-1], 'expert', backward))  3.97 us
  transfers between devices with their start and end apart: 27, of which 10 were waited for; matrix products, arithmetic and copies ran while one was open for 7% of the time, Pallas kernels for 20%

profile of v2, /device:TPU:0, one launch (start us, length us, event | category | flops | bytes accessed | tf_op | source)
XLA Modules:
  0.0 152.7 jit_solution(15424261823290043134)
XLA Ops:
  7.2 1.7 %copy.59 = bf16[2,128,8,384]{3,2,0,1:T(8,128)(2,1)S(1)} copy(bf16[2,128,8,384]{3,2,1,0:T(8,128)(2,1)} %bitcast.60) | data formatting | bytes 3145728 | tf_op jit(solution)/shard_map/reshape | solution.py:145
  8.9 1.4 constant_dynamic-update-slice_fusion.2
  10.7 1.4 constant_dynamic-update-slice_fusion.1
  12.1 1.4 constant_dynamic-update-slice_fusion.refs_6_.refs_8_
  13.5 0.5 collective-permute-start
  14.0 2.6 %collective-permute-start.1 = (bf16[64,2048]{1,0:T(8,128)(2,1)S(1)}, bf16[64,2048]{1,0:T(8,128)(2,1)S(1)}, u32[]{:S(2)}, u32[]{:S(2)}) collective-permute-start(bf16[64,2048]{1,0:T(8,128)(2,1)S(1)} %copy-done.1), channel_id=1, source_target_pairs={{0,4},{4,8},{8,12},{12,14},{14,10},{10,6},{6,2},{2,0},{1,5},{5,9},... | collective-permute-start | bytes 786440 | tf_op jit(solution)/shard_map/ppermute | solution.py:175
  16.6 2.0 %collective-permute-start.3 = (bf16[64,2048]{1,0:T(8,128)(2,1)S(1)}, bf16[64,2048]{1,0:T(8,128)(2,1)S(1)}, u32[]{:S(2)}, u32[]{:S(2)}) collective-permute-start(bf16[64,2048]{1,0:T(8,128)(2,1)S(1)} %copy-done.2), channel_id=1, source_target_pairs={{0,4},{4,8},{8,12},{12,14},{14,10},{10,6},{6,2},{2,0},{1,5},{5,9},... | collective-permute-start | bytes 786440 | tf_op jit(solution)/shard_map/ppermute | solution.py:177
  18.6 0.7 compare_reduce_fusion
  19.3 0.7 fusion.1
  19.9 0.6 gather_fusion
  20.6 35.3 %all-gather.1 = bf16[8,64,16]{1,2,0:T(8,128)(2,1)S(1)} all-gather(bf16[1,64,16]{1,2,0:T(8,128)(2,1)S(1)} %bitcast.67), channel_id=2, replica_groups=mesh['group'=2,'expert'=8,'dp'=2] {'expert'}, dimensions={0}, use_global_device_ids=true | all-gather | bytes 18432 | tf_op jit(solution)/shard_map/all_gather | solution.py:159
  55.9 0.6 gather_fusion.1
  56.6 2.0 %collective-permute-start.6 = (bf16[64,2048]{1,0:T(8,128)(2,1)S(1)}, bf16[64,2048]{1,0:T(8,128)(2,1)}, u32[]{:S(2)}, u32[]{:S(2)}) collective-permute-start(bf16[64,2048]{1,0:T(8,128)(2,1)S(1)} %collective-permute-done.2.refs_2_), channel_id=1, source_target_pairs={{4,0},{8,4},{12,8},{14,12},{10,14},{6,10},{2,6},{0,2},{5,1},{9,5},... | collective-permute-start | bytes 786440 | tf_op jit(solution)/shard_map/ppermute | solution.py:176
  58.7 2.0 %collective-permute-start.8 = (bf16[64,2048]{1,0:T(8,128)(2,1)S(1)}, bf16[64,2048]{1,0:T(8,128)(2,1)}, u32[]{:S(2)}, u32[]{:S(2)}) collective-permute-start(bf16[64,2048]{1,0:T(8,128)(2,1)S(1)} %collective-permute-done.4.refs_4_), channel_id=1, source_target_pairs={{4,0},{8,4},{12,8},{14,12},{10,14},{6,10},{2,6},{0,2},{5,1},{9,5},... | collective-permute-start | bytes 786440 | tf_op jit(solution)/shard_map/ppermute | solution.py:178
  60.8 5.1 %collective-permute-done.5.refs_1_ = bf16[64,2048]{1,0:T(8,128)(2,1)S(1)} collective-permute-done((bf16[64,2048]{1,0:T(8,128)(2,1)S(1)}, bf16[64,2048]{1,0:T(8,128)(2,1)S(1)}, u32[]{:S(2)}, u32[]{:S(2)}) %collective-permute-start.5) | collective-permute-done | bytes 262176 | tf_op jit(solution)/shard_map/ppermute | solution.py:175
  66.0 2.0 %collective-permute-start.10 = (bf16[64,2048]{1,0:T(8,128)(2,1)}, bf16[64,2048]{1,0:T(8,128)(2,1)S(1)}, u32[]{:S(2)}, u32[]{:S(2)}) collective-permute-start(bf16[64,2048]{1,0:T(8,128)(2,1)} %collective-permute-done.6.refs_2_), channel_id=1, source_target_pairs={{4,0},{8,4},{12,8},{14,12},{10,14},{6,10},{2,6},{0,2},{5,1},{9,5},... | collective-permute-start | bytes 786440 | tf_op jit(solution)/shard_map/ppermute | solution.py:176
  68.0 3.6 %collective-permute-done.7.refs_3_ = bf16[64,2048]{1,0:T(8,128)(2,1)} collective-permute-done((bf16[64,2048]{1,0:T(8,128)(2,1)S(1)}, bf16[64,2048]{1,0:T(8,128)(2,1)}, u32[]{:S(2)}, u32[]{:S(2)}) %collective-permute-start.7) | collective-permute-done | bytes 262176 | tf_op jit(solution)/shard_map/ppermute | solution.py:177
  71.6 2.0 %collective-permute-start.12 = (bf16[64,2048]{1,0:T(8,128)(2,1)}, bf16[64,2048]{1,0:T(8,128)(2,1)S(1)}, u32[]{:S(2)}, u32[]{:S(2)}) collective-permute-start(bf16[64,2048]{1,0:T(8,128)(2,1)} %collective-permute-done.8.refs_4_), channel_id=1, source_target_pairs={{4,0},{8,4},{12,8},{14,12},{10,14},{6,10},{2,6},{0,2},{5,1},{9,5},... | collective-permute-start | bytes 786440 | tf_op jit(solution)/shard_map/ppermute | solution.py:178
  74.4 1.5 collective-permute-done.9.refs_1_
  75.8 0.3 collective-permute-start.13
  76.2 1.8 %collective-permute-start.14 = (bf16[32,2048]{1,0:T(8,128)(2,1)S(1)}, bf16[32,2048]{1,0:T(8,128)(2,1)S(1)}, u32[]{:S(2)}, u32[]{:S(2)}) collective-permute-start(bf16[32,2048]{1,0:T(8,128)(2,1)S(1)} %slice.118), channel_id=1, source_target_pairs={{4,0},{8,4},{12,8},{14,12},{10,14},{6,10},{2,6},{0,2},{5,1},{9,5},... | collective-permute-start | bytes 393224 | tf_op jit(solution)/shard_map/ppermute | solution.py:182
  78.0 0.6 collective-permute-done.11.refs_3_
  78.6 0.3 collective-permute-start.15
  79.0 1.8 %collective-permute-start.16 = (bf16[32,2048]{1,0:T(8,128)(2,1)S(1)}, bf16[32,2048]{1,0:T(8,128)(2,1)S(1)}, u32[]{:S(2)}, u32[]{:S(2)}) collective-permute-start(bf16[32,2048]{1,0:T(8,128)(2,1)S(1)} %slice.120), channel_id=1, source_target_pairs={{4,0},{8,4},{12,8},{14,12},{10,14},{6,10},{2,6},{0,2},{5,1},{9,5},... | collective-permute-start | bytes 393224 | tf_op jit(solution)/shard_map/ppermute | solution.py:186
  80.8 7.5 %shard_map.124 = (f32[128,2048]{1,0:T(8,128)S(1)}, f32[32,768]{1,0:T(8,128)S(1)}, f32[32,2048]{1,0:T(8,128)S(1)}) custom-call(s32[2]{0:T(128)S(1)} %add_multiply_fusion.refs_0_, bf16[64,2048]{1,0:T(8,128)(2,1)S(1)} %collective-permute-done.9.refs_1_, bf16[64,2048]{1,0:T(8,128)(2,1)S(1)} %collective-permute-done.10.refs_2_, ...), custom_call_target="tpu_custom_call" | custom-call | flops 2013265920 | bytes 11715584 | tf_op jit(solution)/shard_map/pallas_call | solution.py:98
  88.5 7.7 %shard_map.125 = (f32[64,2048]{1,0:T(8,128)S(1)}, f32[32,768]{1,0:T(8,128)S(1)}, f32[32,2048]{1,0:T(8,128)S(1)}) custom-call(s32[2]{0:T(128)S(1)} %add_multiply_fusion.refs_0_, bf16[32,2048]{1,0:T(8,128)(2,1)S(1)} %collective-permute-done.13.refs_1_, bf16[32,2048]{1,0:T(8,128)(2,1)S(1)} %collective-permute-done.14.refs_2_, ...), custom_call_target="tpu_custom_call" | custom-call | flops 1006632960 | bytes 10666496 | tf_op jit(solution)/shard_map/pallas_call | solution.py:98
  96.3 2.0 %collective-permute-start.21 = (bf16[32,2048]{1,0:T(8,128)(2,1)S(1)}, bf16[32,2048]{1,0:T(8,128)(2,1)S(1)}, u32[]{:S(2)}, u32[]{:S(2)}) collective-permute-start(bf16[32,2048]{1,0:T(8,128)(2,1)S(1)} %get-tuple-element.44), channel_id=1, source_target_pairs={{0,4},{4,8},{8,12},{12,14},{14,10},{10,6},{6,2},{2,0},{1,5},{5,9},... | collective-permute-start | bytes 393224 | tf_op jit(solution)/shard_map/ppermute | solution.py:217
  98.3 7.7 %shard_map.123 = (f32[128,2048]{1,0:T(8,128)S(1)}, f32[32,768]{1,0:T(8,128)S(1)}, f32[32,2048]{1,0:T(8,128)S(1)}) custom-call(s32[2]{0:T(128)S(1)} %add_multiply_fusion.refs_0_, bf16[64,2048]{1,0:T(8,128)(2,1)S(1)} %collective-permute-done.5.refs_1_, bf16[64,2048]{1,0:T(8,128)(2,1)} %collective-permute-done.6.refs_2_, ...), custom_call_target="tpu_custom_call" | custom-call | flops 2013265920 | bytes 11715584 | tf_op jit(solution)/shard_map/pallas_call | solution.py:98
  106.1 7.6 %shard_map.122 = (f32[128,2048]{1,0:T(8,128)S(1)}, f32[32,768]{1,0:T(8,128)S(1)}, f32[32,2048]{1,0:T(8,128)S(1)}) custom-call(s32[2]{0:T(128)S(1)} %add_multiply_fusion.refs_0_, bf16[64,2048]{1,0:T(8,128)(2,1)S(1)} %collective-permute-done.1.refs_1_, bf16[64,2048]{1,0:T(8,128)(2,1)S(1)} %collective-permute-done.2.refs_2_, ...), custom_call_target="tpu_custom_call" | custom-call | flops 2013265920 | bytes 11715584 | tf_op jit(solution)/shard_map/pallas_call | solution.py:98
  113.8 0.3 collective-permute-start.18
  114.1 1.8 %collective-permute-start.22 = (bf16[64,2048]{1,0:T(8,128)(2,1)S(1)}, bf16[64,2048]{1,0:T(8,128)(2,1)S(1)}, u32[]{:S(2)}, u32[]{:S(2)}) collective-permute-start(bf16[64,2048]{1,0:T(8,128)(2,1)S(1)} %pad_maximum_fusion.1), channel_id=1, source_target_pairs={{0,4},{4,8},{8,12},{12,14},{14,10},{10,6},{6,2},{2,0},{1,5},{5,9},... | collective-permute-start | bytes 786440 | tf_op jit(solution)/shard_map/ppermute | solution.py:229
  116.0 7.7 %shard_map.121 = (f32[64,2048]{1,0:T(8,128)S(1)}, f32[32,768]{1,0:T(8,128)S(1)}, f32[32,2048]{1,0:T(8,128)S(1)}) custom-call(s32[2]{0:T(128)S(1)} %add_multiply_fusion.refs_0_, bf16[64,2048]{1,0:T(8,128)(2,1)S(1)} %copy-done.1, bf16[64,2048]{1,0:T(8,128)(2,1)S(1)} %copy-done.2, f32[64,2]{1,0:T(8,128)S(1)} %copy.52.refs_3_, bf16[32,768]{1,0:T(8,128)(2,1)S(1)} %bitcast.56, ...), custom_call_target="tpu_custom_call" | custom-call | flops 1006632960 | bytes 10666496 | tf_op jit(solution)/shard_map/pallas_call | solution.py:98
  123.8 0.9 add_convert_fusion.4
  124.7 0.2 collective-permute-start.19
  124.9 1.8 %collective-permute-start.23 = (bf16[64,2048]{1,0:T(8,128)(2,1)}, bf16[64,2048]{1,0:T(8,128)(2,1)}, u32[]{:S(2)}, u32[]{:S(2)}) collective-permute-start(bf16[64,2048]{1,0:T(8,128)(2,1)} %get-tuple-element.38), channel_id=1, source_target_pairs={{0,4},{4,8},{8,12},{12,14},{14,10},{10,6},{6,2},{2,0},{1,5},{5,9},... | collective-permute-start | bytes 786440 | tf_op jit(solution)/shard_map/ppermute | solution.py:229
  126.7 0.2 copy.57
  126.9 0.9 reshape.132
  127.9 4.2 %collective-permute-done.19 = bf16[64,2048]{1,0:T(8,128)(2,1)} collective-permute-done((bf16[64,2048]{1,0:T(8,128)(2,1)}, bf16[64,2048]{1,0:T(8,128)(2,1)}, u32[]{:S(2)}, u32[]{:S(2)}) %collective-permute-start.19) | collective-permute-done | bytes 262176 | tf_op jit(solution)/shard_map/ppermute | solution.py:228
  132.1 1.8 %add_convert_fusion.3 = (bf16[64,2048]{1,0:T(8,128)(2,1)S(1)}, bf16[64,2048]{1,0:T(8,128)(2,1)}) fusion(bf16[64,2048]{1,0:T(8,128)(2,1)} %collective-permute-done.19, f32[128,2048]{1,0:T(8,128)S(1)} %get-tuple-element.21, bf16[64,2048]{1,0:T(8,128)(2,1)} %collective-permute-done.23), kind=kLoop, calls=%fused_computation.5 | loop fusion | flops 786432 | bytes 2097152 | tf_op jit(solution)/shard_map/convert_element_type | solution.py:228
  134.0 1.2 collective-permute-start.24
  135.2 0.8 collective-permute-start.20
  136.0 0.8 add_add_fusion
  136.8 1.1 reshape.133
  137.9 0.7 copy.58
  138.6 1.9 %collective-permute-done.24 = bf16[64,2048]{1,0:T(8,128)(2,1)S(1)} collective-permute-done((bf16[64,2048]{1,0:T(8,128)(2,1)}, bf16[64,2048]{1,0:T(8,128)(2,1)S(1)}, u32[]{:S(2)}, u32[]{:S(2)}) %collective-permute-start.24) | collective-permute-done | bytes 262176 | tf_op jit(solution)/shard_map/ppermute | solution.py:229
  140.6 1.0 collective-permute-done.20
  141.6 0.8 add_convert_fusion
  142.4 3.5 %reduce-scatter.5.cloned.1.call-done = f32[2,16,1024]{2,1,0:T(8,128)} async-done(((f32[2,16,2048]{2,1,0:T(8,128)}), f32[2,16,1024]{2,1,0:T(8,128)}) %reduce-scatter.5.cloned.1.call-update) | async-done | bytes 131088 | tf_op jit(solution)/shard_map/reduce_scatter | solution.py:241
  (96 shorter events, 2.3 us)
Async XLA Ops:
  7.2 3.2 %copy-start.10 = (bf16[2,1024,384]{2,1,0:T(8,128)(2,1)S(1)}, bf16[2,1024,384]{2,1,0:T(8,128)(2,1)}, u32[]{:S(2)}) copy-start(bf16[2,1024,384]{2,1,0:T(8,128)(2,1)} %param.15) | copy-start | bytes 4718596
  7.2 129.7 %reduce-scatter.7.cloned.1.call-start = ((), (), s32[]{:S(2)}) async-start(), calls=%async_computation.3 | async-start | bytes 294912
  7.2 3.3 %copy-start.11 = (bf16[2,1024,384]{2,1,0:T(8,128)(2,1)S(1)}, bf16[2,1024,384]{2,1,0:T(8,128)(2,1)}, u32[]{:S(2)}) copy-start(bf16[2,1024,384]{2,1,0:T(8,128)(2,1)} %param.16) | copy-start | bytes 4718596
  10.5 3.5 %copy-start.1 = (bf16[64,2048]{1,0:T(8,128)(2,1)S(1)}, bf16[64,2048]{1,0:T(8,128)(2,1)}, u32[]{:S(2)}) copy-start(bf16[64,2048]{1,0:T(8,128)(2,1)} %refs_1_.1) | copy-start | bytes 786436
  10.5 6.1 %copy-start.2 = (bf16[64,2048]{1,0:T(8,128)(2,1)S(1)}, bf16[64,2048]{1,0:T(8,128)(2,1)}, u32[]{:S(2)}) copy-start(bf16[64,2048]{1,0:T(8,128)(2,1)} %refs_2_.1) | copy-start | bytes 786436
  10.5 8.1 %copy-start.14 = (bf16[64,8]{0,1:T(8,128)(2,1)S(1)}, bf16[64,8]{0,1:T(8,128)(2,1)}, u32[]{:S(2)}) copy-start(bf16[64,8]{0,1:T(8,128)(2,1)} %param.13) | copy-start | bytes 3076
  10.5 8.1 %copy-start.9 = (s32[8]{0:T(128)S(1)}, s32[8]{0:T(128)}, u32[]{:S(2)}) copy-start(s32[8]{0:T(128)} %constant.43.clone) | copy-start | bytes 100
  10.5 10.0 %copy-start.13 = (s32[64,8]{0,1:T(8,128)S(1)}, s32[64,8]{0,1:T(8,128)}, u32[]{:S(2)}) copy-start(s32[64,8]{0,1:T(8,128)} %param.12) | copy-start | bytes 6148
  10.6 50.1 %copy-start.12 = (bf16[2,16,384]{2,1,0:T(8,128)(2,1)S(1)}, bf16[2,16,384]{2,1,0:T(8,128)(2,1)}, u32[]{:S(2)}) copy-start(bf16[2,16,384]{2,1,0:T(8,128)(2,1)} %param.17) | copy-start | bytes 73732
  10.7 70.1 %copy-start = (bf16[2,16,2048]{2,1,0:T(8,128)(2,1)S(1)}, bf16[2,16,2048]{2,1,0:T(8,128)(2,1)}, u32[]{:S(2)}) copy-start(bf16[2,16,2048]{2,1,0:T(8,128)(2,1)} %param.18) | copy-start | bytes 393220
  13.5 67.3 %collective-permute-start = (bf16[1024,2304]{1,0:T(8,128)(2,1)}, bf16[1024,2304]{1,0:T(8,128)(2,1)}, u32[]{:S(2)}, u32[]{:S(2)}) collective-permute-start(bf16[1024,2304]{1,0:T(8,128)(2,1)} %constant_dynamic-update-slice_fusion.refs_6_.refs_8_), channel_id=1, source_target_pairs={{0,1},{1,0},{2,3},{3,2},{4,5},{5,4},{6,7},{7,6},{8,9},{9,8},{10,11... | collective-permute-start | bytes 14155784 | tf_op jit(solution)/shard_map/ppermute | solution.py:149
  14.0 42.6 %collective-permute-start.1 = (bf16[64,2048]{1,0:T(8,128)(2,1)S(1)}, bf16[64,2048]{1,0:T(8,128)(2,1)S(1)}, u32[]{:S(2)}, u32[]{:S(2)}) collective-permute-start(bf16[64,2048]{1,0:T(8,128)(2,1)S(1)} %copy-done.1), channel_id=1, source_target_pairs={{0,4},{4,8},{8,12},{12,14},{14,10},{10,6},{6,2},{2,0},{1,5},{5,9},... | collective-permute-start | bytes 786440 | tf_op jit(solution)/shard_map/ppermute | solution.py:175
  16.6 40.0 %collective-permute-start.2 = (bf16[64,2048]{1,0:T(8,128)(2,1)S(1)}, bf16[64,2048]{1,0:T(8,128)(2,1)S(1)}, u32[]{:S(2)}, u32[]{:S(2)}) collective-permute-start(bf16[64,2048]{1,0:T(8,128)(2,1)S(1)} %copy-done.1), channel_id=1, source_target_pairs={{4,0},{8,4},{12,8},{14,12},{10,14},{6,10},{2,6},{0,2},{5,1},{9,5},... | collective-permute-start | bytes 786440 | tf_op jit(solution)/shard_map/ppermute | solution.py:176
  16.6 42.1 %collective-permute-start.3 = (bf16[64,2048]{1,0:T(8,128)(2,1)S(1)}, bf16[64,2048]{1,0:T(8,128)(2,1)S(1)}, u32[]{:S(2)}, u32[]{:S(2)}) collective-permute-start(bf16[64,2048]{1,0:T(8,128)(2,1)S(1)} %copy-done.2), channel_id=1, source_target_pairs={{0,4},{4,8},{8,12},{12,14},{14,10},{10,6},{6,2},{2,0},{1,5},{5,9},... | collective-permute-start | bytes 786440 | tf_op jit(solution)/shard_map/ppermute | solution.py:177
  18.6 40.1 %collective-permute-start.4 = (bf16[64,2048]{1,0:T(8,128)(2,1)S(1)}, bf16[64,2048]{1,0:T(8,128)(2,1)S(1)}, u32[]{:S(2)}, u32[]{:S(2)}) collective-permute-start(bf16[64,2048]{1,0:T(8,128)(2,1)S(1)} %copy-done.2), channel_id=1, source_target_pairs={{4,0},{8,4},{12,8},{14,12},{10,14},{6,10},{2,6},{0,2},{5,1},{9,5},... | collective-permute-start | bytes 786440 | tf_op jit(solution)/shard_map/ppermute | solution.py:178
  56.6 9.2 %collective-permute-start.5 = (bf16[64,2048]{1,0:T(8,128)(2,1)S(1)}, bf16[64,2048]{1,0:T(8,128)(2,1)S(1)}, u32[]{:S(2)}, u32[]{:S(2)}) collective-permute-start(bf16[64,2048]{1,0:T(8,128)(2,1)S(1)} %collective-permute-done.1.refs_1_), channel_id=1, source_target_pairs={{0,4},{4,8},{8,12},{12,14},{14,10},{10,6},{6,2},{2,0},{1,5},{5,9},... | collective-permute-start | bytes 786440 | tf_op jit(solution)/shard_map/ppermute | solution.py:175
  56.6 9.4 %collective-permute-start.6 = (bf16[64,2048]{1,0:T(8,128)(2,1)S(1)}, bf16[64,2048]{1,0:T(8,128)(2,1)}, u32[]{:S(2)}, u32[]{:S(2)}) collective-permute-start(bf16[64,2048]{1,0:T(8,128)(2,1)S(1)} %collective-permute-done.2.refs_2_), channel_id=1, source_target_pairs={{4,0},{8,4},{12,8},{14,12},{10,14},{6,10},{2,6},{0,2},{5,1},{9,5},... | collective-permute-start | bytes 786440 | tf_op jit(solution)/shard_map/ppermute | solution.py:176
  58.6 12.9 %collective-permute-start.7 = (bf16[64,2048]{1,0:T(8,128)(2,1)S(1)}, bf16[64,2048]{1,0:T(8,128)(2,1)}, u32[]{:S(2)}, u32[]{:S(2)}) collective-permute-start(bf16[64,2048]{1,0:T(8,128)(2,1)S(1)} %collective-permute-done.3.refs_3_), channel_id=1, source_target_pairs={{0,4},{4,8},{8,12},{12,14},{14,10},{10,6},{6,2},{2,0},{1,5},{5,9},... | collective-permute-start | bytes 786440 | tf_op jit(solution)/shard_map/ppermute | solution.py:177
  58.7 12.9 %collective-permute-start.8 = (bf16[64,2048]{1,0:T(8,128)(2,1)S(1)}, bf16[64,2048]{1,0:T(8,128)(2,1)}, u32[]{:S(2)}, u32[]{:S(2)}) collective-permute-start(bf16[64,2048]{1,0:T(8,128)(2,1)S(1)} %collective-permute-done.4.refs_4_), channel_id=1, source_target_pairs={{4,0},{8,4},{12,8},{14,12},{10,14},{6,10},{2,6},{0,2},{5,1},{9,5},... | collective-permute-start | bytes 786440 | tf_op jit(solution)/shard_map/ppermute | solution.py:178
  65.8 10.0 %collective-permute-start.9 = (bf16[64,2048]{1,0:T(8,128)(2,1)S(1)}, bf16[64,2048]{1,0:T(8,128)(2,1)S(1)}, u32[]{:S(2)}, u32[]{:S(2)}) collective-permute-start(bf16[64,2048]{1,0:T(8,128)(2,1)S(1)} %collective-permute-done.5.refs_1_), channel_id=1, source_target_pairs={{0,4},{4,8},{8,12},{12,14},{14,10},{10,6},{6,2},{2,0},{1,5},{5,9},... | collective-permute-start | bytes 786440 | tf_op jit(solution)/shard_map/ppermute | solution.py:175
  66.0 10.2 %collective-permute-start.10 = (bf16[64,2048]{1,0:T(8,128)(2,1)}, bf16[64,2048]{1,0:T(8,128)(2,1)S(1)}, u32[]{:S(2)}, u32[]{:S(2)}) collective-permute-start(bf16[64,2048]{1,0:T(8,128)(2,1)} %collective-permute-done.6.refs_2_), channel_id=1, source_target_pairs={{4,0},{8,4},{12,8},{14,12},{10,14},{6,10},{2,6},{0,2},{5,1},{9,5},... | collective-permute-start | bytes 786440 | tf_op jit(solution)/shard_map/ppermute | solution.py:176
  71.6 7.1 %collective-permute-start.11 = (bf16[64,2048]{1,0:T(8,128)(2,1)}, bf16[64,2048]{1,0:T(8,128)(2,1)S(1)}, u32[]{:S(2)}, u32[]{:S(2)}) collective-permute-start(bf16[64,2048]{1,0:T(8,128)(2,1)} %collective-permute-done.7.refs_3_), channel_id=1, source_target_pairs={{0,4},{4,8},{8,12},{12,14},{14,10},{10,6},{6,2},{2,0},{1,5},{5,9},... | collective-permute-start | bytes 786440 | tf_op jit(solution)/shard_map/ppermute | solution.py:177
  71.6 7.3 %collective-permute-start.12 = (bf16[64,2048]{1,0:T(8,128)(2,1)}, bf16[64,2048]{1,0:T(8,128)(2,1)S(1)}, u32[]{:S(2)}, u32[]{:S(2)}) collective-permute-start(bf16[64,2048]{1,0:T(8,128)(2,1)} %collective-permute-done.8.refs_4_), channel_id=1, source_target_pairs={{4,0},{8,4},{12,8},{14,12},{10,14},{6,10},{2,6},{0,2},{5,1},{9,5},... | collective-permute-start | bytes 786440 | tf_op jit(solution)/shard_map/ppermute | solution.py:178
  75.8 12.6 %collective-permute-start.13 = (bf16[32,2048]{1,0:T(8,128)(2,1)S(1)}, bf16[32,2048]{1,0:T(8,128)(2,1)S(1)}, u32[]{:S(2)}, u32[]{:S(2)}) collective-permute-start(bf16[32,2048]{1,0:T(8,128)(2,1)S(1)} %slice.117), channel_id=1, source_target_pairs={{0,4},{4,8},{8,12},{12,14},{14,10},{10,6},{6,2},{2,0},{1,5},{5,9},... | collective-permute-start | bytes 393224 | tf_op jit(solution)/shard_map/ppermute | solution.py:181
  76.2 12.2 %collective-permute-start.14 = (bf16[32,2048]{1,0:T(8,128)(2,1)S(1)}, bf16[32,2048]{1,0:T(8,128)(2,1)S(1)}, u32[]{:S(2)}, u32[]{:S(2)}) collective-permute-start(bf16[32,2048]{1,0:T(8,128)(2,1)S(1)} %slice.118), channel_id=1, source_target_pairs={{4,0},{8,4},{12,8},{14,12},{10,14},{6,10},{2,6},{0,2},{5,1},{9,5},... | collective-permute-start | bytes 393224 | tf_op jit(solution)/shard_map/ppermute | solution.py:182
  78.6 9.8 %collective-permute-start.15 = (bf16[32,2048]{1,0:T(8,128)(2,1)S(1)}, bf16[32,2048]{1,0:T(8,128)(2,1)S(1)}, u32[]{:S(2)}, u32[]{:S(2)}) collective-permute-start(bf16[32,2048]{1,0:T(8,128)(2,1)S(1)} %slice.119), channel_id=1, source_target_pairs={{0,4},{4,8},{8,12},{12,14},{14,10},{10,6},{6,2},{2,0},{1,5},{5,9},... | collective-permute-start | bytes 393224 | tf_op jit(solution)/shard_map/ppermute | solution.py:185
  79.0 9.5 %collective-permute-start.16 = (bf16[32,2048]{1,0:T(8,128)(2,1)S(1)}, bf16[32,2048]{1,0:T(8,128)(2,1)S(1)}, u32[]{:S(2)}, u32[]{:S(2)}) collective-permute-start(bf16[32,2048]{1,0:T(8,128)(2,1)S(1)} %slice.120), channel_id=1, source_target_pairs={{4,0},{8,4},{12,8},{14,12},{10,14},{6,10},{2,6},{0,2},{5,1},{9,5},... | collective-permute-start | bytes 393224 | tf_op jit(solution)/shard_map/ppermute | solution.py:186
  88.3 7.9 %copy-start.3 = (f32[32,2048]{1,0:T(8,128)}, f32[32,2048]{1,0:T(8,128)S(1)}, u32[]{:S(2)}) copy-start(f32[32,2048]{1,0:T(8,128)S(1)} %get-tuple-element.33) | copy-start | bytes 786436
  96.2 2.2 %copy-start.5 = (f32[32,2048]{1,0:T(8,128)}, f32[32,2048]{1,0:T(8,128)S(1)}, u32[]{:S(2)}) copy-start(f32[32,2048]{1,0:T(8,128)S(1)} %get-tuple-element.34) | copy-start | bytes 786436
  96.3 17.4 %collective-permute-start.17 = (bf16[32,2048]{1,0:T(8,128)(2,1)S(1)}, bf16[32,2048]{1,0:T(8,128)(2,1)S(1)}, u32[]{:S(2)}, u32[]{:S(2)}) collective-permute-start(bf16[32,2048]{1,0:T(8,128)(2,1)S(1)} %get-tuple-element.43), channel_id=1, source_target_pairs={{4,0},{8,4},{12,8},{14,12},{10,14},{6,10},{2,6},{0,2},{5,1},{9,5},... | collective-permute-start | bytes 393224 | tf_op jit(solution)/shard_map/ppermute | solution.py:216
  96.3 17.4 %collective-permute-start.21 = (bf16[32,2048]{1,0:T(8,128)(2,1)S(1)}, bf16[32,2048]{1,0:T(8,128)(2,1)S(1)}, u32[]{:S(2)}, u32[]{:S(2)}) collective-permute-start(bf16[32,2048]{1,0:T(8,128)(2,1)S(1)} %get-tuple-element.44), channel_id=1, source_target_pairs={{0,4},{4,8},{8,12},{12,14},{14,10},{10,6},{6,2},{2,0},{1,5},{5,9},... | collective-permute-start | bytes 393224 | tf_op jit(solution)/shard_map/ppermute | solution.py:217
  106.1 7.6 %copy-start.7 = (f32[32,2048]{1,0:T(8,128)}, f32[32,2048]{1,0:T(8,128)S(1)}, u32[]{:S(2)}) copy-start(f32[32,2048]{1,0:T(8,128)S(1)} %get-tuple-element.32) | copy-start | bytes 786436
  113.8 9.9 %collective-permute-start.18 = (bf16[64,2048]{1,0:T(8,128)(2,1)S(1)}, bf16[64,2048]{1,0:T(8,128)(2,1)S(1)}, u32[]{:S(2)}, u32[]{:S(2)}) collective-permute-start(bf16[64,2048]{1,0:T(8,128)(2,1)S(1)} %pad_maximum_fusion), channel_id=1, source_target_pairs={{4,0},{8,4},{12,8},{14,12},{10,14},{6,10},{2,6},{0,2},{5,1},{9,5},... | collective-permute-start | bytes 786440 | tf_op jit(solution)/shard_map/ppermute | solution.py:228
  114.1 9.6 %collective-permute-start.22 = (bf16[64,2048]{1,0:T(8,128)(2,1)S(1)}, bf16[64,2048]{1,0:T(8,128)(2,1)S(1)}, u32[]{:S(2)}, u32[]{:S(2)}) collective-permute-start(bf16[64,2048]{1,0:T(8,128)(2,1)S(1)} %pad_maximum_fusion.1), channel_id=1, source_target_pairs={{0,4},{4,8},{8,12},{12,14},{14,10},{10,6},{6,2},{2,0},{1,5},{5,9},... | collective-permute-start | bytes 786440 | tf_op jit(solution)/shard_map/ppermute | solution.py:229
  123.7 12.3 %copy-start.4 = (f32[32,2048]{1,0:T(8,128)S(1)}, f32[32,2048]{1,0:T(8,128)}, u32[]{:S(2)}) copy-start(f32[32,2048]{1,0:T(8,128)} %copy-done.3) | copy-start | bytes 786436
  123.7 12.3 %copy-start.6 = (f32[32,2048]{1,0:T(8,128)S(1)}, f32[32,2048]{1,0:T(8,128)}, u32[]{:S(2)}) copy-start(f32[32,2048]{1,0:T(8,128)} %copy-done.5) | copy-start | bytes 786436
  123.7 12.3 %copy-start.8 = (f32[32,2048]{1,0:T(8,128)S(1)}, f32[32,2048]{1,0:T(8,128)}, u32[]{:S(2)}) copy-start(f32[32,2048]{1,0:T(8,128)} %copy-done.7) | copy-start | bytes 786436
  124.7 7.5 %collective-permute-start.19 = (bf16[64,2048]{1,0:T(8,128)(2,1)}, bf16[64,2048]{1,0:T(8,128)(2,1)}, u32[]{:S(2)}, u32[]{:S(2)}) collective-permute-start(bf16[64,2048]{1,0:T(8,128)(2,1)} %get-tuple-element.37), channel_id=1, source_target_pairs={{4,0},{8,4},{12,8},{14,12},{10,14},{6,10},{2,6},{0,2},{5,1},{9,5},... | collective-permute-start | bytes 786440 | tf_op jit(solution)/shard_map/ppermute | solution.py:228
  124.9 7.2 %collective-permute-start.23 = (bf16[64,2048]{1,0:T(8,128)(2,1)}, bf16[64,2048]{1,0:T(8,128)(2,1)}, u32[]{:S(2)}, u32[]{:S(2)}) collective-permute-start(bf16[64,2048]{1,0:T(8,128)(2,1)} %get-tuple-element.38), channel_id=1, source_target_pairs={{0,4},{4,8},{8,12},{12,14},{14,10},{10,6},{6,2},{2,0},{1,5},{5,9},... | collective-permute-start | bytes 786440 | tf_op jit(solution)/shard_map/ppermute | solution.py:229
  127.8 18.0 %reduce-scatter.5.cloned.1.call-start = ((), (), s32[]{:S(2)}) async-start(), calls=%async_computation.2 | async-start | bytes 393216 | tf_op jit(solution)/shard_map/reduce_scatter | solution.py:241
  134.0 6.6 %collective-permute-start.24 = (bf16[64,2048]{1,0:T(8,128)(2,1)}, bf16[64,2048]{1,0:T(8,128)(2,1)S(1)}, u32[]{:S(2)}, u32[]{:S(2)}) collective-permute-start(bf16[64,2048]{1,0:T(8,128)(2,1)} %get-tuple-element.36), channel_id=1, source_target_pairs={{0,4},{4,8},{8,12},{12,14},{14,10},{10,6},{6,2},{2,0},{1,5},{5,9},... | collective-permute-start | bytes 786440 | tf_op jit(solution)/shard_map/ppermute | solution.py:229
  135.2 6.4 %collective-permute-start.20 = (bf16[64,2048]{1,0:T(8,128)(2,1)S(1)}, bf16[64,2048]{1,0:T(8,128)(2,1)S(1)}, u32[]{:S(2)}, u32[]{:S(2)}) collective-permute-start(bf16[64,2048]{1,0:T(8,128)(2,1)S(1)} %get-tuple-element.35), channel_id=1, source_target_pairs={{4,0},{8,4},{12,8},{14,12},{10,14},{6,10},{2,6},{0,2},{5,1},{9,5},... | collective-permute-start | bytes 786440 | tf_op jit(solution)/shard_map/ppermute | solution.py:228
Sparse Core Ops, SparseCore 0:
  128.0 6.1 reduce-scatter.6
  137.0 8.7 reduce-scatter.4

commit v3 on v1

v3 whole, which is shorter than its diff:
```python
import functools

import jax
import jax.numpy as jnp
from jax import lax
from jax.experimental import pallas as pl
from jax.experimental.pallas import tpu as pltpu
from jax.sharding import PartitionSpec as P

adapter_scale = 2.0
f32 = jnp.float32
bf16 = jnp.bfloat16
lane_count = 128


def ring_order(count, snake):
    if snake and count % 2 == 0:
        return list(range(0, count, 2)) + list(range(count - 1, 0, -2))
    return list(range(count))


def matmul(a, b):
    return jnp.dot(a, b, preferred_element_type=f32)


def matmul_bt(a, b):
    return lax.dot_general(a, b, (((1,), (1,)), ((), ())), preferred_element_type=f32)


def matmul_at(a, b):
    return lax.dot_general(a, b, (((0,), (0,)), ((), ())), preferred_element_type=f32)


def stacked(piece_refs, span):
    return jnp.concatenate([ref[:, span] for ref in piece_refs], axis=0)


class Plan:
    def __init__(self, parts, depth, model_width, hidden_width, rank, experts):
        self.parts = parts
        self.depth = depth
        self.model_width = model_width
        self.hidden_width = hidden_width
        self.rank = rank
        self.experts = experts
        self.wide = experts * hidden_width
        self.ranks = experts * rank

    def spans(self, position_ref):
        if self.parts == 1:
            return [slice(0, self.model_width)]
        return [
            pl.ds(pl.multiple_of(position_ref[part], self.depth), self.depth)
            for part in range(self.parts)
        ]

    def forward(self, position_ref, token_refs, factor_in_ref, weight_refs):
        gate_pre, up_pre = 0.0, 0.0
        for span, weight in zip(self.spans(position_ref), weight_refs):
            tokens_in = stacked(token_refs, span)
            gate_pre += matmul(tokens_in, weight[:, : self.wide])
            up_pre += matmul(tokens_in, weight[:, self.wide : 2 * self.wide])
        logistic = 1.0 / (1.0 + jnp.exp(-gate_pre))
        activation = gate_pre * logistic
        derivative = logistic * (1.0 + gate_pre * (1.0 - logistic))
        hidden = (activation * up_pre).astype(bf16)
        low_rank = matmul_bt(hidden, factor_in_ref[...])
        return activation, up_pre * derivative, hidden, low_rank

    def scales(self, position_ref, grad_refs):
        columns = stacked(grad_refs, slice(self.model_width, None)).astype(f32)
        lane = lax.broadcasted_iota(jnp.int32, columns.shape, 1)
        first = position_ref[self.parts]
        return [
            jnp.sum(jnp.where(lane == first + j, columns, 0.0), axis=1, keepdims=True)
            for j in range(self.experts)
        ]

    def spread(self, scales, width):
        rows = scales[0].shape[0]
        at = lax.broadcasted_iota(jnp.int32, (rows, self.experts * width), 1)
        out = jnp.broadcast_to(scales[0], at.shape)
        for j in range(1, self.experts):
            out = jnp.where(at >= j * width, scales[j], out)
        return out

    def backward(
        self, position_ref, grad_refs, activation, slope, factor_in_ref, factor_out_ref, weight_refs, rows_ref
    ):
        scales = self.scales(position_ref, grad_refs)
        adapter_back, grad_down = 0.0, 0.0
        spans = self.spans(position_ref)
        for span, weight in zip(spans, weight_refs):
            grad_in = stacked(grad_refs, span)
            adapter_back += matmul_bt(grad_in, factor_out_ref[:, span])
            grad_down += matmul(grad_in, weight[:, 2 * self.wide :])
        adapter_back = adapter_back.astype(bf16)
        grad_hidden = self.spread(scales, self.hidden_width) * (
            grad_down + adapter_scale * matmul(adapter_back, factor_in_ref[...])
        )
        grad_gate = (grad_hidden * slope).astype(bf16)
        grad_up = (grad_hidden * activation).astype(bf16)
        for span, weight in zip(spans, weight_refs):
            rows_ref[:, span] = matmul_bt(grad_gate, weight[:, : self.wide]) + matmul_bt(
                grad_up, weight[:, self.wide : 2 * self.wide]
            )
        rank_scale = self.spread(scales, self.rank)
        return rank_scale, (rank_scale * adapter_back.astype(f32)).astype(bf16)

    def adapters(self, grad_refs, hidden, low_scaled, back_scaled, total_refs, out_refs):
        grad_all = stacked(grad_refs, slice(0, self.model_width))
        for total, out, value in zip(
            total_refs, out_refs, (matmul_at(back_scaled, hidden), matmul_at(low_scaled, grad_all))
        ):
            out[...] = total[...] + adapter_scale * value


def whole_kernel(plan, pieces, *refs):
    position_ref, refs = refs[0], refs[1:]
    token_refs, grad_refs, refs = refs[:pieces], refs[pieces : 2 * pieces], refs[2 * pieces :]
    factor_in_ref, factor_out_ref, refs = refs[0], refs[1], refs[2:]
    weight_refs, refs = refs[: plan.parts], refs[plan.parts :]
    total_refs, rows_ref, out_refs = refs[:2], refs[2], refs[3:]
    activation, slope, hidden, low_rank = plan.forward(
        position_ref, token_refs, factor_in_ref, weight_refs
    )
    rank_scale, back_scaled = plan.backward(
        position_ref, grad_refs, activation, slope, factor_in_ref, factor_out_ref, weight_refs, rows_ref
    )
    low_scaled = (rank_scale * low_rank).astype(bf16)
    plan.adapters(grad_refs, hidden, low_scaled, back_scaled, total_refs, out_refs)


def prepare_kernel(plan, *refs):
    raw_refs, refs = refs[:3], refs[3:]
    out_grad_ref, ids_ref, route_ref, factor_ref = refs[:4]
    packed_ref, grads_ref, factor_in_ref, sems = refs[4:]
    copies = []
    for kind in range(3):
        for expert in range(plan.experts):
            at = kind * plan.wide + expert * plan.hidden_width
            copies.append(
                pltpu.make_async_copy(
                    raw_refs[kind].at[expert],
                    packed_ref.at[:, at : at + plan.hidden_width],
                    sems.at[kind * plan.experts + expert],
                )
            )
    for copy in copies:
        copy.start()
    rows, lanes = grads_ref.shape[0], grads_ref.shape[1] - plan.model_width
    lane = lax.broadcasted_iota(jnp.int32, (rows, lanes), 1)
    ids, route = ids_ref[...], route_ref[...].astype(f32)
    dense = jnp.zeros((rows, lanes), f32)
    for k in range(ids.shape[1]):
        dense = jnp.where(ids[:, k : k + 1] == lane, route[:, k : k + 1], dense)
    grads_ref[:, : plan.model_width] = out_grad_ref[...]
    grads_ref[:, plan.model_width :] = dense.astype(bf16)
    factor_in_ref[...] = jnp.zeros(factor_in_ref.shape, bf16)
    for expert in range(plan.experts):
        factor_in_ref[
            expert * plan.rank : (expert + 1) * plan.rank,
            expert * plan.hidden_width : (expert + 1) * plan.hidden_width,
        ] = factor_ref[expert]
    for copy in copies:
        copy.wait()


def forward_kernel(plan, pieces, *refs):
    position_ref, refs = refs[0], refs[1:]
    token_refs, refs = refs[:pieces], refs[pieces:]
    factor_in_ref, refs = refs[0], refs[1:]
    weight_refs, out_refs = refs[: plan.parts], refs[plan.parts :]
    for out, value in zip(
        out_refs, plan.forward(position_ref, token_refs, factor_in_ref, weight_refs)
    ):
        out[...] = value


def backward_kernel(plan, pieces, *refs):
    position_ref, refs = refs[0], refs[1:]
    grad_refs, refs = refs[:pieces], refs[pieces:]
    activation_ref, slope_ref, low_rank_ref, refs = refs[0], refs[1], refs[2], refs[3:]
    factor_in_ref, factor_out_ref, refs = refs[0], refs[1], refs[2:]
    weight_refs, refs = refs[: plan.parts], refs[plan.parts :]
    rows_ref, low_scaled_ref, back_scaled_ref = refs
    rank_scale, back_scaled = plan.backward(
        position_ref,
        grad_refs,
        activation_ref[...],
        slope_ref[...],
        factor_in_ref,
        factor_out_ref,
        weight_refs,
        rows_ref,
    )
    low_scaled_ref[...] = (rank_scale * low_rank_ref[...]).astype(bf16)
    back_scaled_ref[...] = back_scaled


def adapters_kernel(plan, pieces, *refs):
    grad_refs, refs = refs[1 : 1 + pieces], refs[1 + pieces :]
    hidden_ref, low_scaled_ref, back_scaled_ref, refs = refs[0], refs[1], refs[2], refs[3:]
    plan.adapters(
        grad_refs, hidden_ref[...], low_scaled_ref[...], back_scaled_ref[...], refs[:2], refs[2:]
    )


def call(kernel, plan, pieces, position, operands, outs, flops):
    return pl.pallas_call(
        functools.partial(kernel, plan, pieces),
        out_shape=tuple(jax.ShapeDtypeStruct(shape, dtype) for shape, dtype in outs),
        in_specs=[pl.BlockSpec(memory_space=pltpu.SMEM)]
        + [pl.BlockSpec(memory_space=pltpu.VMEM)] * len(operands),
        out_specs=(pl.BlockSpec(memory_space=pltpu.VMEM),) * len(outs),
        compiler_params=pltpu.CompilerParams(vmem_limit_bytes=16 * 1024 * 1024),
        cost_estimate=pl.CostEstimate(
            flops=flops,
            bytes_accessed=sum(op.size * op.dtype.itemsize for op in operands),
            transcendentals=0,
        ),
    )(position, *operands)


def per_device(
    snake,
    tokens,
    out_grad,
    expert_ids,
    route_weight,
    gate_weight,
    up_weight,
    down_weight,
    adapter_in,
    adapter_out,
):
    peer_count = lax.axis_size("expert")
    dp_count = lax.axis_size("dp")
    token_count, model_width = tokens.shape
    local_count, depth, hidden_width = gate_weight.shape
    rank = adapter_in.shape[1]
    expert_total = local_count * peer_count
    order = ring_order(peer_count, snake)
    forward = [(order[i], order[(i + 1) % peer_count]) for i in range(peer_count)]
    backward = [(b, a) for a, b in forward]
    me = lax.axis_index("expert")
    dp_me = lax.axis_index("dp")
    parts = 2 if dp_count == 2 else 1
    plan = Plan(parts, depth, model_width, hidden_width, rank, local_count)
    wide, ranks = plan.wide, plan.ranks

    lanes = -(-expert_total // lane_count) * lane_count
    mine, grads, factor_in = pl.pallas_call(
        functools.partial(prepare_kernel, plan),
        out_shape=(
            jax.ShapeDtypeStruct((depth, 3 * wide), bf16),
            jax.ShapeDtypeStruct((token_count, model_width + lanes), bf16),
            jax.ShapeDtypeStruct((ranks, wide), bf16),
        ),
        in_specs=[pl.BlockSpec(memory_space=pltpu.HBM)] * 3 + [pl.BlockSpec(memory_space=pltpu.VMEM)] * 4,
        out_specs=(pl.BlockSpec(memory_space=pltpu.VMEM),) * 3,
        scratch_shapes=[pltpu.SemaphoreType.DMA((3 * local_count,))],
        compiler_params=pltpu.CompilerParams(vmem_limit_bytes=16 * 1024 * 1024),
    )(gate_weight, up_weight, down_weight, out_grad, expert_ids, route_weight, adapter_in)
    first_expert = me * local_count
    if parts == 2:
        weights = [mine, lax.ppermute(mine, "dp", [(0, 1), (1, 0)])]
        position = jnp.stack([dp_me * depth, (1 - dp_me) * depth, first_expert]).astype(jnp.int32)
    else:
        weights = [lax.all_gather(mine, "dp", axis=0, tiled=True)]
        position = jnp.stack([0 * first_expert, first_expert]).astype(jnp.int32)
    factor_out = adapter_out.reshape(ranks, model_width)

    full = (peer_count - 1) // 2
    split = peer_count % 2 == 0
    half = token_count // 2
    matmul_flops = 2 * model_width * wide
    totals = (jnp.zeros((ranks, wide), f32), jnp.zeros((ranks, model_width), f32))
    total_shapes = [((ranks, wide), f32), ((ranks, model_width), f32)]
    behind, ahead = [(tokens, grads)], [(tokens, grads)]
    rows_at = [None]

    def run(d):
        pieces = [behind[d], ahead[d]] + ([behind[0]] if d == 1 else [])
        rows = len(pieces) * token_count
        rows_d, *outs = call(
            whole_kernel,
            plan,
            len(pieces),
            position,
            [p[0] for p in pieces] + [p[1] for p in pieces] + [factor_in, factor_out, *weights, *totals],
            [((rows, model_width), f32)] + total_shapes,
            5 * rows * matmul_flops,
        )
        rows_at.append(rows_d)
        return outs

    def after(value, *arrays):
        held = []
        for x in arrays:
            x, value = lax.optimization_barrier((x, value))
            held.append(x)
        return value, held

    for d in range(full):
        if d > 1:
            totals, (tokens_b, tokens_a, grads_b, grads_a) = after(
                totals, behind[d][0], ahead[d][0], behind[d][1], ahead[d][1]
            )
            behind[d], ahead[d] = (tokens_b, grads_b), (tokens_a, grads_a)
        behind.append(tuple(lax.ppermute(x, "expert", forward) for x in behind[d]))
        ahead.append(tuple(lax.ppermute(x, "expert", backward) for x in ahead[d]))
        if d > 0:
            totals = run(d)
    if split:
        totals, (tokens_b, tokens_a, grads_b, grads_a) = after(
            totals, behind[full][0], ahead[full][0], behind[full][1], ahead[full][1]
        )
        far_behind = [lax.ppermute(x[:half], "expert", forward) for x in (tokens_b, grads_b)]
        far_ahead = [lax.ppermute(x[half:], "expert", backward) for x in (tokens_a, grads_a)]
        far_tokens = [far_behind[0], far_ahead[0]]
        far_grads = [far_behind[1], far_ahead[1]]
        activation, slope, hidden, low_rank = call(
            forward_kernel,
            plan,
            2,
            position,
            far_tokens + [factor_in, *weights],
            [((token_count, wide), f32)] * 2 + [((token_count, wide), bf16), ((token_count, ranks), f32)],
            2 * token_count * matmul_flops,
        )
        rows_far, low_scaled, back_scaled = call(
            backward_kernel,
            plan,
            2,
            position,
            far_grads + [activation, slope, low_rank, factor_in, factor_out, *weights],
            [((token_count, model_width), f32)] + [((token_count, ranks), bf16)] * 2,
            3 * token_count * matmul_flops,
        )
        moving_back = lax.ppermute(rows_far[:half].astype(bf16), "expert", backward)
        moving_ahead = lax.ppermute(rows_far[half:].astype(bf16), "expert", forward)
        totals, low_scaled = lax.optimization_barrier((totals, low_scaled))
    if full > 1:
        totals = run(full)
    if split:
        totals = call(
            adapters_kernel,
            plan,
            2,
            position,
            far_grads + [hidden, low_scaled, back_scaled, *totals],
            total_shapes,
            4 * token_count * ranks * (model_width + wide),
        )

    for d in range(full, 0, -1):
        back = rows_at[d][:token_count]
        front = rows_at[d][token_count : 2 * token_count]
        if d < full:
            back = back + moving_back.astype(f32)
            front = front + moving_ahead.astype(f32)
        elif split:
            back = jnp.concatenate([back[:half] + moving_back.astype(f32), back[half:]])
            front = jnp.concatenate([front[:half], front[half:] + moving_ahead.astype(f32)])
        moving_back = lax.ppermute(back.astype(bf16), "expert", backward)
        moving_ahead = lax.ppermute(front.astype(bf16), "expert", forward)
    rows_own = rows_at[1][2 * token_count :]
    grad_tokens = (rows_own + moving_back.astype(f32) + moving_ahead.astype(f32)).astype(bf16)

    grad_in = jnp.stack(
        [
            totals[0][j * rank : (j + 1) * rank, j * hidden_width : (j + 1) * hidden_width]
            for j in range(local_count)
        ]
    )
    narrow = hidden_width // dp_count
    both = jnp.concatenate(
        [
            grad_in.reshape(ranks, dp_count, narrow),
            totals[1].reshape(ranks, dp_count, model_width // dp_count),
        ],
        axis=2,
    ).transpose(1, 0, 2)
    summed = lax.psum_scatter(both, "dp", scatter_dimension=0, tiled=False)
    grad_in_all = summed[:, :narrow].reshape(local_count, rank, narrow)
    grad_out_all = summed[:, narrow:].reshape(local_count, rank, model_width // dp_count)
    return (grad_tokens, grad_in_all, grad_out_all)


def solution(mesh):
    snake = mesh.shape["dp"] == 2
    return jax.shard_map(
        functools.partial(per_device, snake),
        mesh=mesh,
        in_specs=(
            P(("group", "expert", "dp"), None),
            P(("group", "expert", "dp"), None),
            P(("group", "expert", "dp"), None),
            P(("group", "expert", "dp"), None),
            P("expert", "dp", None),
            P("expert", "dp", None),
            P("expert", "dp", None),
            P("expert", None, None),
            P("expert", None, None),
        ),
        out_specs=(
            P(("group", "expert", "dp"), None),
            P(("group", "expert"), None, "dp"),
            P(("group", "expert"), None, "dp"),
        ),
        check_vma=False,
    )
```

time: 268 us -> 121 us (0.45)
  waiting for transfers between devices: 182 us -> 29.4 us
  Pallas kernels: 0 us -> 38.2 us
  blocking collectives: 32.3 us -> 0 us
  matrix products: 31 us -> 0 us
  starting transfers between devices: 0.49 us -> 26 us
  local copies, waits for them, and re-layouts: 6.66 us -> 10.7 us
    all_gather x5 -> x0, waiting for transfers between devices: 100 us -> none  [the longest x1 52.6 us: per_device(): all_tokens = lax.all_gather(tokens, 'expert', axis=0, tiled=True)]
    reduce_scatter x2 -> x1, waiting for transfers between devices: 78.7 us -> 0.01 us  [per_device(): summed = lax.psum_scatter(both, 'dp', scatter_dimension=0, tiled=False)]
    pallas_call x0 -> x7, Pallas kernels: none -> 38.2 us  [the longest x6 35.3 us: call(): pl.pallas_call(functools.partial(kernel, plan, pieces), out_shape=tuple((...]
    all_gather x1 -> x0, blocking collectives: 32.3 us -> none  [per_device(): all_weight = lax.all_gather(dense_weight, 'expert', axis=0, tiled=True)]
    dot_general x18 -> x0, matrix products: 31 us -> none  [the longest x2 6.33 us: expert_grads(): up_pre = jnp.dot(tokens_in, w_up, preferred_element_type=jnp.float32)]
    ppermute x0 -> x25, waiting for transfers between devices: none -> 29.4 us  [the longest x6 12.4 us: per_device(): lax.ppermute(x, 'expert', forward)]
    ppermute x0 -> x25, starting transfers between devices: none -> 26 us  [the longest x6 9.22 us: per_device(): ahead.append(tuple((lax.ppermute(x, 'expert', backward) for x in ahead[d])))]
    unnamed x9 -> x1, waiting for transfers between devices: 3.18 us -> 0.02 us
  transfers between devices with their start and end apart: 8 -> 26, of which waited for: 7 -> 11; matrix products, arithmetic and copies ran while one was open for 9% -> 4% of each run, Pallas kernels for 0% -> 24%
where the time goes in v3:
time: 121 us
  Pallas kernels  38.2 us (32%)
  waiting for transfers between devices  29.4 us (24%)
  starting transfers between devices  26 us (21%)
  between operations  14.3 us (12%)
  local copies, waits for them, and re-layouts  10.7 us (9%)
  other arithmetic  2.12 us (2%)
    pallas_call x6, Pallas kernels, call(): pl.pallas_call(functools.partial(kernel, plan, pieces), out_shape=tuple((...  35.3 us
    ppermute x6, waiting for transfers between devices, per_device(): lax.ppermute(x, 'expert', forward)  12.4 us
    ppermute x3, waiting for transfers between devices, per_device(): moving_back = lax.ppermute(back.astype(bf16), 'expert', backward)  10.5 us
    ppermute x6, starting transfers between devices, per_device(): ahead.append(tuple((lax.ppermute(x, 'expert', backward) for x in ahead[d])))  9.22 us
    unnamed x16, local copies, waits for them, and re-layouts  7.46 us
    ppermute x3, waiting for transfers between devices, per_device(): moving_ahead = lax.ppermute(front.astype(bf16), 'expert', forward)  5.24 us
    ppermute x6, starting transfers between devices, per_device(): lax.ppermute(x, 'expert', forward)  3.7 us
    ppermute x3, starting transfers between devices, per_device(): moving_ahead = lax.ppermute(front.astype(bf16), 'expert', forward)  3.65 us
  transfers between devices with their start and end apart: 26, of which 11 were waited for; matrix products, arithmetic and copies ran while one was open for 4% of the time, Pallas kernels for 24%

profile of v3, /device:TPU:0, one launch (start us, length us, event | category | flops | bytes accessed | tf_op | source)
XLA Modules:
  0.0 120.8 jit_solution(15371293074331238987)
XLA Ops:
  7.2 0.8 copy.15.refs_5_
  8.0 0.8 copy.14.refs_4_
  8.8 1.4 %copy-done.1 = bf16[2,1024,384]{2,1,0:T(8,128)(2,1)S(1)} copy-done((bf16[2,1024,384]{2,1,0:T(8,128)(2,1)S(1)}, bf16[2,1024,384]{2,1,0:T(8,128)(2,1)}, u32[]{:S(2)}) %copy-start.1) | copy-done | bytes 1572888
  10.2 1.4 %copy-done.2 = bf16[2,1024,384]{2,1,0:T(8,128)(2,1)S(1)} copy-done((bf16[2,1024,384]{2,1,0:T(8,128)(2,1)S(1)}, bf16[2,1024,384]{2,1,0:T(8,128)(2,1)}, u32[]{:S(2)}) %copy-start.2) | copy-done | bytes 1572888
  11.6 1.4 %copy-done.3 = bf16[2,1024,384]{2,1,0:T(8,128)(2,1)S(1)} copy-done((bf16[2,1024,384]{2,1,0:T(8,128)(2,1)S(1)}, bf16[2,1024,384]{2,1,0:T(8,128)(2,1)}, u32[]{:S(2)}) %copy-start.3) | copy-done | bytes 1572888
  13.0 0.9 copy-done.4
  13.9 0.7 copy-done.6
  14.7 2.9 %shard_map.112 = (bf16[1024,2304]{1,0:T(8,128)(2,1)}, bf16[64,2176]{1,0:T(8,128)(2,1)S(1)}, bf16[32,768]{1,0:T(8,128)(2,1)S(1)}) custom-call(bf16[2,1024,384]{2,1,0:T(8,128)(2,1)S(1)} %copy-done.1, bf16[2,1024,384]{2,1,0:T(8,128)(2,1)S(1)} %copy-done.2, bf16[2,1024,384]{2,1,0:T(8,128)(2,1)S(1)} %copy-done.3, bf16[64,2048]{1,0:T(8,128)(2,1)S(1)} %copy-done.4, ...), custom_call_target="tpu_custom_call" | custom-call | tf_op jit(solution)/shard_map/pallas_call | solution.py:253
  17.5 0.5 collective-permute-start.4
  18.1 2.6 %collective-permute-start.3 = (bf16[64,2176]{1,0:T(8,128)(2,1)S(1)}, bf16[64,2176]{1,0:T(8,128)(2,1)S(1)}, u32[]{:S(2)}, u32[]{:S(2)}) collective-permute-start(bf16[64,2176]{1,0:T(8,128)(2,1)S(1)} %get-tuple-element.51.refs_6_), channel_id=1, source_target_pairs={{4,0},{8,4},{12,8},{14,12},{10,14},{6,10},{2,6},{0,2},{5,1},{9,5},... | collective-permute-start | bytes 835592 | tf_op jit(solution)/shard_map/ppermute | solution.py:312
  20.8 1.9 %collective-permute-start = (bf16[64,2048]{1,0:T(8,128)(2,1)S(1)}, bf16[64,2048]{1,0:T(8,128)(2,1)S(1)}, u32[]{:S(2)}, u32[]{:S(2)}) collective-permute-start(bf16[64,2048]{1,0:T(8,128)(2,1)S(1)} %copy-done.5), channel_id=1, source_target_pairs={{0,4},{4,8},{8,12},{12,14},{14,10},{10,6},{6,2},{2,0},{1,5},{5,9},... | collective-permute-start | bytes 786440 | tf_op jit(solution)/shard_map/ppermute | solution.py:311
  22.9 12.1 %collective-permute-done.refs_1_ = bf16[64,2048]{1,0:T(8,128)(2,1)S(1)} collective-permute-done((bf16[64,2048]{1,0:T(8,128)(2,1)S(1)}, bf16[64,2048]{1,0:T(8,128)(2,1)S(1)}, u32[]{:S(2)}, u32[]{:S(2)}) %collective-permute-start) | collective-permute-done | bytes 262176 | tf_op jit(solution)/shard_map/ppermute | solution.py:311
  35.0 0.4 collective-permute-start.5
  35.3 1.7 %collective-permute-start.6 = (bf16[64,2048]{1,0:T(8,128)(2,1)S(1)}, bf16[64,2048]{1,0:T(8,128)(2,1)S(1)}, u32[]{:S(2)}, u32[]{:S(2)}) collective-permute-start(bf16[64,2048]{1,0:T(8,128)(2,1)S(1)} %collective-permute-done.1.refs_2_), channel_id=1, source_target_pairs={{4,0},{8,4},{12,8},{14,12},{10,14},{6,10},{2,6},{0,2},{5,1},{9,5},... | collective-permute-start | bytes 786440 | tf_op jit(solution)/shard_map/ppermute | solution.py:312
  37.0 1.6 %collective-permute-start.8 = (bf16[64,2176]{1,0:T(8,128)(2,1)S(1)}, bf16[64,2176]{1,0:T(8,128)(2,1)S(1)}, u32[]{:S(2)}, u32[]{:S(2)}) collective-permute-start(bf16[64,2176]{1,0:T(8,128)(2,1)S(1)} %collective-permute-done.3.refs_5_), channel_id=1, source_target_pairs={{4,0},{8,4},{12,8},{14,12},{10,14},{6,10},{2,6},{0,2},{5,1},{9,5},... | collective-permute-start | bytes 835592 | tf_op jit(solution)/shard_map/ppermute | solution.py:312
  38.6 0.5 collective-permute-start.7
  39.1 8.3 %shard_map.113 = (f32[192,2048]{1,0:T(8,128)S(1)}, f32[32,768]{1,0:T(8,128)S(1)}, f32[32,2048]{1,0:T(8,128)S(1)}) custom-call(s32[3]{0:T(128)S(1)} %pad_add_fusion.refs_0_, bf16[64,2048]{1,0:T(8,128)(2,1)S(1)} %collective-permute-done.refs_1_, bf16[64,2048]{1,0:T(8,128)(2,1)S(1)} %collective-permute-done.1.refs_2_, bf16[64,2048]{1,0:T(8,128)(2,1)S(1)} %copy-done.5, ...), custom_call_target="tpu_custom_call" | custom-call | flops 3019898880 | bytes 11599872 | tf_op jit(solution)/shard_map/pallas_call | solution.py:210
  47.5 0.4 collective-permute-start.9
  47.9 1.7 %collective-permute-start.10 = (bf16[64,2048]{1,0:T(8,128)(2,1)S(1)}, bf16[64,2048]{1,0:T(8,128)(2,1)S(1)}, u32[]{:S(2)}, u32[]{:S(2)}) collective-permute-start(bf16[64,2048]{1,0:T(8,128)(2,1)S(1)} %collective-permute-done.6.refs_2_), channel_id=1, source_target_pairs={{4,0},{8,4},{12,8},{14,12},{10,14},{6,10},{2,6},{0,2},{5,1},{9,5},... | collective-permute-start | bytes 786440 | tf_op jit(solution)/shard_map/ppermute | solution.py:312
  49.9 1.7 %collective-permute-start.12 = (bf16[64,2176]{1,0:T(8,128)(2,1)S(1)}, bf16[64,2176]{1,0:T(8,128)(2,1)S(1)}, u32[]{:S(2)}, u32[]{:S(2)}) collective-permute-start(bf16[64,2176]{1,0:T(8,128)(2,1)S(1)} %collective-permute-done.8.refs_4_), channel_id=1, source_target_pairs={{4,0},{8,4},{12,8},{14,12},{10,14},{6,10},{2,6},{0,2},{5,1},{9,5},... | collective-permute-start | bytes 835592 | tf_op jit(solution)/shard_map/ppermute | solution.py:312
  51.6 7.3 %shard_map.114 = (f32[128,2048]{1,0:T(8,128)S(1)}, f32[32,768]{1,0:T(8,128)S(1)}, f32[32,2048]{1,0:T(8,128)S(1)}) custom-call(s32[3]{0:T(128)S(1)} %pad_add_fusion.refs_0_, bf16[64,2048]{1,0:T(8,128)(2,1)S(1)} %collective-permute-done.5.refs_1_, bf16[64,2048]{1,0:T(8,128)(2,1)S(1)} %collective-permute-done.6.refs_2_, ...), custom_call_target="tpu_custom_call" | custom-call | flops 2013265920 | bytes 11059200 | tf_op jit(solution)/shard_map/pallas_call | solution.py:210
  58.9 0.4 collective-permute-start.15
  59.3 1.7 %collective-permute-start.16 = (bf16[32,2048]{1,0:T(8,128)(2,1)S(1)}, bf16[32,2048]{1,0:T(8,128)(2,1)S(1)}, u32[]{:S(2)}, u32[]{:S(2)}) collective-permute-start(bf16[32,2048]{1,0:T(8,128)(2,1)S(1)} %slice.73), channel_id=1, source_target_pairs={{4,0},{8,4},{12,8},{14,12},{10,14},{6,10},{2,6},{0,2},{5,1},{9,5},... | collective-permute-start | bytes 393224 | tf_op jit(solution)/shard_map/ppermute | solution.py:320
  61.0 0.4 collective-permute-done.11.refs_3_
  61.7 1.6 %collective-permute-start.13 = (bf16[32,2176]{1,0:T(8,128)(2,1)S(1)}, bf16[32,2176]{1,0:T(8,128)(2,1)S(1)}, u32[]{:S(2)}, u32[]{:S(2)}) collective-permute-start(bf16[32,2176]{1,0:T(8,128)(2,1)S(1)} %slice.70), channel_id=1, source_target_pairs={{0,4},{4,8},{8,12},{12,14},{14,10},{10,6},{6,2},{2,0},{1,5},{5,9},... | collective-permute-start | bytes 417800 | tf_op jit(solution)/shard_map/ppermute | solution.py:319
  63.3 0.5 collective-permute-start.14
  63.8 0.5 collective-permute-done.15.refs_1_
  64.7 5.2 %shard_map.115 = (f32[64,768]{1,0:T(8,128)S(1)}, f32[64,768]{1,0:T(8,128)S(1)}, bf16[64,768]{1,0:T(8,128)(2,1)S(1)}, f32[64,32]{1,0:T(8,128)S(1)}) custom-call(s32[3]{0:T(128)S(1)} %pad_add_fusion.refs_0_, bf16[32,2048]{1,0:T(8,128)(2,1)S(1)} %collective-permute-done.15.refs_1_, bf16[32,2048]{1,0:T(8,128)(2,1)S(1)} %collective-permute-done.16.refs_2_, ...), custom_call_target="tpu_custom_call" | custom-call | flops 402653184 | bytes 9748480 | tf_op jit(solution)/shard_map/pallas_call | solution.py:210
  69.9 6.4 %shard_map.116 = (f32[64,2048]{1,0:T(8,128)S(1)}, bf16[64,32]{1,0:T(8,128)(2,1)S(1)}, bf16[64,32]{1,0:T(8,128)(2,1)S(1)}) custom-call(s32[3]{0:T(128)S(1)} %pad_add_fusion.refs_0_, bf16[32,2176]{1,0:T(8,128)(2,1)S(1)} %collective-permute-done.13.refs_1_, bf16[32,2176]{1,0:T(8,128)(2,1)S(1)} %collective-permute-done.14.refs_2_, ...), custom_call_target="tpu_custom_call" | custom-call | flops 603979776 | bytes 10297344 | tf_op jit(solution)/shard_map/pallas_call | solution.py:210
  76.4 1.5 %collective-permute-start.17 = (bf16[32,2048]{1,0:T(8,128)(2,1)S(1)}, bf16[32,2048]{1,0:T(8,128)(2,1)S(1)}, u32[]{:S(2)}, u32[]{:S(2)}) collective-permute-start(bf16[32,2048]{1,0:T(8,128)(2,1)S(1)} %get-tuple-element.107), channel_id=1, source_target_pairs={{4,0},{8,4},{12,8},{14,12},{10,14},{6,10},{2,6},{0,2},{5,1},{9,5},... | collective-permute-start | bytes 393224 | tf_op jit(solution)/shard_map/ppermute | solution.py:341
  77.9 0.6 collective-permute-start.21
  78.5 7.3 %shard_map.117 = (f32[128,2048]{1,0:T(8,128)S(1)}, f32[32,768]{1,0:T(8,128)S(1)}, f32[32,2048]{1,0:T(8,128)S(1)}) custom-call(s32[3]{0:T(128)S(1)} %pad_add_fusion.refs_0_, bf16[64,2048]{1,0:T(8,128)(2,1)S(1)} %collective-permute-done.9.refs_1_, bf16[64,2048]{1,0:T(8,128)(2,1)S(1)} %collective-permute-done.10.refs_2_, ...), custom_call_target="tpu_custom_call" | custom-call | flops 2013265920 | bytes 11059200 | tf_op jit(solution)/shard_map/pallas_call | solution.py:210
  86.0 1.6 %collective-permute-start.22 = (bf16[64,2048]{1,0:T(8,128)(2,1)S(1)}, bf16[64,2048]{1,0:T(8,128)(2,1)S(1)}, u32[]{:S(2)}, u32[]{:S(2)}) collective-permute-start(bf16[64,2048]{1,0:T(8,128)(2,1)S(1)} %pad_maximum_fusion.1), channel_id=1, source_target_pairs={{0,4},{4,8},{8,12},{12,14},{14,10},{10,6},{6,2},{2,0},{1,5},{5,9},... | collective-permute-start | bytes 786440 | tf_op jit(solution)/shard_map/ppermute | solution.py:367
  87.6 0.6 collective-permute-start.18
  88.1 0.8 shard_map.118
  88.9 3.6 %collective-permute-done.22 = bf16[64,2048]{1,0:T(8,128)(2,1)S(1)} collective-permute-done((bf16[64,2048]{1,0:T(8,128)(2,1)S(1)}, bf16[64,2048]{1,0:T(8,128)(2,1)S(1)}, u32[]{:S(2)}, u32[]{:S(2)}) %collective-permute-start.22) | collective-permute-done | bytes 262176 | tf_op jit(solution)/shard_map/ppermute | solution.py:367
  92.5 3.5 %collective-permute-done.18 = bf16[64,2048]{1,0:T(8,128)(2,1)S(1)} collective-permute-done((bf16[64,2048]{1,0:T(8,128)(2,1)S(1)}, bf16[64,2048]{1,0:T(8,128)(2,1)S(1)}, u32[]{:S(2)}, u32[]{:S(2)}) %collective-permute-start.18) | collective-permute-done | bytes 262176 | tf_op jit(solution)/shard_map/ppermute | solution.py:366
  96.1 0.6 collective-permute-start.19
  96.7 1.5 %collective-permute-start.23 = (bf16[64,2048]{1,0:T(8,128)(2,1)S(1)}, bf16[64,2048]{1,0:T(8,128)(2,1)S(1)}, u32[]{:S(2)}, u32[]{:S(2)}) collective-permute-start(bf16[64,2048]{1,0:T(8,128)(2,1)S(1)} %get-tuple-element.102), channel_id=1, source_target_pairs={{0,4},{4,8},{8,12},{12,14},{14,10},{10,6},{6,2},{2,0},{1,5},{5,9},... | collective-permute-start | bytes 786440 | tf_op jit(solution)/shard_map/ppermute | solution.py:367
  98.3 0.9 maximum_bitcast_fusion
  99.2 5.8 %collective-permute-done.19 = bf16[64,2048]{1,0:T(8,128)(2,1)S(1)} collective-permute-done((bf16[64,2048]{1,0:T(8,128)(2,1)S(1)}, bf16[64,2048]{1,0:T(8,128)(2,1)S(1)}, u32[]{:S(2)}, u32[]{:S(2)}) %collective-permute-start.19) | collective-permute-done | bytes 262176 | tf_op jit(solution)/shard_map/ppermute | solution.py:366
  105.3 1.5 %collective-permute-start.20 = (bf16[64,2048]{1,0:T(8,128)(2,1)S(1)}, bf16[64,2048]{1,0:T(8,128)(2,1)S(1)}, u32[]{:S(2)}, u32[]{:S(2)}) collective-permute-start(bf16[64,2048]{1,0:T(8,128)(2,1)S(1)} %get-tuple-element.99), channel_id=1, source_target_pairs={{4,0},{8,4},{12,8},{14,12},{10,14},{6,10},{2,6},{0,2},{5,1},{9,5},... | collective-permute-start | bytes 786440 | tf_op jit(solution)/shard_map/ppermute | solution.py:366
  106.8 0.6 collective-permute-start.24
  107.4 1.4 %slice.90 = f32[32,192]{1,0:T(8,128)} slice(f32[32,1216]{1,0:T(8,128)} %bitcast.23), slice={[0:32], [0:192]} | slice | bytes 49152 | tf_op jit(solution)/shard_map/slice | solution.py:386
  108.8 1.7 %slice.91 = f32[32,1024]{1,0:T(8,128)} slice(f32[32,1216]{1,0:T(8,128)} %bitcast.24), slice={[0:32], [192:1216]} | slice | bytes 262144 | tf_op jit(solution)/shard_map/slice | solution.py:387
  110.5 1.3 %collective-permute-done.20 = bf16[64,2048]{1,0:T(8,128)(2,1)S(1)} collective-permute-done((bf16[64,2048]{1,0:T(8,128)(2,1)S(1)}, bf16[64,2048]{1,0:T(8,128)(2,1)S(1)}, u32[]{:S(2)}, u32[]{:S(2)}) %collective-permute-start.20) | collective-permute-done | bytes 262176 | tf_op jit(solution)/shard_map/ppermute | solution.py:366
  111.8 1.4 %collective-permute-done.24 = bf16[64,2048]{1,0:T(8,128)(2,1)S(1)} collective-permute-done((bf16[64,2048]{1,0:T(8,128)(2,1)S(1)}, bf16[64,2048]{1,0:T(8,128)(2,1)S(1)}, u32[]{:S(2)}, u32[]{:S(2)}) %collective-permute-start.24) | collective-permute-done | bytes 262176 | tf_op jit(solution)/shard_map/ppermute | solution.py:367
  113.2 0.8 add_convert_fusion
  (53 shorter events, 2.3 us)
Async XLA Ops:
  7.2 100.2 %reduce-scatter.2.cloned.1.call-start = ((), (), s32[]{:S(2)}) async-start(), calls=%async_computation.1 | async-start | bytes 491520 | tf_op jit(solution)/shard_map/reduce_scatter | solution.py:385
  8.8 1.4 %copy-start.1 = (bf16[2,1024,384]{2,1,0:T(8,128)(2,1)S(1)}, bf16[2,1024,384]{2,1,0:T(8,128)(2,1)}, u32[]{:S(2)}) copy-start(bf16[2,1024,384]{2,1,0:T(8,128)(2,1)} %refs_0_.1) | copy-start | bytes 4718596
  10.2 1.4 %copy-start.2 = (bf16[2,1024,384]{2,1,0:T(8,128)(2,1)S(1)}, bf16[2,1024,384]{2,1,0:T(8,128)(2,1)}, u32[]{:S(2)}) copy-start(bf16[2,1024,384]{2,1,0:T(8,128)(2,1)} %refs_1_.1) | copy-start | bytes 4718596
  11.6 1.4 %copy-start.3 = (bf16[2,1024,384]{2,1,0:T(8,128)(2,1)S(1)}, bf16[2,1024,384]{2,1,0:T(8,128)(2,1)}, u32[]{:S(2)}) copy-start(bf16[2,1024,384]{2,1,0:T(8,128)(2,1)} %refs_2_.1) | copy-start | bytes 4718596
  13.0 0.9 copy-start.4
  13.9 0.7 copy-start.6
  14.7 6.1 %copy-start.5 = (bf16[64,2048]{1,0:T(8,128)(2,1)S(1)}, bf16[64,2048]{1,0:T(8,128)(2,1)}, u32[]{:S(2)}) copy-start(bf16[64,2048]{1,0:T(8,128)(2,1)} %refs_3_.3) | copy-start | bytes 786436
  14.7 24.4 %copy-start = (bf16[2,16,2048]{2,1,0:T(8,128)(2,1)S(1)}, bf16[2,16,2048]{2,1,0:T(8,128)(2,1)}, u32[]{:S(2)}) copy-start(bf16[2,16,2048]{2,1,0:T(8,128)(2,1)} %param.17) | copy-start | bytes 393220
  17.5 21.5 %collective-permute-start.4 = (bf16[1024,2304]{1,0:T(8,128)(2,1)}, bf16[1024,2304]{1,0:T(8,128)(2,1)}, u32[]{:S(2)}, u32[]{:S(2)}) collective-permute-start(bf16[1024,2304]{1,0:T(8,128)(2,1)} %get-tuple-element.53.refs_9_.refs_7_.refs_4_.refs_8_), channel_id=1, source_target_pairs={{0,1},{1,0},{2,3},{3,2},{4,5},{5,4},{6,7},{7,6},{8,9},{9,8},{10,11... | collective-permute-start | bytes 14155784 | tf_op jit(solution)/shard_map/ppermute | solution.py:267
  18.1 18.9 %collective-permute-start.3 = (bf16[64,2176]{1,0:T(8,128)(2,1)S(1)}, bf16[64,2176]{1,0:T(8,128)(2,1)S(1)}, u32[]{:S(2)}, u32[]{:S(2)}) collective-permute-start(bf16[64,2176]{1,0:T(8,128)(2,1)S(1)} %get-tuple-element.51.refs_6_), channel_id=1, source_target_pairs={{4,0},{8,4},{12,8},{14,12},{10,14},{6,10},{2,6},{0,2},{5,1},{9,5},... | collective-permute-start | bytes 835592 | tf_op jit(solution)/shard_map/ppermute | solution.py:312
  20.6 18.0 %collective-permute-start.2 = (bf16[64,2176]{1,0:T(8,128)(2,1)S(1)}, bf16[64,2176]{1,0:T(8,128)(2,1)S(1)}, u32[]{:S(2)}, u32[]{:S(2)}) collective-permute-start(bf16[64,2176]{1,0:T(8,128)(2,1)S(1)} %get-tuple-element.51.refs_6_), channel_id=1, source_target_pairs={{0,4},{4,8},{8,12},{12,14},{14,10},{10,6},{6,2},{2,0},{1,5},{5,9},... | collective-permute-start | bytes 835592 | tf_op jit(solution)/shard_map/ppermute | solution.py:311
  20.8 14.2 %collective-permute-start = (bf16[64,2048]{1,0:T(8,128)(2,1)S(1)}, bf16[64,2048]{1,0:T(8,128)(2,1)S(1)}, u32[]{:S(2)}, u32[]{:S(2)}) collective-permute-start(bf16[64,2048]{1,0:T(8,128)(2,1)S(1)} %copy-done.5), channel_id=1, source_target_pairs={{0,4},{4,8},{8,12},{12,14},{14,10},{10,6},{6,2},{2,0},{1,5},{5,9},... | collective-permute-start | bytes 786440 | tf_op jit(solution)/shard_map/ppermute | solution.py:311
  22.7 12.6 %collective-permute-start.1 = (bf16[64,2048]{1,0:T(8,128)(2,1)S(1)}, bf16[64,2048]{1,0:T(8,128)(2,1)S(1)}, u32[]{:S(2)}, u32[]{:S(2)}) collective-permute-start(bf16[64,2048]{1,0:T(8,128)(2,1)S(1)} %copy-done.5), channel_id=1, source_target_pairs={{4,0},{8,4},{12,8},{14,12},{10,14},{6,10},{2,6},{0,2},{5,1},{9,5},... | collective-permute-start | bytes 786440 | tf_op jit(solution)/shard_map/ppermute | solution.py:312
  35.0 12.5 %collective-permute-start.5 = (bf16[64,2048]{1,0:T(8,128)(2,1)S(1)}, bf16[64,2048]{1,0:T(8,128)(2,1)S(1)}, u32[]{:S(2)}, u32[]{:S(2)}) collective-permute-start(bf16[64,2048]{1,0:T(8,128)(2,1)S(1)} %collective-permute-done.refs_1_), channel_id=1, source_target_pairs={{0,4},{4,8},{8,12},{12,14},{14,10},{10,6},{6,2},{2,0},{1,5},{5,9},... | collective-permute-start | bytes 786440 | tf_op jit(solution)/shard_map/ppermute | solution.py:311
  35.3 12.5 %collective-permute-start.6 = (bf16[64,2048]{1,0:T(8,128)(2,1)S(1)}, bf16[64,2048]{1,0:T(8,128)(2,1)S(1)}, u32[]{:S(2)}, u32[]{:S(2)}) collective-permute-start(bf16[64,2048]{1,0:T(8,128)(2,1)S(1)} %collective-permute-done.1.refs_2_), channel_id=1, source_target_pairs={{4,0},{8,4},{12,8},{14,12},{10,14},{6,10},{2,6},{0,2},{5,1},{9,5},... | collective-permute-start | bytes 786440 | tf_op jit(solution)/shard_map/ppermute | solution.py:312
  37.0 12.9 %collective-permute-start.8 = (bf16[64,2176]{1,0:T(8,128)(2,1)S(1)}, bf16[64,2176]{1,0:T(8,128)(2,1)S(1)}, u32[]{:S(2)}, u32[]{:S(2)}) collective-permute-start(bf16[64,2176]{1,0:T(8,128)(2,1)S(1)} %collective-permute-done.3.refs_5_), channel_id=1, source_target_pairs={{4,0},{8,4},{12,8},{14,12},{10,14},{6,10},{2,6},{0,2},{5,1},{9,5},... | collective-permute-start | bytes 835592 | tf_op jit(solution)/shard_map/ppermute | solution.py:312
  38.6 11.0 %collective-permute-start.7 = (bf16[64,2176]{1,0:T(8,128)(2,1)S(1)}, bf16[64,2176]{1,0:T(8,128)(2,1)S(1)}, u32[]{:S(2)}, u32[]{:S(2)}) collective-permute-start(bf16[64,2176]{1,0:T(8,128)(2,1)S(1)} %collective-permute-done.2.refs_4_), channel_id=1, source_target_pairs={{0,4},{4,8},{8,12},{12,14},{14,10},{10,6},{6,2},{2,0},{1,5},{5,9},... | collective-permute-start | bytes 835592 | tf_op jit(solution)/shard_map/ppermute | solution.py:311
  47.5 11.4 %collective-permute-start.9 = (bf16[64,2048]{1,0:T(8,128)(2,1)S(1)}, bf16[64,2048]{1,0:T(8,128)(2,1)S(1)}, u32[]{:S(2)}, u32[]{:S(2)}) collective-permute-start(bf16[64,2048]{1,0:T(8,128)(2,1)S(1)} %collective-permute-done.5.refs_1_), channel_id=1, source_target_pairs={{0,4},{4,8},{8,12},{12,14},{14,10},{10,6},{6,2},{2,0},{1,5},{5,9},... | collective-permute-start | bytes 786440 | tf_op jit(solution)/shard_map/ppermute | solution.py:311
  47.9 11.0 %collective-permute-start.10 = (bf16[64,2048]{1,0:T(8,128)(2,1)S(1)}, bf16[64,2048]{1,0:T(8,128)(2,1)S(1)}, u32[]{:S(2)}, u32[]{:S(2)}) collective-permute-start(bf16[64,2048]{1,0:T(8,128)(2,1)S(1)} %collective-permute-done.6.refs_2_), channel_id=1, source_target_pairs={{4,0},{8,4},{12,8},{14,12},{10,14},{6,10},{2,6},{0,2},{5,1},{9,5},... | collective-permute-start | bytes 786440 | tf_op jit(solution)/shard_map/ppermute | solution.py:312
  49.5 11.8 %collective-permute-start.11 = (bf16[64,2176]{1,0:T(8,128)(2,1)S(1)}, bf16[64,2176]{1,0:T(8,128)(2,1)S(1)}, u32[]{:S(2)}, u32[]{:S(2)}) collective-permute-start(bf16[64,2176]{1,0:T(8,128)(2,1)S(1)} %collective-permute-done.7.refs_3_), channel_id=1, source_target_pairs={{0,4},{4,8},{8,12},{12,14},{14,10},{10,6},{6,2},{2,0},{1,5},{5,9},... | collective-permute-start | bytes 835592 | tf_op jit(solution)/shard_map/ppermute | solution.py:311
  49.9 11.8 %collective-permute-start.12 = (bf16[64,2176]{1,0:T(8,128)(2,1)S(1)}, bf16[64,2176]{1,0:T(8,128)(2,1)S(1)}, u32[]{:S(2)}, u32[]{:S(2)}) collective-permute-start(bf16[64,2176]{1,0:T(8,128)(2,1)S(1)} %collective-permute-done.8.refs_4_), channel_id=1, source_target_pairs={{4,0},{8,4},{12,8},{14,12},{10,14},{6,10},{2,6},{0,2},{5,1},{9,5},... | collective-permute-start | bytes 835592 | tf_op jit(solution)/shard_map/ppermute | solution.py:312
  58.9 5.4 %collective-permute-start.15 = (bf16[32,2048]{1,0:T(8,128)(2,1)S(1)}, bf16[32,2048]{1,0:T(8,128)(2,1)S(1)}, u32[]{:S(2)}, u32[]{:S(2)}) collective-permute-start(bf16[32,2048]{1,0:T(8,128)(2,1)S(1)} %slice.72), channel_id=1, source_target_pairs={{0,4},{4,8},{8,12},{12,14},{14,10},{10,6},{6,2},{2,0},{1,5},{5,9},... | collective-permute-start | bytes 393224 | tf_op jit(solution)/shard_map/ppermute | solution.py:319
  59.3 5.3 %collective-permute-start.16 = (bf16[32,2048]{1,0:T(8,128)(2,1)S(1)}, bf16[32,2048]{1,0:T(8,128)(2,1)S(1)}, u32[]{:S(2)}, u32[]{:S(2)}) collective-permute-start(bf16[32,2048]{1,0:T(8,128)(2,1)S(1)} %slice.73), channel_id=1, source_target_pairs={{4,0},{8,4},{12,8},{14,12},{10,14},{6,10},{2,6},{0,2},{5,1},{9,5},... | collective-permute-start | bytes 393224 | tf_op jit(solution)/shard_map/ppermute | solution.py:320
  61.7 8.1 %collective-permute-start.13 = (bf16[32,2176]{1,0:T(8,128)(2,1)S(1)}, bf16[32,2176]{1,0:T(8,128)(2,1)S(1)}, u32[]{:S(2)}, u32[]{:S(2)}) collective-permute-start(bf16[32,2176]{1,0:T(8,128)(2,1)S(1)} %slice.70), channel_id=1, source_target_pairs={{0,4},{4,8},{8,12},{12,14},{14,10},{10,6},{6,2},{2,0},{1,5},{5,9},... | collective-permute-start | bytes 417800 | tf_op jit(solution)/shard_map/ppermute | solution.py:319
  63.3 6.5 %collective-permute-start.14 = (bf16[32,2176]{1,0:T(8,128)(2,1)S(1)}, bf16[32,2176]{1,0:T(8,128)(2,1)S(1)}, u32[]{:S(2)}, u32[]{:S(2)}) collective-permute-start(bf16[32,2176]{1,0:T(8,128)(2,1)S(1)} %slice.71), channel_id=1, source_target_pairs={{4,0},{8,4},{12,8},{14,12},{10,14},{6,10},{2,6},{0,2},{5,1},{9,5},... | collective-permute-start | bytes 417800 | tf_op jit(solution)/shard_map/ppermute | solution.py:320
  76.4 9.5 %collective-permute-start.17 = (bf16[32,2048]{1,0:T(8,128)(2,1)S(1)}, bf16[32,2048]{1,0:T(8,128)(2,1)S(1)}, u32[]{:S(2)}, u32[]{:S(2)}) collective-permute-start(bf16[32,2048]{1,0:T(8,128)(2,1)S(1)} %get-tuple-element.107), channel_id=1, source_target_pairs={{4,0},{8,4},{12,8},{14,12},{10,14},{6,10},{2,6},{0,2},{5,1},{9,5},... | collective-permute-start | bytes 393224 | tf_op jit(solution)/shard_map/ppermute | solution.py:341
  77.9 8.0 %collective-permute-start.21 = (bf16[32,2048]{1,0:T(8,128)(2,1)S(1)}, bf16[32,2048]{1,0:T(8,128)(2,1)S(1)}, u32[]{:S(2)}, u32[]{:S(2)}) collective-permute-start(bf16[32,2048]{1,0:T(8,128)(2,1)S(1)} %get-tuple-element.108), channel_id=1, source_target_pairs={{0,4},{4,8},{8,12},{12,14},{14,10},{10,6},{6,2},{2,0},{1,5},{5,9},... | collective-permute-start | bytes 393224 | tf_op jit(solution)/shard_map/ppermute | solution.py:342
  86.0 6.5 %collective-permute-start.22 = (bf16[64,2048]{1,0:T(8,128)(2,1)S(1)}, bf16[64,2048]{1,0:T(8,128)(2,1)S(1)}, u32[]{:S(2)}, u32[]{:S(2)}) collective-permute-start(bf16[64,2048]{1,0:T(8,128)(2,1)S(1)} %pad_maximum_fusion.1), channel_id=1, source_target_pairs={{0,4},{4,8},{8,12},{12,14},{14,10},{10,6},{6,2},{2,0},{1,5},{5,9},... | collective-permute-start | bytes 786440 | tf_op jit(solution)/shard_map/ppermute | solution.py:367
  87.6 8.4 %collective-permute-start.18 = (bf16[64,2048]{1,0:T(8,128)(2,1)S(1)}, bf16[64,2048]{1,0:T(8,128)(2,1)S(1)}, u32[]{:S(2)}, u32[]{:S(2)}) collective-permute-start(bf16[64,2048]{1,0:T(8,128)(2,1)S(1)} %pad_maximum_fusion), channel_id=1, source_target_pairs={{4,0},{8,4},{12,8},{14,12},{10,14},{6,10},{2,6},{0,2},{5,1},{9,5},... | collective-permute-start | bytes 786440 | tf_op jit(solution)/shard_map/ppermute | solution.py:366
  96.1 8.9 %collective-permute-start.19 = (bf16[64,2048]{1,0:T(8,128)(2,1)S(1)}, bf16[64,2048]{1,0:T(8,128)(2,1)S(1)}, u32[]{:S(2)}, u32[]{:S(2)}) collective-permute-start(bf16[64,2048]{1,0:T(8,128)(2,1)S(1)} %get-tuple-element.101), channel_id=1, source_target_pairs={{4,0},{8,4},{12,8},{14,12},{10,14},{6,10},{2,6},{0,2},{5,1},{9,5},... | collective-permute-start | bytes 786440 | tf_op jit(solution)/shard_map/ppermute | solution.py:366
  96.7 8.5 %collective-permute-start.23 = (bf16[64,2048]{1,0:T(8,128)(2,1)S(1)}, bf16[64,2048]{1,0:T(8,128)(2,1)S(1)}, u32[]{:S(2)}, u32[]{:S(2)}) collective-permute-start(bf16[64,2048]{1,0:T(8,128)(2,1)S(1)} %get-tuple-element.102), channel_id=1, source_target_pairs={{0,4},{4,8},{8,12},{12,14},{14,10},{10,6},{6,2},{2,0},{1,5},{5,9},... | collective-permute-start | bytes 786440 | tf_op jit(solution)/shard_map/ppermute | solution.py:367
  105.3 6.4 %collective-permute-start.20 = (bf16[64,2048]{1,0:T(8,128)(2,1)S(1)}, bf16[64,2048]{1,0:T(8,128)(2,1)S(1)}, u32[]{:S(2)}, u32[]{:S(2)}) collective-permute-start(bf16[64,2048]{1,0:T(8,128)(2,1)S(1)} %get-tuple-element.99), channel_id=1, source_target_pairs={{4,0},{8,4},{12,8},{14,12},{10,14},{6,10},{2,6},{0,2},{5,1},{9,5},... | collective-permute-start | bytes 786440 | tf_op jit(solution)/shard_map/ppermute | solution.py:366
  106.8 6.4 %collective-permute-start.24 = (bf16[64,2048]{1,0:T(8,128)(2,1)S(1)}, bf16[64,2048]{1,0:T(8,128)(2,1)S(1)}, u32[]{:S(2)}, u32[]{:S(2)}) collective-permute-start(bf16[64,2048]{1,0:T(8,128)(2,1)S(1)} %get-tuple-element.100), channel_id=1, source_target_pairs={{0,4},{4,8},{8,12},{12,14},{14,10},{10,6},{6,2},{2,0},{1,5},{5,9},... | collective-permute-start | bytes 786440 | tf_op jit(solution)/shard_map/ppermute | solution.py:367
Sparse Core Ops, SparseCore 0:
  99.3 7.9 reduce-scatter.1

commit v4 on v3

--- a/solution.py
+++ b/solution.py
@@ -46,17 +46,17 @@
         self.wide = experts * hidden_width
         self.ranks = experts * rank
 
-    def spans(self, position_ref):
+    def spans(self):
         if self.parts == 1:
             return [slice(0, self.model_width)]
+        core = lax.axis_index("dp")
         return [
-            pl.ds(pl.multiple_of(position_ref[part], self.depth), self.depth)
-            for part in range(self.parts)
+            pl.ds(pl.multiple_of(at * self.depth, self.depth), self.depth) for at in (core, 1 - core)
         ]
 
-    def forward(self, position_ref, token_refs, factor_in_ref, weight_refs):
+    def forward(self, token_refs, factor_in_ref, weight_refs):
         gate_pre, up_pre = 0.0, 0.0
-        for span, weight in zip(self.spans(position_ref), weight_refs):
+        for span, weight in zip(self.spans(), weight_refs):
             tokens_in = stacked(token_refs, span)
             gate_pre += matmul(tokens_in, weight[:, : self.wide])
             up_pre += matmul(tokens_in, weight[:, self.wide : 2 * self.wide])
@@ -67,10 +67,10 @@
         low_rank = matmul_bt(hidden, factor_in_ref[...])
         return activation, up_pre * derivative, hidden, low_rank
 
-    def scales(self, position_ref, grad_refs):
+    def scales(self, grad_refs):
         columns = stacked(grad_refs, slice(self.model_width, None)).astype(f32)
         lane = lax.broadcasted_iota(jnp.int32, columns.shape, 1)
-        first = position_ref[self.parts]
+        first = lax.axis_index("expert") * self.experts
         return [
             jnp.sum(jnp.where(lane == first + j, columns, 0.0), axis=1, keepdims=True)
             for j in range(self.experts)
@@ -85,11 +85,11 @@
         return out
 
     def backward(
-        self, position_ref, grad_refs, activation, slope, factor_in_ref, factor_out_ref, weight_refs, rows_ref
+        self, grad_refs, activation, slope, factor_in_ref, factor_out_ref, weight_refs, rows_ref
     ):
-        scales = self.scales(position_ref, grad_refs)
+        scales = self.scales(grad_refs)
         adapter_back, grad_down = 0.0, 0.0
-        spans = self.spans(position_ref)
+        spans = self.spans()
         for span, weight in zip(spans, weight_refs):
             grad_in = stacked(grad_refs, span)
             adapter_back += matmul_bt(grad_in, factor_out_ref[:, span])
@@ -116,16 +116,15 @@
 
 
 def whole_kernel(plan, pieces, *refs):
-    position_ref, refs = refs[0], refs[1:]
     token_refs, grad_refs, refs = refs[:pieces], refs[pieces : 2 * pieces], refs[2 * pieces :]
     factor_in_ref, factor_out_ref, refs = refs[0], refs[1], refs[2:]
     weight_refs, refs = refs[: plan.parts], refs[plan.parts :]
     total_refs, rows_ref, out_refs = refs[:2], refs[2], refs[3:]
     activation, slope, hidden, low_rank = plan.forward(
-        position_ref, token_refs, factor_in_ref, weight_refs
+        token_refs, factor_in_ref, weight_refs
     )
     rank_scale, back_scaled = plan.backward(
-        position_ref, grad_refs, activation, slope, factor_in_ref, factor_out_ref, weight_refs, rows_ref
+        grad_refs, activation, slope, factor_in_ref, factor_out_ref, weight_refs, rows_ref
     )
     low_scaled = (rank_scale * low_rank).astype(bf16)
     plan.adapters(grad_refs, hidden, low_scaled, back_scaled, total_refs, out_refs)
@@ -149,13 +148,13 @@
     for copy in copies:
         copy.start()
     rows, lanes = grads_ref.shape[0], grads_ref.shape[1] - plan.model_width
-    lane = lax.broadcasted_iota(jnp.int32, (rows, lanes), 1)
+    expert_at = lax.broadcasted_iota(jnp.int32, (lanes, rows), 0)
     ids, route = ids_ref[...], route_ref[...].astype(f32)
-    dense = jnp.zeros((rows, lanes), f32)
-    for k in range(ids.shape[1]):
-        dense = jnp.where(ids[:, k : k + 1] == lane, route[:, k : k + 1], dense)
+    dense = jnp.zeros((lanes, rows), f32)
+    for k in range(ids.shape[0]):
+        dense = jnp.where(ids[k : k + 1, :] == expert_at, route[k : k + 1, :], dense)
     grads_ref[:, : plan.model_width] = out_grad_ref[...]
-    grads_ref[:, plan.model_width :] = dense.astype(bf16)
+    grads_ref[:, plan.model_width :] = dense.T.astype(bf16)
     factor_in_ref[...] = jnp.zeros(factor_in_ref.shape, bf16)
     for expert in range(plan.experts):
         factor_in_ref[
@@ -167,25 +166,22 @@
 
 
 def forward_kernel(plan, pieces, *refs):
-    position_ref, refs = refs[0], refs[1:]
     token_refs, refs = refs[:pieces], refs[pieces:]
     factor_in_ref, refs = refs[0], refs[1:]
     weight_refs, out_refs = refs[: plan.parts], refs[plan.parts :]
     for out, value in zip(
-        out_refs, plan.forward(position_ref, token_refs, factor_in_ref, weight_refs)
+        out_refs, plan.forward(token_refs, factor_in_ref, weight_refs)
     ):
         out[...] = value
 
 
 def backward_kernel(plan, pieces, *refs):
-    position_ref, refs = refs[0], refs[1:]
     grad_refs, refs = refs[:pieces], refs[pieces:]
     activation_ref, slope_ref, low_rank_ref, refs = refs[0], refs[1], refs[2], refs[3:]
     factor_in_ref, factor_out_ref, refs = refs[0], refs[1], refs[2:]
     weight_refs, refs = refs[: plan.parts], refs[plan.parts :]
     rows_ref, low_scaled_ref, back_scaled_ref = refs
     rank_scale, back_scaled = plan.backward(
-        position_ref,
         grad_refs,
         activation_ref[...],
         slope_ref[...],
@@ -199,19 +195,46 @@
 
 
 def adapters_kernel(plan, pieces, *refs):
-    grad_refs, refs = refs[1 : 1 + pieces], refs[1 + pieces :]
+    grad_refs, refs = refs[:pieces], refs[pieces:]
     hidden_ref, low_scaled_ref, back_scaled_ref, refs = refs[0], refs[1], refs[2], refs[3:]
     plan.adapters(
         grad_refs, hidden_ref[...], low_scaled_ref[...], back_scaled_ref[...], refs[:2], refs[2:]
     )
 
 
-def call(kernel, plan, pieces, position, operands, outs, flops):
+def add_kernel(row_count, span, *refs):
+    rows_ref, refs = refs[0], refs[1:]
+    ways = len(refs) // 2
+    for way in range(ways):
+        rows = rows_ref[way * row_count : (way + 1) * row_count, span]
+        refs[ways + way][...] = (rows + refs[way][...].astype(f32)).astype(bf16)
+
+
+def add_sums(rows, span, incoming):
+    shape = incoming[0].shape
+    return pl.pallas_call(
+        functools.partial(add_kernel, shape[0], span),
+        out_shape=tuple(jax.ShapeDtypeStruct(shape, bf16) for _ in incoming),
+        in_specs=[pl.BlockSpec(memory_space=pltpu.VMEM)] * (1 + len(incoming)),
+        out_specs=(pl.BlockSpec(memory_space=pltpu.VMEM),) * len(incoming),
+        compiler_params=pltpu.CompilerParams(vmem_limit_bytes=16 * 1024 * 1024),
+    )(rows, *incoming)
+
+
+def last_kernel(first_row, spans, *refs):
+    rows_ref, out_ref = refs[0], refs[-1]
+    for at, span in enumerate(spans):
+        total = rows_ref[first_row : first_row + out_ref.shape[0], span]
+        for incoming in refs[1 + 2 * at : 3 + 2 * at]:
+            total = total + incoming[...].astype(f32)
+        out_ref[:, span] = total.astype(bf16)
+
+
+def call(kernel, plan, pieces, operands, outs, flops):
     return pl.pallas_call(
         functools.partial(kernel, plan, pieces),
         out_shape=tuple(jax.ShapeDtypeStruct(shape, dtype) for shape, dtype in outs),
-        in_specs=[pl.BlockSpec(memory_space=pltpu.SMEM)]
-        + [pl.BlockSpec(memory_space=pltpu.VMEM)] * len(operands),
+        in_specs=[pl.BlockSpec(memory_space=pltpu.VMEM)] * len(operands),
         out_specs=(pl.BlockSpec(memory_space=pltpu.VMEM),) * len(outs),
         compiler_params=pltpu.CompilerParams(vmem_limit_bytes=16 * 1024 * 1024),
         cost_estimate=pl.CostEstimate(
@@ -219,7 +242,7 @@
             bytes_accessed=sum(op.size * op.dtype.itemsize for op in operands),
             transcendentals=0,
         ),
-    )(position, *operands)
+    )(*operands)
 
 
 def per_device(
@@ -243,8 +266,7 @@
     order = ring_order(peer_count, snake)
     forward = [(order[i], order[(i + 1) % peer_count]) for i in range(peer_count)]
     backward = [(b, a) for a, b in forward]
-    me = lax.axis_index("expert")
-    dp_me = lax.axis_index("dp")
+    swap = [(0, 1), (1, 0)]
     parts = 2 if dp_count == 2 else 1
     plan = Plan(parts, depth, model_width, hidden_width, rank, local_count)
     wide, ranks = plan.wide, plan.ranks
@@ -261,14 +283,13 @@
         out_specs=(pl.BlockSpec(memory_space=pltpu.VMEM),) * 3,
         scratch_shapes=[pltpu.SemaphoreType.DMA((3 * local_count,))],
         compiler_params=pltpu.CompilerParams(vmem_limit_bytes=16 * 1024 * 1024),
-    )(gate_weight, up_weight, down_weight, out_grad, expert_ids, route_weight, adapter_in)
-    first_expert = me * local_count
-    if parts == 2:
-        weights = [mine, lax.ppermute(mine, "dp", [(0, 1), (1, 0)])]
-        position = jnp.stack([dp_me * depth, (1 - dp_me) * depth, first_expert]).astype(jnp.int32)
-    else:
-        weights = [lax.all_gather(mine, "dp", axis=0, tiled=True)]
-        position = jnp.stack([0 * first_expert, first_expert]).astype(jnp.int32)
+    )(
+        *(pltpu.with_memory_space_constraint(w, pltpu.HBM) for w in (gate_weight, up_weight, down_weight)),
+        out_grad,
+        expert_ids.T,
+        route_weight.T,
+        adapter_in,
+    )
     factor_out = adapter_out.reshape(ranks, model_width)
 
     full = (peer_count - 1) // 2
@@ -287,7 +308,6 @@
             whole_kernel,
             plan,
             len(pieces),
-            position,
             [p[0] for p in pieces] + [p[1] for p in pieces] + [factor_in, factor_out, *weights, *totals],
             [((rows, model_width), f32)] + total_shapes,
             5 * rows * matmul_flops,
@@ -301,6 +321,13 @@
             x, value = lax.optimization_barrier((x, value))
             held.append(x)
         return value, held
+
+    middle = model_width // 2
+    columns = {"left": slice(0, middle), "right": slice(middle, None)}
+    moving = {}
+
+    def send(value, way):
+        return lax.ppermute(value.astype(bf16), "expert", forward if way == "ahead" else backward)
 
     for d in range(full):
         if d > 1:
@@ -310,7 +337,17 @@
             behind[d], ahead[d] = (tokens_b, grads_b), (tokens_a, grads_a)
         behind.append(tuple(lax.ppermute(x, "expert", forward) for x in behind[d]))
         ahead.append(tuple(lax.ppermute(x, "expert", backward) for x in ahead[d]))
-        if d > 0:
+        if d == 0:
+            sent, (mine,) = after(behind[1][0], mine)
+            behind[1] = (sent, behind[1][1])
+            sent, (mine,) = after(ahead[1][0], mine)
+            ahead[1] = (sent, ahead[1][1])
+            if parts == 2:
+                weights = [mine, lax.ppermute(mine, "dp", swap)]
+            else:
+                weights = [lax.all_gather(mine, "dp", axis=0, tiled=True)]
+            weights = [pltpu.with_memory_space_constraint(w, pltpu.VMEM) for w in weights]
+        else:
             totals = run(d)
     if split:
         totals, (tokens_b, tokens_a, grads_b, grads_a) = after(
@@ -324,7 +361,6 @@
             forward_kernel,
             plan,
             2,
-            position,
             far_tokens + [factor_in, *weights],
             [((token_count, wide), f32)] * 2 + [((token_count, wide), bf16), ((token_count, ranks), f32)],
             2 * token_count * matmul_flops,
@@ -333,13 +369,12 @@
             backward_kernel,
             plan,
             2,
-            position,
             far_grads + [activation, slope, low_rank, factor_in, factor_out, *weights],
             [((token_count, model_width), f32)] + [((token_count, ranks), bf16)] * 2,
             3 * token_count * matmul_flops,
         )
-        moving_back = lax.ppermute(rows_far[:half].astype(bf16), "expert", backward)
-        moving_ahead = lax.ppermute(rows_far[half:].astype(bf16), "expert", forward)
+        moving["left", "back"] = send(rows_far[:, :middle], "back")
+        moving["right", "ahead"] = send(rows_far[:, middle:], "ahead")
         totals, low_scaled = lax.optimization_barrier((totals, low_scaled))
     if full > 1:
         totals = run(full)
@@ -348,25 +383,31 @@
             adapters_kernel,
             plan,
             2,
-            position,
             far_grads + [hidden, low_scaled, back_scaled, *totals],
             total_shapes,
             4 * token_count * ranks * (model_width + wide),
         )
 
+    ways = ("back", "ahead")
     for d in range(full, 0, -1):
-        back = rows_at[d][:token_count]
-        front = rows_at[d][token_count : 2 * token_count]
-        if d < full:
-            back = back + moving_back.astype(f32)
-            front = front + moving_ahead.astype(f32)
-        elif split:
-            back = jnp.concatenate([back[:half] + moving_back.astype(f32), back[half:]])
-            front = jnp.concatenate([front[:half], front[half:] + moving_ahead.astype(f32)])
-        moving_back = lax.ppermute(back.astype(bf16), "expert", backward)
-        moving_ahead = lax.ppermute(front.astype(bf16), "expert", forward)
-    rows_own = rows_at[1][2 * token_count :]
-    grad_tokens = (rows_own + moving_back.astype(f32) + moving_ahead.astype(f32)).astype(bf16)
+        for side, span in columns.items():
+            blocks = {
+                way: rows_at[d][at * token_count : (at + 1) * token_count, span]
+                for at, way in enumerate(ways)
+            }
+            if all((side, way) in moving for way in ways):
+                blocks = dict(zip(ways, add_sums(rows_at[d], span, [moving[side, way] for way in ways])))
+            for way in ways:
+                if d == full and (side, way) in moving:
+                    blocks[way] = blocks[way] + moving[side, way].astype(f32)
+                moving[side, way] = send(blocks[way], way)
+    grad_tokens = pl.pallas_call(
+        functools.partial(last_kernel, 2 * token_count, list(columns.values())),
+        out_shape=jax.ShapeDtypeStruct((token_count, model_width), bf16),
+        in_specs=[pl.BlockSpec(memory_space=pltpu.VMEM)] * 5,
+        out_specs=pl.BlockSpec(memory_space=pltpu.VMEM),
+        compiler_params=pltpu.CompilerParams(vmem_limit_bytes=16 * 1024 * 1024),
+    )(rows_at[1], *(moving[side, way] for side in columns for way in ways))
 
     grad_in = jnp.stack(
         [
@@ -382,7 +423,11 @@
         ],
         axis=2,
     ).transpose(1, 0, 2)
-    summed = lax.psum_scatter(both, "dp", scatter_dimension=0, tiled=False)
+    if dp_count == 2:
+        core = lax.axis_index("dp")
+        summed = both[core] + lax.ppermute(both[1 - core], "dp", swap)
+    else:
+        summed = lax.psum_scatter(both, "dp", scatter_dimension=0, tiled=False)
     grad_in_all = summed[:, :narrow].reshape(local_count, rank, narrow)
     grad_out_all = summed[:, narrow:].reshape(local_count, rank, model_width // dp_count)
     return (grad_tokens, grad_in_all, grad_out_all)

time: 121 us -> 92.8 us (0.77)
  Pallas kernels: 38.2 us -> 22 us
  between operations: 14.3 us -> 0.95 us
  waiting for transfers between devices: 29.4 us -> 21 us
  starting transfers between devices: 26 us -> 31.8 us
  local copies, waits for them, and re-layouts: 10.7 us -> 14.6 us
    pallas_call x6, Pallas kernels: 35.3 us -> 18.6 us  [call(): pl.pallas_call(functools.partial(kernel, plan, pieces), out_shape=tuple((...]
    ppermute x9 -> x16, waiting for transfers between devices: 15.8 us -> 6.96 us  [the longest x14 6.96 us: send(): lax.ppermute(value.astype(bf16), 'expert', forward if way == 'ahead' else...]
    ppermute x6, starting transfers between devices: 3.7 us -> 11 us  [per_device(): lax.ppermute(x, 'expert', forward)]
    ppermute x6, starting transfers between devices: 9.22 us -> 2.24 us  [per_device(): ahead.append(tuple((lax.ppermute(x, 'expert', backward) for x in ahead[d])))]
    ppermute x9 -> x16, starting transfers between devices: 8.91 us -> 14.5 us  [the longest x14 14.4 us: send(): lax.ppermute(value.astype(bf16), 'expert', forward if way == 'ahead' else...]
    ppermute x6, waiting for transfers between devices: 0.34 us -> 3.24 us  [per_device(): ahead.append(tuple((lax.ppermute(x, 'expert', backward) for x in ahead[d])))]
    ppermute x6, waiting for transfers between devices: 12.4 us -> 10.2 us  [per_device(): lax.ppermute(x, 'expert', forward)]
    slice x2, local copies, waits for them, and re-layouts: 0.04 us -> 1.41 us  [the longest x1 0.71 us: per_device(): moving['right', 'ahead'] = send(rows_far[:, middle:], 'ahead')]
  transfers between devices with their start and end apart: 26 -> 32, of which waited for: 11 -> 13; matrix products, arithmetic and copies ran while one was open for 4% -> 8% of each run, Pallas kernels for 24% -> 19%
where the time goes in v4:
time: 92.8 us; the launch traced here: 92.4 us
  starting transfers between devices  31.8 us (34%)
  Pallas kernels  22 us (24%)
  waiting for transfers between devices  21 us (23%)
  local copies, waits for them, and re-layouts  14.6 us (16%)
  other arithmetic  1.98 us (2%)
  between operations  0.95 us (1%)
    pallas_call x6, Pallas kernels, call(): pl.pallas_call(functools.partial(kernel, plan, pieces), out_shape=tuple((...  18.6 us
    ppermute x14, starting transfers between devices, send(): lax.ppermute(value.astype(bf16), 'expert', forward if way == 'ahead' else...  14.4 us
    ppermute x6, starting transfers between devices, per_device(): lax.ppermute(x, 'expert', forward)  11 us
    ppermute x6, waiting for transfers between devices, per_device(): lax.ppermute(x, 'expert', forward)  10.2 us
    unnamed x41, local copies, waits for them, and re-layouts  8.8 us
    ppermute x14, waiting for transfers between devices, send(): lax.ppermute(value.astype(bf16), 'expert', forward if way == 'ahead' else...  6.96 us
    ppermute x6, waiting for transfers between devices, per_device(): ahead.append(tuple((lax.ppermute(x, 'expert', backward) for x in ahead[d])))  3.24 us
    ppermute x2, starting transfers between devices, per_device(): lax.ppermute(x[:half], 'expert', forward)  3.15 us
  transfers between devices with their start and end apart: 32, of which 13 were waited for; matrix products, arithmetic and copies ran while one was open for 8% of the time, Pallas kernels for 19%

profile of v4, /device:TPU:0, one launch (start us, length us, event | category | flops | bytes accessed | tf_op | source)
XLA Modules:
  0.0 92.4 jit_solution(2249262641766249335)
XLA Ops:
  0.6 3.1 %collective-permute-start = (bf16[64,2048]{1,0:T(8,128)(2,1)}, bf16[64,2048]{1,0:T(8,128)(2,1)S(1)}, u32[]{:S(2)}, u32[]{:S(2)}) collective-permute-start(bf16[64,2048]{1,0:T(8,128)(2,1)} %refs_2_.3), channel_id=1, source_target_pairs={{0,4},{4,8},{8,12},{12,14},{14,10},{10,6},{6,2},{2,0},{1,5},{5,9},... | collective-permute-start | bytes 786440 | tf_op jit(solution)/shard_map/ppermute | solution.py:338
  3.7 0.9 %copy-done.14 = bf16[64,2048]{1,0:T(8,128)(2,1)S(1)} copy-done((bf16[64,2048]{1,0:T(8,128)(2,1)S(1)}, bf16[64,2048]{1,0:T(8,128)(2,1)}, u32[]{:S(2)}) %copy-start.14) | copy-done | bytes 262168
  4.7 0.7 copy-done.17
  5.4 0.7 copy-done.18
  6.1 0.7 copy-done.19
  6.8 2.4 %shard_map.112 = (bf16[1024,2304]{1,0:T(8,128)(2,1)S(1)}, bf16[64,2176]{1,0:T(8,128)(2,1)S(1)}, bf16[32,768]{1,0:T(8,128)(2,1)S(1)}) custom-call(bf16[2,1024,384]{2,1,0:T(8,128)(2,1)} %refs_0_.1, bf16[2,1024,384]{2,1,0:T(8,128)(2,1)} %refs_1_.1, bf16[2,1024,384]{2,1,0:T(8,128)(2,1)} %refs_2_.2, bf16[64,2048]{1,0:T(8,128)(2,1)S(1)} %copy-done.14, ...), custom_call_target="tpu_custom_call" | custom-call | tf_op jit(solution)/shard_map/pallas_call | solution.py:275
  9.2 0.9 collective-permute-done.refs_0_
  10.1 1.5 %collective-permute-done.1.refs_1_ = bf16[64,2048]{1,0:T(8,128)(2,1)S(1)} collective-permute-done((bf16[64,2048]{1,0:T(8,128)(2,1)}, bf16[64,2048]{1,0:T(8,128)(2,1)S(1)}, u32[]{:S(2)}, u32[]{:S(2)}) %collective-permute-start.1) | collective-permute-done | bytes 262176 | tf_op jit(solution)/shard_map/ppermute | solution.py:339
  11.7 1.6 %collective-permute-start.2 = (bf16[64,2176]{1,0:T(8,128)(2,1)S(1)}, bf16[64,2176]{1,0:T(8,128)(2,1)S(1)}, u32[]{:S(2)}, u32[]{:S(2)}) collective-permute-start(bf16[64,2176]{1,0:T(8,128)(2,1)S(1)} %get-tuple-element.67.refs_5_), channel_id=1, source_target_pairs={{0,4},{4,8},{8,12},{12,14},{14,10},{10,6},{6,2},{2,0},{1,5},{5,9},... | collective-permute-start | bytes 835592 | tf_op jit(solution)/shard_map/ppermute | solution.py:338
  13.7 1.6 %collective-permute-start.5 = (bf16[64,2048]{1,0:T(8,128)(2,1)S(1)}, bf16[64,2048]{1,0:T(8,128)(2,1)S(1)}, u32[]{:S(2)}, u32[]{:S(2)}) collective-permute-start(bf16[64,2048]{1,0:T(8,128)(2,1)S(1)} %collective-permute-done.refs_0_), channel_id=1, source_target_pairs={{0,4},{4,8},{8,12},{12,14},{14,10},{10,6},{6,2},{2,0},{1,5},{5,9},... | collective-permute-start | bytes 786440 | tf_op jit(solution)/shard_map/ppermute | solution.py:338
  15.7 5.4 %collective-permute-done.2.refs_3_ = bf16[64,2176]{1,0:T(8,128)(2,1)S(1)} collective-permute-done((bf16[64,2176]{1,0:T(8,128)(2,1)S(1)}, bf16[64,2176]{1,0:T(8,128)(2,1)S(1)}, u32[]{:S(2)}, u32[]{:S(2)}) %collective-permute-start.2) | collective-permute-done | bytes 278560 | tf_op jit(solution)/shard_map/ppermute | solution.py:338
  21.1 1.6 %collective-permute-start.7 = (bf16[64,2176]{1,0:T(8,128)(2,1)S(1)}, bf16[64,2176]{1,0:T(8,128)(2,1)S(1)}, u32[]{:S(2)}, u32[]{:S(2)}) collective-permute-start(bf16[64,2176]{1,0:T(8,128)(2,1)S(1)} %collective-permute-done.2.refs_3_), channel_id=1, source_target_pairs={{0,4},{4,8},{8,12},{12,14},{14,10},{10,6},{6,2},{2,0},{1,5},{5,9},... | collective-permute-start | bytes 835592 | tf_op jit(solution)/shard_map/ppermute | solution.py:338
  23.3 4.4 %shard_map.113 = (f32[192,2048]{1,0:T(8,128)S(1)}, f32[32,768]{1,0:T(8,128)S(1)}, f32[32,2048]{1,0:T(8,128)S(1)}) custom-call(bf16[64,2048]{1,0:T(8,128)(2,1)S(1)} %collective-permute-done.refs_0_, bf16[64,2048]{1,0:T(8,128)(2,1)S(1)} %collective-permute-done.1.refs_1_, bf16[64,2048]{1,0:T(8,128)(2,1)S(1)} %copy-done.11, ...), custom_call_target="tpu_custom_call" | custom-call | flops 3019898880 | bytes 11599872 | tf_op jit(solution)/shard_map/pallas_call | solution.py:234
  27.7 1.6 %collective-permute-start.9 = (bf16[64,2048]{1,0:T(8,128)(2,1)S(1)}, bf16[64,2048]{1,0:T(8,128)(2,1)S(1)}, u32[]{:S(2)}, u32[]{:S(2)}) collective-permute-start(bf16[64,2048]{1,0:T(8,128)(2,1)S(1)} %collective-permute-done.5.refs_0_), channel_id=1, source_target_pairs={{0,4},{4,8},{8,12},{12,14},{14,10},{10,6},{6,2},{2,0},{1,5},{5,9},... | collective-permute-start | bytes 786440 | tf_op jit(solution)/shard_map/ppermute | solution.py:338
  29.8 2.9 %collective-permute-done.7.refs_2_ = bf16[64,2176]{1,0:T(8,128)(2,1)S(1)} collective-permute-done((bf16[64,2176]{1,0:T(8,128)(2,1)S(1)}, bf16[64,2176]{1,0:T(8,128)(2,1)S(1)}, u32[]{:S(2)}, u32[]{:S(2)}) %collective-permute-start.7) | collective-permute-done | bytes 278560 | tf_op jit(solution)/shard_map/ppermute | solution.py:338
  32.7 1.6 %collective-permute-start.11 = (bf16[64,2176]{1,0:T(8,128)(2,1)S(1)}, bf16[64,2176]{1,0:T(8,128)(2,1)S(1)}, u32[]{:S(2)}, u32[]{:S(2)}) collective-permute-start(bf16[64,2176]{1,0:T(8,128)(2,1)S(1)} %collective-permute-done.7.refs_2_), channel_id=1, source_target_pairs={{0,4},{4,8},{8,12},{12,14},{14,10},{10,6},{6,2},{2,0},{1,5},{5,9},... | collective-permute-start | bytes 835592 | tf_op jit(solution)/shard_map/ppermute | solution.py:338
  34.8 3.5 %shard_map.114 = (f32[128,2048]{1,0:T(8,128)S(1)}, f32[32,768]{1,0:T(8,128)S(1)}, f32[32,2048]{1,0:T(8,128)S(1)}) custom-call(bf16[64,2048]{1,0:T(8,128)(2,1)S(1)} %collective-permute-done.5.refs_0_, bf16[64,2048]{1,0:T(8,128)(2,1)S(1)} %collective-permute-done.6.refs_1_, bf16[64,2176]{1,0:T(8,128)(2,1)S(1)} %collective-permute-done.7.refs_2_, ...), custom_call_target="tpu_custom_call" | custom-call | flops 2013265920 | bytes 11059200 | tf_op jit(solution)/shard_map/pallas_call | solution.py:234
  38.4 1.6 %collective-permute-done.10.refs_1_ = bf16[64,2048]{1,0:T(8,128)(2,1)S(1)} collective-permute-done((bf16[64,2048]{1,0:T(8,128)(2,1)S(1)}, bf16[64,2048]{1,0:T(8,128)(2,1)S(1)}, u32[]{:S(2)}, u32[]{:S(2)}) %collective-permute-start.10) | collective-permute-done | bytes 262176 | tf_op jit(solution)/shard_map/ppermute | solution.py:339
  40.0 0.7 slice.48
  40.7 1.6 %collective-permute-start.15 = (bf16[32,2048]{1,0:T(8,128)(2,1)}, bf16[32,2048]{1,0:T(8,128)(2,1)}, u32[]{:S(2)}, u32[]{:S(2)}) collective-permute-start(bf16[32,2048]{1,0:T(8,128)(2,1)} %slice.48), channel_id=1, source_target_pairs={{0,4},{4,8},{8,12},{12,14},{14,10},{10,6},{6,2},{2,0},{1,5},{5,9},... | collective-permute-start | bytes 393224 | tf_op jit(solution)/shard_map/ppermute | solution.py:356
  43.4 0.9 %collective-permute-done.11.refs_2_ = bf16[64,2176]{1,0:T(8,128)(2,1)S(1)} collective-permute-done((bf16[64,2176]{1,0:T(8,128)(2,1)S(1)}, bf16[64,2176]{1,0:T(8,128)(2,1)S(1)}, u32[]{:S(2)}, u32[]{:S(2)}) %collective-permute-start.11) | collective-permute-done | bytes 278560 | tf_op jit(solution)/shard_map/ppermute | solution.py:338
  45.0 1.6 %collective-permute-start.13 = (bf16[32,2176]{1,0:T(8,128)(2,1)}, bf16[32,2176]{1,0:T(8,128)(2,1)S(1)}, u32[]{:S(2)}, u32[]{:S(2)}) collective-permute-start(bf16[32,2176]{1,0:T(8,128)(2,1)} %slice.46), channel_id=1, source_target_pairs={{0,4},{4,8},{8,12},{12,14},{14,10},{10,6},{6,2},{2,0},{1,5},{5,9},... | collective-permute-start | bytes 417800 | tf_op jit(solution)/shard_map/ppermute | solution.py:356
  46.6 0.7 slice.47
  48.2 2.3 %copy-done.1 = bf16[1024,2304]{1,0:T(8,128)(2,1)S(1)} copy-done((bf16[1024,2304]{1,0:T(8,128)(2,1)S(1)}, bf16[1024,2304]{1,0:T(8,128)(2,1)}, u32[]{:S(2)}) %copy-start.1) | copy-done | bytes 4718616
  50.5 2.3 %copy-done.3 = bf16[1024,2304]{1,0:T(8,128)(2,1)S(1)} copy-done((bf16[1024,2304]{1,0:T(8,128)(2,1)S(1)}, bf16[1024,2304]{1,0:T(8,128)(2,1)}, u32[]{:S(2)}) %copy-start.3) | copy-done | bytes 4718616
  52.9 2.5 %shard_map.115 = (f32[64,768]{1,0:T(8,128)S(1)}, f32[64,768]{1,0:T(8,128)S(1)}, bf16[64,768]{1,0:T(8,128)(2,1)S(1)}, f32[64,32]{1,0:T(8,128)S(1)}) custom-call(bf16[32,2048]{1,0:T(8,128)(2,1)} %collective-permute-done.15.refs_0_, bf16[32,2048]{1,0:T(8,128)(2,1)} %collective-permute-done.16.refs_1_, ...), custom_call_target="tpu_custom_call" | custom-call | flops 402653184 | bytes 9748480 | tf_op jit(solution)/shard_map/pallas_call | solution.py:234
  55.4 3.6 %shard_map.116 = (f32[64,2048]{1,0:T(8,128)S(1)}, bf16[64,32]{1,0:T(8,128)(2,1)S(1)}, bf16[64,32]{1,0:T(8,128)(2,1)S(1)}) custom-call(bf16[32,2176]{1,0:T(8,128)(2,1)S(1)} %collective-permute-done.13.refs_0_, bf16[32,2176]{1,0:T(8,128)(2,1)} %collective-permute-done.14.refs_1_, f32[64,768]{1,0:T(8,128)S(1)} %get-tuple-element.100.refs_2_, ...), custom_call_target="tpu_custom_call" | custom-call | flops 603979776 | bytes 10297344 | tf_op jit(solution)/shard_map/pallas_call | solution.py:234
  59.1 0.7 fusion.3
  59.8 1.5 %collective-permute-start.25 = (bf16[64,1024]{1,0:T(8,128)(2,1)}, bf16[64,1024]{1,0:T(8,128)(2,1)}, u32[]{:S(2)}, u32[]{:S(2)}) collective-permute-start(bf16[64,1024]{1,0:T(8,128)(2,1)} %get-tuple-element.129), channel_id=1, source_target_pairs={{0,4},{4,8},{8,12},{12,14},{14,10},{10,6},{6,2},{2,0},{1,5},{5,9},... | collective-permute-start | bytes 393224 | tf_op jit(solution)/shard_map/ppermute | solution.py:330
  61.8 3.5 %shard_map.117 = (f32[128,2048]{1,0:T(8,128)S(1)}, f32[32,768]{1,0:T(8,128)S(1)}, f32[32,2048]{1,0:T(8,128)S(1)}) custom-call(bf16[64,2048]{1,0:T(8,128)(2,1)S(1)} %copy-done.8, bf16[64,2048]{1,0:T(8,128)(2,1)S(1)} %copy-done.10, bf16[64,2176]{1,0:T(8,128)(2,1)S(1)} %collective-permute-done.11.refs_2_, bf16[64,2176]{1,0:T(8,128)(2,1)S(1)} %collective-permute-done.12.refs_3_, ...), custom_call_target="tpu_custom_call" | custom-call | flops 2013265920 | bytes 11059200 | tf_op jit(solution)/shard_map/pallas_call | solution.py:234
  65.3 1.0 %copy-done.5 = f32[128,2048]{1,0:T(8,128)} copy-done((f32[128,2048]{1,0:T(8,128)}, f32[128,2048]{1,0:T(8,128)S(1)}, u32[]{:S(2)}) %copy-start.5) | copy-done | bytes 1048600
  66.4 0.7 fusion.2
  67.1 1.5 %collective-permute-start.19 = (bf16[64,1024]{1,0:T(8,128)(2,1)}, bf16[64,1024]{1,0:T(8,128)(2,1)S(1)}, u32[]{:S(2)}, u32[]{:S(2)}) collective-permute-start(bf16[64,1024]{1,0:T(8,128)(2,1)} %get-tuple-element.126), channel_id=1, source_target_pairs={{0,4},{4,8},{8,12},{12,14},{14,10},{10,6},{6,2},{2,0},{1,5},{5,9},... | collective-permute-start | bytes 393224 | tf_op jit(solution)/shard_map/ppermute | solution.py:330
  69.2 1.1 %shard_map.123 = (f32[32,768]{1,0:T(8,128)S(1)}, f32[32,2048]{1,0:T(8,128)S(1)}) custom-call(bf16[32,2176]{1,0:T(8,128)(2,1)S(1)} %collective-permute-done.13.refs_0_, bf16[32,2176]{1,0:T(8,128)(2,1)} %collective-permute-done.14.refs_1_, bf16[64,768]{1,0:T(8,128)(2,1)S(1)} %get-tuple-element.116.refs_2_, bf16[64,32]{1,0:T(8,128)(2,1)S(1)} %get-tuple-element.117.refs_3_, ...), custom_call_target="tpu_custom_call" | custom-call | flops 23068672 | bytes 745472 | tf_op jit(solution)/shard_map/pallas_call | solution.py:234
  70.7 1.2 %add_convert_fusion = (bf16[64,1024]{1,0:T(8,128)(2,1)S(1)}, bf16[64,1024]{1,0:T(8,128)(2,1)S(1)}) fusion(bf16[64,1024]{1,0:T(8,128)(2,1)} %collective-permute-done.25, f32[128,2048]{1,0:T(8,128)} %copy-done.5, bf16[64,1024]{1,0:T(8,128)(2,1)} %collective-permute-done.17), kind=kLoop, calls=%fused_computation.4 | loop fusion | flops 393216 | bytes 1048576 | tf_op jit(solution)/shard_map/convert_element_type | solution.py:330
  72.4 1.6 %collective-permute-start.26 = (bf16[64,1024]{1,0:T(8,128)(2,1)S(1)}, bf16[64,1024]{1,0:T(8,128)(2,1)S(1)}, u32[]{:S(2)}, u32[]{:S(2)}) collective-permute-start(bf16[64,1024]{1,0:T(8,128)(2,1)S(1)} %get-tuple-element.123), channel_id=1, source_target_pairs={{0,4},{4,8},{8,12},{12,14},{14,10},{10,6},{6,2},{2,0},{1,5},{5,9},... | collective-permute-start | bytes 393224 | tf_op jit(solution)/shard_map/ppermute | solution.py:330
  73.9 0.7 fusion.1
  74.7 2.2 %collective-permute-done.18.refs_1_ = bf16[64,1024]{1,0:T(8,128)(2,1)S(1)} collective-permute-done((bf16[64,1024]{1,0:T(8,128)(2,1)S(1)}, bf16[64,1024]{1,0:T(8,128)(2,1)S(1)}, u32[]{:S(2)}, u32[]{:S(2)}) %collective-permute-start.18) | collective-permute-done | bytes 131104 | tf_op jit(solution)/shard_map/ppermute | solution.py:330
  77.4 1.6 %collective-permute-start.21 = (bf16[64,1024]{1,0:T(8,128)(2,1)S(1)}, bf16[64,1024]{1,0:T(8,128)(2,1)S(1)}, u32[]{:S(2)}, u32[]{:S(2)}) collective-permute-start(bf16[64,1024]{1,0:T(8,128)(2,1)S(1)} %get-tuple-element.109), channel_id=1, source_target_pairs={{0,4},{4,8},{8,12},{12,14},{14,10},{10,6},{6,2},{2,0},{1,5},{5,9},... | collective-permute-start | bytes 393224 | tf_op jit(solution)/shard_map/ppermute | solution.py:330
  79.6 1.6 %collective-permute-start.28 = (bf16[64,1024]{1,0:T(8,128)(2,1)S(1)}, bf16[64,1024]{1,0:T(8,128)(2,1)S(1)}, u32[]{:S(2)}, u32[]{:S(2)}) collective-permute-start(bf16[64,1024]{1,0:T(8,128)(2,1)S(1)} %get-tuple-element.113), channel_id=1, source_target_pairs={{0,4},{4,8},{8,12},{12,14},{14,10},{10,6},{6,2},{2,0},{1,5},{5,9},... | collective-permute-start | bytes 393224 | tf_op jit(solution)/shard_map/ppermute | solution.py:330
  81.2 1.4 %collective-permute-done.20.refs_1_ = bf16[64,1024]{1,0:T(8,128)(2,1)S(1)} collective-permute-done((bf16[64,1024]{1,0:T(8,128)(2,1)S(1)}, bf16[64,1024]{1,0:T(8,128)(2,1)S(1)}, u32[]{:S(2)}, u32[]{:S(2)}) %collective-permute-start.20) | collective-permute-done | bytes 131104 | tf_op jit(solution)/shard_map/ppermute | solution.py:330
  82.6 1.0 %collective-permute-start.22 = (bf16[64,1024]{1,0:T(8,128)(2,1)S(1)}, bf16[64,1024]{1,0:T(8,128)(2,1)S(1)}, u32[]{:S(2)}, u32[]{:S(2)}) collective-permute-start(bf16[64,1024]{1,0:T(8,128)(2,1)S(1)} %get-tuple-element.110), channel_id=1, source_target_pairs={{4,0},{8,4},{12,8},{14,12},{10,14},{6,10},{2,6},{0,2},{5,1},{9,5},... | collective-permute-start | bytes 393224 | tf_op jit(solution)/shard_map/ppermute | solution.py:330
  83.6 1.1 %collective-permute-start.23 = (bf16[64,1024]{1,0:T(8,128)(2,1)S(1)}, bf16[64,1024]{1,0:T(8,128)(2,1)S(1)}, u32[]{:S(2)}, u32[]{:S(2)}) collective-permute-start(bf16[64,1024]{1,0:T(8,128)(2,1)S(1)} %get-tuple-element.111), channel_id=1, source_target_pairs={{0,4},{4,8},{8,12},{12,14},{14,10},{10,6},{6,2},{2,0},{1,5},{5,9},... | collective-permute-start | bytes 393224 | tf_op jit(solution)/shard_map/ppermute | solution.py:330
  84.7 0.8 collective-permute-done.27.refs_1_
  86.6 1.4 %collective-permute-start.30 = (bf16[64,1024]{1,0:T(8,128)(2,1)S(1)}, bf16[64,1024]{1,0:T(8,128)(2,1)S(1)}, u32[]{:S(2)}, u32[]{:S(2)}) collective-permute-start(bf16[64,1024]{1,0:T(8,128)(2,1)S(1)} %get-tuple-element.115), channel_id=1, source_target_pairs={{0,4},{4,8},{8,12},{12,14},{14,10},{10,6},{6,2},{2,0},{1,5},{5,9},... | collective-permute-start | bytes 393224 | tf_op jit(solution)/shard_map/ppermute | solution.py:330
  88.7 0.8 slice.65
  89.5 1.5 %collective-permute-done.29.refs_3_ = bf16[64,1024]{1,0:T(8,128)(2,1)S(1)} collective-permute-done((bf16[64,1024]{1,0:T(8,128)(2,1)S(1)}, bf16[64,1024]{1,0:T(8,128)(2,1)S(1)}, u32[]{:S(2)}, u32[]{:S(2)}) %collective-permute-start.29) | collective-permute-done | bytes 131104 | tf_op jit(solution)/shard_map/ppermute | solution.py:330
  91.6 0.8 shard_map.122
  (88 shorter events, 10.8 us)
Async XLA Ops:
  0.6 9.5 %collective-permute-start = (bf16[64,2048]{1,0:T(8,128)(2,1)}, bf16[64,2048]{1,0:T(8,128)(2,1)S(1)}, u32[]{:S(2)}, u32[]{:S(2)}) collective-permute-start(bf16[64,2048]{1,0:T(8,128)(2,1)} %refs_2_.3), channel_id=1, source_target_pairs={{0,4},{4,8},{8,12},{12,14},{14,10},{10,6},{6,2},{2,0},{1,5},{5,9},... | collective-permute-start | bytes 786440 | tf_op jit(solution)/shard_map/ppermute | solution.py:338
  3.7 8.0 %collective-permute-start.1 = (bf16[64,2048]{1,0:T(8,128)(2,1)}, bf16[64,2048]{1,0:T(8,128)(2,1)S(1)}, u32[]{:S(2)}, u32[]{:S(2)}) collective-permute-start(bf16[64,2048]{1,0:T(8,128)(2,1)} %refs_2_.3), channel_id=1, source_target_pairs={{4,0},{8,4},{12,8},{14,12},{10,14},{6,10},{2,6},{0,2},{5,1},{9,5},... | collective-permute-start | bytes 786440 | tf_op jit(solution)/shard_map/ppermute | solution.py:339
  6.8 16.5 %copy-start.6 = (bf16[2,16,2048]{2,1,0:T(8,128)(2,1)S(1)}, bf16[2,16,2048]{2,1,0:T(8,128)(2,1)}, u32[]{:S(2)}) copy-start(bf16[2,16,2048]{2,1,0:T(8,128)(2,1)} %param.17) | copy-start | bytes 393220
  6.8 16.5 %copy-start.11 = (bf16[64,2048]{1,0:T(8,128)(2,1)S(1)}, bf16[64,2048]{1,0:T(8,128)(2,1)}, u32[]{:S(2)}) copy-start(bf16[64,2048]{1,0:T(8,128)(2,1)} %refs_2_.3) | copy-start | bytes 786436
  9.2 25.6 %copy-start = (bf16[1024,2304]{1,0:T(8,128)(2,1)}, bf16[1024,2304]{1,0:T(8,128)(2,1)S(1)}, u32[]{:S(2)}) copy-start(bf16[1024,2304]{1,0:T(8,128)(2,1)S(1)} %get-tuple-element.69.refs_8_.refs_6_.refs_3_.refs_7_) | copy-start | bytes 14155780
  11.7 11.5 %collective-permute-start.4 = (bf16[1024,2304]{1,0:T(8,128)(2,1)S(1)}, bf16[1024,2304]{1,0:T(8,128)(2,1)S(1)}, u32[]{:S(2)}, u32[]{:S(2)}) collective-permute-start(bf16[1024,2304]{1,0:T(8,128)(2,1)S(1)} %get-tuple-element.69.refs_8_.refs_6_.refs_3_.refs_7_), channel_id=1, source_target_pairs={{0,1},{1,0},{2,3},{3,2},{4,5},{5,4},{6,7},{7,6},{8,9},{9,8},{10,11... | collective-permute-start | bytes 14155784 | tf_op jit(solution)/shard_map/ppermute | solution.py:346
  11.7 9.5 %collective-permute-start.2 = (bf16[64,2176]{1,0:T(8,128)(2,1)S(1)}, bf16[64,2176]{1,0:T(8,128)(2,1)S(1)}, u32[]{:S(2)}, u32[]{:S(2)}) collective-permute-start(bf16[64,2176]{1,0:T(8,128)(2,1)S(1)} %get-tuple-element.67.refs_5_), channel_id=1, source_target_pairs={{0,4},{4,8},{8,12},{12,14},{14,10},{10,6},{6,2},{2,0},{1,5},{5,9},... | collective-permute-start | bytes 835592 | tf_op jit(solution)/shard_map/ppermute | solution.py:338
  13.3 9.5 %collective-permute-start.3 = (bf16[64,2176]{1,0:T(8,128)(2,1)S(1)}, bf16[64,2176]{1,0:T(8,128)(2,1)S(1)}, u32[]{:S(2)}, u32[]{:S(2)}) collective-permute-start(bf16[64,2176]{1,0:T(8,128)(2,1)S(1)} %get-tuple-element.67.refs_5_), channel_id=1, source_target_pairs={{4,0},{8,4},{12,8},{14,12},{10,14},{6,10},{2,6},{0,2},{5,1},{9,5},... | collective-permute-start | bytes 835592 | tf_op jit(solution)/shard_map/ppermute | solution.py:339
  13.7 14.0 %collective-permute-start.5 = (bf16[64,2048]{1,0:T(8,128)(2,1)S(1)}, bf16[64,2048]{1,0:T(8,128)(2,1)S(1)}, u32[]{:S(2)}, u32[]{:S(2)}) collective-permute-start(bf16[64,2048]{1,0:T(8,128)(2,1)S(1)} %collective-permute-done.refs_0_), channel_id=1, source_target_pairs={{0,4},{4,8},{8,12},{12,14},{14,10},{10,6},{6,2},{2,0},{1,5},{5,9},... | collective-permute-start | bytes 786440 | tf_op jit(solution)/shard_map/ppermute | solution.py:338
  15.3 14.1 %collective-permute-start.6 = (bf16[64,2048]{1,0:T(8,128)(2,1)S(1)}, bf16[64,2048]{1,0:T(8,128)(2,1)S(1)}, u32[]{:S(2)}, u32[]{:S(2)}) collective-permute-start(bf16[64,2048]{1,0:T(8,128)(2,1)S(1)} %collective-permute-done.1.refs_1_), channel_id=1, source_target_pairs={{4,0},{8,4},{12,8},{14,12},{10,14},{6,10},{2,6},{0,2},{5,1},{9,5},... | collective-permute-start | bytes 786440 | tf_op jit(solution)/shard_map/ppermute | solution.py:339
  21.1 11.6 %collective-permute-start.7 = (bf16[64,2176]{1,0:T(8,128)(2,1)S(1)}, bf16[64,2176]{1,0:T(8,128)(2,1)S(1)}, u32[]{:S(2)}, u32[]{:S(2)}) collective-permute-start(bf16[64,2176]{1,0:T(8,128)(2,1)S(1)} %collective-permute-done.2.refs_3_), channel_id=1, source_target_pairs={{0,4},{4,8},{8,12},{12,14},{14,10},{10,6},{6,2},{2,0},{1,5},{5,9},... | collective-permute-start | bytes 835592 | tf_op jit(solution)/shard_map/ppermute | solution.py:338
  22.8 11.6 %collective-permute-start.8 = (bf16[64,2176]{1,0:T(8,128)(2,1)S(1)}, bf16[64,2176]{1,0:T(8,128)(2,1)S(1)}, u32[]{:S(2)}, u32[]{:S(2)}) collective-permute-start(bf16[64,2176]{1,0:T(8,128)(2,1)S(1)} %collective-permute-done.3.refs_4_), channel_id=1, source_target_pairs={{4,0},{8,4},{12,8},{14,12},{10,14},{6,10},{2,6},{0,2},{5,1},{9,5},... | collective-permute-start | bytes 835592 | tf_op jit(solution)/shard_map/ppermute | solution.py:339
  23.2 11.6 %copy-start.2 = (bf16[1024,2304]{1,0:T(8,128)(2,1)}, bf16[1024,2304]{1,0:T(8,128)(2,1)S(1)}, u32[]{:S(2)}) copy-start(bf16[1024,2304]{1,0:T(8,128)(2,1)S(1)} %collective-permute-done.4.refs_9_.refs_7_.refs_4_.refs_8_) | copy-start | bytes 14155780
  27.7 10.6 %collective-permute-start.9 = (bf16[64,2048]{1,0:T(8,128)(2,1)S(1)}, bf16[64,2048]{1,0:T(8,128)(2,1)S(1)}, u32[]{:S(2)}, u32[]{:S(2)}) collective-permute-start(bf16[64,2048]{1,0:T(8,128)(2,1)S(1)} %collective-permute-done.5.refs_0_), channel_id=1, source_target_pairs={{0,4},{4,8},{8,12},{12,14},{14,10},{10,6},{6,2},{2,0},{1,5},{5,9},... | collective-permute-start | bytes 786440 | tf_op jit(solution)/shard_map/ppermute | solution.py:338
  29.4 10.6 %collective-permute-start.10 = (bf16[64,2048]{1,0:T(8,128)(2,1)S(1)}, bf16[64,2048]{1,0:T(8,128)(2,1)S(1)}, u32[]{:S(2)}, u32[]{:S(2)}) collective-permute-start(bf16[64,2048]{1,0:T(8,128)(2,1)S(1)} %collective-permute-done.6.refs_1_), channel_id=1, source_target_pairs={{4,0},{8,4},{12,8},{14,12},{10,14},{6,10},{2,6},{0,2},{5,1},{9,5},... | collective-permute-start | bytes 786440 | tf_op jit(solution)/shard_map/ppermute | solution.py:339
  32.7 11.6 %collective-permute-start.11 = (bf16[64,2176]{1,0:T(8,128)(2,1)S(1)}, bf16[64,2176]{1,0:T(8,128)(2,1)S(1)}, u32[]{:S(2)}, u32[]{:S(2)}) collective-permute-start(bf16[64,2176]{1,0:T(8,128)(2,1)S(1)} %collective-permute-done.7.refs_2_), channel_id=1, source_target_pairs={{0,4},{4,8},{8,12},{12,14},{14,10},{10,6},{6,2},{2,0},{1,5},{5,9},... | collective-permute-start | bytes 835592 | tf_op jit(solution)/shard_map/ppermute | solution.py:338
  34.3 12.2 %collective-permute-start.12 = (bf16[64,2176]{1,0:T(8,128)(2,1)S(1)}, bf16[64,2176]{1,0:T(8,128)(2,1)S(1)}, u32[]{:S(2)}, u32[]{:S(2)}) collective-permute-start(bf16[64,2176]{1,0:T(8,128)(2,1)S(1)} %collective-permute-done.8.refs_3_), channel_id=1, source_target_pairs={{4,0},{8,4},{12,8},{14,12},{10,14},{6,10},{2,6},{0,2},{5,1},{9,5},... | collective-permute-start | bytes 835592 | tf_op jit(solution)/shard_map/ppermute | solution.py:339
  38.3 9.4 %copy-start.12 = (f32[32,2048]{1,0:T(8,128)}, f32[32,2048]{1,0:T(8,128)S(1)}, u32[]{:S(2)}) copy-start(f32[32,2048]{1,0:T(8,128)S(1)} %get-tuple-element.105.refs_9_) | copy-start | bytes 786436
  38.3 9.4 %copy-start.15 = (f32[32,768]{1,0:T(8,128)}, f32[32,768]{1,0:T(8,128)S(1)}, u32[]{:S(2)}) copy-start(f32[32,768]{1,0:T(8,128)S(1)} %get-tuple-element.104.refs_8_) | copy-start | bytes 294916
  38.3 8.2 %copy-start.7 = (bf16[64,2048]{1,0:T(8,128)(2,1)}, bf16[64,2048]{1,0:T(8,128)(2,1)S(1)}, u32[]{:S(2)}) copy-start(bf16[64,2048]{1,0:T(8,128)(2,1)S(1)} %collective-permute-done.9.refs_0_) | copy-start | bytes 786436
  40.0 7.3 %copy-start.9 = (bf16[64,2048]{1,0:T(8,128)(2,1)}, bf16[64,2048]{1,0:T(8,128)(2,1)S(1)}, u32[]{:S(2)}) copy-start(bf16[64,2048]{1,0:T(8,128)(2,1)S(1)} %collective-permute-done.10.refs_1_) | copy-start | bytes 786436
  40.7 7.0 %collective-permute-start.15 = (bf16[32,2048]{1,0:T(8,128)(2,1)}, bf16[32,2048]{1,0:T(8,128)(2,1)}, u32[]{:S(2)}, u32[]{:S(2)}) collective-permute-start(bf16[32,2048]{1,0:T(8,128)(2,1)} %slice.48), channel_id=1, source_target_pairs={{0,4},{4,8},{8,12},{12,14},{14,10},{10,6},{6,2},{2,0},{1,5},{5,9},... | collective-permute-start | bytes 393224 | tf_op jit(solution)/shard_map/ppermute | solution.py:356
  42.9 5.3 %collective-permute-start.16 = (bf16[32,2048]{1,0:T(8,128)(2,1)}, bf16[32,2048]{1,0:T(8,128)(2,1)}, u32[]{:S(2)}, u32[]{:S(2)}) collective-permute-start(bf16[32,2048]{1,0:T(8,128)(2,1)} %slice.49), channel_id=1, source_target_pairs={{4,0},{8,4},{12,8},{14,12},{10,14},{6,10},{2,6},{0,2},{5,1},{9,5},... | collective-permute-start | bytes 393224 | tf_op jit(solution)/shard_map/ppermute | solution.py:357
  45.0 10.4 %collective-permute-start.13 = (bf16[32,2176]{1,0:T(8,128)(2,1)}, bf16[32,2176]{1,0:T(8,128)(2,1)S(1)}, u32[]{:S(2)}, u32[]{:S(2)}) collective-permute-start(bf16[32,2176]{1,0:T(8,128)(2,1)} %slice.46), channel_id=1, source_target_pairs={{0,4},{4,8},{8,12},{12,14},{14,10},{10,6},{6,2},{2,0},{1,5},{5,9},... | collective-permute-start | bytes 417800 | tf_op jit(solution)/shard_map/ppermute | solution.py:356
  47.2 8.2 %collective-permute-start.14 = (bf16[32,2176]{1,0:T(8,128)(2,1)}, bf16[32,2176]{1,0:T(8,128)(2,1)}, u32[]{:S(2)}, u32[]{:S(2)}) collective-permute-start(bf16[32,2176]{1,0:T(8,128)(2,1)} %slice.47), channel_id=1, source_target_pairs={{4,0},{8,4},{12,8},{14,12},{10,14},{6,10},{2,6},{0,2},{5,1},{9,5},... | collective-permute-start | bytes 417800 | tf_op jit(solution)/shard_map/ppermute | solution.py:357
  48.2 2.3 %copy-start.1 = (bf16[1024,2304]{1,0:T(8,128)(2,1)S(1)}, bf16[1024,2304]{1,0:T(8,128)(2,1)}, u32[]{:S(2)}) copy-start(bf16[1024,2304]{1,0:T(8,128)(2,1)} %copy-done) | copy-start | bytes 14155780
  50.5 2.3 %copy-start.3 = (bf16[1024,2304]{1,0:T(8,128)(2,1)S(1)}, bf16[1024,2304]{1,0:T(8,128)(2,1)}, u32[]{:S(2)}) copy-start(bf16[1024,2304]{1,0:T(8,128)(2,1)} %copy-done.2) | copy-start | bytes 14155780
  52.9 2.5 %copy-start.4 = (bf16[1024,2304]{1,0:T(8,128)(2,1)S(1)}, bf16[1024,2304]{1,0:T(8,128)(2,1)}, u32[]{:S(2)}) copy-start(bf16[1024,2304]{1,0:T(8,128)(2,1)} %copy-done.2) | copy-start | bytes 14155780
  55.4 6.4 %copy-start.8 = (bf16[64,2048]{1,0:T(8,128)(2,1)S(1)}, bf16[64,2048]{1,0:T(8,128)(2,1)}, u32[]{:S(2)}) copy-start(bf16[64,2048]{1,0:T(8,128)(2,1)} %copy-done.7) | copy-start | bytes 786436
  55.4 6.4 %copy-start.10 = (bf16[64,2048]{1,0:T(8,128)(2,1)S(1)}, bf16[64,2048]{1,0:T(8,128)(2,1)}, u32[]{:S(2)}) copy-start(bf16[64,2048]{1,0:T(8,128)(2,1)} %copy-done.9) | copy-start | bytes 786436
  55.4 6.4 %copy-start.13 = (f32[32,2048]{1,0:T(8,128)S(1)}, f32[32,2048]{1,0:T(8,128)}, u32[]{:S(2)}) copy-start(f32[32,2048]{1,0:T(8,128)} %copy-done.12) | copy-start | bytes 786436
  55.4 6.4 %copy-start.16 = (f32[32,768]{1,0:T(8,128)S(1)}, f32[32,768]{1,0:T(8,128)}, u32[]{:S(2)}) copy-start(f32[32,768]{1,0:T(8,128)} %copy-done.15) | copy-start | bytes 294916
  59.8 10.9 %collective-permute-start.25 = (bf16[64,1024]{1,0:T(8,128)(2,1)}, bf16[64,1024]{1,0:T(8,128)(2,1)}, u32[]{:S(2)}, u32[]{:S(2)}) collective-permute-start(bf16[64,1024]{1,0:T(8,128)(2,1)} %get-tuple-element.129), channel_id=1, source_target_pairs={{0,4},{4,8},{8,12},{12,14},{14,10},{10,6},{6,2},{2,0},{1,5},{5,9},... | collective-permute-start | bytes 393224 | tf_op jit(solution)/shard_map/ppermute | solution.py:330
  61.3 9.3 %collective-permute-start.17 = (bf16[64,1024]{1,0:T(8,128)(2,1)}, bf16[64,1024]{1,0:T(8,128)(2,1)}, u32[]{:S(2)}, u32[]{:S(2)}) collective-permute-start(bf16[64,1024]{1,0:T(8,128)(2,1)} %get-tuple-element.130), channel_id=1, source_target_pairs={{4,0},{8,4},{12,8},{14,12},{10,14},{6,10},{2,6},{0,2},{5,1},{9,5},... | collective-permute-start | bytes 393224 | tf_op jit(solution)/shard_map/ppermute | solution.py:330
  65.3 1.0 %copy-start.5 = (f32[128,2048]{1,0:T(8,128)}, f32[128,2048]{1,0:T(8,128)S(1)}, u32[]{:S(2)}) copy-start(f32[128,2048]{1,0:T(8,128)S(1)} %get-tuple-element.106) | copy-start | bytes 3145732
  67.1 7.6 %collective-permute-start.19 = (bf16[64,1024]{1,0:T(8,128)(2,1)}, bf16[64,1024]{1,0:T(8,128)(2,1)S(1)}, u32[]{:S(2)}, u32[]{:S(2)}) collective-permute-start(bf16[64,1024]{1,0:T(8,128)(2,1)} %get-tuple-element.126), channel_id=1, source_target_pairs={{0,4},{4,8},{8,12},{12,14},{14,10},{10,6},{6,2},{2,0},{1,5},{5,9},... | collective-permute-start | bytes 393224 | tf_op jit(solution)/shard_map/ppermute | solution.py:330
  68.6 10.4 %collective-permute-start.24 = (bf16[64,1024]{1,0:T(8,128)(2,1)}, bf16[64,1024]{1,0:T(8,128)(2,1)S(1)}, u32[]{:S(2)}, u32[]{:S(2)}) collective-permute-start(bf16[64,1024]{1,0:T(8,128)(2,1)} %get-tuple-element.125), channel_id=1, source_target_pairs={{4,0},{8,4},{12,8},{14,12},{10,14},{6,10},{2,6},{0,2},{5,1},{9,5},... | collective-permute-start | bytes 393224 | tf_op jit(solution)/shard_map/ppermute | solution.py:330
  71.9 5.0 %collective-permute-start.18 = (bf16[64,1024]{1,0:T(8,128)(2,1)S(1)}, bf16[64,1024]{1,0:T(8,128)(2,1)S(1)}, u32[]{:S(2)}, u32[]{:S(2)}) collective-permute-start(bf16[64,1024]{1,0:T(8,128)(2,1)S(1)} %get-tuple-element.124), channel_id=1, source_target_pairs={{4,0},{8,4},{12,8},{14,12},{10,14},{6,10},{2,6},{0,2},{5,1},{9,5},... | collective-permute-start | bytes 393224 | tf_op jit(solution)/shard_map/ppermute | solution.py:330
  72.4 6.7 %collective-permute-start.26 = (bf16[64,1024]{1,0:T(8,128)(2,1)S(1)}, bf16[64,1024]{1,0:T(8,128)(2,1)S(1)}, u32[]{:S(2)}, u32[]{:S(2)}) collective-permute-start(bf16[64,1024]{1,0:T(8,128)(2,1)S(1)} %get-tuple-element.123), channel_id=1, source_target_pairs={{0,4},{4,8},{8,12},{12,14},{14,10},{10,6},{6,2},{2,0},{1,5},{5,9},... | collective-permute-start | bytes 393224 | tf_op jit(solution)/shard_map/ppermute | solution.py:330
  74.6 13.4 %collective-permute-start.31 = (f32[32,1216]{1,0:T(8,128)S(1)}, f32[32,1216]{1,0:T(8,128)S(1)}, u32[]{:S(2)}, u32[]{:S(2)}) collective-permute-start(f32[32,1216]{1,0:T(8,128)S(1)} %bitcast.20), channel_id=1, source_target_pairs={{0,1},{1,0},{2,3},{3,2},{4,5},{5,4},{6,7},{7,6},{8,9},{9,8},{10,11... | collective-permute-start | bytes 466952 | tf_op jit(solution)/shard_map/ppermute | solution.py:428
  76.9 5.6 %collective-permute-start.20 = (bf16[64,1024]{1,0:T(8,128)(2,1)S(1)}, bf16[64,1024]{1,0:T(8,128)(2,1)S(1)}, u32[]{:S(2)}, u32[]{:S(2)}) collective-permute-start(bf16[64,1024]{1,0:T(8,128)(2,1)S(1)} %get-tuple-element.108), channel_id=1, source_target_pairs={{4,0},{8,4},{12,8},{14,12},{10,14},{6,10},{2,6},{0,2},{5,1},{9,5},... | collective-permute-start | bytes 393224 | tf_op jit(solution)/shard_map/ppermute | solution.py:330
  77.4 5.1 %collective-permute-start.21 = (bf16[64,1024]{1,0:T(8,128)(2,1)S(1)}, bf16[64,1024]{1,0:T(8,128)(2,1)S(1)}, u32[]{:S(2)}, u32[]{:S(2)}) collective-permute-start(bf16[64,1024]{1,0:T(8,128)(2,1)S(1)} %get-tuple-element.109), channel_id=1, source_target_pairs={{0,4},{4,8},{8,12},{12,14},{14,10},{10,6},{6,2},{2,0},{1,5},{5,9},... | collective-permute-start | bytes 393224 | tf_op jit(solution)/shard_map/ppermute | solution.py:330
  79.1 6.4 %collective-permute-start.27 = (bf16[64,1024]{1,0:T(8,128)(2,1)S(1)}, bf16[64,1024]{1,0:T(8,128)(2,1)S(1)}, u32[]{:S(2)}, u32[]{:S(2)}) collective-permute-start(bf16[64,1024]{1,0:T(8,128)(2,1)S(1)} %get-tuple-element.112), channel_id=1, source_target_pairs={{4,0},{8,4},{12,8},{14,12},{10,14},{6,10},{2,6},{0,2},{5,1},{9,5},... | collective-permute-start | bytes 393224 | tf_op jit(solution)/shard_map/ppermute | solution.py:330
  79.6 6.4 %collective-permute-start.28 = (bf16[64,1024]{1,0:T(8,128)(2,1)S(1)}, bf16[64,1024]{1,0:T(8,128)(2,1)S(1)}, u32[]{:S(2)}, u32[]{:S(2)}) collective-permute-start(bf16[64,1024]{1,0:T(8,128)(2,1)S(1)} %get-tuple-element.113), channel_id=1, source_target_pairs={{0,4},{4,8},{8,12},{12,14},{14,10},{10,6},{6,2},{2,0},{1,5},{5,9},... | collective-permute-start | bytes 393224 | tf_op jit(solution)/shard_map/ppermute | solution.py:330
  82.6 6.9 %collective-permute-start.22 = (bf16[64,1024]{1,0:T(8,128)(2,1)S(1)}, bf16[64,1024]{1,0:T(8,128)(2,1)S(1)}, u32[]{:S(2)}, u32[]{:S(2)}) collective-permute-start(bf16[64,1024]{1,0:T(8,128)(2,1)S(1)} %get-tuple-element.110), channel_id=1, source_target_pairs={{4,0},{8,4},{12,8},{14,12},{10,14},{6,10},{2,6},{0,2},{5,1},{9,5},... | collective-permute-start | bytes 393224 | tf_op jit(solution)/shard_map/ppermute | solution.py:330
  83.6 5.9 %collective-permute-start.23 = (bf16[64,1024]{1,0:T(8,128)(2,1)S(1)}, bf16[64,1024]{1,0:T(8,128)(2,1)S(1)}, u32[]{:S(2)}, u32[]{:S(2)}) collective-permute-start(bf16[64,1024]{1,0:T(8,128)(2,1)S(1)} %get-tuple-element.111), channel_id=1, source_target_pairs={{0,4},{4,8},{8,12},{12,14},{14,10},{10,6},{6,2},{2,0},{1,5},{5,9},... | collective-permute-start | bytes 393224 | tf_op jit(solution)/shard_map/ppermute | solution.py:330
  86.0 5.0 %collective-permute-start.29 = (bf16[64,1024]{1,0:T(8,128)(2,1)S(1)}, bf16[64,1024]{1,0:T(8,128)(2,1)S(1)}, u32[]{:S(2)}, u32[]{:S(2)}) collective-permute-start(bf16[64,1024]{1,0:T(8,128)(2,1)S(1)} %get-tuple-element.114), channel_id=1, source_target_pairs={{4,0},{8,4},{12,8},{14,12},{10,14},{6,10},{2,6},{0,2},{5,1},{9,5},... | collective-permute-start | bytes 393224 | tf_op jit(solution)/shard_map/ppermute | solution.py:330
  86.6 5.0 %collective-permute-start.30 = (bf16[64,1024]{1,0:T(8,128)(2,1)S(1)}, bf16[64,1024]{1,0:T(8,128)(2,1)S(1)}, u32[]{:S(2)}, u32[]{:S(2)}) collective-permute-start(bf16[64,1024]{1,0:T(8,128)(2,1)S(1)} %get-tuple-element.115), channel_id=1, source_target_pairs={{0,4},{4,8},{8,12},{12,14},{14,10},{10,6},{6,2},{2,0},{1,5},{5,9},... | collective-permute-start | bytes 393224 | tf_op jit(solution)/shard_map/ppermute | solution.py:330
  (4 other events, 3.1 us)

commit v5 on v4

v5 whole, which is shorter than its diff:
```python
import functools

import jax
import jax.numpy as jnp
from jax import lax
from jax.experimental import pallas as pl
from jax.experimental.pallas import tpu as pltpu
from jax.sharding import PartitionSpec as P

adapter_scale = 2.0
f32 = jnp.float32
bf16 = jnp.bfloat16
lane_count = 128


def ring_order(count, snake):
    if snake and count % 2 == 0:
        return list(range(0, count, 2)) + list(range(count - 1, 0, -2))
    return list(range(count))


def matmul(a, b):
    return jnp.dot(a, b, preferred_element_type=f32)


def matmul_bt(a, b):
    return lax.dot_general(a, b, (((1,), (1,)), ((), ())), preferred_element_type=f32)


def matmul_at(a, b):
    return lax.dot_general(a, b, (((0,), (0,)), ((), ())), preferred_element_type=f32)


def stacked(piece_refs, span):
    return jnp.concatenate([ref[:, span] for ref in piece_refs], axis=0)


class Plan:
    def __init__(self, parts, depth, model_width, hidden_width, rank, experts):
        self.parts = parts
        self.depth = depth
        self.model_width = model_width
        self.hidden_width = hidden_width
        self.rank = rank
        self.experts = experts
        self.wide = experts * hidden_width
        self.ranks = experts * rank

    def spans(self):
        if self.parts == 1:
            return [slice(0, self.model_width)]
        core = lax.axis_index("dp")
        return [
            pl.ds(pl.multiple_of(at * self.depth, self.depth), self.depth) for at in (core, 1 - core)
        ]

    def forward(self, token_refs, factor_in_ref, weight_refs):
        gate_pre, up_pre = 0.0, 0.0
        for span, weight in zip(self.spans(), weight_refs):
            tokens_in = stacked(token_refs, span)
            gate_pre += matmul(tokens_in, weight[:, : self.wide])
            up_pre += matmul(tokens_in, weight[:, self.wide : 2 * self.wide])
        logistic = 1.0 / (1.0 + jnp.exp(-gate_pre))
        activation = gate_pre * logistic
        derivative = logistic * (1.0 + gate_pre * (1.0 - logistic))
        hidden = (activation * up_pre).astype(bf16)
        low_rank = matmul_bt(hidden, factor_in_ref[...])
        return activation, up_pre * derivative, hidden, low_rank

    def scales(self, grad_refs):
        columns = stacked(grad_refs, slice(self.model_width, None)).astype(f32)
        lane = lax.broadcasted_iota(jnp.int32, columns.shape, 1)
        first = lax.axis_index("expert") * self.experts
        return [
            jnp.sum(jnp.where(lane == first + j, columns, 0.0), axis=1, keepdims=True)
            for j in range(self.experts)
        ]

    def spread(self, scales, width):
        rows = scales[0].shape[0]
        at = lax.broadcasted_iota(jnp.int32, (rows, self.experts * width), 1)
        out = jnp.broadcast_to(scales[0], at.shape)
        for j in range(1, self.experts):
            out = jnp.where(at >= j * width, scales[j], out)
        return out

    def backward(
        self, grad_refs, activation, slope, factor_in_ref, factor_out_ref, weight_refs, rows_ref
    ):
        scales = self.scales(grad_refs)
        adapter_back, grad_down = 0.0, 0.0
        spans = self.spans()
        for span, weight in zip(spans, weight_refs):
            grad_in = stacked(grad_refs, span)
            adapter_back += matmul_bt(grad_in, factor_out_ref[:, span])
            grad_down += matmul(grad_in, weight[:, 2 * self.wide :])
        adapter_back = adapter_back.astype(bf16)
        grad_hidden = self.spread(scales, self.hidden_width) * (
            grad_down + adapter_scale * matmul(adapter_back, factor_in_ref[...])
        )
        grad_gate = (grad_hidden * slope).astype(bf16)
        grad_up = (grad_hidden * activation).astype(bf16)
        for span, weight in zip(spans, weight_refs):
            rows_ref[:, span] = matmul_bt(grad_gate, weight[:, : self.wide]) + matmul_bt(
                grad_up, weight[:, self.wide : 2 * self.wide]
            )
        rank_scale = self.spread(scales, self.rank)
        return rank_scale, (rank_scale * adapter_back.astype(f32)).astype(bf16)

    def adapters(self, grad_refs, hidden, low_scaled, back_scaled, total_refs, out_refs):
        grad_all = stacked(grad_refs, slice(0, self.model_width))
        for total, out, value in zip(
            total_refs, out_refs, (matmul_at(back_scaled, hidden), matmul_at(low_scaled, grad_all))
        ):
            out[...] = total[...] + adapter_scale * value


def whole_kernel(plan, pieces, blocks, *refs):
    token_refs, grad_refs, refs = refs[:pieces], refs[pieces : 2 * pieces], refs[2 * pieces :]
    factor_in_ref, factor_out_ref, refs = refs[0], refs[1], refs[2:]
    weight_refs, refs = refs[: plan.parts], refs[plan.parts :]
    total_refs, rows_ref, out_refs, send_refs = refs[:2], refs[2], refs[3:5], refs[5:]
    activation, slope, hidden, low_rank = plan.forward(token_refs, factor_in_ref, weight_refs)
    rank_scale, back_scaled = plan.backward(
        grad_refs, activation, slope, factor_in_ref, factor_out_ref, weight_refs, rows_ref
    )
    for (first_row, span), send_ref in zip(blocks, send_refs):
        send_ref[...] = rows_ref[first_row : first_row + send_ref.shape[0], span].astype(bf16)
    low_scaled = (rank_scale * low_rank).astype(bf16)
    plan.adapters(grad_refs, hidden, low_scaled, back_scaled, total_refs, out_refs)


def prepare_kernel(plan, *refs):
    raw_refs, refs = refs[:3], refs[3:]
    out_grad_ref, ids_ref, route_ref, factor_ref = refs[:4]
    packed_ref, grads_ref, factor_in_ref, ids_held, route_held, sems = refs[4:]
    width, rank = plan.hidden_width, plan.rank
    pairs = [(ids_ref, ids_held), (route_ref, route_held)]
    pairs.append((out_grad_ref, grads_ref.at[:, : plan.model_width]))
    for kind in range(3):
        for expert in range(plan.experts):
            at = kind * plan.wide + expert * width
            pairs.append((raw_refs[kind].at[expert], packed_ref.at[:, at : at + width]))
    for expert in range(plan.experts):
        block = factor_in_ref.at[
            expert * rank : (expert + 1) * rank, expert * width : (expert + 1) * width
        ]
        pairs.append((factor_ref.at[expert], block))
    copies = [
        pltpu.make_async_copy(source, target, sems.at[at])
        for at, (source, target) in enumerate(pairs)
    ]
    for copy in copies:
        copy.start()
    for expert in range(plan.experts):
        for other in range(plan.experts):
            if other != expert:
                factor_in_ref[
                    expert * rank : (expert + 1) * rank, other * width : (other + 1) * width
                ] = jnp.zeros((rank, width), bf16)
    copies[0].wait()
    copies[1].wait()
    rows, lanes = grads_ref.shape[0], grads_ref.shape[1] - plan.model_width
    expert_at = lax.broadcasted_iota(jnp.int32, (lanes, rows), 0)
    ids, route = ids_held[...], route_held[...].astype(f32)
    dense = jnp.zeros((lanes, rows), f32)
    for k in range(ids.shape[0]):
        dense = jnp.where(ids[k : k + 1, :] == expert_at, route[k : k + 1, :], dense)
    grads_ref[:, plan.model_width :] = dense.T.astype(bf16)
    for copy in copies[2:]:
        copy.wait()


def add_kernel(blocks, *refs):
    rows_ref, refs = refs[0], refs[1:]
    for (first_row, span), incoming, out in zip(blocks, refs, refs[len(blocks) :]):
        rows = rows_ref[first_row : first_row + out.shape[0], span]
        out[...] = (rows + incoming[...].astype(f32)).astype(bf16)


def add_sums(rows, blocks, incoming):
    return pl.pallas_call(
        functools.partial(add_kernel, blocks),
        out_shape=tuple(jax.ShapeDtypeStruct(x.shape, bf16) for x in incoming),
        in_specs=[pl.BlockSpec(memory_space=pltpu.VMEM)] * (1 + len(incoming)),
        out_specs=(pl.BlockSpec(memory_space=pltpu.VMEM),) * len(incoming),
        compiler_params=pltpu.CompilerParams(vmem_limit_bytes=16 * 1024 * 1024),
    )(rows, *incoming)


def halves_kernel(plan, total_in_ref, total_out_ref, keep_ref, send_ref):
    first = lax.axis_index("dp") == 0
    middle, narrow = plan.model_width // 2, plan.hidden_width // 2
    low, high = total_out_ref[:, :middle], total_out_ref[:, middle:]
    keep_ref[:, :middle] = jnp.where(first, low, high)
    send_ref[:, :middle] = jnp.where(first, high, low)
    for expert in range(plan.experts):
        rows = slice(expert * plan.rank, (expert + 1) * plan.rank)
        block = total_in_ref[rows, expert * plan.hidden_width : (expert + 1) * plan.hidden_width]
        low, high = block[:, :narrow], block[:, narrow:]
        keep_ref[rows, middle:] = jnp.where(first, low, high)
        send_ref[rows, middle:] = jnp.where(first, high, low)


def joined_kernel(plan, keep_ref, other_ref, in_ref, out_ref):
    middle = plan.model_width // 2
    for expert in range(plan.experts):
        rows = slice(expert * plan.rank, (expert + 1) * plan.rank)
        out_ref[expert] = keep_ref[rows, :middle] + other_ref[rows, :middle]
        in_ref[expert] = keep_ref[rows, middle:] + other_ref[rows, middle:]


def last_kernel(first_row, spans, *refs):
    rows_ref, out_ref = refs[0], refs[-1]
    for at, span in enumerate(spans):
        total = rows_ref[first_row : first_row + out_ref.shape[0], span]
        for incoming in refs[1 + 2 * at : 3 + 2 * at]:
            total = total + incoming[...].astype(f32)
        out_ref[:, span] = total.astype(bf16)


def simple_call(kernel, operands, outs):
    return pl.pallas_call(
        kernel,
        out_shape=tuple(jax.ShapeDtypeStruct(shape, dtype) for shape, dtype in outs),
        in_specs=[pl.BlockSpec(memory_space=pltpu.VMEM)] * len(operands),
        out_specs=(pl.BlockSpec(memory_space=pltpu.VMEM),) * len(outs),
        compiler_params=pltpu.CompilerParams(vmem_limit_bytes=16 * 1024 * 1024),
    )(*operands)


def expert_call(plan, pieces, blocks, block_rows, operands, totals):
    rows = sum(piece[0].shape[0] for piece in pieces)
    operands = [p[0] for p in pieces] + [p[1] for p in pieces] + [*operands, *totals]
    outs = [((rows, plan.model_width), f32)] + [(total.shape, f32) for total in totals]
    outs += [((block_rows, plan.model_width // 2), bf16)] * len(blocks)
    return pl.pallas_call(
        functools.partial(whole_kernel, plan, len(pieces), blocks),
        out_shape=tuple(jax.ShapeDtypeStruct(shape, dtype) for shape, dtype in outs),
        in_specs=[pl.BlockSpec(memory_space=pltpu.VMEM)] * len(operands),
        out_specs=(pl.BlockSpec(memory_space=pltpu.VMEM),) * len(outs),
        compiler_params=pltpu.CompilerParams(vmem_limit_bytes=16 * 1024 * 1024),
        cost_estimate=pl.CostEstimate(
            flops=10 * rows * plan.model_width * plan.wide,
            bytes_accessed=sum(op.size * op.dtype.itemsize for op in operands),
            transcendentals=0,
        ),
    )(*operands)


def per_device(
    snake,
    tokens,
    out_grad,
    expert_ids,
    route_weight,
    gate_weight,
    up_weight,
    down_weight,
    adapter_in,
    adapter_out,
):
    peer_count = lax.axis_size("expert")
    dp_count = lax.axis_size("dp")
    token_count, model_width = tokens.shape
    local_count, depth, hidden_width = gate_weight.shape
    rank = adapter_in.shape[1]
    expert_total = local_count * peer_count
    order = ring_order(peer_count, snake)
    forward = [(order[i], order[(i + 1) % peer_count]) for i in range(peer_count)]
    backward = [(b, a) for a, b in forward]
    swap = [(0, 1), (1, 0)]
    parts = 2 if dp_count == 2 else 1
    plan = Plan(parts, depth, model_width, hidden_width, rank, local_count)
    wide, ranks = plan.wide, plan.ranks

    lanes = -(-expert_total // lane_count) * lane_count
    mine, grads, factor_in = pl.pallas_call(
        functools.partial(prepare_kernel, plan),
        out_shape=(
            jax.ShapeDtypeStruct((depth, 3 * wide), bf16),
            jax.ShapeDtypeStruct((token_count, model_width + lanes), bf16),
            jax.ShapeDtypeStruct((ranks, wide), bf16),
        ),
        in_specs=[pl.BlockSpec(memory_space=pltpu.HBM)] * 7,
        out_specs=(pl.BlockSpec(memory_space=pltpu.VMEM),) * 3,
        scratch_shapes=[
            pltpu.VMEM(expert_ids.shape[::-1], jnp.int32),
            pltpu.VMEM(route_weight.shape[::-1], bf16),
            pltpu.SemaphoreType.DMA((3 + 4 * local_count,)),
        ],
        compiler_params=pltpu.CompilerParams(vmem_limit_bytes=16 * 1024 * 1024),
    )(
        *(
            pltpu.with_memory_space_constraint(x, pltpu.HBM)
            for x in (
                gate_weight,
                up_weight,
                down_weight,
                out_grad,
                expert_ids.T,
                route_weight.T,
                adapter_in,
            )
        )
    )
    if parts == 2:
        weights = [mine, lax.ppermute(mine, "dp", swap)]
    else:
        weights = [lax.all_gather(mine, "dp", axis=0, tiled=True)]
    weights = [pltpu.with_memory_space_constraint(w, pltpu.VMEM) for w in weights]
    factor_out = adapter_out.reshape(ranks, model_width)

    full = (peer_count - 1) // 2
    split = peer_count % 2 == 0
    totals = (jnp.zeros((ranks, wide), f32), jnp.zeros((ranks, model_width), f32))
    behind, ahead = [(tokens, grads)], [(tokens, grads)]
    rows_at = [None]

    middle = model_width // 2
    columns = {"left": slice(0, middle), "right": slice(middle, None)}
    ways = {"back": (0, backward), "ahead": (token_count, forward)}
    moving = {}

    def send(value, way):
        return lax.ppermute(value, "expert", ways[way][1])

    def run(pieces, blocks, totals):
        return expert_call(
            plan, pieces, blocks, token_count, [factor_in, factor_out, *weights], totals
        )

    def after(value, *arrays):
        held = []
        for x in arrays:
            x, value = lax.optimization_barrier((x, value))
            held.append(x)
        return value, held

    for d in range(full):
        if d > 1:
            totals, (tokens_b, grads_a) = after(totals, behind[d][0], ahead[d][1])
            tokens_a, grads_b = ahead[d][0], behind[d][1]
            behind[d], ahead[d] = (tokens_b, grads_b), (tokens_a, grads_a)
        behind.append(tuple(lax.ppermute(x, "expert", forward) for x in behind[d]))
        ahead.append(tuple(lax.ppermute(x, "expert", backward) for x in ahead[d]))
        if d > 0:
            pieces = [behind[d], ahead[d]] + ([behind[0]] if d == 1 else [])
            rows_d, *totals = run(pieces, [], totals)
            rows_at.append(rows_d)
    first_sends = [("left", "ahead"), ("right", "back")]
    if not split:
        first_sends += [("left", "back"), ("right", "ahead")]
    if split:
        totals, (tokens_b, grads_a) = after(totals, behind[full][0], ahead[full][1])
        far = (lax.ppermute(tokens_b, "expert", forward), lax.ppermute(grads_a, "expert", backward))
    if full > 0:
        pieces = [behind[full], ahead[full]] + ([behind[0]] if full == 1 else [])
        rows_d, *outs = run(pieces, [(ways[way][0], columns[side]) for side, way in first_sends], totals)
        rows_at.append(rows_d)
        totals, ready = outs[:2], outs[2:]
    if split:
        last, ready = after(far[1], *ready)
        far = (far[0], last)
    for (side, way), value in zip(first_sends, ready):
        moving[side, way] = send(value, way)
    if split:
        _, *outs = run([far], [(0, columns["left"]), (0, columns["right"])], totals)
        totals = outs[:2]
        moving["left", "back"] = send(outs[2], "back")
        moving["right", "ahead"] = send(outs[3], "ahead")
        blocks = [(0, columns["left"]), (token_count, columns["right"])]
        for block, key in zip(blocks, [("left", "back"), ("right", "ahead")]):
            (value,) = add_sums(rows_at[full], [block], [moving[key]])
            moving[key] = send(value, key[1])
    for d in range(full - 1, 0, -1):
        for side, span in columns.items():
            blocks = [(first_row, span) for first_row, _ in ways.values()]
            values = add_sums(rows_at[d], blocks, [moving[side, way] for way in ways])
            for way, value in zip(ways, values):
                moving[side, way] = send(value, way)
    grad_tokens = pl.pallas_call(
        functools.partial(last_kernel, 2 * token_count, list(columns.values())),
        out_shape=jax.ShapeDtypeStruct((token_count, model_width), bf16),
        in_specs=[pl.BlockSpec(memory_space=pltpu.VMEM)] * 5,
        out_specs=pl.BlockSpec(memory_space=pltpu.VMEM),
        compiler_params=pltpu.CompilerParams(vmem_limit_bytes=16 * 1024 * 1024),
    )(rows_at[1], *(moving[side, way] for side in columns for way in ways))

    narrow = hidden_width // dp_count
    if dp_count == 2:
        half = ((ranks, middle + narrow), f32)
        keep, other = simple_call(functools.partial(halves_kernel, plan), totals, [half, half])
        grad_in_all, grad_out_all = simple_call(
            functools.partial(joined_kernel, plan),
            [keep, lax.ppermute(other, "dp", swap)],
            [((local_count, rank, narrow), f32), ((local_count, rank, middle), f32)],
        )
        return (grad_tokens, grad_in_all, grad_out_all)
    grad_in = jnp.stack(
        [
            totals[0][j * rank : (j + 1) * rank, j * hidden_width : (j + 1) * hidden_width]
            for j in range(local_count)
        ]
    )
    both = jnp.concatenate(
        [
            grad_in.reshape(ranks, dp_count, narrow),
            totals[1].reshape(ranks, dp_count, model_width // dp_count),
        ],
        axis=2,
    ).transpose(1, 0, 2)
    summed = lax.psum_scatter(both, "dp", scatter_dimension=0, tiled=False)
    grad_in_all = summed[:, :narrow].reshape(local_count, rank, narrow)
    grad_out_all = summed[:, narrow:].reshape(local_count, rank, model_width // dp_count)
    return (grad_tokens, grad_in_all, grad_out_all)


def solution(mesh):
    snake = mesh.shape["dp"] == 2
    return jax.shard_map(
        functools.partial(per_device, snake),
        mesh=mesh,
        in_specs=(
            P(("group", "expert", "dp"), None),
            P(("group", "expert", "dp"), None),
            P(("group", "expert", "dp"), None),
            P(("group", "expert", "dp"), None),
            P("expert", "dp", None),
            P("expert", "dp", None),
            P("expert", "dp", None),
            P("expert", None, None),
            P("expert", None, None),
        ),
        out_specs=(
            P(("group", "expert", "dp"), None),
            P(("group", "expert"), None, "dp"),
            P(("group", "expert"), None, "dp"),
        ),
        check_vma=False,
    )
```

time: 92.8 us -> 87 us (0.938)
  local copies, waits for them, and re-layouts: 14.6 us -> 0.03 us
  waiting for transfers between devices: 21 us -> 34.7 us
  other arithmetic: 1.98 us -> 0 us
  Pallas kernels: 22 us -> 20.4 us
    unnamed x41 -> x4, local copies, waits for them, and re-layouts: 8.8 us -> 0.01 us
    ppermute x6, waiting for transfers between devices: 3.24 us -> 9.75 us  [per_device(): ahead.append(tuple((lax.ppermute(x, 'expert', backward) for x in ahead[d])))]
    slice x8 -> x0, local copies, waits for them, and re-layouts: 5.47 us -> none  [the longest x2 1.37 us: per_device(): x[:half]]
    ppermute x6, waiting for transfers between devices: 10.2 us -> 13.9 us  [per_device(): lax.ppermute(x, 'expert', forward)]
    ppermute x19 -> x17, waiting for transfers between devices: 7.49 us -> 11 us  [the longest x14 11 us: send(): return lax.ppermute(value, 'expert', ways[way][1])]
    pallas_call x10 -> x12, Pallas kernels: 18.8 us -> 17 us  [the longest x4 15.9 us: expert_call(): pl.pallas_call(functools.partial(whole_kernel, plan, len(pieces), blocks)...]
    convert_element_type x1 -> x0, other arithmetic: 1.18 us -> none  [send(): value.astype(bf16)]
    ppermute x6, starting transfers between devices: 2.24 us -> 1.2 us  [per_device(): ahead.append(tuple((lax.ppermute(x, 'expert', backward) for x in ahead[d])))]
  transfers between devices with their start and end apart: 32 -> 30, of which waited for: 13 -> 15; matrix products, arithmetic and copies ran while one was open for 8% -> 0% of each run, Pallas kernels for 19% -> 14%
where the time goes in v5:
time: 87 us; the launch traced here: 86.9 us
  waiting for transfers between devices  34.7 us (40%)
  starting transfers between devices  31 us (36%)
  Pallas kernels  20.4 us (23%)
    pallas_call x4, Pallas kernels, expert_call(): pl.pallas_call(functools.partial(whole_kernel, plan, len(pieces), blocks)...  15.9 us
    ppermute x14, starting transfers between devices, send(): return lax.ppermute(value, 'expert', ways[way][1])  15.6 us
    ppermute x6, waiting for transfers between devices, per_device(): lax.ppermute(x, 'expert', forward)  13.9 us
    ppermute x6, starting transfers between devices, per_device(): lax.ppermute(x, 'expert', forward)  11.6 us
    ppermute x14, waiting for transfers between devices, send(): return lax.ppermute(value, 'expert', ways[way][1])  11 us
    ppermute x6, waiting for transfers between devices, per_device(): ahead.append(tuple((lax.ppermute(x, 'expert', backward) for x in ahead[d])))  9.75 us
    pallas_call x1, Pallas kernels, per_device(): pl.pallas_call(functools.partial(prepare_kernel, plan), out_shape=(jax.Sh...  2.57 us
  transfers between devices with their start and end apart: 30, of which 15 were waited for; matrix products, arithmetic and copies ran while one was open for 0% of the time, Pallas kernels for 14%

profile of v5, /device:TPU:0, one launch (start us, length us, event | category | flops | bytes accessed | tf_op | source)
XLA Modules:
  0.0 86.9 jit_solution(8614963752850151238)
XLA Ops:
  0.7 2.6 %shard_map.112 = (bf16[1024,2304]{1,0:T(8,128)(2,1)S(1)}, bf16[64,2176]{1,0:T(8,128)(2,1)S(1)}, bf16[32,768]{1,0:T(8,128)(2,1)S(1)}) custom-call(bf16[2,1024,384]{2,1,0:T(8,128)(2,1)} %refs_0_.1, bf16[2,1024,384]{2,1,0:T(8,128)(2,1)} %refs_1_.1, bf16[2,1024,384]{2,1,0:T(8,128)(2,1)} %refs_2_.2, bf16[64,2048]{1,0:T(8,128)(2,1)} %refs_3_.1, s32[8,64]{1,0:T(8,128)} %bitcast.7, ...), custom_call_target="tpu_custom_call" | custom-call | tf_op jit(solution)/shard_map/pallas_call | solution.py:278
  3.2 0.5 collective-permute-start.4
  3.8 2.6 %collective-permute-start.2 = (bf16[64,2176]{1,0:T(8,128)(2,1)S(1)}, bf16[64,2176]{1,0:T(8,128)(2,1)S(1)}, u32[]{:S(2)}, u32[]{:S(2)}) collective-permute-start(bf16[64,2176]{1,0:T(8,128)(2,1)S(1)} %get-tuple-element.49.refs_5_), channel_id=1, source_target_pairs={{0,4},{4,8},{8,12},{12,14},{14,10},{10,6},{6,2},{2,0},{1,5},{5,9},... | collective-permute-start | bytes 835592 | tf_op jit(solution)/shard_map/ppermute | solution.py:345
  6.4 2.0 %collective-permute-start = (bf16[64,2048]{1,0:T(8,128)(2,1)S(1)}, bf16[64,2048]{1,0:T(8,128)(2,1)S(1)}, u32[]{:S(2)}, u32[]{:S(2)}) collective-permute-start(bf16[64,2048]{1,0:T(8,128)(2,1)S(1)} %copy-done.1), channel_id=1, source_target_pairs={{0,4},{4,8},{8,12},{12,14},{14,10},{10,6},{6,2},{2,0},{1,5},{5,9},... | collective-permute-start | bytes 786440 | tf_op jit(solution)/shard_map/ppermute | solution.py:345
  8.4 10.8 %collective-permute-done.refs_0_ = bf16[64,2048]{1,0:T(8,128)(2,1)S(1)} collective-permute-done((bf16[64,2048]{1,0:T(8,128)(2,1)S(1)}, bf16[64,2048]{1,0:T(8,128)(2,1)S(1)}, u32[]{:S(2)}, u32[]{:S(2)}) %collective-permute-start) | collective-permute-done | bytes 262176 | tf_op jit(solution)/shard_map/ppermute | solution.py:345
  19.2 1.8 %collective-permute-start.5 = (bf16[64,2048]{1,0:T(8,128)(2,1)S(1)}, bf16[64,2048]{1,0:T(8,128)(2,1)S(1)}, u32[]{:S(2)}, u32[]{:S(2)}) collective-permute-start(bf16[64,2048]{1,0:T(8,128)(2,1)S(1)} %collective-permute-done.refs_0_), channel_id=1, source_target_pairs={{0,4},{4,8},{8,12},{12,14},{14,10},{10,6},{6,2},{2,0},{1,5},{5,9},... | collective-permute-start | bytes 786440 | tf_op jit(solution)/shard_map/ppermute | solution.py:345
  21.0 0.2 collective-permute-start.6
  21.2 1.8 %collective-permute-start.7 = (bf16[64,2176]{1,0:T(8,128)(2,1)S(1)}, bf16[64,2176]{1,0:T(8,128)(2,1)S(1)}, u32[]{:S(2)}, u32[]{:S(2)}) collective-permute-start(bf16[64,2176]{1,0:T(8,128)(2,1)S(1)} %collective-permute-done.2.refs_3_), channel_id=1, source_target_pairs={{0,4},{4,8},{8,12},{12,14},{14,10},{10,6},{6,2},{2,0},{1,5},{5,9},... | collective-permute-start | bytes 835592 | tf_op jit(solution)/shard_map/ppermute | solution.py:345
  23.1 0.2 collective-permute-start.8
  23.3 4.4 %shard_map.113 = (f32[192,2048]{1,0:T(8,128)S(1)}, f32[32,768]{1,0:T(8,128)S(1)}, f32[32,2048]{1,0:T(8,128)S(1)}) custom-call(bf16[64,2048]{1,0:T(8,128)(2,1)S(1)} %collective-permute-done.refs_0_, bf16[64,2048]{1,0:T(8,128)(2,1)S(1)} %collective-permute-done.1.refs_1_, bf16[64,2048]{1,0:T(8,128)(2,1)S(1)} %copy-done.1, ...), custom_call_target="tpu_custom_call" | custom-call | flops 3019898880 | bytes 11599872 | tf_op jit(solution)/shard_map/pallas_call | solution.py:237
  27.7 0.6 collective-permute-done.5.refs_0_
  28.4 6.2 %collective-permute-done.8.refs_3_ = bf16[64,2176]{1,0:T(8,128)(2,1)S(1)} collective-permute-done((bf16[64,2176]{1,0:T(8,128)(2,1)S(1)}, bf16[64,2176]{1,0:T(8,128)(2,1)S(1)}, u32[]{:S(2)}, u32[]{:S(2)}) %collective-permute-start.8) | collective-permute-done | bytes 278560 | tf_op jit(solution)/shard_map/ppermute | solution.py:346
  34.6 0.4 collective-permute-start.12
  35.0 1.6 %collective-permute-start.9 = (bf16[64,2048]{1,0:T(8,128)(2,1)S(1)}, bf16[64,2048]{1,0:T(8,128)(2,1)S(1)}, u32[]{:S(2)}, u32[]{:S(2)}) collective-permute-start(bf16[64,2048]{1,0:T(8,128)(2,1)S(1)} %collective-permute-done.5.refs_0_), channel_id=1, source_target_pairs={{0,4},{4,8},{8,12},{12,14},{14,10},{10,6},{6,2},{2,0},{1,5},{5,9},... | collective-permute-start | bytes 786440 | tf_op jit(solution)/shard_map/ppermute | solution.py:345
  36.6 0.4 collective-permute-start.10
  37.0 1.6 %collective-permute-start.11 = (bf16[64,2176]{1,0:T(8,128)(2,1)S(1)}, bf16[64,2176]{1,0:T(8,128)(2,1)S(1)}, u32[]{:S(2)}, u32[]{:S(2)}) collective-permute-start(bf16[64,2176]{1,0:T(8,128)(2,1)S(1)} %collective-permute-done.7.refs_2_), channel_id=1, source_target_pairs={{0,4},{4,8},{8,12},{12,14},{14,10},{10,6},{6,2},{2,0},{1,5},{5,9},... | collective-permute-start | bytes 835592 | tf_op jit(solution)/shard_map/ppermute | solution.py:345
  38.6 3.5 %shard_map.114 = (f32[128,2048]{1,0:T(8,128)S(1)}, f32[32,768]{1,0:T(8,128)S(1)}, f32[32,2048]{1,0:T(8,128)S(1)}) custom-call(bf16[64,2048]{1,0:T(8,128)(2,1)S(1)} %collective-permute-done.5.refs_0_, bf16[64,2048]{1,0:T(8,128)(2,1)S(1)} %collective-permute-done.6.refs_1_, bf16[64,2176]{1,0:T(8,128)(2,1)S(1)} %collective-permute-done.7.refs_2_, ...), custom_call_target="tpu_custom_call" | custom-call | flops 2013265920 | bytes 11059200 | tf_op jit(solution)/shard_map/pallas_call | solution.py:237
  42.1 2.1 %collective-permute-done.9.refs_0_ = bf16[64,2048]{1,0:T(8,128)(2,1)S(1)} collective-permute-done((bf16[64,2048]{1,0:T(8,128)(2,1)S(1)}, bf16[64,2048]{1,0:T(8,128)(2,1)S(1)}, u32[]{:S(2)}, u32[]{:S(2)}) %collective-permute-start.9) | collective-permute-done | bytes 262176 | tf_op jit(solution)/shard_map/ppermute | solution.py:345
  44.2 1.5 %collective-permute-start.14 = (bf16[64,2176]{1,0:T(8,128)(2,1)S(1)}, bf16[64,2176]{1,0:T(8,128)(2,1)S(1)}, u32[]{:S(2)}, u32[]{:S(2)}) collective-permute-start(bf16[64,2176]{1,0:T(8,128)(2,1)S(1)} %collective-permute-done.12.refs_3_), channel_id=1, source_target_pairs={{4,0},{8,4},{12,8},{14,12},{10,14},{6,10},{2,6},{0,2},{5,1},{9,5},... | collective-permute-start | bytes 835592 | tf_op jit(solution)/shard_map/ppermute | solution.py:356
  45.8 0.5 collective-permute-start.13
  46.3 3.5 %collective-permute-done.10.refs_1_ = bf16[64,2048]{1,0:T(8,128)(2,1)S(1)} collective-permute-done((bf16[64,2048]{1,0:T(8,128)(2,1)S(1)}, bf16[64,2048]{1,0:T(8,128)(2,1)S(1)}, u32[]{:S(2)}, u32[]{:S(2)}) %collective-permute-start.10) | collective-permute-done | bytes 262176 | tf_op jit(solution)/shard_map/ppermute | solution.py:346
  49.8 0.4 collective-permute-done.11.refs_2_
  50.2 3.6 %shard_map.115 = (f32[128,2048]{1,0:T(8,128)S(1)}, f32[32,768]{1,0:T(8,128)S(1)}, f32[32,2048]{1,0:T(8,128)S(1)}, bf16[64,1024]{1,0:T(8,128)(2,1)S(1)}, bf16[64,1024]{1,0:T(8,128)(2,1)S(1)}) custom-call(bf16[64,2048]{1,0:T(8,128)(2,1)S(1)} %collective-permute-done.9.refs_0_, bf16[64,2048]{1,0:T(8,128)(2,1)S(1)} %collective-permute-done.10.refs_1_, ...), custom_call_target="tpu_custom_call" | custom-call | flops 2013265920 | bytes 11059200 | tf_op jit(solution)/shard_map/pallas_call | solution.py:237
  53.8 4.4 %shard_map.116 = (f32[64,2048]{1,0:T(8,128)}, f32[32,768]{1,0:T(8,128)S(1)}, f32[32,2048]{1,0:T(8,128)S(1)}, bf16[64,1024]{1,0:T(8,128)(2,1)S(1)}, bf16[64,1024]{1,0:T(8,128)(2,1)S(1)}) custom-call(bf16[64,2048]{1,0:T(8,128)(2,1)S(1)} %collective-permute-done.13.refs_0_, bf16[64,2176]{1,0:T(8,128)(2,1)S(1)} %collective-permute-done.14.refs_1_, ...), custom_call_target="tpu_custom_call" | custom-call | flops 1006632960 | bytes 10518528 | tf_op jit(solution)/shard_map/pallas_call | solution.py:237
  58.2 1.5 %collective-permute-start.15 = (bf16[64,1024]{1,0:T(8,128)(2,1)S(1)}, bf16[64,1024]{1,0:T(8,128)(2,1)S(1)}, u32[]{:S(2)}, u32[]{:S(2)}) collective-permute-start(bf16[64,1024]{1,0:T(8,128)(2,1)S(1)} %get-tuple-element.77), channel_id=1, source_target_pairs={{4,0},{8,4},{12,8},{14,12},{10,14},{6,10},{2,6},{0,2},{5,1},{9,5},... | collective-permute-start | bytes 393224 | tf_op jit(solution)/shard_map/ppermute | solution.py:326
  59.7 0.5 collective-permute-start.23
  60.3 1.6 %collective-permute-start.17 = (bf16[64,1024]{1,0:T(8,128)(2,1)S(1)}, bf16[64,1024]{1,0:T(8,128)(2,1)S(1)}, u32[]{:S(2)}, u32[]{:S(2)}) collective-permute-start(bf16[64,1024]{1,0:T(8,128)(2,1)S(1)} %get-tuple-element.78), channel_id=1, source_target_pairs={{0,4},{4,8},{8,12},{12,14},{14,10},{10,6},{6,2},{2,0},{1,5},{5,9},... | collective-permute-start | bytes 393224 | tf_op jit(solution)/shard_map/ppermute | solution.py:326
  61.8 2.8 %collective-permute-done.15.refs_1_ = bf16[64,1024]{1,0:T(8,128)(2,1)S(1)} collective-permute-done((bf16[64,1024]{1,0:T(8,128)(2,1)S(1)}, bf16[64,1024]{1,0:T(8,128)(2,1)S(1)}, u32[]{:S(2)}, u32[]{:S(2)}) %collective-permute-start.15) | collective-permute-done | bytes 131104 | tf_op jit(solution)/shard_map/ppermute | solution.py:326
  64.6 1.5 %collective-permute-start.16 = (bf16[64,1024]{1,0:T(8,128)(2,1)S(1)}, bf16[64,1024]{1,0:T(8,128)(2,1)S(1)}, u32[]{:S(2)}, u32[]{:S(2)}) collective-permute-start(bf16[64,1024]{1,0:T(8,128)(2,1)S(1)} %shard_map.117), channel_id=1, source_target_pairs={{4,0},{8,4},{12,8},{14,12},{10,14},{6,10},{2,6},{0,2},{5,1},{9,5},... | collective-permute-start | bytes 393224 | tf_op jit(solution)/shard_map/ppermute | solution.py:326
  66.1 1.6 %collective-permute-start.22 = (bf16[64,1024]{1,0:T(8,128)(2,1)S(1)}, bf16[64,1024]{1,0:T(8,128)(2,1)S(1)}, u32[]{:S(2)}, u32[]{:S(2)}) collective-permute-start(bf16[64,1024]{1,0:T(8,128)(2,1)S(1)} %get-tuple-element.83), channel_id=1, source_target_pairs={{4,0},{8,4},{12,8},{14,12},{10,14},{6,10},{2,6},{0,2},{5,1},{9,5},... | collective-permute-start | bytes 393224 | tf_op jit(solution)/shard_map/ppermute | solution.py:326
  67.7 0.5 collective-permute-start.24
  68.2 2.3 %collective-permute-done.16.refs_1_ = bf16[64,1024]{1,0:T(8,128)(2,1)S(1)} collective-permute-done((bf16[64,1024]{1,0:T(8,128)(2,1)S(1)}, bf16[64,1024]{1,0:T(8,128)(2,1)S(1)}, u32[]{:S(2)}, u32[]{:S(2)}) %collective-permute-start.16) | collective-permute-done | bytes 131104 | tf_op jit(solution)/shard_map/ppermute | solution.py:326
  70.6 0.7 collective-permute-start.18
  71.4 1.5 %collective-permute-start.19 = (bf16[64,1024]{1,0:T(8,128)(2,1)S(1)}, bf16[64,1024]{1,0:T(8,128)(2,1)S(1)}, u32[]{:S(2)}, u32[]{:S(2)}) collective-permute-start(bf16[64,1024]{1,0:T(8,128)(2,1)S(1)} %get-tuple-element.80), channel_id=1, source_target_pairs={{0,4},{4,8},{8,12},{12,14},{14,10},{10,6},{6,2},{2,0},{1,5},{5,9},... | collective-permute-start | bytes 393224 | tf_op jit(solution)/shard_map/ppermute | solution.py:326
  72.8 0.6 collective-permute-done.24.refs_2_
  73.5 1.6 %collective-permute-start.25 = (bf16[64,1024]{1,0:T(8,128)(2,1)S(1)}, bf16[64,1024]{1,0:T(8,128)(2,1)S(1)}, u32[]{:S(2)}, u32[]{:S(2)}) collective-permute-start(bf16[64,1024]{1,0:T(8,128)(2,1)S(1)} %get-tuple-element.85), channel_id=1, source_target_pairs={{4,0},{8,4},{12,8},{14,12},{10,14},{6,10},{2,6},{0,2},{5,1},{9,5},... | collective-permute-start | bytes 393224 | tf_op jit(solution)/shard_map/ppermute | solution.py:326
  75.1 0.5 collective-permute-start.26
  75.6 0.1 shard_map.124
  75.8 0.5 collective-permute-done.19.refs_2_
  76.4 2.1 %collective-permute-start.20 = (bf16[64,1024]{1,0:T(8,128)(2,1)S(1)}, bf16[64,1024]{1,0:T(8,128)(2,1)S(1)}, u32[]{:S(2)}, u32[]{:S(2)}) collective-permute-start(bf16[64,1024]{1,0:T(8,128)(2,1)S(1)} %get-tuple-element.81), channel_id=1, source_target_pairs={{4,0},{8,4},{12,8},{14,12},{10,14},{6,10},{2,6},{0,2},{5,1},{9,5},... | collective-permute-start | bytes 393224 | tf_op jit(solution)/shard_map/ppermute | solution.py:326
  78.5 1.6 %collective-permute-done.26.refs_2_ = bf16[64,1024]{1,0:T(8,128)(2,1)S(1)} collective-permute-done((bf16[64,1024]{1,0:T(8,128)(2,1)S(1)}, bf16[64,1024]{1,0:T(8,128)(2,1)S(1)}, u32[]{:S(2)}, u32[]{:S(2)}) %collective-permute-start.26) | collective-permute-done | bytes 131104 | tf_op jit(solution)/shard_map/ppermute | solution.py:326
  80.1 1.0 %collective-permute-start.27 = (bf16[64,1024]{1,0:T(8,128)(2,1)S(1)}, bf16[64,1024]{1,0:T(8,128)(2,1)S(1)}, u32[]{:S(2)}, u32[]{:S(2)}) collective-permute-start(bf16[64,1024]{1,0:T(8,128)(2,1)S(1)} %get-tuple-element.87), channel_id=1, source_target_pairs={{4,0},{8,4},{12,8},{14,12},{10,14},{6,10},{2,6},{0,2},{5,1},{9,5},... | collective-permute-start | bytes 393224 | tf_op jit(solution)/shard_map/ppermute | solution.py:326
  81.1 1.1 %collective-permute-start.28 = (bf16[64,1024]{1,0:T(8,128)(2,1)S(1)}, bf16[64,1024]{1,0:T(8,128)(2,1)S(1)}, u32[]{:S(2)}, u32[]{:S(2)}) collective-permute-start(bf16[64,1024]{1,0:T(8,128)(2,1)S(1)} %get-tuple-element.88), channel_id=1, source_target_pairs={{0,4},{4,8},{8,12},{12,14},{14,10},{10,6},{6,2},{2,0},{1,5},{5,9},... | collective-permute-start | bytes 393224 | tf_op jit(solution)/shard_map/ppermute | solution.py:326
  82.2 0.7 shard_map.125
  82.9 1.7 %collective-permute-done.21.refs_2_ = bf16[64,1024]{1,0:T(8,128)(2,1)S(1)} collective-permute-done((bf16[64,1024]{1,0:T(8,128)(2,1)S(1)}, bf16[64,1024]{1,0:T(8,128)(2,1)S(1)}, u32[]{:S(2)}, u32[]{:S(2)}) %collective-permute-start.21) | collective-permute-done | bytes 131104 | tf_op jit(solution)/shard_map/ppermute | solution.py:326
  84.6 0.5 collective-permute-done.27.refs_3_
  85.2 0.9 %collective-permute-done.28.refs_4_ = bf16[64,1024]{1,0:T(8,128)(2,1)S(1)} collective-permute-done((bf16[64,1024]{1,0:T(8,128)(2,1)S(1)}, bf16[64,1024]{1,0:T(8,128)(2,1)S(1)}, u32[]{:S(2)}, u32[]{:S(2)}) %collective-permute-start.28) | collective-permute-done | bytes 131104 | tf_op jit(solution)/shard_map/ppermute | solution.py:326
  86.1 0.8 shard_map.123
  (32 shorter events, 0.4 us)
Async XLA Ops:
  0.6 5.8 %copy-start.1 = (bf16[64,2048]{1,0:T(8,128)(2,1)S(1)}, bf16[64,2048]{1,0:T(8,128)(2,1)}, u32[]{:S(2)}) copy-start(bf16[64,2048]{1,0:T(8,128)(2,1)} %refs_2_.3) | copy-start | bytes 786436
  0.6 22.7 %copy-start = (bf16[2,16,2048]{2,1,0:T(8,128)(2,1)S(1)}, bf16[2,16,2048]{2,1,0:T(8,128)(2,1)}, u32[]{:S(2)}) copy-start(bf16[2,16,2048]{2,1,0:T(8,128)(2,1)} %param.17) | copy-start | bytes 393220
  3.2 20.0 %collective-permute-start.4 = (bf16[1024,2304]{1,0:T(8,128)(2,1)S(1)}, bf16[1024,2304]{1,0:T(8,128)(2,1)S(1)}, u32[]{:S(2)}, u32[]{:S(2)}) collective-permute-start(bf16[1024,2304]{1,0:T(8,128)(2,1)S(1)} %get-tuple-element.51.refs_8_.refs_6_.refs_4_), channel_id=1, source_target_pairs={{0,1},{1,0},{2,3},{3,2},{4,5},{5,4},{6,7},{7,6},{8,9},{9,8},{10,11... | collective-permute-start | bytes 14155784 | tf_op jit(solution)/shard_map/ppermute | solution.py:308
  3.8 17.5 %collective-permute-start.2 = (bf16[64,2176]{1,0:T(8,128)(2,1)S(1)}, bf16[64,2176]{1,0:T(8,128)(2,1)S(1)}, u32[]{:S(2)}, u32[]{:S(2)}) collective-permute-start(bf16[64,2176]{1,0:T(8,128)(2,1)S(1)} %get-tuple-element.49.refs_5_), channel_id=1, source_target_pairs={{0,4},{4,8},{8,12},{12,14},{14,10},{10,6},{6,2},{2,0},{1,5},{5,9},... | collective-permute-start | bytes 835592 | tf_op jit(solution)/shard_map/ppermute | solution.py:345
  6.4 16.7 %collective-permute-start.3 = (bf16[64,2176]{1,0:T(8,128)(2,1)S(1)}, bf16[64,2176]{1,0:T(8,128)(2,1)S(1)}, u32[]{:S(2)}, u32[]{:S(2)}) collective-permute-start(bf16[64,2176]{1,0:T(8,128)(2,1)S(1)} %get-tuple-element.49.refs_5_), channel_id=1, source_target_pairs={{4,0},{8,4},{12,8},{14,12},{10,14},{6,10},{2,6},{0,2},{5,1},{9,5},... | collective-permute-start | bytes 835592 | tf_op jit(solution)/shard_map/ppermute | solution.py:346
  6.4 12.8 %collective-permute-start = (bf16[64,2048]{1,0:T(8,128)(2,1)S(1)}, bf16[64,2048]{1,0:T(8,128)(2,1)S(1)}, u32[]{:S(2)}, u32[]{:S(2)}) collective-permute-start(bf16[64,2048]{1,0:T(8,128)(2,1)S(1)} %copy-done.1), channel_id=1, source_target_pairs={{0,4},{4,8},{8,12},{12,14},{14,10},{10,6},{6,2},{2,0},{1,5},{5,9},... | collective-permute-start | bytes 786440 | tf_op jit(solution)/shard_map/ppermute | solution.py:345
  8.4 12.6 %collective-permute-start.1 = (bf16[64,2048]{1,0:T(8,128)(2,1)S(1)}, bf16[64,2048]{1,0:T(8,128)(2,1)S(1)}, u32[]{:S(2)}, u32[]{:S(2)}) collective-permute-start(bf16[64,2048]{1,0:T(8,128)(2,1)S(1)} %copy-done.1), channel_id=1, source_target_pairs={{4,0},{8,4},{12,8},{14,12},{10,14},{6,10},{2,6},{0,2},{5,1},{9,5},... | collective-permute-start | bytes 786440 | tf_op jit(solution)/shard_map/ppermute | solution.py:346
  19.2 9.2 %collective-permute-start.5 = (bf16[64,2048]{1,0:T(8,128)(2,1)S(1)}, bf16[64,2048]{1,0:T(8,128)(2,1)S(1)}, u32[]{:S(2)}, u32[]{:S(2)}) collective-permute-start(bf16[64,2048]{1,0:T(8,128)(2,1)S(1)} %collective-permute-done.refs_0_), channel_id=1, source_target_pairs={{0,4},{4,8},{8,12},{12,14},{14,10},{10,6},{6,2},{2,0},{1,5},{5,9},... | collective-permute-start | bytes 786440 | tf_op jit(solution)/shard_map/ppermute | solution.py:345
  21.0 15.6 %collective-permute-start.6 = (bf16[64,2048]{1,0:T(8,128)(2,1)S(1)}, bf16[64,2048]{1,0:T(8,128)(2,1)S(1)}, u32[]{:S(2)}, u32[]{:S(2)}) collective-permute-start(bf16[64,2048]{1,0:T(8,128)(2,1)S(1)} %collective-permute-done.1.refs_1_), channel_id=1, source_target_pairs={{4,0},{8,4},{12,8},{14,12},{10,14},{6,10},{2,6},{0,2},{5,1},{9,5},... | collective-permute-start | bytes 786440 | tf_op jit(solution)/shard_map/ppermute | solution.py:346
  21.2 15.8 %collective-permute-start.7 = (bf16[64,2176]{1,0:T(8,128)(2,1)S(1)}, bf16[64,2176]{1,0:T(8,128)(2,1)S(1)}, u32[]{:S(2)}, u32[]{:S(2)}) collective-permute-start(bf16[64,2176]{1,0:T(8,128)(2,1)S(1)} %collective-permute-done.2.refs_3_), channel_id=1, source_target_pairs={{0,4},{4,8},{8,12},{12,14},{14,10},{10,6},{6,2},{2,0},{1,5},{5,9},... | collective-permute-start | bytes 835592 | tf_op jit(solution)/shard_map/ppermute | solution.py:345
  23.1 11.5 %collective-permute-start.8 = (bf16[64,2176]{1,0:T(8,128)(2,1)S(1)}, bf16[64,2176]{1,0:T(8,128)(2,1)S(1)}, u32[]{:S(2)}, u32[]{:S(2)}) collective-permute-start(bf16[64,2176]{1,0:T(8,128)(2,1)S(1)} %collective-permute-done.3.refs_4_), channel_id=1, source_target_pairs={{4,0},{8,4},{12,8},{14,12},{10,14},{6,10},{2,6},{0,2},{5,1},{9,5},... | collective-permute-start | bytes 835592 | tf_op jit(solution)/shard_map/ppermute | solution.py:346
  34.6 9.6 %collective-permute-start.12 = (bf16[64,2176]{1,0:T(8,128)(2,1)S(1)}, bf16[64,2176]{1,0:T(8,128)(2,1)S(1)}, u32[]{:S(2)}, u32[]{:S(2)}) collective-permute-start(bf16[64,2176]{1,0:T(8,128)(2,1)S(1)} %collective-permute-done.8.refs_3_), channel_id=1, source_target_pairs={{4,0},{8,4},{12,8},{14,12},{10,14},{6,10},{2,6},{0,2},{5,1},{9,5},... | collective-permute-start | bytes 835592 | tf_op jit(solution)/shard_map/ppermute | solution.py:346
  35.0 9.2 %collective-permute-start.9 = (bf16[64,2048]{1,0:T(8,128)(2,1)S(1)}, bf16[64,2048]{1,0:T(8,128)(2,1)S(1)}, u32[]{:S(2)}, u32[]{:S(2)}) collective-permute-start(bf16[64,2048]{1,0:T(8,128)(2,1)S(1)} %collective-permute-done.5.refs_0_), channel_id=1, source_target_pairs={{0,4},{4,8},{8,12},{12,14},{14,10},{10,6},{6,2},{2,0},{1,5},{5,9},... | collective-permute-start | bytes 786440 | tf_op jit(solution)/shard_map/ppermute | solution.py:345
  36.6 13.2 %collective-permute-start.10 = (bf16[64,2048]{1,0:T(8,128)(2,1)S(1)}, bf16[64,2048]{1,0:T(8,128)(2,1)S(1)}, u32[]{:S(2)}, u32[]{:S(2)}) collective-permute-start(bf16[64,2048]{1,0:T(8,128)(2,1)S(1)} %collective-permute-done.6.refs_1_), channel_id=1, source_target_pairs={{4,0},{8,4},{12,8},{14,12},{10,14},{6,10},{2,6},{0,2},{5,1},{9,5},... | collective-permute-start | bytes 786440 | tf_op jit(solution)/shard_map/ppermute | solution.py:346
  37.0 13.2 %collective-permute-start.11 = (bf16[64,2176]{1,0:T(8,128)(2,1)S(1)}, bf16[64,2176]{1,0:T(8,128)(2,1)S(1)}, u32[]{:S(2)}, u32[]{:S(2)}) collective-permute-start(bf16[64,2176]{1,0:T(8,128)(2,1)S(1)} %collective-permute-done.7.refs_2_), channel_id=1, source_target_pairs={{0,4},{4,8},{8,12},{12,14},{14,10},{10,6},{6,2},{2,0},{1,5},{5,9},... | collective-permute-start | bytes 835592 | tf_op jit(solution)/shard_map/ppermute | solution.py:345
  44.2 9.5 %collective-permute-start.14 = (bf16[64,2176]{1,0:T(8,128)(2,1)S(1)}, bf16[64,2176]{1,0:T(8,128)(2,1)S(1)}, u32[]{:S(2)}, u32[]{:S(2)}) collective-permute-start(bf16[64,2176]{1,0:T(8,128)(2,1)S(1)} %collective-permute-done.12.refs_3_), channel_id=1, source_target_pairs={{4,0},{8,4},{12,8},{14,12},{10,14},{6,10},{2,6},{0,2},{5,1},{9,5},... | collective-permute-start | bytes 835592 | tf_op jit(solution)/shard_map/ppermute | solution.py:356
  45.8 8.0 %collective-permute-start.13 = (bf16[64,2048]{1,0:T(8,128)(2,1)S(1)}, bf16[64,2048]{1,0:T(8,128)(2,1)S(1)}, u32[]{:S(2)}, u32[]{:S(2)}) collective-permute-start(bf16[64,2048]{1,0:T(8,128)(2,1)S(1)} %collective-permute-done.9.refs_0_), channel_id=1, source_target_pairs={{0,4},{4,8},{8,12},{12,14},{14,10},{10,6},{6,2},{2,0},{1,5},{5,9},... | collective-permute-start | bytes 786440 | tf_op jit(solution)/shard_map/ppermute | solution.py:356
  58.2 6.4 %collective-permute-start.15 = (bf16[64,1024]{1,0:T(8,128)(2,1)S(1)}, bf16[64,1024]{1,0:T(8,128)(2,1)S(1)}, u32[]{:S(2)}, u32[]{:S(2)}) collective-permute-start(bf16[64,1024]{1,0:T(8,128)(2,1)S(1)} %get-tuple-element.77), channel_id=1, source_target_pairs={{4,0},{8,4},{12,8},{14,12},{10,14},{6,10},{2,6},{0,2},{5,1},{9,5},... | collective-permute-start | bytes 393224 | tf_op jit(solution)/shard_map/ppermute | solution.py:326
  59.7 8.0 %collective-permute-start.23 = (bf16[64,1024]{1,0:T(8,128)(2,1)S(1)}, bf16[64,1024]{1,0:T(8,128)(2,1)S(1)}, u32[]{:S(2)}, u32[]{:S(2)}) collective-permute-start(bf16[64,1024]{1,0:T(8,128)(2,1)S(1)} %get-tuple-element.84), channel_id=1, source_target_pairs={{0,4},{4,8},{8,12},{12,14},{14,10},{10,6},{6,2},{2,0},{1,5},{5,9},... | collective-permute-start | bytes 393224 | tf_op jit(solution)/shard_map/ppermute | solution.py:326
  60.3 8.0 %collective-permute-start.17 = (bf16[64,1024]{1,0:T(8,128)(2,1)S(1)}, bf16[64,1024]{1,0:T(8,128)(2,1)S(1)}, u32[]{:S(2)}, u32[]{:S(2)}) collective-permute-start(bf16[64,1024]{1,0:T(8,128)(2,1)S(1)} %get-tuple-element.78), channel_id=1, source_target_pairs={{0,4},{4,8},{8,12},{12,14},{14,10},{10,6},{6,2},{2,0},{1,5},{5,9},... | collective-permute-start | bytes 393224 | tf_op jit(solution)/shard_map/ppermute | solution.py:326
  64.6 5.9 %collective-permute-start.16 = (bf16[64,1024]{1,0:T(8,128)(2,1)S(1)}, bf16[64,1024]{1,0:T(8,128)(2,1)S(1)}, u32[]{:S(2)}, u32[]{:S(2)}) collective-permute-start(bf16[64,1024]{1,0:T(8,128)(2,1)S(1)} %shard_map.117), channel_id=1, source_target_pairs={{4,0},{8,4},{12,8},{14,12},{10,14},{6,10},{2,6},{0,2},{5,1},{9,5},... | collective-permute-start | bytes 393224 | tf_op jit(solution)/shard_map/ppermute | solution.py:326
  66.1 6.7 %collective-permute-start.22 = (bf16[64,1024]{1,0:T(8,128)(2,1)S(1)}, bf16[64,1024]{1,0:T(8,128)(2,1)S(1)}, u32[]{:S(2)}, u32[]{:S(2)}) collective-permute-start(bf16[64,1024]{1,0:T(8,128)(2,1)S(1)} %get-tuple-element.83), channel_id=1, source_target_pairs={{4,0},{8,4},{12,8},{14,12},{10,14},{6,10},{2,6},{0,2},{5,1},{9,5},... | collective-permute-start | bytes 393224 | tf_op jit(solution)/shard_map/ppermute | solution.py:326
  67.7 5.7 %collective-permute-start.24 = (bf16[64,1024]{1,0:T(8,128)(2,1)S(1)}, bf16[64,1024]{1,0:T(8,128)(2,1)S(1)}, u32[]{:S(2)}, u32[]{:S(2)}) collective-permute-start(bf16[64,1024]{1,0:T(8,128)(2,1)S(1)} %shard_map.120), channel_id=1, source_target_pairs={{0,4},{4,8},{8,12},{12,14},{14,10},{10,6},{6,2},{2,0},{1,5},{5,9},... | collective-permute-start | bytes 393224 | tf_op jit(solution)/shard_map/ppermute | solution.py:326
  70.6 5.2 %collective-permute-start.18 = (bf16[64,1024]{1,0:T(8,128)(2,1)S(1)}, bf16[64,1024]{1,0:T(8,128)(2,1)S(1)}, u32[]{:S(2)}, u32[]{:S(2)}) collective-permute-start(bf16[64,1024]{1,0:T(8,128)(2,1)S(1)} %get-tuple-element.79), channel_id=1, source_target_pairs={{4,0},{8,4},{12,8},{14,12},{10,14},{6,10},{2,6},{0,2},{5,1},{9,5},... | collective-permute-start | bytes 393224 | tf_op jit(solution)/shard_map/ppermute | solution.py:326
  71.4 5.0 %collective-permute-start.19 = (bf16[64,1024]{1,0:T(8,128)(2,1)S(1)}, bf16[64,1024]{1,0:T(8,128)(2,1)S(1)}, u32[]{:S(2)}, u32[]{:S(2)}) collective-permute-start(bf16[64,1024]{1,0:T(8,128)(2,1)S(1)} %get-tuple-element.80), channel_id=1, source_target_pairs={{0,4},{4,8},{8,12},{12,14},{14,10},{10,6},{6,2},{2,0},{1,5},{5,9},... | collective-permute-start | bytes 393224 | tf_op jit(solution)/shard_map/ppermute | solution.py:326
  73.5 5.0 %collective-permute-start.25 = (bf16[64,1024]{1,0:T(8,128)(2,1)S(1)}, bf16[64,1024]{1,0:T(8,128)(2,1)S(1)}, u32[]{:S(2)}, u32[]{:S(2)}) collective-permute-start(bf16[64,1024]{1,0:T(8,128)(2,1)S(1)} %get-tuple-element.85), channel_id=1, source_target_pairs={{4,0},{8,4},{12,8},{14,12},{10,14},{6,10},{2,6},{0,2},{5,1},{9,5},... | collective-permute-start | bytes 393224 | tf_op jit(solution)/shard_map/ppermute | solution.py:326
  75.1 5.0 %collective-permute-start.26 = (bf16[64,1024]{1,0:T(8,128)(2,1)S(1)}, bf16[64,1024]{1,0:T(8,128)(2,1)S(1)}, u32[]{:S(2)}, u32[]{:S(2)}) collective-permute-start(bf16[64,1024]{1,0:T(8,128)(2,1)S(1)} %get-tuple-element.86), channel_id=1, source_target_pairs={{0,4},{4,8},{8,12},{12,14},{14,10},{10,6},{6,2},{2,0},{1,5},{5,9},... | collective-permute-start | bytes 393224 | tf_op jit(solution)/shard_map/ppermute | solution.py:326
  75.7 6.5 %collective-permute-start.29 = (f32[32,1216]{1,0:T(8,128)S(1)}, f32[32,1216]{1,0:T(8,128)S(1)}, u32[]{:S(2)}, u32[]{:S(2)}) collective-permute-start(f32[32,1216]{1,0:T(8,128)S(1)} %get-tuple-element.92), channel_id=1, source_target_pairs={{0,1},{1,0},{2,3},{3,2},{4,5},{5,4},{6,7},{7,6},{8,9},{9,8},{10,11... | collective-permute-start | bytes 466952 | tf_op jit(solution)/shard_map/ppermute | solution.py:396
  76.4 6.5 %collective-permute-start.20 = (bf16[64,1024]{1,0:T(8,128)(2,1)S(1)}, bf16[64,1024]{1,0:T(8,128)(2,1)S(1)}, u32[]{:S(2)}, u32[]{:S(2)}) collective-permute-start(bf16[64,1024]{1,0:T(8,128)(2,1)S(1)} %get-tuple-element.81), channel_id=1, source_target_pairs={{4,0},{8,4},{12,8},{14,12},{10,14},{6,10},{2,6},{0,2},{5,1},{9,5},... | collective-permute-start | bytes 393224 | tf_op jit(solution)/shard_map/ppermute | solution.py:326
  78.4 6.2 %collective-permute-start.21 = (bf16[64,1024]{1,0:T(8,128)(2,1)S(1)}, bf16[64,1024]{1,0:T(8,128)(2,1)S(1)}, u32[]{:S(2)}, u32[]{:S(2)}) collective-permute-start(bf16[64,1024]{1,0:T(8,128)(2,1)S(1)} %get-tuple-element.82), channel_id=1, source_target_pairs={{0,4},{4,8},{8,12},{12,14},{14,10},{10,6},{6,2},{2,0},{1,5},{5,9},... | collective-permute-start | bytes 393224 | tf_op jit(solution)/shard_map/ppermute | solution.py:326
  80.1 5.0 %collective-permute-start.27 = (bf16[64,1024]{1,0:T(8,128)(2,1)S(1)}, bf16[64,1024]{1,0:T(8,128)(2,1)S(1)}, u32[]{:S(2)}, u32[]{:S(2)}) collective-permute-start(bf16[64,1024]{1,0:T(8,128)(2,1)S(1)} %get-tuple-element.87), channel_id=1, source_target_pairs={{4,0},{8,4},{12,8},{14,12},{10,14},{6,10},{2,6},{0,2},{5,1},{9,5},... | collective-permute-start | bytes 393224 | tf_op jit(solution)/shard_map/ppermute | solution.py:326
  81.1 5.0 %collective-permute-start.28 = (bf16[64,1024]{1,0:T(8,128)(2,1)S(1)}, bf16[64,1024]{1,0:T(8,128)(2,1)S(1)}, u32[]{:S(2)}, u32[]{:S(2)}) collective-permute-start(bf16[64,1024]{1,0:T(8,128)(2,1)S(1)} %get-tuple-element.88), channel_id=1, source_target_pairs={{0,4},{4,8},{8,12},{12,14},{14,10},{10,6},{6,2},{2,0},{1,5},{5,9},... | collective-permute-start | bytes 393224 | tf_op jit(solution)/shard_map/ppermute | solution.py:326

commit v6 on v5

--- a/solution.py
+++ b/solution.py
@@ -133,10 +133,12 @@
 def prepare_kernel(plan, *refs):
     raw_refs, refs = refs[:3], refs[3:]
     out_grad_ref, ids_ref, route_ref, factor_ref = refs[:4]
-    packed_ref, grads_ref, factor_in_ref, ids_held, route_held, sems = refs[4:]
+    tokens_ref, refs = refs[4], refs[5:]
+    packed_ref, grads_ref, tokens_held_ref, factor_in_ref, ids_held, route_held, sems = refs
     width, rank = plan.hidden_width, plan.rank
     pairs = [(ids_ref, ids_held), (route_ref, route_held)]
     pairs.append((out_grad_ref, grads_ref.at[:, : plan.model_width]))
+    pairs.append((tokens_ref, tokens_held_ref.at[:, : plan.model_width]))
     for kind in range(3):
         for expert in range(plan.experts):
             at = kind * plan.wide + expert * width
@@ -166,7 +168,9 @@
     dense = jnp.zeros((lanes, rows), f32)
     for k in range(ids.shape[0]):
         dense = jnp.where(ids[k : k + 1, :] == expert_at, route[k : k + 1, :], dense)
-    grads_ref[:, plan.model_width :] = dense.T.astype(bf16)
+    dense = dense.T.astype(bf16)
+    grads_ref[:, plan.model_width :] = dense
+    tokens_held_ref[:, plan.model_width :] = dense
     for copy in copies[2:]:
         copy.wait()
 
@@ -186,6 +190,16 @@
         out_specs=(pl.BlockSpec(memory_space=pltpu.VMEM),) * len(incoming),
         compiler_params=pltpu.CompilerParams(vmem_limit_bytes=16 * 1024 * 1024),
     )(rows, *incoming)
+
+
+def half_rows_kernel(half, first_ref, second_ref, top_ref, bottom_ref):
+    top_ref[...] = first_ref[:half]
+    bottom_ref[...] = second_ref[half:]
+
+
+def halves(first, second, half):
+    out = ((half, first.shape[1]), first.dtype)
+    return simple_call(functools.partial(half_rows_kernel, half), [first, second], [out, out])
 
 
 def halves_kernel(plan, total_in_ref, total_out_ref, keep_ref, send_ref):
@@ -275,19 +289,20 @@
     wide, ranks = plan.wide, plan.ranks
 
     lanes = -(-expert_total // lane_count) * lane_count
-    mine, grads, factor_in = pl.pallas_call(
+    mine, grads, tokens_held, factor_in = pl.pallas_call(
         functools.partial(prepare_kernel, plan),
         out_shape=(
             jax.ShapeDtypeStruct((depth, 3 * wide), bf16),
             jax.ShapeDtypeStruct((token_count, model_width + lanes), bf16),
+            jax.ShapeDtypeStruct((token_count, model_width + lanes), bf16),
             jax.ShapeDtypeStruct((ranks, wide), bf16),
         ),
-        in_specs=[pl.BlockSpec(memory_space=pltpu.HBM)] * 7,
-        out_specs=(pl.BlockSpec(memory_space=pltpu.VMEM),) * 3,
+        in_specs=[pl.BlockSpec(memory_space=pltpu.HBM)] * 8,
+        out_specs=(pl.BlockSpec(memory_space=pltpu.VMEM),) * 4,
         scratch_shapes=[
             pltpu.VMEM(expert_ids.shape[::-1], jnp.int32),
             pltpu.VMEM(route_weight.shape[::-1], bf16),
-            pltpu.SemaphoreType.DMA((3 + 4 * local_count,)),
+            pltpu.SemaphoreType.DMA((4 + 4 * local_count,)),
         ],
         compiler_params=pltpu.CompilerParams(vmem_limit_bytes=16 * 1024 * 1024),
     )(
@@ -301,6 +316,7 @@
                 expert_ids.T,
                 route_weight.T,
                 adapter_in,
+                tokens,
             )
         )
     )
@@ -314,7 +330,7 @@
     full = (peer_count - 1) // 2
     split = peer_count % 2 == 0
     totals = (jnp.zeros((ranks, wide), f32), jnp.zeros((ranks, model_width), f32))
-    behind, ahead = [(tokens, grads)], [(tokens, grads)]
+    behind, ahead = [(tokens_held, grads)], [(tokens_held, grads)]
     rows_at = [None]
 
     middle = model_width // 2
@@ -339,8 +355,8 @@
 
     for d in range(full):
         if d > 1:
-            totals, (tokens_b, grads_a) = after(totals, behind[d][0], ahead[d][1])
-            tokens_a, grads_b = ahead[d][0], behind[d][1]
+            totals, (tokens_b, tokens_a) = after(totals, behind[d][0], ahead[d][0])
+            grads_b, grads_a = behind[d][1], ahead[d][1]
             behind[d], ahead[d] = (tokens_b, grads_b), (tokens_a, grads_a)
         behind.append(tuple(lax.ppermute(x, "expert", forward) for x in behind[d]))
         ahead.append(tuple(lax.ppermute(x, "expert", backward) for x in ahead[d]))
@@ -352,20 +368,26 @@
     if not split:
         first_sends += [("left", "back"), ("right", "ahead")]
     if split:
-        totals, (tokens_b, grads_a) = after(totals, behind[full][0], ahead[full][1])
-        far = (lax.ppermute(tokens_b, "expert", forward), lax.ppermute(grads_a, "expert", backward))
+        half = token_count // 2
+        totals, (tokens_b, tokens_a) = after(totals, behind[full][0], ahead[full][0])
+        tokens_b, tokens_a = halves(tokens_b, tokens_a, half)
+        grads_b, grads_a = halves(behind[full][1], ahead[full][1], half)
+        far = [
+            tuple(lax.ppermute(x, "expert", forward) for x in (tokens_b, grads_b)),
+            tuple(lax.ppermute(x, "expert", backward) for x in (tokens_a, grads_a)),
+        ]
     if full > 0:
         pieces = [behind[full], ahead[full]] + ([behind[0]] if full == 1 else [])
         rows_d, *outs = run(pieces, [(ways[way][0], columns[side]) for side, way in first_sends], totals)
         rows_at.append(rows_d)
         totals, ready = outs[:2], outs[2:]
     if split:
-        last, ready = after(far[1], *ready)
-        far = (far[0], last)
+        last, ready = after(far[1][1], *ready)
+        far[1] = (far[1][0], last)
     for (side, way), value in zip(first_sends, ready):
         moving[side, way] = send(value, way)
     if split:
-        _, *outs = run([far], [(0, columns["left"]), (0, columns["right"])], totals)
+        _, *outs = run(far, [(0, columns["left"]), (0, columns["right"])], totals)
         totals = outs[:2]
         moving["left", "back"] = send(outs[2], "back")
         moving["right", "ahead"] = send(outs[3], "ahead")

time: 87 us -> 84.1 us (0.967)
  waiting for transfers between devices: 34.7 us -> 30.5 us
  starting transfers between devices: 31 us -> 32 us
    ppermute x6, waiting for transfers between devices: 9.75 us -> 2.58 us  [per_device(): ahead.append(tuple((lax.ppermute(x, 'expert', backward) for x in ahead[d])))]
    ppermute x6 -> x8, starting transfers between devices: 11.6 us -> 16.1 us  [per_device(): lax.ppermute(x, 'expert', forward)]
    ppermute x6 -> x8, waiting for transfers between devices: 13.9 us -> 16.5 us  [per_device(): lax.ppermute(x, 'expert', forward)]
    ppermute x6, starting transfers between devices: 1.2 us -> 0.02 us  [per_device(): ahead.append(tuple((lax.ppermute(x, 'expert', backward) for x in ahead[d])))]
    ppermute x14, starting transfers between devices: 15.6 us -> 14.5 us  [send(): return lax.ppermute(value, 'expert', ways[way][1])]
    ppermute x2, starting transfers between devices: 2.03 us -> 0.9 us  [per_device(): lax.ppermute(x, 'expert', backward)]
    ppermute x2, waiting for transfers between devices: 0.01 us -> 1 us  [per_device(): lax.ppermute(x, 'expert', backward)]
  transfers between devices with their start and end apart: 30 -> 32, of which waited for: 15 -> 17; matrix products, arithmetic and copies ran while one was open for 0% -> 0% of each run, Pallas kernels for 14% -> 15%
where the time goes in v6:
time: 84.1 us; the launch traced here: 83.9 us
  starting transfers between devices  32 us (38%)
  waiting for transfers between devices  30.5 us (36%)
  Pallas kernels  20.5 us (24%)
    ppermute x8, waiting for transfers between devices, per_device(): lax.ppermute(x, 'expert', forward)  16.5 us
    ppermute x8, starting transfers between devices, per_device(): lax.ppermute(x, 'expert', forward)  16.1 us
    pallas_call x4, Pallas kernels, expert_call(): pl.pallas_call(functools.partial(whole_kernel, plan, len(pieces), blocks)...  16 us
    ppermute x14, starting transfers between devices, send(): return lax.ppermute(value, 'expert', ways[way][1])  14.5 us
    ppermute x14, waiting for transfers between devices, send(): return lax.ppermute(value, 'expert', ways[way][1])  10.5 us
    pallas_call x1, Pallas kernels, per_device(): pl.pallas_call(functools.partial(prepare_kernel, plan), out_shape=(jax.Sh...  2.65 us
    ppermute x6, waiting for transfers between devices, per_device(): ahead.append(tuple((lax.ppermute(x, 'expert', backward) for x in ahead[d])))  2.58 us
  transfers between devices with their start and end apart: 32, of which 17 were waited for; matrix products, arithmetic and copies ran while one was open for 0% of the time, Pallas kernels for 15%

profile of v6, /device:TPU:0, one launch (start us, length us, event | category | flops | bytes accessed | tf_op | source)
XLA Modules:
  0.0 83.9 jit_solution(14763506659745301793)
XLA Ops:
  0.6 2.6 %shard_map.112 = (bf16[1024,2304]{1,0:T(8,128)(2,1)S(1)}, bf16[64,2176]{1,0:T(8,128)(2,1)S(1)}, bf16[64,2176]{1,0:T(8,128)(2,1)S(1)}, bf16[32,768]{1,0:T(8,128)(2,1)S(1)}) custom-call(bf16[2,1024,384]{2,1,0:T(8,128)(2,1)} %refs_0_.1, bf16[2,1024,384]{2,1,0:T(8,128)(2,1)} %refs_1_.1, bf16[2,1024,384]{2,1,0:T(8,128)(2,1)} %refs_2_.1, ...), custom_call_target="tpu_custom_call" | custom-call | tf_op jit(solution)/shard_map/pallas_call | solution.py:292
  3.3 0.5 collective-permute-start.4
  3.8 2.6 %collective-permute-start.2 = (bf16[64,2176]{1,0:T(8,128)(2,1)S(1)}, bf16[64,2176]{1,0:T(8,128)(2,1)S(1)}, u32[]{:S(2)}, u32[]{:S(2)}) collective-permute-start(bf16[64,2176]{1,0:T(8,128)(2,1)S(1)} %get-tuple-element.55.refs_5_), channel_id=1, source_target_pairs={{0,4},{4,8},{8,12},{12,14},{14,10},{10,6},{6,2},{2,0},{1,5},{5,9},... | collective-permute-start | bytes 835592 | tf_op jit(solution)/shard_map/ppermute | solution.py:361
  6.5 2.0 %collective-permute-start = (bf16[64,2176]{1,0:T(8,128)(2,1)S(1)}, bf16[64,2176]{1,0:T(8,128)(2,1)S(1)}, u32[]{:S(2)}, u32[]{:S(2)}) collective-permute-start(bf16[64,2176]{1,0:T(8,128)(2,1)S(1)} %get-tuple-element.54.refs_2_), channel_id=1, source_target_pairs={{0,4},{4,8},{8,12},{12,14},{14,10},{10,6},{6,2},{2,0},{1,5},{5,9},... | collective-permute-start | bytes 835592 | tf_op jit(solution)/shard_map/ppermute | solution.py:361
  8.5 5.4 %collective-permute-done.2.refs_3_ = bf16[64,2176]{1,0:T(8,128)(2,1)S(1)} collective-permute-done((bf16[64,2176]{1,0:T(8,128)(2,1)S(1)}, bf16[64,2176]{1,0:T(8,128)(2,1)S(1)}, u32[]{:S(2)}, u32[]{:S(2)}) %collective-permute-start.2) | collective-permute-done | bytes 278560 | tf_op jit(solution)/shard_map/ppermute | solution.py:361
  13.9 2.0 %collective-permute-start.7 = (bf16[64,2176]{1,0:T(8,128)(2,1)S(1)}, bf16[64,2176]{1,0:T(8,128)(2,1)S(1)}, u32[]{:S(2)}, u32[]{:S(2)}) collective-permute-start(bf16[64,2176]{1,0:T(8,128)(2,1)S(1)} %collective-permute-done.2.refs_3_), channel_id=1, source_target_pairs={{0,4},{4,8},{8,12},{12,14},{14,10},{10,6},{6,2},{2,0},{1,5},{5,9},... | collective-permute-start | bytes 835592 | tf_op jit(solution)/shard_map/ppermute | solution.py:361
  16.0 3.9 %collective-permute-done.refs_0_ = bf16[64,2176]{1,0:T(8,128)(2,1)S(1)} collective-permute-done((bf16[64,2176]{1,0:T(8,128)(2,1)S(1)}, bf16[64,2176]{1,0:T(8,128)(2,1)S(1)}, u32[]{:S(2)}, u32[]{:S(2)}) %collective-permute-start) | collective-permute-done | bytes 278560 | tf_op jit(solution)/shard_map/ppermute | solution.py:361
  19.9 2.0 %collective-permute-start.5 = (bf16[64,2176]{1,0:T(8,128)(2,1)S(1)}, bf16[64,2176]{1,0:T(8,128)(2,1)S(1)}, u32[]{:S(2)}, u32[]{:S(2)}) collective-permute-start(bf16[64,2176]{1,0:T(8,128)(2,1)S(1)} %collective-permute-done.refs_0_), channel_id=1, source_target_pairs={{0,4},{4,8},{8,12},{12,14},{14,10},{10,6},{6,2},{2,0},{1,5},{5,9},... | collective-permute-start | bytes 835592 | tf_op jit(solution)/shard_map/ppermute | solution.py:361
  21.9 3.9 %collective-permute-done.7.refs_2_ = bf16[64,2176]{1,0:T(8,128)(2,1)S(1)} collective-permute-done((bf16[64,2176]{1,0:T(8,128)(2,1)S(1)}, bf16[64,2176]{1,0:T(8,128)(2,1)S(1)}, u32[]{:S(2)}, u32[]{:S(2)}) %collective-permute-start.7) | collective-permute-done | bytes 278560 | tf_op jit(solution)/shard_map/ppermute | solution.py:361
  25.8 2.0 %collective-permute-start.11 = (bf16[64,2176]{1,0:T(8,128)(2,1)S(1)}, bf16[64,2176]{1,0:T(8,128)(2,1)S(1)}, u32[]{:S(2)}, u32[]{:S(2)}) collective-permute-start(bf16[64,2176]{1,0:T(8,128)(2,1)S(1)} %collective-permute-done.7.refs_2_), channel_id=1, source_target_pairs={{0,4},{4,8},{8,12},{12,14},{14,10},{10,6},{6,2},{2,0},{1,5},{5,9},... | collective-permute-start | bytes 835592 | tf_op jit(solution)/shard_map/ppermute | solution.py:361
  27.9 4.4 %shard_map.113 = (f32[192,2048]{1,0:T(8,128)S(1)}, f32[32,768]{1,0:T(8,128)S(1)}, f32[32,2048]{1,0:T(8,128)S(1)}) custom-call(bf16[64,2176]{1,0:T(8,128)(2,1)S(1)} %collective-permute-done.refs_0_, bf16[64,2176]{1,0:T(8,128)(2,1)S(1)} %collective-permute-done.1.refs_1_, bf16[64,2176]{1,0:T(8,128)(2,1)S(1)} %get-tuple-element.54.refs_2_, ...), custom_call_target="tpu_custom_call" | custom-call | flops 3019898880 | bytes 11649024 | tf_op jit(solution)/shard_map/pallas_call | solution.py:251
  32.4 2.1 %collective-permute-start.9 = (bf16[64,2176]{1,0:T(8,128)(2,1)S(1)}, bf16[64,2176]{1,0:T(8,128)(2,1)S(1)}, u32[]{:S(2)}, u32[]{:S(2)}) collective-permute-start(bf16[64,2176]{1,0:T(8,128)(2,1)S(1)} %collective-permute-done.5.refs_0_), channel_id=1, source_target_pairs={{0,4},{4,8},{8,12},{12,14},{14,10},{10,6},{6,2},{2,0},{1,5},{5,9},... | collective-permute-start | bytes 835592 | tf_op jit(solution)/shard_map/ppermute | solution.py:361
  34.5 3.3 %collective-permute-done.11.refs_2_.first_ref = bf16[64,2176]{1,0:T(8,128)(2,1)S(1)} collective-permute-done((bf16[64,2176]{1,0:T(8,128)(2,1)S(1)}, bf16[64,2176]{1,0:T(8,128)(2,1)S(1)}, u32[]{:S(2)}, u32[]{:S(2)}) %collective-permute-start.11) | collective-permute-done | bytes 278560 | tf_op jit(solution)/shard_map/ppermute | solution.py:361
  37.8 2.1 %collective-permute-done.12.refs_3_.second_ref = bf16[64,2176]{1,0:T(8,128)(2,1)S(1)} collective-permute-done((bf16[64,2176]{1,0:T(8,128)(2,1)S(1)}, bf16[64,2176]{1,0:T(8,128)(2,1)S(1)}, u32[]{:S(2)}, u32[]{:S(2)}) %collective-permute-start.12) | collective-permute-done | bytes 278560 | tf_op jit(solution)/shard_map/ppermute | solution.py:362
  39.9 1.6 %collective-permute-start.15 = (bf16[32,2176]{1,0:T(8,128)(2,1)S(1)}, bf16[32,2176]{1,0:T(8,128)(2,1)S(1)}, u32[]{:S(2)}, u32[]{:S(2)}) collective-permute-start(bf16[32,2176]{1,0:T(8,128)(2,1)S(1)} %get-tuple-element.79), channel_id=1, source_target_pairs={{0,4},{4,8},{8,12},{12,14},{14,10},{10,6},{6,2},{2,0},{1,5},{5,9},... | collective-permute-start | bytes 417800 | tf_op jit(solution)/shard_map/ppermute | solution.py:376
  41.5 0.4 collective-permute-start.16
  41.9 3.5 %shard_map.114 = (f32[128,2048]{1,0:T(8,128)S(1)}, f32[32,768]{1,0:T(8,128)S(1)}, f32[32,2048]{1,0:T(8,128)S(1)}) custom-call(bf16[64,2176]{1,0:T(8,128)(2,1)S(1)} %collective-permute-done.5.refs_0_, bf16[64,2176]{1,0:T(8,128)(2,1)S(1)} %collective-permute-done.6.refs_1_, bf16[64,2176]{1,0:T(8,128)(2,1)S(1)} %collective-permute-done.7.refs_2_, ...), custom_call_target="tpu_custom_call" | custom-call | flops 2013265920 | bytes 11091968 | tf_op jit(solution)/shard_map/pallas_call | solution.py:251
  45.4 0.4 collective-permute-done.10.refs_1_.second_ref
  45.8 1.6 %collective-permute-start.13 = (bf16[32,2176]{1,0:T(8,128)(2,1)S(1)}, bf16[32,2176]{1,0:T(8,128)(2,1)S(1)}, u32[]{:S(2)}, u32[]{:S(2)}) collective-permute-start(bf16[32,2176]{1,0:T(8,128)(2,1)S(1)} %get-tuple-element.77), channel_id=1, source_target_pairs={{0,4},{4,8},{8,12},{12,14},{14,10},{10,6},{6,2},{2,0},{1,5},{5,9},... | collective-permute-start | bytes 417800 | tf_op jit(solution)/shard_map/ppermute | solution.py:376
  47.5 0.5 collective-permute-start.14
  47.9 3.6 %shard_map.115 = (f32[128,2048]{1,0:T(8,128)S(1)}, f32[32,768]{1,0:T(8,128)S(1)}, f32[32,2048]{1,0:T(8,128)S(1)}, bf16[64,1024]{1,0:T(8,128)(2,1)S(1)}, bf16[64,1024]{1,0:T(8,128)(2,1)S(1)}) custom-call(bf16[64,2176]{1,0:T(8,128)(2,1)S(1)} %collective-permute-done.9.refs_0_.first_ref, bf16[64,2176]{1,0:T(8,128)(2,1)S(1)} %collective-permute-done.10.refs_1_.second_ref, ...), custom_call_target="tpu_custom_call" | custom-call | flops 2013265920 | bytes 11091968 | tf_op jit(solution)/shard_map/pallas_call | solution.py:251
  51.5 1.0 %collective-permute-done.14.refs_1_ = bf16[32,2176]{1,0:T(8,128)(2,1)S(1)} collective-permute-done((bf16[32,2176]{1,0:T(8,128)(2,1)S(1)}, bf16[32,2176]{1,0:T(8,128)(2,1)S(1)}, u32[]{:S(2)}, u32[]{:S(2)}) %collective-permute-start.14) | collective-permute-done | bytes 139296 | tf_op jit(solution)/shard_map/ppermute | solution.py:377
  52.5 4.5 %shard_map.118 = (f32[64,2048]{1,0:T(8,128)}, f32[32,768]{1,0:T(8,128)S(1)}, f32[32,2048]{1,0:T(8,128)S(1)}, bf16[64,1024]{1,0:T(8,128)(2,1)S(1)}, bf16[64,1024]{1,0:T(8,128)(2,1)S(1)}) custom-call(bf16[32,2176]{1,0:T(8,128)(2,1)S(1)} %collective-permute-done.13.refs_0_, bf16[32,2176]{1,0:T(8,128)(2,1)S(1)} %collective-permute-done.14.refs_1_, ...), custom_call_target="tpu_custom_call" | custom-call | flops 1006632960 | bytes 10534912 | tf_op jit(solution)/shard_map/pallas_call | solution.py:251
  57.0 0.4 collective-permute-start.17
  57.4 1.6 %collective-permute-start.25 = (bf16[64,1024]{1,0:T(8,128)(2,1)S(1)}, bf16[64,1024]{1,0:T(8,128)(2,1)S(1)}, u32[]{:S(2)}, u32[]{:S(2)}) collective-permute-start(bf16[64,1024]{1,0:T(8,128)(2,1)S(1)} %get-tuple-element.94), channel_id=1, source_target_pairs={{0,4},{4,8},{8,12},{12,14},{14,10},{10,6},{6,2},{2,0},{1,5},{5,9},... | collective-permute-start | bytes 393224 | tf_op jit(solution)/shard_map/ppermute | solution.py:342
  59.0 1.6 %collective-permute-start.19 = (bf16[64,1024]{1,0:T(8,128)(2,1)S(1)}, bf16[64,1024]{1,0:T(8,128)(2,1)S(1)}, u32[]{:S(2)}, u32[]{:S(2)}) collective-permute-start(bf16[64,1024]{1,0:T(8,128)(2,1)S(1)} %get-tuple-element.88), channel_id=1, source_target_pairs={{0,4},{4,8},{8,12},{12,14},{14,10},{10,6},{6,2},{2,0},{1,5},{5,9},... | collective-permute-start | bytes 393224 | tf_op jit(solution)/shard_map/ppermute | solution.py:342
  60.6 2.5 %collective-permute-done.17.refs_1_ = bf16[64,1024]{1,0:T(8,128)(2,1)S(1)} collective-permute-done((bf16[64,1024]{1,0:T(8,128)(2,1)S(1)}, bf16[64,1024]{1,0:T(8,128)(2,1)S(1)}, u32[]{:S(2)}, u32[]{:S(2)}) %collective-permute-start.17) | collective-permute-done | bytes 131104 | tf_op jit(solution)/shard_map/ppermute | solution.py:342
  63.1 0.5 collective-permute-start.18
  63.7 2.0 %collective-permute-start.26 = (bf16[64,1024]{1,0:T(8,128)(2,1)S(1)}, bf16[64,1024]{1,0:T(8,128)(2,1)S(1)}, u32[]{:S(2)}, u32[]{:S(2)}) collective-permute-start(bf16[64,1024]{1,0:T(8,128)(2,1)S(1)} %shard_map.122), channel_id=1, source_target_pairs={{0,4},{4,8},{8,12},{12,14},{14,10},{10,6},{6,2},{2,0},{1,5},{5,9},... | collective-permute-start | bytes 393224 | tf_op jit(solution)/shard_map/ppermute | solution.py:342
  65.7 3.7 %collective-permute-done.18.refs_1_ = bf16[64,1024]{1,0:T(8,128)(2,1)S(1)} collective-permute-done((bf16[64,1024]{1,0:T(8,128)(2,1)S(1)}, bf16[64,1024]{1,0:T(8,128)(2,1)S(1)}, u32[]{:S(2)}, u32[]{:S(2)}) %collective-permute-start.18) | collective-permute-done | bytes 131104 | tf_op jit(solution)/shard_map/ppermute | solution.py:342
  69.5 0.5 collective-permute-start.20
  70.0 1.6 %collective-permute-start.21 = (bf16[64,1024]{1,0:T(8,128)(2,1)S(1)}, bf16[64,1024]{1,0:T(8,128)(2,1)S(1)}, u32[]{:S(2)}, u32[]{:S(2)}) collective-permute-start(bf16[64,1024]{1,0:T(8,128)(2,1)S(1)} %get-tuple-element.90), channel_id=1, source_target_pairs={{0,4},{4,8},{8,12},{12,14},{14,10},{10,6},{6,2},{2,0},{1,5},{5,9},... | collective-permute-start | bytes 393224 | tf_op jit(solution)/shard_map/ppermute | solution.py:342
  71.6 0.2 collective-permute-done.24.refs_1_
  71.9 0.5 collective-permute-start.27
  72.4 1.6 %collective-permute-start.28 = (bf16[64,1024]{1,0:T(8,128)(2,1)S(1)}, bf16[64,1024]{1,0:T(8,128)(2,1)S(1)}, u32[]{:S(2)}, u32[]{:S(2)}) collective-permute-start(bf16[64,1024]{1,0:T(8,128)(2,1)S(1)} %get-tuple-element.96), channel_id=1, source_target_pairs={{0,4},{4,8},{8,12},{12,14},{14,10},{10,6},{6,2},{2,0},{1,5},{5,9},... | collective-permute-start | bytes 393224 | tf_op jit(solution)/shard_map/ppermute | solution.py:342
  73.9 0.1 shard_map.126
  74.1 0.4 collective-permute-done.20.refs_1_
  74.5 0.4 collective-permute-done.21.refs_2_
  75.2 2.0 %collective-permute-start.23 = (bf16[64,1024]{1,0:T(8,128)(2,1)S(1)}, bf16[64,1024]{1,0:T(8,128)(2,1)S(1)}, u32[]{:S(2)}, u32[]{:S(2)}) collective-permute-start(bf16[64,1024]{1,0:T(8,128)(2,1)S(1)} %get-tuple-element.92), channel_id=1, source_target_pairs={{0,4},{4,8},{8,12},{12,14},{14,10},{10,6},{6,2},{2,0},{1,5},{5,9},... | collective-permute-start | bytes 393224 | tf_op jit(solution)/shard_map/ppermute | solution.py:342
  77.1 0.2 collective-permute-done.28.refs_2_
  77.4 0.3 collective-permute-start.29
  77.7 1.8 %collective-permute-start.30 = (bf16[64,1024]{1,0:T(8,128)(2,1)S(1)}, bf16[64,1024]{1,0:T(8,128)(2,1)S(1)}, u32[]{:S(2)}, u32[]{:S(2)}) collective-permute-start(bf16[64,1024]{1,0:T(8,128)(2,1)S(1)} %get-tuple-element.98), channel_id=1, source_target_pairs={{0,4},{4,8},{8,12},{12,14},{14,10},{10,6},{6,2},{2,0},{1,5},{5,9},... | collective-permute-start | bytes 393224 | tf_op jit(solution)/shard_map/ppermute | solution.py:342
  79.5 0.7 shard_map.127
  80.1 1.2 %collective-permute-done.22.refs_1_ = bf16[64,1024]{1,0:T(8,128)(2,1)S(1)} collective-permute-done((bf16[64,1024]{1,0:T(8,128)(2,1)S(1)}, bf16[64,1024]{1,0:T(8,128)(2,1)S(1)}, u32[]{:S(2)}, u32[]{:S(2)}) %collective-permute-start.22) | collective-permute-done | bytes 131104 | tf_op jit(solution)/shard_map/ppermute | solution.py:342
  81.4 0.2 collective-permute-done.23.refs_2_
  81.5 1.4 %collective-permute-done.29.refs_3_ = bf16[64,1024]{1,0:T(8,128)(2,1)S(1)} collective-permute-done((bf16[64,1024]{1,0:T(8,128)(2,1)S(1)}, bf16[64,1024]{1,0:T(8,128)(2,1)S(1)}, u32[]{:S(2)}, u32[]{:S(2)}) %collective-permute-start.29) | collective-permute-done | bytes 131104 | tf_op jit(solution)/shard_map/ppermute | solution.py:342
  83.0 0.2 collective-permute-done.30.refs_4_
  83.1 0.8 shard_map.125
  (36 shorter events, 0.7 us)
Async XLA Ops:
  0.6 27.3 %copy-start = (bf16[2,16,2048]{2,1,0:T(8,128)(2,1)S(1)}, bf16[2,16,2048]{2,1,0:T(8,128)(2,1)}, u32[]{:S(2)}) copy-start(bf16[2,16,2048]{2,1,0:T(8,128)(2,1)} %param.17) | copy-start | bytes 393220
  3.3 24.6 %collective-permute-start.4 = (bf16[1024,2304]{1,0:T(8,128)(2,1)S(1)}, bf16[1024,2304]{1,0:T(8,128)(2,1)S(1)}, u32[]{:S(2)}, u32[]{:S(2)}) collective-permute-start(bf16[1024,2304]{1,0:T(8,128)(2,1)S(1)} %get-tuple-element.57.refs_8_.refs_6_), channel_id=1, source_target_pairs={{0,1},{1,0},{2,3},{3,2},{4,5},{5,4},{6,7},{7,6},{8,9},{9,8},{10,11... | collective-permute-start | bytes 14155784 | tf_op jit(solution)/shard_map/ppermute | solution.py:324
  3.8 10.1 %collective-permute-start.2 = (bf16[64,2176]{1,0:T(8,128)(2,1)S(1)}, bf16[64,2176]{1,0:T(8,128)(2,1)S(1)}, u32[]{:S(2)}, u32[]{:S(2)}) collective-permute-start(bf16[64,2176]{1,0:T(8,128)(2,1)S(1)} %get-tuple-element.55.refs_5_), channel_id=1, source_target_pairs={{0,4},{4,8},{8,12},{12,14},{14,10},{10,6},{6,2},{2,0},{1,5},{5,9},... | collective-permute-start | bytes 835592 | tf_op jit(solution)/shard_map/ppermute | solution.py:361
  6.5 9.5 %collective-permute-start.3 = (bf16[64,2176]{1,0:T(8,128)(2,1)S(1)}, bf16[64,2176]{1,0:T(8,128)(2,1)S(1)}, u32[]{:S(2)}, u32[]{:S(2)}) collective-permute-start(bf16[64,2176]{1,0:T(8,128)(2,1)S(1)} %get-tuple-element.55.refs_5_), channel_id=1, source_target_pairs={{4,0},{8,4},{12,8},{14,12},{10,14},{6,10},{2,6},{0,2},{5,1},{9,5},... | collective-permute-start | bytes 835592 | tf_op jit(solution)/shard_map/ppermute | solution.py:362
  6.5 13.4 %collective-permute-start = (bf16[64,2176]{1,0:T(8,128)(2,1)S(1)}, bf16[64,2176]{1,0:T(8,128)(2,1)S(1)}, u32[]{:S(2)}, u32[]{:S(2)}) collective-permute-start(bf16[64,2176]{1,0:T(8,128)(2,1)S(1)} %get-tuple-element.54.refs_2_), channel_id=1, source_target_pairs={{0,4},{4,8},{8,12},{12,14},{14,10},{10,6},{6,2},{2,0},{1,5},{5,9},... | collective-permute-start | bytes 835592 | tf_op jit(solution)/shard_map/ppermute | solution.py:361
  8.5 13.4 %collective-permute-start.1 = (bf16[64,2176]{1,0:T(8,128)(2,1)S(1)}, bf16[64,2176]{1,0:T(8,128)(2,1)S(1)}, u32[]{:S(2)}, u32[]{:S(2)}) collective-permute-start(bf16[64,2176]{1,0:T(8,128)(2,1)S(1)} %get-tuple-element.54.refs_2_), channel_id=1, source_target_pairs={{4,0},{8,4},{12,8},{14,12},{10,14},{6,10},{2,6},{0,2},{5,1},{9,5},... | collective-permute-start | bytes 835592 | tf_op jit(solution)/shard_map/ppermute | solution.py:362
  13.9 11.9 %collective-permute-start.7 = (bf16[64,2176]{1,0:T(8,128)(2,1)S(1)}, bf16[64,2176]{1,0:T(8,128)(2,1)S(1)}, u32[]{:S(2)}, u32[]{:S(2)}) collective-permute-start(bf16[64,2176]{1,0:T(8,128)(2,1)S(1)} %collective-permute-done.2.refs_3_), channel_id=1, source_target_pairs={{0,4},{4,8},{8,12},{12,14},{14,10},{10,6},{6,2},{2,0},{1,5},{5,9},... | collective-permute-start | bytes 835592 | tf_op jit(solution)/shard_map/ppermute | solution.py:361
  16.0 11.9 %collective-permute-start.8 = (bf16[64,2176]{1,0:T(8,128)(2,1)S(1)}, bf16[64,2176]{1,0:T(8,128)(2,1)S(1)}, u32[]{:S(2)}, u32[]{:S(2)}) collective-permute-start(bf16[64,2176]{1,0:T(8,128)(2,1)S(1)} %collective-permute-done.3.refs_4_), channel_id=1, source_target_pairs={{4,0},{8,4},{12,8},{14,12},{10,14},{6,10},{2,6},{0,2},{5,1},{9,5},... | collective-permute-start | bytes 835592 | tf_op jit(solution)/shard_map/ppermute | solution.py:362
  19.9 12.5 %collective-permute-start.5 = (bf16[64,2176]{1,0:T(8,128)(2,1)S(1)}, bf16[64,2176]{1,0:T(8,128)(2,1)S(1)}, u32[]{:S(2)}, u32[]{:S(2)}) collective-permute-start(bf16[64,2176]{1,0:T(8,128)(2,1)S(1)} %collective-permute-done.refs_0_), channel_id=1, source_target_pairs={{0,4},{4,8},{8,12},{12,14},{14,10},{10,6},{6,2},{2,0},{1,5},{5,9},... | collective-permute-start | bytes 835592 | tf_op jit(solution)/shard_map/ppermute | solution.py:361
  21.9 12.5 %collective-permute-start.6 = (bf16[64,2176]{1,0:T(8,128)(2,1)S(1)}, bf16[64,2176]{1,0:T(8,128)(2,1)S(1)}, u32[]{:S(2)}, u32[]{:S(2)}) collective-permute-start(bf16[64,2176]{1,0:T(8,128)(2,1)S(1)} %collective-permute-done.1.refs_1_), channel_id=1, source_target_pairs={{4,0},{8,4},{12,8},{14,12},{10,14},{6,10},{2,6},{0,2},{5,1},{9,5},... | collective-permute-start | bytes 835592 | tf_op jit(solution)/shard_map/ppermute | solution.py:362
  25.8 11.9 %collective-permute-start.11 = (bf16[64,2176]{1,0:T(8,128)(2,1)S(1)}, bf16[64,2176]{1,0:T(8,128)(2,1)S(1)}, u32[]{:S(2)}, u32[]{:S(2)}) collective-permute-start(bf16[64,2176]{1,0:T(8,128)(2,1)S(1)} %collective-permute-done.7.refs_2_), channel_id=1, source_target_pairs={{0,4},{4,8},{8,12},{12,14},{14,10},{10,6},{6,2},{2,0},{1,5},{5,9},... | collective-permute-start | bytes 835592 | tf_op jit(solution)/shard_map/ppermute | solution.py:361
  27.9 11.9 %collective-permute-start.12 = (bf16[64,2176]{1,0:T(8,128)(2,1)S(1)}, bf16[64,2176]{1,0:T(8,128)(2,1)S(1)}, u32[]{:S(2)}, u32[]{:S(2)}) collective-permute-start(bf16[64,2176]{1,0:T(8,128)(2,1)S(1)} %collective-permute-done.8.refs_3_), channel_id=1, source_target_pairs={{4,0},{8,4},{12,8},{14,12},{10,14},{6,10},{2,6},{0,2},{5,1},{9,5},... | collective-permute-start | bytes 835592 | tf_op jit(solution)/shard_map/ppermute | solution.py:362
  32.4 13.0 %collective-permute-start.9 = (bf16[64,2176]{1,0:T(8,128)(2,1)S(1)}, bf16[64,2176]{1,0:T(8,128)(2,1)S(1)}, u32[]{:S(2)}, u32[]{:S(2)}) collective-permute-start(bf16[64,2176]{1,0:T(8,128)(2,1)S(1)} %collective-permute-done.5.refs_0_), channel_id=1, source_target_pairs={{0,4},{4,8},{8,12},{12,14},{14,10},{10,6},{6,2},{2,0},{1,5},{5,9},... | collective-permute-start | bytes 835592 | tf_op jit(solution)/shard_map/ppermute | solution.py:361
  34.5 11.3 %collective-permute-start.10 = (bf16[64,2176]{1,0:T(8,128)(2,1)S(1)}, bf16[64,2176]{1,0:T(8,128)(2,1)S(1)}, u32[]{:S(2)}, u32[]{:S(2)}) collective-permute-start(bf16[64,2176]{1,0:T(8,128)(2,1)S(1)} %collective-permute-done.6.refs_1_), channel_id=1, source_target_pairs={{4,0},{8,4},{12,8},{14,12},{10,14},{6,10},{2,6},{0,2},{5,1},{9,5},... | collective-permute-start | bytes 835592 | tf_op jit(solution)/shard_map/ppermute | solution.py:362
  39.9 11.6 %collective-permute-start.15 = (bf16[32,2176]{1,0:T(8,128)(2,1)S(1)}, bf16[32,2176]{1,0:T(8,128)(2,1)S(1)}, u32[]{:S(2)}, u32[]{:S(2)}) collective-permute-start(bf16[32,2176]{1,0:T(8,128)(2,1)S(1)} %get-tuple-element.79), channel_id=1, source_target_pairs={{0,4},{4,8},{8,12},{12,14},{14,10},{10,6},{6,2},{2,0},{1,5},{5,9},... | collective-permute-start | bytes 417800 | tf_op jit(solution)/shard_map/ppermute | solution.py:376
  41.5 10.0 %collective-permute-start.16 = (bf16[32,2176]{1,0:T(8,128)(2,1)S(1)}, bf16[32,2176]{1,0:T(8,128)(2,1)S(1)}, u32[]{:S(2)}, u32[]{:S(2)}) collective-permute-start(bf16[32,2176]{1,0:T(8,128)(2,1)S(1)} %get-tuple-element.82), channel_id=1, source_target_pairs={{4,0},{8,4},{12,8},{14,12},{10,14},{6,10},{2,6},{0,2},{5,1},{9,5},... | collective-permute-start | bytes 417800 | tf_op jit(solution)/shard_map/ppermute | solution.py:377
  45.8 5.7 %collective-permute-start.13 = (bf16[32,2176]{1,0:T(8,128)(2,1)S(1)}, bf16[32,2176]{1,0:T(8,128)(2,1)S(1)}, u32[]{:S(2)}, u32[]{:S(2)}) collective-permute-start(bf16[32,2176]{1,0:T(8,128)(2,1)S(1)} %get-tuple-element.77), channel_id=1, source_target_pairs={{0,4},{4,8},{8,12},{12,14},{14,10},{10,6},{6,2},{2,0},{1,5},{5,9},... | collective-permute-start | bytes 417800 | tf_op jit(solution)/shard_map/ppermute | solution.py:376
  47.5 5.1 %collective-permute-start.14 = (bf16[32,2176]{1,0:T(8,128)(2,1)S(1)}, bf16[32,2176]{1,0:T(8,128)(2,1)S(1)}, u32[]{:S(2)}, u32[]{:S(2)}) collective-permute-start(bf16[32,2176]{1,0:T(8,128)(2,1)S(1)} %get-tuple-element.78), channel_id=1, source_target_pairs={{4,0},{8,4},{12,8},{14,12},{10,14},{6,10},{2,6},{0,2},{5,1},{9,5},... | collective-permute-start | bytes 417800 | tf_op jit(solution)/shard_map/ppermute | solution.py:377
  57.0 6.1 %collective-permute-start.17 = (bf16[64,1024]{1,0:T(8,128)(2,1)S(1)}, bf16[64,1024]{1,0:T(8,128)(2,1)S(1)}, u32[]{:S(2)}, u32[]{:S(2)}) collective-permute-start(bf16[64,1024]{1,0:T(8,128)(2,1)S(1)} %get-tuple-element.87), channel_id=1, source_target_pairs={{4,0},{8,4},{12,8},{14,12},{10,14},{6,10},{2,6},{0,2},{5,1},{9,5},... | collective-permute-start | bytes 393224 | tf_op jit(solution)/shard_map/ppermute | solution.py:342
  57.4 6.3 %collective-permute-start.25 = (bf16[64,1024]{1,0:T(8,128)(2,1)S(1)}, bf16[64,1024]{1,0:T(8,128)(2,1)S(1)}, u32[]{:S(2)}, u32[]{:S(2)}) collective-permute-start(bf16[64,1024]{1,0:T(8,128)(2,1)S(1)} %get-tuple-element.94), channel_id=1, source_target_pairs={{0,4},{4,8},{8,12},{12,14},{14,10},{10,6},{6,2},{2,0},{1,5},{5,9},... | collective-permute-start | bytes 393224 | tf_op jit(solution)/shard_map/ppermute | solution.py:342
  59.0 6.7 %collective-permute-start.19 = (bf16[64,1024]{1,0:T(8,128)(2,1)S(1)}, bf16[64,1024]{1,0:T(8,128)(2,1)S(1)}, u32[]{:S(2)}, u32[]{:S(2)}) collective-permute-start(bf16[64,1024]{1,0:T(8,128)(2,1)S(1)} %get-tuple-element.88), channel_id=1, source_target_pairs={{0,4},{4,8},{8,12},{12,14},{14,10},{10,6},{6,2},{2,0},{1,5},{5,9},... | collective-permute-start | bytes 393224 | tf_op jit(solution)/shard_map/ppermute | solution.py:342
  63.1 6.4 %collective-permute-start.18 = (bf16[64,1024]{1,0:T(8,128)(2,1)S(1)}, bf16[64,1024]{1,0:T(8,128)(2,1)S(1)}, u32[]{:S(2)}, u32[]{:S(2)}) collective-permute-start(bf16[64,1024]{1,0:T(8,128)(2,1)S(1)} %shard_map.119), channel_id=1, source_target_pairs={{4,0},{8,4},{12,8},{14,12},{10,14},{6,10},{2,6},{0,2},{5,1},{9,5},... | collective-permute-start | bytes 393224 | tf_op jit(solution)/shard_map/ppermute | solution.py:342
  63.6 8.2 %collective-permute-start.24 = (bf16[64,1024]{1,0:T(8,128)(2,1)S(1)}, bf16[64,1024]{1,0:T(8,128)(2,1)S(1)}, u32[]{:S(2)}, u32[]{:S(2)}) collective-permute-start(bf16[64,1024]{1,0:T(8,128)(2,1)S(1)} %get-tuple-element.93), channel_id=1, source_target_pairs={{4,0},{8,4},{12,8},{14,12},{10,14},{6,10},{2,6},{0,2},{5,1},{9,5},... | collective-permute-start | bytes 393224 | tf_op jit(solution)/shard_map/ppermute | solution.py:342
  63.7 8.1 %collective-permute-start.26 = (bf16[64,1024]{1,0:T(8,128)(2,1)S(1)}, bf16[64,1024]{1,0:T(8,128)(2,1)S(1)}, u32[]{:S(2)}, u32[]{:S(2)}) collective-permute-start(bf16[64,1024]{1,0:T(8,128)(2,1)S(1)} %shard_map.122), channel_id=1, source_target_pairs={{0,4},{4,8},{8,12},{12,14},{14,10},{10,6},{6,2},{2,0},{1,5},{5,9},... | collective-permute-start | bytes 393224 | tf_op jit(solution)/shard_map/ppermute | solution.py:342
  69.5 5.0 %collective-permute-start.20 = (bf16[64,1024]{1,0:T(8,128)(2,1)S(1)}, bf16[64,1024]{1,0:T(8,128)(2,1)S(1)}, u32[]{:S(2)}, u32[]{:S(2)}) collective-permute-start(bf16[64,1024]{1,0:T(8,128)(2,1)S(1)} %get-tuple-element.89), channel_id=1, source_target_pairs={{4,0},{8,4},{12,8},{14,12},{10,14},{6,10},{2,6},{0,2},{5,1},{9,5},... | collective-permute-start | bytes 393224 | tf_op jit(solution)/shard_map/ppermute | solution.py:342
  70.0 5.0 %collective-permute-start.21 = (bf16[64,1024]{1,0:T(8,128)(2,1)S(1)}, bf16[64,1024]{1,0:T(8,128)(2,1)S(1)}, u32[]{:S(2)}, u32[]{:S(2)}) collective-permute-start(bf16[64,1024]{1,0:T(8,128)(2,1)S(1)} %get-tuple-element.90), channel_id=1, source_target_pairs={{0,4},{4,8},{8,12},{12,14},{14,10},{10,6},{6,2},{2,0},{1,5},{5,9},... | collective-permute-start | bytes 393224 | tf_op jit(solution)/shard_map/ppermute | solution.py:342
  71.9 5.3 %collective-permute-start.27 = (bf16[64,1024]{1,0:T(8,128)(2,1)S(1)}, bf16[64,1024]{1,0:T(8,128)(2,1)S(1)}, u32[]{:S(2)}, u32[]{:S(2)}) collective-permute-start(bf16[64,1024]{1,0:T(8,128)(2,1)S(1)} %get-tuple-element.95), channel_id=1, source_target_pairs={{4,0},{8,4},{12,8},{14,12},{10,14},{6,10},{2,6},{0,2},{5,1},{9,5},... | collective-permute-start | bytes 393224 | tf_op jit(solution)/shard_map/ppermute | solution.py:342
  72.4 5.0 %collective-permute-start.28 = (bf16[64,1024]{1,0:T(8,128)(2,1)S(1)}, bf16[64,1024]{1,0:T(8,128)(2,1)S(1)}, u32[]{:S(2)}, u32[]{:S(2)}) collective-permute-start(bf16[64,1024]{1,0:T(8,128)(2,1)S(1)} %get-tuple-element.96), channel_id=1, source_target_pairs={{0,4},{4,8},{8,12},{12,14},{14,10},{10,6},{6,2},{2,0},{1,5},{5,9},... | collective-permute-start | bytes 393224 | tf_op jit(solution)/shard_map/ppermute | solution.py:342
  74.1 5.4 %collective-permute-start.31 = (f32[32,1216]{1,0:T(8,128)S(1)}, f32[32,1216]{1,0:T(8,128)S(1)}, u32[]{:S(2)}, u32[]{:S(2)}) collective-permute-start(f32[32,1216]{1,0:T(8,128)S(1)} %get-tuple-element.102), channel_id=1, source_target_pairs={{0,1},{1,0},{2,3},{3,2},{4,5},{5,4},{6,7},{7,6},{8,9},{9,8},{10,11... | collective-permute-start | bytes 466952 | tf_op jit(solution)/shard_map/ppermute | solution.py:418
  75.0 6.3 %collective-permute-start.22 = (bf16[64,1024]{1,0:T(8,128)(2,1)S(1)}, bf16[64,1024]{1,0:T(8,128)(2,1)S(1)}, u32[]{:S(2)}, u32[]{:S(2)}) collective-permute-start(bf16[64,1024]{1,0:T(8,128)(2,1)S(1)} %get-tuple-element.91), channel_id=1, source_target_pairs={{4,0},{8,4},{12,8},{14,12},{10,14},{6,10},{2,6},{0,2},{5,1},{9,5},... | collective-permute-start | bytes 393224 | tf_op jit(solution)/shard_map/ppermute | solution.py:342
  75.2 6.4 %collective-permute-start.23 = (bf16[64,1024]{1,0:T(8,128)(2,1)S(1)}, bf16[64,1024]{1,0:T(8,128)(2,1)S(1)}, u32[]{:S(2)}, u32[]{:S(2)}) collective-permute-start(bf16[64,1024]{1,0:T(8,128)(2,1)S(1)} %get-tuple-element.92), channel_id=1, source_target_pairs={{0,4},{4,8},{8,12},{12,14},{14,10},{10,6},{6,2},{2,0},{1,5},{5,9},... | collective-permute-start | bytes 393224 | tf_op jit(solution)/shard_map/ppermute | solution.py:342
  77.4 5.6 %collective-permute-start.29 = (bf16[64,1024]{1,0:T(8,128)(2,1)S(1)}, bf16[64,1024]{1,0:T(8,128)(2,1)S(1)}, u32[]{:S(2)}, u32[]{:S(2)}) collective-permute-start(bf16[64,1024]{1,0:T(8,128)(2,1)S(1)} %get-tuple-element.97), channel_id=1, source_target_pairs={{4,0},{8,4},{12,8},{14,12},{10,14},{6,10},{2,6},{0,2},{5,1},{9,5},... | collective-permute-start | bytes 393224 | tf_op jit(solution)/shard_map/ppermute | solution.py:342
  77.7 5.4 %collective-permute-start.30 = (bf16[64,1024]{1,0:T(8,128)(2,1)S(1)}, bf16[64,1024]{1,0:T(8,128)(2,1)S(1)}, u32[]{:S(2)}, u32[]{:S(2)}) collective-permute-start(bf16[64,1024]{1,0:T(8,128)(2,1)S(1)} %get-tuple-element.98), channel_id=1, source_target_pairs={{0,4},{4,8},{8,12},{12,14},{14,10},{10,6},{6,2},{2,0},{1,5},{5,9},... | collective-permute-start | bytes 393224 | tf_op jit(solution)/shard_map/ppermute | solution.py:342

commit v7 on v1

v7 whole, which is shorter than its diff:
```python
import functools

import jax
import jax.numpy as jnp
from jax import lax
from jax.experimental import pallas as pl
from jax.experimental.pallas import tpu as pltpu
from jax.sharding import PartitionSpec as P

adapter_scale = 2.0
f32 = jnp.float32
bf16 = jnp.bfloat16
lane_count = 128


def ring_order(count, snake):
    if snake and count % 2 == 0:
        return list(range(0, count, 2)) + list(range(count - 1, 0, -2))
    return list(range(count))


def matmul(a, b):
    return jnp.dot(a, b, preferred_element_type=f32)


def matmul_bt(a, b):
    return lax.dot_general(a, b, (((1,), (1,)), ((), ())), preferred_element_type=f32)


def matmul_at(a, b):
    return lax.dot_general(a, b, (((0,), (0,)), ((), ())), preferred_element_type=f32)


def stacked(piece_refs, span):
    return jnp.concatenate([ref[:, span] for ref in piece_refs], axis=0)


class Plan:
    def __init__(self, parts, depth, model_width, hidden_width, rank, experts):
        self.parts = parts
        self.depth = depth
        self.model_width = model_width
        self.hidden_width = hidden_width
        self.rank = rank
        self.experts = experts
        self.wide = experts * hidden_width
        self.ranks = experts * rank

    def spans(self, first):
        if self.parts == 1:
            return [slice(first, first + self.model_width)]
        core = lax.axis_index("dp")
        return [
            pl.ds(pl.multiple_of(first + at * self.depth, self.depth), self.depth)
            for at in (core, 1 - core)
        ]

    def scales(self, piece_refs):
        columns = stacked(piece_refs, slice(2 * self.model_width, None)).astype(f32)
        lane = lax.broadcasted_iota(jnp.int32, columns.shape, 1)
        first = lax.axis_index("expert") * self.experts
        return [
            jnp.sum(jnp.where(lane == first + j, columns, 0.0), axis=1, keepdims=True)
            for j in range(self.experts)
        ]

    def spread(self, scales, width):
        rows = scales[0].shape[0]
        at = lax.broadcasted_iota(jnp.int32, (rows, self.experts * width), 1)
        out = jnp.broadcast_to(scales[0], at.shape)
        for j in range(1, self.experts):
            out = jnp.where(at >= j * width, scales[j], out)
        return out


def expert_kernel(plan, pieces, blocks, *refs):
    piece_refs, refs = refs[:pieces], refs[pieces:]
    factor_in_ref, factor_out_ref, refs = refs[0], refs[1], refs[2:]
    weight_refs, refs = refs[: plan.parts], refs[plan.parts :]
    total_in_ref, total_out_ref, rows_ref, sum_in_ref, sum_out_ref, *send_refs = refs
    wide = plan.wide

    gate_pre, up_pre = 0.0, 0.0
    for span, weight in zip(plan.spans(0), weight_refs):
        tokens_in = stacked(piece_refs, span)
        gate_pre += matmul(tokens_in, weight[:, :wide])
        up_pre += matmul(tokens_in, weight[:, wide : 2 * wide])
    adapter_back, grad_down = 0.0, 0.0
    for span, at, weight in zip(plan.spans(plan.model_width), plan.spans(0), weight_refs):
        grad_in = stacked(piece_refs, span)
        adapter_back += matmul_bt(grad_in, factor_out_ref[:, at])
        grad_down += matmul(grad_in, weight[:, 2 * wide :])
    adapter_back = adapter_back.astype(bf16)
    scales = plan.scales(piece_refs)
    logistic = 1.0 / (1.0 + jnp.exp(-gate_pre))
    activation = gate_pre * logistic
    derivative = logistic * (1.0 + gate_pre * (1.0 - logistic))
    hidden = (activation * up_pre).astype(bf16)
    grad_hidden = plan.spread(scales, plan.hidden_width) * (
        grad_down + adapter_scale * matmul(adapter_back, factor_in_ref[...])
    )
    grad_gate = (grad_hidden * up_pre * derivative).astype(bf16)
    grad_up = (grad_hidden * activation).astype(bf16)
    for span, weight in zip(plan.spans(0), weight_refs):
        rows_ref[:, span] = matmul_bt(grad_gate, weight[:, :wide]) + matmul_bt(
            grad_up, weight[:, wide : 2 * wide]
        )
    for first_row, send_ref in zip(blocks, send_refs):
        send_ref[...] = rows_ref[first_row : first_row + send_ref.shape[0], :].astype(bf16)

    rank_scale = plan.spread(scales, plan.rank)
    back_scaled = (rank_scale * adapter_back.astype(f32)).astype(bf16)
    low_scaled = (rank_scale * matmul_bt(hidden, factor_in_ref[...])).astype(bf16)
    grad_all = stacked(piece_refs, slice(plan.model_width, 2 * plan.model_width))
    sum_in_ref[...] = total_in_ref[...] + adapter_scale * matmul_at(back_scaled, hidden)
    sum_out_ref[...] = total_out_ref[...] + adapter_scale * matmul_at(low_scaled, grad_all)


def start_all(pairs, sems):
    copies = [
        pltpu.make_async_copy(source, target, sems.at[at])
        for at, (source, target) in enumerate(pairs)
    ]
    for copy in copies:
        copy.start()
    return copies


def piece_kernel(plan, tokens_ref, grads_ref, ids_ref, route_ref, *refs):
    *piece_refs, ids_held, route_held, sems = refs
    rows = piece_refs[0].shape[0]
    pairs = [(ids_ref, ids_held), (route_ref, route_held)]
    for at, piece_ref in enumerate(piece_refs):
        for kind, source in enumerate((tokens_ref, grads_ref)):
            columns = slice(kind * plan.model_width, (kind + 1) * plan.model_width)
            pairs.append((source.at[at * rows : (at + 1) * rows], piece_ref.at[:, columns]))
    copies = start_all(pairs, sems)
    copies[0].wait()
    copies[1].wait()
    lanes = piece_refs[0].shape[1] - 2 * plan.model_width
    ids, route = ids_held[...], route_held[...].astype(f32)
    expert_at = lax.broadcasted_iota(jnp.int32, (lanes, ids.shape[1]), 0)
    dense = jnp.zeros(expert_at.shape, f32)
    for k in range(ids.shape[0]):
        dense = jnp.where(ids[k : k + 1, :] == expert_at, route[k : k + 1, :], dense)
    dense = dense.T.astype(bf16)
    for at, piece_ref in enumerate(piece_refs):
        piece_ref[:, 2 * plan.model_width :] = dense[at * rows : (at + 1) * rows, :]
    for copy in copies[2:]:
        copy.wait()


def weight_kernel(plan, *refs):
    raw_refs, factor_ref = refs[:3], refs[3]
    packed_ref, factor_in_ref, sems = refs[4:]
    width, rank = plan.hidden_width, plan.rank
    pairs = []
    for kind in range(3):
        for expert in range(plan.experts):
            at = kind * plan.wide + expert * width
            pairs.append((raw_refs[kind].at[expert], packed_ref.at[:, at : at + width]))
    for expert in range(plan.experts):
        block = factor_in_ref.at[
            expert * rank : (expert + 1) * rank, expert * width : (expert + 1) * width
        ]
        pairs.append((factor_ref.at[expert], block))
    copies = start_all(pairs, sems)
    for expert in range(plan.experts):
        for other in range(plan.experts):
            if other != expert:
                factor_in_ref[
                    expert * rank : (expert + 1) * rank, other * width : (other + 1) * width
                ] = jnp.zeros((rank, width), bf16)
    for copy in copies:
        copy.wait()


def add_kernel(first_rows, *refs):
    count = len(first_rows)
    for at, first_row in enumerate(first_rows):
        out = refs[2 * count + at]
        rows = refs[at][first_row : first_row + out.shape[0], :]
        out[...] = (rows + refs[count + at][...].astype(f32)).astype(bf16)


def last_kernel(batches, *refs):
    out_ref = refs[-1]
    for at in range(batches):
        rows_ref, back_ref, ahead_ref = refs[3 * at : 3 * at + 3]
        count = back_ref.shape[0]
        total = rows_ref[:count, :] + back_ref[...].astype(f32) + ahead_ref[...].astype(f32)
        out_ref[at * count : (at + 1) * count, :] = total.astype(bf16)


def halves_kernel(plan, total_in_ref, total_out_ref, keep_ref, send_ref):
    first = lax.axis_index("dp") == 0
    middle, narrow = plan.model_width // 2, plan.hidden_width // 2
    low, high = total_out_ref[:, :middle], total_out_ref[:, middle:]
    keep_ref[:, :middle] = jnp.where(first, low, high)
    send_ref[:, :middle] = jnp.where(first, high, low)
    for expert in range(plan.experts):
        rows = slice(expert * plan.rank, (expert + 1) * plan.rank)
        block = total_in_ref[rows, expert * plan.hidden_width : (expert + 1) * plan.hidden_width]
        low, high = block[:, :narrow], block[:, narrow:]
        keep_ref[rows, middle:] = jnp.where(first, low, high)
        send_ref[rows, middle:] = jnp.where(first, high, low)


def joined_kernel(plan, keep_ref, other_ref, in_ref, out_ref):
    middle = plan.model_width // 2
    for expert in range(plan.experts):
        rows = slice(expert * plan.rank, (expert + 1) * plan.rank)
        out_ref[expert] = keep_ref[rows, :middle] + other_ref[rows, :middle]
        in_ref[expert] = keep_ref[rows, middle:] + other_ref[rows, middle:]


def simple_call(kernel, operands, outs, scratch=(), space=pltpu.VMEM, flops=0, limit=16):
    return pl.pallas_call(
        kernel,
        out_shape=tuple(jax.ShapeDtypeStruct(shape, dtype) for shape, dtype in outs),
        in_specs=[pl.BlockSpec(memory_space=space)] * len(operands),
        out_specs=(pl.BlockSpec(memory_space=pltpu.VMEM),) * len(outs),
        scratch_shapes=list(scratch),
        compiler_params=pltpu.CompilerParams(vmem_limit_bytes=limit * 1024 * 1024),
        cost_estimate=pl.CostEstimate(
            flops=flops,
            bytes_accessed=sum(op.size * op.dtype.itemsize for op in operands),
            transcendentals=0,
        ),
    )(*operands)


def held_in(space, arrays):
    return [pltpu.with_memory_space_constraint(x, space) for x in arrays]


def per_device(
    snake,
    tokens,
    out_grad,
    expert_ids,
    route_weight,
    gate_weight,
    up_weight,
    down_weight,
    adapter_in,
    adapter_out,
):
    peer_count = lax.axis_size("expert")
    dp_count = lax.axis_size("dp")
    token_count, model_width = tokens.shape
    local_count, depth, hidden_width = gate_weight.shape
    rank = adapter_in.shape[1]
    expert_total = local_count * peer_count
    order = ring_order(peer_count, snake)
    forward = [(order[i], order[(i + 1) % peer_count]) for i in range(peer_count)]
    backward = [(b, a) for a, b in forward]
    swap = [(0, 1), (1, 0)]
    parts = 2 if dp_count == 2 else 1
    plan = Plan(parts, depth, model_width, hidden_width, rank, local_count)
    wide, ranks = plan.wide, plan.ranks
    batches = 2
    rows = token_count // batches

    lanes = -(-expert_total // lane_count) * lane_count
    own = simple_call(
        functools.partial(piece_kernel, plan),
        held_in(pltpu.HBM, (tokens, out_grad, expert_ids.T, route_weight.T)),
        [((rows, 2 * model_width + lanes), bf16)] * batches,
        [
            pltpu.VMEM(expert_ids.shape[::-1], jnp.int32),
            pltpu.VMEM(route_weight.shape[::-1], bf16),
            pltpu.SemaphoreType.DMA((2 + 2 * batches,)),
        ],
        pltpu.HBM,
    )

    full = (peer_count - 1) // 2
    split = peer_count % 2 == 0
    ways = {"back": backward, "ahead": forward}
    long_way = ["back", "ahead"]
    short_way = ["ahead", "back"]
    pieces = [{(0, "own"): own[at]} for at in range(batches)]
    after_first = {}

    def behind(value, x):
        return lax.optimization_barrier((x, value))[0]

    totals = [jnp.zeros((ranks, wide), f32), jnp.zeros((ranks, model_width), f32)]
    rows_of = [{} for _ in range(batches)]
    moving = [{} for _ in range(batches)]

    def run_many(members, totals):
        for start in range(0, len(members), 12):
            group = members[start : start + 12]
            sent = [
                (at, key)
                for at, key in group
                if key[0] > 0 and key in ((full + split, long_way[at]), (full, short_way[at]))
            ]
            rows_here, *outs = simple_call(
                functools.partial(
                    expert_kernel, plan, len(group), [group.index(member) * rows for member in sent]
                ),
                [pieces[at][key] for at, key in group] + [factor_in, factor_out, *weights, *totals],
                [((len(group) * rows, model_width), f32)]
                + [(total.shape, f32) for total in totals]
                + [((rows, model_width), bf16)] * len(sent),
                flops=10 * len(group) * rows * model_width * wide,
                limit=24,
            )
            totals = outs[:2]
            for (at, key), value in zip(sent, outs[2:]):
                moving[at][key] = value
            for index, (at, key) in enumerate(group):
                rows_of[at][key] = (rows_here, index * rows)
        return totals

    ties = [(0, 1, 1, 'both')]
    early = [[1]]
    done = []
    for d in range(1, full + 1 + split):
        for at in range(batches):
            for way in ways:
                if d <= full or way == long_way[at]:
                    last = pieces[at].get((d - 1, way), own[at])
                    for kernel, hop, batch, side in ties:
                        if hop == d - full and batch == at and side in (way, "both") and kernel < len(done):
                            last = behind(done[kernel][0], last)
                    opposite = forward if way == "back" else backward
                    pieces[at][d, way] = lax.ppermute(last, "expert", opposite)
        if d == 1:
            mine, factor_in = simple_call(
                functools.partial(weight_kernel, plan),
                held_in(pltpu.HBM, (gate_weight, up_weight, down_weight, adapter_in)),
                [((depth, 3 * wide), bf16), ((ranks, wide), bf16)],
                [pltpu.SemaphoreType.DMA((4 * local_count,))],
                pltpu.HBM,
            )
            if parts == 2:
                weights = [mine, lax.ppermute(mine, "dp", swap)]
            else:
                weights = [lax.all_gather(mine, "dp", axis=0, tiled=True)]
            weights = held_in(pltpu.VMEM, weights)
            factor_out = adapter_out.reshape(ranks, model_width)
        if d == full - 1:
            for kernel in early:
                totals = run_many([(at, key) for at in kernel for key in pieces[at]], totals)
                done.append(totals)

    for at in range(batches):
        totals = run_many([(at, key) for key in pieces[at] if key not in rows_of[at]], totals)

    for d in range(full + split, 0, -1):
        for at in range(batches):
            keys = [(d, way) for way in ways if (d, way) in rows_of[at]]
            added = [key for key in keys if key not in moving[at]]
            if added:
                held = [rows_of[at][key] for key in added]
                values = simple_call(
                    functools.partial(add_kernel, [first_row for _, first_row in held]),
                    [rows_here for rows_here, _ in held]
                    + [moving[at].pop((d + 1, way)) for _, way in added],
                    [((rows, model_width), bf16)] * len(added),
                )
                moving[at].update(zip(added, values))
            for key in keys:
                moving[at][key] = lax.ppermute(moving[at][key], "expert", ways[key[1]])
    operands = []
    for at in range(batches):
        operands += [rows_of[at][0, "own"][0], moving[at][1, "back"], moving[at][1, "ahead"]]
    (grad_tokens,) = simple_call(
        functools.partial(last_kernel, batches), operands, [((token_count, model_width), bf16)]
    )

    narrow = hidden_width // dp_count
    if dp_count == 2:
        middle = model_width // 2
        half = ((ranks, middle + narrow), f32)
        keep, other = simple_call(functools.partial(halves_kernel, plan), totals, [half, half])
        grad_in_all, grad_out_all = simple_call(
            functools.partial(joined_kernel, plan),
            [keep, lax.ppermute(other, "dp", swap)],
            [((local_count, rank, narrow), f32), ((local_count, rank, middle), f32)],
        )
        return (grad_tokens, grad_in_all, grad_out_all)
    grad_in = jnp.stack(
        [
            totals[0][j * rank : (j + 1) * rank, j * hidden_width : (j + 1) * hidden_width]
            for j in range(local_count)
        ]
    )
    both = jnp.concatenate(
        [
            grad_in.reshape(ranks, dp_count, narrow),
            totals[1].reshape(ranks, dp_count, model_width // dp_count),
        ],
        axis=2,
    ).transpose(1, 0, 2)
    summed = lax.psum_scatter(both, "dp", scatter_dimension=0, tiled=False)
    grad_in_all = summed[:, :narrow].reshape(local_count, rank, narrow)
    grad_out_all = summed[:, narrow:].reshape(local_count, rank, model_width // dp_count)
    return (grad_tokens, grad_in_all, grad_out_all)


def solution(mesh):
    snake = mesh.shape["dp"] == 2
    return jax.shard_map(
        functools.partial(per_device, snake),
        mesh=mesh,
        in_specs=(
            P(("group", "expert", "dp"), None),
            P(("group", "expert", "dp"), None),
            P(("group", "expert", "dp"), None),
            P(("group", "expert", "dp"), None),
            P("expert", "dp", None),
            P("expert", "dp", None),
            P("expert", "dp", None),
            P("expert", None, None),
            P("expert", None, None),
        ),
        out_specs=(
            P(("group", "expert", "dp"), None),
            P(("group", "expert"), None, "dp"),
            P(("group", "expert"), None, "dp"),
        ),
        check_vma=False,
    )
```

time: 268 us -> 85.8 us (0.32)
  waiting for transfers between devices: 182 us -> 33.2 us
  blocking collectives: 32.3 us -> 0 us
  starting transfers between devices: 0.49 us -> 32.2 us
  matrix products: 31 us -> 0 us
  Pallas kernels: 0 us -> 19.5 us
  between operations: 14.4 us -> 0.76 us
  local copies, waits for them, and re-layouts: 6.66 us -> 0.03 us
    all_gather x5 -> x0, waiting for transfers between devices: 100 us -> none  [the longest x1 52.6 us: per_device(): all_tokens = lax.all_gather(tokens, 'expert', axis=0, tiled=True)]
    reduce_scatter x2 -> x0, waiting for transfers between devices: 78.7 us -> none  [the longest x1 73.3 us: per_device(): lax.psum_scatter(rows.astype(jnp.bfloat16), 'expert', scatter_dimension=0...]
    ppermute x0 -> x30, waiting for transfers between devices: none -> 33.2 us  [the longest x14 22.3 us: per_device(): pieces[at][d, way] = lax.ppermute(last, 'expert', opposite)]
    all_gather x1 -> x0, blocking collectives: 32.3 us -> none  [per_device(): all_weight = lax.all_gather(dense_weight, 'expert', axis=0, tiled=True)]
    ppermute x0 -> x30, starting transfers between devices: none -> 32.2 us  [the longest x14 16.2 us: per_device(): pieces[at][d, way] = lax.ppermute(last, 'expert', opposite)]
    dot_general x18 -> x0, matrix products: 31 us -> none  [the longest x2 6.33 us: expert_grads(): up_pre = jnp.dot(tokens_in, w_up, preferred_element_type=jnp.float32)]
    pallas_call x0 -> x14, Pallas kernels: none -> 19.5 us  [simple_call(): pl.pallas_call(kernel, out_shape=tuple((jax.ShapeDtypeStruct(shape, dtype...]
    unnamed x47 -> x2, local copies, waits for them, and re-layouts: 6.64 us -> 0.01 us
  transfers between devices with their start and end apart: 8 -> 30, of which waited for: 7 -> 16; matrix products, arithmetic and copies ran while one was open for 9% -> 0% of each run, Pallas kernels for 0% -> 19%
where the time goes in v7:
time: 85.8 us; the launch traced here: 85.7 us
  waiting for transfers between devices  33.2 us (39%)
  starting transfers between devices  32.2 us (38%)
  Pallas kernels  19.5 us (23%)
    ppermute x14, waiting for transfers between devices, per_device(): pieces[at][d, way] = lax.ppermute(last, 'expert', opposite)  22.3 us
    pallas_call x14, Pallas kernels, simple_call(): pl.pallas_call(kernel, out_shape=tuple((jax.ShapeDtypeStruct(shape, dtype...  19.5 us
    ppermute x14, starting transfers between devices, per_device(): pieces[at][d, way] = lax.ppermute(last, 'expert', opposite)  16.2 us
    ppermute x14, starting transfers between devices, per_device(): moving[at][key] = lax.ppermute(moving[at][key], 'expert', ways[key[1]])  15.4 us
    ppermute x14, waiting for transfers between devices, per_device(): moving[at][key] = lax.ppermute(moving[at][key], 'expert', ways[key[1]])  10.9 us
  transfers between devices with their start and end apart: 30, of which 16 were waited for; matrix products, arithmetic and copies ran while one was open for 0% of the time, Pallas kernels for 19%

profile of v7, /device:TPU:0, one launch (start us, length us, event | category | flops | bytes accessed | tf_op | source)
XLA Modules:
  0.0 85.7 jit_solution(17355542502524014835)
XLA Ops:
  0.6 2.4 %shard_map.113 = (bf16[1024,2304]{1,0:T(8,128)(2,1)S(1)}, bf16[32,768]{1,0:T(8,128)(2,1)S(1)}) custom-call(bf16[2,1024,384]{2,1,0:T(8,128)(2,1)} %refs_0_.1, bf16[2,1024,384]{2,1,0:T(8,128)(2,1)} %refs_1_.1, bf16[2,1024,384]{2,1,0:T(8,128)(2,1)} %refs_2_.1, bf16[2,16,384]{2,1,0:T(8,128)(2,1)} %refs_3_.1), custom_call_target="tpu_custom_call" | custom-call | bytes 4743168 | tf_op jit(solution)/shard_map/pallas_call | solution.py:218
  3.1 0.5 collective-permute-start.7
  3.6 1.2 %shard_map.112 = (bf16[32,4224]{1,0:T(8,128)(2,1)S(1)}, bf16[32,4224]{1,0:T(8,128)(2,1)S(1)}) custom-call(bf16[64,2048]{1,0:T(8,128)(2,1)} %tokens_ref.1, bf16[64,2048]{1,0:T(8,128)(2,1)} %grads_ref.1, s32[8,64]{1,0:T(8,128)} %bitcast.6, bf16[8,64]{1,0:T(8,128)(2,1)} %bitcast.7), custom_call_target="tpu_custom_call" | custom-call | bytes 527360 | tf_op jit(solution)/shard_map/pallas_call | solution.py:218
  4.8 2.6 %collective-permute-start = (bf16[32,4224]{1,0:T(8,128)(2,1)S(1)}, bf16[32,4224]{1,0:T(8,128)(2,1)S(1)}, u32[]{:S(2)}, u32[]{:S(2)}) collective-permute-start(bf16[32,4224]{1,0:T(8,128)(2,1)S(1)} %get-tuple-element.33.refs_0_), channel_id=1, source_target_pairs={{0,4},{4,8},{8,12},{12,14},{14,10},{10,6},{6,2},{2,0},{1,5},{5,9},... | collective-permute-start | bytes 811016 | tf_op jit(solution)/shard_map/ppermute | solution.py:331
  7.4 1.9 %collective-permute-start.1 = (bf16[32,4224]{1,0:T(8,128)(2,1)S(1)}, bf16[32,4224]{1,0:T(8,128)(2,1)S(1)}, u32[]{:S(2)}, u32[]{:S(2)}) collective-permute-start(bf16[32,4224]{1,0:T(8,128)(2,1)S(1)} %get-tuple-element.33.refs_0_), channel_id=1, source_target_pairs={{4,0},{8,4},{12,8},{14,12},{10,14},{6,10},{2,6},{0,2},{5,1},{9,5},... | collective-permute-start | bytes 811016 | tf_op jit(solution)/shard_map/ppermute | solution.py:331
  9.4 5.1 %collective-permute-done.refs_1_ = bf16[32,4224]{1,0:T(8,128)(2,1)S(1)} collective-permute-done((bf16[32,4224]{1,0:T(8,128)(2,1)S(1)}, bf16[32,4224]{1,0:T(8,128)(2,1)S(1)}, u32[]{:S(2)}, u32[]{:S(2)}) %collective-permute-start) | collective-permute-done | bytes 270368 | tf_op jit(solution)/shard_map/ppermute | solution.py:331
  14.5 1.8 %collective-permute-start.2 = (bf16[32,4224]{1,0:T(8,128)(2,1)S(1)}, bf16[32,4224]{1,0:T(8,128)(2,1)S(1)}, u32[]{:S(2)}, u32[]{:S(2)}) collective-permute-start(bf16[32,4224]{1,0:T(8,128)(2,1)S(1)} %collective-permute-done.refs_1_), channel_id=1, source_target_pairs={{0,4},{4,8},{8,12},{12,14},{14,10},{10,6},{6,2},{2,0},{1,5},{5,9},... | collective-permute-start | bytes 811016 | tf_op jit(solution)/shard_map/ppermute | solution.py:331
  16.3 1.6 %collective-permute-start.8 = (bf16[32,4224]{1,0:T(8,128)(2,1)S(1)}, bf16[32,4224]{1,0:T(8,128)(2,1)S(1)}, u32[]{:S(2)}, u32[]{:S(2)}) collective-permute-start(bf16[32,4224]{1,0:T(8,128)(2,1)S(1)} %get-tuple-element.36.refs_0_), channel_id=1, source_target_pairs={{0,4},{4,8},{8,12},{12,14},{14,10},{10,6},{6,2},{2,0},{1,5},{5,9},... | collective-permute-start | bytes 811016 | tf_op jit(solution)/shard_map/ppermute | solution.py:331
  17.9 0.4 collective-permute-start.11
  18.3 4.2 %collective-permute-done.1.refs_2_ = bf16[32,4224]{1,0:T(8,128)(2,1)S(1)} collective-permute-done((bf16[32,4224]{1,0:T(8,128)(2,1)S(1)}, bf16[32,4224]{1,0:T(8,128)(2,1)S(1)}, u32[]{:S(2)}, u32[]{:S(2)}) %collective-permute-start.1) | collective-permute-done | bytes 270368 | tf_op jit(solution)/shard_map/ppermute | solution.py:331
  22.5 1.3 %collective-permute-done.2.refs_3_ = bf16[32,4224]{1,0:T(8,128)(2,1)S(1)} collective-permute-done((bf16[32,4224]{1,0:T(8,128)(2,1)S(1)}, bf16[32,4224]{1,0:T(8,128)(2,1)S(1)}, u32[]{:S(2)}, u32[]{:S(2)}) %collective-permute-start.2) | collective-permute-done | bytes 270368 | tf_op jit(solution)/shard_map/ppermute | solution.py:331
  23.8 1.9 %collective-permute-start.4 = (bf16[32,4224]{1,0:T(8,128)(2,1)S(1)}, bf16[32,4224]{1,0:T(8,128)(2,1)S(1)}, u32[]{:S(2)}, u32[]{:S(2)}) collective-permute-start(bf16[32,4224]{1,0:T(8,128)(2,1)S(1)} %collective-permute-done.2.refs_3_), channel_id=1, source_target_pairs={{0,4},{4,8},{8,12},{12,14},{14,10},{10,6},{6,2},{2,0},{1,5},{5,9},... | collective-permute-start | bytes 811016 | tf_op jit(solution)/shard_map/ppermute | solution.py:331
  25.7 3.9 %collective-permute-done.8.refs_1_ = bf16[32,4224]{1,0:T(8,128)(2,1)S(1)} collective-permute-done((bf16[32,4224]{1,0:T(8,128)(2,1)S(1)}, bf16[32,4224]{1,0:T(8,128)(2,1)S(1)}, u32[]{:S(2)}, u32[]{:S(2)}) %collective-permute-start.8) | collective-permute-done | bytes 270368 | tf_op jit(solution)/shard_map/ppermute | solution.py:331
  29.6 1.9 %collective-permute-start.10 = (bf16[32,4224]{1,0:T(8,128)(2,1)S(1)}, bf16[32,4224]{1,0:T(8,128)(2,1)S(1)}, u32[]{:S(2)}, u32[]{:S(2)}) collective-permute-start(bf16[32,4224]{1,0:T(8,128)(2,1)S(1)} %collective-permute-done.8.refs_1_), channel_id=1, source_target_pairs={{0,4},{4,8},{8,12},{12,14},{14,10},{10,6},{6,2},{2,0},{1,5},{5,9},... | collective-permute-start | bytes 811016 | tf_op jit(solution)/shard_map/ppermute | solution.py:331
  31.5 0.2 collective-permute-start.20
  31.7 2.5 %collective-permute-done.3.refs_4_ = bf16[32,4224]{1,0:T(8,128)(2,1)S(1)} collective-permute-done((bf16[32,4224]{1,0:T(8,128)(2,1)S(1)}, bf16[32,4224]{1,0:T(8,128)(2,1)S(1)}, u32[]{:S(2)}, u32[]{:S(2)}) %collective-permute-start.3) | collective-permute-done | bytes 270368 | tf_op jit(solution)/shard_map/ppermute | solution.py:331
  34.1 1.3 %collective-permute-done.4.refs_5_ = bf16[32,4224]{1,0:T(8,128)(2,1)S(1)} collective-permute-done((bf16[32,4224]{1,0:T(8,128)(2,1)S(1)}, bf16[32,4224]{1,0:T(8,128)(2,1)S(1)}, u32[]{:S(2)}, u32[]{:S(2)}) %collective-permute-start.4) | collective-permute-done | bytes 270368 | tf_op jit(solution)/shard_map/ppermute | solution.py:331
  35.4 1.9 %collective-permute-start.6 = (bf16[32,4224]{1,0:T(8,128)(2,1)S(1)}, bf16[32,4224]{1,0:T(8,128)(2,1)S(1)}, u32[]{:S(2)}, u32[]{:S(2)}) collective-permute-start(bf16[32,4224]{1,0:T(8,128)(2,1)S(1)} %collective-permute-done.4.refs_5_), channel_id=1, source_target_pairs={{0,4},{4,8},{8,12},{12,14},{14,10},{10,6},{6,2},{2,0},{1,5},{5,9},... | collective-permute-start | bytes 811016 | tf_op jit(solution)/shard_map/ppermute | solution.py:331
  37.3 3.9 %collective-permute-done.10.refs_3_ = bf16[32,4224]{1,0:T(8,128)(2,1)S(1)} collective-permute-done((bf16[32,4224]{1,0:T(8,128)(2,1)S(1)}, bf16[32,4224]{1,0:T(8,128)(2,1)S(1)}, u32[]{:S(2)}, u32[]{:S(2)}) %collective-permute-start.10) | collective-permute-done | bytes 270368 | tf_op jit(solution)/shard_map/ppermute | solution.py:331
  41.2 1.9 %collective-permute-start.19 = (bf16[32,4224]{1,0:T(8,128)(2,1)S(1)}, bf16[32,4224]{1,0:T(8,128)(2,1)S(1)}, u32[]{:S(2)}, u32[]{:S(2)}) collective-permute-start(bf16[32,4224]{1,0:T(8,128)(2,1)S(1)} %collective-permute-done.10.refs_3_), channel_id=1, source_target_pairs={{0,4},{4,8},{8,12},{12,14},{14,10},{10,6},{6,2},{2,0},{1,5},{5,9},... | collective-permute-start | bytes 811016 | tf_op jit(solution)/shard_map/ppermute | solution.py:331
  43.1 4.6 %shard_map.114 = (f32[160,2048]{1,0:T(8,128)S(1)}, f32[32,768]{1,0:T(8,128)S(1)}, f32[32,2048]{1,0:T(8,128)S(1)}) custom-call(bf16[32,4224]{1,0:T(8,128)(2,1)S(1)} %get-tuple-element.36.refs_0_, bf16[32,4224]{1,0:T(8,128)(2,1)S(1)} %collective-permute-done.8.refs_1_, bf16[32,4224]{1,0:T(8,128)(2,1)S(1)} %collective-permute-done.9.refs_2_, ...), custom_call_target="tpu_custom_call" | custom-call | flops 2516582400 | bytes 11329536 | tf_op jit(solution)/shard_map/pallas_call | solution.py:218
  47.7 0.2 collective-permute-start.21
  47.9 5.4 %shard_map.115 = (f32[256,2048]{1,0:T(8,128)S(1)}, f32[32,768]{1,0:T(8,128)S(1)}, f32[32,2048]{1,0:T(8,128)S(1)}, bf16[32,2048]{1,0:T(8,128)(2,1)S(1)}, bf16[32,2048]{1,0:T(8,128)(2,1)S(1)}) custom-call(bf16[32,4224]{1,0:T(8,128)(2,1)S(1)} %get-tuple-element.33.refs_0_, bf16[32,4224]{1,0:T(8,128)(2,1)S(1)} %collective-permute-done.refs_1_, ...), custom_call_target="tpu_custom_call" | custom-call | flops 4026531840 | bytes 12140544 | tf_op jit(solution)/shard_map/pallas_call | solution.py:218
  53.3 1.8 %collective-permute-start.12 = (bf16[32,2048]{1,0:T(8,128)(2,1)S(1)}, bf16[32,2048]{1,0:T(8,128)(2,1)S(1)}, u32[]{:S(2)}, u32[]{:S(2)}) collective-permute-start(bf16[32,2048]{1,0:T(8,128)(2,1)S(1)} %get-tuple-element.40), channel_id=1, source_target_pairs={{4,0},{8,4},{12,8},{14,12},{10,14},{6,10},{2,6},{0,2},{5,1},{9,5},... | collective-permute-start | bytes 393224 | tf_op jit(solution)/shard_map/ppermute | solution.py:368
  55.1 4.0 %shard_map.119 = (f32[96,2048]{1,0:T(8,128)S(1)}, f32[32,768]{1,0:T(8,128)S(1)}, f32[32,2048]{1,0:T(8,128)S(1)}, bf16[32,2048]{1,0:T(8,128)(2,1)S(1)}, bf16[32,2048]{1,0:T(8,128)(2,1)S(1)}) custom-call(bf16[32,4224]{1,0:T(8,128)(2,1)S(1)} %collective-permute-done.19.refs_0_, bf16[32,4224]{1,0:T(8,128)(2,1)S(1)} %collective-permute-done.20.refs_1_, ...), custom_call_target="tpu_custom_call" | custom-call | flops 1509949440 | bytes 10788864 | tf_op jit(solution)/shard_map/pallas_call | solution.py:218
  59.2 1.7 %collective-permute-start.23 = (bf16[32,2048]{1,0:T(8,128)(2,1)S(1)}, bf16[32,2048]{1,0:T(8,128)(2,1)S(1)}, u32[]{:S(2)}, u32[]{:S(2)}) collective-permute-start(bf16[32,2048]{1,0:T(8,128)(2,1)S(1)} %get-tuple-element.52), channel_id=1, source_target_pairs={{0,4},{4,8},{8,12},{12,14},{14,10},{10,6},{6,2},{2,0},{1,5},{5,9},... | collective-permute-start | bytes 393224 | tf_op jit(solution)/shard_map/ppermute | solution.py:368
  60.9 1.6 %collective-permute-start.14 = (bf16[32,2048]{1,0:T(8,128)(2,1)S(1)}, bf16[32,2048]{1,0:T(8,128)(2,1)S(1)}, u32[]{:S(2)}, u32[]{:S(2)}) collective-permute-start(bf16[32,2048]{1,0:T(8,128)(2,1)S(1)} %get-tuple-element.41), channel_id=1, source_target_pairs={{0,4},{4,8},{8,12},{12,14},{14,10},{10,6},{6,2},{2,0},{1,5},{5,9},... | collective-permute-start | bytes 393224 | tf_op jit(solution)/shard_map/ppermute | solution.py:368
  62.5 0.5 collective-permute-start.13
  63.0 0.4 collective-permute-start.22
  63.4 1.9 %collective-permute-done.23.refs_1_ = bf16[32,2048]{1,0:T(8,128)(2,1)S(1)} collective-permute-done((bf16[32,2048]{1,0:T(8,128)(2,1)S(1)}, bf16[32,2048]{1,0:T(8,128)(2,1)S(1)}, u32[]{:S(2)}, u32[]{:S(2)}) %collective-permute-start.23) | collective-permute-done | bytes 131104 | tf_op jit(solution)/shard_map/ppermute | solution.py:368
  65.3 0.8 collective-permute-start.24
  66.2 1.9 %collective-permute-done.14.refs_3_ = bf16[32,2048]{1,0:T(8,128)(2,1)S(1)} collective-permute-done((bf16[32,2048]{1,0:T(8,128)(2,1)S(1)}, bf16[32,2048]{1,0:T(8,128)(2,1)S(1)}, u32[]{:S(2)}, u32[]{:S(2)}) %collective-permute-start.14) | collective-permute-done | bytes 131104 | tf_op jit(solution)/shard_map/ppermute | solution.py:368
  68.1 1.6 %collective-permute-start.15 = (bf16[32,2048]{1,0:T(8,128)(2,1)S(1)}, bf16[32,2048]{1,0:T(8,128)(2,1)S(1)}, u32[]{:S(2)}, u32[]{:S(2)}) collective-permute-start(bf16[32,2048]{1,0:T(8,128)(2,1)S(1)} %get-tuple-element.42), channel_id=1, source_target_pairs={{4,0},{8,4},{12,8},{14,12},{10,14},{6,10},{2,6},{0,2},{5,1},{9,5},... | collective-permute-start | bytes 393224 | tf_op jit(solution)/shard_map/ppermute | solution.py:368
  69.7 0.7 collective-permute-start.16
  70.5 1.1 %collective-permute-done.24.refs_3_ = bf16[32,2048]{1,0:T(8,128)(2,1)S(1)} collective-permute-done((bf16[32,2048]{1,0:T(8,128)(2,1)S(1)}, bf16[32,2048]{1,0:T(8,128)(2,1)S(1)}, u32[]{:S(2)}, u32[]{:S(2)}) %collective-permute-start.24) | collective-permute-done | bytes 131104 | tf_op jit(solution)/shard_map/ppermute | solution.py:368
  71.6 1.6 %collective-permute-start.25 = (bf16[32,2048]{1,0:T(8,128)(2,1)S(1)}, bf16[32,2048]{1,0:T(8,128)(2,1)S(1)}, u32[]{:S(2)}, u32[]{:S(2)}) collective-permute-start(bf16[32,2048]{1,0:T(8,128)(2,1)S(1)} %get-tuple-element.53), channel_id=1, source_target_pairs={{4,0},{8,4},{12,8},{14,12},{10,14},{6,10},{2,6},{0,2},{5,1},{9,5},... | collective-permute-start | bytes 393224 | tf_op jit(solution)/shard_map/ppermute | solution.py:368
  73.2 0.5 collective-permute-start.26
  73.9 0.8 collective-permute-done.16.refs_3_
  74.8 1.6 %collective-permute-start.17 = (bf16[32,2048]{1,0:T(8,128)(2,1)S(1)}, bf16[32,2048]{1,0:T(8,128)(2,1)S(1)}, u32[]{:S(2)}, u32[]{:S(2)}) collective-permute-start(bf16[32,2048]{1,0:T(8,128)(2,1)S(1)} %get-tuple-element.44), channel_id=1, source_target_pairs={{4,0},{8,4},{12,8},{14,12},{10,14},{6,10},{2,6},{0,2},{5,1},{9,5},... | collective-permute-start | bytes 393224 | tf_op jit(solution)/shard_map/ppermute | solution.py:368
  76.4 0.4 collective-permute-start.18
  76.8 1.4 %collective-permute-done.26.refs_3_ = bf16[32,2048]{1,0:T(8,128)(2,1)S(1)} collective-permute-done((bf16[32,2048]{1,0:T(8,128)(2,1)S(1)}, bf16[32,2048]{1,0:T(8,128)(2,1)S(1)}, u32[]{:S(2)}, u32[]{:S(2)}) %collective-permute-start.26) | collective-permute-done | bytes 131104 | tf_op jit(solution)/shard_map/ppermute | solution.py:368
  78.2 1.7 %collective-permute-start.27 = (bf16[32,2048]{1,0:T(8,128)(2,1)S(1)}, bf16[32,2048]{1,0:T(8,128)(2,1)S(1)}, u32[]{:S(2)}, u32[]{:S(2)}) collective-permute-start(bf16[32,2048]{1,0:T(8,128)(2,1)S(1)} %get-tuple-element.55), channel_id=1, source_target_pairs={{4,0},{8,4},{12,8},{14,12},{10,14},{6,10},{2,6},{0,2},{5,1},{9,5},... | collective-permute-start | bytes 393224 | tf_op jit(solution)/shard_map/ppermute | solution.py:368
  79.9 0.4 collective-permute-start.28
  80.3 0.7 shard_map.125
  81.1 1.6 %collective-permute-done.18.refs_2_ = bf16[32,2048]{1,0:T(8,128)(2,1)S(1)} collective-permute-done((bf16[32,2048]{1,0:T(8,128)(2,1)S(1)}, bf16[32,2048]{1,0:T(8,128)(2,1)S(1)}, u32[]{:S(2)}, u32[]{:S(2)}) %collective-permute-start.18) | collective-permute-done | bytes 131104 | tf_op jit(solution)/shard_map/ppermute | solution.py:368
  82.8 0.5 collective-permute-done.27.refs_4_
  83.3 1.6 %collective-permute-done.28.refs_5_ = bf16[32,2048]{1,0:T(8,128)(2,1)S(1)} collective-permute-done((bf16[32,2048]{1,0:T(8,128)(2,1)S(1)}, bf16[32,2048]{1,0:T(8,128)(2,1)S(1)}, u32[]{:S(2)}, u32[]{:S(2)}) %collective-permute-start.28) | collective-permute-done | bytes 131104 | tf_op jit(solution)/shard_map/ppermute | solution.py:368
  84.9 0.8 shard_map.123
  (30 shorter events, 0.7 us)
Async XLA Ops:
  0.6 42.5 %copy-start = (bf16[2,16,2048]{2,1,0:T(8,128)(2,1)S(1)}, bf16[2,16,2048]{2,1,0:T(8,128)(2,1)}, u32[]{:S(2)}) copy-start(bf16[2,16,2048]{2,1,0:T(8,128)(2,1)} %param.17) | copy-start | bytes 393220
  3.1 40.0 %collective-permute-start.7 = (bf16[1024,2304]{1,0:T(8,128)(2,1)S(1)}, bf16[1024,2304]{1,0:T(8,128)(2,1)S(1)}, u32[]{:S(2)}, u32[]{:S(2)}) collective-permute-start(bf16[1024,2304]{1,0:T(8,128)(2,1)S(1)} %get-tuple-element.35.refs_7_.refs_10_.refs_5_), channel_id=1, source_target_pairs={{0,1},{1,0},{2,3},{3,2},{4,5},{5,4},{6,7},{7,6},{8,9},{9,8},{10,11... | collective-permute-start | bytes 14155784 | tf_op jit(solution)/shard_map/ppermute | solution.py:341
  4.8 9.7 %collective-permute-start = (bf16[32,4224]{1,0:T(8,128)(2,1)S(1)}, bf16[32,4224]{1,0:T(8,128)(2,1)S(1)}, u32[]{:S(2)}, u32[]{:S(2)}) collective-permute-start(bf16[32,4224]{1,0:T(8,128)(2,1)S(1)} %get-tuple-element.33.refs_0_), channel_id=1, source_target_pairs={{0,4},{4,8},{8,12},{12,14},{14,10},{10,6},{6,2},{2,0},{1,5},{5,9},... | collective-permute-start | bytes 811016 | tf_op jit(solution)/shard_map/ppermute | solution.py:331
  7.4 10.5 %collective-permute-start.9 = (bf16[32,4224]{1,0:T(8,128)(2,1)S(1)}, bf16[32,4224]{1,0:T(8,128)(2,1)S(1)}, u32[]{:S(2)}, u32[]{:S(2)}) collective-permute-start(bf16[32,4224]{1,0:T(8,128)(2,1)S(1)} %get-tuple-element.36.refs_0_), channel_id=1, source_target_pairs={{4,0},{8,4},{12,8},{14,12},{10,14},{6,10},{2,6},{0,2},{5,1},{9,5},... | collective-permute-start | bytes 811016 | tf_op jit(solution)/shard_map/ppermute | solution.py:331
  7.4 15.1 %collective-permute-start.1 = (bf16[32,4224]{1,0:T(8,128)(2,1)S(1)}, bf16[32,4224]{1,0:T(8,128)(2,1)S(1)}, u32[]{:S(2)}, u32[]{:S(2)}) collective-permute-start(bf16[32,4224]{1,0:T(8,128)(2,1)S(1)} %get-tuple-element.33.refs_0_), channel_id=1, source_target_pairs={{4,0},{8,4},{12,8},{14,12},{10,14},{6,10},{2,6},{0,2},{5,1},{9,5},... | collective-permute-start | bytes 811016 | tf_op jit(solution)/shard_map/ppermute | solution.py:331
  14.5 9.4 %collective-permute-start.2 = (bf16[32,4224]{1,0:T(8,128)(2,1)S(1)}, bf16[32,4224]{1,0:T(8,128)(2,1)S(1)}, u32[]{:S(2)}, u32[]{:S(2)}) collective-permute-start(bf16[32,4224]{1,0:T(8,128)(2,1)S(1)} %collective-permute-done.refs_1_), channel_id=1, source_target_pairs={{0,4},{4,8},{8,12},{12,14},{14,10},{10,6},{6,2},{2,0},{1,5},{5,9},... | collective-permute-start | bytes 811016 | tf_op jit(solution)/shard_map/ppermute | solution.py:331
  16.3 13.3 %collective-permute-start.8 = (bf16[32,4224]{1,0:T(8,128)(2,1)S(1)}, bf16[32,4224]{1,0:T(8,128)(2,1)S(1)}, u32[]{:S(2)}, u32[]{:S(2)}) collective-permute-start(bf16[32,4224]{1,0:T(8,128)(2,1)S(1)} %get-tuple-element.36.refs_0_), channel_id=1, source_target_pairs={{0,4},{4,8},{8,12},{12,14},{14,10},{10,6},{6,2},{2,0},{1,5},{5,9},... | collective-permute-start | bytes 811016 | tf_op jit(solution)/shard_map/ppermute | solution.py:331
  17.9 13.6 %collective-permute-start.11 = (bf16[32,4224]{1,0:T(8,128)(2,1)S(1)}, bf16[32,4224]{1,0:T(8,128)(2,1)S(1)}, u32[]{:S(2)}, u32[]{:S(2)}) collective-permute-start(bf16[32,4224]{1,0:T(8,128)(2,1)S(1)} %collective-permute-done.9.refs_2_), channel_id=1, source_target_pairs={{4,0},{8,4},{12,8},{14,12},{10,14},{6,10},{2,6},{0,2},{5,1},{9,5},... | collective-permute-start | bytes 811016 | tf_op jit(solution)/shard_map/ppermute | solution.py:331
  22.5 11.6 %collective-permute-start.3 = (bf16[32,4224]{1,0:T(8,128)(2,1)S(1)}, bf16[32,4224]{1,0:T(8,128)(2,1)S(1)}, u32[]{:S(2)}, u32[]{:S(2)}) collective-permute-start(bf16[32,4224]{1,0:T(8,128)(2,1)S(1)} %collective-permute-done.1.refs_2_), channel_id=1, source_target_pairs={{4,0},{8,4},{12,8},{14,12},{10,14},{6,10},{2,6},{0,2},{5,1},{9,5},... | collective-permute-start | bytes 811016 | tf_op jit(solution)/shard_map/ppermute | solution.py:331
  23.8 11.6 %collective-permute-start.4 = (bf16[32,4224]{1,0:T(8,128)(2,1)S(1)}, bf16[32,4224]{1,0:T(8,128)(2,1)S(1)}, u32[]{:S(2)}, u32[]{:S(2)}) collective-permute-start(bf16[32,4224]{1,0:T(8,128)(2,1)S(1)} %collective-permute-done.2.refs_3_), channel_id=1, source_target_pairs={{0,4},{4,8},{8,12},{12,14},{14,10},{10,6},{6,2},{2,0},{1,5},{5,9},... | collective-permute-start | bytes 811016 | tf_op jit(solution)/shard_map/ppermute | solution.py:331
  29.6 11.6 %collective-permute-start.10 = (bf16[32,4224]{1,0:T(8,128)(2,1)S(1)}, bf16[32,4224]{1,0:T(8,128)(2,1)S(1)}, u32[]{:S(2)}, u32[]{:S(2)}) collective-permute-start(bf16[32,4224]{1,0:T(8,128)(2,1)S(1)} %collective-permute-done.8.refs_1_), channel_id=1, source_target_pairs={{0,4},{4,8},{8,12},{12,14},{14,10},{10,6},{6,2},{2,0},{1,5},{5,9},... | collective-permute-start | bytes 811016 | tf_op jit(solution)/shard_map/ppermute | solution.py:331
  31.5 16.2 %collective-permute-start.20 = (bf16[32,4224]{1,0:T(8,128)(2,1)S(1)}, bf16[32,4224]{1,0:T(8,128)(2,1)S(1)}, u32[]{:S(2)}, u32[]{:S(2)}) collective-permute-start(bf16[32,4224]{1,0:T(8,128)(2,1)S(1)} %collective-permute-done.11.refs_4_), channel_id=1, source_target_pairs={{4,0},{8,4},{12,8},{14,12},{10,14},{6,10},{2,6},{0,2},{5,1},{9,5},... | collective-permute-start | bytes 811016 | tf_op jit(solution)/shard_map/ppermute | solution.py:331
  34.1 13.8 %collective-permute-start.5 = (bf16[32,4224]{1,0:T(8,128)(2,1)S(1)}, bf16[32,4224]{1,0:T(8,128)(2,1)S(1)}, u32[]{:S(2)}, u32[]{:S(2)}) collective-permute-start(bf16[32,4224]{1,0:T(8,128)(2,1)S(1)} %collective-permute-done.3.refs_4_), channel_id=1, source_target_pairs={{4,0},{8,4},{12,8},{14,12},{10,14},{6,10},{2,6},{0,2},{5,1},{9,5},... | collective-permute-start | bytes 811016 | tf_op jit(solution)/shard_map/ppermute | solution.py:331
  35.4 12.5 %collective-permute-start.6 = (bf16[32,4224]{1,0:T(8,128)(2,1)S(1)}, bf16[32,4224]{1,0:T(8,128)(2,1)S(1)}, u32[]{:S(2)}, u32[]{:S(2)}) collective-permute-start(bf16[32,4224]{1,0:T(8,128)(2,1)S(1)} %collective-permute-done.4.refs_5_), channel_id=1, source_target_pairs={{0,4},{4,8},{8,12},{12,14},{14,10},{10,6},{6,2},{2,0},{1,5},{5,9},... | collective-permute-start | bytes 811016 | tf_op jit(solution)/shard_map/ppermute | solution.py:331
  41.2 13.9 %collective-permute-start.19 = (bf16[32,4224]{1,0:T(8,128)(2,1)S(1)}, bf16[32,4224]{1,0:T(8,128)(2,1)S(1)}, u32[]{:S(2)}, u32[]{:S(2)}) collective-permute-start(bf16[32,4224]{1,0:T(8,128)(2,1)S(1)} %collective-permute-done.10.refs_3_), channel_id=1, source_target_pairs={{0,4},{4,8},{8,12},{12,14},{14,10},{10,6},{6,2},{2,0},{1,5},{5,9},... | collective-permute-start | bytes 811016 | tf_op jit(solution)/shard_map/ppermute | solution.py:331
  47.7 7.4 %collective-permute-start.21 = (bf16[32,4224]{1,0:T(8,128)(2,1)S(1)}, bf16[32,4224]{1,0:T(8,128)(2,1)S(1)}, u32[]{:S(2)}, u32[]{:S(2)}) collective-permute-start(bf16[32,4224]{1,0:T(8,128)(2,1)S(1)} %collective-permute-done.20.refs_1_), channel_id=1, source_target_pairs={{4,0},{8,4},{12,8},{14,12},{10,14},{6,10},{2,6},{0,2},{5,1},{9,5},... | collective-permute-start | bytes 811016 | tf_op jit(solution)/shard_map/ppermute | solution.py:331
  53.3 9.1 %collective-permute-start.12 = (bf16[32,2048]{1,0:T(8,128)(2,1)S(1)}, bf16[32,2048]{1,0:T(8,128)(2,1)S(1)}, u32[]{:S(2)}, u32[]{:S(2)}) collective-permute-start(bf16[32,2048]{1,0:T(8,128)(2,1)S(1)} %get-tuple-element.40), channel_id=1, source_target_pairs={{4,0},{8,4},{12,8},{14,12},{10,14},{6,10},{2,6},{0,2},{5,1},{9,5},... | collective-permute-start | bytes 393224 | tf_op jit(solution)/shard_map/ppermute | solution.py:368
  59.2 6.1 %collective-permute-start.23 = (bf16[32,2048]{1,0:T(8,128)(2,1)S(1)}, bf16[32,2048]{1,0:T(8,128)(2,1)S(1)}, u32[]{:S(2)}, u32[]{:S(2)}) collective-permute-start(bf16[32,2048]{1,0:T(8,128)(2,1)S(1)} %get-tuple-element.52), channel_id=1, source_target_pairs={{0,4},{4,8},{8,12},{12,14},{14,10},{10,6},{6,2},{2,0},{1,5},{5,9},... | collective-permute-start | bytes 393224 | tf_op jit(solution)/shard_map/ppermute | solution.py:368
  60.9 7.2 %collective-permute-start.14 = (bf16[32,2048]{1,0:T(8,128)(2,1)S(1)}, bf16[32,2048]{1,0:T(8,128)(2,1)S(1)}, u32[]{:S(2)}, u32[]{:S(2)}) collective-permute-start(bf16[32,2048]{1,0:T(8,128)(2,1)S(1)} %get-tuple-element.41), channel_id=1, source_target_pairs={{0,4},{4,8},{8,12},{12,14},{14,10},{10,6},{6,2},{2,0},{1,5},{5,9},... | collective-permute-start | bytes 393224 | tf_op jit(solution)/shard_map/ppermute | solution.py:368
  62.5 5.6 %collective-permute-start.13 = (bf16[32,2048]{1,0:T(8,128)(2,1)S(1)}, bf16[32,2048]{1,0:T(8,128)(2,1)S(1)}, u32[]{:S(2)}, u32[]{:S(2)}) collective-permute-start(bf16[32,2048]{1,0:T(8,128)(2,1)S(1)} %shard_map.116), channel_id=1, source_target_pairs={{4,0},{8,4},{12,8},{14,12},{10,14},{6,10},{2,6},{0,2},{5,1},{9,5},... | collective-permute-start | bytes 393224 | tf_op jit(solution)/shard_map/ppermute | solution.py:368
  63.0 7.5 %collective-permute-start.22 = (bf16[32,2048]{1,0:T(8,128)(2,1)S(1)}, bf16[32,2048]{1,0:T(8,128)(2,1)S(1)}, u32[]{:S(2)}, u32[]{:S(2)}) collective-permute-start(bf16[32,2048]{1,0:T(8,128)(2,1)S(1)} %get-tuple-element.50), channel_id=1, source_target_pairs={{4,0},{8,4},{12,8},{14,12},{10,14},{6,10},{2,6},{0,2},{5,1},{9,5},... | collective-permute-start | bytes 393224 | tf_op jit(solution)/shard_map/ppermute | solution.py:368
  65.3 6.3 %collective-permute-start.24 = (bf16[32,2048]{1,0:T(8,128)(2,1)S(1)}, bf16[32,2048]{1,0:T(8,128)(2,1)S(1)}, u32[]{:S(2)}, u32[]{:S(2)}) collective-permute-start(bf16[32,2048]{1,0:T(8,128)(2,1)S(1)} %shard_map.120), channel_id=1, source_target_pairs={{0,4},{4,8},{8,12},{12,14},{14,10},{10,6},{6,2},{2,0},{1,5},{5,9},... | collective-permute-start | bytes 393224 | tf_op jit(solution)/shard_map/ppermute | solution.py:368
  68.1 5.8 %collective-permute-start.15 = (bf16[32,2048]{1,0:T(8,128)(2,1)S(1)}, bf16[32,2048]{1,0:T(8,128)(2,1)S(1)}, u32[]{:S(2)}, u32[]{:S(2)}) collective-permute-start(bf16[32,2048]{1,0:T(8,128)(2,1)S(1)} %get-tuple-element.42), channel_id=1, source_target_pairs={{4,0},{8,4},{12,8},{14,12},{10,14},{6,10},{2,6},{0,2},{5,1},{9,5},... | collective-permute-start | bytes 393224 | tf_op jit(solution)/shard_map/ppermute | solution.py:368
  69.7 5.0 %collective-permute-start.16 = (bf16[32,2048]{1,0:T(8,128)(2,1)S(1)}, bf16[32,2048]{1,0:T(8,128)(2,1)S(1)}, u32[]{:S(2)}, u32[]{:S(2)}) collective-permute-start(bf16[32,2048]{1,0:T(8,128)(2,1)S(1)} %get-tuple-element.43), channel_id=1, source_target_pairs={{0,4},{4,8},{8,12},{12,14},{14,10},{10,6},{6,2},{2,0},{1,5},{5,9},... | collective-permute-start | bytes 393224 | tf_op jit(solution)/shard_map/ppermute | solution.py:368
  71.6 5.2 %collective-permute-start.25 = (bf16[32,2048]{1,0:T(8,128)(2,1)S(1)}, bf16[32,2048]{1,0:T(8,128)(2,1)S(1)}, u32[]{:S(2)}, u32[]{:S(2)}) collective-permute-start(bf16[32,2048]{1,0:T(8,128)(2,1)S(1)} %get-tuple-element.53), channel_id=1, source_target_pairs={{4,0},{8,4},{12,8},{14,12},{10,14},{6,10},{2,6},{0,2},{5,1},{9,5},... | collective-permute-start | bytes 393224 | tf_op jit(solution)/shard_map/ppermute | solution.py:368
  73.2 5.0 %collective-permute-start.26 = (bf16[32,2048]{1,0:T(8,128)(2,1)S(1)}, bf16[32,2048]{1,0:T(8,128)(2,1)S(1)}, u32[]{:S(2)}, u32[]{:S(2)}) collective-permute-start(bf16[32,2048]{1,0:T(8,128)(2,1)S(1)} %get-tuple-element.54), channel_id=1, source_target_pairs={{0,4},{4,8},{8,12},{12,14},{14,10},{10,6},{6,2},{2,0},{1,5},{5,9},... | collective-permute-start | bytes 393224 | tf_op jit(solution)/shard_map/ppermute | solution.py:368
  73.9 6.5 %collective-permute-start.29 = (f32[32,1216]{1,0:T(8,128)S(1)}, f32[32,1216]{1,0:T(8,128)S(1)}, u32[]{:S(2)}, u32[]{:S(2)}) collective-permute-start(f32[32,1216]{1,0:T(8,128)S(1)} %get-tuple-element.60), channel_id=1, source_target_pairs={{0,1},{1,0},{2,3},{3,2},{4,5},{5,4},{6,7},{7,6},{8,9},{9,8},{10,11... | collective-permute-start | bytes 466952 | tf_op jit(solution)/shard_map/ppermute | solution.py:383
  74.8 6.4 %collective-permute-start.17 = (bf16[32,2048]{1,0:T(8,128)(2,1)S(1)}, bf16[32,2048]{1,0:T(8,128)(2,1)S(1)}, u32[]{:S(2)}, u32[]{:S(2)}) collective-permute-start(bf16[32,2048]{1,0:T(8,128)(2,1)S(1)} %get-tuple-element.44), channel_id=1, source_target_pairs={{4,0},{8,4},{12,8},{14,12},{10,14},{6,10},{2,6},{0,2},{5,1},{9,5},... | collective-permute-start | bytes 393224 | tf_op jit(solution)/shard_map/ppermute | solution.py:368
  76.4 6.4 %collective-permute-start.18 = (bf16[32,2048]{1,0:T(8,128)(2,1)S(1)}, bf16[32,2048]{1,0:T(8,128)(2,1)S(1)}, u32[]{:S(2)}, u32[]{:S(2)}) collective-permute-start(bf16[32,2048]{1,0:T(8,128)(2,1)S(1)} %get-tuple-element.45), channel_id=1, source_target_pairs={{0,4},{4,8},{8,12},{12,14},{14,10},{10,6},{6,2},{2,0},{1,5},{5,9},... | collective-permute-start | bytes 393224 | tf_op jit(solution)/shard_map/ppermute | solution.py:368
  78.2 5.0 %collective-permute-start.27 = (bf16[32,2048]{1,0:T(8,128)(2,1)S(1)}, bf16[32,2048]{1,0:T(8,128)(2,1)S(1)}, u32[]{:S(2)}, u32[]{:S(2)}) collective-permute-start(bf16[32,2048]{1,0:T(8,128)(2,1)S(1)} %get-tuple-element.55), channel_id=1, source_target_pairs={{4,0},{8,4},{12,8},{14,12},{10,14},{6,10},{2,6},{0,2},{5,1},{9,5},... | collective-permute-start | bytes 393224 | tf_op jit(solution)/shard_map/ppermute | solution.py:368
  79.9 5.0 %collective-permute-start.28 = (bf16[32,2048]{1,0:T(8,128)(2,1)S(1)}, bf16[32,2048]{1,0:T(8,128)(2,1)S(1)}, u32[]{:S(2)}, u32[]{:S(2)}) collective-permute-start(bf16[32,2048]{1,0:T(8,128)(2,1)S(1)} %get-tuple-element.56), channel_id=1, source_target_pairs={{0,4},{4,8},{8,12},{12,14},{14,10},{10,6},{6,2},{2,0},{1,5},{5,9},... | collective-permute-start | bytes 393224 | tf_op jit(solution)/shard_map/ppermute | solution.py:368

commit v8 on v6

--- a/solution.py
+++ b/solution.py
@@ -115,11 +115,16 @@
             out[...] = total[...] + adapter_scale * value
 
 
-def whole_kernel(plan, pieces, blocks, *refs):
+def whole_kernel(plan, pieces, blocks, keep_rows, *refs):
     token_refs, grad_refs, refs = refs[:pieces], refs[pieces : 2 * pieces], refs[2 * pieces :]
     factor_in_ref, factor_out_ref, refs = refs[0], refs[1], refs[2:]
     weight_refs, refs = refs[: plan.parts], refs[plan.parts :]
-    total_refs, rows_ref, out_refs, send_refs = refs[:2], refs[2], refs[3:5], refs[5:]
+    total_refs, refs = refs[:2], refs[2:]
+    if keep_rows:
+        rows_ref, refs = refs[0], refs[1:]
+    else:
+        *refs, rows_ref = refs
+    out_refs, send_refs = refs[:2], refs[2:]
     activation, slope, hidden, low_rank = plan.forward(token_refs, factor_in_ref, weight_refs)
     rank_scale, back_scaled = plan.backward(
         grad_refs, activation, slope, factor_in_ref, factor_out_ref, weight_refs, rows_ref
@@ -176,20 +181,27 @@
 
 
 def add_kernel(blocks, *refs):
-    rows_ref, refs = refs[0], refs[1:]
-    for (first_row, span), incoming, out in zip(blocks, refs, refs[len(blocks) :]):
-        rows = rows_ref[first_row : first_row + out.shape[0], span]
-        out[...] = (rows + incoming[...].astype(f32)).astype(bf16)
-
-
-def add_sums(rows, blocks, incoming):
+    rows_ref, refs = refs[0], list(refs[1:])
+    outs = refs[-len(blocks) :]
+    for (first_row, span, arrived), out in zip(blocks, outs):
+        total = rows_ref[first_row : first_row + out.shape[0], span]
+        for columns in arrived:
+            total = total + refs.pop(0)[:, columns].astype(f32)
+        out[...] = total.astype(bf16)
+
+
+def add_sums(rows, row_count, blocks, arrived):
+    operands = [rows, *arrived]
     return pl.pallas_call(
         functools.partial(add_kernel, blocks),
-        out_shape=tuple(jax.ShapeDtypeStruct(x.shape, bf16) for x in incoming),
-        in_specs=[pl.BlockSpec(memory_space=pltpu.VMEM)] * (1 + len(incoming)),
-        out_specs=(pl.BlockSpec(memory_space=pltpu.VMEM),) * len(incoming),
+        out_shape=tuple(
+            jax.ShapeDtypeStruct((row_count, len(range(*span.indices(rows.shape[1])))), bf16)
+            for _, span, _ in blocks
+        ),
+        in_specs=[pl.BlockSpec(memory_space=pltpu.VMEM)] * len(operands),
+        out_specs=(pl.BlockSpec(memory_space=pltpu.VMEM),) * len(blocks),
         compiler_params=pltpu.CompilerParams(vmem_limit_bytes=16 * 1024 * 1024),
-    )(rows, *incoming)
+    )(*operands)
 
 
 def half_rows_kernel(half, first_ref, second_ref, top_ref, bottom_ref):
@@ -243,13 +255,16 @@
     )(*operands)
 
 
-def expert_call(plan, pieces, blocks, block_rows, operands, totals):
+def expert_call(plan, pieces, blocks, block_rows, operands, totals, keep_rows):
     rows = sum(piece[0].shape[0] for piece in pieces)
     operands = [p[0] for p in pieces] + [p[1] for p in pieces] + [*operands, *totals]
-    outs = [((rows, plan.model_width), f32)] + [(total.shape, f32) for total in totals]
-    outs += [((block_rows, plan.model_width // 2), bf16)] * len(blocks)
+    shape = (rows, plan.model_width)
+    outs = [(shape, f32)] * keep_rows + [(total.shape, f32) for total in totals]
+    widths = [len(range(*span.indices(plan.model_width))) for _, span in blocks]
+    outs += [((block_rows, width), bf16) for width in widths]
     return pl.pallas_call(
-        functools.partial(whole_kernel, plan, len(pieces), blocks),
+        functools.partial(whole_kernel, plan, len(pieces), blocks, keep_rows),
+        scratch_shapes=[] if keep_rows else [pltpu.VMEM(shape, f32)],
         out_shape=tuple(jax.ShapeDtypeStruct(shape, dtype) for shape, dtype in outs),
         in_specs=[pl.BlockSpec(memory_space=pltpu.VMEM)] * len(operands),
         out_specs=(pl.BlockSpec(memory_space=pltpu.VMEM),) * len(outs),
@@ -334,17 +349,18 @@
     rows_at = [None]
 
     middle = model_width // 2
-    columns = {"left": slice(0, middle), "right": slice(middle, None)}
+    columns = {"left": slice(0, middle), "right": slice(middle, model_width)}
+    everything = slice(0, model_width)
     ways = {"back": (0, backward), "ahead": (token_count, forward)}
+    skips = {"left": "back", "right": "ahead"}
     moving = {}
 
     def send(value, way):
         return lax.ppermute(value, "expert", ways[way][1])
 
-    def run(pieces, blocks, totals):
-        return expert_call(
-            plan, pieces, blocks, token_count, [factor_in, factor_out, *weights], totals
-        )
+    def run(pieces, blocks, totals, keep_rows=True):
+        operands = [factor_in, factor_out, *weights]
+        return expert_call(plan, pieces, blocks, token_count, operands, totals, keep_rows)
 
     def after(value, *arrays):
         held = []
@@ -364,9 +380,6 @@
             pieces = [behind[d], ahead[d]] + ([behind[0]] if d == 1 else [])
             rows_d, *totals = run(pieces, [], totals)
             rows_at.append(rows_d)
-    first_sends = [("left", "ahead"), ("right", "back")]
-    if not split:
-        first_sends += [("left", "back"), ("right", "ahead")]
     if split:
         half = token_count // 2
         totals, (tokens_b, tokens_a) = after(totals, behind[full][0], ahead[full][0])
@@ -376,30 +389,31 @@
             tuple(lax.ppermute(x, "expert", forward) for x in (tokens_b, grads_b)),
             tuple(lax.ppermute(x, "expert", backward) for x in (tokens_a, grads_a)),
         ]
-    if full > 0:
-        pieces = [behind[full], ahead[full]] + ([behind[0]] if full == 1 else [])
-        rows_d, *outs = run(pieces, [(ways[way][0], columns[side]) for side, way in first_sends], totals)
-        rows_at.append(rows_d)
-        totals, ready = outs[:2], outs[2:]
+    pieces = [behind[full], ahead[full]]
+    rows_d, *outs = run(pieces, [(first_row, everything) for first_row, _ in ways.values()], totals)
+    totals = outs[:2]
+    for way, value in zip(ways, outs[2:]):
+        for side in columns:
+            moving[side, way] = send(value, way) if side == "left" else moving["left", way]
+    skipped = {}
     if split:
-        last, ready = after(far[1][1], *ready)
-        far[1] = (far[1][0], last)
-    for (side, way), value in zip(first_sends, ready):
-        moving[side, way] = send(value, way)
-    if split:
-        _, *outs = run(far, [(0, columns["left"]), (0, columns["right"])], totals)
+        outs = run(far, [(0, span) for span in columns.values()], totals, keep_rows=False)
         totals = outs[:2]
-        moving["left", "back"] = send(outs[2], "back")
-        moving["right", "ahead"] = send(outs[3], "ahead")
-        blocks = [(0, columns["left"]), (token_count, columns["right"])]
-        for block, key in zip(blocks, [("left", "back"), ("right", "ahead")]):
-            (value,) = add_sums(rows_at[full], [block], [moving[key]])
-            moving[key] = send(value, key[1])
+        for (side, way), value in zip(skips.items(), outs[2:]):
+            step = -full if way == "back" else full
+            pairs = [(order[i], order[(i + step) % peer_count]) for i in range(peer_count)]
+            skipped[side, way] = lax.ppermute(value, "expert", pairs)
     for d in range(full - 1, 0, -1):
         for side, span in columns.items():
-            blocks = [(first_row, span) for first_row, _ in ways.values()]
-            values = add_sums(rows_at[d], blocks, [moving[side, way] for way in ways])
-            for way, value in zip(ways, values):
+            blocks, arrived = [], []
+            for way, (first_row, _) in ways.items():
+                taken = [span if d == full - 1 else slice(0, middle)]
+                arrived.append(moving[side, way])
+                if d == 1 and (side, way) in skipped:
+                    taken.append(slice(0, middle))
+                    arrived.append(skipped[side, way])
+                blocks.append((first_row, span, taken))
+            for way, value in zip(ways, add_sums(rows_at[d], token_count, blocks, arrived)):
                 moving[side, way] = send(value, way)
     grad_tokens = pl.pallas_call(
         functools.partial(last_kernel, 2 * token_count, list(columns.values())),

time: 84.1 us -> 82.8 us (0.985)
  waiting for transfers between devices: 30.5 us -> 24.9 us
  starting transfers between devices: 32 us -> 36.2 us
    ppermute x14 -> x10, waiting for transfers between devices: 10.5 us -> 4.92 us  [send(): return lax.ppermute(value, 'expert', ways[way][1])]
    ppermute x0 -> x2, starting transfers between devices: none -> 4.87 us  [per_device(): skipped[side, way] = lax.ppermute(value, 'expert', pairs)]
    ppermute x2, waiting for transfers between devices: 1 us -> 0.01 us  [per_device(): lax.ppermute(x, 'expert', backward)]
    ppermute x0 -> x2, waiting for transfers between devices: none -> 0.98 us  [per_device(): skipped[side, way] = lax.ppermute(value, 'expert', pairs)]
    ppermute x14 -> x10, starting transfers between devices: 14.5 us -> 13.8 us  [send(): return lax.ppermute(value, 'expert', ways[way][1])]
  transfers between devices with their start and end apart: 32 -> 30, of which waited for: 17 -> 11; matrix products, arithmetic and copies ran while one was open for 0% -> 0% of each run, Pallas kernels for 15% -> 21%
where the time goes in v8:
time: 82.8 us; the launch traced here: 82.6 us
  starting transfers between devices  36.2 us (44%)
  waiting for transfers between devices  24.9 us (30%)
  Pallas kernels  20.7 us (25%)
    ppermute x8, waiting for transfers between devices, per_device(): lax.ppermute(x, 'expert', forward)  16.5 us
    pallas_call x4, Pallas kernels, expert_call(): pl.pallas_call(functools.partial(whole_kernel, plan, len(pieces), blocks,...  16.2 us
    ppermute x8, starting transfers between devices, per_device(): lax.ppermute(x, 'expert', forward)  16.1 us
    ppermute x10, starting transfers between devices, send(): return lax.ppermute(value, 'expert', ways[way][1])  13.8 us
    ppermute x10, waiting for transfers between devices, send(): return lax.ppermute(value, 'expert', ways[way][1])  4.92 us
    ppermute x2, starting transfers between devices, per_device(): skipped[side, way] = lax.ppermute(value, 'expert', pairs)  4.87 us
    pallas_call x1, Pallas kernels, per_device(): pl.pallas_call(functools.partial(prepare_kernel, plan), out_shape=(jax.Sh...  2.65 us
    ppermute x6, waiting for transfers between devices, per_device(): ahead.append(tuple((lax.ppermute(x, 'expert', backward) for x in ahead[d])))  2.58 us
  transfers between devices with their start and end apart: 30, of which 11 were waited for; matrix products, arithmetic and copies ran while one was open for 0% of the time, Pallas kernels for 21%

profile of v8, /device:TPU:0, one launch (start us, length us, event | category | flops | bytes accessed | tf_op | source)
XLA Modules:
  0.0 82.6 jit_solution(9070342299643403759)
XLA Ops:
  0.6 2.6 %shard_map.112 = (bf16[1024,2304]{1,0:T(8,128)(2,1)S(1)}, bf16[64,2176]{1,0:T(8,128)(2,1)S(1)}, bf16[64,2176]{1,0:T(8,128)(2,1)S(1)}, bf16[32,768]{1,0:T(8,128)(2,1)S(1)}) custom-call(bf16[2,1024,384]{2,1,0:T(8,128)(2,1)} %refs_0_.1, bf16[2,1024,384]{2,1,0:T(8,128)(2,1)} %refs_1_.1, bf16[2,1024,384]{2,1,0:T(8,128)(2,1)} %refs_2_.1, ...), custom_call_target="tpu_custom_call" | custom-call | tf_op jit(solution)/shard_map/pallas_call | solution.py:307
  3.3 0.5 collective-permute-start.4
  3.8 2.6 %collective-permute-start.2 = (bf16[64,2176]{1,0:T(8,128)(2,1)S(1)}, bf16[64,2176]{1,0:T(8,128)(2,1)S(1)}, u32[]{:S(2)}, u32[]{:S(2)}) collective-permute-start(bf16[64,2176]{1,0:T(8,128)(2,1)S(1)} %get-tuple-element.50.refs_5_), channel_id=1, source_target_pairs={{0,4},{4,8},{8,12},{12,14},{14,10},{10,6},{6,2},{2,0},{1,5},{5,9},... | collective-permute-start | bytes 835592 | tf_op jit(solution)/shard_map/ppermute | solution.py:377
  6.5 2.0 %collective-permute-start = (bf16[64,2176]{1,0:T(8,128)(2,1)S(1)}, bf16[64,2176]{1,0:T(8,128)(2,1)S(1)}, u32[]{:S(2)}, u32[]{:S(2)}) collective-permute-start(bf16[64,2176]{1,0:T(8,128)(2,1)S(1)} %get-tuple-element.49.refs_2_), channel_id=1, source_target_pairs={{0,4},{4,8},{8,12},{12,14},{14,10},{10,6},{6,2},{2,0},{1,5},{5,9},... | collective-permute-start | bytes 835592 | tf_op jit(solution)/shard_map/ppermute | solution.py:377
  8.5 0.0 collective-permute-start.1
  8.5 5.4 %collective-permute-done.2.refs_3_ = bf16[64,2176]{1,0:T(8,128)(2,1)S(1)} collective-permute-done((bf16[64,2176]{1,0:T(8,128)(2,1)S(1)}, bf16[64,2176]{1,0:T(8,128)(2,1)S(1)}, u32[]{:S(2)}, u32[]{:S(2)}) %collective-permute-start.2) | collective-permute-done | bytes 278560 | tf_op jit(solution)/shard_map/ppermute | solution.py:377
  13.9 2.0 %collective-permute-start.7 = (bf16[64,2176]{1,0:T(8,128)(2,1)S(1)}, bf16[64,2176]{1,0:T(8,128)(2,1)S(1)}, u32[]{:S(2)}, u32[]{:S(2)}) collective-permute-start(bf16[64,2176]{1,0:T(8,128)(2,1)S(1)} %collective-permute-done.2.refs_3_), channel_id=1, source_target_pairs={{0,4},{4,8},{8,12},{12,14},{14,10},{10,6},{6,2},{2,0},{1,5},{5,9},... | collective-permute-start | bytes 835592 | tf_op jit(solution)/shard_map/ppermute | solution.py:377
  15.9 0.0 collective-permute-done.3.refs_4_
  16.0 3.9 %collective-permute-done.refs_0_ = bf16[64,2176]{1,0:T(8,128)(2,1)S(1)} collective-permute-done((bf16[64,2176]{1,0:T(8,128)(2,1)S(1)}, bf16[64,2176]{1,0:T(8,128)(2,1)S(1)}, u32[]{:S(2)}, u32[]{:S(2)}) %collective-permute-start) | collective-permute-done | bytes 278560 | tf_op jit(solution)/shard_map/ppermute | solution.py:377
  19.9 2.0 %collective-permute-start.5 = (bf16[64,2176]{1,0:T(8,128)(2,1)S(1)}, bf16[64,2176]{1,0:T(8,128)(2,1)S(1)}, u32[]{:S(2)}, u32[]{:S(2)}) collective-permute-start(bf16[64,2176]{1,0:T(8,128)(2,1)S(1)} %collective-permute-done.refs_0_), channel_id=1, source_target_pairs={{0,4},{4,8},{8,12},{12,14},{14,10},{10,6},{6,2},{2,0},{1,5},{5,9},... | collective-permute-start | bytes 835592 | tf_op jit(solution)/shard_map/ppermute | solution.py:377
  21.9 0.0 collective-permute-done.1.refs_1_
  21.9 3.9 %collective-permute-done.7.refs_2_ = bf16[64,2176]{1,0:T(8,128)(2,1)S(1)} collective-permute-done((bf16[64,2176]{1,0:T(8,128)(2,1)S(1)}, bf16[64,2176]{1,0:T(8,128)(2,1)S(1)}, u32[]{:S(2)}, u32[]{:S(2)}) %collective-permute-start.7) | collective-permute-done | bytes 278560 | tf_op jit(solution)/shard_map/ppermute | solution.py:377
  25.8 2.0 %collective-permute-start.11 = (bf16[64,2176]{1,0:T(8,128)(2,1)S(1)}, bf16[64,2176]{1,0:T(8,128)(2,1)S(1)}, u32[]{:S(2)}, u32[]{:S(2)}) collective-permute-start(bf16[64,2176]{1,0:T(8,128)(2,1)S(1)} %collective-permute-done.7.refs_2_), channel_id=1, source_target_pairs={{0,4},{4,8},{8,12},{12,14},{14,10},{10,6},{6,2},{2,0},{1,5},{5,9},... | collective-permute-start | bytes 835592 | tf_op jit(solution)/shard_map/ppermute | solution.py:377
  27.9 0.0 collective-permute-done.8.refs_3_
  27.9 4.4 %shard_map.113 = (f32[192,2048]{1,0:T(8,128)S(1)}, f32[32,768]{1,0:T(8,128)S(1)}, f32[32,2048]{1,0:T(8,128)S(1)}) custom-call(bf16[64,2176]{1,0:T(8,128)(2,1)S(1)} %collective-permute-done.refs_0_, bf16[64,2176]{1,0:T(8,128)(2,1)S(1)} %collective-permute-done.1.refs_1_, bf16[64,2176]{1,0:T(8,128)(2,1)S(1)} %get-tuple-element.49.refs_2_, ...), custom_call_target="tpu_custom_call" | custom-call | flops 3019898880 | bytes 11649024 | tf_op jit(solution)/shard_map/pallas_call | solution.py:265
  32.4 2.1 %collective-permute-start.9 = (bf16[64,2176]{1,0:T(8,128)(2,1)S(1)}, bf16[64,2176]{1,0:T(8,128)(2,1)S(1)}, u32[]{:S(2)}, u32[]{:S(2)}) collective-permute-start(bf16[64,2176]{1,0:T(8,128)(2,1)S(1)} %collective-permute-done.5.refs_0_), channel_id=1, source_target_pairs={{0,4},{4,8},{8,12},{12,14},{14,10},{10,6},{6,2},{2,0},{1,5},{5,9},... | collective-permute-start | bytes 835592 | tf_op jit(solution)/shard_map/ppermute | solution.py:377
  34.5 0.0 collective-permute-start.10
  34.5 3.3 %collective-permute-done.11.refs_2_.first_ref = bf16[64,2176]{1,0:T(8,128)(2,1)S(1)} collective-permute-done((bf16[64,2176]{1,0:T(8,128)(2,1)S(1)}, bf16[64,2176]{1,0:T(8,128)(2,1)S(1)}, u32[]{:S(2)}, u32[]{:S(2)}) %collective-permute-start.11) | collective-permute-done | bytes 278560 | tf_op jit(solution)/shard_map/ppermute | solution.py:377
  37.8 2.1 %collective-permute-done.12.refs_3_.second_ref = bf16[64,2176]{1,0:T(8,128)(2,1)S(1)} collective-permute-done((bf16[64,2176]{1,0:T(8,128)(2,1)S(1)}, bf16[64,2176]{1,0:T(8,128)(2,1)S(1)}, u32[]{:S(2)}, u32[]{:S(2)}) %collective-permute-start.12) | collective-permute-done | bytes 278560 | tf_op jit(solution)/shard_map/ppermute | solution.py:378
  39.9 1.6 %collective-permute-start.18 = (bf16[32,2176]{1,0:T(8,128)(2,1)S(1)}, bf16[32,2176]{1,0:T(8,128)(2,1)S(1)}, u32[]{:S(2)}, u32[]{:S(2)}) collective-permute-start(bf16[32,2176]{1,0:T(8,128)(2,1)S(1)} %get-tuple-element.76), channel_id=1, source_target_pairs={{0,4},{4,8},{8,12},{12,14},{14,10},{10,6},{6,2},{2,0},{1,5},{5,9},... | collective-permute-start | bytes 417800 | tf_op jit(solution)/shard_map/ppermute | solution.py:389
  41.5 0.4 collective-permute-start.19
  41.9 3.5 %shard_map.114 = (f32[128,2048]{1,0:T(8,128)S(1)}, f32[32,768]{1,0:T(8,128)S(1)}, f32[32,2048]{1,0:T(8,128)S(1)}) custom-call(bf16[64,2176]{1,0:T(8,128)(2,1)S(1)} %collective-permute-done.5.refs_0_, bf16[64,2176]{1,0:T(8,128)(2,1)S(1)} %collective-permute-done.6.refs_1_, bf16[64,2176]{1,0:T(8,128)(2,1)S(1)} %collective-permute-done.7.refs_2_, ...), custom_call_target="tpu_custom_call" | custom-call | flops 2013265920 | bytes 11091968 | tf_op jit(solution)/shard_map/pallas_call | solution.py:265
  45.4 0.4 collective-permute-done.10.refs_1_.second_ref
  45.8 1.6 %collective-permute-start.16 = (bf16[32,2176]{1,0:T(8,128)(2,1)S(1)}, bf16[32,2176]{1,0:T(8,128)(2,1)S(1)}, u32[]{:S(2)}, u32[]{:S(2)}) collective-permute-start(bf16[32,2176]{1,0:T(8,128)(2,1)S(1)} %get-tuple-element.74), channel_id=1, source_target_pairs={{0,4},{4,8},{8,12},{12,14},{14,10},{10,6},{6,2},{2,0},{1,5},{5,9},... | collective-permute-start | bytes 417800 | tf_op jit(solution)/shard_map/ppermute | solution.py:389
  47.5 0.4 collective-permute-start.17
  47.9 4.6 %shard_map.115 = (f32[128,2048]{1,0:T(8,128)}, f32[32,768]{1,0:T(8,128)S(1)}, f32[32,2048]{1,0:T(8,128)S(1)}, bf16[64,2048]{1,0:T(8,128)(2,1)S(1)}, bf16[64,2048]{1,0:T(8,128)(2,1)S(1)}) custom-call(bf16[64,2176]{1,0:T(8,128)(2,1)S(1)} %collective-permute-done.9.refs_0_.first_ref, bf16[64,2176]{1,0:T(8,128)(2,1)S(1)} %collective-permute-done.10.refs_1_.second_ref, ...), custom_call_target="tpu_custom_call" | custom-call | flops 2013265920 | bytes 11091968 | tf_op jit(solution)/shard_map/pallas_call | solution.py:265
  52.5 0.0 collective-permute-start.13
  52.5 2.0 %collective-permute-start.14 = (bf16[64,2048]{1,0:T(8,128)(2,1)S(1)}, bf16[64,2048]{1,0:T(8,128)(2,1)S(1)}, u32[]{:S(2)}, u32[]{:S(2)}) collective-permute-start(bf16[64,2048]{1,0:T(8,128)(2,1)S(1)} %get-tuple-element.70), channel_id=1, source_target_pairs={{0,4},{4,8},{8,12},{12,14},{14,10},{10,6},{6,2},{2,0},{1,5},{5,9},... | collective-permute-start | bytes 786440 | tf_op jit(solution)/shard_map/ppermute | solution.py:359
  54.5 3.7 %shard_map.119 = (f32[32,768]{1,0:T(8,128)S(1)}, f32[32,2048]{1,0:T(8,128)S(1)}, bf16[64,1024]{1,0:T(8,128)(2,1)S(1)}, bf16[64,1024]{1,0:T(8,128)(2,1)S(1)}) custom-call(bf16[32,2176]{1,0:T(8,128)(2,1)S(1)} %collective-permute-done.16.refs_0_, bf16[32,2176]{1,0:T(8,128)(2,1)S(1)} %collective-permute-done.17.refs_1_, ...), custom_call_target="tpu_custom_call" | custom-call | flops 1006632960 | bytes 10534912 | tf_op jit(solution)/shard_map/pallas_call | solution.py:265
  58.2 2.4 %collective-permute-start.20 = (bf16[64,1024]{1,0:T(8,128)(2,1)S(1)}, bf16[64,1024]{1,0:T(8,128)(2,1)S(1)}, u32[]{:S(2)}, u32[]{:S(2)}) collective-permute-start(bf16[64,1024]{1,0:T(8,128)(2,1)S(1)} %get-tuple-element.80), channel_id=1, source_target_pairs={{0,10},{4,6},{8,2},{12,0},{14,4},{10,8},{6,12},{2,14},{1,11},{5,7}... | collective-permute-start | bytes 393224 | tf_op jit(solution)/shard_map/ppermute | solution.py:405
  60.7 1.6 %collective-permute-start.15 = (bf16[64,1024]{1,0:T(8,128)(2,1)S(1)}, bf16[64,1024]{1,0:T(8,128)(2,1)S(1)}, u32[]{:S(2)}, u32[]{:S(2)}) collective-permute-start(bf16[64,1024]{1,0:T(8,128)(2,1)S(1)} %get-tuple-element.71), channel_id=1, source_target_pairs={{4,0},{8,4},{12,8},{14,12},{10,14},{6,10},{2,6},{0,2},{5,1},{9,5},... | collective-permute-start | bytes 393224 | tf_op jit(solution)/shard_map/ppermute | solution.py:359
  62.3 0.4 collective-permute-start.21
  62.8 2.4 %collective-permute-start.26 = (bf16[64,1024]{1,0:T(8,128)(2,1)S(1)}, bf16[64,1024]{1,0:T(8,128)(2,1)S(1)}, u32[]{:S(2)}, u32[]{:S(2)}) collective-permute-start(bf16[64,1024]{1,0:T(8,128)(2,1)S(1)} %get-tuple-element.86), channel_id=1, source_target_pairs={{0,12},{4,14},{8,10},{12,6},{14,2},{10,0},{6,4},{2,8},{1,13},{5,15... | collective-permute-start | bytes 393224 | tf_op jit(solution)/shard_map/ppermute | solution.py:405
  65.3 1.7 %collective-permute-start.24 = (bf16[64,1024]{1,0:T(8,128)(2,1)S(1)}, bf16[64,1024]{1,0:T(8,128)(2,1)S(1)}, u32[]{:S(2)}, u32[]{:S(2)}) collective-permute-start(bf16[64,1024]{1,0:T(8,128)(2,1)S(1)} %get-tuple-element.84), channel_id=1, source_target_pairs={{4,0},{8,4},{12,8},{14,12},{10,14},{6,10},{2,6},{0,2},{5,1},{9,5},... | collective-permute-start | bytes 393224 | tf_op jit(solution)/shard_map/ppermute | solution.py:359
  67.0 1.2 %collective-permute-start.25 = (bf16[64,1024]{1,0:T(8,128)(2,1)S(1)}, bf16[64,1024]{1,0:T(8,128)(2,1)S(1)}, u32[]{:S(2)}, u32[]{:S(2)}) collective-permute-start(bf16[64,1024]{1,0:T(8,128)(2,1)S(1)} %get-tuple-element.85), channel_id=1, source_target_pairs={{0,4},{4,8},{8,12},{12,14},{14,10},{10,6},{6,2},{2,0},{1,5},{5,9},... | collective-permute-start | bytes 393224 | tf_op jit(solution)/shard_map/ppermute | solution.py:359
  68.2 0.1 shard_map.124
  68.3 0.5 collective-permute-done.15.refs_1_
  68.9 0.1 shard_map.120
  68.9 4.7 %collective-permute-start.22 = (bf16[64,1024]{1,0:T(8,128)(2,1)S(1)}, bf16[64,1024]{1,0:T(8,128)(2,1)S(1)}, u32[]{:S(2)}, u32[]{:S(2)}) collective-permute-start(bf16[64,1024]{1,0:T(8,128)(2,1)S(1)} %get-tuple-element.82), channel_id=1, source_target_pairs={{4,0},{8,4},{12,8},{14,12},{10,14},{6,10},{2,6},{0,2},{5,1},{9,5},... | collective-permute-start | bytes 393224 | tf_op jit(solution)/shard_map/ppermute | solution.py:359
  73.6 1.0 %collective-permute-done.26.refs_3_ = bf16[64,1024]{1,0:T(8,128)(2,1)S(1)} collective-permute-done((bf16[64,1024]{1,0:T(8,128)(2,1)S(1)}, bf16[64,1024]{1,0:T(8,128)(2,1)S(1)}, u32[]{:S(2)}, u32[]{:S(2)}) %collective-permute-start.26) | collective-permute-done | bytes 131104 | tf_op jit(solution)/shard_map/ppermute | solution.py:405
  74.6 0.1 shard_map.122
  74.7 2.1 %collective-permute-start.27 = (bf16[64,1024]{1,0:T(8,128)(2,1)S(1)}, bf16[64,1024]{1,0:T(8,128)(2,1)S(1)}, u32[]{:S(2)}, u32[]{:S(2)}) collective-permute-start(bf16[64,1024]{1,0:T(8,128)(2,1)S(1)} %get-tuple-element.87), channel_id=1, source_target_pairs={{4,0},{8,4},{12,8},{14,12},{10,14},{6,10},{2,6},{0,2},{5,1},{9,5},... | collective-permute-start | bytes 393224 | tf_op jit(solution)/shard_map/ppermute | solution.py:359
  76.7 0.0 collective-permute-start.28
  76.8 0.7 shard_map.125
  77.4 0.1 collective-permute-done.22.refs_1_
  77.5 2.9 %collective-permute-done.23.refs_2_ = bf16[64,1024]{1,0:T(8,128)(2,1)S(1)} collective-permute-done((bf16[64,1024]{1,0:T(8,128)(2,1)S(1)}, bf16[64,1024]{1,0:T(8,128)(2,1)S(1)}, u32[]{:S(2)}, u32[]{:S(2)}) %collective-permute-start.23) | collective-permute-done | bytes 131104 | tf_op jit(solution)/shard_map/ppermute | solution.py:359
  80.4 1.4 %collective-permute-done.28.refs_4_ = bf16[64,1024]{1,0:T(8,128)(2,1)S(1)} collective-permute-done((bf16[64,1024]{1,0:T(8,128)(2,1)S(1)}, bf16[64,1024]{1,0:T(8,128)(2,1)S(1)}, u32[]{:S(2)}, u32[]{:S(2)}) %collective-permute-start.28) | collective-permute-done | bytes 131104 | tf_op jit(solution)/shard_map/ppermute | solution.py:359
  81.8 0.8 shard_map.123
  (30 shorter events, 0.2 us)
Async XLA Ops:
  0.6 27.3 %copy-start = (bf16[2,16,2048]{2,1,0:T(8,128)(2,1)S(1)}, bf16[2,16,2048]{2,1,0:T(8,128)(2,1)}, u32[]{:S(2)}) copy-start(bf16[2,16,2048]{2,1,0:T(8,128)(2,1)} %param.17) | copy-start | bytes 393220
  3.3 24.6 %collective-permute-start.4 = (bf16[1024,2304]{1,0:T(8,128)(2,1)S(1)}, bf16[1024,2304]{1,0:T(8,128)(2,1)S(1)}, u32[]{:S(2)}, u32[]{:S(2)}) collective-permute-start(bf16[1024,2304]{1,0:T(8,128)(2,1)S(1)} %get-tuple-element.52.refs_8_.refs_6_), channel_id=1, source_target_pairs={{0,1},{1,0},{2,3},{3,2},{4,5},{5,4},{6,7},{7,6},{8,9},{9,8},{10,11... | collective-permute-start | bytes 14155784 | tf_op jit(solution)/shard_map/ppermute | solution.py:339
  3.8 10.1 %collective-permute-start.2 = (bf16[64,2176]{1,0:T(8,128)(2,1)S(1)}, bf16[64,2176]{1,0:T(8,128)(2,1)S(1)}, u32[]{:S(2)}, u32[]{:S(2)}) collective-permute-start(bf16[64,2176]{1,0:T(8,128)(2,1)S(1)} %get-tuple-element.50.refs_5_), channel_id=1, source_target_pairs={{0,4},{4,8},{8,12},{12,14},{14,10},{10,6},{6,2},{2,0},{1,5},{5,9},... | collective-permute-start | bytes 835592 | tf_op jit(solution)/shard_map/ppermute | solution.py:377
  6.5 9.5 %collective-permute-start.3 = (bf16[64,2176]{1,0:T(8,128)(2,1)S(1)}, bf16[64,2176]{1,0:T(8,128)(2,1)S(1)}, u32[]{:S(2)}, u32[]{:S(2)}) collective-permute-start(bf16[64,2176]{1,0:T(8,128)(2,1)S(1)} %get-tuple-element.50.refs_5_), channel_id=1, source_target_pairs={{4,0},{8,4},{12,8},{14,12},{10,14},{6,10},{2,6},{0,2},{5,1},{9,5},... | collective-permute-start | bytes 835592 | tf_op jit(solution)/shard_map/ppermute | solution.py:378
  6.5 13.4 %collective-permute-start = (bf16[64,2176]{1,0:T(8,128)(2,1)S(1)}, bf16[64,2176]{1,0:T(8,128)(2,1)S(1)}, u32[]{:S(2)}, u32[]{:S(2)}) collective-permute-start(bf16[64,2176]{1,0:T(8,128)(2,1)S(1)} %get-tuple-element.49.refs_2_), channel_id=1, source_target_pairs={{0,4},{4,8},{8,12},{12,14},{14,10},{10,6},{6,2},{2,0},{1,5},{5,9},... | collective-permute-start | bytes 835592 | tf_op jit(solution)/shard_map/ppermute | solution.py:377
  8.5 13.4 %collective-permute-start.1 = (bf16[64,2176]{1,0:T(8,128)(2,1)S(1)}, bf16[64,2176]{1,0:T(8,128)(2,1)S(1)}, u32[]{:S(2)}, u32[]{:S(2)}) collective-permute-start(bf16[64,2176]{1,0:T(8,128)(2,1)S(1)} %get-tuple-element.49.refs_2_), channel_id=1, source_target_pairs={{4,0},{8,4},{12,8},{14,12},{10,14},{6,10},{2,6},{0,2},{5,1},{9,5},... | collective-permute-start | bytes 835592 | tf_op jit(solution)/shard_map/ppermute | solution.py:378
  13.9 11.9 %collective-permute-start.7 = (bf16[64,2176]{1,0:T(8,128)(2,1)S(1)}, bf16[64,2176]{1,0:T(8,128)(2,1)S(1)}, u32[]{:S(2)}, u32[]{:S(2)}) collective-permute-start(bf16[64,2176]{1,0:T(8,128)(2,1)S(1)} %collective-permute-done.2.refs_3_), channel_id=1, source_target_pairs={{0,4},{4,8},{8,12},{12,14},{14,10},{10,6},{6,2},{2,0},{1,5},{5,9},... | collective-permute-start | bytes 835592 | tf_op jit(solution)/shard_map/ppermute | solution.py:377
  16.0 11.9 %collective-permute-start.8 = (bf16[64,2176]{1,0:T(8,128)(2,1)S(1)}, bf16[64,2176]{1,0:T(8,128)(2,1)S(1)}, u32[]{:S(2)}, u32[]{:S(2)}) collective-permute-start(bf16[64,2176]{1,0:T(8,128)(2,1)S(1)} %collective-permute-done.3.refs_4_), channel_id=1, source_target_pairs={{4,0},{8,4},{12,8},{14,12},{10,14},{6,10},{2,6},{0,2},{5,1},{9,5},... | collective-permute-start | bytes 835592 | tf_op jit(solution)/shard_map/ppermute | solution.py:378
  19.9 12.5 %collective-permute-start.5 = (bf16[64,2176]{1,0:T(8,128)(2,1)S(1)}, bf16[64,2176]{1,0:T(8,128)(2,1)S(1)}, u32[]{:S(2)}, u32[]{:S(2)}) collective-permute-start(bf16[64,2176]{1,0:T(8,128)(2,1)S(1)} %collective-permute-done.refs_0_), channel_id=1, source_target_pairs={{0,4},{4,8},{8,12},{12,14},{14,10},{10,6},{6,2},{2,0},{1,5},{5,9},... | collective-permute-start | bytes 835592 | tf_op jit(solution)/shard_map/ppermute | solution.py:377
  21.9 12.5 %collective-permute-start.6 = (bf16[64,2176]{1,0:T(8,128)(2,1)S(1)}, bf16[64,2176]{1,0:T(8,128)(2,1)S(1)}, u32[]{:S(2)}, u32[]{:S(2)}) collective-permute-start(bf16[64,2176]{1,0:T(8,128)(2,1)S(1)} %collective-permute-done.1.refs_1_), channel_id=1, source_target_pairs={{4,0},{8,4},{12,8},{14,12},{10,14},{6,10},{2,6},{0,2},{5,1},{9,5},... | collective-permute-start | bytes 835592 | tf_op jit(solution)/shard_map/ppermute | solution.py:378
  25.8 11.9 %collective-permute-start.11 = (bf16[64,2176]{1,0:T(8,128)(2,1)S(1)}, bf16[64,2176]{1,0:T(8,128)(2,1)S(1)}, u32[]{:S(2)}, u32[]{:S(2)}) collective-permute-start(bf16[64,2176]{1,0:T(8,128)(2,1)S(1)} %collective-permute-done.7.refs_2_), channel_id=1, source_target_pairs={{0,4},{4,8},{8,12},{12,14},{14,10},{10,6},{6,2},{2,0},{1,5},{5,9},... | collective-permute-start | bytes 835592 | tf_op jit(solution)/shard_map/ppermute | solution.py:377
  27.9 11.9 %collective-permute-start.12 = (bf16[64,2176]{1,0:T(8,128)(2,1)S(1)}, bf16[64,2176]{1,0:T(8,128)(2,1)S(1)}, u32[]{:S(2)}, u32[]{:S(2)}) collective-permute-start(bf16[64,2176]{1,0:T(8,128)(2,1)S(1)} %collective-permute-done.8.refs_3_), channel_id=1, source_target_pairs={{4,0},{8,4},{12,8},{14,12},{10,14},{6,10},{2,6},{0,2},{5,1},{9,5},... | collective-permute-start | bytes 835592 | tf_op jit(solution)/shard_map/ppermute | solution.py:378
  32.4 13.0 %collective-permute-start.9 = (bf16[64,2176]{1,0:T(8,128)(2,1)S(1)}, bf16[64,2176]{1,0:T(8,128)(2,1)S(1)}, u32[]{:S(2)}, u32[]{:S(2)}) collective-permute-start(bf16[64,2176]{1,0:T(8,128)(2,1)S(1)} %collective-permute-done.5.refs_0_), channel_id=1, source_target_pairs={{0,4},{4,8},{8,12},{12,14},{14,10},{10,6},{6,2},{2,0},{1,5},{5,9},... | collective-permute-start | bytes 835592 | tf_op jit(solution)/shard_map/ppermute | solution.py:377
  34.5 11.3 %collective-permute-start.10 = (bf16[64,2176]{1,0:T(8,128)(2,1)S(1)}, bf16[64,2176]{1,0:T(8,128)(2,1)S(1)}, u32[]{:S(2)}, u32[]{:S(2)}) collective-permute-start(bf16[64,2176]{1,0:T(8,128)(2,1)S(1)} %collective-permute-done.6.refs_1_), channel_id=1, source_target_pairs={{4,0},{8,4},{12,8},{14,12},{10,14},{6,10},{2,6},{0,2},{5,1},{9,5},... | collective-permute-start | bytes 835592 | tf_op jit(solution)/shard_map/ppermute | solution.py:378
  39.9 12.6 %collective-permute-start.18 = (bf16[32,2176]{1,0:T(8,128)(2,1)S(1)}, bf16[32,2176]{1,0:T(8,128)(2,1)S(1)}, u32[]{:S(2)}, u32[]{:S(2)}) collective-permute-start(bf16[32,2176]{1,0:T(8,128)(2,1)S(1)} %get-tuple-element.76), channel_id=1, source_target_pairs={{0,4},{4,8},{8,12},{12,14},{14,10},{10,6},{6,2},{2,0},{1,5},{5,9},... | collective-permute-start | bytes 417800 | tf_op jit(solution)/shard_map/ppermute | solution.py:389
  41.5 13.0 %collective-permute-start.19 = (bf16[32,2176]{1,0:T(8,128)(2,1)S(1)}, bf16[32,2176]{1,0:T(8,128)(2,1)S(1)}, u32[]{:S(2)}, u32[]{:S(2)}) collective-permute-start(bf16[32,2176]{1,0:T(8,128)(2,1)S(1)} %get-tuple-element.77), channel_id=1, source_target_pairs={{4,0},{8,4},{12,8},{14,12},{10,14},{6,10},{2,6},{0,2},{5,1},{9,5},... | collective-permute-start | bytes 417800 | tf_op jit(solution)/shard_map/ppermute | solution.py:390
  45.8 8.7 %collective-permute-start.16 = (bf16[32,2176]{1,0:T(8,128)(2,1)S(1)}, bf16[32,2176]{1,0:T(8,128)(2,1)S(1)}, u32[]{:S(2)}, u32[]{:S(2)}) collective-permute-start(bf16[32,2176]{1,0:T(8,128)(2,1)S(1)} %get-tuple-element.74), channel_id=1, source_target_pairs={{0,4},{4,8},{8,12},{12,14},{14,10},{10,6},{6,2},{2,0},{1,5},{5,9},... | collective-permute-start | bytes 417800 | tf_op jit(solution)/shard_map/ppermute | solution.py:389
  47.5 7.0 %collective-permute-start.17 = (bf16[32,2176]{1,0:T(8,128)(2,1)S(1)}, bf16[32,2176]{1,0:T(8,128)(2,1)S(1)}, u32[]{:S(2)}, u32[]{:S(2)}) collective-permute-start(bf16[32,2176]{1,0:T(8,128)(2,1)S(1)} %get-tuple-element.75), channel_id=1, source_target_pairs={{4,0},{8,4},{12,8},{14,12},{10,14},{6,10},{2,6},{0,2},{5,1},{9,5},... | collective-permute-start | bytes 417800 | tf_op jit(solution)/shard_map/ppermute | solution.py:390
  52.5 8.2 %collective-permute-start.13 = (bf16[64,2048]{1,0:T(8,128)(2,1)S(1)}, bf16[64,2048]{1,0:T(8,128)(2,1)S(1)}, u32[]{:S(2)}, u32[]{:S(2)}) collective-permute-start(bf16[64,2048]{1,0:T(8,128)(2,1)S(1)} %get-tuple-element.69), channel_id=1, source_target_pairs={{4,0},{8,4},{12,8},{14,12},{10,14},{6,10},{2,6},{0,2},{5,1},{9,5},... | collective-permute-start | bytes 786440 | tf_op jit(solution)/shard_map/ppermute | solution.py:359
  52.5 8.2 %collective-permute-start.14 = (bf16[64,2048]{1,0:T(8,128)(2,1)S(1)}, bf16[64,2048]{1,0:T(8,128)(2,1)S(1)}, u32[]{:S(2)}, u32[]{:S(2)}) collective-permute-start(bf16[64,2048]{1,0:T(8,128)(2,1)S(1)} %get-tuple-element.70), channel_id=1, source_target_pairs={{0,4},{4,8},{8,12},{12,14},{14,10},{10,6},{6,2},{2,0},{1,5},{5,9},... | collective-permute-start | bytes 786440 | tf_op jit(solution)/shard_map/ppermute | solution.py:359
  58.2 8.8 %collective-permute-start.20 = (bf16[64,1024]{1,0:T(8,128)(2,1)S(1)}, bf16[64,1024]{1,0:T(8,128)(2,1)S(1)}, u32[]{:S(2)}, u32[]{:S(2)}) collective-permute-start(bf16[64,1024]{1,0:T(8,128)(2,1)S(1)} %get-tuple-element.80), channel_id=1, source_target_pairs={{0,10},{4,6},{8,2},{12,0},{14,4},{10,8},{6,12},{2,14},{1,11},{5,7}... | collective-permute-start | bytes 393224 | tf_op jit(solution)/shard_map/ppermute | solution.py:405
  60.7 8.1 %collective-permute-start.15 = (bf16[64,1024]{1,0:T(8,128)(2,1)S(1)}, bf16[64,1024]{1,0:T(8,128)(2,1)S(1)}, u32[]{:S(2)}, u32[]{:S(2)}) collective-permute-start(bf16[64,1024]{1,0:T(8,128)(2,1)S(1)} %get-tuple-element.71), channel_id=1, source_target_pairs={{4,0},{8,4},{12,8},{14,12},{10,14},{6,10},{2,6},{0,2},{5,1},{9,5},... | collective-permute-start | bytes 393224 | tf_op jit(solution)/shard_map/ppermute | solution.py:359
  62.3 6.5 %collective-permute-start.21 = (bf16[64,1024]{1,0:T(8,128)(2,1)S(1)}, bf16[64,1024]{1,0:T(8,128)(2,1)S(1)}, u32[]{:S(2)}, u32[]{:S(2)}) collective-permute-start(bf16[64,1024]{1,0:T(8,128)(2,1)S(1)} %get-tuple-element.81), channel_id=1, source_target_pairs={{0,4},{4,8},{8,12},{12,14},{14,10},{10,6},{6,2},{2,0},{1,5},{5,9},... | collective-permute-start | bytes 393224 | tf_op jit(solution)/shard_map/ppermute | solution.py:359
  62.8 11.8 %collective-permute-start.26 = (bf16[64,1024]{1,0:T(8,128)(2,1)S(1)}, bf16[64,1024]{1,0:T(8,128)(2,1)S(1)}, u32[]{:S(2)}, u32[]{:S(2)}) collective-permute-start(bf16[64,1024]{1,0:T(8,128)(2,1)S(1)} %get-tuple-element.86), channel_id=1, source_target_pairs={{0,12},{4,14},{8,10},{12,6},{14,2},{10,0},{6,4},{2,8},{1,13},{5,15... | collective-permute-start | bytes 393224 | tf_op jit(solution)/shard_map/ppermute | solution.py:405
  65.3 9.3 %collective-permute-start.24 = (bf16[64,1024]{1,0:T(8,128)(2,1)S(1)}, bf16[64,1024]{1,0:T(8,128)(2,1)S(1)}, u32[]{:S(2)}, u32[]{:S(2)}) collective-permute-start(bf16[64,1024]{1,0:T(8,128)(2,1)S(1)} %get-tuple-element.84), channel_id=1, source_target_pairs={{4,0},{8,4},{12,8},{14,12},{10,14},{6,10},{2,6},{0,2},{5,1},{9,5},... | collective-permute-start | bytes 393224 | tf_op jit(solution)/shard_map/ppermute | solution.py:359
  67.0 7.6 %collective-permute-start.25 = (bf16[64,1024]{1,0:T(8,128)(2,1)S(1)}, bf16[64,1024]{1,0:T(8,128)(2,1)S(1)}, u32[]{:S(2)}, u32[]{:S(2)}) collective-permute-start(bf16[64,1024]{1,0:T(8,128)(2,1)S(1)} %get-tuple-element.85), channel_id=1, source_target_pairs={{0,4},{4,8},{8,12},{12,14},{14,10},{10,6},{6,2},{2,0},{1,5},{5,9},... | collective-permute-start | bytes 393224 | tf_op jit(solution)/shard_map/ppermute | solution.py:359
  68.9 7.9 %collective-permute-start.29 = (f32[32,1216]{1,0:T(8,128)S(1)}, f32[32,1216]{1,0:T(8,128)S(1)}, u32[]{:S(2)}, u32[]{:S(2)}) collective-permute-start(f32[32,1216]{1,0:T(8,128)S(1)} %get-tuple-element.92), channel_id=1, source_target_pairs={{0,1},{1,0},{2,3},{3,2},{4,5},{5,4},{6,7},{7,6},{8,9},{9,8},{10,11... | collective-permute-start | bytes 466952 | tf_op jit(solution)/shard_map/ppermute | solution.py:432
  68.9 8.6 %collective-permute-start.22 = (bf16[64,1024]{1,0:T(8,128)(2,1)S(1)}, bf16[64,1024]{1,0:T(8,128)(2,1)S(1)}, u32[]{:S(2)}, u32[]{:S(2)}) collective-permute-start(bf16[64,1024]{1,0:T(8,128)(2,1)S(1)} %get-tuple-element.82), channel_id=1, source_target_pairs={{4,0},{8,4},{12,8},{14,12},{10,14},{6,10},{2,6},{0,2},{5,1},{9,5},... | collective-permute-start | bytes 393224 | tf_op jit(solution)/shard_map/ppermute | solution.py:359
  74.6 5.8 %collective-permute-start.23 = (bf16[64,1024]{1,0:T(8,128)(2,1)S(1)}, bf16[64,1024]{1,0:T(8,128)(2,1)S(1)}, u32[]{:S(2)}, u32[]{:S(2)}) collective-permute-start(bf16[64,1024]{1,0:T(8,128)(2,1)S(1)} %get-tuple-element.83), channel_id=1, source_target_pairs={{0,4},{4,8},{8,12},{12,14},{14,10},{10,6},{6,2},{2,0},{1,5},{5,9},... | collective-permute-start | bytes 393224 | tf_op jit(solution)/shard_map/ppermute | solution.py:359
  74.7 5.7 %collective-permute-start.27 = (bf16[64,1024]{1,0:T(8,128)(2,1)S(1)}, bf16[64,1024]{1,0:T(8,128)(2,1)S(1)}, u32[]{:S(2)}, u32[]{:S(2)}) collective-permute-start(bf16[64,1024]{1,0:T(8,128)(2,1)S(1)} %get-tuple-element.87), channel_id=1, source_target_pairs={{4,0},{8,4},{12,8},{14,12},{10,14},{6,10},{2,6},{0,2},{5,1},{9,5},... | collective-permute-start | bytes 393224 | tf_op jit(solution)/shard_map/ppermute | solution.py:359
  76.7 5.1 %collective-permute-start.28 = (bf16[64,1024]{1,0:T(8,128)(2,1)S(1)}, bf16[64,1024]{1,0:T(8,128)(2,1)S(1)}, u32[]{:S(2)}, u32[]{:S(2)}) collective-permute-start(bf16[64,1024]{1,0:T(8,128)(2,1)S(1)} %get-tuple-element.88), channel_id=1, source_target_pairs={{0,4},{4,8},{8,12},{12,14},{14,10},{10,6},{6,2},{2,0},{1,5},{5,9},... | collective-permute-start | bytes 393224 | tf_op jit(solution)/shard_map/ppermute | solution.py:359

commit v9 on v8

--- a/solution.py
+++ b/solution.py
@@ -180,23 +180,26 @@
         copy.wait()
 
 
-def add_kernel(blocks, *refs):
+def add_kernel(blocks, skip, *refs):
     rows_ref, refs = refs[0], list(refs[1:])
-    outs = refs[-len(blocks) :]
-    for (first_row, span, arrived), out in zip(blocks, outs):
-        total = rows_ref[first_row : first_row + out.shape[0], span]
-        for columns in arrived:
-            total = total + refs.pop(0)[:, columns].astype(f32)
+    skipped_ref = refs.pop(len(blocks)) if skip else None
+    for at, (first_row, span, taken, way) in enumerate(blocks):
+        out = refs[len(blocks) + at]
+        rows = rows_ref[first_row : first_row + out.shape[0], span]
+        total = rows + refs[at][:, taken].astype(f32)
+        if skip:
+            here = skip[0]() == (way == "ahead")
+            total = total + jnp.where(here, skipped_ref[:, skip[1]].astype(f32), 0.0)
         out[...] = total.astype(bf16)
 
 
-def add_sums(rows, row_count, blocks, arrived):
+def add_sums(rows, row_count, blocks, arrived, skip):
     operands = [rows, *arrived]
     return pl.pallas_call(
-        functools.partial(add_kernel, blocks),
+        functools.partial(add_kernel, blocks, skip),
         out_shape=tuple(
             jax.ShapeDtypeStruct((row_count, len(range(*span.indices(rows.shape[1])))), bf16)
-            for _, span, _ in blocks
+            for _, span, _, _ in blocks
         ),
         in_specs=[pl.BlockSpec(memory_space=pltpu.VMEM)] * len(operands),
         out_specs=(pl.BlockSpec(memory_space=pltpu.VMEM),) * len(blocks),
@@ -352,7 +355,6 @@
     columns = {"left": slice(0, middle), "right": slice(middle, model_width)}
     everything = slice(0, model_width)
     ways = {"back": (0, backward), "ahead": (token_count, forward)}
-    skips = {"left": "back", "right": "ahead"}
     moving = {}
 
     def send(value, way):
@@ -390,30 +392,37 @@
             tuple(lax.ppermute(x, "expert", backward) for x in (tokens_a, grads_a)),
         ]
     pieces = [behind[full], ahead[full]]
-    rows_d, *outs = run(pieces, [(first_row, everything) for first_row, _ in ways.values()], totals)
+    blocks = [(first_row, everything) for first_row, _ in ways.values()]
+    outs = run(pieces, blocks, totals, keep_rows=False)
     totals = outs[:2]
     for way, value in zip(ways, outs[2:]):
         for side in columns:
             moving[side, way] = send(value, way) if side == "left" else moving["left", way]
-    skipped = {}
+    skipped = []
     if split:
-        outs = run(far, [(0, span) for span in columns.values()], totals, keep_rows=False)
-        totals = outs[:2]
-        for (side, way), value in zip(skips.items(), outs[2:]):
-            step = -full if way == "back" else full
-            pairs = [(order[i], order[(i + step) % peer_count]) for i in range(peer_count)]
-            skipped[side, way] = lax.ppermute(value, "expert", pairs)
+        *totals, value = run(far, [(0, everything)], totals, keep_rows=False)
+        pairs = [
+            (order[i], order[(i + (full if i % 2 == 0 else -full)) % peer_count])
+            for i in range(peer_count)
+        ]
+        skipped.append(lax.ppermute(value, "expert", pairs))
+
+    def goes_ahead():
+        me = lax.axis_index("expert")
+        place = jnp.where(me % 2 == 0, me // 2, peer_count - 1 - me // 2) if snake else me
+        return (place + full) % 2 == 0
+
     for d in range(full - 1, 0, -1):
         for side, span in columns.items():
             blocks, arrived = [], []
             for way, (first_row, _) in ways.items():
-                taken = [span if d == full - 1 else slice(0, middle)]
+                blocks.append((first_row, span, span if d == full - 1 else slice(0, middle), way))
                 arrived.append(moving[side, way])
-                if d == 1 and (side, way) in skipped:
-                    taken.append(slice(0, middle))
-                    arrived.append(skipped[side, way])
-                blocks.append((first_row, span, taken))
-            for way, value in zip(ways, add_sums(rows_at[d], token_count, blocks, arrived)):
+            skip = (goes_ahead, span) if d == 1 and split else None
+            values = add_sums(
+                rows_at[d], token_count, blocks, arrived + (skipped if skip else []), skip
+            )
+            for way, value in zip(ways, values):
                 moving[side, way] = send(value, way)
     grad_tokens = pl.pallas_call(
         functools.partial(last_kernel, 2 * token_count, list(columns.values())),

time: 82.8 us -> 79.3 us (0.958)
  starting transfers between devices: 36.2 us -> 31.5 us
  waiting for transfers between devices: 24.9 us -> 27 us
  Pallas kernels: 20.7 us -> 19.8 us
    ppermute x10, starting transfers between devices: 13.8 us -> 10.4 us  [send(): return lax.ppermute(value, 'expert', ways[way][1])]
    ppermute x10, waiting for transfers between devices: 4.92 us -> 8 us  [send(): return lax.ppermute(value, 'expert', ways[way][1])]
    ppermute x2 -> x1, starting transfers between devices: 4.87 us -> 3.59 us  [per_device(): skipped.append(lax.ppermute(value, 'expert', pairs))]
    ppermute x2 -> x1, waiting for transfers between devices: 0.98 us -> 0.01 us  [per_device(): skipped.append(lax.ppermute(value, 'expert', pairs))]
    pallas_call x4, Pallas kernels: 16.2 us -> 15.2 us  [expert_call(): pl.pallas_call(functools.partial(whole_kernel, plan, len(pieces), blocks,...]
  transfers between devices with their start and end apart: 30 -> 29, of which waited for: 11 -> 11; matrix products, arithmetic and copies ran while one was open for 0% -> 0% of each run, Pallas kernels for 21% -> 21%
where the time goes in v9:
time: 79.3 us; the launch traced here: 79.2 us
  starting transfers between devices  31.5 us (40%)
  waiting for transfers between devices  27 us (34%)
  Pallas kernels  19.8 us (25%)
    ppermute x8, waiting for transfers between devices, per_device(): lax.ppermute(x, 'expert', forward)  16.5 us
    ppermute x8, starting transfers between devices, per_device(): lax.ppermute(x, 'expert', forward)  16.1 us
    pallas_call x4, Pallas kernels, expert_call(): pl.pallas_call(functools.partial(whole_kernel, plan, len(pieces), blocks,...  15.2 us
    ppermute x10, starting transfers between devices, send(): return lax.ppermute(value, 'expert', ways[way][1])  10.4 us
    ppermute x10, waiting for transfers between devices, send(): return lax.ppermute(value, 'expert', ways[way][1])  8 us
    ppermute x1, starting transfers between devices, per_device(): skipped.append(lax.ppermute(value, 'expert', pairs))  3.59 us
    pallas_call x1, Pallas kernels, per_device(): pl.pallas_call(functools.partial(prepare_kernel, plan), out_shape=(jax.Sh...  2.65 us
    ppermute x6, waiting for transfers between devices, per_device(): ahead.append(tuple((lax.ppermute(x, 'expert', backward) for x in ahead[d])))  2.58 us
  transfers between devices with their start and end apart: 29, of which 11 were waited for; matrix products, arithmetic and copies ran while one was open for 0% of the time, Pallas kernels for 21%

profile of v9, /device:TPU:0, one launch (start us, length us, event | category | flops | bytes accessed | tf_op | source)
XLA Modules:
  0.0 79.2 jit_solution(6024627591592398113)
XLA Ops:
  0.6 2.6 %shard_map.112 = (bf16[1024,2304]{1,0:T(8,128)(2,1)S(1)}, bf16[64,2176]{1,0:T(8,128)(2,1)S(1)}, bf16[64,2176]{1,0:T(8,128)(2,1)S(1)}, bf16[32,768]{1,0:T(8,128)(2,1)S(1)}) custom-call(bf16[2,1024,384]{2,1,0:T(8,128)(2,1)} %refs_0_.1, bf16[2,1024,384]{2,1,0:T(8,128)(2,1)} %refs_1_.1, bf16[2,1024,384]{2,1,0:T(8,128)(2,1)} %refs_2_.1, ...), custom_call_target="tpu_custom_call" | custom-call | tf_op jit(solution)/shard_map/pallas_call | solution.py:310
  3.3 0.5 collective-permute-start.4
  3.8 2.6 %collective-permute-start.2 = (bf16[64,2176]{1,0:T(8,128)(2,1)S(1)}, bf16[64,2176]{1,0:T(8,128)(2,1)S(1)}, u32[]{:S(2)}, u32[]{:S(2)}) collective-permute-start(bf16[64,2176]{1,0:T(8,128)(2,1)S(1)} %get-tuple-element.49.refs_5_), channel_id=1, source_target_pairs={{0,4},{4,8},{8,12},{12,14},{14,10},{10,6},{6,2},{2,0},{1,5},{5,9},... | collective-permute-start | bytes 835592 | tf_op jit(solution)/shard_map/ppermute | solution.py:379
  6.5 2.0 %collective-permute-start = (bf16[64,2176]{1,0:T(8,128)(2,1)S(1)}, bf16[64,2176]{1,0:T(8,128)(2,1)S(1)}, u32[]{:S(2)}, u32[]{:S(2)}) collective-permute-start(bf16[64,2176]{1,0:T(8,128)(2,1)S(1)} %get-tuple-element.48.refs_2_), channel_id=1, source_target_pairs={{0,4},{4,8},{8,12},{12,14},{14,10},{10,6},{6,2},{2,0},{1,5},{5,9},... | collective-permute-start | bytes 835592 | tf_op jit(solution)/shard_map/ppermute | solution.py:379
  8.5 5.4 %collective-permute-done.2.refs_3_ = bf16[64,2176]{1,0:T(8,128)(2,1)S(1)} collective-permute-done((bf16[64,2176]{1,0:T(8,128)(2,1)S(1)}, bf16[64,2176]{1,0:T(8,128)(2,1)S(1)}, u32[]{:S(2)}, u32[]{:S(2)}) %collective-permute-start.2) | collective-permute-done | bytes 278560 | tf_op jit(solution)/shard_map/ppermute | solution.py:379
  13.9 2.0 %collective-permute-start.7 = (bf16[64,2176]{1,0:T(8,128)(2,1)S(1)}, bf16[64,2176]{1,0:T(8,128)(2,1)S(1)}, u32[]{:S(2)}, u32[]{:S(2)}) collective-permute-start(bf16[64,2176]{1,0:T(8,128)(2,1)S(1)} %collective-permute-done.2.refs_3_), channel_id=1, source_target_pairs={{0,4},{4,8},{8,12},{12,14},{14,10},{10,6},{6,2},{2,0},{1,5},{5,9},... | collective-permute-start | bytes 835592 | tf_op jit(solution)/shard_map/ppermute | solution.py:379
  15.9 0.0 collective-permute-done.3.refs_4_
  16.0 0.0 collective-permute-start.8
  16.0 3.9 %collective-permute-done.refs_0_ = bf16[64,2176]{1,0:T(8,128)(2,1)S(1)} collective-permute-done((bf16[64,2176]{1,0:T(8,128)(2,1)S(1)}, bf16[64,2176]{1,0:T(8,128)(2,1)S(1)}, u32[]{:S(2)}, u32[]{:S(2)}) %collective-permute-start) | collective-permute-done | bytes 278560 | tf_op jit(solution)/shard_map/ppermute | solution.py:379
  19.9 2.0 %collective-permute-start.5 = (bf16[64,2176]{1,0:T(8,128)(2,1)S(1)}, bf16[64,2176]{1,0:T(8,128)(2,1)S(1)}, u32[]{:S(2)}, u32[]{:S(2)}) collective-permute-start(bf16[64,2176]{1,0:T(8,128)(2,1)S(1)} %collective-permute-done.refs_0_), channel_id=1, source_target_pairs={{0,4},{4,8},{8,12},{12,14},{14,10},{10,6},{6,2},{2,0},{1,5},{5,9},... | collective-permute-start | bytes 835592 | tf_op jit(solution)/shard_map/ppermute | solution.py:379
  21.9 0.0 collective-permute-done.1.refs_1_
  21.9 3.9 %collective-permute-done.7.refs_2_ = bf16[64,2176]{1,0:T(8,128)(2,1)S(1)} collective-permute-done((bf16[64,2176]{1,0:T(8,128)(2,1)S(1)}, bf16[64,2176]{1,0:T(8,128)(2,1)S(1)}, u32[]{:S(2)}, u32[]{:S(2)}) %collective-permute-start.7) | collective-permute-done | bytes 278560 | tf_op jit(solution)/shard_map/ppermute | solution.py:379
  25.8 2.0 %collective-permute-start.11 = (bf16[64,2176]{1,0:T(8,128)(2,1)S(1)}, bf16[64,2176]{1,0:T(8,128)(2,1)S(1)}, u32[]{:S(2)}, u32[]{:S(2)}) collective-permute-start(bf16[64,2176]{1,0:T(8,128)(2,1)S(1)} %collective-permute-done.7.refs_2_), channel_id=1, source_target_pairs={{0,4},{4,8},{8,12},{12,14},{14,10},{10,6},{6,2},{2,0},{1,5},{5,9},... | collective-permute-start | bytes 835592 | tf_op jit(solution)/shard_map/ppermute | solution.py:379
  27.9 0.0 collective-permute-done.8.refs_3_
  27.9 4.4 %shard_map.113 = (f32[192,2048]{1,0:T(8,128)S(1)}, f32[32,768]{1,0:T(8,128)S(1)}, f32[32,2048]{1,0:T(8,128)S(1)}) custom-call(bf16[64,2176]{1,0:T(8,128)(2,1)S(1)} %collective-permute-done.refs_0_, bf16[64,2176]{1,0:T(8,128)(2,1)S(1)} %collective-permute-done.1.refs_1_, bf16[64,2176]{1,0:T(8,128)(2,1)S(1)} %get-tuple-element.48.refs_2_, ...), custom_call_target="tpu_custom_call" | custom-call | flops 3019898880 | bytes 11649024 | tf_op jit(solution)/shard_map/pallas_call | solution.py:268
  32.4 2.1 %collective-permute-start.9 = (bf16[64,2176]{1,0:T(8,128)(2,1)S(1)}, bf16[64,2176]{1,0:T(8,128)(2,1)S(1)}, u32[]{:S(2)}, u32[]{:S(2)}) collective-permute-start(bf16[64,2176]{1,0:T(8,128)(2,1)S(1)} %collective-permute-done.5.refs_0_), channel_id=1, source_target_pairs={{0,4},{4,8},{8,12},{12,14},{14,10},{10,6},{6,2},{2,0},{1,5},{5,9},... | collective-permute-start | bytes 835592 | tf_op jit(solution)/shard_map/ppermute | solution.py:379
  34.5 0.0 collective-permute-start.10
  34.5 3.3 %collective-permute-done.11.refs_2_.first_ref = bf16[64,2176]{1,0:T(8,128)(2,1)S(1)} collective-permute-done((bf16[64,2176]{1,0:T(8,128)(2,1)S(1)}, bf16[64,2176]{1,0:T(8,128)(2,1)S(1)}, u32[]{:S(2)}, u32[]{:S(2)}) %collective-permute-start.11) | collective-permute-done | bytes 278560 | tf_op jit(solution)/shard_map/ppermute | solution.py:379
  37.8 2.1 %collective-permute-done.12.refs_3_.second_ref = bf16[64,2176]{1,0:T(8,128)(2,1)S(1)} collective-permute-done((bf16[64,2176]{1,0:T(8,128)(2,1)S(1)}, bf16[64,2176]{1,0:T(8,128)(2,1)S(1)}, u32[]{:S(2)}, u32[]{:S(2)}) %collective-permute-start.12) | collective-permute-done | bytes 278560 | tf_op jit(solution)/shard_map/ppermute | solution.py:380
  39.9 1.6 %collective-permute-start.19 = (bf16[32,2176]{1,0:T(8,128)(2,1)S(1)}, bf16[32,2176]{1,0:T(8,128)(2,1)S(1)}, u32[]{:S(2)}, u32[]{:S(2)}) collective-permute-start(bf16[32,2176]{1,0:T(8,128)(2,1)S(1)} %get-tuple-element.76), channel_id=1, source_target_pairs={{0,4},{4,8},{8,12},{12,14},{14,10},{10,6},{6,2},{2,0},{1,5},{5,9},... | collective-permute-start | bytes 417800 | tf_op jit(solution)/shard_map/ppermute | solution.py:391
  41.5 0.4 collective-permute-start.20
  41.9 3.5 %shard_map.114 = (f32[128,2048]{1,0:T(8,128)S(1)}, f32[32,768]{1,0:T(8,128)S(1)}, f32[32,2048]{1,0:T(8,128)S(1)}) custom-call(bf16[64,2176]{1,0:T(8,128)(2,1)S(1)} %collective-permute-done.5.refs_0_, bf16[64,2176]{1,0:T(8,128)(2,1)S(1)} %collective-permute-done.6.refs_1_, bf16[64,2176]{1,0:T(8,128)(2,1)S(1)} %collective-permute-done.7.refs_2_, ...), custom_call_target="tpu_custom_call" | custom-call | flops 2013265920 | bytes 11091968 | tf_op jit(solution)/shard_map/pallas_call | solution.py:268
  45.4 0.4 collective-permute-done.10.refs_1_.second_ref
  45.8 1.6 %collective-permute-start.17 = (bf16[32,2176]{1,0:T(8,128)(2,1)S(1)}, bf16[32,2176]{1,0:T(8,128)(2,1)S(1)}, u32[]{:S(2)}, u32[]{:S(2)}) collective-permute-start(bf16[32,2176]{1,0:T(8,128)(2,1)S(1)} %get-tuple-element.74), channel_id=1, source_target_pairs={{0,4},{4,8},{8,12},{12,14},{14,10},{10,6},{6,2},{2,0},{1,5},{5,9},... | collective-permute-start | bytes 417800 | tf_op jit(solution)/shard_map/ppermute | solution.py:391
  47.5 0.4 collective-permute-start.18
  47.9 3.6 %shard_map.115 = (f32[32,768]{1,0:T(8,128)S(1)}, f32[32,2048]{1,0:T(8,128)S(1)}, bf16[64,2048]{1,0:T(8,128)(2,1)S(1)}, bf16[64,2048]{1,0:T(8,128)(2,1)S(1)}) custom-call(bf16[64,2176]{1,0:T(8,128)(2,1)S(1)} %collective-permute-done.9.refs_0_.first_ref, bf16[64,2176]{1,0:T(8,128)(2,1)S(1)} %collective-permute-done.10.refs_1_.second_ref, ...), custom_call_target="tpu_custom_call" | custom-call | flops 2013265920 | bytes 11091968 | tf_op jit(solution)/shard_map/pallas_call | solution.py:268
  51.5 0.1 collective-permute-start.13
  51.6 2.0 %collective-permute-start.14 = (bf16[64,2048]{1,0:T(8,128)(2,1)S(1)}, bf16[64,2048]{1,0:T(8,128)(2,1)S(1)}, u32[]{:S(2)}, u32[]{:S(2)}) collective-permute-start(bf16[64,2048]{1,0:T(8,128)(2,1)S(1)} %get-tuple-element.69), channel_id=1, source_target_pairs={{0,4},{4,8},{8,12},{12,14},{14,10},{10,6},{6,2},{2,0},{1,5},{5,9},... | collective-permute-start | bytes 786440 | tf_op jit(solution)/shard_map/ppermute | solution.py:361
  53.6 3.7 %shard_map.119 = (f32[32,768]{1,0:T(8,128)S(1)}, f32[32,2048]{1,0:T(8,128)S(1)}, bf16[64,2048]{1,0:T(8,128)(2,1)S(1)}) custom-call(bf16[32,2176]{1,0:T(8,128)(2,1)S(1)} %collective-permute-done.17.refs_0_, bf16[32,2176]{1,0:T(8,128)(2,1)S(1)} %collective-permute-done.18.refs_1_, bf16[32,2176]{1,0:T(8,128)(2,1)S(1)} %collective-permute-done.19.refs_2_, ...), custom_call_target="tpu_custom_call" | custom-call | flops 1006632960 | bytes 10534912 | tf_op jit(solution)/shard_map/pallas_call | solution.py:268
  57.3 3.6 %collective-permute-start.21 = (bf16[64,2048]{1,0:T(8,128)(2,1)S(1)}, bf16[64,2048]{1,0:T(8,128)(2,1)S(1)}, u32[]{:S(2)}, u32[]{:S(2)}) collective-permute-start(bf16[64,2048]{1,0:T(8,128)(2,1)S(1)} %get-tuple-element.80), channel_id=1, source_target_pairs={{0,12},{4,6},{8,10},{12,0},{14,2},{10,8},{6,4},{2,14},{1,13},{5,7}... | collective-permute-start | bytes 786440 | tf_op jit(solution)/shard_map/ppermute | solution.py:408
  61.0 0.5 collective-permute-start.15
  61.4 1.6 %collective-permute-start.16 = (bf16[64,1024]{1,0:T(8,128)(2,1)S(1)}, bf16[64,1024]{1,0:T(8,128)(2,1)S(1)}, u32[]{:S(2)}, u32[]{:S(2)}) collective-permute-start(bf16[64,1024]{1,0:T(8,128)(2,1)S(1)} %get-tuple-element.71), channel_id=1, source_target_pairs={{0,4},{4,8},{8,12},{12,14},{14,10},{10,6},{6,2},{2,0},{1,5},{5,9},... | collective-permute-start | bytes 393224 | tf_op jit(solution)/shard_map/ppermute | solution.py:361
  63.1 0.5 collective-permute-start.24
  63.6 1.6 %collective-permute-start.25 = (bf16[64,1024]{1,0:T(8,128)(2,1)S(1)}, bf16[64,1024]{1,0:T(8,128)(2,1)S(1)}, u32[]{:S(2)}, u32[]{:S(2)}) collective-permute-start(bf16[64,1024]{1,0:T(8,128)(2,1)S(1)} %get-tuple-element.84), channel_id=1, source_target_pairs={{0,4},{4,8},{8,12},{12,14},{14,10},{10,6},{6,2},{2,0},{1,5},{5,9},... | collective-permute-start | bytes 393224 | tf_op jit(solution)/shard_map/ppermute | solution.py:361
  65.2 0.1 shard_map.124
  65.3 4.1 %collective-permute-done.15.refs_1_ = bf16[64,1024]{1,0:T(8,128)(2,1)S(1)} collective-permute-done((bf16[64,1024]{1,0:T(8,128)(2,1)S(1)}, bf16[64,1024]{1,0:T(8,128)(2,1)S(1)}, u32[]{:S(2)}, u32[]{:S(2)}) %collective-permute-start.15) | collective-permute-done | bytes 131104 | tf_op jit(solution)/shard_map/ppermute | solution.py:361
  69.4 0.1 shard_map.120
  69.5 1.1 %collective-permute-start.22 = (bf16[64,1024]{1,0:T(8,128)(2,1)S(1)}, bf16[64,1024]{1,0:T(8,128)(2,1)S(1)}, u32[]{:S(2)}, u32[]{:S(2)}) collective-permute-start(bf16[64,1024]{1,0:T(8,128)(2,1)S(1)} %get-tuple-element.81), channel_id=1, source_target_pairs={{4,0},{8,4},{12,8},{14,12},{10,14},{6,10},{2,6},{0,2},{5,1},{9,5},... | collective-permute-start | bytes 393224 | tf_op jit(solution)/shard_map/ppermute | solution.py:361
  70.6 1.0 %collective-permute-start.23 = (bf16[64,1024]{1,0:T(8,128)(2,1)S(1)}, bf16[64,1024]{1,0:T(8,128)(2,1)S(1)}, u32[]{:S(2)}, u32[]{:S(2)}) collective-permute-start(bf16[64,1024]{1,0:T(8,128)(2,1)S(1)} %get-tuple-element.82), channel_id=1, source_target_pairs={{0,4},{4,8},{8,12},{12,14},{14,10},{10,6},{6,2},{2,0},{1,5},{5,9},... | collective-permute-start | bytes 393224 | tf_op jit(solution)/shard_map/ppermute | solution.py:361
  71.6 0.1 shard_map.122
  71.7 1.1 %collective-permute-start.26 = (bf16[64,1024]{1,0:T(8,128)(2,1)S(1)}, bf16[64,1024]{1,0:T(8,128)(2,1)S(1)}, u32[]{:S(2)}, u32[]{:S(2)}) collective-permute-start(bf16[64,1024]{1,0:T(8,128)(2,1)S(1)} %get-tuple-element.85), channel_id=1, source_target_pairs={{4,0},{8,4},{12,8},{14,12},{10,14},{6,10},{2,6},{0,2},{5,1},{9,5},... | collective-permute-start | bytes 393224 | tf_op jit(solution)/shard_map/ppermute | solution.py:361
  72.8 1.0 %collective-permute-start.27 = (bf16[64,1024]{1,0:T(8,128)(2,1)S(1)}, bf16[64,1024]{1,0:T(8,128)(2,1)S(1)}, u32[]{:S(2)}, u32[]{:S(2)}) collective-permute-start(bf16[64,1024]{1,0:T(8,128)(2,1)S(1)} %get-tuple-element.86), channel_id=1, source_target_pairs={{0,4},{4,8},{8,12},{12,14},{14,10},{10,6},{6,2},{2,0},{1,5},{5,9},... | collective-permute-start | bytes 393224 | tf_op jit(solution)/shard_map/ppermute | solution.py:361
  73.8 0.7 shard_map.125
  74.5 1.4 %collective-permute-done.22.refs_1_ = bf16[64,1024]{1,0:T(8,128)(2,1)S(1)} collective-permute-done((bf16[64,1024]{1,0:T(8,128)(2,1)S(1)}, bf16[64,1024]{1,0:T(8,128)(2,1)S(1)}, u32[]{:S(2)}, u32[]{:S(2)}) %collective-permute-start.22) | collective-permute-done | bytes 131104 | tf_op jit(solution)/shard_map/ppermute | solution.py:361
  75.8 1.0 %collective-permute-done.23.refs_2_ = bf16[64,1024]{1,0:T(8,128)(2,1)S(1)} collective-permute-done((bf16[64,1024]{1,0:T(8,128)(2,1)S(1)}, bf16[64,1024]{1,0:T(8,128)(2,1)S(1)}, u32[]{:S(2)}, u32[]{:S(2)}) %collective-permute-start.23) | collective-permute-done | bytes 131104 | tf_op jit(solution)/shard_map/ppermute | solution.py:361
  76.8 1.5 %collective-permute-done.26.refs_3_ = bf16[64,1024]{1,0:T(8,128)(2,1)S(1)} collective-permute-done((bf16[64,1024]{1,0:T(8,128)(2,1)S(1)}, bf16[64,1024]{1,0:T(8,128)(2,1)S(1)}, u32[]{:S(2)}, u32[]{:S(2)}) %collective-permute-start.26) | collective-permute-done | bytes 131104 | tf_op jit(solution)/shard_map/ppermute | solution.py:361
  78.3 0.1 collective-permute-done.27.refs_4_
  78.4 0.8 shard_map.123
  (28 shorter events, 0.2 us)
Async XLA Ops:
  0.6 27.3 %copy-start = (bf16[2,16,2048]{2,1,0:T(8,128)(2,1)S(1)}, bf16[2,16,2048]{2,1,0:T(8,128)(2,1)}, u32[]{:S(2)}) copy-start(bf16[2,16,2048]{2,1,0:T(8,128)(2,1)} %param.17) | copy-start | bytes 393220
  3.3 24.6 %collective-permute-start.4 = (bf16[1024,2304]{1,0:T(8,128)(2,1)S(1)}, bf16[1024,2304]{1,0:T(8,128)(2,1)S(1)}, u32[]{:S(2)}, u32[]{:S(2)}) collective-permute-start(bf16[1024,2304]{1,0:T(8,128)(2,1)S(1)} %get-tuple-element.51.refs_8_.refs_6_), channel_id=1, source_target_pairs={{0,1},{1,0},{2,3},{3,2},{4,5},{5,4},{6,7},{7,6},{8,9},{9,8},{10,11... | collective-permute-start | bytes 14155784 | tf_op jit(solution)/shard_map/ppermute | solution.py:342
  3.8 10.1 %collective-permute-start.2 = (bf16[64,2176]{1,0:T(8,128)(2,1)S(1)}, bf16[64,2176]{1,0:T(8,128)(2,1)S(1)}, u32[]{:S(2)}, u32[]{:S(2)}) collective-permute-start(bf16[64,2176]{1,0:T(8,128)(2,1)S(1)} %get-tuple-element.49.refs_5_), channel_id=1, source_target_pairs={{0,4},{4,8},{8,12},{12,14},{14,10},{10,6},{6,2},{2,0},{1,5},{5,9},... | collective-permute-start | bytes 835592 | tf_op jit(solution)/shard_map/ppermute | solution.py:379
  6.5 9.5 %collective-permute-start.3 = (bf16[64,2176]{1,0:T(8,128)(2,1)S(1)}, bf16[64,2176]{1,0:T(8,128)(2,1)S(1)}, u32[]{:S(2)}, u32[]{:S(2)}) collective-permute-start(bf16[64,2176]{1,0:T(8,128)(2,1)S(1)} %get-tuple-element.49.refs_5_), channel_id=1, source_target_pairs={{4,0},{8,4},{12,8},{14,12},{10,14},{6,10},{2,6},{0,2},{5,1},{9,5},... | collective-permute-start | bytes 835592 | tf_op jit(solution)/shard_map/ppermute | solution.py:380
  6.5 13.4 %collective-permute-start = (bf16[64,2176]{1,0:T(8,128)(2,1)S(1)}, bf16[64,2176]{1,0:T(8,128)(2,1)S(1)}, u32[]{:S(2)}, u32[]{:S(2)}) collective-permute-start(bf16[64,2176]{1,0:T(8,128)(2,1)S(1)} %get-tuple-element.48.refs_2_), channel_id=1, source_target_pairs={{0,4},{4,8},{8,12},{12,14},{14,10},{10,6},{6,2},{2,0},{1,5},{5,9},... | collective-permute-start | bytes 835592 | tf_op jit(solution)/shard_map/ppermute | solution.py:379
  8.5 13.4 %collective-permute-start.1 = (bf16[64,2176]{1,0:T(8,128)(2,1)S(1)}, bf16[64,2176]{1,0:T(8,128)(2,1)S(1)}, u32[]{:S(2)}, u32[]{:S(2)}) collective-permute-start(bf16[64,2176]{1,0:T(8,128)(2,1)S(1)} %get-tuple-element.48.refs_2_), channel_id=1, source_target_pairs={{4,0},{8,4},{12,8},{14,12},{10,14},{6,10},{2,6},{0,2},{5,1},{9,5},... | collective-permute-start | bytes 835592 | tf_op jit(solution)/shard_map/ppermute | solution.py:380
  13.9 11.9 %collective-permute-start.7 = (bf16[64,2176]{1,0:T(8,128)(2,1)S(1)}, bf16[64,2176]{1,0:T(8,128)(2,1)S(1)}, u32[]{:S(2)}, u32[]{:S(2)}) collective-permute-start(bf16[64,2176]{1,0:T(8,128)(2,1)S(1)} %collective-permute-done.2.refs_3_), channel_id=1, source_target_pairs={{0,4},{4,8},{8,12},{12,14},{14,10},{10,6},{6,2},{2,0},{1,5},{5,9},... | collective-permute-start | bytes 835592 | tf_op jit(solution)/shard_map/ppermute | solution.py:379
  16.0 11.9 %collective-permute-start.8 = (bf16[64,2176]{1,0:T(8,128)(2,1)S(1)}, bf16[64,2176]{1,0:T(8,128)(2,1)S(1)}, u32[]{:S(2)}, u32[]{:S(2)}) collective-permute-start(bf16[64,2176]{1,0:T(8,128)(2,1)S(1)} %collective-permute-done.3.refs_4_), channel_id=1, source_target_pairs={{4,0},{8,4},{12,8},{14,12},{10,14},{6,10},{2,6},{0,2},{5,1},{9,5},... | collective-permute-start | bytes 835592 | tf_op jit(solution)/shard_map/ppermute | solution.py:380
  19.9 12.5 %collective-permute-start.5 = (bf16[64,2176]{1,0:T(8,128)(2,1)S(1)}, bf16[64,2176]{1,0:T(8,128)(2,1)S(1)}, u32[]{:S(2)}, u32[]{:S(2)}) collective-permute-start(bf16[64,2176]{1,0:T(8,128)(2,1)S(1)} %collective-permute-done.refs_0_), channel_id=1, source_target_pairs={{0,4},{4,8},{8,12},{12,14},{14,10},{10,6},{6,2},{2,0},{1,5},{5,9},... | collective-permute-start | bytes 835592 | tf_op jit(solution)/shard_map/ppermute | solution.py:379
  21.9 12.5 %collective-permute-start.6 = (bf16[64,2176]{1,0:T(8,128)(2,1)S(1)}, bf16[64,2176]{1,0:T(8,128)(2,1)S(1)}, u32[]{:S(2)}, u32[]{:S(2)}) collective-permute-start(bf16[64,2176]{1,0:T(8,128)(2,1)S(1)} %collective-permute-done.1.refs_1_), channel_id=1, source_target_pairs={{4,0},{8,4},{12,8},{14,12},{10,14},{6,10},{2,6},{0,2},{5,1},{9,5},... | collective-permute-start | bytes 835592 | tf_op jit(solution)/shard_map/ppermute | solution.py:380
  25.8 11.9 %collective-permute-start.11 = (bf16[64,2176]{1,0:T(8,128)(2,1)S(1)}, bf16[64,2176]{1,0:T(8,128)(2,1)S(1)}, u32[]{:S(2)}, u32[]{:S(2)}) collective-permute-start(bf16[64,2176]{1,0:T(8,128)(2,1)S(1)} %collective-permute-done.7.refs_2_), channel_id=1, source_target_pairs={{0,4},{4,8},{8,12},{12,14},{14,10},{10,6},{6,2},{2,0},{1,5},{5,9},... | collective-permute-start | bytes 835592 | tf_op jit(solution)/shard_map/ppermute | solution.py:379
  27.9 11.9 %collective-permute-start.12 = (bf16[64,2176]{1,0:T(8,128)(2,1)S(1)}, bf16[64,2176]{1,0:T(8,128)(2,1)S(1)}, u32[]{:S(2)}, u32[]{:S(2)}) collective-permute-start(bf16[64,2176]{1,0:T(8,128)(2,1)S(1)} %collective-permute-done.8.refs_3_), channel_id=1, source_target_pairs={{4,0},{8,4},{12,8},{14,12},{10,14},{6,10},{2,6},{0,2},{5,1},{9,5},... | collective-permute-start | bytes 835592 | tf_op jit(solution)/shard_map/ppermute | solution.py:380
  32.4 13.0 %collective-permute-start.9 = (bf16[64,2176]{1,0:T(8,128)(2,1)S(1)}, bf16[64,2176]{1,0:T(8,128)(2,1)S(1)}, u32[]{:S(2)}, u32[]{:S(2)}) collective-permute-start(bf16[64,2176]{1,0:T(8,128)(2,1)S(1)} %collective-permute-done.5.refs_0_), channel_id=1, source_target_pairs={{0,4},{4,8},{8,12},{12,14},{14,10},{10,6},{6,2},{2,0},{1,5},{5,9},... | collective-permute-start | bytes 835592 | tf_op jit(solution)/shard_map/ppermute | solution.py:379
  34.5 11.3 %collective-permute-start.10 = (bf16[64,2176]{1,0:T(8,128)(2,1)S(1)}, bf16[64,2176]{1,0:T(8,128)(2,1)S(1)}, u32[]{:S(2)}, u32[]{:S(2)}) collective-permute-start(bf16[64,2176]{1,0:T(8,128)(2,1)S(1)} %collective-permute-done.6.refs_1_), channel_id=1, source_target_pairs={{4,0},{8,4},{12,8},{14,12},{10,14},{6,10},{2,6},{0,2},{5,1},{9,5},... | collective-permute-start | bytes 835592 | tf_op jit(solution)/shard_map/ppermute | solution.py:380
  39.9 11.7 %collective-permute-start.19 = (bf16[32,2176]{1,0:T(8,128)(2,1)S(1)}, bf16[32,2176]{1,0:T(8,128)(2,1)S(1)}, u32[]{:S(2)}, u32[]{:S(2)}) collective-permute-start(bf16[32,2176]{1,0:T(8,128)(2,1)S(1)} %get-tuple-element.76), channel_id=1, source_target_pairs={{0,4},{4,8},{8,12},{12,14},{14,10},{10,6},{6,2},{2,0},{1,5},{5,9},... | collective-permute-start | bytes 417800 | tf_op jit(solution)/shard_map/ppermute | solution.py:391
  41.5 12.1 %collective-permute-start.20 = (bf16[32,2176]{1,0:T(8,128)(2,1)S(1)}, bf16[32,2176]{1,0:T(8,128)(2,1)S(1)}, u32[]{:S(2)}, u32[]{:S(2)}) collective-permute-start(bf16[32,2176]{1,0:T(8,128)(2,1)S(1)} %get-tuple-element.77), channel_id=1, source_target_pairs={{4,0},{8,4},{12,8},{14,12},{10,14},{6,10},{2,6},{0,2},{5,1},{9,5},... | collective-permute-start | bytes 417800 | tf_op jit(solution)/shard_map/ppermute | solution.py:392
  45.8 7.8 %collective-permute-start.17 = (bf16[32,2176]{1,0:T(8,128)(2,1)S(1)}, bf16[32,2176]{1,0:T(8,128)(2,1)S(1)}, u32[]{:S(2)}, u32[]{:S(2)}) collective-permute-start(bf16[32,2176]{1,0:T(8,128)(2,1)S(1)} %get-tuple-element.74), channel_id=1, source_target_pairs={{0,4},{4,8},{8,12},{12,14},{14,10},{10,6},{6,2},{2,0},{1,5},{5,9},... | collective-permute-start | bytes 417800 | tf_op jit(solution)/shard_map/ppermute | solution.py:391
  47.5 6.1 %collective-permute-start.18 = (bf16[32,2176]{1,0:T(8,128)(2,1)S(1)}, bf16[32,2176]{1,0:T(8,128)(2,1)S(1)}, u32[]{:S(2)}, u32[]{:S(2)}) collective-permute-start(bf16[32,2176]{1,0:T(8,128)(2,1)S(1)} %get-tuple-element.75), channel_id=1, source_target_pairs={{4,0},{8,4},{12,8},{14,12},{10,14},{6,10},{2,6},{0,2},{5,1},{9,5},... | collective-permute-start | bytes 417800 | tf_op jit(solution)/shard_map/ppermute | solution.py:392
  51.5 9.4 %collective-permute-start.13 = (bf16[64,2048]{1,0:T(8,128)(2,1)S(1)}, bf16[64,2048]{1,0:T(8,128)(2,1)S(1)}, u32[]{:S(2)}, u32[]{:S(2)}) collective-permute-start(bf16[64,2048]{1,0:T(8,128)(2,1)S(1)} %get-tuple-element.68), channel_id=1, source_target_pairs={{4,0},{8,4},{12,8},{14,12},{10,14},{6,10},{2,6},{0,2},{5,1},{9,5},... | collective-permute-start | bytes 786440 | tf_op jit(solution)/shard_map/ppermute | solution.py:361
  51.6 9.3 %collective-permute-start.14 = (bf16[64,2048]{1,0:T(8,128)(2,1)S(1)}, bf16[64,2048]{1,0:T(8,128)(2,1)S(1)}, u32[]{:S(2)}, u32[]{:S(2)}) collective-permute-start(bf16[64,2048]{1,0:T(8,128)(2,1)S(1)} %get-tuple-element.69), channel_id=1, source_target_pairs={{0,4},{4,8},{8,12},{12,14},{14,10},{10,6},{6,2},{2,0},{1,5},{5,9},... | collective-permute-start | bytes 786440 | tf_op jit(solution)/shard_map/ppermute | solution.py:361
  57.3 12.1 %collective-permute-start.21 = (bf16[64,2048]{1,0:T(8,128)(2,1)S(1)}, bf16[64,2048]{1,0:T(8,128)(2,1)S(1)}, u32[]{:S(2)}, u32[]{:S(2)}) collective-permute-start(bf16[64,2048]{1,0:T(8,128)(2,1)S(1)} %get-tuple-element.80), channel_id=1, source_target_pairs={{0,12},{4,6},{8,10},{12,0},{14,2},{10,8},{6,4},{2,14},{1,13},{5,7}... | collective-permute-start | bytes 786440 | tf_op jit(solution)/shard_map/ppermute | solution.py:408
  61.0 8.4 %collective-permute-start.15 = (bf16[64,1024]{1,0:T(8,128)(2,1)S(1)}, bf16[64,1024]{1,0:T(8,128)(2,1)S(1)}, u32[]{:S(2)}, u32[]{:S(2)}) collective-permute-start(bf16[64,1024]{1,0:T(8,128)(2,1)S(1)} %get-tuple-element.70), channel_id=1, source_target_pairs={{4,0},{8,4},{12,8},{14,12},{10,14},{6,10},{2,6},{0,2},{5,1},{9,5},... | collective-permute-start | bytes 393224 | tf_op jit(solution)/shard_map/ppermute | solution.py:361
  61.4 7.9 %collective-permute-start.16 = (bf16[64,1024]{1,0:T(8,128)(2,1)S(1)}, bf16[64,1024]{1,0:T(8,128)(2,1)S(1)}, u32[]{:S(2)}, u32[]{:S(2)}) collective-permute-start(bf16[64,1024]{1,0:T(8,128)(2,1)S(1)} %get-tuple-element.71), channel_id=1, source_target_pairs={{0,4},{4,8},{8,12},{12,14},{14,10},{10,6},{6,2},{2,0},{1,5},{5,9},... | collective-permute-start | bytes 393224 | tf_op jit(solution)/shard_map/ppermute | solution.py:361
  63.1 8.5 %collective-permute-start.24 = (bf16[64,1024]{1,0:T(8,128)(2,1)S(1)}, bf16[64,1024]{1,0:T(8,128)(2,1)S(1)}, u32[]{:S(2)}, u32[]{:S(2)}) collective-permute-start(bf16[64,1024]{1,0:T(8,128)(2,1)S(1)} %get-tuple-element.83), channel_id=1, source_target_pairs={{4,0},{8,4},{12,8},{14,12},{10,14},{6,10},{2,6},{0,2},{5,1},{9,5},... | collective-permute-start | bytes 393224 | tf_op jit(solution)/shard_map/ppermute | solution.py:361
  63.6 8.0 %collective-permute-start.25 = (bf16[64,1024]{1,0:T(8,128)(2,1)S(1)}, bf16[64,1024]{1,0:T(8,128)(2,1)S(1)}, u32[]{:S(2)}, u32[]{:S(2)}) collective-permute-start(bf16[64,1024]{1,0:T(8,128)(2,1)S(1)} %get-tuple-element.84), channel_id=1, source_target_pairs={{0,4},{4,8},{8,12},{12,14},{14,10},{10,6},{6,2},{2,0},{1,5},{5,9},... | collective-permute-start | bytes 393224 | tf_op jit(solution)/shard_map/ppermute | solution.py:361
  69.4 4.4 %collective-permute-start.28 = (f32[32,1216]{1,0:T(8,128)S(1)}, f32[32,1216]{1,0:T(8,128)S(1)}, u32[]{:S(2)}, u32[]{:S(2)}) collective-permute-start(f32[32,1216]{1,0:T(8,128)S(1)} %get-tuple-element.90), channel_id=1, source_target_pairs={{0,1},{1,0},{2,3},{3,2},{4,5},{5,4},{6,7},{7,6},{8,9},{9,8},{10,11... | collective-permute-start | bytes 466952 | tf_op jit(solution)/shard_map/ppermute | solution.py:441
  69.5 6.3 %collective-permute-start.22 = (bf16[64,1024]{1,0:T(8,128)(2,1)S(1)}, bf16[64,1024]{1,0:T(8,128)(2,1)S(1)}, u32[]{:S(2)}, u32[]{:S(2)}) collective-permute-start(bf16[64,1024]{1,0:T(8,128)(2,1)S(1)} %get-tuple-element.81), channel_id=1, source_target_pairs={{4,0},{8,4},{12,8},{14,12},{10,14},{6,10},{2,6},{0,2},{5,1},{9,5},... | collective-permute-start | bytes 393224 | tf_op jit(solution)/shard_map/ppermute | solution.py:361
  70.6 6.2 %collective-permute-start.23 = (bf16[64,1024]{1,0:T(8,128)(2,1)S(1)}, bf16[64,1024]{1,0:T(8,128)(2,1)S(1)}, u32[]{:S(2)}, u32[]{:S(2)}) collective-permute-start(bf16[64,1024]{1,0:T(8,128)(2,1)S(1)} %get-tuple-element.82), channel_id=1, source_target_pairs={{0,4},{4,8},{8,12},{12,14},{14,10},{10,6},{6,2},{2,0},{1,5},{5,9},... | collective-permute-start | bytes 393224 | tf_op jit(solution)/shard_map/ppermute | solution.py:361
  71.7 6.6 %collective-permute-start.26 = (bf16[64,1024]{1,0:T(8,128)(2,1)S(1)}, bf16[64,1024]{1,0:T(8,128)(2,1)S(1)}, u32[]{:S(2)}, u32[]{:S(2)}) collective-permute-start(bf16[64,1024]{1,0:T(8,128)(2,1)S(1)} %get-tuple-element.85), channel_id=1, source_target_pairs={{4,0},{8,4},{12,8},{14,12},{10,14},{6,10},{2,6},{0,2},{5,1},{9,5},... | collective-permute-start | bytes 393224 | tf_op jit(solution)/shard_map/ppermute | solution.py:361
  72.8 5.6 %collective-permute-start.27 = (bf16[64,1024]{1,0:T(8,128)(2,1)S(1)}, bf16[64,1024]{1,0:T(8,128)(2,1)S(1)}, u32[]{:S(2)}, u32[]{:S(2)}) collective-permute-start(bf16[64,1024]{1,0:T(8,128)(2,1)S(1)} %get-tuple-element.86), channel_id=1, source_target_pairs={{0,4},{4,8},{8,12},{12,14},{14,10},{10,6},{6,2},{2,0},{1,5},{5,9},... | collective-permute-start | bytes 393224 | tf_op jit(solution)/shard_map/ppermute | solution.py:361

commit v10 on v9

--- a/solution.py
+++ b/solution.py
@@ -36,7 +36,7 @@
 
 
 class Plan:
-    def __init__(self, parts, depth, model_width, hidden_width, rank, experts):
+    def __init__(self, parts, depth, model_width, hidden_width, rank, experts, peers, snake):
         self.parts = parts
         self.depth = depth
         self.model_width = model_width
@@ -45,6 +45,8 @@
         self.experts = experts
         self.wide = experts * hidden_width
         self.ranks = experts * rank
+        self.peers = peers
+        self.snake = snake
 
     def spans(self):
         if self.parts == 1:
@@ -67,14 +69,26 @@
         low_rank = matmul_bt(hidden, factor_in_ref[...])
         return activation, up_pre * derivative, hidden, low_rank
 
-    def scales(self, grad_refs):
-        columns = stacked(grad_refs, slice(self.model_width, None)).astype(f32)
-        lane = lax.broadcasted_iota(jnp.int32, columns.shape, 1)
-        first = lax.axis_index("expert") * self.experts
-        return [
-            jnp.sum(jnp.where(lane == first + j, columns, 0.0), axis=1, keepdims=True)
-            for j in range(self.experts)
-        ]
+    def scales(self, share_ref, offsets, rows):
+        place = self.place()
+        pieces = []
+        for offset in offsets:
+            source = self.device_at(lax.rem(place + offset + self.peers, self.peers))
+            block = jnp.zeros(share_ref.shape[1:], f32)
+            for peer in range(self.peers):
+                block = jnp.where(source == peer, share_ref[peer], block)
+            pieces.append(block.T[:rows, :])
+        columns = jnp.concatenate(pieces, axis=0)
+        return [columns[:, j : j + 1] for j in range(self.experts)]
+
+    def place(self):
+        me = lax.axis_index("expert")
+        return jnp.where(me % 2 == 0, me // 2, self.peers - 1 - me // 2) if self.snake else me
+
+    def device_at(self, place):
+        if not self.snake:
+            return place
+        return jnp.where(place < self.peers // 2, 2 * place, 2 * (self.peers - 1 - place) + 1)
 
     def spread(self, scales, width):
         rows = scales[0].shape[0]
@@ -85,9 +99,8 @@
         return out
 
     def backward(
-        self, grad_refs, activation, slope, factor_in_ref, factor_out_ref, weight_refs, rows_ref
+        self, grad_refs, scales, activation, slope, factor_in_ref, factor_out_ref, weight_refs, rows_ref
     ):
-        scales = self.scales(grad_refs)
         adapter_back, grad_down = 0.0, 0.0
         spans = self.spans()
         for span, weight in zip(spans, weight_refs):
@@ -115,9 +128,9 @@
             out[...] = total[...] + adapter_scale * value
 
 
-def whole_kernel(plan, pieces, blocks, keep_rows, *refs):
+def whole_kernel(plan, pieces, blocks, keep_rows, offsets, piece_rows, *refs):
     token_refs, grad_refs, refs = refs[:pieces], refs[pieces : 2 * pieces], refs[2 * pieces :]
-    factor_in_ref, factor_out_ref, refs = refs[0], refs[1], refs[2:]
+    share_ref, factor_in_ref, factor_out_ref, refs = refs[0], refs[1], refs[2], refs[3:]
     weight_refs, refs = refs[: plan.parts], refs[plan.parts :]
     total_refs, refs = refs[:2], refs[2:]
     if keep_rows:
@@ -127,7 +140,14 @@
     out_refs, send_refs = refs[:2], refs[2:]
     activation, slope, hidden, low_rank = plan.forward(token_refs, factor_in_ref, weight_refs)
     rank_scale, back_scaled = plan.backward(
-        grad_refs, activation, slope, factor_in_ref, factor_out_ref, weight_refs, rows_ref
+        grad_refs,
+        plan.scales(share_ref, offsets, piece_rows),
+        activation,
+        slope,
+        factor_in_ref,
+        factor_out_ref,
+        weight_refs,
+        rows_ref,
     )
     for (first_row, span), send_ref in zip(blocks, send_refs):
         send_ref[...] = rows_ref[first_row : first_row + send_ref.shape[0], span].astype(bf16)
@@ -136,14 +156,10 @@
 
 
 def prepare_kernel(plan, *refs):
-    raw_refs, refs = refs[:3], refs[3:]
-    out_grad_ref, ids_ref, route_ref, factor_ref = refs[:4]
-    tokens_ref, refs = refs[4], refs[5:]
-    packed_ref, grads_ref, tokens_held_ref, factor_in_ref, ids_held, route_held, sems = refs
+    raw_refs, ids_ref, route_ref, factor_ref = refs[:3], refs[3], refs[4], refs[5]
+    packed_ref, share_ref, factor_in_ref, ids_held, route_held, sems = refs[6:]
     width, rank = plan.hidden_width, plan.rank
     pairs = [(ids_ref, ids_held), (route_ref, route_held)]
-    pairs.append((out_grad_ref, grads_ref.at[:, : plan.model_width]))
-    pairs.append((tokens_ref, tokens_held_ref.at[:, : plan.model_width]))
     for kind in range(3):
         for expert in range(plan.experts):
             at = kind * plan.wide + expert * width
@@ -167,15 +183,18 @@
                 ] = jnp.zeros((rank, width), bf16)
     copies[0].wait()
     copies[1].wait()
-    rows, lanes = grads_ref.shape[0], grads_ref.shape[1] - plan.model_width
-    expert_at = lax.broadcasted_iota(jnp.int32, (lanes, rows), 0)
     ids, route = ids_held[...], route_held[...].astype(f32)
-    dense = jnp.zeros((lanes, rows), f32)
+    rows = ids.shape[1]
+    sublanes, lanes = share_ref.shape[1:]
+    row_at = lax.broadcasted_iota(jnp.int32, (plan.peers * sublanes, rows), 0)
+    expert_at = row_at // sublanes * plan.experts + row_at % sublanes
+    expert_at = jnp.where(row_at % sublanes < plan.experts, expert_at, -1)
+    dense = jnp.zeros(expert_at.shape, f32)
     for k in range(ids.shape[0]):
         dense = jnp.where(ids[k : k + 1, :] == expert_at, route[k : k + 1, :], dense)
-    dense = dense.T.astype(bf16)
-    grads_ref[:, plan.model_width :] = dense
-    tokens_held_ref[:, plan.model_width :] = dense
+    share_ref[...] = jnp.zeros(share_ref.shape, f32)
+    for peer in range(plan.peers):
+        share_ref[peer, :, :rows] = dense[peer * sublanes : (peer + 1) * sublanes, :]
     for copy in copies[2:]:
         copy.wait()
 
@@ -203,7 +222,7 @@
         ),
         in_specs=[pl.BlockSpec(memory_space=pltpu.VMEM)] * len(operands),
         out_specs=(pl.BlockSpec(memory_space=pltpu.VMEM),) * len(blocks),
-        compiler_params=pltpu.CompilerParams(vmem_limit_bytes=16 * 1024 * 1024),
+        compiler_params=pltpu.CompilerParams(vmem_limit_bytes=20 * 1024 * 1024),
     )(*operands)
 
 
@@ -254,11 +273,11 @@
         out_shape=tuple(jax.ShapeDtypeStruct(shape, dtype) for shape, dtype in outs),
         in_specs=[pl.BlockSpec(memory_space=pltpu.VMEM)] * len(operands),
         out_specs=(pl.BlockSpec(memory_space=pltpu.VMEM),) * len(outs),
-        compiler_params=pltpu.CompilerParams(vmem_limit_bytes=16 * 1024 * 1024),
+        compiler_params=pltpu.CompilerParams(vmem_limit_bytes=20 * 1024 * 1024),
     )(*operands)
 
 
-def expert_call(plan, pieces, blocks, block_rows, operands, totals, keep_rows):
+def expert_call(plan, pieces, offsets, blocks, block_rows, operands, totals, keep_rows):
     rows = sum(piece[0].shape[0] for piece in pieces)
     operands = [p[0] for p in pieces] + [p[1] for p in pieces] + [*operands, *totals]
     shape = (rows, plan.model_width)
@@ -266,12 +285,12 @@
     widths = [len(range(*span.indices(plan.model_width))) for _, span in blocks]
     outs += [((block_rows, width), bf16) for width in widths]
     return pl.pallas_call(
-        functools.partial(whole_kernel, plan, len(pieces), blocks, keep_rows),
+        functools.partial(whole_kernel, plan, len(pieces), blocks, keep_rows, offsets, block_rows),
         scratch_shapes=[] if keep_rows else [pltpu.VMEM(shape, f32)],
         out_shape=tuple(jax.ShapeDtypeStruct(shape, dtype) for shape, dtype in outs),
         in_specs=[pl.BlockSpec(memory_space=pltpu.VMEM)] * len(operands),
         out_specs=(pl.BlockSpec(memory_space=pltpu.VMEM),) * len(outs),
-        compiler_params=pltpu.CompilerParams(vmem_limit_bytes=16 * 1024 * 1024),
+        compiler_params=pltpu.CompilerParams(vmem_limit_bytes=20 * 1024 * 1024),
         cost_estimate=pl.CostEstimate(
             flops=10 * rows * plan.model_width * plan.wide,
             bytes_accessed=sum(op.size * op.dtype.itemsize for op in operands),
@@ -303,41 +322,33 @@
     backward = [(b, a) for a, b in forward]
     swap = [(0, 1), (1, 0)]
     parts = 2 if dp_count == 2 else 1
-    plan = Plan(parts, depth, model_width, hidden_width, rank, local_count)
+    plan = Plan(parts, depth, model_width, hidden_width, rank, local_count, peer_count, snake)
     wide, ranks = plan.wide, plan.ranks
 
-    lanes = -(-expert_total // lane_count) * lane_count
-    mine, grads, tokens_held, factor_in = pl.pallas_call(
+    sublanes = -(-local_count // 8) * 8
+    lanes = -(-token_count // lane_count) * lane_count
+    mine, share, factor_in = pl.pallas_call(
         functools.partial(prepare_kernel, plan),
         out_shape=(
             jax.ShapeDtypeStruct((depth, 3 * wide), bf16),
-            jax.ShapeDtypeStruct((token_count, model_width + lanes), bf16),
-            jax.ShapeDtypeStruct((token_count, model_width + lanes), bf16),
+            jax.ShapeDtypeStruct((peer_count, sublanes, lanes), f32),
             jax.ShapeDtypeStruct((ranks, wide), bf16),
         ),
-        in_specs=[pl.BlockSpec(memory_space=pltpu.HBM)] * 8,
-        out_specs=(pl.BlockSpec(memory_space=pltpu.VMEM),) * 4,
+        in_specs=[pl.BlockSpec(memory_space=pltpu.HBM)] * 6,
+        out_specs=(pl.BlockSpec(memory_space=pltpu.VMEM),) * 3,
         scratch_shapes=[
             pltpu.VMEM(expert_ids.shape[::-1], jnp.int32),
             pltpu.VMEM(route_weight.shape[::-1], bf16),
-            pltpu.SemaphoreType.DMA((4 + 4 * local_count,)),
+            pltpu.SemaphoreType.DMA((2 + 4 * local_count,)),
         ],
-        compiler_params=pltpu.CompilerParams(vmem_limit_bytes=16 * 1024 * 1024),
+        compiler_params=pltpu.CompilerParams(vmem_limit_bytes=20 * 1024 * 1024),
     )(
         *(
             pltpu.with_memory_space_constraint(x, pltpu.HBM)
-            for x in (
-                gate_weight,
-                up_weight,
-                down_weight,
-                out_grad,
-                expert_ids.T,
-                route_weight.T,
-                adapter_in,
-                tokens,
-            )
+            for x in (gate_weight, up_weight, down_weight, expert_ids.T, route_weight.T, adapter_in)
         )
     )
+    share = lax.all_to_all(share, "expert", split_axis=0, concat_axis=0, tiled=True)
     if parts == 2:
         weights = [mine, lax.ppermute(mine, "dp", swap)]
     else:
@@ -348,7 +359,7 @@
     full = (peer_count - 1) // 2
     split = peer_count % 2 == 0
     totals = (jnp.zeros((ranks, wide), f32), jnp.zeros((ranks, model_width), f32))
-    behind, ahead = [(tokens_held, grads)], [(tokens_held, grads)]
+    behind, ahead = [(tokens, out_grad)], [(tokens, out_grad)]
     rows_at = [None]
 
     middle = model_width // 2
@@ -360,9 +371,11 @@
     def send(value, way):
         return lax.ppermute(value, "expert", ways[way][1])
 
-    def run(pieces, blocks, totals, keep_rows=True):
-        operands = [factor_in, factor_out, *weights]
-        return expert_call(plan, pieces, blocks, token_count, operands, totals, keep_rows)
+    def run(pieces, offsets, blocks, totals, keep_rows=True):
+        operands = [share, factor_in, factor_out, *weights]
+        return expert_call(
+            plan, pieces, offsets, blocks, token_count, operands, totals, keep_rows
+        )
 
     def after(value, *arrays):
         held = []
@@ -380,7 +393,7 @@
         ahead.append(tuple(lax.ppermute(x, "expert", backward) for x in ahead[d]))
         if d > 0:
             pieces = [behind[d], ahead[d]] + ([behind[0]] if d == 1 else [])
-            rows_d, *totals = run(pieces, [], totals)
+            rows_d, *totals = run(pieces, [-d, d] + [0] * (d == 1), [], totals)
             rows_at.append(rows_d)
     if split:
         half = token_count // 2
@@ -393,14 +406,14 @@
         ]
     pieces = [behind[full], ahead[full]]
     blocks = [(first_row, everything) for first_row, _ in ways.values()]
-    outs = run(pieces, blocks, totals, keep_rows=False)
+    outs = run(pieces, [-full, full], blocks, totals, keep_rows=False)
     totals = outs[:2]
     for way, value in zip(ways, outs[2:]):
         for side in columns:
             moving[side, way] = send(value, way) if side == "left" else moving["left", way]
     skipped = []
     if split:
-        *totals, value = run(far, [(0, everything)], totals, keep_rows=False)
+        *totals, value = run(far, [peer_count // 2], [(0, everything)], totals, keep_rows=False)
         pairs = [
             (order[i], order[(i + (full if i % 2 == 0 else -full)) % peer_count])
             for i in range(peer_count)
@@ -408,9 +421,7 @@
         skipped.append(lax.ppermute(value, "expert", pairs))
 
     def goes_ahead():
-        me = lax.axis_index("expert")
-        place = jnp.where(me % 2 == 0, me // 2, peer_count - 1 - me // 2) if snake else me
-        return (place + full) % 2 == 0
+        return (plan.place() + full) % 2 == 0
 
     for d in range(full - 1, 0, -1):
         for side, span in columns.items():
@@ -429,7 +440,7 @@
         out_shape=jax.ShapeDtypeStruct((token_count, model_width), bf16),
         in_specs=[pl.BlockSpec(memory_space=pltpu.VMEM)] * 5,
         out_specs=pl.BlockSpec(memory_space=pltpu.VMEM),
-        compiler_params=pltpu.CompilerParams(vmem_limit_bytes=16 * 1024 * 1024),
+        compiler_params=pltpu.CompilerParams(vmem_limit_bytes=20 * 1024 * 1024),
     )(rows_at[1], *(moving[side, way] for side in columns for way in ways))
 
     narrow = hidden_width // dp_count

time: 79.3 us -> 90.8 us (1.15)
  Pallas kernels: 19.8 us -> 37 us
  waiting for transfers between devices: 27 us -> 16.5 us
  starting transfers between devices: 31.5 us -> 36.2 us
    pallas_call x4, Pallas kernels: 15.2 us -> 30.4 us  [expert_call(): pl.pallas_call(functools.partial(whole_kernel, plan, len(pieces), blocks,...]
    ppermute x8, waiting for transfers between devices: 16.5 us -> 5.86 us  [per_device(): lax.ppermute(x, 'expert', forward)]
    all_to_all x0 -> x1, starting transfers between devices: none -> 6.25 us  [per_device(): lax.all_to_all(share, 'expert', split_axis=0, concat_axis=0, tiled=True)]
    ppermute x8, starting transfers between devices: 16.1 us -> 13.1 us  [per_device(): lax.ppermute(x, 'expert', forward)]
    ppermute x6, waiting for transfers between devices: 2.58 us -> 0.17 us  [per_device(): ahead.append(tuple((lax.ppermute(x, 'expert', backward) for x in ahead[d])))]
    all_to_all x0 -> x1, waiting for transfers between devices: none -> 2.29 us  [per_device(): lax.all_to_all(share, 'expert', split_axis=0, concat_axis=0, tiled=True)]
    pallas_call x1, Pallas kernels: 2.65 us -> 4.67 us  [per_device(): pl.pallas_call(functools.partial(prepare_kernel, plan), out_shape=(jax.Sh...]
    ppermute x2, starting transfers between devices: 0.9 us -> 2.58 us  [per_device(): lax.ppermute(x, 'expert', backward)]
  transfers between devices with their start and end apart: 29 -> 30, of which waited for: 11 -> 9; matrix products, arithmetic and copies ran while one was open for 0% -> 0% of each run, Pallas kernels for 21% -> 35%
where the time goes in v10:
time: 90.8 us; the launch traced here: 90.6 us
  Pallas kernels  37 us (41%)
  starting transfers between devices  36.2 us (40%)
  waiting for transfers between devices  16.5 us (18%)
    pallas_call x4, Pallas kernels, expert_call(): pl.pallas_call(functools.partial(whole_kernel, plan, len(pieces), blocks,...  30.4 us
    ppermute x8, starting transfers between devices, per_device(): lax.ppermute(x, 'expert', forward)  13.1 us
    ppermute x10, starting transfers between devices, send(): return lax.ppermute(value, 'expert', ways[way][1])  10.4 us
    ppermute x10, waiting for transfers between devices, send(): return lax.ppermute(value, 'expert', ways[way][1])  8.19 us
    all_to_all x1, starting transfers between devices, per_device(): lax.all_to_all(share, 'expert', split_axis=0, concat_axis=0, tiled=True)  6.25 us
    ppermute x8, waiting for transfers between devices, per_device(): lax.ppermute(x, 'expert', forward)  5.86 us
    pallas_call x1, Pallas kernels, per_device(): pl.pallas_call(functools.partial(prepare_kernel, plan), out_shape=(jax.Sh...  4.67 us
    ppermute x2, starting transfers between devices, per_device(): lax.ppermute(x, 'expert', backward)  2.58 us
  transfers between devices with their start and end apart: 30, of which 9 were waited for; matrix products, arithmetic and copies ran while one was open for 0% of the time, Pallas kernels for 35%

profile of v10, /device:TPU:0, one launch (start us, length us, event | category | flops | bytes accessed | tf_op | source)
XLA Modules:
  0.0 90.6 jit_solution(27300374565949752)
XLA Ops:
  0.7 4.7 %shard_map.112 = (bf16[1024,2304]{1,0:T(8,128)(2,1)}, f32[8,8,128]{2,1,0:T(8,128)}, bf16[32,768]{1,0:T(8,128)(2,1)S(1)}) custom-call(bf16[2,1024,384]{2,1,0:T(8,128)(2,1)} %refs_0_.1, bf16[2,1024,384]{2,1,0:T(8,128)(2,1)} %refs_1_.1, bf16[2,1024,384]{2,1,0:T(8,128)(2,1)} %refs_2_.2, s32[8,64]{1,0:T(8,128)} %bitcast.7, bf16[8,64]{1,0:T(8,128)(2,1)} %bitcast.8, ...), custom_call_target="tpu_custom_call" | custom-call | tf_op jit(solution)/shard_map/pallas_call | solution.py:330
  5.3 0.5 collective-permute-start.4
  5.9 2.6 %collective-permute-start.2 = (bf16[64,2048]{1,0:T(8,128)(2,1)S(1)}, bf16[64,2048]{1,0:T(8,128)(2,1)S(1)}, u32[]{:S(2)}, u32[]{:S(2)}) collective-permute-start(bf16[64,2048]{1,0:T(8,128)(2,1)S(1)} %copy-done.2), channel_id=1, source_target_pairs={{0,4},{4,8},{8,12},{12,14},{14,10},{10,6},{6,2},{2,0},{1,5},{5,9},... | collective-permute-start | bytes 786440 | tf_op jit(solution)/shard_map/ppermute | solution.py:392
  8.5 0.0 collective-permute-start.3
  8.5 2.0 %collective-permute-start = (bf16[64,2048]{1,0:T(8,128)(2,1)S(1)}, bf16[64,2048]{1,0:T(8,128)(2,1)S(1)}, u32[]{:S(2)}, u32[]{:S(2)}) collective-permute-start(bf16[64,2048]{1,0:T(8,128)(2,1)S(1)} %copy-done.1), channel_id=1, source_target_pairs={{0,4},{4,8},{8,12},{12,14},{14,10},{10,6},{6,2},{2,0},{1,5},{5,9},... | collective-permute-start | bytes 786440 | tf_op jit(solution)/shard_map/ppermute | solution.py:392
  10.5 0.0 collective-permute-start.1
  10.5 5.0 %collective-permute-done.2.refs_3_ = bf16[64,2048]{1,0:T(8,128)(2,1)S(1)} collective-permute-done((bf16[64,2048]{1,0:T(8,128)(2,1)S(1)}, bf16[64,2048]{1,0:T(8,128)(2,1)S(1)}, u32[]{:S(2)}, u32[]{:S(2)}) %collective-permute-start.2) | collective-permute-done | bytes 262176 | tf_op jit(solution)/shard_map/ppermute | solution.py:392
  15.6 2.0 %collective-permute-start.7 = (bf16[64,2048]{1,0:T(8,128)(2,1)S(1)}, bf16[64,2048]{1,0:T(8,128)(2,1)S(1)}, u32[]{:S(2)}, u32[]{:S(2)}) collective-permute-start(bf16[64,2048]{1,0:T(8,128)(2,1)S(1)} %collective-permute-done.2.refs_3_), channel_id=1, source_target_pairs={{0,4},{4,8},{8,12},{12,14},{14,10},{10,6},{6,2},{2,0},{1,5},{5,9},... | collective-permute-start | bytes 786440 | tf_op jit(solution)/shard_map/ppermute | solution.py:392
  17.6 0.0 collective-permute-done.3.refs_4_
  17.7 6.3 %all-to-all-start = ((f32[8,8,128]{2,1,0:T(8,128)}), f32[8,8,128]{2,1,0:T(8,128)S(1)}, u32[]{:S(2)}, u32[]{:S(2)}) async-start(f32[8,8,128]{2,1,0:T(8,128)} %get-tuple-element.47), calls=%async_computation | async-start | bytes 65536 | tf_op jit(solution)/shard_map/all_to_all | solution.py:351
  23.9 0.0 collective-permute-done.refs_0_
  23.9 2.0 %collective-permute-start.5 = (bf16[64,2048]{1,0:T(8,128)(2,1)S(1)}, bf16[64,2048]{1,0:T(8,128)(2,1)S(1)}, u32[]{:S(2)}, u32[]{:S(2)}) collective-permute-start(bf16[64,2048]{1,0:T(8,128)(2,1)S(1)} %collective-permute-done.refs_0_), channel_id=1, source_target_pairs={{0,4},{4,8},{8,12},{12,14},{14,10},{10,6},{6,2},{2,0},{1,5},{5,9},... | collective-permute-start | bytes 786440 | tf_op jit(solution)/shard_map/ppermute | solution.py:392
  25.9 0.1 collective-permute-start.6
  26.0 0.8 collective-permute-done.7.refs_2_
  26.8 2.0 %collective-permute-start.11 = (bf16[64,2048]{1,0:T(8,128)(2,1)S(1)}, bf16[64,2048]{1,0:T(8,128)(2,1)S(1)}, u32[]{:S(2)}, u32[]{:S(2)}) collective-permute-start(bf16[64,2048]{1,0:T(8,128)(2,1)S(1)} %collective-permute-done.7.refs_2_), channel_id=1, source_target_pairs={{0,4},{4,8},{8,12},{12,14},{14,10},{10,6},{6,2},{2,0},{1,5},{5,9},... | collective-permute-start | bytes 786440 | tf_op jit(solution)/shard_map/ppermute | solution.py:392
  28.9 0.1 collective-permute-done.8.refs_3_
  29.0 2.3 %all-to-all-done.refs_6_.refs_4_ = f32[8,8,128]{2,1,0:T(8,128)S(1)} async-done(((f32[8,8,128]{2,1,0:T(8,128)}), f32[8,8,128]{2,1,0:T(8,128)S(1)}, u32[]{:S(2)}, u32[]{:S(2)}) %all-to-all-start) | async-done | bytes 32800 | tf_op jit(solution)/shard_map/all_to_all | solution.py:351
  31.3 8.3 %shard_map.113 = (f32[192,2048]{1,0:T(8,128)S(1)}, f32[32,768]{1,0:T(8,128)S(1)}, f32[32,2048]{1,0:T(8,128)S(1)}) custom-call(bf16[64,2048]{1,0:T(8,128)(2,1)S(1)} %collective-permute-done.refs_0_, bf16[64,2048]{1,0:T(8,128)(2,1)S(1)} %collective-permute-done.1.refs_1_, bf16[64,2048]{1,0:T(8,128)(2,1)S(1)} %copy-done.1, ...), custom_call_target="tpu_custom_call" | custom-call | flops 3019898880 | bytes 11583488 | tf_op jit(solution)/shard_map/pallas_call | solution.py:287
  39.7 0.8 collective-permute-start.9
  40.5 1.3 %collective-permute-start.10 = (bf16[64,2048]{1,0:T(8,128)(2,1)S(1)}, bf16[64,2048]{1,0:T(8,128)(2,1)S(1)}, u32[]{:S(2)}, u32[]{:S(2)}) collective-permute-start(bf16[64,2048]{1,0:T(8,128)(2,1)S(1)} %collective-permute-done.6.refs_1_), channel_id=1, source_target_pairs={{4,0},{8,4},{12,8},{14,12},{10,14},{6,10},{2,6},{0,2},{5,1},{9,5},... | collective-permute-start | bytes 786440 | tf_op jit(solution)/shard_map/ppermute | solution.py:393
  41.8 0.8 collective-permute-start.19
  42.6 1.3 %collective-permute-start.20 = (bf16[32,2048]{1,0:T(8,128)(2,1)S(1)}, bf16[32,2048]{1,0:T(8,128)(2,1)S(1)}, u32[]{:S(2)}, u32[]{:S(2)}) collective-permute-start(bf16[32,2048]{1,0:T(8,128)(2,1)S(1)} %get-tuple-element.75), channel_id=1, source_target_pairs={{4,0},{8,4},{12,8},{14,12},{10,14},{6,10},{2,6},{0,2},{5,1},{9,5},... | collective-permute-start | bytes 393224 | tf_op jit(solution)/shard_map/ppermute | solution.py:405
  43.9 7.3 %shard_map.114 = (f32[128,2048]{1,0:T(8,128)S(1)}, f32[32,768]{1,0:T(8,128)S(1)}, f32[32,2048]{1,0:T(8,128)S(1)}) custom-call(bf16[64,2048]{1,0:T(8,128)(2,1)S(1)} %collective-permute-done.5.refs_0_, bf16[64,2048]{1,0:T(8,128)(2,1)S(1)} %collective-permute-done.6.refs_1_, bf16[64,2048]{1,0:T(8,128)(2,1)S(1)} %collective-permute-done.7.refs_2_, ...), custom_call_target="tpu_custom_call" | custom-call | flops 2013265920 | bytes 11059200 | tf_op jit(solution)/shard_map/pallas_call | solution.py:287
  51.2 0.8 collective-permute-start.17
  52.0 1.3 %collective-permute-start.18 = (bf16[32,2048]{1,0:T(8,128)(2,1)S(1)}, bf16[32,2048]{1,0:T(8,128)(2,1)S(1)}, u32[]{:S(2)}, u32[]{:S(2)}) collective-permute-start(bf16[32,2048]{1,0:T(8,128)(2,1)S(1)} %get-tuple-element.73), channel_id=1, source_target_pairs={{4,0},{8,4},{12,8},{14,12},{10,14},{6,10},{2,6},{0,2},{5,1},{9,5},... | collective-permute-start | bytes 393224 | tf_op jit(solution)/shard_map/ppermute | solution.py:405
  53.3 7.4 %shard_map.115 = (f32[32,768]{1,0:T(8,128)S(1)}, f32[32,2048]{1,0:T(8,128)S(1)}, bf16[64,2048]{1,0:T(8,128)(2,1)S(1)}, bf16[64,2048]{1,0:T(8,128)(2,1)S(1)}) custom-call(bf16[64,2048]{1,0:T(8,128)(2,1)S(1)} %collective-permute-done.9.refs_0_.first_ref, bf16[64,2048]{1,0:T(8,128)(2,1)S(1)} %collective-permute-done.10.refs_1_.second_ref, ...), custom_call_target="tpu_custom_call" | custom-call | flops 2013265920 | bytes 11059200 | tf_op jit(solution)/shard_map/pallas_call | solution.py:287
  60.6 1.3 %collective-permute-start.13 = (bf16[64,2048]{1,0:T(8,128)(2,1)S(1)}, bf16[64,2048]{1,0:T(8,128)(2,1)S(1)}, u32[]{:S(2)}, u32[]{:S(2)}) collective-permute-start(bf16[64,2048]{1,0:T(8,128)(2,1)S(1)} %get-tuple-element.66), channel_id=1, source_target_pairs={{4,0},{8,4},{12,8},{14,12},{10,14},{6,10},{2,6},{0,2},{5,1},{9,5},... | collective-permute-start | bytes 786440 | tf_op jit(solution)/shard_map/ppermute | solution.py:372
  62.0 0.7 collective-permute-start.14
  62.7 7.4 %shard_map.119 = (f32[32,768]{1,0:T(8,128)S(1)}, f32[32,2048]{1,0:T(8,128)S(1)}, bf16[64,2048]{1,0:T(8,128)(2,1)S(1)}) custom-call(bf16[32,2048]{1,0:T(8,128)(2,1)S(1)} %collective-permute-done.17.refs_0_, bf16[32,2048]{1,0:T(8,128)(2,1)S(1)} %collective-permute-done.18.refs_1_, bf16[32,2048]{1,0:T(8,128)(2,1)S(1)} %collective-permute-done.19.refs_2_, ...), custom_call_target="tpu_custom_call" | custom-call | flops 1006632960 | bytes 10534912 | tf_op jit(solution)/shard_map/pallas_call | solution.py:287
  70.2 2.0 %collective-permute-start.21 = (bf16[64,2048]{1,0:T(8,128)(2,1)S(1)}, bf16[64,2048]{1,0:T(8,128)(2,1)S(1)}, u32[]{:S(2)}, u32[]{:S(2)}) collective-permute-start(bf16[64,2048]{1,0:T(8,128)(2,1)S(1)} %get-tuple-element.78), channel_id=1, source_target_pairs={{0,12},{4,6},{8,10},{12,0},{14,2},{10,8},{6,4},{2,14},{1,13},{5,7}... | collective-permute-start | bytes 786440 | tf_op jit(solution)/shard_map/ppermute | solution.py:421
  72.2 1.5 %collective-permute-start.15 = (bf16[64,1024]{1,0:T(8,128)(2,1)S(1)}, bf16[64,1024]{1,0:T(8,128)(2,1)S(1)}, u32[]{:S(2)}, u32[]{:S(2)}) collective-permute-start(bf16[64,1024]{1,0:T(8,128)(2,1)S(1)} %get-tuple-element.68), channel_id=1, source_target_pairs={{4,0},{8,4},{12,8},{14,12},{10,14},{6,10},{2,6},{0,2},{5,1},{9,5},... | collective-permute-start | bytes 393224 | tf_op jit(solution)/shard_map/ppermute | solution.py:372
  73.7 0.5 collective-permute-start.16
  74.3 1.5 %collective-permute-start.24 = (bf16[64,1024]{1,0:T(8,128)(2,1)S(1)}, bf16[64,1024]{1,0:T(8,128)(2,1)S(1)}, u32[]{:S(2)}, u32[]{:S(2)}) collective-permute-start(bf16[64,1024]{1,0:T(8,128)(2,1)S(1)} %get-tuple-element.81), channel_id=1, source_target_pairs={{4,0},{8,4},{12,8},{14,12},{10,14},{6,10},{2,6},{0,2},{5,1},{9,5},... | collective-permute-start | bytes 393224 | tf_op jit(solution)/shard_map/ppermute | solution.py:372
  75.9 0.5 collective-permute-start.25
  76.4 0.1 shard_map.124
  76.6 4.3 %collective-permute-done.15.refs_1_ = bf16[64,1024]{1,0:T(8,128)(2,1)S(1)} collective-permute-done((bf16[64,1024]{1,0:T(8,128)(2,1)S(1)}, bf16[64,1024]{1,0:T(8,128)(2,1)S(1)}, u32[]{:S(2)}, u32[]{:S(2)}) %collective-permute-start.15) | collective-permute-done | bytes 131104 | tf_op jit(solution)/shard_map/ppermute | solution.py:372
  80.9 0.1 shard_map.120
  81.0 0.9 %collective-permute-start.22 = (bf16[64,1024]{1,0:T(8,128)(2,1)S(1)}, bf16[64,1024]{1,0:T(8,128)(2,1)S(1)}, u32[]{:S(2)}, u32[]{:S(2)}) collective-permute-start(bf16[64,1024]{1,0:T(8,128)(2,1)S(1)} %get-tuple-element.79), channel_id=1, source_target_pairs={{4,0},{8,4},{12,8},{14,12},{10,14},{6,10},{2,6},{0,2},{5,1},{9,5},... | collective-permute-start | bytes 393224 | tf_op jit(solution)/shard_map/ppermute | solution.py:372
  81.9 1.1 %collective-permute-start.23 = (bf16[64,1024]{1,0:T(8,128)(2,1)S(1)}, bf16[64,1024]{1,0:T(8,128)(2,1)S(1)}, u32[]{:S(2)}, u32[]{:S(2)}) collective-permute-start(bf16[64,1024]{1,0:T(8,128)(2,1)S(1)} %get-tuple-element.80), channel_id=1, source_target_pairs={{0,4},{4,8},{8,12},{12,14},{14,10},{10,6},{6,2},{2,0},{1,5},{5,9},... | collective-permute-start | bytes 393224 | tf_op jit(solution)/shard_map/ppermute | solution.py:372
  83.1 0.1 shard_map.122
  83.2 0.9 %collective-permute-start.26 = (bf16[64,1024]{1,0:T(8,128)(2,1)S(1)}, bf16[64,1024]{1,0:T(8,128)(2,1)S(1)}, u32[]{:S(2)}, u32[]{:S(2)}) collective-permute-start(bf16[64,1024]{1,0:T(8,128)(2,1)S(1)} %get-tuple-element.83), channel_id=1, source_target_pairs={{4,0},{8,4},{12,8},{14,12},{10,14},{6,10},{2,6},{0,2},{5,1},{9,5},... | collective-permute-start | bytes 393224 | tf_op jit(solution)/shard_map/ppermute | solution.py:372
  84.1 1.1 %collective-permute-start.27 = (bf16[64,1024]{1,0:T(8,128)(2,1)S(1)}, bf16[64,1024]{1,0:T(8,128)(2,1)S(1)}, u32[]{:S(2)}, u32[]{:S(2)}) collective-permute-start(bf16[64,1024]{1,0:T(8,128)(2,1)S(1)} %get-tuple-element.84), channel_id=1, source_target_pairs={{0,4},{4,8},{8,12},{12,14},{14,10},{10,6},{6,2},{2,0},{1,5},{5,9},... | collective-permute-start | bytes 393224 | tf_op jit(solution)/shard_map/ppermute | solution.py:372
  85.3 0.7 shard_map.125
  86.0 1.4 %collective-permute-done.22.refs_1_ = bf16[64,1024]{1,0:T(8,128)(2,1)S(1)} collective-permute-done((bf16[64,1024]{1,0:T(8,128)(2,1)S(1)}, bf16[64,1024]{1,0:T(8,128)(2,1)S(1)}, u32[]{:S(2)}, u32[]{:S(2)}) %collective-permute-start.22) | collective-permute-done | bytes 131104 | tf_op jit(solution)/shard_map/ppermute | solution.py:372
  87.3 0.8 collective-permute-done.23.refs_2_
  88.2 1.6 %collective-permute-done.26.refs_3_ = bf16[64,1024]{1,0:T(8,128)(2,1)S(1)} collective-permute-done((bf16[64,1024]{1,0:T(8,128)(2,1)S(1)}, bf16[64,1024]{1,0:T(8,128)(2,1)S(1)}, u32[]{:S(2)}, u32[]{:S(2)}) %collective-permute-start.26) | collective-permute-done | bytes 131104 | tf_op jit(solution)/shard_map/ppermute | solution.py:372
  89.8 0.1 collective-permute-done.27.refs_4_
  89.8 0.8 shard_map.123
  (34 shorter events, 0.2 us)
Async XLA Ops:
  0.6 5.2 %copy-start.2 = (bf16[64,2048]{1,0:T(8,128)(2,1)S(1)}, bf16[64,2048]{1,0:T(8,128)(2,1)}, u32[]{:S(2)}) copy-start(bf16[64,2048]{1,0:T(8,128)(2,1)} %refs_5_.3) | copy-start | bytes 786436
  0.6 7.9 %copy-start.1 = (bf16[64,2048]{1,0:T(8,128)(2,1)S(1)}, bf16[64,2048]{1,0:T(8,128)(2,1)}, u32[]{:S(2)}) copy-start(bf16[64,2048]{1,0:T(8,128)(2,1)} %refs_2_.3) | copy-start | bytes 786436
  0.7 30.7 %copy-start = (bf16[2,16,2048]{2,1,0:T(8,128)(2,1)S(1)}, bf16[2,16,2048]{2,1,0:T(8,128)(2,1)}, u32[]{:S(2)}) copy-start(bf16[2,16,2048]{2,1,0:T(8,128)(2,1)} %param.17) | copy-start | bytes 393220
  5.3 25.9 %collective-permute-start.4 = (bf16[1024,2304]{1,0:T(8,128)(2,1)}, bf16[1024,2304]{1,0:T(8,128)(2,1)}, u32[]{:S(2)}, u32[]{:S(2)}) collective-permute-start(bf16[1024,2304]{1,0:T(8,128)(2,1)} %get-tuple-element.49.refs_9_.refs_7_), channel_id=1, source_target_pairs={{0,1},{1,0},{2,3},{3,2},{4,5},{5,4},{6,7},{7,6},{8,9},{9,8},{10,11... | collective-permute-start | bytes 14155784 | tf_op jit(solution)/shard_map/ppermute | solution.py:353
  5.9 9.7 %collective-permute-start.2 = (bf16[64,2048]{1,0:T(8,128)(2,1)S(1)}, bf16[64,2048]{1,0:T(8,128)(2,1)S(1)}, u32[]{:S(2)}, u32[]{:S(2)}) collective-permute-start(bf16[64,2048]{1,0:T(8,128)(2,1)S(1)} %copy-done.2), channel_id=1, source_target_pairs={{0,4},{4,8},{8,12},{12,14},{14,10},{10,6},{6,2},{2,0},{1,5},{5,9},... | collective-permute-start | bytes 786440 | tf_op jit(solution)/shard_map/ppermute | solution.py:392
  8.5 9.2 %collective-permute-start.3 = (bf16[64,2048]{1,0:T(8,128)(2,1)S(1)}, bf16[64,2048]{1,0:T(8,128)(2,1)S(1)}, u32[]{:S(2)}, u32[]{:S(2)}) collective-permute-start(bf16[64,2048]{1,0:T(8,128)(2,1)S(1)} %copy-done.2), channel_id=1, source_target_pairs={{4,0},{8,4},{12,8},{14,12},{10,14},{6,10},{2,6},{0,2},{5,1},{9,5},... | collective-permute-start | bytes 786440 | tf_op jit(solution)/shard_map/ppermute | solution.py:393
  8.5 15.4 %collective-permute-start = (bf16[64,2048]{1,0:T(8,128)(2,1)S(1)}, bf16[64,2048]{1,0:T(8,128)(2,1)S(1)}, u32[]{:S(2)}, u32[]{:S(2)}) collective-permute-start(bf16[64,2048]{1,0:T(8,128)(2,1)S(1)} %copy-done.1), channel_id=1, source_target_pairs={{0,4},{4,8},{8,12},{12,14},{14,10},{10,6},{6,2},{2,0},{1,5},{5,9},... | collective-permute-start | bytes 786440 | tf_op jit(solution)/shard_map/ppermute | solution.py:392
  10.5 15.4 %collective-permute-start.1 = (bf16[64,2048]{1,0:T(8,128)(2,1)S(1)}, bf16[64,2048]{1,0:T(8,128)(2,1)S(1)}, u32[]{:S(2)}, u32[]{:S(2)}) collective-permute-start(bf16[64,2048]{1,0:T(8,128)(2,1)S(1)} %copy-done.1), channel_id=1, source_target_pairs={{4,0},{8,4},{12,8},{14,12},{10,14},{6,10},{2,6},{0,2},{5,1},{9,5},... | collective-permute-start | bytes 786440 | tf_op jit(solution)/shard_map/ppermute | solution.py:393
  15.6 11.2 %collective-permute-start.7 = (bf16[64,2048]{1,0:T(8,128)(2,1)S(1)}, bf16[64,2048]{1,0:T(8,128)(2,1)S(1)}, u32[]{:S(2)}, u32[]{:S(2)}) collective-permute-start(bf16[64,2048]{1,0:T(8,128)(2,1)S(1)} %collective-permute-done.2.refs_3_), channel_id=1, source_target_pairs={{0,4},{4,8},{8,12},{12,14},{14,10},{10,6},{6,2},{2,0},{1,5},{5,9},... | collective-permute-start | bytes 786440 | tf_op jit(solution)/shard_map/ppermute | solution.py:392
  17.7 11.3 %collective-permute-start.8 = (bf16[64,2048]{1,0:T(8,128)(2,1)S(1)}, bf16[64,2048]{1,0:T(8,128)(2,1)S(1)}, u32[]{:S(2)}, u32[]{:S(2)}) collective-permute-start(bf16[64,2048]{1,0:T(8,128)(2,1)S(1)} %collective-permute-done.3.refs_4_), channel_id=1, source_target_pairs={{4,0},{8,4},{12,8},{14,12},{10,14},{6,10},{2,6},{0,2},{5,1},{9,5},... | collective-permute-start | bytes 786440 | tf_op jit(solution)/shard_map/ppermute | solution.py:393
  17.7 13.6 %all-to-all-start = ((f32[8,8,128]{2,1,0:T(8,128)}), f32[8,8,128]{2,1,0:T(8,128)S(1)}, u32[]{:S(2)}, u32[]{:S(2)}) async-start(f32[8,8,128]{2,1,0:T(8,128)} %get-tuple-element.47), calls=%async_computation | async-start | bytes 65536 | tf_op jit(solution)/shard_map/all_to_all | solution.py:351
  23.9 15.8 %collective-permute-start.5 = (bf16[64,2048]{1,0:T(8,128)(2,1)S(1)}, bf16[64,2048]{1,0:T(8,128)(2,1)S(1)}, u32[]{:S(2)}, u32[]{:S(2)}) collective-permute-start(bf16[64,2048]{1,0:T(8,128)(2,1)S(1)} %collective-permute-done.refs_0_), channel_id=1, source_target_pairs={{0,4},{4,8},{8,12},{12,14},{14,10},{10,6},{6,2},{2,0},{1,5},{5,9},... | collective-permute-start | bytes 786440 | tf_op jit(solution)/shard_map/ppermute | solution.py:392
  25.9 14.5 %collective-permute-start.6 = (bf16[64,2048]{1,0:T(8,128)(2,1)S(1)}, bf16[64,2048]{1,0:T(8,128)(2,1)S(1)}, u32[]{:S(2)}, u32[]{:S(2)}) collective-permute-start(bf16[64,2048]{1,0:T(8,128)(2,1)S(1)} %collective-permute-done.1.refs_1_), channel_id=1, source_target_pairs={{4,0},{8,4},{12,8},{14,12},{10,14},{6,10},{2,6},{0,2},{5,1},{9,5},... | collective-permute-start | bytes 786440 | tf_op jit(solution)/shard_map/ppermute | solution.py:393
  26.8 15.0 %collective-permute-start.11 = (bf16[64,2048]{1,0:T(8,128)(2,1)S(1)}, bf16[64,2048]{1,0:T(8,128)(2,1)S(1)}, u32[]{:S(2)}, u32[]{:S(2)}) collective-permute-start(bf16[64,2048]{1,0:T(8,128)(2,1)S(1)} %collective-permute-done.7.refs_2_), channel_id=1, source_target_pairs={{0,4},{4,8},{8,12},{12,14},{14,10},{10,6},{6,2},{2,0},{1,5},{5,9},... | collective-permute-start | bytes 786440 | tf_op jit(solution)/shard_map/ppermute | solution.py:392
  29.0 12.8 %collective-permute-start.12 = (bf16[64,2048]{1,0:T(8,128)(2,1)S(1)}, bf16[64,2048]{1,0:T(8,128)(2,1)S(1)}, u32[]{:S(2)}, u32[]{:S(2)}) collective-permute-start(bf16[64,2048]{1,0:T(8,128)(2,1)S(1)} %collective-permute-done.8.refs_3_), channel_id=1, source_target_pairs={{4,0},{8,4},{12,8},{14,12},{10,14},{6,10},{2,6},{0,2},{5,1},{9,5},... | collective-permute-start | bytes 786440 | tf_op jit(solution)/shard_map/ppermute | solution.py:393
  39.7 11.5 %collective-permute-start.9 = (bf16[64,2048]{1,0:T(8,128)(2,1)S(1)}, bf16[64,2048]{1,0:T(8,128)(2,1)S(1)}, u32[]{:S(2)}, u32[]{:S(2)}) collective-permute-start(bf16[64,2048]{1,0:T(8,128)(2,1)S(1)} %collective-permute-done.5.refs_0_), channel_id=1, source_target_pairs={{0,4},{4,8},{8,12},{12,14},{14,10},{10,6},{6,2},{2,0},{1,5},{5,9},... | collective-permute-start | bytes 786440 | tf_op jit(solution)/shard_map/ppermute | solution.py:392
  40.5 10.7 %collective-permute-start.10 = (bf16[64,2048]{1,0:T(8,128)(2,1)S(1)}, bf16[64,2048]{1,0:T(8,128)(2,1)S(1)}, u32[]{:S(2)}, u32[]{:S(2)}) collective-permute-start(bf16[64,2048]{1,0:T(8,128)(2,1)S(1)} %collective-permute-done.6.refs_1_), channel_id=1, source_target_pairs={{4,0},{8,4},{12,8},{14,12},{10,14},{6,10},{2,6},{0,2},{5,1},{9,5},... | collective-permute-start | bytes 786440 | tf_op jit(solution)/shard_map/ppermute | solution.py:393
  41.8 20.2 %collective-permute-start.19 = (bf16[32,2048]{1,0:T(8,128)(2,1)S(1)}, bf16[32,2048]{1,0:T(8,128)(2,1)S(1)}, u32[]{:S(2)}, u32[]{:S(2)}) collective-permute-start(bf16[32,2048]{1,0:T(8,128)(2,1)S(1)} %get-tuple-element.74), channel_id=1, source_target_pairs={{0,4},{4,8},{8,12},{12,14},{14,10},{10,6},{6,2},{2,0},{1,5},{5,9},... | collective-permute-start | bytes 393224 | tf_op jit(solution)/shard_map/ppermute | solution.py:404
  42.6 20.1 %collective-permute-start.20 = (bf16[32,2048]{1,0:T(8,128)(2,1)S(1)}, bf16[32,2048]{1,0:T(8,128)(2,1)S(1)}, u32[]{:S(2)}, u32[]{:S(2)}) collective-permute-start(bf16[32,2048]{1,0:T(8,128)(2,1)S(1)} %get-tuple-element.75), channel_id=1, source_target_pairs={{4,0},{8,4},{12,8},{14,12},{10,14},{6,10},{2,6},{0,2},{5,1},{9,5},... | collective-permute-start | bytes 393224 | tf_op jit(solution)/shard_map/ppermute | solution.py:405
  51.2 11.5 %collective-permute-start.17 = (bf16[32,2048]{1,0:T(8,128)(2,1)S(1)}, bf16[32,2048]{1,0:T(8,128)(2,1)S(1)}, u32[]{:S(2)}, u32[]{:S(2)}) collective-permute-start(bf16[32,2048]{1,0:T(8,128)(2,1)S(1)} %get-tuple-element.72), channel_id=1, source_target_pairs={{0,4},{4,8},{8,12},{12,14},{14,10},{10,6},{6,2},{2,0},{1,5},{5,9},... | collective-permute-start | bytes 393224 | tf_op jit(solution)/shard_map/ppermute | solution.py:404
  52.0 10.8 %collective-permute-start.18 = (bf16[32,2048]{1,0:T(8,128)(2,1)S(1)}, bf16[32,2048]{1,0:T(8,128)(2,1)S(1)}, u32[]{:S(2)}, u32[]{:S(2)}) collective-permute-start(bf16[32,2048]{1,0:T(8,128)(2,1)S(1)} %get-tuple-element.73), channel_id=1, source_target_pairs={{4,0},{8,4},{12,8},{14,12},{10,14},{6,10},{2,6},{0,2},{5,1},{9,5},... | collective-permute-start | bytes 393224 | tf_op jit(solution)/shard_map/ppermute | solution.py:405
  60.6 11.5 %collective-permute-start.13 = (bf16[64,2048]{1,0:T(8,128)(2,1)S(1)}, bf16[64,2048]{1,0:T(8,128)(2,1)S(1)}, u32[]{:S(2)}, u32[]{:S(2)}) collective-permute-start(bf16[64,2048]{1,0:T(8,128)(2,1)S(1)} %get-tuple-element.66), channel_id=1, source_target_pairs={{4,0},{8,4},{12,8},{14,12},{10,14},{6,10},{2,6},{0,2},{5,1},{9,5},... | collective-permute-start | bytes 786440 | tf_op jit(solution)/shard_map/ppermute | solution.py:372
  62.0 10.2 %collective-permute-start.14 = (bf16[64,2048]{1,0:T(8,128)(2,1)S(1)}, bf16[64,2048]{1,0:T(8,128)(2,1)S(1)}, u32[]{:S(2)}, u32[]{:S(2)}) collective-permute-start(bf16[64,2048]{1,0:T(8,128)(2,1)S(1)} %get-tuple-element.67), channel_id=1, source_target_pairs={{0,4},{4,8},{8,12},{12,14},{14,10},{10,6},{6,2},{2,0},{1,5},{5,9},... | collective-permute-start | bytes 786440 | tf_op jit(solution)/shard_map/ppermute | solution.py:372
  70.2 10.7 %collective-permute-start.21 = (bf16[64,2048]{1,0:T(8,128)(2,1)S(1)}, bf16[64,2048]{1,0:T(8,128)(2,1)S(1)}, u32[]{:S(2)}, u32[]{:S(2)}) collective-permute-start(bf16[64,2048]{1,0:T(8,128)(2,1)S(1)} %get-tuple-element.78), channel_id=1, source_target_pairs={{0,12},{4,6},{8,10},{12,0},{14,2},{10,8},{6,4},{2,14},{1,13},{5,7}... | collective-permute-start | bytes 786440 | tf_op jit(solution)/shard_map/ppermute | solution.py:421
  72.2 8.7 %collective-permute-start.15 = (bf16[64,1024]{1,0:T(8,128)(2,1)S(1)}, bf16[64,1024]{1,0:T(8,128)(2,1)S(1)}, u32[]{:S(2)}, u32[]{:S(2)}) collective-permute-start(bf16[64,1024]{1,0:T(8,128)(2,1)S(1)} %get-tuple-element.68), channel_id=1, source_target_pairs={{4,0},{8,4},{12,8},{14,12},{10,14},{6,10},{2,6},{0,2},{5,1},{9,5},... | collective-permute-start | bytes 393224 | tf_op jit(solution)/shard_map/ppermute | solution.py:372
  73.7 7.1 %collective-permute-start.16 = (bf16[64,1024]{1,0:T(8,128)(2,1)S(1)}, bf16[64,1024]{1,0:T(8,128)(2,1)S(1)}, u32[]{:S(2)}, u32[]{:S(2)}) collective-permute-start(bf16[64,1024]{1,0:T(8,128)(2,1)S(1)} %get-tuple-element.69), channel_id=1, source_target_pairs={{0,4},{4,8},{8,12},{12,14},{14,10},{10,6},{6,2},{2,0},{1,5},{5,9},... | collective-permute-start | bytes 393224 | tf_op jit(solution)/shard_map/ppermute | solution.py:372
  74.3 8.7 %collective-permute-start.24 = (bf16[64,1024]{1,0:T(8,128)(2,1)S(1)}, bf16[64,1024]{1,0:T(8,128)(2,1)S(1)}, u32[]{:S(2)}, u32[]{:S(2)}) collective-permute-start(bf16[64,1024]{1,0:T(8,128)(2,1)S(1)} %get-tuple-element.81), channel_id=1, source_target_pairs={{4,0},{8,4},{12,8},{14,12},{10,14},{6,10},{2,6},{0,2},{5,1},{9,5},... | collective-permute-start | bytes 393224 | tf_op jit(solution)/shard_map/ppermute | solution.py:372
  75.9 7.2 %collective-permute-start.25 = (bf16[64,1024]{1,0:T(8,128)(2,1)S(1)}, bf16[64,1024]{1,0:T(8,128)(2,1)S(1)}, u32[]{:S(2)}, u32[]{:S(2)}) collective-permute-start(bf16[64,1024]{1,0:T(8,128)(2,1)S(1)} %get-tuple-element.82), channel_id=1, source_target_pairs={{0,4},{4,8},{8,12},{12,14},{14,10},{10,6},{6,2},{2,0},{1,5},{5,9},... | collective-permute-start | bytes 393224 | tf_op jit(solution)/shard_map/ppermute | solution.py:372
  80.9 4.4 %collective-permute-start.28 = (f32[32,1216]{1,0:T(8,128)S(1)}, f32[32,1216]{1,0:T(8,128)S(1)}, u32[]{:S(2)}, u32[]{:S(2)}) collective-permute-start(f32[32,1216]{1,0:T(8,128)S(1)} %get-tuple-element.88), channel_id=1, source_target_pairs={{0,1},{1,0},{2,3},{3,2},{4,5},{5,4},{6,7},{7,6},{8,9},{9,8},{10,11... | collective-permute-start | bytes 466952 | tf_op jit(solution)/shard_map/ppermute | solution.py:452
  81.0 6.3 %collective-permute-start.22 = (bf16[64,1024]{1,0:T(8,128)(2,1)S(1)}, bf16[64,1024]{1,0:T(8,128)(2,1)S(1)}, u32[]{:S(2)}, u32[]{:S(2)}) collective-permute-start(bf16[64,1024]{1,0:T(8,128)(2,1)S(1)} %get-tuple-element.79), channel_id=1, source_target_pairs={{4,0},{8,4},{12,8},{14,12},{10,14},{6,10},{2,6},{0,2},{5,1},{9,5},... | collective-permute-start | bytes 393224 | tf_op jit(solution)/shard_map/ppermute | solution.py:372
  81.9 6.3 %collective-permute-start.23 = (bf16[64,1024]{1,0:T(8,128)(2,1)S(1)}, bf16[64,1024]{1,0:T(8,128)(2,1)S(1)}, u32[]{:S(2)}, u32[]{:S(2)}) collective-permute-start(bf16[64,1024]{1,0:T(8,128)(2,1)S(1)} %get-tuple-element.80), channel_id=1, source_target_pairs={{0,4},{4,8},{8,12},{12,14},{14,10},{10,6},{6,2},{2,0},{1,5},{5,9},... | collective-permute-start | bytes 393224 | tf_op jit(solution)/shard_map/ppermute | solution.py:372
  83.2 6.6 %collective-permute-start.26 = (bf16[64,1024]{1,0:T(8,128)(2,1)S(1)}, bf16[64,1024]{1,0:T(8,128)(2,1)S(1)}, u32[]{:S(2)}, u32[]{:S(2)}) collective-permute-start(bf16[64,1024]{1,0:T(8,128)(2,1)S(1)} %get-tuple-element.83), channel_id=1, source_target_pairs={{4,0},{8,4},{12,8},{14,12},{10,14},{6,10},{2,6},{0,2},{5,1},{9,5},... | collective-permute-start | bytes 393224 | tf_op jit(solution)/shard_map/ppermute | solution.py:372
  84.1 5.7 %collective-permute-start.27 = (bf16[64,1024]{1,0:T(8,128)(2,1)S(1)}, bf16[64,1024]{1,0:T(8,128)(2,1)S(1)}, u32[]{:S(2)}, u32[]{:S(2)}) collective-permute-start(bf16[64,1024]{1,0:T(8,128)(2,1)S(1)} %get-tuple-element.84), channel_id=1, source_target_pairs={{0,4},{4,8},{8,12},{12,14},{14,10},{10,6},{6,2},{2,0},{1,5},{5,9},... | collective-permute-start | bytes 393224 | tf_op jit(solution)/shard_map/ppermute | solution.py:372

commit v11 on v9

--- a/solution.py
+++ b/solution.py
@@ -115,24 +115,66 @@
             out[...] = total[...] + adapter_scale * value
 
 
-def whole_kernel(plan, pieces, blocks, keep_rows, *refs):
+def whole_kernel(plan, pieces, *refs):
     token_refs, grad_refs, refs = refs[:pieces], refs[pieces : 2 * pieces], refs[2 * pieces :]
     factor_in_ref, factor_out_ref, refs = refs[0], refs[1], refs[2:]
     weight_refs, refs = refs[: plan.parts], refs[plan.parts :]
     total_refs, refs = refs[:2], refs[2:]
-    if keep_rows:
-        rows_ref, refs = refs[0], refs[1:]
-    else:
-        *refs, rows_ref = refs
-    out_refs, send_refs = refs[:2], refs[2:]
+    rows_ref, out_refs = refs[0], refs[1:]
     activation, slope, hidden, low_rank = plan.forward(token_refs, factor_in_ref, weight_refs)
     rank_scale, back_scaled = plan.backward(
         grad_refs, activation, slope, factor_in_ref, factor_out_ref, weight_refs, rows_ref
     )
-    for (first_row, span), send_ref in zip(blocks, send_refs):
-        send_ref[...] = rows_ref[first_row : first_row + send_ref.shape[0], span].astype(bf16)
     low_scaled = (rank_scale * low_rank).astype(bf16)
     plan.adapters(grad_refs, hidden, low_scaled, back_scaled, total_refs, out_refs)
+
+
+def forward_kernel(plan, pieces, *refs):
+    token_refs, factor_in_ref, refs = refs[:pieces], refs[pieces], refs[pieces + 1 :]
+    weight_refs, out_refs = refs[: plan.parts], refs[plan.parts :]
+    for out, value in zip(out_refs, plan.forward(token_refs, factor_in_ref, weight_refs)):
+        out[...] = value
+
+
+def finish(plan, grad_refs, forward, factor_in_ref, factor_out_ref, weight_refs, refs):
+    low_scaled_ref, back_scaled_ref, *send_refs, rows_ref = refs
+    activation, slope, low_rank = forward
+    rank_scale, back_scaled = plan.backward(
+        grad_refs, activation, slope, factor_in_ref, factor_out_ref, weight_refs, rows_ref
+    )
+    for at, send_ref in enumerate(send_refs):
+        count = send_ref.shape[0]
+        send_ref[...] = rows_ref[at * count : (at + 1) * count, :].astype(bf16)
+    low_scaled_ref[...] = (rank_scale * low_rank).astype(bf16)
+    back_scaled_ref[...] = back_scaled
+
+
+def backward_kernel(plan, pieces, *refs):
+    grad_refs, refs = refs[:pieces], refs[pieces:]
+    activation_ref, slope_ref, low_rank_ref, factor_in_ref, factor_out_ref = refs[:5]
+    weight_refs, refs = refs[5 : 5 + plan.parts], refs[5 + plan.parts :]
+    forward = (activation_ref[...], slope_ref[...], low_rank_ref[...])
+    finish(plan, grad_refs, forward, factor_in_ref, factor_out_ref, weight_refs, refs)
+
+
+def rows_kernel(plan, pieces, *refs):
+    token_refs, grad_refs, refs = refs[:pieces], refs[pieces : 2 * pieces], refs[2 * pieces :]
+    factor_in_ref, factor_out_ref, refs = refs[0], refs[1], refs[2:]
+    weight_refs, hidden_ref, refs = refs[: plan.parts], refs[plan.parts], refs[plan.parts + 1 :]
+    activation, slope, hidden, low_rank = plan.forward(token_refs, factor_in_ref, weight_refs)
+    hidden_ref[...] = hidden
+    forward = (activation, slope, low_rank)
+    finish(plan, grad_refs, forward, factor_in_ref, factor_out_ref, weight_refs, refs)
+
+
+def adapters_kernel(plan, pieces, groups, *refs):
+    grad_refs, refs = refs[:pieces], refs[pieces:]
+    hidden, low_scaled, back_scaled = [
+        jnp.concatenate([ref[...] for ref in refs[at * groups : (at + 1) * groups]], axis=0)
+        for at in range(3)
+    ]
+    refs = refs[3 * groups :]
+    plan.adapters(grad_refs, hidden, low_scaled, back_scaled, refs[:2], refs[2:])
 
 
 def prepare_kernel(plan, *refs):
@@ -248,9 +290,15 @@
         out_ref[:, span] = total.astype(bf16)
 
 
-def simple_call(kernel, operands, outs):
+def simple_call(kernel, operands, outs, scratch=(), flops=0):
     return pl.pallas_call(
         kernel,
+        scratch_shapes=list(scratch),
+        cost_estimate=pl.CostEstimate(
+            flops=flops,
+            bytes_accessed=sum(op.size * op.dtype.itemsize for op in operands),
+            transcendentals=0,
+        ),
         out_shape=tuple(jax.ShapeDtypeStruct(shape, dtype) for shape, dtype in outs),
         in_specs=[pl.BlockSpec(memory_space=pltpu.VMEM)] * len(operands),
         out_specs=(pl.BlockSpec(memory_space=pltpu.VMEM),) * len(outs),
@@ -258,26 +306,14 @@
     )(*operands)
 
 
-def expert_call(plan, pieces, blocks, block_rows, operands, totals, keep_rows):
+def expert_call(plan, pieces, operands, totals):
     rows = sum(piece[0].shape[0] for piece in pieces)
-    operands = [p[0] for p in pieces] + [p[1] for p in pieces] + [*operands, *totals]
-    shape = (rows, plan.model_width)
-    outs = [(shape, f32)] * keep_rows + [(total.shape, f32) for total in totals]
-    widths = [len(range(*span.indices(plan.model_width))) for _, span in blocks]
-    outs += [((block_rows, width), bf16) for width in widths]
-    return pl.pallas_call(
-        functools.partial(whole_kernel, plan, len(pieces), blocks, keep_rows),
-        scratch_shapes=[] if keep_rows else [pltpu.VMEM(shape, f32)],
-        out_shape=tuple(jax.ShapeDtypeStruct(shape, dtype) for shape, dtype in outs),
-        in_specs=[pl.BlockSpec(memory_space=pltpu.VMEM)] * len(operands),
-        out_specs=(pl.BlockSpec(memory_space=pltpu.VMEM),) * len(outs),
-        compiler_params=pltpu.CompilerParams(vmem_limit_bytes=16 * 1024 * 1024),
-        cost_estimate=pl.CostEstimate(
-            flops=10 * rows * plan.model_width * plan.wide,
-            bytes_accessed=sum(op.size * op.dtype.itemsize for op in operands),
-            transcendentals=0,
-        ),
-    )(*operands)
+    return simple_call(
+        functools.partial(whole_kernel, plan, len(pieces)),
+        [p[0] for p in pieces] + [p[1] for p in pieces] + [*operands, *totals],
+        [((rows, plan.model_width), f32)] + [(total.shape, f32) for total in totals],
+        flops=10 * rows * plan.model_width * plan.wide,
+    )
 
 
 def per_device(
@@ -360,9 +396,21 @@
     def send(value, way):
         return lax.ppermute(value, "expert", ways[way][1])
 
-    def run(pieces, blocks, totals, keep_rows=True):
-        operands = [factor_in, factor_out, *weights]
-        return expert_call(plan, pieces, blocks, token_count, operands, totals, keep_rows)
+    flops = 2 * token_count * model_width * wide
+
+    def forward_part(pieces, count):
+        rows = count * token_count
+        return simple_call(
+            functools.partial(forward_kernel, plan, len(pieces)),
+            [piece[0] for piece in pieces] + [factor_in, *weights],
+            [((rows, wide), f32)] * 2 + [((rows, wide), bf16), ((rows, ranks), f32)],
+            flops=2 * count * flops,
+        )
+
+    def finished(count):
+        rows = count * token_count
+        outs = [((rows, ranks), bf16)] * 2 + [((token_count, model_width), bf16)] * count
+        return outs, [pltpu.VMEM((rows, model_width), f32)]
 
     def after(value, *arrays):
         held = []
@@ -373,39 +421,67 @@
 
     for d in range(full):
         if d > 1:
-            totals, (tokens_b, tokens_a) = after(totals, behind[d][0], ahead[d][0])
-            grads_b, grads_a = behind[d][1], ahead[d][1]
-            behind[d], ahead[d] = (tokens_b, grads_b), (tokens_a, grads_a)
+            totals, (grads_b, grads_a) = after(totals, behind[d][1], ahead[d][1])
+            behind[d], ahead[d] = (behind[d][0], grads_b), (ahead[d][0], grads_a)
         behind.append(tuple(lax.ppermute(x, "expert", forward) for x in behind[d]))
         ahead.append(tuple(lax.ppermute(x, "expert", backward) for x in ahead[d]))
         if d > 0:
             pieces = [behind[d], ahead[d]] + ([behind[0]] if d == 1 else [])
-            rows_d, *totals = run(pieces, [], totals)
+            rows_d, *totals = expert_call(
+                plan, pieces, [factor_in, factor_out, *weights], totals
+            )
             rows_at.append(rows_d)
+    pieces = [behind[full], ahead[full]]
+    activation, slope, hidden, low_rank = forward_part(pieces, 2)
     if split:
         half = token_count // 2
         totals, (tokens_b, tokens_a) = after(totals, behind[full][0], ahead[full][0])
+        _, (grads_b, grads_a) = after(low_rank, behind[full][1], ahead[full][1])
         tokens_b, tokens_a = halves(tokens_b, tokens_a, half)
-        grads_b, grads_a = halves(behind[full][1], ahead[full][1], half)
+        grads_b, grads_a = halves(grads_b, grads_a, half)
         far = [
             tuple(lax.ppermute(x, "expert", forward) for x in (tokens_b, grads_b)),
             tuple(lax.ppermute(x, "expert", backward) for x in (tokens_a, grads_a)),
         ]
-    pieces = [behind[full], ahead[full]]
-    blocks = [(first_row, everything) for first_row, _ in ways.values()]
-    outs = run(pieces, blocks, totals, keep_rows=False)
-    totals = outs[:2]
-    for way, value in zip(ways, outs[2:]):
+    outs, scratch = finished(2)
+    low_scaled, back_scaled, *values = simple_call(
+        functools.partial(backward_kernel, plan, 2),
+        [piece[1] for piece in pieces]
+        + [activation, slope, low_rank, factor_in, factor_out, *weights],
+        outs,
+        scratch,
+        6 * flops,
+    )
+    for way, value in zip(ways, values):
         for side in columns:
             moving[side, way] = send(value, way) if side == "left" else moving["left", way]
+    late = [(hidden, low_scaled, back_scaled)]
+    late_grads = [piece[1] for piece in pieces]
     skipped = []
     if split:
-        *totals, value = run(far, [(0, everything)], totals, keep_rows=False)
+        outs, scratch = finished(1)
+        hidden, low_scaled, back_scaled, value = simple_call(
+            functools.partial(rows_kernel, plan, 2),
+            [piece[0] for piece in far]
+            + [piece[1] for piece in far]
+            + [factor_in, factor_out, *weights],
+            [((token_count, wide), bf16), *outs],
+            scratch,
+            5 * flops,
+        )
+        late.append((hidden, low_scaled, back_scaled))
+        late_grads += [piece[1] for piece in far]
         pairs = [
             (order[i], order[(i + (full if i % 2 == 0 else -full)) % peer_count])
             for i in range(peer_count)
         ]
         skipped.append(lax.ppermute(value, "expert", pairs))
+    totals = simple_call(
+        functools.partial(adapters_kernel, plan, len(late_grads), len(late)),
+        late_grads + [x for kind in zip(*late) for x in kind] + [*totals],
+        [(total.shape, f32) for total in totals],
+        flops=flops // 4,
+    )
 
     def goes_ahead():
         me = lax.axis_index("expert")

time: 79.3 us -> 79.5 us (level)
  waiting for transfers between devices: 27 us -> 24.5 us
  starting transfers between devices: 31.5 us -> 33.4 us
  Pallas kernels: 19.8 us -> 20.7 us
    ppermute x8, starting transfers between devices: 16.1 us -> 1.97 us  [per_device(): lax.ppermute(x, 'expert', forward)]
    ppermute x8, waiting for transfers between devices: 16.5 us -> 4.58 us  [per_device(): lax.ppermute(x, 'expert', forward)]
    ppermute x6, starting transfers between devices: 0.02 us -> 11.3 us  [per_device(): ahead.append(tuple((lax.ppermute(x, 'expert', backward) for x in ahead[d])))]
    ppermute x6, waiting for transfers between devices: 2.58 us -> 13.2 us  [per_device(): ahead.append(tuple((lax.ppermute(x, 'expert', backward) for x in ahead[d])))]
    ppermute x2, starting transfers between devices: 0.9 us -> 3.64 us  [per_device(): lax.ppermute(x, 'expert', backward)]
    ppermute x10, starting transfers between devices: 10.4 us -> 12.7 us  [send(): return lax.ppermute(value, 'expert', ways[way][1])]
    ppermute x10, waiting for transfers between devices: 8 us -> 6.63 us  [send(): return lax.ppermute(value, 'expert', ways[way][1])]
    pallas_call x8 -> x10, Pallas kernels: 16.1 us -> 17 us  [simple_call(): pl.pallas_call(kernel, scratch_shapes=list(scratch), cost_estimate=pl.Cos...]
  transfers between devices with their start and end apart: 29 -> 29, of which waited for: 11 -> 12; matrix products, arithmetic and copies ran while one was open for 0% -> 0% of each run, Pallas kernels for 21% -> 22%
where the time goes in v11:
time: 79.5 us; the launch traced here: 79.4 us
  starting transfers between devices  33.4 us (42%)
  waiting for transfers between devices  24.5 us (31%)
  Pallas kernels  20.7 us (26%)
    pallas_call x10, Pallas kernels, simple_call(): pl.pallas_call(kernel, scratch_shapes=list(scratch), cost_estimate=pl.Cos...  17 us
    ppermute x6, waiting for transfers between devices, per_device(): ahead.append(tuple((lax.ppermute(x, 'expert', backward) for x in ahead[d])))  13.2 us
    ppermute x10, starting transfers between devices, send(): return lax.ppermute(value, 'expert', ways[way][1])  12.7 us
    ppermute x6, starting transfers between devices, per_device(): ahead.append(tuple((lax.ppermute(x, 'expert', backward) for x in ahead[d])))  11.3 us
    ppermute x10, waiting for transfers between devices, send(): return lax.ppermute(value, 'expert', ways[way][1])  6.63 us
    ppermute x8, waiting for transfers between devices, per_device(): lax.ppermute(x, 'expert', forward)  4.58 us
    ppermute x2, starting transfers between devices, per_device(): lax.ppermute(x, 'expert', backward)  3.64 us
    ppermute x1, starting transfers between devices, per_device(): skipped.append(lax.ppermute(value, 'expert', pairs))  3.18 us
  transfers between devices with their start and end apart: 29, of which 12 were waited for; matrix products, arithmetic and copies ran while one was open for 0% of the time, Pallas kernels for 22%

profile of v11, /device:TPU:0, one launch (start us, length us, event | category | flops | bytes accessed | tf_op | source)
XLA Modules:
  0.0 79.4 jit_solution(7392282684469244591)
XLA Ops:
  0.6 2.6 %shard_map.112 = (bf16[1024,2304]{1,0:T(8,128)(2,1)S(1)}, bf16[64,2176]{1,0:T(8,128)(2,1)S(1)}, bf16[64,2176]{1,0:T(8,128)(2,1)S(1)}, bf16[32,768]{1,0:T(8,128)(2,1)S(1)}) custom-call(bf16[2,1024,384]{2,1,0:T(8,128)(2,1)} %refs_0_.1, bf16[2,1024,384]{2,1,0:T(8,128)(2,1)} %refs_1_.1, bf16[2,1024,384]{2,1,0:T(8,128)(2,1)} %refs_2_.1, ...), custom_call_target="tpu_custom_call" | custom-call | tf_op jit(solution)/shard_map/pallas_call | solution.py:346
  3.3 0.5 collective-permute-start.4
  3.8 2.6 %collective-permute-start.1 = (bf16[64,2176]{1,0:T(8,128)(2,1)S(1)}, bf16[64,2176]{1,0:T(8,128)(2,1)S(1)}, u32[]{:S(2)}, u32[]{:S(2)}) collective-permute-start(bf16[64,2176]{1,0:T(8,128)(2,1)S(1)} %get-tuple-element.56.refs_2_), channel_id=1, source_target_pairs={{4,0},{8,4},{12,8},{14,12},{10,14},{6,10},{2,6},{0,2},{5,1},{9,5},... | collective-permute-start | bytes 835592 | tf_op jit(solution)/shard_map/ppermute | solution.py:427
  6.4 0.2 collective-permute-start
  6.5 1.9 %collective-permute-start.3 = (bf16[64,2176]{1,0:T(8,128)(2,1)S(1)}, bf16[64,2176]{1,0:T(8,128)(2,1)S(1)}, u32[]{:S(2)}, u32[]{:S(2)}) collective-permute-start(bf16[64,2176]{1,0:T(8,128)(2,1)S(1)} %get-tuple-element.57.refs_5_), channel_id=1, source_target_pairs={{4,0},{8,4},{12,8},{14,12},{10,14},{6,10},{2,6},{0,2},{5,1},{9,5},... | collective-permute-start | bytes 835592 | tf_op jit(solution)/shard_map/ppermute | solution.py:427
  8.4 0.2 collective-permute-start.2
  8.6 5.4 %collective-permute-done.1.refs_1_ = bf16[64,2176]{1,0:T(8,128)(2,1)S(1)} collective-permute-done((bf16[64,2176]{1,0:T(8,128)(2,1)S(1)}, bf16[64,2176]{1,0:T(8,128)(2,1)S(1)}, u32[]{:S(2)}, u32[]{:S(2)}) %collective-permute-start.1) | collective-permute-done | bytes 278560 | tf_op jit(solution)/shard_map/ppermute | solution.py:427
  14.0 1.9 %collective-permute-start.6 = (bf16[64,2176]{1,0:T(8,128)(2,1)S(1)}, bf16[64,2176]{1,0:T(8,128)(2,1)S(1)}, u32[]{:S(2)}, u32[]{:S(2)}) collective-permute-start(bf16[64,2176]{1,0:T(8,128)(2,1)S(1)} %collective-permute-done.1.refs_1_), channel_id=1, source_target_pairs={{4,0},{8,4},{12,8},{14,12},{10,14},{6,10},{2,6},{0,2},{5,1},{9,5},... | collective-permute-start | bytes 835592 | tf_op jit(solution)/shard_map/ppermute | solution.py:427
  15.9 0.1 collective-permute-start.5
  16.0 3.9 %collective-permute-done.3.refs_4_ = bf16[64,2176]{1,0:T(8,128)(2,1)S(1)} collective-permute-done((bf16[64,2176]{1,0:T(8,128)(2,1)S(1)}, bf16[64,2176]{1,0:T(8,128)(2,1)S(1)}, u32[]{:S(2)}, u32[]{:S(2)}) %collective-permute-start.3) | collective-permute-done | bytes 278560 | tf_op jit(solution)/shard_map/ppermute | solution.py:427
  19.9 1.9 %collective-permute-start.8 = (bf16[64,2176]{1,0:T(8,128)(2,1)S(1)}, bf16[64,2176]{1,0:T(8,128)(2,1)S(1)}, u32[]{:S(2)}, u32[]{:S(2)}) collective-permute-start(bf16[64,2176]{1,0:T(8,128)(2,1)S(1)} %collective-permute-done.3.refs_4_), channel_id=1, source_target_pairs={{4,0},{8,4},{12,8},{14,12},{10,14},{6,10},{2,6},{0,2},{5,1},{9,5},... | collective-permute-start | bytes 835592 | tf_op jit(solution)/shard_map/ppermute | solution.py:427
  21.8 0.1 collective-permute-start.7
  22.0 3.9 %collective-permute-done.6.refs_1_ = bf16[64,2176]{1,0:T(8,128)(2,1)S(1)} collective-permute-done((bf16[64,2176]{1,0:T(8,128)(2,1)S(1)}, bf16[64,2176]{1,0:T(8,128)(2,1)S(1)}, u32[]{:S(2)}, u32[]{:S(2)}) %collective-permute-start.6) | collective-permute-done | bytes 278560 | tf_op jit(solution)/shard_map/ppermute | solution.py:427
  25.9 1.9 %collective-permute-start.12 = (bf16[64,2176]{1,0:T(8,128)(2,1)S(1)}, bf16[64,2176]{1,0:T(8,128)(2,1)S(1)}, u32[]{:S(2)}, u32[]{:S(2)}) collective-permute-start(bf16[64,2176]{1,0:T(8,128)(2,1)S(1)} %collective-permute-done.6.refs_1_), channel_id=1, source_target_pairs={{4,0},{8,4},{12,8},{14,12},{10,14},{6,10},{2,6},{0,2},{5,1},{9,5},... | collective-permute-start | bytes 835592 | tf_op jit(solution)/shard_map/ppermute | solution.py:427
  27.8 0.1 collective-permute-start.11
  28.0 4.5 %shard_map.113 = (f32[192,2048]{1,0:T(8,128)S(1)}, f32[32,768]{1,0:T(8,128)S(1)}, f32[32,2048]{1,0:T(8,128)S(1)}) custom-call(bf16[64,2176]{1,0:T(8,128)(2,1)S(1)} %collective-permute-done.refs_0_, bf16[64,2176]{1,0:T(8,128)(2,1)S(1)} %collective-permute-done.1.refs_1_, bf16[64,2176]{1,0:T(8,128)(2,1)S(1)} %get-tuple-element.56.refs_2_, ...), custom_call_target="tpu_custom_call" | custom-call | flops 3019898880 | bytes 11649024 | tf_op jit(solution)/shard_map/pallas_call | solution.py:294
  32.5 1.3 %collective-permute-done.7.refs_2_ = bf16[64,2176]{1,0:T(8,128)(2,1)S(1)} collective-permute-done((bf16[64,2176]{1,0:T(8,128)(2,1)S(1)}, bf16[64,2176]{1,0:T(8,128)(2,1)S(1)}, u32[]{:S(2)}, u32[]{:S(2)}) %collective-permute-start.7) | collective-permute-done | bytes 278560 | tf_op jit(solution)/shard_map/ppermute | solution.py:426
  33.8 0.7 collective-permute-start.9
  34.5 1.3 %collective-permute-start.10 = (bf16[64,2176]{1,0:T(8,128)(2,1)S(1)}, bf16[64,2176]{1,0:T(8,128)(2,1)S(1)}, u32[]{:S(2)}, u32[]{:S(2)}) collective-permute-start(bf16[64,2176]{1,0:T(8,128)(2,1)S(1)} %collective-permute-done.8.refs_3_), channel_id=1, source_target_pairs={{4,0},{8,4},{12,8},{14,12},{10,14},{6,10},{2,6},{0,2},{5,1},{9,5},... | collective-permute-start | bytes 835592 | tf_op jit(solution)/shard_map/ppermute | solution.py:427
  35.8 3.5 %shard_map.114 = (f32[128,2048]{1,0:T(8,128)S(1)}, f32[32,768]{1,0:T(8,128)S(1)}, f32[32,2048]{1,0:T(8,128)S(1)}) custom-call(bf16[64,2176]{1,0:T(8,128)(2,1)S(1)} %collective-permute-done.5.refs_0_, bf16[64,2176]{1,0:T(8,128)(2,1)S(1)} %collective-permute-done.6.refs_1_, bf16[64,2176]{1,0:T(8,128)(2,1)S(1)} %collective-permute-done.7.refs_2_, ...), custom_call_target="tpu_custom_call" | custom-call | flops 2013265920 | bytes 11091968 | tf_op jit(solution)/shard_map/pallas_call | solution.py:294
  39.3 0.4 collective-permute-done.11.refs_0_.first_ref
  39.8 0.3 collective-permute-start.17
  40.1 1.8 %collective-permute-start.18 = (bf16[32,2176]{1,0:T(8,128)(2,1)S(1)}, bf16[32,2176]{1,0:T(8,128)(2,1)S(1)}, u32[]{:S(2)}, u32[]{:S(2)}) collective-permute-start(bf16[32,2176]{1,0:T(8,128)(2,1)S(1)} %get-tuple-element.84), channel_id=1, source_target_pairs={{4,0},{8,4},{12,8},{14,12},{10,14},{6,10},{2,6},{0,2},{5,1},{9,5},... | collective-permute-start | bytes 417800 | tf_op jit(solution)/shard_map/ppermute | solution.py:444
  41.9 1.2 %shard_map.115 = (f32[128,768]{1,0:T(8,128)S(1)}, f32[128,768]{1,0:T(8,128)S(1)}, bf16[128,768]{1,0:T(8,128)(2,1)S(1)}, f32[128,32]{1,0:T(8,128)S(1)}) custom-call(bf16[64,2176]{1,0:T(8,128)(2,1)S(1)} %collective-permute-done.11.refs_0_.first_ref, bf16[64,2176]{1,0:T(8,128)(2,1)S(1)} %collective-permute-done.12.refs_1_.second_ref, ...), custom_call_target="tpu_custom_call" | custom-call | flops 805306368 | bytes 10043392 | tf_op jit(solution)/shard_map/pallas_call | solution.py:294
  43.0 2.7 %collective-permute-done.9.refs_0_.first_ref = bf16[64,2176]{1,0:T(8,128)(2,1)S(1)} collective-permute-done((bf16[64,2176]{1,0:T(8,128)(2,1)S(1)}, bf16[64,2176]{1,0:T(8,128)(2,1)S(1)}, u32[]{:S(2)}, u32[]{:S(2)}) %collective-permute-start.9) | collective-permute-done | bytes 278560 | tf_op jit(solution)/shard_map/ppermute | solution.py:426
  45.7 0.2 collective-permute-start.19
  45.9 1.9 %collective-permute-start.20 = (bf16[32,2176]{1,0:T(8,128)(2,1)S(1)}, bf16[32,2176]{1,0:T(8,128)(2,1)S(1)}, u32[]{:S(2)}, u32[]{:S(2)}) collective-permute-start(bf16[32,2176]{1,0:T(8,128)(2,1)S(1)} %get-tuple-element.87), channel_id=1, source_target_pairs={{4,0},{8,4},{12,8},{14,12},{10,14},{6,10},{2,6},{0,2},{5,1},{9,5},... | collective-permute-start | bytes 417800 | tf_op jit(solution)/shard_map/ppermute | solution.py:444
  47.8 2.9 %shard_map.116 = (bf16[128,32]{1,0:T(8,128)(2,1)S(1)}, bf16[128,32]{1,0:T(8,128)(2,1)S(1)}, bf16[64,2048]{1,0:T(8,128)(2,1)S(1)}, bf16[64,2048]{1,0:T(8,128)(2,1)S(1)}) custom-call(bf16[64,2176]{1,0:T(8,128)(2,1)S(1)} %collective-permute-done.9.refs_0_.first_ref, bf16[64,2176]{1,0:T(8,128)(2,1)S(1)} %collective-permute-done.10.refs_1_.second_ref, ...), custom_call_target="tpu_custom_call" | custom-call | flops 1207959552 | bytes 10977280 | tf_op jit(solution)/shard_map/pallas_call | solution.py:294
  50.7 1.6 %collective-permute-start.13 = (bf16[64,2048]{1,0:T(8,128)(2,1)S(1)}, bf16[64,2048]{1,0:T(8,128)(2,1)S(1)}, u32[]{:S(2)}, u32[]{:S(2)}) collective-permute-start(bf16[64,2048]{1,0:T(8,128)(2,1)S(1)} %get-tuple-element.73), channel_id=1, source_target_pairs={{4,0},{8,4},{12,8},{14,12},{10,14},{6,10},{2,6},{0,2},{5,1},{9,5},... | collective-permute-start | bytes 786440 | tf_op jit(solution)/shard_map/ppermute | solution.py:397
  52.3 0.5 collective-permute-start.14
  52.8 3.7 %shard_map.120 = (bf16[64,768]{1,0:T(8,128)(2,1)S(1)}, bf16[64,32]{1,0:T(8,128)(2,1)S(1)}, bf16[64,32]{1,0:T(8,128)(2,1)S(1)}, bf16[64,2048]{1,0:T(8,128)(2,1)S(1)}) custom-call(bf16[32,2176]{1,0:T(8,128)(2,1)S(1)} %collective-permute-done.17.refs_0_, bf16[32,2176]{1,0:T(8,128)(2,1)S(1)} %collective-permute-done.18.refs_1_, ...), custom_call_target="tpu_custom_call" | custom-call | flops 1006632960 | bytes 10174464 | tf_op jit(solution)/shard_map/pallas_call | solution.py:294
  56.6 3.2 %collective-permute-start.21 = (bf16[64,2048]{1,0:T(8,128)(2,1)S(1)}, bf16[64,2048]{1,0:T(8,128)(2,1)S(1)}, u32[]{:S(2)}, u32[]{:S(2)}) collective-permute-start(bf16[64,2048]{1,0:T(8,128)(2,1)S(1)} %get-tuple-element.88), channel_id=1, source_target_pairs={{0,12},{4,6},{8,10},{12,0},{14,2},{10,8},{6,4},{2,14},{1,13},{5,7}... | collective-permute-start | bytes 786440 | tf_op jit(solution)/shard_map/ppermute | solution.py:478
  59.8 1.5 %collective-permute-start.24 = (bf16[64,1024]{1,0:T(8,128)(2,1)S(1)}, bf16[64,1024]{1,0:T(8,128)(2,1)S(1)}, u32[]{:S(2)}, u32[]{:S(2)}) collective-permute-start(bf16[64,1024]{1,0:T(8,128)(2,1)S(1)} %get-tuple-element.91), channel_id=1, source_target_pairs={{4,0},{8,4},{12,8},{14,12},{10,14},{6,10},{2,6},{0,2},{5,1},{9,5},... | collective-permute-start | bytes 393224 | tf_op jit(solution)/shard_map/ppermute | solution.py:397
  61.4 0.5 collective-permute-start.25
  61.9 4.4 %collective-permute-start.15 = (bf16[64,1024]{1,0:T(8,128)(2,1)S(1)}, bf16[64,1024]{1,0:T(8,128)(2,1)S(1)}, u32[]{:S(2)}, u32[]{:S(2)}) collective-permute-start(bf16[64,1024]{1,0:T(8,128)(2,1)S(1)} %get-tuple-element.75), channel_id=1, source_target_pairs={{4,0},{8,4},{12,8},{14,12},{10,14},{6,10},{2,6},{0,2},{5,1},{9,5},... | collective-permute-start | bytes 393224 | tf_op jit(solution)/shard_map/ppermute | solution.py:397
  66.4 0.4 shard_map.125
  66.7 0.1 shard_map.126
  66.9 1.6 %collective-permute-done.24.refs_1_ = bf16[64,1024]{1,0:T(8,128)(2,1)S(1)} collective-permute-done((bf16[64,1024]{1,0:T(8,128)(2,1)S(1)}, bf16[64,1024]{1,0:T(8,128)(2,1)S(1)}, u32[]{:S(2)}, u32[]{:S(2)}) %collective-permute-start.24) | collective-permute-done | bytes 131104 | tf_op jit(solution)/shard_map/ppermute | solution.py:397
  68.4 0.8 collective-permute-done.25.refs_2_
  69.3 2.1 %collective-permute-start.26 = (bf16[64,1024]{1,0:T(8,128)(2,1)S(1)}, bf16[64,1024]{1,0:T(8,128)(2,1)S(1)}, u32[]{:S(2)}, u32[]{:S(2)}) collective-permute-start(bf16[64,1024]{1,0:T(8,128)(2,1)S(1)} %get-tuple-element.93), channel_id=1, source_target_pairs={{4,0},{8,4},{12,8},{14,12},{10,14},{6,10},{2,6},{0,2},{5,1},{9,5},... | collective-permute-start | bytes 393224 | tf_op jit(solution)/shard_map/ppermute | solution.py:397
  71.4 0.1 shard_map.121
  71.5 2.1 %collective-permute-start.22 = (bf16[64,1024]{1,0:T(8,128)(2,1)S(1)}, bf16[64,1024]{1,0:T(8,128)(2,1)S(1)}, u32[]{:S(2)}, u32[]{:S(2)}) collective-permute-start(bf16[64,1024]{1,0:T(8,128)(2,1)S(1)} %get-tuple-element.89), channel_id=1, source_target_pairs={{4,0},{8,4},{12,8},{14,12},{10,14},{6,10},{2,6},{0,2},{5,1},{9,5},... | collective-permute-start | bytes 393224 | tf_op jit(solution)/shard_map/ppermute | solution.py:397
  73.6 0.7 shard_map.127
  74.3 1.4 %collective-permute-done.26.refs_3_ = bf16[64,1024]{1,0:T(8,128)(2,1)S(1)} collective-permute-done((bf16[64,1024]{1,0:T(8,128)(2,1)S(1)}, bf16[64,1024]{1,0:T(8,128)(2,1)S(1)}, u32[]{:S(2)}, u32[]{:S(2)}) %collective-permute-start.26) | collective-permute-done | bytes 131104 | tf_op jit(solution)/shard_map/ppermute | solution.py:397
  75.7 1.3 %collective-permute-done.27.refs_4_ = bf16[64,1024]{1,0:T(8,128)(2,1)S(1)} collective-permute-done((bf16[64,1024]{1,0:T(8,128)(2,1)S(1)}, bf16[64,1024]{1,0:T(8,128)(2,1)S(1)}, u32[]{:S(2)}, u32[]{:S(2)}) %collective-permute-start.27) | collective-permute-done | bytes 131104 | tf_op jit(solution)/shard_map/ppermute | solution.py:397
  77.0 0.4 collective-permute-done.22.refs_1_
  77.3 1.2 %collective-permute-done.23.refs_2_ = bf16[64,1024]{1,0:T(8,128)(2,1)S(1)} collective-permute-done((bf16[64,1024]{1,0:T(8,128)(2,1)S(1)}, bf16[64,1024]{1,0:T(8,128)(2,1)S(1)}, u32[]{:S(2)}, u32[]{:S(2)}) %collective-permute-start.23) | collective-permute-done | bytes 131104 | tf_op jit(solution)/shard_map/ppermute | solution.py:397
  78.6 0.8 shard_map.124
  (30 shorter events, 0.4 us)
Async XLA Ops:
  0.6 27.4 %copy-start = (bf16[2,16,2048]{2,1,0:T(8,128)(2,1)S(1)}, bf16[2,16,2048]{2,1,0:T(8,128)(2,1)}, u32[]{:S(2)}) copy-start(bf16[2,16,2048]{2,1,0:T(8,128)(2,1)} %param.17) | copy-start | bytes 393220
  3.3 24.7 %collective-permute-start.4 = (bf16[1024,2304]{1,0:T(8,128)(2,1)S(1)}, bf16[1024,2304]{1,0:T(8,128)(2,1)S(1)}, u32[]{:S(2)}, u32[]{:S(2)}) collective-permute-start(bf16[1024,2304]{1,0:T(8,128)(2,1)S(1)} %get-tuple-element.59.refs_8_.refs_6_.refs_3_.refs_7_), channel_id=1, source_target_pairs={{0,1},{1,0},{2,3},{3,2},{4,5},{5,4},{6,7},{7,6},{8,9},{9,8},{10,11... | collective-permute-start | bytes 14155784 | tf_op jit(solution)/shard_map/ppermute | solution.py:378
  3.8 10.1 %collective-permute-start.1 = (bf16[64,2176]{1,0:T(8,128)(2,1)S(1)}, bf16[64,2176]{1,0:T(8,128)(2,1)S(1)}, u32[]{:S(2)}, u32[]{:S(2)}) collective-permute-start(bf16[64,2176]{1,0:T(8,128)(2,1)S(1)} %get-tuple-element.56.refs_2_), channel_id=1, source_target_pairs={{4,0},{8,4},{12,8},{14,12},{10,14},{6,10},{2,6},{0,2},{5,1},{9,5},... | collective-permute-start | bytes 835592 | tf_op jit(solution)/shard_map/ppermute | solution.py:427
  6.4 9.5 %collective-permute-start = (bf16[64,2176]{1,0:T(8,128)(2,1)S(1)}, bf16[64,2176]{1,0:T(8,128)(2,1)S(1)}, u32[]{:S(2)}, u32[]{:S(2)}) collective-permute-start(bf16[64,2176]{1,0:T(8,128)(2,1)S(1)} %get-tuple-element.56.refs_2_), channel_id=1, source_target_pairs={{0,4},{4,8},{8,12},{12,14},{14,10},{10,6},{6,2},{2,0},{1,5},{5,9},... | collective-permute-start | bytes 835592 | tf_op jit(solution)/shard_map/ppermute | solution.py:426
  6.5 13.4 %collective-permute-start.3 = (bf16[64,2176]{1,0:T(8,128)(2,1)S(1)}, bf16[64,2176]{1,0:T(8,128)(2,1)S(1)}, u32[]{:S(2)}, u32[]{:S(2)}) collective-permute-start(bf16[64,2176]{1,0:T(8,128)(2,1)S(1)} %get-tuple-element.57.refs_5_), channel_id=1, source_target_pairs={{4,0},{8,4},{12,8},{14,12},{10,14},{6,10},{2,6},{0,2},{5,1},{9,5},... | collective-permute-start | bytes 835592 | tf_op jit(solution)/shard_map/ppermute | solution.py:427
  8.4 13.4 %collective-permute-start.2 = (bf16[64,2176]{1,0:T(8,128)(2,1)S(1)}, bf16[64,2176]{1,0:T(8,128)(2,1)S(1)}, u32[]{:S(2)}, u32[]{:S(2)}) collective-permute-start(bf16[64,2176]{1,0:T(8,128)(2,1)S(1)} %get-tuple-element.57.refs_5_), channel_id=1, source_target_pairs={{0,4},{4,8},{8,12},{12,14},{14,10},{10,6},{6,2},{2,0},{1,5},{5,9},... | collective-permute-start | bytes 835592 | tf_op jit(solution)/shard_map/ppermute | solution.py:426
  14.0 11.9 %collective-permute-start.6 = (bf16[64,2176]{1,0:T(8,128)(2,1)S(1)}, bf16[64,2176]{1,0:T(8,128)(2,1)S(1)}, u32[]{:S(2)}, u32[]{:S(2)}) collective-permute-start(bf16[64,2176]{1,0:T(8,128)(2,1)S(1)} %collective-permute-done.1.refs_1_), channel_id=1, source_target_pairs={{4,0},{8,4},{12,8},{14,12},{10,14},{6,10},{2,6},{0,2},{5,1},{9,5},... | collective-permute-start | bytes 835592 | tf_op jit(solution)/shard_map/ppermute | solution.py:427
  15.9 11.9 %collective-permute-start.5 = (bf16[64,2176]{1,0:T(8,128)(2,1)S(1)}, bf16[64,2176]{1,0:T(8,128)(2,1)S(1)}, u32[]{:S(2)}, u32[]{:S(2)}) collective-permute-start(bf16[64,2176]{1,0:T(8,128)(2,1)S(1)} %collective-permute-done.refs_0_), channel_id=1, source_target_pairs={{0,4},{4,8},{8,12},{12,14},{14,10},{10,6},{6,2},{2,0},{1,5},{5,9},... | collective-permute-start | bytes 835592 | tf_op jit(solution)/shard_map/ppermute | solution.py:426
  19.9 14.5 %collective-permute-start.8 = (bf16[64,2176]{1,0:T(8,128)(2,1)S(1)}, bf16[64,2176]{1,0:T(8,128)(2,1)S(1)}, u32[]{:S(2)}, u32[]{:S(2)}) collective-permute-start(bf16[64,2176]{1,0:T(8,128)(2,1)S(1)} %collective-permute-done.3.refs_4_), channel_id=1, source_target_pairs={{4,0},{8,4},{12,8},{14,12},{10,14},{6,10},{2,6},{0,2},{5,1},{9,5},... | collective-permute-start | bytes 835592 | tf_op jit(solution)/shard_map/ppermute | solution.py:427
  21.8 11.9 %collective-permute-start.7 = (bf16[64,2176]{1,0:T(8,128)(2,1)S(1)}, bf16[64,2176]{1,0:T(8,128)(2,1)S(1)}, u32[]{:S(2)}, u32[]{:S(2)}) collective-permute-start(bf16[64,2176]{1,0:T(8,128)(2,1)S(1)} %collective-permute-done.2.refs_3_), channel_id=1, source_target_pairs={{0,4},{4,8},{8,12},{12,14},{14,10},{10,6},{6,2},{2,0},{1,5},{5,9},... | collective-permute-start | bytes 835592 | tf_op jit(solution)/shard_map/ppermute | solution.py:426
  25.9 13.8 %collective-permute-start.12 = (bf16[64,2176]{1,0:T(8,128)(2,1)S(1)}, bf16[64,2176]{1,0:T(8,128)(2,1)S(1)}, u32[]{:S(2)}, u32[]{:S(2)}) collective-permute-start(bf16[64,2176]{1,0:T(8,128)(2,1)S(1)} %collective-permute-done.6.refs_1_), channel_id=1, source_target_pairs={{4,0},{8,4},{12,8},{14,12},{10,14},{6,10},{2,6},{0,2},{5,1},{9,5},... | collective-permute-start | bytes 835592 | tf_op jit(solution)/shard_map/ppermute | solution.py:427
  27.8 11.9 %collective-permute-start.11 = (bf16[64,2176]{1,0:T(8,128)(2,1)S(1)}, bf16[64,2176]{1,0:T(8,128)(2,1)S(1)}, u32[]{:S(2)}, u32[]{:S(2)}) collective-permute-start(bf16[64,2176]{1,0:T(8,128)(2,1)S(1)} %collective-permute-done.5.refs_0_), channel_id=1, source_target_pairs={{0,4},{4,8},{8,12},{12,14},{14,10},{10,6},{6,2},{2,0},{1,5},{5,9},... | collective-permute-start | bytes 835592 | tf_op jit(solution)/shard_map/ppermute | solution.py:426
  33.8 11.9 %collective-permute-start.9 = (bf16[64,2176]{1,0:T(8,128)(2,1)S(1)}, bf16[64,2176]{1,0:T(8,128)(2,1)S(1)}, u32[]{:S(2)}, u32[]{:S(2)}) collective-permute-start(bf16[64,2176]{1,0:T(8,128)(2,1)S(1)} %collective-permute-done.7.refs_2_), channel_id=1, source_target_pairs={{0,4},{4,8},{8,12},{12,14},{14,10},{10,6},{6,2},{2,0},{1,5},{5,9},... | collective-permute-start | bytes 835592 | tf_op jit(solution)/shard_map/ppermute | solution.py:426
  34.5 11.2 %collective-permute-start.10 = (bf16[64,2176]{1,0:T(8,128)(2,1)S(1)}, bf16[64,2176]{1,0:T(8,128)(2,1)S(1)}, u32[]{:S(2)}, u32[]{:S(2)}) collective-permute-start(bf16[64,2176]{1,0:T(8,128)(2,1)S(1)} %collective-permute-done.8.refs_3_), channel_id=1, source_target_pairs={{4,0},{8,4},{12,8},{14,12},{10,14},{6,10},{2,6},{0,2},{5,1},{9,5},... | collective-permute-start | bytes 835592 | tf_op jit(solution)/shard_map/ppermute | solution.py:427
  39.8 12.6 %collective-permute-start.17 = (bf16[32,2176]{1,0:T(8,128)(2,1)S(1)}, bf16[32,2176]{1,0:T(8,128)(2,1)S(1)}, u32[]{:S(2)}, u32[]{:S(2)}) collective-permute-start(bf16[32,2176]{1,0:T(8,128)(2,1)S(1)} %get-tuple-element.83), channel_id=1, source_target_pairs={{0,4},{4,8},{8,12},{12,14},{14,10},{10,6},{6,2},{2,0},{1,5},{5,9},... | collective-permute-start | bytes 417800 | tf_op jit(solution)/shard_map/ppermute | solution.py:443
  40.1 12.7 %collective-permute-start.18 = (bf16[32,2176]{1,0:T(8,128)(2,1)S(1)}, bf16[32,2176]{1,0:T(8,128)(2,1)S(1)}, u32[]{:S(2)}, u32[]{:S(2)}) collective-permute-start(bf16[32,2176]{1,0:T(8,128)(2,1)S(1)} %get-tuple-element.84), channel_id=1, source_target_pairs={{4,0},{8,4},{12,8},{14,12},{10,14},{6,10},{2,6},{0,2},{5,1},{9,5},... | collective-permute-start | bytes 417800 | tf_op jit(solution)/shard_map/ppermute | solution.py:444
  45.7 7.1 %collective-permute-start.19 = (bf16[32,2176]{1,0:T(8,128)(2,1)S(1)}, bf16[32,2176]{1,0:T(8,128)(2,1)S(1)}, u32[]{:S(2)}, u32[]{:S(2)}) collective-permute-start(bf16[32,2176]{1,0:T(8,128)(2,1)S(1)} %get-tuple-element.86), channel_id=1, source_target_pairs={{0,4},{4,8},{8,12},{12,14},{14,10},{10,6},{6,2},{2,0},{1,5},{5,9},... | collective-permute-start | bytes 417800 | tf_op jit(solution)/shard_map/ppermute | solution.py:443
  45.9 6.9 %collective-permute-start.20 = (bf16[32,2176]{1,0:T(8,128)(2,1)S(1)}, bf16[32,2176]{1,0:T(8,128)(2,1)S(1)}, u32[]{:S(2)}, u32[]{:S(2)}) collective-permute-start(bf16[32,2176]{1,0:T(8,128)(2,1)S(1)} %get-tuple-element.87), channel_id=1, source_target_pairs={{4,0},{8,4},{12,8},{14,12},{10,14},{6,10},{2,6},{0,2},{5,1},{9,5},... | collective-permute-start | bytes 417800 | tf_op jit(solution)/shard_map/ppermute | solution.py:444
  50.7 9.0 %collective-permute-start.13 = (bf16[64,2048]{1,0:T(8,128)(2,1)S(1)}, bf16[64,2048]{1,0:T(8,128)(2,1)S(1)}, u32[]{:S(2)}, u32[]{:S(2)}) collective-permute-start(bf16[64,2048]{1,0:T(8,128)(2,1)S(1)} %get-tuple-element.73), channel_id=1, source_target_pairs={{4,0},{8,4},{12,8},{14,12},{10,14},{6,10},{2,6},{0,2},{5,1},{9,5},... | collective-permute-start | bytes 786440 | tf_op jit(solution)/shard_map/ppermute | solution.py:397
  52.3 7.4 %collective-permute-start.14 = (bf16[64,2048]{1,0:T(8,128)(2,1)S(1)}, bf16[64,2048]{1,0:T(8,128)(2,1)S(1)}, u32[]{:S(2)}, u32[]{:S(2)}) collective-permute-start(bf16[64,2048]{1,0:T(8,128)(2,1)S(1)} %get-tuple-element.74), channel_id=1, source_target_pairs={{0,4},{4,8},{8,12},{12,14},{14,10},{10,6},{6,2},{2,0},{1,5},{5,9},... | collective-permute-start | bytes 786440 | tf_op jit(solution)/shard_map/ppermute | solution.py:397
  56.6 12.6 %collective-permute-start.21 = (bf16[64,2048]{1,0:T(8,128)(2,1)S(1)}, bf16[64,2048]{1,0:T(8,128)(2,1)S(1)}, u32[]{:S(2)}, u32[]{:S(2)}) collective-permute-start(bf16[64,2048]{1,0:T(8,128)(2,1)S(1)} %get-tuple-element.88), channel_id=1, source_target_pairs={{0,12},{4,6},{8,10},{12,0},{14,2},{10,8},{6,4},{2,14},{1,13},{5,7}... | collective-permute-start | bytes 786440 | tf_op jit(solution)/shard_map/ppermute | solution.py:478
  59.8 8.6 %collective-permute-start.24 = (bf16[64,1024]{1,0:T(8,128)(2,1)S(1)}, bf16[64,1024]{1,0:T(8,128)(2,1)S(1)}, u32[]{:S(2)}, u32[]{:S(2)}) collective-permute-start(bf16[64,1024]{1,0:T(8,128)(2,1)S(1)} %get-tuple-element.91), channel_id=1, source_target_pairs={{4,0},{8,4},{12,8},{14,12},{10,14},{6,10},{2,6},{0,2},{5,1},{9,5},... | collective-permute-start | bytes 393224 | tf_op jit(solution)/shard_map/ppermute | solution.py:397
  61.4 7.8 %collective-permute-start.25 = (bf16[64,1024]{1,0:T(8,128)(2,1)S(1)}, bf16[64,1024]{1,0:T(8,128)(2,1)S(1)}, u32[]{:S(2)}, u32[]{:S(2)}) collective-permute-start(bf16[64,1024]{1,0:T(8,128)(2,1)S(1)} %get-tuple-element.92), channel_id=1, source_target_pairs={{0,4},{4,8},{8,12},{12,14},{14,10},{10,6},{6,2},{2,0},{1,5},{5,9},... | collective-permute-start | bytes 393224 | tf_op jit(solution)/shard_map/ppermute | solution.py:397
  61.9 9.5 %collective-permute-start.15 = (bf16[64,1024]{1,0:T(8,128)(2,1)S(1)}, bf16[64,1024]{1,0:T(8,128)(2,1)S(1)}, u32[]{:S(2)}, u32[]{:S(2)}) collective-permute-start(bf16[64,1024]{1,0:T(8,128)(2,1)S(1)} %get-tuple-element.75), channel_id=1, source_target_pairs={{4,0},{8,4},{12,8},{14,12},{10,14},{6,10},{2,6},{0,2},{5,1},{9,5},... | collective-permute-start | bytes 393224 | tf_op jit(solution)/shard_map/ppermute | solution.py:397
  66.4 5.0 %collective-permute-start.16 = (bf16[64,1024]{1,0:T(8,128)(2,1)S(1)}, bf16[64,1024]{1,0:T(8,128)(2,1)S(1)}, u32[]{:S(2)}, u32[]{:S(2)}) collective-permute-start(bf16[64,1024]{1,0:T(8,128)(2,1)S(1)} %get-tuple-element.76), channel_id=1, source_target_pairs={{0,4},{4,8},{8,12},{12,14},{14,10},{10,6},{6,2},{2,0},{1,5},{5,9},... | collective-permute-start | bytes 393224 | tf_op jit(solution)/shard_map/ppermute | solution.py:397
  68.4 5.2 %collective-permute-start.28 = (f32[32,1216]{1,0:T(8,128)S(1)}, f32[32,1216]{1,0:T(8,128)S(1)}, u32[]{:S(2)}, u32[]{:S(2)}) collective-permute-start(f32[32,1216]{1,0:T(8,128)S(1)} %get-tuple-element.106), channel_id=1, source_target_pairs={{0,1},{1,0},{2,3},{3,2},{4,5},{5,4},{6,7},{7,6},{8,9},{9,8},{10,11... | collective-permute-start | bytes 466952 | tf_op jit(solution)/shard_map/ppermute | solution.py:517
  69.3 6.4 %collective-permute-start.26 = (bf16[64,1024]{1,0:T(8,128)(2,1)S(1)}, bf16[64,1024]{1,0:T(8,128)(2,1)S(1)}, u32[]{:S(2)}, u32[]{:S(2)}) collective-permute-start(bf16[64,1024]{1,0:T(8,128)(2,1)S(1)} %get-tuple-element.93), channel_id=1, source_target_pairs={{4,0},{8,4},{12,8},{14,12},{10,14},{6,10},{2,6},{0,2},{5,1},{9,5},... | collective-permute-start | bytes 393224 | tf_op jit(solution)/shard_map/ppermute | solution.py:397
  71.4 5.6 %collective-permute-start.27 = (bf16[64,1024]{1,0:T(8,128)(2,1)S(1)}, bf16[64,1024]{1,0:T(8,128)(2,1)S(1)}, u32[]{:S(2)}, u32[]{:S(2)}) collective-permute-start(bf16[64,1024]{1,0:T(8,128)(2,1)S(1)} %get-tuple-element.94), channel_id=1, source_target_pairs={{0,4},{4,8},{8,12},{12,14},{14,10},{10,6},{6,2},{2,0},{1,5},{5,9},... | collective-permute-start | bytes 393224 | tf_op jit(solution)/shard_map/ppermute | solution.py:397
  71.5 5.8 %collective-permute-start.22 = (bf16[64,1024]{1,0:T(8,128)(2,1)S(1)}, bf16[64,1024]{1,0:T(8,128)(2,1)S(1)}, u32[]{:S(2)}, u32[]{:S(2)}) collective-permute-start(bf16[64,1024]{1,0:T(8,128)(2,1)S(1)} %get-tuple-element.89), channel_id=1, source_target_pairs={{4,0},{8,4},{12,8},{14,12},{10,14},{6,10},{2,6},{0,2},{5,1},{9,5},... | collective-permute-start | bytes 393224 | tf_op jit(solution)/shard_map/ppermute | solution.py:397
  73.6 5.0 %collective-permute-start.23 = (bf16[64,1024]{1,0:T(8,128)(2,1)S(1)}, bf16[64,1024]{1,0:T(8,128)(2,1)S(1)}, u32[]{:S(2)}, u32[]{:S(2)}) collective-permute-start(bf16[64,1024]{1,0:T(8,128)(2,1)S(1)} %get-tuple-element.90), channel_id=1, source_target_pairs={{0,4},{4,8},{8,12},{12,14},{14,10},{10,6},{6,2},{2,0},{1,5},{5,9},... | collective-permute-start | bytes 393224 | tf_op jit(solution)/shard_map/ppermute | solution.py:397

commit v12 on v9

--- a/solution.py
+++ b/solution.py
@@ -67,8 +67,8 @@
         low_rank = matmul_bt(hidden, factor_in_ref[...])
         return activation, up_pre * derivative, hidden, low_rank
 
-    def scales(self, grad_refs):
-        columns = stacked(grad_refs, slice(self.model_width, None)).astype(f32)
+    def scales(self, token_refs):
+        columns = stacked(token_refs, slice(self.model_width, None)).astype(f32)
         lane = lax.broadcasted_iota(jnp.int32, columns.shape, 1)
         first = lax.axis_index("expert") * self.experts
         return [
@@ -85,9 +85,9 @@
         return out
 
     def backward(
-        self, grad_refs, activation, slope, factor_in_ref, factor_out_ref, weight_refs, rows_ref
+        self, token_refs, grad_refs, activation, slope, factor_in_ref, factor_out_ref, weight_refs, rows_ref
     ):
-        scales = self.scales(grad_refs)
+        scales = self.scales(token_refs)
         adapter_back, grad_down = 0.0, 0.0
         spans = self.spans()
         for span, weight in zip(spans, weight_refs):
@@ -127,7 +127,7 @@
     out_refs, send_refs = refs[:2], refs[2:]
     activation, slope, hidden, low_rank = plan.forward(token_refs, factor_in_ref, weight_refs)
     rank_scale, back_scaled = plan.backward(
-        grad_refs, activation, slope, factor_in_ref, factor_out_ref, weight_refs, rows_ref
+        token_refs, grad_refs, activation, slope, factor_in_ref, factor_out_ref, weight_refs, rows_ref
     )
     for (first_row, span), send_ref in zip(blocks, send_refs):
         send_ref[...] = rows_ref[first_row : first_row + send_ref.shape[0], span].astype(bf16)
@@ -142,7 +142,7 @@
     packed_ref, grads_ref, tokens_held_ref, factor_in_ref, ids_held, route_held, sems = refs
     width, rank = plan.hidden_width, plan.rank
     pairs = [(ids_ref, ids_held), (route_ref, route_held)]
-    pairs.append((out_grad_ref, grads_ref.at[:, : plan.model_width]))
+    pairs.append((out_grad_ref, grads_ref))
     pairs.append((tokens_ref, tokens_held_ref.at[:, : plan.model_width]))
     for kind in range(3):
         for expert in range(plan.experts):
@@ -167,14 +167,13 @@
                 ] = jnp.zeros((rank, width), bf16)
     copies[0].wait()
     copies[1].wait()
-    rows, lanes = grads_ref.shape[0], grads_ref.shape[1] - plan.model_width
+    rows, lanes = grads_ref.shape[0], tokens_held_ref.shape[1] - plan.model_width
     expert_at = lax.broadcasted_iota(jnp.int32, (lanes, rows), 0)
     ids, route = ids_held[...], route_held[...].astype(f32)
     dense = jnp.zeros((lanes, rows), f32)
     for k in range(ids.shape[0]):
         dense = jnp.where(ids[k : k + 1, :] == expert_at, route[k : k + 1, :], dense)
     dense = dense.T.astype(bf16)
-    grads_ref[:, plan.model_width :] = dense
     tokens_held_ref[:, plan.model_width :] = dense
     for copy in copies[2:]:
         copy.wait()
@@ -311,7 +310,7 @@
         functools.partial(prepare_kernel, plan),
         out_shape=(
             jax.ShapeDtypeStruct((depth, 3 * wide), bf16),
-            jax.ShapeDtypeStruct((token_count, model_width + lanes), bf16),
+            jax.ShapeDtypeStruct((token_count, model_width), bf16),
             jax.ShapeDtypeStruct((token_count, model_width + lanes), bf16),
             jax.ShapeDtypeStruct((ranks, wide), bf16),
         ),

time: 79.3 us -> 78.3 us (0.987)
  waiting for transfers between devices: 27 us -> 25.9 us
    ppermute x8, waiting for transfers between devices: 16.5 us -> 15.3 us  [per_device(): lax.ppermute(x, 'expert', forward)]
where the time goes in v12:
time: 78.3 us; the launch traced here: 78.1 us
  starting transfers between devices  31.5 us (40%)
  waiting for transfers between devices  25.9 us (33%)
  Pallas kernels  19.9 us (25%)
    ppermute x8, starting transfers between devices, per_device(): lax.ppermute(x, 'expert', forward)  16.1 us
    pallas_call x4, Pallas kernels, expert_call(): pl.pallas_call(functools.partial(whole_kernel, plan, len(pieces), blocks,...  15.3 us
    ppermute x8, waiting for transfers between devices, per_device(): lax.ppermute(x, 'expert', forward)  15.3 us
    ppermute x10, starting transfers between devices, send(): return lax.ppermute(value, 'expert', ways[way][1])  10.4 us
    ppermute x10, waiting for transfers between devices, send(): return lax.ppermute(value, 'expert', ways[way][1])  8.01 us
    ppermute x1, starting transfers between devices, per_device(): skipped.append(lax.ppermute(value, 'expert', pairs))  3.59 us
    pallas_call x1, Pallas kernels, per_device(): pl.pallas_call(functools.partial(prepare_kernel, plan), out_shape=(jax.Sh...  2.65 us
    ppermute x6, waiting for transfers between devices, per_device(): ahead.append(tuple((lax.ppermute(x, 'expert', backward) for x in ahead[d])))  2.58 us
  transfers between devices with their start and end apart: 29, of which 11 were waited for; matrix products, arithmetic and copies ran while one was open for 0% of the time, Pallas kernels for 21%

profile of v12, /device:TPU:0, one launch (start us, length us, event | category | flops | bytes accessed | tf_op | source)
XLA Modules:
  0.0 78.1 jit_solution(8749530245855361866)
XLA Ops:
  0.6 2.6 %shard_map.112 = (bf16[1024,2304]{1,0:T(8,128)(2,1)S(1)}, bf16[64,2048]{1,0:T(8,128)(2,1)S(1)}, bf16[64,2176]{1,0:T(8,128)(2,1)S(1)}, bf16[32,768]{1,0:T(8,128)(2,1)S(1)}) custom-call(bf16[2,1024,384]{2,1,0:T(8,128)(2,1)} %refs_0_.1, bf16[2,1024,384]{2,1,0:T(8,128)(2,1)} %refs_1_.1, bf16[2,1024,384]{2,1,0:T(8,128)(2,1)} %refs_2_.1, ...), custom_call_target="tpu_custom_call" | custom-call | tf_op jit(solution)/shard_map/pallas_call | solution.py:309
  3.3 0.5 collective-permute-start.4
  3.8 2.6 %collective-permute-start.2 = (bf16[64,2048]{1,0:T(8,128)(2,1)S(1)}, bf16[64,2048]{1,0:T(8,128)(2,1)S(1)}, u32[]{:S(2)}, u32[]{:S(2)}) collective-permute-start(bf16[64,2048]{1,0:T(8,128)(2,1)S(1)} %get-tuple-element.49.refs_5_), channel_id=1, source_target_pairs={{0,4},{4,8},{8,12},{12,14},{14,10},{10,6},{6,2},{2,0},{1,5},{5,9},... | collective-permute-start | bytes 786440 | tf_op jit(solution)/shard_map/ppermute | solution.py:378
  6.5 2.0 %collective-permute-start = (bf16[64,2176]{1,0:T(8,128)(2,1)S(1)}, bf16[64,2176]{1,0:T(8,128)(2,1)S(1)}, u32[]{:S(2)}, u32[]{:S(2)}) collective-permute-start(bf16[64,2176]{1,0:T(8,128)(2,1)S(1)} %get-tuple-element.48.refs_2_), channel_id=1, source_target_pairs={{0,4},{4,8},{8,12},{12,14},{14,10},{10,6},{6,2},{2,0},{1,5},{5,9},... | collective-permute-start | bytes 835592 | tf_op jit(solution)/shard_map/ppermute | solution.py:378
  8.5 5.0 %collective-permute-done.2.refs_3_ = bf16[64,2048]{1,0:T(8,128)(2,1)S(1)} collective-permute-done((bf16[64,2048]{1,0:T(8,128)(2,1)S(1)}, bf16[64,2048]{1,0:T(8,128)(2,1)S(1)}, u32[]{:S(2)}, u32[]{:S(2)}) %collective-permute-start.2) | collective-permute-done | bytes 262176 | tf_op jit(solution)/shard_map/ppermute | solution.py:378
  13.5 2.0 %collective-permute-start.7 = (bf16[64,2048]{1,0:T(8,128)(2,1)S(1)}, bf16[64,2048]{1,0:T(8,128)(2,1)S(1)}, u32[]{:S(2)}, u32[]{:S(2)}) collective-permute-start(bf16[64,2048]{1,0:T(8,128)(2,1)S(1)} %collective-permute-done.2.refs_3_), channel_id=1, source_target_pairs={{0,4},{4,8},{8,12},{12,14},{14,10},{10,6},{6,2},{2,0},{1,5},{5,9},... | collective-permute-start | bytes 786440 | tf_op jit(solution)/shard_map/ppermute | solution.py:378
  15.6 0.0 collective-permute-done.3.refs_4_
  15.6 3.9 %collective-permute-done.refs_0_ = bf16[64,2176]{1,0:T(8,128)(2,1)S(1)} collective-permute-done((bf16[64,2176]{1,0:T(8,128)(2,1)S(1)}, bf16[64,2176]{1,0:T(8,128)(2,1)S(1)}, u32[]{:S(2)}, u32[]{:S(2)}) %collective-permute-start) | collective-permute-done | bytes 278560 | tf_op jit(solution)/shard_map/ppermute | solution.py:378
  19.5 2.0 %collective-permute-start.5 = (bf16[64,2176]{1,0:T(8,128)(2,1)S(1)}, bf16[64,2176]{1,0:T(8,128)(2,1)S(1)}, u32[]{:S(2)}, u32[]{:S(2)}) collective-permute-start(bf16[64,2176]{1,0:T(8,128)(2,1)S(1)} %collective-permute-done.refs_0_), channel_id=1, source_target_pairs={{0,4},{4,8},{8,12},{12,14},{14,10},{10,6},{6,2},{2,0},{1,5},{5,9},... | collective-permute-start | bytes 835592 | tf_op jit(solution)/shard_map/ppermute | solution.py:378
  21.5 0.0 collective-permute-done.1.refs_1_
  21.6 0.0 collective-permute-start.6
  21.6 3.5 %collective-permute-done.7.refs_2_ = bf16[64,2048]{1,0:T(8,128)(2,1)S(1)} collective-permute-done((bf16[64,2048]{1,0:T(8,128)(2,1)S(1)}, bf16[64,2048]{1,0:T(8,128)(2,1)S(1)}, u32[]{:S(2)}, u32[]{:S(2)}) %collective-permute-start.7) | collective-permute-done | bytes 262176 | tf_op jit(solution)/shard_map/ppermute | solution.py:378
  25.1 2.0 %collective-permute-start.11 = (bf16[64,2048]{1,0:T(8,128)(2,1)S(1)}, bf16[64,2048]{1,0:T(8,128)(2,1)S(1)}, u32[]{:S(2)}, u32[]{:S(2)}) collective-permute-start(bf16[64,2048]{1,0:T(8,128)(2,1)S(1)} %collective-permute-done.7.refs_2_), channel_id=1, source_target_pairs={{0,4},{4,8},{8,12},{12,14},{14,10},{10,6},{6,2},{2,0},{1,5},{5,9},... | collective-permute-start | bytes 786440 | tf_op jit(solution)/shard_map/ppermute | solution.py:378
  27.1 0.0 collective-permute-done.8.refs_3_
  27.2 0.0 collective-permute-start.12
  27.2 4.6 %shard_map.113 = (f32[192,2048]{1,0:T(8,128)S(1)}, f32[32,768]{1,0:T(8,128)S(1)}, f32[32,2048]{1,0:T(8,128)S(1)}) custom-call(bf16[64,2176]{1,0:T(8,128)(2,1)S(1)} %collective-permute-done.refs_0_, bf16[64,2176]{1,0:T(8,128)(2,1)S(1)} %collective-permute-done.1.refs_1_, bf16[64,2176]{1,0:T(8,128)(2,1)S(1)} %get-tuple-element.48.refs_2_, ...), custom_call_target="tpu_custom_call" | custom-call | flops 3019898880 | bytes 11599872 | tf_op jit(solution)/shard_map/pallas_call | solution.py:267
  31.8 2.1 %collective-permute-start.9 = (bf16[64,2176]{1,0:T(8,128)(2,1)S(1)}, bf16[64,2176]{1,0:T(8,128)(2,1)S(1)}, u32[]{:S(2)}, u32[]{:S(2)}) collective-permute-start(bf16[64,2176]{1,0:T(8,128)(2,1)S(1)} %collective-permute-done.5.refs_0_), channel_id=1, source_target_pairs={{0,4},{4,8},{8,12},{12,14},{14,10},{10,6},{6,2},{2,0},{1,5},{5,9},... | collective-permute-start | bytes 835592 | tf_op jit(solution)/shard_map/ppermute | solution.py:378
  33.9 2.8 %collective-permute-done.11.refs_2_.first_ref = bf16[64,2048]{1,0:T(8,128)(2,1)S(1)} collective-permute-done((bf16[64,2048]{1,0:T(8,128)(2,1)S(1)}, bf16[64,2048]{1,0:T(8,128)(2,1)S(1)}, u32[]{:S(2)}, u32[]{:S(2)}) %collective-permute-start.11) | collective-permute-done | bytes 262176 | tf_op jit(solution)/shard_map/ppermute | solution.py:378
  36.7 2.1 %collective-permute-done.12.refs_3_.second_ref = bf16[64,2048]{1,0:T(8,128)(2,1)S(1)} collective-permute-done((bf16[64,2048]{1,0:T(8,128)(2,1)S(1)}, bf16[64,2048]{1,0:T(8,128)(2,1)S(1)}, u32[]{:S(2)}, u32[]{:S(2)}) %collective-permute-start.12) | collective-permute-done | bytes 262176 | tf_op jit(solution)/shard_map/ppermute | solution.py:379
  38.8 1.6 %collective-permute-start.19 = (bf16[32,2048]{1,0:T(8,128)(2,1)S(1)}, bf16[32,2048]{1,0:T(8,128)(2,1)S(1)}, u32[]{:S(2)}, u32[]{:S(2)}) collective-permute-start(bf16[32,2048]{1,0:T(8,128)(2,1)S(1)} %get-tuple-element.76), channel_id=1, source_target_pairs={{0,4},{4,8},{8,12},{12,14},{14,10},{10,6},{6,2},{2,0},{1,5},{5,9},... | collective-permute-start | bytes 393224 | tf_op jit(solution)/shard_map/ppermute | solution.py:390
  40.4 0.4 collective-permute-start.20
  40.9 3.5 %shard_map.114 = (f32[128,2048]{1,0:T(8,128)S(1)}, f32[32,768]{1,0:T(8,128)S(1)}, f32[32,2048]{1,0:T(8,128)S(1)}) custom-call(bf16[64,2176]{1,0:T(8,128)(2,1)S(1)} %collective-permute-done.5.refs_0_, bf16[64,2176]{1,0:T(8,128)(2,1)S(1)} %collective-permute-done.6.refs_1_, bf16[64,2048]{1,0:T(8,128)(2,1)S(1)} %collective-permute-done.7.refs_2_, ...), custom_call_target="tpu_custom_call" | custom-call | flops 2013265920 | bytes 11059200 | tf_op jit(solution)/shard_map/pallas_call | solution.py:267
  44.4 0.4 collective-permute-done.10.refs_1_.second_ref
  44.8 1.6 %collective-permute-start.17 = (bf16[32,2176]{1,0:T(8,128)(2,1)S(1)}, bf16[32,2176]{1,0:T(8,128)(2,1)S(1)}, u32[]{:S(2)}, u32[]{:S(2)}) collective-permute-start(bf16[32,2176]{1,0:T(8,128)(2,1)S(1)} %get-tuple-element.74), channel_id=1, source_target_pairs={{0,4},{4,8},{8,12},{12,14},{14,10},{10,6},{6,2},{2,0},{1,5},{5,9},... | collective-permute-start | bytes 417800 | tf_op jit(solution)/shard_map/ppermute | solution.py:390
  46.4 0.4 collective-permute-start.18
  46.9 3.6 %shard_map.115 = (f32[32,768]{1,0:T(8,128)S(1)}, f32[32,2048]{1,0:T(8,128)S(1)}, bf16[64,2048]{1,0:T(8,128)(2,1)S(1)}, bf16[64,2048]{1,0:T(8,128)(2,1)S(1)}) custom-call(bf16[64,2176]{1,0:T(8,128)(2,1)S(1)} %collective-permute-done.9.refs_0_.first_ref, bf16[64,2176]{1,0:T(8,128)(2,1)S(1)} %collective-permute-done.10.refs_1_.second_ref, ...), custom_call_target="tpu_custom_call" | custom-call | flops 2013265920 | bytes 11059200 | tf_op jit(solution)/shard_map/pallas_call | solution.py:267
  50.4 0.1 collective-permute-start.13
  50.5 2.0 %collective-permute-start.14 = (bf16[64,2048]{1,0:T(8,128)(2,1)S(1)}, bf16[64,2048]{1,0:T(8,128)(2,1)S(1)}, u32[]{:S(2)}, u32[]{:S(2)}) collective-permute-start(bf16[64,2048]{1,0:T(8,128)(2,1)S(1)} %get-tuple-element.69), channel_id=1, source_target_pairs={{0,4},{4,8},{8,12},{12,14},{14,10},{10,6},{6,2},{2,0},{1,5},{5,9},... | collective-permute-start | bytes 786440 | tf_op jit(solution)/shard_map/ppermute | solution.py:360
  52.5 3.7 %shard_map.119 = (f32[32,768]{1,0:T(8,128)S(1)}, f32[32,2048]{1,0:T(8,128)S(1)}, bf16[64,2048]{1,0:T(8,128)(2,1)S(1)}) custom-call(bf16[32,2176]{1,0:T(8,128)(2,1)S(1)} %collective-permute-done.17.refs_0_, bf16[32,2176]{1,0:T(8,128)(2,1)S(1)} %collective-permute-done.18.refs_1_, bf16[32,2048]{1,0:T(8,128)(2,1)S(1)} %collective-permute-done.19.refs_2_, ...), custom_call_target="tpu_custom_call" | custom-call | flops 1006632960 | bytes 10518528 | tf_op jit(solution)/shard_map/pallas_call | solution.py:267
  56.2 3.6 %collective-permute-start.21 = (bf16[64,2048]{1,0:T(8,128)(2,1)S(1)}, bf16[64,2048]{1,0:T(8,128)(2,1)S(1)}, u32[]{:S(2)}, u32[]{:S(2)}) collective-permute-start(bf16[64,2048]{1,0:T(8,128)(2,1)S(1)} %get-tuple-element.80), channel_id=1, source_target_pairs={{0,12},{4,6},{8,10},{12,0},{14,2},{10,8},{6,4},{2,14},{1,13},{5,7}... | collective-permute-start | bytes 786440 | tf_op jit(solution)/shard_map/ppermute | solution.py:407
  59.9 0.5 collective-permute-start.15
  60.4 1.6 %collective-permute-start.16 = (bf16[64,1024]{1,0:T(8,128)(2,1)S(1)}, bf16[64,1024]{1,0:T(8,128)(2,1)S(1)}, u32[]{:S(2)}, u32[]{:S(2)}) collective-permute-start(bf16[64,1024]{1,0:T(8,128)(2,1)S(1)} %get-tuple-element.71), channel_id=1, source_target_pairs={{0,4},{4,8},{8,12},{12,14},{14,10},{10,6},{6,2},{2,0},{1,5},{5,9},... | collective-permute-start | bytes 393224 | tf_op jit(solution)/shard_map/ppermute | solution.py:360
  62.0 0.5 collective-permute-start.24
  62.5 1.6 %collective-permute-start.25 = (bf16[64,1024]{1,0:T(8,128)(2,1)S(1)}, bf16[64,1024]{1,0:T(8,128)(2,1)S(1)}, u32[]{:S(2)}, u32[]{:S(2)}) collective-permute-start(bf16[64,1024]{1,0:T(8,128)(2,1)S(1)} %get-tuple-element.84), channel_id=1, source_target_pairs={{0,4},{4,8},{8,12},{12,14},{14,10},{10,6},{6,2},{2,0},{1,5},{5,9},... | collective-permute-start | bytes 393224 | tf_op jit(solution)/shard_map/ppermute | solution.py:360
  64.1 0.1 shard_map.124
  64.2 4.1 %collective-permute-done.15.refs_1_ = bf16[64,1024]{1,0:T(8,128)(2,1)S(1)} collective-permute-done((bf16[64,1024]{1,0:T(8,128)(2,1)S(1)}, bf16[64,1024]{1,0:T(8,128)(2,1)S(1)}, u32[]{:S(2)}, u32[]{:S(2)}) %collective-permute-start.15) | collective-permute-done | bytes 131104 | tf_op jit(solution)/shard_map/ppermute | solution.py:360
  68.3 0.1 shard_map.120
  68.4 1.1 %collective-permute-start.22 = (bf16[64,1024]{1,0:T(8,128)(2,1)S(1)}, bf16[64,1024]{1,0:T(8,128)(2,1)S(1)}, u32[]{:S(2)}, u32[]{:S(2)}) collective-permute-start(bf16[64,1024]{1,0:T(8,128)(2,1)S(1)} %get-tuple-element.81), channel_id=1, source_target_pairs={{4,0},{8,4},{12,8},{14,12},{10,14},{6,10},{2,6},{0,2},{5,1},{9,5},... | collective-permute-start | bytes 393224 | tf_op jit(solution)/shard_map/ppermute | solution.py:360
  69.5 1.0 %collective-permute-start.23 = (bf16[64,1024]{1,0:T(8,128)(2,1)S(1)}, bf16[64,1024]{1,0:T(8,128)(2,1)S(1)}, u32[]{:S(2)}, u32[]{:S(2)}) collective-permute-start(bf16[64,1024]{1,0:T(8,128)(2,1)S(1)} %get-tuple-element.82), channel_id=1, source_target_pairs={{0,4},{4,8},{8,12},{12,14},{14,10},{10,6},{6,2},{2,0},{1,5},{5,9},... | collective-permute-start | bytes 393224 | tf_op jit(solution)/shard_map/ppermute | solution.py:360
  70.5 0.1 shard_map.122
  70.6 1.1 %collective-permute-start.26 = (bf16[64,1024]{1,0:T(8,128)(2,1)S(1)}, bf16[64,1024]{1,0:T(8,128)(2,1)S(1)}, u32[]{:S(2)}, u32[]{:S(2)}) collective-permute-start(bf16[64,1024]{1,0:T(8,128)(2,1)S(1)} %get-tuple-element.85), channel_id=1, source_target_pairs={{4,0},{8,4},{12,8},{14,12},{10,14},{6,10},{2,6},{0,2},{5,1},{9,5},... | collective-permute-start | bytes 393224 | tf_op jit(solution)/shard_map/ppermute | solution.py:360
  71.7 1.0 %collective-permute-start.27 = (bf16[64,1024]{1,0:T(8,128)(2,1)S(1)}, bf16[64,1024]{1,0:T(8,128)(2,1)S(1)}, u32[]{:S(2)}, u32[]{:S(2)}) collective-permute-start(bf16[64,1024]{1,0:T(8,128)(2,1)S(1)} %get-tuple-element.86), channel_id=1, source_target_pairs={{0,4},{4,8},{8,12},{12,14},{14,10},{10,6},{6,2},{2,0},{1,5},{5,9},... | collective-permute-start | bytes 393224 | tf_op jit(solution)/shard_map/ppermute | solution.py:360
  72.7 0.7 shard_map.125
  73.4 1.4 %collective-permute-done.22.refs_1_ = bf16[64,1024]{1,0:T(8,128)(2,1)S(1)} collective-permute-done((bf16[64,1024]{1,0:T(8,128)(2,1)S(1)}, bf16[64,1024]{1,0:T(8,128)(2,1)S(1)}, u32[]{:S(2)}, u32[]{:S(2)}) %collective-permute-start.22) | collective-permute-done | bytes 131104 | tf_op jit(solution)/shard_map/ppermute | solution.py:360
  74.8 1.0 %collective-permute-done.23.refs_2_ = bf16[64,1024]{1,0:T(8,128)(2,1)S(1)} collective-permute-done((bf16[64,1024]{1,0:T(8,128)(2,1)S(1)}, bf16[64,1024]{1,0:T(8,128)(2,1)S(1)}, u32[]{:S(2)}, u32[]{:S(2)}) %collective-permute-start.23) | collective-permute-done | bytes 131104 | tf_op jit(solution)/shard_map/ppermute | solution.py:360
  75.7 1.4 %collective-permute-done.26.refs_3_ = bf16[64,1024]{1,0:T(8,128)(2,1)S(1)} collective-permute-done((bf16[64,1024]{1,0:T(8,128)(2,1)S(1)}, bf16[64,1024]{1,0:T(8,128)(2,1)S(1)}, u32[]{:S(2)}, u32[]{:S(2)}) %collective-permute-start.26) | collective-permute-done | bytes 131104 | tf_op jit(solution)/shard_map/ppermute | solution.py:360
  77.2 0.1 collective-permute-done.27.refs_4_
  77.3 0.8 %shard_map.123 = bf16[64,2048]{1,0:T(8,128)(2,1)} custom-call(f32[192,2048]{1,0:T(8,128)S(1)} %get-tuple-element.52.refs_0_, bf16[64,1024]{1,0:T(8,128)(2,1)S(1)} %collective-permute-done.22.refs_1_, bf16[64,1024]{1,0:T(8,128)(2,1)S(1)} %collective-permute-done.23.refs_2_, bf16[64,1024]{1,0:T(8,128)(2,1)S(1)} %collective-permute-done.26.refs_3_, ...), custom_call_target="tpu_custom_call" | custom-call | tf_op jit(solution)/shard_map/pallas_call | solution.py:426
  (28 shorter events, 0.2 us)
Async XLA Ops:
  0.6 26.6 %copy-start = (bf16[2,16,2048]{2,1,0:T(8,128)(2,1)S(1)}, bf16[2,16,2048]{2,1,0:T(8,128)(2,1)}, u32[]{:S(2)}) copy-start(bf16[2,16,2048]{2,1,0:T(8,128)(2,1)} %param.17) | copy-start | bytes 393220
  3.3 23.9 %collective-permute-start.4 = (bf16[1024,2304]{1,0:T(8,128)(2,1)S(1)}, bf16[1024,2304]{1,0:T(8,128)(2,1)S(1)}, u32[]{:S(2)}, u32[]{:S(2)}) collective-permute-start(bf16[1024,2304]{1,0:T(8,128)(2,1)S(1)} %get-tuple-element.51.refs_8_.refs_6_), channel_id=1, source_target_pairs={{0,1},{1,0},{2,3},{3,2},{4,5},{5,4},{6,7},{7,6},{8,9},{9,8},{10,11... | collective-permute-start | bytes 14155784 | tf_op jit(solution)/shard_map/ppermute | solution.py:341
  3.8 9.7 %collective-permute-start.2 = (bf16[64,2048]{1,0:T(8,128)(2,1)S(1)}, bf16[64,2048]{1,0:T(8,128)(2,1)S(1)}, u32[]{:S(2)}, u32[]{:S(2)}) collective-permute-start(bf16[64,2048]{1,0:T(8,128)(2,1)S(1)} %get-tuple-element.49.refs_5_), channel_id=1, source_target_pairs={{0,4},{4,8},{8,12},{12,14},{14,10},{10,6},{6,2},{2,0},{1,5},{5,9},... | collective-permute-start | bytes 786440 | tf_op jit(solution)/shard_map/ppermute | solution.py:378
  6.5 9.1 %collective-permute-start.3 = (bf16[64,2048]{1,0:T(8,128)(2,1)S(1)}, bf16[64,2048]{1,0:T(8,128)(2,1)S(1)}, u32[]{:S(2)}, u32[]{:S(2)}) collective-permute-start(bf16[64,2048]{1,0:T(8,128)(2,1)S(1)} %get-tuple-element.49.refs_5_), channel_id=1, source_target_pairs={{4,0},{8,4},{12,8},{14,12},{10,14},{6,10},{2,6},{0,2},{5,1},{9,5},... | collective-permute-start | bytes 786440 | tf_op jit(solution)/shard_map/ppermute | solution.py:379
  6.5 13.0 %collective-permute-start = (bf16[64,2176]{1,0:T(8,128)(2,1)S(1)}, bf16[64,2176]{1,0:T(8,128)(2,1)S(1)}, u32[]{:S(2)}, u32[]{:S(2)}) collective-permute-start(bf16[64,2176]{1,0:T(8,128)(2,1)S(1)} %get-tuple-element.48.refs_2_), channel_id=1, source_target_pairs={{0,4},{4,8},{8,12},{12,14},{14,10},{10,6},{6,2},{2,0},{1,5},{5,9},... | collective-permute-start | bytes 835592 | tf_op jit(solution)/shard_map/ppermute | solution.py:378
  8.5 13.1 %collective-permute-start.1 = (bf16[64,2176]{1,0:T(8,128)(2,1)S(1)}, bf16[64,2176]{1,0:T(8,128)(2,1)S(1)}, u32[]{:S(2)}, u32[]{:S(2)}) collective-permute-start(bf16[64,2176]{1,0:T(8,128)(2,1)S(1)} %get-tuple-element.48.refs_2_), channel_id=1, source_target_pairs={{4,0},{8,4},{12,8},{14,12},{10,14},{6,10},{2,6},{0,2},{5,1},{9,5},... | collective-permute-start | bytes 835592 | tf_op jit(solution)/shard_map/ppermute | solution.py:379
  13.5 11.6 %collective-permute-start.7 = (bf16[64,2048]{1,0:T(8,128)(2,1)S(1)}, bf16[64,2048]{1,0:T(8,128)(2,1)S(1)}, u32[]{:S(2)}, u32[]{:S(2)}) collective-permute-start(bf16[64,2048]{1,0:T(8,128)(2,1)S(1)} %collective-permute-done.2.refs_3_), channel_id=1, source_target_pairs={{0,4},{4,8},{8,12},{12,14},{14,10},{10,6},{6,2},{2,0},{1,5},{5,9},... | collective-permute-start | bytes 786440 | tf_op jit(solution)/shard_map/ppermute | solution.py:378
  15.6 11.6 %collective-permute-start.8 = (bf16[64,2048]{1,0:T(8,128)(2,1)S(1)}, bf16[64,2048]{1,0:T(8,128)(2,1)S(1)}, u32[]{:S(2)}, u32[]{:S(2)}) collective-permute-start(bf16[64,2048]{1,0:T(8,128)(2,1)S(1)} %collective-permute-done.3.refs_4_), channel_id=1, source_target_pairs={{4,0},{8,4},{12,8},{14,12},{10,14},{6,10},{2,6},{0,2},{5,1},{9,5},... | collective-permute-start | bytes 786440 | tf_op jit(solution)/shard_map/ppermute | solution.py:379
  19.5 12.3 %collective-permute-start.5 = (bf16[64,2176]{1,0:T(8,128)(2,1)S(1)}, bf16[64,2176]{1,0:T(8,128)(2,1)S(1)}, u32[]{:S(2)}, u32[]{:S(2)}) collective-permute-start(bf16[64,2176]{1,0:T(8,128)(2,1)S(1)} %collective-permute-done.refs_0_), channel_id=1, source_target_pairs={{0,4},{4,8},{8,12},{12,14},{14,10},{10,6},{6,2},{2,0},{1,5},{5,9},... | collective-permute-start | bytes 835592 | tf_op jit(solution)/shard_map/ppermute | solution.py:378
  21.6 12.3 %collective-permute-start.6 = (bf16[64,2176]{1,0:T(8,128)(2,1)S(1)}, bf16[64,2176]{1,0:T(8,128)(2,1)S(1)}, u32[]{:S(2)}, u32[]{:S(2)}) collective-permute-start(bf16[64,2176]{1,0:T(8,128)(2,1)S(1)} %collective-permute-done.1.refs_1_), channel_id=1, source_target_pairs={{4,0},{8,4},{12,8},{14,12},{10,14},{6,10},{2,6},{0,2},{5,1},{9,5},... | collective-permute-start | bytes 835592 | tf_op jit(solution)/shard_map/ppermute | solution.py:379
  25.1 11.6 %collective-permute-start.11 = (bf16[64,2048]{1,0:T(8,128)(2,1)S(1)}, bf16[64,2048]{1,0:T(8,128)(2,1)S(1)}, u32[]{:S(2)}, u32[]{:S(2)}) collective-permute-start(bf16[64,2048]{1,0:T(8,128)(2,1)S(1)} %collective-permute-done.7.refs_2_), channel_id=1, source_target_pairs={{0,4},{4,8},{8,12},{12,14},{14,10},{10,6},{6,2},{2,0},{1,5},{5,9},... | collective-permute-start | bytes 786440 | tf_op jit(solution)/shard_map/ppermute | solution.py:378
  27.2 11.6 %collective-permute-start.12 = (bf16[64,2048]{1,0:T(8,128)(2,1)S(1)}, bf16[64,2048]{1,0:T(8,128)(2,1)S(1)}, u32[]{:S(2)}, u32[]{:S(2)}) collective-permute-start(bf16[64,2048]{1,0:T(8,128)(2,1)S(1)} %collective-permute-done.8.refs_3_), channel_id=1, source_target_pairs={{4,0},{8,4},{12,8},{14,12},{10,14},{6,10},{2,6},{0,2},{5,1},{9,5},... | collective-permute-start | bytes 786440 | tf_op jit(solution)/shard_map/ppermute | solution.py:379
  31.8 12.5 %collective-permute-start.9 = (bf16[64,2176]{1,0:T(8,128)(2,1)S(1)}, bf16[64,2176]{1,0:T(8,128)(2,1)S(1)}, u32[]{:S(2)}, u32[]{:S(2)}) collective-permute-start(bf16[64,2176]{1,0:T(8,128)(2,1)S(1)} %collective-permute-done.5.refs_0_), channel_id=1, source_target_pairs={{0,4},{4,8},{8,12},{12,14},{14,10},{10,6},{6,2},{2,0},{1,5},{5,9},... | collective-permute-start | bytes 835592 | tf_op jit(solution)/shard_map/ppermute | solution.py:378
  33.9 10.8 %collective-permute-start.10 = (bf16[64,2176]{1,0:T(8,128)(2,1)S(1)}, bf16[64,2176]{1,0:T(8,128)(2,1)S(1)}, u32[]{:S(2)}, u32[]{:S(2)}) collective-permute-start(bf16[64,2176]{1,0:T(8,128)(2,1)S(1)} %collective-permute-done.6.refs_1_), channel_id=1, source_target_pairs={{4,0},{8,4},{12,8},{14,12},{10,14},{6,10},{2,6},{0,2},{5,1},{9,5},... | collective-permute-start | bytes 835592 | tf_op jit(solution)/shard_map/ppermute | solution.py:379
  38.8 11.7 %collective-permute-start.19 = (bf16[32,2048]{1,0:T(8,128)(2,1)S(1)}, bf16[32,2048]{1,0:T(8,128)(2,1)S(1)}, u32[]{:S(2)}, u32[]{:S(2)}) collective-permute-start(bf16[32,2048]{1,0:T(8,128)(2,1)S(1)} %get-tuple-element.76), channel_id=1, source_target_pairs={{0,4},{4,8},{8,12},{12,14},{14,10},{10,6},{6,2},{2,0},{1,5},{5,9},... | collective-permute-start | bytes 393224 | tf_op jit(solution)/shard_map/ppermute | solution.py:390
  40.4 12.1 %collective-permute-start.20 = (bf16[32,2048]{1,0:T(8,128)(2,1)S(1)}, bf16[32,2048]{1,0:T(8,128)(2,1)S(1)}, u32[]{:S(2)}, u32[]{:S(2)}) collective-permute-start(bf16[32,2048]{1,0:T(8,128)(2,1)S(1)} %get-tuple-element.77), channel_id=1, source_target_pairs={{4,0},{8,4},{12,8},{14,12},{10,14},{6,10},{2,6},{0,2},{5,1},{9,5},... | collective-permute-start | bytes 393224 | tf_op jit(solution)/shard_map/ppermute | solution.py:391
  44.8 7.8 %collective-permute-start.17 = (bf16[32,2176]{1,0:T(8,128)(2,1)S(1)}, bf16[32,2176]{1,0:T(8,128)(2,1)S(1)}, u32[]{:S(2)}, u32[]{:S(2)}) collective-permute-start(bf16[32,2176]{1,0:T(8,128)(2,1)S(1)} %get-tuple-element.74), channel_id=1, source_target_pairs={{0,4},{4,8},{8,12},{12,14},{14,10},{10,6},{6,2},{2,0},{1,5},{5,9},... | collective-permute-start | bytes 417800 | tf_op jit(solution)/shard_map/ppermute | solution.py:390
  46.4 6.1 %collective-permute-start.18 = (bf16[32,2176]{1,0:T(8,128)(2,1)S(1)}, bf16[32,2176]{1,0:T(8,128)(2,1)S(1)}, u32[]{:S(2)}, u32[]{:S(2)}) collective-permute-start(bf16[32,2176]{1,0:T(8,128)(2,1)S(1)} %get-tuple-element.75), channel_id=1, source_target_pairs={{4,0},{8,4},{12,8},{14,12},{10,14},{6,10},{2,6},{0,2},{5,1},{9,5},... | collective-permute-start | bytes 417800 | tf_op jit(solution)/shard_map/ppermute | solution.py:391
  50.4 9.4 %collective-permute-start.13 = (bf16[64,2048]{1,0:T(8,128)(2,1)S(1)}, bf16[64,2048]{1,0:T(8,128)(2,1)S(1)}, u32[]{:S(2)}, u32[]{:S(2)}) collective-permute-start(bf16[64,2048]{1,0:T(8,128)(2,1)S(1)} %get-tuple-element.68), channel_id=1, source_target_pairs={{4,0},{8,4},{12,8},{14,12},{10,14},{6,10},{2,6},{0,2},{5,1},{9,5},... | collective-permute-start | bytes 786440 | tf_op jit(solution)/shard_map/ppermute | solution.py:360
  50.5 9.3 %collective-permute-start.14 = (bf16[64,2048]{1,0:T(8,128)(2,1)S(1)}, bf16[64,2048]{1,0:T(8,128)(2,1)S(1)}, u32[]{:S(2)}, u32[]{:S(2)}) collective-permute-start(bf16[64,2048]{1,0:T(8,128)(2,1)S(1)} %get-tuple-element.69), channel_id=1, source_target_pairs={{0,4},{4,8},{8,12},{12,14},{14,10},{10,6},{6,2},{2,0},{1,5},{5,9},... | collective-permute-start | bytes 786440 | tf_op jit(solution)/shard_map/ppermute | solution.py:360
  56.2 12.1 %collective-permute-start.21 = (bf16[64,2048]{1,0:T(8,128)(2,1)S(1)}, bf16[64,2048]{1,0:T(8,128)(2,1)S(1)}, u32[]{:S(2)}, u32[]{:S(2)}) collective-permute-start(bf16[64,2048]{1,0:T(8,128)(2,1)S(1)} %get-tuple-element.80), channel_id=1, source_target_pairs={{0,12},{4,6},{8,10},{12,0},{14,2},{10,8},{6,4},{2,14},{1,13},{5,7}... | collective-permute-start | bytes 786440 | tf_op jit(solution)/shard_map/ppermute | solution.py:407
  59.9 8.4 %collective-permute-start.15 = (bf16[64,1024]{1,0:T(8,128)(2,1)S(1)}, bf16[64,1024]{1,0:T(8,128)(2,1)S(1)}, u32[]{:S(2)}, u32[]{:S(2)}) collective-permute-start(bf16[64,1024]{1,0:T(8,128)(2,1)S(1)} %get-tuple-element.70), channel_id=1, source_target_pairs={{4,0},{8,4},{12,8},{14,12},{10,14},{6,10},{2,6},{0,2},{5,1},{9,5},... | collective-permute-start | bytes 393224 | tf_op jit(solution)/shard_map/ppermute | solution.py:360
  60.4 7.9 %collective-permute-start.16 = (bf16[64,1024]{1,0:T(8,128)(2,1)S(1)}, bf16[64,1024]{1,0:T(8,128)(2,1)S(1)}, u32[]{:S(2)}, u32[]{:S(2)}) collective-permute-start(bf16[64,1024]{1,0:T(8,128)(2,1)S(1)} %get-tuple-element.71), channel_id=1, source_target_pairs={{0,4},{4,8},{8,12},{12,14},{14,10},{10,6},{6,2},{2,0},{1,5},{5,9},... | collective-permute-start | bytes 393224 | tf_op jit(solution)/shard_map/ppermute | solution.py:360
  62.0 8.5 %collective-permute-start.24 = (bf16[64,1024]{1,0:T(8,128)(2,1)S(1)}, bf16[64,1024]{1,0:T(8,128)(2,1)S(1)}, u32[]{:S(2)}, u32[]{:S(2)}) collective-permute-start(bf16[64,1024]{1,0:T(8,128)(2,1)S(1)} %get-tuple-element.83), channel_id=1, source_target_pairs={{4,0},{8,4},{12,8},{14,12},{10,14},{6,10},{2,6},{0,2},{5,1},{9,5},... | collective-permute-start | bytes 393224 | tf_op jit(solution)/shard_map/ppermute | solution.py:360
  62.5 8.0 %collective-permute-start.25 = (bf16[64,1024]{1,0:T(8,128)(2,1)S(1)}, bf16[64,1024]{1,0:T(8,128)(2,1)S(1)}, u32[]{:S(2)}, u32[]{:S(2)}) collective-permute-start(bf16[64,1024]{1,0:T(8,128)(2,1)S(1)} %get-tuple-element.84), channel_id=1, source_target_pairs={{0,4},{4,8},{8,12},{12,14},{14,10},{10,6},{6,2},{2,0},{1,5},{5,9},... | collective-permute-start | bytes 393224 | tf_op jit(solution)/shard_map/ppermute | solution.py:360
  68.3 4.4 %collective-permute-start.28 = (f32[32,1216]{1,0:T(8,128)S(1)}, f32[32,1216]{1,0:T(8,128)S(1)}, u32[]{:S(2)}, u32[]{:S(2)}) collective-permute-start(f32[32,1216]{1,0:T(8,128)S(1)} %get-tuple-element.90), channel_id=1, source_target_pairs={{0,1},{1,0},{2,3},{3,2},{4,5},{5,4},{6,7},{7,6},{8,9},{9,8},{10,11... | collective-permute-start | bytes 466952 | tf_op jit(solution)/shard_map/ppermute | solution.py:440
  68.4 6.3 %collective-permute-start.22 = (bf16[64,1024]{1,0:T(8,128)(2,1)S(1)}, bf16[64,1024]{1,0:T(8,128)(2,1)S(1)}, u32[]{:S(2)}, u32[]{:S(2)}) collective-permute-start(bf16[64,1024]{1,0:T(8,128)(2,1)S(1)} %get-tuple-element.81), channel_id=1, source_target_pairs={{4,0},{8,4},{12,8},{14,12},{10,14},{6,10},{2,6},{0,2},{5,1},{9,5},... | collective-permute-start | bytes 393224 | tf_op jit(solution)/shard_map/ppermute | solution.py:360
  69.5 6.2 %collective-permute-start.23 = (bf16[64,1024]{1,0:T(8,128)(2,1)S(1)}, bf16[64,1024]{1,0:T(8,128)(2,1)S(1)}, u32[]{:S(2)}, u32[]{:S(2)}) collective-permute-start(bf16[64,1024]{1,0:T(8,128)(2,1)S(1)} %get-tuple-element.82), channel_id=1, source_target_pairs={{0,4},{4,8},{8,12},{12,14},{14,10},{10,6},{6,2},{2,0},{1,5},{5,9},... | collective-permute-start | bytes 393224 | tf_op jit(solution)/shard_map/ppermute | solution.py:360
  70.6 6.6 %collective-permute-start.26 = (bf16[64,1024]{1,0:T(8,128)(2,1)S(1)}, bf16[64,1024]{1,0:T(8,128)(2,1)S(1)}, u32[]{:S(2)}, u32[]{:S(2)}) collective-permute-start(bf16[64,1024]{1,0:T(8,128)(2,1)S(1)} %get-tuple-element.85), channel_id=1, source_target_pairs={{4,0},{8,4},{12,8},{14,12},{10,14},{6,10},{2,6},{0,2},{5,1},{9,5},... | collective-permute-start | bytes 393224 | tf_op jit(solution)/shard_map/ppermute | solution.py:360
  71.7 5.6 %collective-permute-start.27 = (bf16[64,1024]{1,0:T(8,128)(2,1)S(1)}, bf16[64,1024]{1,0:T(8,128)(2,1)S(1)}, u32[]{:S(2)}, u32[]{:S(2)}) collective-permute-start(bf16[64,1024]{1,0:T(8,128)(2,1)S(1)} %get-tuple-element.86), channel_id=1, source_target_pairs={{0,4},{4,8},{8,12},{12,14},{14,10},{10,6},{6,2},{2,0},{1,5},{5,9},... | collective-permute-start | bytes 393224 | tf_op jit(solution)/shard_map/ppermute | solution.py:360

commit v13 on v12

--- a/solution.py
+++ b/solution.py
@@ -1,4 +1,5 @@
 import functools
+import math
 
 import jax
 import jax.numpy as jnp
@@ -45,6 +46,7 @@
         self.experts = experts
         self.wide = experts * hidden_width
         self.ranks = experts * rank
+        self.cuts = 4 if depth % 64 == 0 else 1
 
     def spans(self):
         if self.parts == 1:
@@ -85,7 +87,7 @@
         return out
 
     def backward(
-        self, token_refs, grad_refs, activation, slope, factor_in_ref, factor_out_ref, weight_refs, rows_ref
+        self, token_refs, grad_refs, activation, slope, factor_in_ref, factor_out_ref, weight_refs, turned_refs, rows_ref
     ):
         scales = self.scales(token_refs)
         adapter_back, grad_down = 0.0, 0.0
@@ -100,10 +102,15 @@
         )
         grad_gate = (grad_hidden * slope).astype(bf16)
         grad_up = (grad_hidden * activation).astype(bf16)
-        for span, weight in zip(spans, weight_refs):
-            rows_ref[:, span] = matmul_bt(grad_gate, weight[:, : self.wide]) + matmul_bt(
-                grad_up, weight[:, self.wide : 2 * self.wide]
-            )
+        for span, weight, turned in zip(spans, weight_refs, turned_refs or weight_refs):
+            if turned_refs:
+                rows_ref[:, span] = matmul(grad_gate, turned[: self.wide, :]) + matmul(
+                    grad_up, turned[self.wide :, :]
+                )
+            else:
+                rows_ref[:, span] = matmul_bt(grad_gate, weight[:, : self.wide]) + matmul_bt(
+                    grad_up, weight[:, self.wide : 2 * self.wide]
+                )
         rank_scale = self.spread(scales, self.rank)
         return rank_scale, (rank_scale * adapter_back.astype(f32)).astype(bf16)
 
@@ -115,10 +122,12 @@
             out[...] = total[...] + adapter_scale * value
 
 
-def whole_kernel(plan, pieces, blocks, keep_rows, *refs):
+def whole_kernel(plan, pieces, blocks, keep_rows, is_turned, *refs):
     token_refs, grad_refs, refs = refs[:pieces], refs[pieces : 2 * pieces], refs[2 * pieces :]
     factor_in_ref, factor_out_ref, refs = refs[0], refs[1], refs[2:]
     weight_refs, refs = refs[: plan.parts], refs[plan.parts :]
+    turned_refs = refs[: plan.parts] if is_turned else ()
+    refs = refs[len(turned_refs) :]
     total_refs, refs = refs[:2], refs[2:]
     if keep_rows:
         rows_ref, refs = refs[0], refs[1:]
@@ -127,7 +136,7 @@
     out_refs, send_refs = refs[:2], refs[2:]
     activation, slope, hidden, low_rank = plan.forward(token_refs, factor_in_ref, weight_refs)
     rank_scale, back_scaled = plan.backward(
-        token_refs, grad_refs, activation, slope, factor_in_ref, factor_out_ref, weight_refs, rows_ref
+        token_refs, grad_refs, activation, slope, factor_in_ref, factor_out_ref, weight_refs, turned_refs, rows_ref
     )
     for (first_row, span), send_ref in zip(blocks, send_refs):
         send_ref[...] = rows_ref[first_row : first_row + send_ref.shape[0], span].astype(bf16)
@@ -140,14 +149,17 @@
     out_grad_ref, ids_ref, route_ref, factor_ref = refs[:4]
     tokens_ref, refs = refs[4], refs[5:]
     packed_ref, grads_ref, tokens_held_ref, factor_in_ref, ids_held, route_held, sems = refs
-    width, rank = plan.hidden_width, plan.rank
+    width, rank, cuts = plan.hidden_width, plan.rank, plan.cuts
     pairs = [(ids_ref, ids_held), (route_ref, route_held)]
     pairs.append((out_grad_ref, grads_ref))
     pairs.append((tokens_ref, tokens_held_ref.at[:, : plan.model_width]))
     for kind in range(3):
         for expert in range(plan.experts):
             at = kind * plan.wide + expert * width
-            pairs.append((raw_refs[kind].at[expert], packed_ref.at[:, at : at + width]))
+            for cut in range(cuts):
+                rows = slice(cut * plan.depth // cuts, (cut + 1) * plan.depth // cuts)
+                source = raw_refs[kind].at[expert, rows, :]
+                pairs.append((source, packed_ref.at[rows, at : at + width]))
     for expert in range(plan.experts):
         block = factor_in_ref.at[
             expert * rank : (expert + 1) * rank, expert * width : (expert + 1) * width
@@ -206,6 +218,13 @@
     )(*operands)
 
 
+def turn_kernel(plan, *refs):
+    for weight_ref, turned_ref in zip(refs, refs[plan.parts :]):
+        step = math.gcd(2 * plan.wide, 256)
+        for at in range(0, 2 * plan.wide, step):
+            turned_ref[at : at + step, :] = weight_ref[:, at : at + step].T
+
+
 def half_rows_kernel(half, first_ref, second_ref, top_ref, bottom_ref):
     top_ref[...] = first_ref[:half]
     bottom_ref[...] = second_ref[half:]
@@ -257,7 +276,7 @@
     )(*operands)
 
 
-def expert_call(plan, pieces, blocks, block_rows, operands, totals, keep_rows):
+def expert_call(plan, pieces, blocks, block_rows, operands, totals, keep_rows, is_turned):
     rows = sum(piece[0].shape[0] for piece in pieces)
     operands = [p[0] for p in pieces] + [p[1] for p in pieces] + [*operands, *totals]
     shape = (rows, plan.model_width)
@@ -265,7 +284,7 @@
     widths = [len(range(*span.indices(plan.model_width))) for _, span in blocks]
     outs += [((block_rows, width), bf16) for width in widths]
     return pl.pallas_call(
-        functools.partial(whole_kernel, plan, len(pieces), blocks, keep_rows),
+        functools.partial(whole_kernel, plan, len(pieces), blocks, keep_rows, is_turned),
         scratch_shapes=[] if keep_rows else [pltpu.VMEM(shape, f32)],
         out_shape=tuple(jax.ShapeDtypeStruct(shape, dtype) for shape, dtype in outs),
         in_specs=[pl.BlockSpec(memory_space=pltpu.VMEM)] * len(operands),
@@ -319,7 +338,7 @@
         scratch_shapes=[
             pltpu.VMEM(expert_ids.shape[::-1], jnp.int32),
             pltpu.VMEM(route_weight.shape[::-1], bf16),
-            pltpu.SemaphoreType.DMA((4 + 4 * local_count,)),
+            pltpu.SemaphoreType.DMA((4 + (3 * plan.cuts + 1) * local_count,)),
         ],
         compiler_params=pltpu.CompilerParams(vmem_limit_bytes=16 * 1024 * 1024),
     )(
@@ -359,9 +378,11 @@
     def send(value, way):
         return lax.ppermute(value, "expert", ways[way][1])
 
-    def run(pieces, blocks, totals, keep_rows=True):
-        operands = [factor_in, factor_out, *weights]
-        return expert_call(plan, pieces, blocks, token_count, operands, totals, keep_rows)
+    def run(pieces, blocks, totals, keep_rows=True, turned=()):
+        operands = [factor_in, factor_out, *weights, *turned]
+        return expert_call(
+            plan, pieces, blocks, token_count, operands, totals, keep_rows, bool(turned)
+        )
 
     def after(value, *arrays):
         held = []
@@ -381,25 +402,32 @@
             pieces = [behind[d], ahead[d]] + ([behind[0]] if d == 1 else [])
             rows_d, *totals = run(pieces, [], totals)
             rows_at.append(rows_d)
+    turned = simple_call(
+        functools.partial(turn_kernel, plan),
+        weights,
+        [((2 * wide, w.shape[0]), bf16) for w in weights],
+    )
     if split:
         half = token_count // 2
         totals, (tokens_b, tokens_a) = after(totals, behind[full][0], ahead[full][0])
+        (grads_b,) = after(turned[0], behind[full][1])[1]
+        (grads_a,) = after(turned[0], ahead[full][1])[1]
         tokens_b, tokens_a = halves(tokens_b, tokens_a, half)
-        grads_b, grads_a = halves(behind[full][1], ahead[full][1], half)
+        grads_b, grads_a = halves(grads_b, grads_a, half)
         far = [
             tuple(lax.ppermute(x, "expert", forward) for x in (tokens_b, grads_b)),
             tuple(lax.ppermute(x, "expert", backward) for x in (tokens_a, grads_a)),
         ]
     pieces = [behind[full], ahead[full]]
     blocks = [(first_row, everything) for first_row, _ in ways.values()]
-    outs = run(pieces, blocks, totals, keep_rows=False)
+    outs = run(pieces, blocks, totals, keep_rows=False, turned=turned)
     totals = outs[:2]
     for way, value in zip(ways, outs[2:]):
         for side in columns:
             moving[side, way] = send(value, way) if side == "left" else moving["left", way]
     skipped = []
     if split:
-        *totals, value = run(far, [(0, everything)], totals, keep_rows=False)
+        *totals, value = run(far, [(0, everything)], totals, keep_rows=False, turned=turned)
         pairs = [
             (order[i], order[(i + (full if i % 2 == 0 else -full)) % peer_count])
             for i in range(peer_count)

time: 78.3 us -> 77.5 us (0.990)
  starting transfers between devices: 31.5 us -> 30.5 us
    ppermute x8, waiting for transfers between devices: 15.3 us -> 13.5 us  [per_device(): lax.ppermute(x, 'expert', forward)]
    pallas_call x4 -> x5, Pallas kernels: 0.86 us -> 2.64 us  [simple_call(): pl.pallas_call(kernel, out_shape=tuple((jax.ShapeDtypeStruct(shape, dtype...]
    pallas_call x4, Pallas kernels: 15.3 us -> 13.9 us  [expert_call(): pl.pallas_call(functools.partial(whole_kernel, plan, len(pieces), blocks,...]
    ppermute x2, waiting for transfers between devices: 0.01 us -> 0.99 us  [per_device(): lax.ppermute(x, 'expert', backward)]
    ppermute x1, starting transfers between devices: 3.59 us -> 2.6 us  [per_device(): skipped.append(lax.ppermute(value, 'expert', pairs))]
  transfers between devices with their start and end apart: 29 -> 29, of which waited for: 11 -> 12; matrix products, arithmetic and copies ran while one was open for 0% -> 0% of each run, Pallas kernels for 21% -> 22%
where the time goes in v13:
time: 77.5 us; the launch traced here: 77.4 us
  starting transfers between devices  30.5 us (39%)
  waiting for transfers between devices  25.7 us (33%)
  Pallas kernels  20.4 us (26%)
    ppermute x8, starting transfers between devices, per_device(): lax.ppermute(x, 'expert', forward)  16.1 us
    pallas_call x4, Pallas kernels, expert_call(): pl.pallas_call(functools.partial(whole_kernel, plan, len(pieces), blocks,...  13.9 us
    ppermute x8, waiting for transfers between devices, per_device(): lax.ppermute(x, 'expert', forward)  13.5 us
    ppermute x10, starting transfers between devices, send(): return lax.ppermute(value, 'expert', ways[way][1])  10.4 us
    ppermute x10, waiting for transfers between devices, send(): return lax.ppermute(value, 'expert', ways[way][1])  8.6 us
    pallas_call x1, Pallas kernels, per_device(): pl.pallas_call(functools.partial(prepare_kernel, plan), out_shape=(jax.Sh...  2.78 us
    pallas_call x5, Pallas kernels, simple_call(): pl.pallas_call(kernel, out_shape=tuple((jax.ShapeDtypeStruct(shape, dtype...  2.64 us
    ppermute x1, starting transfers between devices, per_device(): skipped.append(lax.ppermute(value, 'expert', pairs))  2.6 us
  transfers between devices with their start and end apart: 29, of which 12 were waited for; matrix products, arithmetic and copies ran while one was open for 0% of the time, Pallas kernels for 22%

profile of v13, /device:TPU:0, one launch (start us, length us, event | category | flops | bytes accessed | tf_op | source)
XLA Modules:
  0.0 77.4 jit_solution(8336059807167708741)
XLA Ops:
  0.6 2.8 %shard_map.112 = (bf16[1024,2304]{1,0:T(8,128)(2,1)S(1)}, bf16[64,2048]{1,0:T(8,128)(2,1)S(1)}, bf16[64,2176]{1,0:T(8,128)(2,1)S(1)}, bf16[32,768]{1,0:T(8,128)(2,1)S(1)}) custom-call(bf16[2,1024,384]{2,1,0:T(8,128)(2,1)} %refs_0_.1, bf16[2,1024,384]{2,1,0:T(8,128)(2,1)} %refs_1_.1, bf16[2,1024,384]{2,1,0:T(8,128)(2,1)} %refs_2_.1, ...), custom_call_target="tpu_custom_call" | custom-call | tf_op jit(solution)/shard_map/pallas_call | solution.py:328
  3.4 0.5 collective-permute-start.4
  3.9 2.6 %collective-permute-start.2 = (bf16[64,2048]{1,0:T(8,128)(2,1)S(1)}, bf16[64,2048]{1,0:T(8,128)(2,1)S(1)}, u32[]{:S(2)}, u32[]{:S(2)}) collective-permute-start(bf16[64,2048]{1,0:T(8,128)(2,1)S(1)} %get-tuple-element.53.refs_5_), channel_id=1, source_target_pairs={{0,4},{4,8},{8,12},{12,14},{14,10},{10,6},{6,2},{2,0},{1,5},{5,9},... | collective-permute-start | bytes 786440 | tf_op jit(solution)/shard_map/ppermute | solution.py:399
  6.6 2.0 %collective-permute-start = (bf16[64,2176]{1,0:T(8,128)(2,1)S(1)}, bf16[64,2176]{1,0:T(8,128)(2,1)S(1)}, u32[]{:S(2)}, u32[]{:S(2)}) collective-permute-start(bf16[64,2176]{1,0:T(8,128)(2,1)S(1)} %get-tuple-element.52.refs_2_), channel_id=1, source_target_pairs={{0,4},{4,8},{8,12},{12,14},{14,10},{10,6},{6,2},{2,0},{1,5},{5,9},... | collective-permute-start | bytes 835592 | tf_op jit(solution)/shard_map/ppermute | solution.py:399
  8.6 5.0 %collective-permute-done.2.refs_3_ = bf16[64,2048]{1,0:T(8,128)(2,1)S(1)} collective-permute-done((bf16[64,2048]{1,0:T(8,128)(2,1)S(1)}, bf16[64,2048]{1,0:T(8,128)(2,1)S(1)}, u32[]{:S(2)}, u32[]{:S(2)}) %collective-permute-start.2) | collective-permute-done | bytes 262176 | tf_op jit(solution)/shard_map/ppermute | solution.py:399
  13.7 2.0 %collective-permute-start.7 = (bf16[64,2048]{1,0:T(8,128)(2,1)S(1)}, bf16[64,2048]{1,0:T(8,128)(2,1)S(1)}, u32[]{:S(2)}, u32[]{:S(2)}) collective-permute-start(bf16[64,2048]{1,0:T(8,128)(2,1)S(1)} %collective-permute-done.2.refs_3_), channel_id=1, source_target_pairs={{0,4},{4,8},{8,12},{12,14},{14,10},{10,6},{6,2},{2,0},{1,5},{5,9},... | collective-permute-start | bytes 786440 | tf_op jit(solution)/shard_map/ppermute | solution.py:399
  15.7 0.0 collective-permute-done.3.refs_4_
  15.7 3.9 %collective-permute-done.refs_0_ = bf16[64,2176]{1,0:T(8,128)(2,1)S(1)} collective-permute-done((bf16[64,2176]{1,0:T(8,128)(2,1)S(1)}, bf16[64,2176]{1,0:T(8,128)(2,1)S(1)}, u32[]{:S(2)}, u32[]{:S(2)}) %collective-permute-start) | collective-permute-done | bytes 278560 | tf_op jit(solution)/shard_map/ppermute | solution.py:399
  19.6 2.0 %collective-permute-start.5 = (bf16[64,2176]{1,0:T(8,128)(2,1)S(1)}, bf16[64,2176]{1,0:T(8,128)(2,1)S(1)}, u32[]{:S(2)}, u32[]{:S(2)}) collective-permute-start(bf16[64,2176]{1,0:T(8,128)(2,1)S(1)} %collective-permute-done.refs_0_), channel_id=1, source_target_pairs={{0,4},{4,8},{8,12},{12,14},{14,10},{10,6},{6,2},{2,0},{1,5},{5,9},... | collective-permute-start | bytes 835592 | tf_op jit(solution)/shard_map/ppermute | solution.py:399
  21.7 0.0 collective-permute-done.1.refs_1_
  21.7 3.5 %collective-permute-done.7.refs_2_ = bf16[64,2048]{1,0:T(8,128)(2,1)S(1)} collective-permute-done((bf16[64,2048]{1,0:T(8,128)(2,1)S(1)}, bf16[64,2048]{1,0:T(8,128)(2,1)S(1)}, u32[]{:S(2)}, u32[]{:S(2)}) %collective-permute-start.7) | collective-permute-done | bytes 262176 | tf_op jit(solution)/shard_map/ppermute | solution.py:399
  25.2 2.0 %collective-permute-start.11 = (bf16[64,2048]{1,0:T(8,128)(2,1)S(1)}, bf16[64,2048]{1,0:T(8,128)(2,1)S(1)}, u32[]{:S(2)}, u32[]{:S(2)}) collective-permute-start(bf16[64,2048]{1,0:T(8,128)(2,1)S(1)} %collective-permute-done.7.refs_2_), channel_id=1, source_target_pairs={{0,4},{4,8},{8,12},{12,14},{14,10},{10,6},{6,2},{2,0},{1,5},{5,9},... | collective-permute-start | bytes 786440 | tf_op jit(solution)/shard_map/ppermute | solution.py:399
  27.3 0.0 collective-permute-done.8.refs_3_
  27.4 4.6 %shard_map.113 = (f32[192,2048]{1,0:T(8,128)S(1)}, f32[32,768]{1,0:T(8,128)S(1)}, f32[32,2048]{1,0:T(8,128)S(1)}) custom-call(bf16[64,2176]{1,0:T(8,128)(2,1)S(1)} %collective-permute-done.refs_0_, bf16[64,2176]{1,0:T(8,128)(2,1)S(1)} %collective-permute-done.1.refs_1_, bf16[64,2176]{1,0:T(8,128)(2,1)S(1)} %get-tuple-element.52.refs_2_, ...), custom_call_target="tpu_custom_call" | custom-call | flops 3019898880 | bytes 11599872 | tf_op jit(solution)/shard_map/pallas_call | solution.py:286
  32.0 2.1 %collective-permute-start.9 = (bf16[64,2176]{1,0:T(8,128)(2,1)S(1)}, bf16[64,2176]{1,0:T(8,128)(2,1)S(1)}, u32[]{:S(2)}, u32[]{:S(2)}) collective-permute-start(bf16[64,2176]{1,0:T(8,128)(2,1)S(1)} %collective-permute-done.5.refs_0_), channel_id=1, source_target_pairs={{0,4},{4,8},{8,12},{12,14},{14,10},{10,6},{6,2},{2,0},{1,5},{5,9},... | collective-permute-start | bytes 835592 | tf_op jit(solution)/shard_map/ppermute | solution.py:399
  34.0 1.8 %shard_map.115 = (bf16[1536,1024]{1,0:T(8,128)(2,1)S(1)}, bf16[1536,1024]{1,0:T(8,128)(2,1)S(1)}) custom-call(bf16[1024,2304]{1,0:T(8,128)(2,1)S(1)} %get-tuple-element.55.refs_8_.refs_6_.refs_0_, bf16[1024,2304]{1,0:T(8,128)(2,1)S(1)} %collective-permute-done.4.refs_9_.refs_7_.refs_1_), custom_call_target="tpu_custom_call" | custom-call | tf_op jit(solution)/shard_map/pallas_call | solution.py:270
  35.8 1.0 %collective-permute-done.11.refs_2_.first_ref = bf16[64,2048]{1,0:T(8,128)(2,1)S(1)} collective-permute-done((bf16[64,2048]{1,0:T(8,128)(2,1)S(1)}, bf16[64,2048]{1,0:T(8,128)(2,1)S(1)}, u32[]{:S(2)}, u32[]{:S(2)}) %collective-permute-start.11) | collective-permute-done | bytes 262176 | tf_op jit(solution)/shard_map/ppermute | solution.py:399
  36.8 2.1 %collective-permute-done.12.refs_3_.second_ref = bf16[64,2048]{1,0:T(8,128)(2,1)S(1)} collective-permute-done((bf16[64,2048]{1,0:T(8,128)(2,1)S(1)}, bf16[64,2048]{1,0:T(8,128)(2,1)S(1)}, u32[]{:S(2)}, u32[]{:S(2)}) %collective-permute-start.12) | collective-permute-done | bytes 262176 | tf_op jit(solution)/shard_map/ppermute | solution.py:400
  38.9 1.6 %collective-permute-start.19 = (bf16[32,2048]{1,0:T(8,128)(2,1)S(1)}, bf16[32,2048]{1,0:T(8,128)(2,1)S(1)}, u32[]{:S(2)}, u32[]{:S(2)}) collective-permute-start(bf16[32,2048]{1,0:T(8,128)(2,1)S(1)} %get-tuple-element.84), channel_id=1, source_target_pairs={{0,4},{4,8},{8,12},{12,14},{14,10},{10,6},{6,2},{2,0},{1,5},{5,9},... | collective-permute-start | bytes 393224 | tf_op jit(solution)/shard_map/ppermute | solution.py:418
  40.6 0.4 collective-permute-start.20
  41.0 3.5 %shard_map.114 = (f32[128,2048]{1,0:T(8,128)S(1)}, f32[32,768]{1,0:T(8,128)S(1)}, f32[32,2048]{1,0:T(8,128)S(1)}) custom-call(bf16[64,2176]{1,0:T(8,128)(2,1)S(1)} %collective-permute-done.5.refs_0_, bf16[64,2176]{1,0:T(8,128)(2,1)S(1)} %collective-permute-done.6.refs_1_, bf16[64,2048]{1,0:T(8,128)(2,1)S(1)} %collective-permute-done.7.refs_2_, ...), custom_call_target="tpu_custom_call" | custom-call | flops 2013265920 | bytes 11059200 | tf_op jit(solution)/shard_map/pallas_call | solution.py:286
  44.5 0.4 collective-permute-done.10.refs_1_.second_ref
  44.9 1.6 %collective-permute-start.17 = (bf16[32,2176]{1,0:T(8,128)(2,1)S(1)}, bf16[32,2176]{1,0:T(8,128)(2,1)S(1)}, u32[]{:S(2)}, u32[]{:S(2)}) collective-permute-start(bf16[32,2176]{1,0:T(8,128)(2,1)S(1)} %get-tuple-element.80), channel_id=1, source_target_pairs={{0,4},{4,8},{8,12},{12,14},{14,10},{10,6},{6,2},{2,0},{1,5},{5,9},... | collective-permute-start | bytes 417800 | tf_op jit(solution)/shard_map/ppermute | solution.py:418
  46.5 0.5 collective-permute-start.18
  47.0 2.7 %shard_map.116 = (f32[32,768]{1,0:T(8,128)S(1)}, f32[32,2048]{1,0:T(8,128)S(1)}, bf16[64,2048]{1,0:T(8,128)(2,1)S(1)}, bf16[64,2048]{1,0:T(8,128)(2,1)S(1)}) custom-call(bf16[64,2176]{1,0:T(8,128)(2,1)S(1)} %collective-permute-done.9.refs_0_.first_ref, bf16[64,2176]{1,0:T(8,128)(2,1)S(1)} %collective-permute-done.10.refs_1_.second_ref, ...), custom_call_target="tpu_custom_call" | custom-call | flops 2013265920 | bytes 17350656 | tf_op jit(solution)/shard_map/pallas_call | solution.py:286
  49.7 0.2 collective-permute-start.13
  49.9 1.9 %collective-permute-start.14 = (bf16[64,2048]{1,0:T(8,128)(2,1)S(1)}, bf16[64,2048]{1,0:T(8,128)(2,1)S(1)}, u32[]{:S(2)}, u32[]{:S(2)}) collective-permute-start(bf16[64,2048]{1,0:T(8,128)(2,1)S(1)} %get-tuple-element.75), channel_id=1, source_target_pairs={{0,4},{4,8},{8,12},{12,14},{14,10},{10,6},{6,2},{2,0},{1,5},{5,9},... | collective-permute-start | bytes 786440 | tf_op jit(solution)/shard_map/ppermute | solution.py:379
  51.8 1.0 %collective-permute-done.18.refs_1_ = bf16[32,2176]{1,0:T(8,128)(2,1)S(1)} collective-permute-done((bf16[32,2176]{1,0:T(8,128)(2,1)S(1)}, bf16[32,2176]{1,0:T(8,128)(2,1)S(1)}, u32[]{:S(2)}, u32[]{:S(2)}) %collective-permute-start.18) | collective-permute-done | bytes 139296 | tf_op jit(solution)/shard_map/ppermute | solution.py:419
  52.8 3.1 %shard_map.120 = (f32[32,768]{1,0:T(8,128)S(1)}, f32[32,2048]{1,0:T(8,128)S(1)}, bf16[64,2048]{1,0:T(8,128)(2,1)S(1)}) custom-call(bf16[32,2176]{1,0:T(8,128)(2,1)S(1)} %collective-permute-done.17.refs_0_, bf16[32,2176]{1,0:T(8,128)(2,1)S(1)} %collective-permute-done.18.refs_1_, bf16[32,2048]{1,0:T(8,128)(2,1)S(1)} %collective-permute-done.19.refs_2_, ...), custom_call_target="tpu_custom_call" | custom-call | flops 1006632960 | bytes 16809984 | tf_op jit(solution)/shard_map/pallas_call | solution.py:286
  55.9 2.6 %collective-permute-start.21 = (bf16[64,2048]{1,0:T(8,128)(2,1)S(1)}, bf16[64,2048]{1,0:T(8,128)(2,1)S(1)}, u32[]{:S(2)}, u32[]{:S(2)}) collective-permute-start(bf16[64,2048]{1,0:T(8,128)(2,1)S(1)} %get-tuple-element.88), channel_id=1, source_target_pairs={{0,12},{4,6},{8,10},{12,0},{14,2},{10,8},{6,4},{2,14},{1,13},{5,7}... | collective-permute-start | bytes 786440 | tf_op jit(solution)/shard_map/ppermute | solution.py:435
  58.6 0.5 collective-permute-start.15
  59.1 1.6 %collective-permute-start.16 = (bf16[64,1024]{1,0:T(8,128)(2,1)S(1)}, bf16[64,1024]{1,0:T(8,128)(2,1)S(1)}, u32[]{:S(2)}, u32[]{:S(2)}) collective-permute-start(bf16[64,1024]{1,0:T(8,128)(2,1)S(1)} %get-tuple-element.77), channel_id=1, source_target_pairs={{0,4},{4,8},{8,12},{12,14},{14,10},{10,6},{6,2},{2,0},{1,5},{5,9},... | collective-permute-start | bytes 393224 | tf_op jit(solution)/shard_map/ppermute | solution.py:379
  60.7 1.3 %collective-permute-start.24 = (bf16[64,1024]{1,0:T(8,128)(2,1)S(1)}, bf16[64,1024]{1,0:T(8,128)(2,1)S(1)}, u32[]{:S(2)}, u32[]{:S(2)}) collective-permute-start(bf16[64,1024]{1,0:T(8,128)(2,1)S(1)} %get-tuple-element.91), channel_id=1, source_target_pairs={{4,0},{8,4},{12,8},{14,12},{10,14},{6,10},{2,6},{0,2},{5,1},{9,5},... | collective-permute-start | bytes 393224 | tf_op jit(solution)/shard_map/ppermute | solution.py:379
  62.0 0.8 %collective-permute-start.25 = (bf16[64,1024]{1,0:T(8,128)(2,1)S(1)}, bf16[64,1024]{1,0:T(8,128)(2,1)S(1)}, u32[]{:S(2)}, u32[]{:S(2)}) collective-permute-start(bf16[64,1024]{1,0:T(8,128)(2,1)S(1)} %get-tuple-element.92), channel_id=1, source_target_pairs={{0,4},{4,8},{8,12},{12,14},{14,10},{10,6},{6,2},{2,0},{1,5},{5,9},... | collective-permute-start | bytes 393224 | tf_op jit(solution)/shard_map/ppermute | solution.py:379
  62.8 0.1 shard_map.125
  62.9 4.7 %collective-permute-done.15.refs_1_ = bf16[64,1024]{1,0:T(8,128)(2,1)S(1)} collective-permute-done((bf16[64,1024]{1,0:T(8,128)(2,1)S(1)}, bf16[64,1024]{1,0:T(8,128)(2,1)S(1)}, u32[]{:S(2)}, u32[]{:S(2)}) %collective-permute-start.15) | collective-permute-done | bytes 131104 | tf_op jit(solution)/shard_map/ppermute | solution.py:379
  67.7 0.1 shard_map.121
  67.8 0.8 collective-permute-start.22
  68.6 1.3 %collective-permute-start.23 = (bf16[64,1024]{1,0:T(8,128)(2,1)S(1)}, bf16[64,1024]{1,0:T(8,128)(2,1)S(1)}, u32[]{:S(2)}, u32[]{:S(2)}) collective-permute-start(bf16[64,1024]{1,0:T(8,128)(2,1)S(1)} %get-tuple-element.90), channel_id=1, source_target_pairs={{0,4},{4,8},{8,12},{12,14},{14,10},{10,6},{6,2},{2,0},{1,5},{5,9},... | collective-permute-start | bytes 393224 | tf_op jit(solution)/shard_map/ppermute | solution.py:379
  69.9 0.1 shard_map.123
  70.0 0.8 collective-permute-start.26
  70.8 1.3 %collective-permute-start.27 = (bf16[64,1024]{1,0:T(8,128)(2,1)S(1)}, bf16[64,1024]{1,0:T(8,128)(2,1)S(1)}, u32[]{:S(2)}, u32[]{:S(2)}) collective-permute-start(bf16[64,1024]{1,0:T(8,128)(2,1)S(1)} %get-tuple-element.94), channel_id=1, source_target_pairs={{0,4},{4,8},{8,12},{12,14},{14,10},{10,6},{6,2},{2,0},{1,5},{5,9},... | collective-permute-start | bytes 393224 | tf_op jit(solution)/shard_map/ppermute | solution.py:379
  72.1 0.7 shard_map.126
  72.7 1.4 %collective-permute-done.22.refs_1_ = bf16[64,1024]{1,0:T(8,128)(2,1)S(1)} collective-permute-done((bf16[64,1024]{1,0:T(8,128)(2,1)S(1)}, bf16[64,1024]{1,0:T(8,128)(2,1)S(1)}, u32[]{:S(2)}, u32[]{:S(2)}) %collective-permute-start.22) | collective-permute-done | bytes 131104 | tf_op jit(solution)/shard_map/ppermute | solution.py:379
  74.1 0.8 %collective-permute-done.23.refs_2_ = bf16[64,1024]{1,0:T(8,128)(2,1)S(1)} collective-permute-done((bf16[64,1024]{1,0:T(8,128)(2,1)S(1)}, bf16[64,1024]{1,0:T(8,128)(2,1)S(1)}, u32[]{:S(2)}, u32[]{:S(2)}) %collective-permute-start.23) | collective-permute-done | bytes 131104 | tf_op jit(solution)/shard_map/ppermute | solution.py:379
  74.9 1.6 %collective-permute-done.26.refs_3_ = bf16[64,1024]{1,0:T(8,128)(2,1)S(1)} collective-permute-done((bf16[64,1024]{1,0:T(8,128)(2,1)S(1)}, bf16[64,1024]{1,0:T(8,128)(2,1)S(1)}, u32[]{:S(2)}, u32[]{:S(2)}) %collective-permute-start.26) | collective-permute-done | bytes 131104 | tf_op jit(solution)/shard_map/ppermute | solution.py:379
  76.5 0.1 collective-permute-done.27.refs_4_
  76.6 0.8 %shard_map.124 = bf16[64,2048]{1,0:T(8,128)(2,1)} custom-call(f32[192,2048]{1,0:T(8,128)S(1)} %get-tuple-element.56.refs_0_, bf16[64,1024]{1,0:T(8,128)(2,1)S(1)} %collective-permute-done.22.refs_1_, bf16[64,1024]{1,0:T(8,128)(2,1)S(1)} %collective-permute-done.23.refs_2_, bf16[64,1024]{1,0:T(8,128)(2,1)S(1)} %collective-permute-done.26.refs_3_, ...), custom_call_target="tpu_custom_call" | custom-call | tf_op jit(solution)/shard_map/pallas_call | solution.py:454
  (29 shorter events, 0.2 us)
Async XLA Ops:
  0.6 26.7 %copy-start = (bf16[2,16,2048]{2,1,0:T(8,128)(2,1)S(1)}, bf16[2,16,2048]{2,1,0:T(8,128)(2,1)}, u32[]{:S(2)}) copy-start(bf16[2,16,2048]{2,1,0:T(8,128)(2,1)} %param.17) | copy-start | bytes 393220
  3.4 23.9 %collective-permute-start.4 = (bf16[1024,2304]{1,0:T(8,128)(2,1)S(1)}, bf16[1024,2304]{1,0:T(8,128)(2,1)S(1)}, u32[]{:S(2)}, u32[]{:S(2)}) collective-permute-start(bf16[1024,2304]{1,0:T(8,128)(2,1)S(1)} %get-tuple-element.55.refs_8_.refs_6_.refs_0_), channel_id=1, source_target_pairs={{0,1},{1,0},{2,3},{3,2},{4,5},{5,4},{6,7},{7,6},{8,9},{9,8},{10,11... | collective-permute-start | bytes 14155784 | tf_op jit(solution)/shard_map/ppermute | solution.py:360
  3.9 9.7 %collective-permute-start.2 = (bf16[64,2048]{1,0:T(8,128)(2,1)S(1)}, bf16[64,2048]{1,0:T(8,128)(2,1)S(1)}, u32[]{:S(2)}, u32[]{:S(2)}) collective-permute-start(bf16[64,2048]{1,0:T(8,128)(2,1)S(1)} %get-tuple-element.53.refs_5_), channel_id=1, source_target_pairs={{0,4},{4,8},{8,12},{12,14},{14,10},{10,6},{6,2},{2,0},{1,5},{5,9},... | collective-permute-start | bytes 786440 | tf_op jit(solution)/shard_map/ppermute | solution.py:399
  6.6 9.1 %collective-permute-start.3 = (bf16[64,2048]{1,0:T(8,128)(2,1)S(1)}, bf16[64,2048]{1,0:T(8,128)(2,1)S(1)}, u32[]{:S(2)}, u32[]{:S(2)}) collective-permute-start(bf16[64,2048]{1,0:T(8,128)(2,1)S(1)} %get-tuple-element.53.refs_5_), channel_id=1, source_target_pairs={{4,0},{8,4},{12,8},{14,12},{10,14},{6,10},{2,6},{0,2},{5,1},{9,5},... | collective-permute-start | bytes 786440 | tf_op jit(solution)/shard_map/ppermute | solution.py:400
  6.6 13.0 %collective-permute-start = (bf16[64,2176]{1,0:T(8,128)(2,1)S(1)}, bf16[64,2176]{1,0:T(8,128)(2,1)S(1)}, u32[]{:S(2)}, u32[]{:S(2)}) collective-permute-start(bf16[64,2176]{1,0:T(8,128)(2,1)S(1)} %get-tuple-element.52.refs_2_), channel_id=1, source_target_pairs={{0,4},{4,8},{8,12},{12,14},{14,10},{10,6},{6,2},{2,0},{1,5},{5,9},... | collective-permute-start | bytes 835592 | tf_op jit(solution)/shard_map/ppermute | solution.py:399
  8.6 13.1 %collective-permute-start.1 = (bf16[64,2176]{1,0:T(8,128)(2,1)S(1)}, bf16[64,2176]{1,0:T(8,128)(2,1)S(1)}, u32[]{:S(2)}, u32[]{:S(2)}) collective-permute-start(bf16[64,2176]{1,0:T(8,128)(2,1)S(1)} %get-tuple-element.52.refs_2_), channel_id=1, source_target_pairs={{4,0},{8,4},{12,8},{14,12},{10,14},{6,10},{2,6},{0,2},{5,1},{9,5},... | collective-permute-start | bytes 835592 | tf_op jit(solution)/shard_map/ppermute | solution.py:400
  13.7 11.6 %collective-permute-start.7 = (bf16[64,2048]{1,0:T(8,128)(2,1)S(1)}, bf16[64,2048]{1,0:T(8,128)(2,1)S(1)}, u32[]{:S(2)}, u32[]{:S(2)}) collective-permute-start(bf16[64,2048]{1,0:T(8,128)(2,1)S(1)} %collective-permute-done.2.refs_3_), channel_id=1, source_target_pairs={{0,4},{4,8},{8,12},{12,14},{14,10},{10,6},{6,2},{2,0},{1,5},{5,9},... | collective-permute-start | bytes 786440 | tf_op jit(solution)/shard_map/ppermute | solution.py:399
  15.7 11.6 %collective-permute-start.8 = (bf16[64,2048]{1,0:T(8,128)(2,1)S(1)}, bf16[64,2048]{1,0:T(8,128)(2,1)S(1)}, u32[]{:S(2)}, u32[]{:S(2)}) collective-permute-start(bf16[64,2048]{1,0:T(8,128)(2,1)S(1)} %collective-permute-done.3.refs_4_), channel_id=1, source_target_pairs={{4,0},{8,4},{12,8},{14,12},{10,14},{6,10},{2,6},{0,2},{5,1},{9,5},... | collective-permute-start | bytes 786440 | tf_op jit(solution)/shard_map/ppermute | solution.py:400
  19.6 12.3 %collective-permute-start.5 = (bf16[64,2176]{1,0:T(8,128)(2,1)S(1)}, bf16[64,2176]{1,0:T(8,128)(2,1)S(1)}, u32[]{:S(2)}, u32[]{:S(2)}) collective-permute-start(bf16[64,2176]{1,0:T(8,128)(2,1)S(1)} %collective-permute-done.refs_0_), channel_id=1, source_target_pairs={{0,4},{4,8},{8,12},{12,14},{14,10},{10,6},{6,2},{2,0},{1,5},{5,9},... | collective-permute-start | bytes 835592 | tf_op jit(solution)/shard_map/ppermute | solution.py:399
  21.7 12.3 %collective-permute-start.6 = (bf16[64,2176]{1,0:T(8,128)(2,1)S(1)}, bf16[64,2176]{1,0:T(8,128)(2,1)S(1)}, u32[]{:S(2)}, u32[]{:S(2)}) collective-permute-start(bf16[64,2176]{1,0:T(8,128)(2,1)S(1)} %collective-permute-done.1.refs_1_), channel_id=1, source_target_pairs={{4,0},{8,4},{12,8},{14,12},{10,14},{6,10},{2,6},{0,2},{5,1},{9,5},... | collective-permute-start | bytes 835592 | tf_op jit(solution)/shard_map/ppermute | solution.py:400
  25.2 11.6 %collective-permute-start.11 = (bf16[64,2048]{1,0:T(8,128)(2,1)S(1)}, bf16[64,2048]{1,0:T(8,128)(2,1)S(1)}, u32[]{:S(2)}, u32[]{:S(2)}) collective-permute-start(bf16[64,2048]{1,0:T(8,128)(2,1)S(1)} %collective-permute-done.7.refs_2_), channel_id=1, source_target_pairs={{0,4},{4,8},{8,12},{12,14},{14,10},{10,6},{6,2},{2,0},{1,5},{5,9},... | collective-permute-start | bytes 786440 | tf_op jit(solution)/shard_map/ppermute | solution.py:399
  27.3 11.6 %collective-permute-start.12 = (bf16[64,2048]{1,0:T(8,128)(2,1)S(1)}, bf16[64,2048]{1,0:T(8,128)(2,1)S(1)}, u32[]{:S(2)}, u32[]{:S(2)}) collective-permute-start(bf16[64,2048]{1,0:T(8,128)(2,1)S(1)} %collective-permute-done.8.refs_3_), channel_id=1, source_target_pairs={{4,0},{8,4},{12,8},{14,12},{10,14},{6,10},{2,6},{0,2},{5,1},{9,5},... | collective-permute-start | bytes 786440 | tf_op jit(solution)/shard_map/ppermute | solution.py:400
  32.0 12.5 %collective-permute-start.9 = (bf16[64,2176]{1,0:T(8,128)(2,1)S(1)}, bf16[64,2176]{1,0:T(8,128)(2,1)S(1)}, u32[]{:S(2)}, u32[]{:S(2)}) collective-permute-start(bf16[64,2176]{1,0:T(8,128)(2,1)S(1)} %collective-permute-done.5.refs_0_), channel_id=1, source_target_pairs={{0,4},{4,8},{8,12},{12,14},{14,10},{10,6},{6,2},{2,0},{1,5},{5,9},... | collective-permute-start | bytes 835592 | tf_op jit(solution)/shard_map/ppermute | solution.py:399
  34.0 10.8 %collective-permute-start.10 = (bf16[64,2176]{1,0:T(8,128)(2,1)S(1)}, bf16[64,2176]{1,0:T(8,128)(2,1)S(1)}, u32[]{:S(2)}, u32[]{:S(2)}) collective-permute-start(bf16[64,2176]{1,0:T(8,128)(2,1)S(1)} %collective-permute-done.6.refs_1_), channel_id=1, source_target_pairs={{4,0},{8,4},{12,8},{14,12},{10,14},{6,10},{2,6},{0,2},{5,1},{9,5},... | collective-permute-start | bytes 835592 | tf_op jit(solution)/shard_map/ppermute | solution.py:400
  38.9 11.0 %collective-permute-start.19 = (bf16[32,2048]{1,0:T(8,128)(2,1)S(1)}, bf16[32,2048]{1,0:T(8,128)(2,1)S(1)}, u32[]{:S(2)}, u32[]{:S(2)}) collective-permute-start(bf16[32,2048]{1,0:T(8,128)(2,1)S(1)} %get-tuple-element.84), channel_id=1, source_target_pairs={{0,4},{4,8},{8,12},{12,14},{14,10},{10,6},{6,2},{2,0},{1,5},{5,9},... | collective-permute-start | bytes 393224 | tf_op jit(solution)/shard_map/ppermute | solution.py:418
  40.6 11.2 %collective-permute-start.20 = (bf16[32,2048]{1,0:T(8,128)(2,1)S(1)}, bf16[32,2048]{1,0:T(8,128)(2,1)S(1)}, u32[]{:S(2)}, u32[]{:S(2)}) collective-permute-start(bf16[32,2048]{1,0:T(8,128)(2,1)S(1)} %get-tuple-element.85), channel_id=1, source_target_pairs={{4,0},{8,4},{12,8},{14,12},{10,14},{6,10},{2,6},{0,2},{5,1},{9,5},... | collective-permute-start | bytes 393224 | tf_op jit(solution)/shard_map/ppermute | solution.py:419
  44.9 6.9 %collective-permute-start.17 = (bf16[32,2176]{1,0:T(8,128)(2,1)S(1)}, bf16[32,2176]{1,0:T(8,128)(2,1)S(1)}, u32[]{:S(2)}, u32[]{:S(2)}) collective-permute-start(bf16[32,2176]{1,0:T(8,128)(2,1)S(1)} %get-tuple-element.80), channel_id=1, source_target_pairs={{0,4},{4,8},{8,12},{12,14},{14,10},{10,6},{6,2},{2,0},{1,5},{5,9},... | collective-permute-start | bytes 417800 | tf_op jit(solution)/shard_map/ppermute | solution.py:418
  46.5 6.3 %collective-permute-start.18 = (bf16[32,2176]{1,0:T(8,128)(2,1)S(1)}, bf16[32,2176]{1,0:T(8,128)(2,1)S(1)}, u32[]{:S(2)}, u32[]{:S(2)}) collective-permute-start(bf16[32,2176]{1,0:T(8,128)(2,1)S(1)} %get-tuple-element.81), channel_id=1, source_target_pairs={{4,0},{8,4},{12,8},{14,12},{10,14},{6,10},{2,6},{0,2},{5,1},{9,5},... | collective-permute-start | bytes 417800 | tf_op jit(solution)/shard_map/ppermute | solution.py:419
  49.7 8.8 %collective-permute-start.13 = (bf16[64,2048]{1,0:T(8,128)(2,1)S(1)}, bf16[64,2048]{1,0:T(8,128)(2,1)S(1)}, u32[]{:S(2)}, u32[]{:S(2)}) collective-permute-start(bf16[64,2048]{1,0:T(8,128)(2,1)S(1)} %get-tuple-element.74), channel_id=1, source_target_pairs={{4,0},{8,4},{12,8},{14,12},{10,14},{6,10},{2,6},{0,2},{5,1},{9,5},... | collective-permute-start | bytes 786440 | tf_op jit(solution)/shard_map/ppermute | solution.py:379
  49.9 8.6 %collective-permute-start.14 = (bf16[64,2048]{1,0:T(8,128)(2,1)S(1)}, bf16[64,2048]{1,0:T(8,128)(2,1)S(1)}, u32[]{:S(2)}, u32[]{:S(2)}) collective-permute-start(bf16[64,2048]{1,0:T(8,128)(2,1)S(1)} %get-tuple-element.75), channel_id=1, source_target_pairs={{0,4},{4,8},{8,12},{12,14},{14,10},{10,6},{6,2},{2,0},{1,5},{5,9},... | collective-permute-start | bytes 786440 | tf_op jit(solution)/shard_map/ppermute | solution.py:379
  55.9 11.7 %collective-permute-start.21 = (bf16[64,2048]{1,0:T(8,128)(2,1)S(1)}, bf16[64,2048]{1,0:T(8,128)(2,1)S(1)}, u32[]{:S(2)}, u32[]{:S(2)}) collective-permute-start(bf16[64,2048]{1,0:T(8,128)(2,1)S(1)} %get-tuple-element.88), channel_id=1, source_target_pairs={{0,12},{4,6},{8,10},{12,0},{14,2},{10,8},{6,4},{2,14},{1,13},{5,7}... | collective-permute-start | bytes 786440 | tf_op jit(solution)/shard_map/ppermute | solution.py:435
  58.6 9.1 %collective-permute-start.15 = (bf16[64,1024]{1,0:T(8,128)(2,1)S(1)}, bf16[64,1024]{1,0:T(8,128)(2,1)S(1)}, u32[]{:S(2)}, u32[]{:S(2)}) collective-permute-start(bf16[64,1024]{1,0:T(8,128)(2,1)S(1)} %get-tuple-element.76), channel_id=1, source_target_pairs={{4,0},{8,4},{12,8},{14,12},{10,14},{6,10},{2,6},{0,2},{5,1},{9,5},... | collective-permute-start | bytes 393224 | tf_op jit(solution)/shard_map/ppermute | solution.py:379
  59.1 8.6 %collective-permute-start.16 = (bf16[64,1024]{1,0:T(8,128)(2,1)S(1)}, bf16[64,1024]{1,0:T(8,128)(2,1)S(1)}, u32[]{:S(2)}, u32[]{:S(2)}) collective-permute-start(bf16[64,1024]{1,0:T(8,128)(2,1)S(1)} %get-tuple-element.77), channel_id=1, source_target_pairs={{0,4},{4,8},{8,12},{12,14},{14,10},{10,6},{6,2},{2,0},{1,5},{5,9},... | collective-permute-start | bytes 393224 | tf_op jit(solution)/shard_map/ppermute | solution.py:379
  60.7 9.1 %collective-permute-start.24 = (bf16[64,1024]{1,0:T(8,128)(2,1)S(1)}, bf16[64,1024]{1,0:T(8,128)(2,1)S(1)}, u32[]{:S(2)}, u32[]{:S(2)}) collective-permute-start(bf16[64,1024]{1,0:T(8,128)(2,1)S(1)} %get-tuple-element.91), channel_id=1, source_target_pairs={{4,0},{8,4},{12,8},{14,12},{10,14},{6,10},{2,6},{0,2},{5,1},{9,5},... | collective-permute-start | bytes 393224 | tf_op jit(solution)/shard_map/ppermute | solution.py:379
  62.0 7.9 %collective-permute-start.25 = (bf16[64,1024]{1,0:T(8,128)(2,1)S(1)}, bf16[64,1024]{1,0:T(8,128)(2,1)S(1)}, u32[]{:S(2)}, u32[]{:S(2)}) collective-permute-start(bf16[64,1024]{1,0:T(8,128)(2,1)S(1)} %get-tuple-element.92), channel_id=1, source_target_pairs={{0,4},{4,8},{8,12},{12,14},{14,10},{10,6},{6,2},{2,0},{1,5},{5,9},... | collective-permute-start | bytes 393224 | tf_op jit(solution)/shard_map/ppermute | solution.py:379
  67.7 4.4 %collective-permute-start.28 = (f32[32,1216]{1,0:T(8,128)S(1)}, f32[32,1216]{1,0:T(8,128)S(1)}, u32[]{:S(2)}, u32[]{:S(2)}) collective-permute-start(f32[32,1216]{1,0:T(8,128)S(1)} %get-tuple-element.98), channel_id=1, source_target_pairs={{0,1},{1,0},{2,3},{3,2},{4,5},{5,4},{6,7},{7,6},{8,9},{9,8},{10,11... | collective-permute-start | bytes 466952 | tf_op jit(solution)/shard_map/ppermute | solution.py:468
  67.8 6.3 %collective-permute-start.22 = (bf16[64,1024]{1,0:T(8,128)(2,1)S(1)}, bf16[64,1024]{1,0:T(8,128)(2,1)S(1)}, u32[]{:S(2)}, u32[]{:S(2)}) collective-permute-start(bf16[64,1024]{1,0:T(8,128)(2,1)S(1)} %get-tuple-element.89), channel_id=1, source_target_pairs={{4,0},{8,4},{12,8},{14,12},{10,14},{6,10},{2,6},{0,2},{5,1},{9,5},... | collective-permute-start | bytes 393224 | tf_op jit(solution)/shard_map/ppermute | solution.py:379
  68.6 6.4 %collective-permute-start.23 = (bf16[64,1024]{1,0:T(8,128)(2,1)S(1)}, bf16[64,1024]{1,0:T(8,128)(2,1)S(1)}, u32[]{:S(2)}, u32[]{:S(2)}) collective-permute-start(bf16[64,1024]{1,0:T(8,128)(2,1)S(1)} %get-tuple-element.90), channel_id=1, source_target_pairs={{0,4},{4,8},{8,12},{12,14},{14,10},{10,6},{6,2},{2,0},{1,5},{5,9},... | collective-permute-start | bytes 393224 | tf_op jit(solution)/shard_map/ppermute | solution.py:379
  70.0 6.6 %collective-permute-start.26 = (bf16[64,1024]{1,0:T(8,128)(2,1)S(1)}, bf16[64,1024]{1,0:T(8,128)(2,1)S(1)}, u32[]{:S(2)}, u32[]{:S(2)}) collective-permute-start(bf16[64,1024]{1,0:T(8,128)(2,1)S(1)} %get-tuple-element.93), channel_id=1, source_target_pairs={{4,0},{8,4},{12,8},{14,12},{10,14},{6,10},{2,6},{0,2},{5,1},{9,5},... | collective-permute-start | bytes 393224 | tf_op jit(solution)/shard_map/ppermute | solution.py:379
  70.8 5.9 %collective-permute-start.27 = (bf16[64,1024]{1,0:T(8,128)(2,1)S(1)}, bf16[64,1024]{1,0:T(8,128)(2,1)S(1)}, u32[]{:S(2)}, u32[]{:S(2)}) collective-permute-start(bf16[64,1024]{1,0:T(8,128)(2,1)S(1)} %get-tuple-element.94), channel_id=1, source_target_pairs={{0,4},{4,8},{8,12},{12,14},{14,10},{10,6},{6,2},{2,0},{1,5},{5,9},... | collective-permute-start | bytes 393224 | tf_op jit(solution)/shard_map/ppermute | solution.py:379

commit v14 on v13

--- a/solution.py
+++ b/solution.py
@@ -427,12 +427,14 @@
             moving[side, way] = send(value, way) if side == "left" else moving["left", way]
     skipped = []
     if split:
-        *totals, value = run(far, [(0, everything)], totals, keep_rows=False, turned=turned)
+        blocks = [(0, span) for span in columns.values()]
+        outs = run(far, blocks, totals, keep_rows=False, turned=turned)
+        totals = outs[:2]
         pairs = [
             (order[i], order[(i + (full if i % 2 == 0 else -full)) % peer_count])
             for i in range(peer_count)
         ]
-        skipped.append(lax.ppermute(value, "expert", pairs))
+        skipped = [lax.ppermute(value, "expert", pairs) for value in outs[2:]]
 
     def goes_ahead():
         me = lax.axis_index("expert")
@@ -440,14 +442,14 @@
         return (place + full) % 2 == 0
 
     for d in range(full - 1, 0, -1):
-        for side, span in columns.items():
+        for at, (side, span) in enumerate(columns.items()):
             blocks, arrived = [], []
             for way, (first_row, _) in ways.items():
                 blocks.append((first_row, span, span if d == full - 1 else slice(0, middle), way))
                 arrived.append(moving[side, way])
-            skip = (goes_ahead, span) if d == 1 and split else None
+            skip = (goes_ahead, slice(0, middle)) if d == 1 and split else None
             values = add_sums(
-                rows_at[d], token_count, blocks, arrived + (skipped if skip else []), skip
+                rows_at[d], token_count, blocks, arrived + (skipped[at : at + 1] if skip else []), skip
             )
             for way, value in zip(ways, values):
                 moving[side, way] = send(value, way)

time: 77.5 us -> 77.6 us (level)
  starting transfers between devices: 30.5 us -> 31.9 us
  waiting for transfers between devices: 25.7 us -> 24.4 us
    ppermute x1 -> x2, starting transfers between devices: 2.6 us -> 5.01 us  [per_device(): skipped = [lax.ppermute(value, 'expert', pairs) for value in outs[2:]]]
    ppermute x10, waiting for transfers between devices: 8.6 us -> 6.26 us  [send(): return lax.ppermute(value, 'expert', ways[way][1])]
    ppermute x1 -> x2, waiting for transfers between devices: 0.01 us -> 1.04 us  [per_device(): skipped = [lax.ppermute(value, 'expert', pairs) for value in outs[2:]]]
    ppermute x10, starting transfers between devices: 10.4 us -> 9.38 us  [send(): return lax.ppermute(value, 'expert', ways[way][1])]
  transfers between devices with their start and end apart: 29 -> 30, of which waited for: 12 -> 15; matrix products, arithmetic and copies ran while one was open for 0% -> 0% of each run, Pallas kernels for 22% -> 22%
where the time goes in v14:
time: 77.6 us; the launch traced here: 77.5 us
  starting transfers between devices  31.9 us (41%)
  waiting for transfers between devices  24.4 us (31%)
  Pallas kernels  20.4 us (26%)
    ppermute x8, starting transfers between devices, per_device(): lax.ppermute(x, 'expert', forward)  16.1 us
    pallas_call x4, Pallas kernels, expert_call(): pl.pallas_call(functools.partial(whole_kernel, plan, len(pieces), blocks,...  13.9 us
    ppermute x8, waiting for transfers between devices, per_device(): lax.ppermute(x, 'expert', forward)  13.5 us
    ppermute x10, starting transfers between devices, send(): return lax.ppermute(value, 'expert', ways[way][1])  9.38 us
    ppermute x10, waiting for transfers between devices, send(): return lax.ppermute(value, 'expert', ways[way][1])  6.26 us
    ppermute x2, starting transfers between devices, per_device(): skipped = [lax.ppermute(value, 'expert', pairs) for value in outs[2:]]  5.01 us
    pallas_call x1, Pallas kernels, per_device(): pl.pallas_call(functools.partial(prepare_kernel, plan), out_shape=(jax.Sh...  2.78 us
    pallas_call x5, Pallas kernels, simple_call(): pl.pallas_call(kernel, out_shape=tuple((jax.ShapeDtypeStruct(shape, dtype...  2.64 us
  transfers between devices with their start and end apart: 30, of which 15 were waited for; matrix products, arithmetic and copies ran while one was open for 0% of the time, Pallas kernels for 22%

profile of v14, /device:TPU:0, one launch (start us, length us, event | category | flops | bytes accessed | tf_op | source)
XLA Modules:
  0.0 77.5 jit_solution(12817622663004082483)
XLA Ops:
  0.6 2.8 %shard_map.112 = (bf16[1024,2304]{1,0:T(8,128)(2,1)S(1)}, bf16[64,2048]{1,0:T(8,128)(2,1)S(1)}, bf16[64,2176]{1,0:T(8,128)(2,1)S(1)}, bf16[32,768]{1,0:T(8,128)(2,1)S(1)}) custom-call(bf16[2,1024,384]{2,1,0:T(8,128)(2,1)} %refs_0_.1, bf16[2,1024,384]{2,1,0:T(8,128)(2,1)} %refs_1_.1, bf16[2,1024,384]{2,1,0:T(8,128)(2,1)} %refs_2_.1, ...), custom_call_target="tpu_custom_call" | custom-call | tf_op jit(solution)/shard_map/pallas_call | solution.py:328
  3.4 0.5 collective-permute-start.4
  3.9 2.6 %collective-permute-start.2 = (bf16[64,2048]{1,0:T(8,128)(2,1)S(1)}, bf16[64,2048]{1,0:T(8,128)(2,1)S(1)}, u32[]{:S(2)}, u32[]{:S(2)}) collective-permute-start(bf16[64,2048]{1,0:T(8,128)(2,1)S(1)} %get-tuple-element.54.refs_5_), channel_id=1, source_target_pairs={{0,4},{4,8},{8,12},{12,14},{14,10},{10,6},{6,2},{2,0},{1,5},{5,9},... | collective-permute-start | bytes 786440 | tf_op jit(solution)/shard_map/ppermute | solution.py:399
  6.6 2.0 %collective-permute-start = (bf16[64,2176]{1,0:T(8,128)(2,1)S(1)}, bf16[64,2176]{1,0:T(8,128)(2,1)S(1)}, u32[]{:S(2)}, u32[]{:S(2)}) collective-permute-start(bf16[64,2176]{1,0:T(8,128)(2,1)S(1)} %get-tuple-element.53.refs_2_), channel_id=1, source_target_pairs={{0,4},{4,8},{8,12},{12,14},{14,10},{10,6},{6,2},{2,0},{1,5},{5,9},... | collective-permute-start | bytes 835592 | tf_op jit(solution)/shard_map/ppermute | solution.py:399
  8.6 5.0 %collective-permute-done.2.refs_3_ = bf16[64,2048]{1,0:T(8,128)(2,1)S(1)} collective-permute-done((bf16[64,2048]{1,0:T(8,128)(2,1)S(1)}, bf16[64,2048]{1,0:T(8,128)(2,1)S(1)}, u32[]{:S(2)}, u32[]{:S(2)}) %collective-permute-start.2) | collective-permute-done | bytes 262176 | tf_op jit(solution)/shard_map/ppermute | solution.py:399
  13.7 2.0 %collective-permute-start.7 = (bf16[64,2048]{1,0:T(8,128)(2,1)S(1)}, bf16[64,2048]{1,0:T(8,128)(2,1)S(1)}, u32[]{:S(2)}, u32[]{:S(2)}) collective-permute-start(bf16[64,2048]{1,0:T(8,128)(2,1)S(1)} %collective-permute-done.2.refs_3_), channel_id=1, source_target_pairs={{0,4},{4,8},{8,12},{12,14},{14,10},{10,6},{6,2},{2,0},{1,5},{5,9},... | collective-permute-start | bytes 786440 | tf_op jit(solution)/shard_map/ppermute | solution.py:399
  15.7 3.9 %collective-permute-done.refs_0_ = bf16[64,2176]{1,0:T(8,128)(2,1)S(1)} collective-permute-done((bf16[64,2176]{1,0:T(8,128)(2,1)S(1)}, bf16[64,2176]{1,0:T(8,128)(2,1)S(1)}, u32[]{:S(2)}, u32[]{:S(2)}) %collective-permute-start) | collective-permute-done | bytes 278560 | tf_op jit(solution)/shard_map/ppermute | solution.py:399
  19.6 2.0 %collective-permute-start.5 = (bf16[64,2176]{1,0:T(8,128)(2,1)S(1)}, bf16[64,2176]{1,0:T(8,128)(2,1)S(1)}, u32[]{:S(2)}, u32[]{:S(2)}) collective-permute-start(bf16[64,2176]{1,0:T(8,128)(2,1)S(1)} %collective-permute-done.refs_0_), channel_id=1, source_target_pairs={{0,4},{4,8},{8,12},{12,14},{14,10},{10,6},{6,2},{2,0},{1,5},{5,9},... | collective-permute-start | bytes 835592 | tf_op jit(solution)/shard_map/ppermute | solution.py:399
  21.7 3.5 %collective-permute-done.7.refs_2_ = bf16[64,2048]{1,0:T(8,128)(2,1)S(1)} collective-permute-done((bf16[64,2048]{1,0:T(8,128)(2,1)S(1)}, bf16[64,2048]{1,0:T(8,128)(2,1)S(1)}, u32[]{:S(2)}, u32[]{:S(2)}) %collective-permute-start.7) | collective-permute-done | bytes 262176 | tf_op jit(solution)/shard_map/ppermute | solution.py:399
  25.2 2.0 %collective-permute-start.11 = (bf16[64,2048]{1,0:T(8,128)(2,1)S(1)}, bf16[64,2048]{1,0:T(8,128)(2,1)S(1)}, u32[]{:S(2)}, u32[]{:S(2)}) collective-permute-start(bf16[64,2048]{1,0:T(8,128)(2,1)S(1)} %collective-permute-done.7.refs_2_), channel_id=1, source_target_pairs={{0,4},{4,8},{8,12},{12,14},{14,10},{10,6},{6,2},{2,0},{1,5},{5,9},... | collective-permute-start | bytes 786440 | tf_op jit(solution)/shard_map/ppermute | solution.py:399
  27.4 4.6 %shard_map.113 = (f32[192,2048]{1,0:T(8,128)S(1)}, f32[32,768]{1,0:T(8,128)S(1)}, f32[32,2048]{1,0:T(8,128)S(1)}) custom-call(bf16[64,2176]{1,0:T(8,128)(2,1)S(1)} %collective-permute-done.refs_0_, bf16[64,2176]{1,0:T(8,128)(2,1)S(1)} %collective-permute-done.1.refs_1_, bf16[64,2176]{1,0:T(8,128)(2,1)S(1)} %get-tuple-element.53.refs_2_, ...), custom_call_target="tpu_custom_call" | custom-call | flops 3019898880 | bytes 11599872 | tf_op jit(solution)/shard_map/pallas_call | solution.py:286
  32.0 2.1 %collective-permute-start.9 = (bf16[64,2176]{1,0:T(8,128)(2,1)S(1)}, bf16[64,2176]{1,0:T(8,128)(2,1)S(1)}, u32[]{:S(2)}, u32[]{:S(2)}) collective-permute-start(bf16[64,2176]{1,0:T(8,128)(2,1)S(1)} %collective-permute-done.5.refs_0_), channel_id=1, source_target_pairs={{0,4},{4,8},{8,12},{12,14},{14,10},{10,6},{6,2},{2,0},{1,5},{5,9},... | collective-permute-start | bytes 835592 | tf_op jit(solution)/shard_map/ppermute | solution.py:399
  34.0 1.8 %shard_map.115 = (bf16[1536,1024]{1,0:T(8,128)(2,1)S(1)}, bf16[1536,1024]{1,0:T(8,128)(2,1)S(1)}) custom-call(bf16[1024,2304]{1,0:T(8,128)(2,1)S(1)} %get-tuple-element.56.refs_8_.refs_6_.refs_0_, bf16[1024,2304]{1,0:T(8,128)(2,1)S(1)} %collective-permute-done.4.refs_9_.refs_7_.refs_1_), custom_call_target="tpu_custom_call" | custom-call | tf_op jit(solution)/shard_map/pallas_call | solution.py:270
  35.8 1.0 %collective-permute-done.11.refs_2_.first_ref = bf16[64,2048]{1,0:T(8,128)(2,1)S(1)} collective-permute-done((bf16[64,2048]{1,0:T(8,128)(2,1)S(1)}, bf16[64,2048]{1,0:T(8,128)(2,1)S(1)}, u32[]{:S(2)}, u32[]{:S(2)}) %collective-permute-start.11) | collective-permute-done | bytes 262176 | tf_op jit(solution)/shard_map/ppermute | solution.py:399
  36.8 2.1 %collective-permute-done.12.refs_3_.second_ref = bf16[64,2048]{1,0:T(8,128)(2,1)S(1)} collective-permute-done((bf16[64,2048]{1,0:T(8,128)(2,1)S(1)}, bf16[64,2048]{1,0:T(8,128)(2,1)S(1)}, u32[]{:S(2)}, u32[]{:S(2)}) %collective-permute-start.12) | collective-permute-done | bytes 262176 | tf_op jit(solution)/shard_map/ppermute | solution.py:400
  38.9 1.6 %collective-permute-start.19 = (bf16[32,2048]{1,0:T(8,128)(2,1)S(1)}, bf16[32,2048]{1,0:T(8,128)(2,1)S(1)}, u32[]{:S(2)}, u32[]{:S(2)}) collective-permute-start(bf16[32,2048]{1,0:T(8,128)(2,1)S(1)} %get-tuple-element.85), channel_id=1, source_target_pairs={{0,4},{4,8},{8,12},{12,14},{14,10},{10,6},{6,2},{2,0},{1,5},{5,9},... | collective-permute-start | bytes 393224 | tf_op jit(solution)/shard_map/ppermute | solution.py:418
  40.6 0.4 collective-permute-start.20
  41.0 3.5 %shard_map.114 = (f32[128,2048]{1,0:T(8,128)S(1)}, f32[32,768]{1,0:T(8,128)S(1)}, f32[32,2048]{1,0:T(8,128)S(1)}) custom-call(bf16[64,2176]{1,0:T(8,128)(2,1)S(1)} %collective-permute-done.5.refs_0_, bf16[64,2176]{1,0:T(8,128)(2,1)S(1)} %collective-permute-done.6.refs_1_, bf16[64,2048]{1,0:T(8,128)(2,1)S(1)} %collective-permute-done.7.refs_2_, ...), custom_call_target="tpu_custom_call" | custom-call | flops 2013265920 | bytes 11059200 | tf_op jit(solution)/shard_map/pallas_call | solution.py:286
  44.5 0.4 collective-permute-done.10.refs_1_.second_ref
  44.9 1.6 %collective-permute-start.17 = (bf16[32,2176]{1,0:T(8,128)(2,1)S(1)}, bf16[32,2176]{1,0:T(8,128)(2,1)S(1)}, u32[]{:S(2)}, u32[]{:S(2)}) collective-permute-start(bf16[32,2176]{1,0:T(8,128)(2,1)S(1)} %get-tuple-element.81), channel_id=1, source_target_pairs={{0,4},{4,8},{8,12},{12,14},{14,10},{10,6},{6,2},{2,0},{1,5},{5,9},... | collective-permute-start | bytes 417800 | tf_op jit(solution)/shard_map/ppermute | solution.py:418
  46.5 0.5 collective-permute-start.18
  47.0 2.7 %shard_map.116 = (f32[32,768]{1,0:T(8,128)S(1)}, f32[32,2048]{1,0:T(8,128)S(1)}, bf16[64,2048]{1,0:T(8,128)(2,1)S(1)}, bf16[64,2048]{1,0:T(8,128)(2,1)S(1)}) custom-call(bf16[64,2176]{1,0:T(8,128)(2,1)S(1)} %collective-permute-done.9.refs_0_.first_ref, bf16[64,2176]{1,0:T(8,128)(2,1)S(1)} %collective-permute-done.10.refs_1_.second_ref, ...), custom_call_target="tpu_custom_call" | custom-call | flops 2013265920 | bytes 17350656 | tf_op jit(solution)/shard_map/pallas_call | solution.py:286
  49.7 0.2 collective-permute-start.13
  49.9 1.9 %collective-permute-start.14 = (bf16[64,2048]{1,0:T(8,128)(2,1)S(1)}, bf16[64,2048]{1,0:T(8,128)(2,1)S(1)}, u32[]{:S(2)}, u32[]{:S(2)}) collective-permute-start(bf16[64,2048]{1,0:T(8,128)(2,1)S(1)} %get-tuple-element.76), channel_id=1, source_target_pairs={{0,4},{4,8},{8,12},{12,14},{14,10},{10,6},{6,2},{2,0},{1,5},{5,9},... | collective-permute-start | bytes 786440 | tf_op jit(solution)/shard_map/ppermute | solution.py:379
  51.8 1.0 %collective-permute-done.18.refs_1_ = bf16[32,2176]{1,0:T(8,128)(2,1)S(1)} collective-permute-done((bf16[32,2176]{1,0:T(8,128)(2,1)S(1)}, bf16[32,2176]{1,0:T(8,128)(2,1)S(1)}, u32[]{:S(2)}, u32[]{:S(2)}) %collective-permute-start.18) | collective-permute-done | bytes 139296 | tf_op jit(solution)/shard_map/ppermute | solution.py:419
  52.8 3.1 %shard_map.120 = (f32[32,768]{1,0:T(8,128)S(1)}, f32[32,2048]{1,0:T(8,128)S(1)}, bf16[64,1024]{1,0:T(8,128)(2,1)S(1)}, bf16[64,1024]{1,0:T(8,128)(2,1)S(1)}) custom-call(bf16[32,2176]{1,0:T(8,128)(2,1)S(1)} %collective-permute-done.17.refs_0_, bf16[32,2176]{1,0:T(8,128)(2,1)S(1)} %collective-permute-done.18.refs_1_, ...), custom_call_target="tpu_custom_call" | custom-call | flops 1006632960 | bytes 16809984 | tf_op jit(solution)/shard_map/pallas_call | solution.py:286
  55.9 2.6 %collective-permute-start.21 = (bf16[64,1024]{1,0:T(8,128)(2,1)S(1)}, bf16[64,1024]{1,0:T(8,128)(2,1)S(1)}, u32[]{:S(2)}, u32[]{:S(2)}) collective-permute-start(bf16[64,1024]{1,0:T(8,128)(2,1)S(1)} %get-tuple-element.89), channel_id=1, source_target_pairs={{0,12},{4,6},{8,10},{12,0},{14,2},{10,8},{6,4},{2,14},{1,13},{5,7}... | collective-permute-start | bytes 393224 | tf_op jit(solution)/shard_map/ppermute | solution.py:437
  58.6 0.5 collective-permute-start.15
  59.1 1.6 %collective-permute-start.16 = (bf16[64,1024]{1,0:T(8,128)(2,1)S(1)}, bf16[64,1024]{1,0:T(8,128)(2,1)S(1)}, u32[]{:S(2)}, u32[]{:S(2)}) collective-permute-start(bf16[64,1024]{1,0:T(8,128)(2,1)S(1)} %get-tuple-element.78), channel_id=1, source_target_pairs={{0,4},{4,8},{8,12},{12,14},{14,10},{10,6},{6,2},{2,0},{1,5},{5,9},... | collective-permute-start | bytes 393224 | tf_op jit(solution)/shard_map/ppermute | solution.py:379
  60.7 2.4 %collective-permute-start.26 = (bf16[64,1024]{1,0:T(8,128)(2,1)S(1)}, bf16[64,1024]{1,0:T(8,128)(2,1)S(1)}, u32[]{:S(2)}, u32[]{:S(2)}) collective-permute-start(bf16[64,1024]{1,0:T(8,128)(2,1)S(1)} %get-tuple-element.94), channel_id=1, source_target_pairs={{0,12},{4,6},{8,10},{12,0},{14,2},{10,8},{6,4},{2,14},{1,13},{5,7}... | collective-permute-start | bytes 393224 | tf_op jit(solution)/shard_map/ppermute | solution.py:437
  63.2 1.1 %collective-permute-start.24 = (bf16[64,1024]{1,0:T(8,128)(2,1)S(1)}, bf16[64,1024]{1,0:T(8,128)(2,1)S(1)}, u32[]{:S(2)}, u32[]{:S(2)}) collective-permute-start(bf16[64,1024]{1,0:T(8,128)(2,1)S(1)} %get-tuple-element.92), channel_id=1, source_target_pairs={{4,0},{8,4},{12,8},{14,12},{10,14},{6,10},{2,6},{0,2},{5,1},{9,5},... | collective-permute-start | bytes 393224 | tf_op jit(solution)/shard_map/ppermute | solution.py:379
  64.4 0.9 %collective-permute-start.25 = (bf16[64,1024]{1,0:T(8,128)(2,1)S(1)}, bf16[64,1024]{1,0:T(8,128)(2,1)S(1)}, u32[]{:S(2)}, u32[]{:S(2)}) collective-permute-start(bf16[64,1024]{1,0:T(8,128)(2,1)S(1)} %get-tuple-element.93), channel_id=1, source_target_pairs={{0,4},{4,8},{8,12},{12,14},{14,10},{10,6},{6,2},{2,0},{1,5},{5,9},... | collective-permute-start | bytes 393224 | tf_op jit(solution)/shard_map/ppermute | solution.py:379
  65.2 0.1 shard_map.125
  65.4 1.7 %collective-permute-done.15.refs_1_ = bf16[64,1024]{1,0:T(8,128)(2,1)S(1)} collective-permute-done((bf16[64,1024]{1,0:T(8,128)(2,1)S(1)}, bf16[64,1024]{1,0:T(8,128)(2,1)S(1)}, u32[]{:S(2)}, u32[]{:S(2)}) %collective-permute-start.15) | collective-permute-done | bytes 131104 | tf_op jit(solution)/shard_map/ppermute | solution.py:379
  67.1 0.1 shard_map.121
  67.2 0.9 %collective-permute-start.22 = (bf16[64,1024]{1,0:T(8,128)(2,1)S(1)}, bf16[64,1024]{1,0:T(8,128)(2,1)S(1)}, u32[]{:S(2)}, u32[]{:S(2)}) collective-permute-start(bf16[64,1024]{1,0:T(8,128)(2,1)S(1)} %get-tuple-element.90), channel_id=1, source_target_pairs={{4,0},{8,4},{12,8},{14,12},{10,14},{6,10},{2,6},{0,2},{5,1},{9,5},... | collective-permute-start | bytes 393224 | tf_op jit(solution)/shard_map/ppermute | solution.py:379
  68.2 1.0 %collective-permute-done.26.refs_3_ = bf16[64,1024]{1,0:T(8,128)(2,1)S(1)} collective-permute-done((bf16[64,1024]{1,0:T(8,128)(2,1)S(1)}, bf16[64,1024]{1,0:T(8,128)(2,1)S(1)}, u32[]{:S(2)}, u32[]{:S(2)}) %collective-permute-start.26) | collective-permute-done | bytes 131104 | tf_op jit(solution)/shard_map/ppermute | solution.py:437
  69.2 0.2 collective-permute-start.23
  69.3 0.6 collective-permute-done.24.refs_1_
  69.9 0.1 shard_map.123
  70.1 1.7 %collective-permute-start.27 = (bf16[64,1024]{1,0:T(8,128)(2,1)S(1)}, bf16[64,1024]{1,0:T(8,128)(2,1)S(1)}, u32[]{:S(2)}, u32[]{:S(2)}) collective-permute-start(bf16[64,1024]{1,0:T(8,128)(2,1)S(1)} %get-tuple-element.95), channel_id=1, source_target_pairs={{4,0},{8,4},{12,8},{14,12},{10,14},{6,10},{2,6},{0,2},{5,1},{9,5},... | collective-permute-start | bytes 393224 | tf_op jit(solution)/shard_map/ppermute | solution.py:379
  71.7 0.4 collective-permute-start.28
  72.1 0.7 shard_map.126
  72.8 0.8 %collective-permute-done.22.refs_1_ = bf16[64,1024]{1,0:T(8,128)(2,1)S(1)} collective-permute-done((bf16[64,1024]{1,0:T(8,128)(2,1)S(1)}, bf16[64,1024]{1,0:T(8,128)(2,1)S(1)}, u32[]{:S(2)}, u32[]{:S(2)}) %collective-permute-start.22) | collective-permute-done | bytes 131104 | tf_op jit(solution)/shard_map/ppermute | solution.py:379
  73.6 1.3 %collective-permute-done.23.refs_2_ = bf16[64,1024]{1,0:T(8,128)(2,1)S(1)} collective-permute-done((bf16[64,1024]{1,0:T(8,128)(2,1)S(1)}, bf16[64,1024]{1,0:T(8,128)(2,1)S(1)}, u32[]{:S(2)}, u32[]{:S(2)}) %collective-permute-start.23) | collective-permute-done | bytes 131104 | tf_op jit(solution)/shard_map/ppermute | solution.py:379
  74.9 1.1 %collective-permute-done.27.refs_3_ = bf16[64,1024]{1,0:T(8,128)(2,1)S(1)} collective-permute-done((bf16[64,1024]{1,0:T(8,128)(2,1)S(1)}, bf16[64,1024]{1,0:T(8,128)(2,1)S(1)}, u32[]{:S(2)}, u32[]{:S(2)}) %collective-permute-start.27) | collective-permute-done | bytes 131104 | tf_op jit(solution)/shard_map/ppermute | solution.py:379
  76.0 0.7 collective-permute-done.28.refs_4_
  76.7 0.8 %shard_map.124 = bf16[64,2048]{1,0:T(8,128)(2,1)} custom-call(f32[192,2048]{1,0:T(8,128)S(1)} %get-tuple-element.57.refs_0_, bf16[64,1024]{1,0:T(8,128)(2,1)S(1)} %collective-permute-done.22.refs_1_, bf16[64,1024]{1,0:T(8,128)(2,1)S(1)} %collective-permute-done.23.refs_2_, bf16[64,1024]{1,0:T(8,128)(2,1)S(1)} %collective-permute-done.27.refs_3_, ...), custom_call_target="tpu_custom_call" | custom-call | tf_op jit(solution)/shard_map/pallas_call | solution.py:456
  (31 shorter events, 0.4 us)
Async XLA Ops:
  0.6 26.7 %copy-start = (bf16[2,16,2048]{2,1,0:T(8,128)(2,1)S(1)}, bf16[2,16,2048]{2,1,0:T(8,128)(2,1)}, u32[]{:S(2)}) copy-start(bf16[2,16,2048]{2,1,0:T(8,128)(2,1)} %param.17) | copy-start | bytes 393220
  3.4 23.9 %collective-permute-start.4 = (bf16[1024,2304]{1,0:T(8,128)(2,1)S(1)}, bf16[1024,2304]{1,0:T(8,128)(2,1)S(1)}, u32[]{:S(2)}, u32[]{:S(2)}) collective-permute-start(bf16[1024,2304]{1,0:T(8,128)(2,1)S(1)} %get-tuple-element.56.refs_8_.refs_6_.refs_0_), channel_id=1, source_target_pairs={{0,1},{1,0},{2,3},{3,2},{4,5},{5,4},{6,7},{7,6},{8,9},{9,8},{10,11... | collective-permute-start | bytes 14155784 | tf_op jit(solution)/shard_map/ppermute | solution.py:360
  3.9 9.7 %collective-permute-start.2 = (bf16[64,2048]{1,0:T(8,128)(2,1)S(1)}, bf16[64,2048]{1,0:T(8,128)(2,1)S(1)}, u32[]{:S(2)}, u32[]{:S(2)}) collective-permute-start(bf16[64,2048]{1,0:T(8,128)(2,1)S(1)} %get-tuple-element.54.refs_5_), channel_id=1, source_target_pairs={{0,4},{4,8},{8,12},{12,14},{14,10},{10,6},{6,2},{2,0},{1,5},{5,9},... | collective-permute-start | bytes 786440 | tf_op jit(solution)/shard_map/ppermute | solution.py:399
  6.6 9.1 %collective-permute-start.3 = (bf16[64,2048]{1,0:T(8,128)(2,1)S(1)}, bf16[64,2048]{1,0:T(8,128)(2,1)S(1)}, u32[]{:S(2)}, u32[]{:S(2)}) collective-permute-start(bf16[64,2048]{1,0:T(8,128)(2,1)S(1)} %get-tuple-element.54.refs_5_), channel_id=1, source_target_pairs={{4,0},{8,4},{12,8},{14,12},{10,14},{6,10},{2,6},{0,2},{5,1},{9,5},... | collective-permute-start | bytes 786440 | tf_op jit(solution)/shard_map/ppermute | solution.py:400
  6.6 13.0 %collective-permute-start = (bf16[64,2176]{1,0:T(8,128)(2,1)S(1)}, bf16[64,2176]{1,0:T(8,128)(2,1)S(1)}, u32[]{:S(2)}, u32[]{:S(2)}) collective-permute-start(bf16[64,2176]{1,0:T(8,128)(2,1)S(1)} %get-tuple-element.53.refs_2_), channel_id=1, source_target_pairs={{0,4},{4,8},{8,12},{12,14},{14,10},{10,6},{6,2},{2,0},{1,5},{5,9},... | collective-permute-start | bytes 835592 | tf_op jit(solution)/shard_map/ppermute | solution.py:399
  8.6 13.1 %collective-permute-start.1 = (bf16[64,2176]{1,0:T(8,128)(2,1)S(1)}, bf16[64,2176]{1,0:T(8,128)(2,1)S(1)}, u32[]{:S(2)}, u32[]{:S(2)}) collective-permute-start(bf16[64,2176]{1,0:T(8,128)(2,1)S(1)} %get-tuple-element.53.refs_2_), channel_id=1, source_target_pairs={{4,0},{8,4},{12,8},{14,12},{10,14},{6,10},{2,6},{0,2},{5,1},{9,5},... | collective-permute-start | bytes 835592 | tf_op jit(solution)/shard_map/ppermute | solution.py:400
  13.7 11.6 %collective-permute-start.7 = (bf16[64,2048]{1,0:T(8,128)(2,1)S(1)}, bf16[64,2048]{1,0:T(8,128)(2,1)S(1)}, u32[]{:S(2)}, u32[]{:S(2)}) collective-permute-start(bf16[64,2048]{1,0:T(8,128)(2,1)S(1)} %collective-permute-done.2.refs_3_), channel_id=1, source_target_pairs={{0,4},{4,8},{8,12},{12,14},{14,10},{10,6},{6,2},{2,0},{1,5},{5,9},... | collective-permute-start | bytes 786440 | tf_op jit(solution)/shard_map/ppermute | solution.py:399
  15.7 11.6 %collective-permute-start.8 = (bf16[64,2048]{1,0:T(8,128)(2,1)S(1)}, bf16[64,2048]{1,0:T(8,128)(2,1)S(1)}, u32[]{:S(2)}, u32[]{:S(2)}) collective-permute-start(bf16[64,2048]{1,0:T(8,128)(2,1)S(1)} %collective-permute-done.3.refs_4_), channel_id=1, source_target_pairs={{4,0},{8,4},{12,8},{14,12},{10,14},{6,10},{2,6},{0,2},{5,1},{9,5},... | collective-permute-start | bytes 786440 | tf_op jit(solution)/shard_map/ppermute | solution.py:400
  19.6 12.3 %collective-permute-start.5 = (bf16[64,2176]{1,0:T(8,128)(2,1)S(1)}, bf16[64,2176]{1,0:T(8,128)(2,1)S(1)}, u32[]{:S(2)}, u32[]{:S(2)}) collective-permute-start(bf16[64,2176]{1,0:T(8,128)(2,1)S(1)} %collective-permute-done.refs_0_), channel_id=1, source_target_pairs={{0,4},{4,8},{8,12},{12,14},{14,10},{10,6},{6,2},{2,0},{1,5},{5,9},... | collective-permute-start | bytes 835592 | tf_op jit(solution)/shard_map/ppermute | solution.py:399
  21.7 12.3 %collective-permute-start.6 = (bf16[64,2176]{1,0:T(8,128)(2,1)S(1)}, bf16[64,2176]{1,0:T(8,128)(2,1)S(1)}, u32[]{:S(2)}, u32[]{:S(2)}) collective-permute-start(bf16[64,2176]{1,0:T(8,128)(2,1)S(1)} %collective-permute-done.1.refs_1_), channel_id=1, source_target_pairs={{4,0},{8,4},{12,8},{14,12},{10,14},{6,10},{2,6},{0,2},{5,1},{9,5},... | collective-permute-start | bytes 835592 | tf_op jit(solution)/shard_map/ppermute | solution.py:400
  25.2 11.6 %collective-permute-start.11 = (bf16[64,2048]{1,0:T(8,128)(2,1)S(1)}, bf16[64,2048]{1,0:T(8,128)(2,1)S(1)}, u32[]{:S(2)}, u32[]{:S(2)}) collective-permute-start(bf16[64,2048]{1,0:T(8,128)(2,1)S(1)} %collective-permute-done.7.refs_2_), channel_id=1, source_target_pairs={{0,4},{4,8},{8,12},{12,14},{14,10},{10,6},{6,2},{2,0},{1,5},{5,9},... | collective-permute-start | bytes 786440 | tf_op jit(solution)/shard_map/ppermute | solution.py:399
  27.3 11.6 %collective-permute-start.12 = (bf16[64,2048]{1,0:T(8,128)(2,1)S(1)}, bf16[64,2048]{1,0:T(8,128)(2,1)S(1)}, u32[]{:S(2)}, u32[]{:S(2)}) collective-permute-start(bf16[64,2048]{1,0:T(8,128)(2,1)S(1)} %collective-permute-done.8.refs_3_), channel_id=1, source_target_pairs={{4,0},{8,4},{12,8},{14,12},{10,14},{6,10},{2,6},{0,2},{5,1},{9,5},... | collective-permute-start | bytes 786440 | tf_op jit(solution)/shard_map/ppermute | solution.py:400
  32.0 12.5 %collective-permute-start.9 = (bf16[64,2176]{1,0:T(8,128)(2,1)S(1)}, bf16[64,2176]{1,0:T(8,128)(2,1)S(1)}, u32[]{:S(2)}, u32[]{:S(2)}) collective-permute-start(bf16[64,2176]{1,0:T(8,128)(2,1)S(1)} %collective-permute-done.5.refs_0_), channel_id=1, source_target_pairs={{0,4},{4,8},{8,12},{12,14},{14,10},{10,6},{6,2},{2,0},{1,5},{5,9},... | collective-permute-start | bytes 835592 | tf_op jit(solution)/shard_map/ppermute | solution.py:399
  34.0 10.8 %collective-permute-start.10 = (bf16[64,2176]{1,0:T(8,128)(2,1)S(1)}, bf16[64,2176]{1,0:T(8,128)(2,1)S(1)}, u32[]{:S(2)}, u32[]{:S(2)}) collective-permute-start(bf16[64,2176]{1,0:T(8,128)(2,1)S(1)} %collective-permute-done.6.refs_1_), channel_id=1, source_target_pairs={{4,0},{8,4},{12,8},{14,12},{10,14},{6,10},{2,6},{0,2},{5,1},{9,5},... | collective-permute-start | bytes 835592 | tf_op jit(solution)/shard_map/ppermute | solution.py:400
  38.9 11.0 %collective-permute-start.19 = (bf16[32,2048]{1,0:T(8,128)(2,1)S(1)}, bf16[32,2048]{1,0:T(8,128)(2,1)S(1)}, u32[]{:S(2)}, u32[]{:S(2)}) collective-permute-start(bf16[32,2048]{1,0:T(8,128)(2,1)S(1)} %get-tuple-element.85), channel_id=1, source_target_pairs={{0,4},{4,8},{8,12},{12,14},{14,10},{10,6},{6,2},{2,0},{1,5},{5,9},... | collective-permute-start | bytes 393224 | tf_op jit(solution)/shard_map/ppermute | solution.py:418
  40.6 11.2 %collective-permute-start.20 = (bf16[32,2048]{1,0:T(8,128)(2,1)S(1)}, bf16[32,2048]{1,0:T(8,128)(2,1)S(1)}, u32[]{:S(2)}, u32[]{:S(2)}) collective-permute-start(bf16[32,2048]{1,0:T(8,128)(2,1)S(1)} %get-tuple-element.86), channel_id=1, source_target_pairs={{4,0},{8,4},{12,8},{14,12},{10,14},{6,10},{2,6},{0,2},{5,1},{9,5},... | collective-permute-start | bytes 393224 | tf_op jit(solution)/shard_map/ppermute | solution.py:419
  44.9 6.9 %collective-permute-start.17 = (bf16[32,2176]{1,0:T(8,128)(2,1)S(1)}, bf16[32,2176]{1,0:T(8,128)(2,1)S(1)}, u32[]{:S(2)}, u32[]{:S(2)}) collective-permute-start(bf16[32,2176]{1,0:T(8,128)(2,1)S(1)} %get-tuple-element.81), channel_id=1, source_target_pairs={{0,4},{4,8},{8,12},{12,14},{14,10},{10,6},{6,2},{2,0},{1,5},{5,9},... | collective-permute-start | bytes 417800 | tf_op jit(solution)/shard_map/ppermute | solution.py:418
  46.5 6.3 %collective-permute-start.18 = (bf16[32,2176]{1,0:T(8,128)(2,1)S(1)}, bf16[32,2176]{1,0:T(8,128)(2,1)S(1)}, u32[]{:S(2)}, u32[]{:S(2)}) collective-permute-start(bf16[32,2176]{1,0:T(8,128)(2,1)S(1)} %get-tuple-element.82), channel_id=1, source_target_pairs={{4,0},{8,4},{12,8},{14,12},{10,14},{6,10},{2,6},{0,2},{5,1},{9,5},... | collective-permute-start | bytes 417800 | tf_op jit(solution)/shard_map/ppermute | solution.py:419
  49.7 8.8 %collective-permute-start.13 = (bf16[64,2048]{1,0:T(8,128)(2,1)S(1)}, bf16[64,2048]{1,0:T(8,128)(2,1)S(1)}, u32[]{:S(2)}, u32[]{:S(2)}) collective-permute-start(bf16[64,2048]{1,0:T(8,128)(2,1)S(1)} %get-tuple-element.75), channel_id=1, source_target_pairs={{4,0},{8,4},{12,8},{14,12},{10,14},{6,10},{2,6},{0,2},{5,1},{9,5},... | collective-permute-start | bytes 786440 | tf_op jit(solution)/shard_map/ppermute | solution.py:379
  49.9 8.6 %collective-permute-start.14 = (bf16[64,2048]{1,0:T(8,128)(2,1)S(1)}, bf16[64,2048]{1,0:T(8,128)(2,1)S(1)}, u32[]{:S(2)}, u32[]{:S(2)}) collective-permute-start(bf16[64,2048]{1,0:T(8,128)(2,1)S(1)} %get-tuple-element.76), channel_id=1, source_target_pairs={{0,4},{4,8},{8,12},{12,14},{14,10},{10,6},{6,2},{2,0},{1,5},{5,9},... | collective-permute-start | bytes 786440 | tf_op jit(solution)/shard_map/ppermute | solution.py:379
  55.9 8.4 %collective-permute-start.21 = (bf16[64,1024]{1,0:T(8,128)(2,1)S(1)}, bf16[64,1024]{1,0:T(8,128)(2,1)S(1)}, u32[]{:S(2)}, u32[]{:S(2)}) collective-permute-start(bf16[64,1024]{1,0:T(8,128)(2,1)S(1)} %get-tuple-element.89), channel_id=1, source_target_pairs={{0,12},{4,6},{8,10},{12,0},{14,2},{10,8},{6,4},{2,14},{1,13},{5,7}... | collective-permute-start | bytes 393224 | tf_op jit(solution)/shard_map/ppermute | solution.py:437
  58.6 8.5 %collective-permute-start.15 = (bf16[64,1024]{1,0:T(8,128)(2,1)S(1)}, bf16[64,1024]{1,0:T(8,128)(2,1)S(1)}, u32[]{:S(2)}, u32[]{:S(2)}) collective-permute-start(bf16[64,1024]{1,0:T(8,128)(2,1)S(1)} %get-tuple-element.77), channel_id=1, source_target_pairs={{4,0},{8,4},{12,8},{14,12},{10,14},{6,10},{2,6},{0,2},{5,1},{9,5},... | collective-permute-start | bytes 393224 | tf_op jit(solution)/shard_map/ppermute | solution.py:379
  59.1 8.0 %collective-permute-start.16 = (bf16[64,1024]{1,0:T(8,128)(2,1)S(1)}, bf16[64,1024]{1,0:T(8,128)(2,1)S(1)}, u32[]{:S(2)}, u32[]{:S(2)}) collective-permute-start(bf16[64,1024]{1,0:T(8,128)(2,1)S(1)} %get-tuple-element.78), channel_id=1, source_target_pairs={{0,4},{4,8},{8,12},{12,14},{14,10},{10,6},{6,2},{2,0},{1,5},{5,9},... | collective-permute-start | bytes 393224 | tf_op jit(solution)/shard_map/ppermute | solution.py:379
  60.7 8.5 %collective-permute-start.26 = (bf16[64,1024]{1,0:T(8,128)(2,1)S(1)}, bf16[64,1024]{1,0:T(8,128)(2,1)S(1)}, u32[]{:S(2)}, u32[]{:S(2)}) collective-permute-start(bf16[64,1024]{1,0:T(8,128)(2,1)S(1)} %get-tuple-element.94), channel_id=1, source_target_pairs={{0,12},{4,6},{8,10},{12,0},{14,2},{10,8},{6,4},{2,14},{1,13},{5,7}... | collective-permute-start | bytes 393224 | tf_op jit(solution)/shard_map/ppermute | solution.py:437
  63.2 6.8 %collective-permute-start.24 = (bf16[64,1024]{1,0:T(8,128)(2,1)S(1)}, bf16[64,1024]{1,0:T(8,128)(2,1)S(1)}, u32[]{:S(2)}, u32[]{:S(2)}) collective-permute-start(bf16[64,1024]{1,0:T(8,128)(2,1)S(1)} %get-tuple-element.92), channel_id=1, source_target_pairs={{4,0},{8,4},{12,8},{14,12},{10,14},{6,10},{2,6},{0,2},{5,1},{9,5},... | collective-permute-start | bytes 393224 | tf_op jit(solution)/shard_map/ppermute | solution.py:379
  64.4 5.6 %collective-permute-start.25 = (bf16[64,1024]{1,0:T(8,128)(2,1)S(1)}, bf16[64,1024]{1,0:T(8,128)(2,1)S(1)}, u32[]{:S(2)}, u32[]{:S(2)}) collective-permute-start(bf16[64,1024]{1,0:T(8,128)(2,1)S(1)} %get-tuple-element.93), channel_id=1, source_target_pairs={{0,4},{4,8},{8,12},{12,14},{14,10},{10,6},{6,2},{2,0},{1,5},{5,9},... | collective-permute-start | bytes 393224 | tf_op jit(solution)/shard_map/ppermute | solution.py:379
  67.1 5.0 %collective-permute-start.29 = (f32[32,1216]{1,0:T(8,128)S(1)}, f32[32,1216]{1,0:T(8,128)S(1)}, u32[]{:S(2)}, u32[]{:S(2)}) collective-permute-start(f32[32,1216]{1,0:T(8,128)S(1)} %get-tuple-element.100), channel_id=1, source_target_pairs={{0,1},{1,0},{2,3},{3,2},{4,5},{5,4},{6,7},{7,6},{8,9},{9,8},{10,11... | collective-permute-start | bytes 466952 | tf_op jit(solution)/shard_map/ppermute | solution.py:470
  67.2 6.3 %collective-permute-start.22 = (bf16[64,1024]{1,0:T(8,128)(2,1)S(1)}, bf16[64,1024]{1,0:T(8,128)(2,1)S(1)}, u32[]{:S(2)}, u32[]{:S(2)}) collective-permute-start(bf16[64,1024]{1,0:T(8,128)(2,1)S(1)} %get-tuple-element.90), channel_id=1, source_target_pairs={{4,0},{8,4},{12,8},{14,12},{10,14},{6,10},{2,6},{0,2},{5,1},{9,5},... | collective-permute-start | bytes 393224 | tf_op jit(solution)/shard_map/ppermute | solution.py:379
  69.2 5.7 %collective-permute-start.23 = (bf16[64,1024]{1,0:T(8,128)(2,1)S(1)}, bf16[64,1024]{1,0:T(8,128)(2,1)S(1)}, u32[]{:S(2)}, u32[]{:S(2)}) collective-permute-start(bf16[64,1024]{1,0:T(8,128)(2,1)S(1)} %get-tuple-element.91), channel_id=1, source_target_pairs={{0,4},{4,8},{8,12},{12,14},{14,10},{10,6},{6,2},{2,0},{1,5},{5,9},... | collective-permute-start | bytes 393224 | tf_op jit(solution)/shard_map/ppermute | solution.py:379
  70.1 6.0 %collective-permute-start.27 = (bf16[64,1024]{1,0:T(8,128)(2,1)S(1)}, bf16[64,1024]{1,0:T(8,128)(2,1)S(1)}, u32[]{:S(2)}, u32[]{:S(2)}) collective-permute-start(bf16[64,1024]{1,0:T(8,128)(2,1)S(1)} %get-tuple-element.95), channel_id=1, source_target_pairs={{4,0},{8,4},{12,8},{14,12},{10,14},{6,10},{2,6},{0,2},{5,1},{9,5},... | collective-permute-start | bytes 393224 | tf_op jit(solution)/shard_map/ppermute | solution.py:379
  71.7 5.0 %collective-permute-start.28 = (bf16[64,1024]{1,0:T(8,128)(2,1)S(1)}, bf16[64,1024]{1,0:T(8,128)(2,1)S(1)}, u32[]{:S(2)}, u32[]{:S(2)}) collective-permute-start(bf16[64,1024]{1,0:T(8,128)(2,1)S(1)} %get-tuple-element.96), channel_id=1, source_target_pairs={{0,4},{4,8},{8,12},{12,14},{14,10},{10,6},{6,2},{2,0},{1,5},{5,9},... | collective-permute-start | bytes 393224 | tf_op jit(solution)/shard_map/ppermute | solution.py:379

commit v15 on v14

--- a/solution.py
+++ b/solution.py
@@ -148,9 +148,9 @@
     raw_refs, refs = refs[:3], refs[3:]
     out_grad_ref, ids_ref, route_ref, factor_ref = refs[:4]
     tokens_ref, refs = refs[4], refs[5:]
-    packed_ref, grads_ref, tokens_held_ref, factor_in_ref, ids_held, route_held, sems = refs
+    packed_ref, grads_ref, tokens_held_ref, factor_in_ref, ids_held, sems = refs
     width, rank, cuts = plan.hidden_width, plan.rank, plan.cuts
-    pairs = [(ids_ref, ids_held), (route_ref, route_held)]
+    pairs = [(ids_ref, ids_held)]
     pairs.append((out_grad_ref, grads_ref))
     pairs.append((tokens_ref, tokens_held_ref.at[:, : plan.model_width]))
     for kind in range(3):
@@ -178,16 +178,15 @@
                     expert * rank : (expert + 1) * rank, other * width : (other + 1) * width
                 ] = jnp.zeros((rank, width), bf16)
     copies[0].wait()
-    copies[1].wait()
     rows, lanes = grads_ref.shape[0], tokens_held_ref.shape[1] - plan.model_width
     expert_at = lax.broadcasted_iota(jnp.int32, (lanes, rows), 0)
-    ids, route = ids_held[...], route_held[...].astype(f32)
+    ids, route = ids_held[...], route_ref[...]
     dense = jnp.zeros((lanes, rows), f32)
     for k in range(ids.shape[0]):
         dense = jnp.where(ids[k : k + 1, :] == expert_at, route[k : k + 1, :], dense)
     dense = dense.T.astype(bf16)
     tokens_held_ref[:, plan.model_width :] = dense
-    for copy in copies[2:]:
+    for copy in copies[1:]:
         copy.wait()
 
 
@@ -296,6 +295,10 @@
             transcendentals=0,
         ),
     )(*operands)
+
+
+def in_hbm(*arrays):
+    return [pltpu.with_memory_space_constraint(x, pltpu.HBM) for x in arrays]
 
 
 def per_device(
@@ -333,28 +336,19 @@
             jax.ShapeDtypeStruct((token_count, model_width + lanes), bf16),
             jax.ShapeDtypeStruct((ranks, wide), bf16),
         ),
-        in_specs=[pl.BlockSpec(memory_space=pltpu.HBM)] * 8,
+        in_specs=[pl.BlockSpec(memory_space=pltpu.HBM)] * 5
+        + [pl.BlockSpec(memory_space=pltpu.VMEM)]
+        + [pl.BlockSpec(memory_space=pltpu.HBM)] * 2,
         out_specs=(pl.BlockSpec(memory_space=pltpu.VMEM),) * 4,
         scratch_shapes=[
             pltpu.VMEM(expert_ids.shape[::-1], jnp.int32),
-            pltpu.VMEM(route_weight.shape[::-1], bf16),
-            pltpu.SemaphoreType.DMA((4 + (3 * plan.cuts + 1) * local_count,)),
+            pltpu.SemaphoreType.DMA((3 + (3 * plan.cuts + 1) * local_count,)),
         ],
         compiler_params=pltpu.CompilerParams(vmem_limit_bytes=16 * 1024 * 1024),
     )(
-        *(
-            pltpu.with_memory_space_constraint(x, pltpu.HBM)
-            for x in (
-                gate_weight,
-                up_weight,
-                down_weight,
-                out_grad,
-                expert_ids.T,
-                route_weight.T,
-                adapter_in,
-                tokens,
-            )
-        )
+        *in_hbm(gate_weight, up_weight, down_weight, out_grad, expert_ids.T),
+        route_weight.T.astype(f32),
+        *in_hbm(adapter_in, tokens),
     )
     if parts == 2:
         weights = [mine, lax.ppermute(mine, "dp", swap)]

time: 77.6 us -> 78.3 us (level)
  no operation moved by 1% of the time
where the time goes in v15:
time: 78.3 us; the launch traced here: 78.1 us
  starting transfers between devices  31.9 us (41%)
  waiting for transfers between devices  24.4 us (31%)
  Pallas kernels  20.4 us (26%)
    ppermute x8, starting transfers between devices, per_device(): lax.ppermute(x, 'expert', forward)  16.1 us
    pallas_call x4, Pallas kernels, expert_call(): pl.pallas_call(functools.partial(whole_kernel, plan, len(pieces), blocks,...  13.9 us
    ppermute x8, waiting for transfers between devices, per_device(): lax.ppermute(x, 'expert', forward)  13.5 us
    ppermute x10, starting transfers between devices, send(): return lax.ppermute(value, 'expert', ways[way][1])  9.36 us
    ppermute x10, waiting for transfers between devices, send(): return lax.ppermute(value, 'expert', ways[way][1])  6.25 us
    ppermute x2, starting transfers between devices, per_device(): skipped = [lax.ppermute(value, 'expert', pairs) for value in outs[2:]]  5.01 us
    pallas_call x1, Pallas kernels, per_device(): pl.pallas_call(functools.partial(prepare_kernel, plan), out_shape=(jax.Sh...  2.72 us
    pallas_call x5, Pallas kernels, simple_call(): pl.pallas_call(kernel, out_shape=tuple((jax.ShapeDtypeStruct(shape, dtype...  2.64 us
  transfers between devices with their start and end apart: 30, of which 15 were waited for; matrix products, arithmetic and copies ran while one was open for 0% of the time, Pallas kernels for 22%

profile of v15, /device:TPU:0, one launch (start us, length us, event | category | flops | bytes accessed | tf_op | source)
XLA Modules:
  0.0 78.1 jit_solution(9288834295073880011)
XLA Ops:
  0.6 0.7 convert_bitcast_fusion.refs_5_
  1.4 2.7 %shard_map.112 = (bf16[1024,2304]{1,0:T(8,128)(2,1)S(1)}, bf16[64,2048]{1,0:T(8,128)(2,1)S(1)}, bf16[64,2176]{1,0:T(8,128)(2,1)S(1)}, bf16[32,768]{1,0:T(8,128)(2,1)S(1)}) custom-call(bf16[2,1024,384]{2,1,0:T(8,128)(2,1)} %refs_0_.1, bf16[2,1024,384]{2,1,0:T(8,128)(2,1)} %refs_1_.1, bf16[2,1024,384]{2,1,0:T(8,128)(2,1)} %refs_2_.1, ...), custom_call_target="tpu_custom_call" | custom-call | tf_op jit(solution)/shard_map/pallas_call | solution.py:331
  4.1 0.5 collective-permute-start.4
  4.6 2.6 %collective-permute-start.2 = (bf16[64,2048]{1,0:T(8,128)(2,1)S(1)}, bf16[64,2048]{1,0:T(8,128)(2,1)S(1)}, u32[]{:S(2)}, u32[]{:S(2)}) collective-permute-start(bf16[64,2048]{1,0:T(8,128)(2,1)S(1)} %get-tuple-element.54.refs_5_), channel_id=1, source_target_pairs={{0,4},{4,8},{8,12},{12,14},{14,10},{10,6},{6,2},{2,0},{1,5},{5,9},... | collective-permute-start | bytes 786440 | tf_op jit(solution)/shard_map/ppermute | solution.py:393
  7.2 2.0 %collective-permute-start = (bf16[64,2176]{1,0:T(8,128)(2,1)S(1)}, bf16[64,2176]{1,0:T(8,128)(2,1)S(1)}, u32[]{:S(2)}, u32[]{:S(2)}) collective-permute-start(bf16[64,2176]{1,0:T(8,128)(2,1)S(1)} %get-tuple-element.53.refs_2_), channel_id=1, source_target_pairs={{0,4},{4,8},{8,12},{12,14},{14,10},{10,6},{6,2},{2,0},{1,5},{5,9},... | collective-permute-start | bytes 835592 | tf_op jit(solution)/shard_map/ppermute | solution.py:393
  9.3 5.0 %collective-permute-done.2.refs_3_ = bf16[64,2048]{1,0:T(8,128)(2,1)S(1)} collective-permute-done((bf16[64,2048]{1,0:T(8,128)(2,1)S(1)}, bf16[64,2048]{1,0:T(8,128)(2,1)S(1)}, u32[]{:S(2)}, u32[]{:S(2)}) %collective-permute-start.2) | collective-permute-done | bytes 262176 | tf_op jit(solution)/shard_map/ppermute | solution.py:393
  14.3 2.0 %collective-permute-start.7 = (bf16[64,2048]{1,0:T(8,128)(2,1)S(1)}, bf16[64,2048]{1,0:T(8,128)(2,1)S(1)}, u32[]{:S(2)}, u32[]{:S(2)}) collective-permute-start(bf16[64,2048]{1,0:T(8,128)(2,1)S(1)} %collective-permute-done.2.refs_3_), channel_id=1, source_target_pairs={{0,4},{4,8},{8,12},{12,14},{14,10},{10,6},{6,2},{2,0},{1,5},{5,9},... | collective-permute-start | bytes 786440 | tf_op jit(solution)/shard_map/ppermute | solution.py:393
  16.4 3.9 %collective-permute-done.refs_0_ = bf16[64,2176]{1,0:T(8,128)(2,1)S(1)} collective-permute-done((bf16[64,2176]{1,0:T(8,128)(2,1)S(1)}, bf16[64,2176]{1,0:T(8,128)(2,1)S(1)}, u32[]{:S(2)}, u32[]{:S(2)}) %collective-permute-start) | collective-permute-done | bytes 278560 | tf_op jit(solution)/shard_map/ppermute | solution.py:393
  20.3 2.0 %collective-permute-start.5 = (bf16[64,2176]{1,0:T(8,128)(2,1)S(1)}, bf16[64,2176]{1,0:T(8,128)(2,1)S(1)}, u32[]{:S(2)}, u32[]{:S(2)}) collective-permute-start(bf16[64,2176]{1,0:T(8,128)(2,1)S(1)} %collective-permute-done.refs_0_), channel_id=1, source_target_pairs={{0,4},{4,8},{8,12},{12,14},{14,10},{10,6},{6,2},{2,0},{1,5},{5,9},... | collective-permute-start | bytes 835592 | tf_op jit(solution)/shard_map/ppermute | solution.py:393
  22.4 3.5 %collective-permute-done.7.refs_2_ = bf16[64,2048]{1,0:T(8,128)(2,1)S(1)} collective-permute-done((bf16[64,2048]{1,0:T(8,128)(2,1)S(1)}, bf16[64,2048]{1,0:T(8,128)(2,1)S(1)}, u32[]{:S(2)}, u32[]{:S(2)}) %collective-permute-start.7) | collective-permute-done | bytes 262176 | tf_op jit(solution)/shard_map/ppermute | solution.py:393
  25.9 2.0 %collective-permute-start.11 = (bf16[64,2048]{1,0:T(8,128)(2,1)S(1)}, bf16[64,2048]{1,0:T(8,128)(2,1)S(1)}, u32[]{:S(2)}, u32[]{:S(2)}) collective-permute-start(bf16[64,2048]{1,0:T(8,128)(2,1)S(1)} %collective-permute-done.7.refs_2_), channel_id=1, source_target_pairs={{0,4},{4,8},{8,12},{12,14},{14,10},{10,6},{6,2},{2,0},{1,5},{5,9},... | collective-permute-start | bytes 786440 | tf_op jit(solution)/shard_map/ppermute | solution.py:393
  28.0 4.6 %shard_map.113 = (f32[192,2048]{1,0:T(8,128)S(1)}, f32[32,768]{1,0:T(8,128)S(1)}, f32[32,2048]{1,0:T(8,128)S(1)}) custom-call(bf16[64,2176]{1,0:T(8,128)(2,1)S(1)} %collective-permute-done.refs_0_, bf16[64,2176]{1,0:T(8,128)(2,1)S(1)} %collective-permute-done.1.refs_1_, bf16[64,2176]{1,0:T(8,128)(2,1)S(1)} %get-tuple-element.53.refs_2_, ...), custom_call_target="tpu_custom_call" | custom-call | flops 3019898880 | bytes 11599872 | tf_op jit(solution)/shard_map/pallas_call | solution.py:285
  32.6 2.1 %collective-permute-start.9 = (bf16[64,2176]{1,0:T(8,128)(2,1)S(1)}, bf16[64,2176]{1,0:T(8,128)(2,1)S(1)}, u32[]{:S(2)}, u32[]{:S(2)}) collective-permute-start(bf16[64,2176]{1,0:T(8,128)(2,1)S(1)} %collective-permute-done.5.refs_0_), channel_id=1, source_target_pairs={{0,4},{4,8},{8,12},{12,14},{14,10},{10,6},{6,2},{2,0},{1,5},{5,9},... | collective-permute-start | bytes 835592 | tf_op jit(solution)/shard_map/ppermute | solution.py:393
  34.7 1.8 %shard_map.115 = (bf16[1536,1024]{1,0:T(8,128)(2,1)S(1)}, bf16[1536,1024]{1,0:T(8,128)(2,1)S(1)}) custom-call(bf16[1024,2304]{1,0:T(8,128)(2,1)S(1)} %get-tuple-element.56.refs_8_.refs_6_.refs_0_, bf16[1024,2304]{1,0:T(8,128)(2,1)S(1)} %collective-permute-done.4.refs_9_.refs_7_.refs_1_), custom_call_target="tpu_custom_call" | custom-call | tf_op jit(solution)/shard_map/pallas_call | solution.py:269
  36.5 1.0 %collective-permute-done.11.refs_2_.first_ref = bf16[64,2048]{1,0:T(8,128)(2,1)S(1)} collective-permute-done((bf16[64,2048]{1,0:T(8,128)(2,1)S(1)}, bf16[64,2048]{1,0:T(8,128)(2,1)S(1)}, u32[]{:S(2)}, u32[]{:S(2)}) %collective-permute-start.11) | collective-permute-done | bytes 262176 | tf_op jit(solution)/shard_map/ppermute | solution.py:393
  37.5 2.1 %collective-permute-done.12.refs_3_.second_ref = bf16[64,2048]{1,0:T(8,128)(2,1)S(1)} collective-permute-done((bf16[64,2048]{1,0:T(8,128)(2,1)S(1)}, bf16[64,2048]{1,0:T(8,128)(2,1)S(1)}, u32[]{:S(2)}, u32[]{:S(2)}) %collective-permute-start.12) | collective-permute-done | bytes 262176 | tf_op jit(solution)/shard_map/ppermute | solution.py:394
  39.6 1.6 %collective-permute-start.19 = (bf16[32,2048]{1,0:T(8,128)(2,1)S(1)}, bf16[32,2048]{1,0:T(8,128)(2,1)S(1)}, u32[]{:S(2)}, u32[]{:S(2)}) collective-permute-start(bf16[32,2048]{1,0:T(8,128)(2,1)S(1)} %get-tuple-element.85), channel_id=1, source_target_pairs={{0,4},{4,8},{8,12},{12,14},{14,10},{10,6},{6,2},{2,0},{1,5},{5,9},... | collective-permute-start | bytes 393224 | tf_op jit(solution)/shard_map/ppermute | solution.py:412
  41.2 0.4 collective-permute-start.20
  41.7 3.5 %shard_map.114 = (f32[128,2048]{1,0:T(8,128)S(1)}, f32[32,768]{1,0:T(8,128)S(1)}, f32[32,2048]{1,0:T(8,128)S(1)}) custom-call(bf16[64,2176]{1,0:T(8,128)(2,1)S(1)} %collective-permute-done.5.refs_0_, bf16[64,2176]{1,0:T(8,128)(2,1)S(1)} %collective-permute-done.6.refs_1_, bf16[64,2048]{1,0:T(8,128)(2,1)S(1)} %collective-permute-done.7.refs_2_, ...), custom_call_target="tpu_custom_call" | custom-call | flops 2013265920 | bytes 11059200 | tf_op jit(solution)/shard_map/pallas_call | solution.py:285
  45.2 0.4 collective-permute-done.10.refs_1_.second_ref
  45.6 1.6 %collective-permute-start.17 = (bf16[32,2176]{1,0:T(8,128)(2,1)S(1)}, bf16[32,2176]{1,0:T(8,128)(2,1)S(1)}, u32[]{:S(2)}, u32[]{:S(2)}) collective-permute-start(bf16[32,2176]{1,0:T(8,128)(2,1)S(1)} %get-tuple-element.81), channel_id=1, source_target_pairs={{0,4},{4,8},{8,12},{12,14},{14,10},{10,6},{6,2},{2,0},{1,5},{5,9},... | collective-permute-start | bytes 417800 | tf_op jit(solution)/shard_map/ppermute | solution.py:412
  47.2 0.5 collective-permute-start.18
  47.6 2.7 %shard_map.116 = (f32[32,768]{1,0:T(8,128)S(1)}, f32[32,2048]{1,0:T(8,128)S(1)}, bf16[64,2048]{1,0:T(8,128)(2,1)S(1)}, bf16[64,2048]{1,0:T(8,128)(2,1)S(1)}) custom-call(bf16[64,2176]{1,0:T(8,128)(2,1)S(1)} %collective-permute-done.9.refs_0_.first_ref, bf16[64,2176]{1,0:T(8,128)(2,1)S(1)} %collective-permute-done.10.refs_1_.second_ref, ...), custom_call_target="tpu_custom_call" | custom-call | flops 2013265920 | bytes 17350656 | tf_op jit(solution)/shard_map/pallas_call | solution.py:285
  50.4 0.2 collective-permute-start.13
  50.6 1.9 %collective-permute-start.14 = (bf16[64,2048]{1,0:T(8,128)(2,1)S(1)}, bf16[64,2048]{1,0:T(8,128)(2,1)S(1)}, u32[]{:S(2)}, u32[]{:S(2)}) collective-permute-start(bf16[64,2048]{1,0:T(8,128)(2,1)S(1)} %get-tuple-element.76), channel_id=1, source_target_pairs={{0,4},{4,8},{8,12},{12,14},{14,10},{10,6},{6,2},{2,0},{1,5},{5,9},... | collective-permute-start | bytes 786440 | tf_op jit(solution)/shard_map/ppermute | solution.py:373
  52.5 1.0 %collective-permute-done.18.refs_1_ = bf16[32,2176]{1,0:T(8,128)(2,1)S(1)} collective-permute-done((bf16[32,2176]{1,0:T(8,128)(2,1)S(1)}, bf16[32,2176]{1,0:T(8,128)(2,1)S(1)}, u32[]{:S(2)}, u32[]{:S(2)}) %collective-permute-start.18) | collective-permute-done | bytes 139296 | tf_op jit(solution)/shard_map/ppermute | solution.py:413
  53.5 3.1 %shard_map.120 = (f32[32,768]{1,0:T(8,128)S(1)}, f32[32,2048]{1,0:T(8,128)S(1)}, bf16[64,1024]{1,0:T(8,128)(2,1)S(1)}, bf16[64,1024]{1,0:T(8,128)(2,1)S(1)}) custom-call(bf16[32,2176]{1,0:T(8,128)(2,1)S(1)} %collective-permute-done.17.refs_0_, bf16[32,2176]{1,0:T(8,128)(2,1)S(1)} %collective-permute-done.18.refs_1_, ...), custom_call_target="tpu_custom_call" | custom-call | flops 1006632960 | bytes 16809984 | tf_op jit(solution)/shard_map/pallas_call | solution.py:285
  56.6 2.6 %collective-permute-start.21 = (bf16[64,1024]{1,0:T(8,128)(2,1)S(1)}, bf16[64,1024]{1,0:T(8,128)(2,1)S(1)}, u32[]{:S(2)}, u32[]{:S(2)}) collective-permute-start(bf16[64,1024]{1,0:T(8,128)(2,1)S(1)} %get-tuple-element.89), channel_id=1, source_target_pairs={{0,12},{4,6},{8,10},{12,0},{14,2},{10,8},{6,4},{2,14},{1,13},{5,7}... | collective-permute-start | bytes 393224 | tf_op jit(solution)/shard_map/ppermute | solution.py:431
  59.2 0.5 collective-permute-start.15
  59.7 1.6 %collective-permute-start.16 = (bf16[64,1024]{1,0:T(8,128)(2,1)S(1)}, bf16[64,1024]{1,0:T(8,128)(2,1)S(1)}, u32[]{:S(2)}, u32[]{:S(2)}) collective-permute-start(bf16[64,1024]{1,0:T(8,128)(2,1)S(1)} %get-tuple-element.78), channel_id=1, source_target_pairs={{0,4},{4,8},{8,12},{12,14},{14,10},{10,6},{6,2},{2,0},{1,5},{5,9},... | collective-permute-start | bytes 393224 | tf_op jit(solution)/shard_map/ppermute | solution.py:373
  61.4 2.4 %collective-permute-start.26 = (bf16[64,1024]{1,0:T(8,128)(2,1)S(1)}, bf16[64,1024]{1,0:T(8,128)(2,1)S(1)}, u32[]{:S(2)}, u32[]{:S(2)}) collective-permute-start(bf16[64,1024]{1,0:T(8,128)(2,1)S(1)} %get-tuple-element.94), channel_id=1, source_target_pairs={{0,12},{4,6},{8,10},{12,0},{14,2},{10,8},{6,4},{2,14},{1,13},{5,7}... | collective-permute-start | bytes 393224 | tf_op jit(solution)/shard_map/ppermute | solution.py:431
  63.8 1.1 %collective-permute-start.24 = (bf16[64,1024]{1,0:T(8,128)(2,1)S(1)}, bf16[64,1024]{1,0:T(8,128)(2,1)S(1)}, u32[]{:S(2)}, u32[]{:S(2)}) collective-permute-start(bf16[64,1024]{1,0:T(8,128)(2,1)S(1)} %get-tuple-element.92), channel_id=1, source_target_pairs={{4,0},{8,4},{12,8},{14,12},{10,14},{6,10},{2,6},{0,2},{5,1},{9,5},... | collective-permute-start | bytes 393224 | tf_op jit(solution)/shard_map/ppermute | solution.py:373
  65.0 0.9 %collective-permute-start.25 = (bf16[64,1024]{1,0:T(8,128)(2,1)S(1)}, bf16[64,1024]{1,0:T(8,128)(2,1)S(1)}, u32[]{:S(2)}, u32[]{:S(2)}) collective-permute-start(bf16[64,1024]{1,0:T(8,128)(2,1)S(1)} %get-tuple-element.93), channel_id=1, source_target_pairs={{0,4},{4,8},{8,12},{12,14},{14,10},{10,6},{6,2},{2,0},{1,5},{5,9},... | collective-permute-start | bytes 393224 | tf_op jit(solution)/shard_map/ppermute | solution.py:373
  65.9 0.1 shard_map.125
  66.0 1.7 %collective-permute-done.15.refs_1_ = bf16[64,1024]{1,0:T(8,128)(2,1)S(1)} collective-permute-done((bf16[64,1024]{1,0:T(8,128)(2,1)S(1)}, bf16[64,1024]{1,0:T(8,128)(2,1)S(1)}, u32[]{:S(2)}, u32[]{:S(2)}) %collective-permute-start.15) | collective-permute-done | bytes 131104 | tf_op jit(solution)/shard_map/ppermute | solution.py:373
  67.8 0.1 shard_map.121
  67.9 0.9 %collective-permute-start.22 = (bf16[64,1024]{1,0:T(8,128)(2,1)S(1)}, bf16[64,1024]{1,0:T(8,128)(2,1)S(1)}, u32[]{:S(2)}, u32[]{:S(2)}) collective-permute-start(bf16[64,1024]{1,0:T(8,128)(2,1)S(1)} %get-tuple-element.90), channel_id=1, source_target_pairs={{4,0},{8,4},{12,8},{14,12},{10,14},{6,10},{2,6},{0,2},{5,1},{9,5},... | collective-permute-start | bytes 393224 | tf_op jit(solution)/shard_map/ppermute | solution.py:373
  68.8 1.0 %collective-permute-done.26.refs_3_ = bf16[64,1024]{1,0:T(8,128)(2,1)S(1)} collective-permute-done((bf16[64,1024]{1,0:T(8,128)(2,1)S(1)}, bf16[64,1024]{1,0:T(8,128)(2,1)S(1)}, u32[]{:S(2)}, u32[]{:S(2)}) %collective-permute-start.26) | collective-permute-done | bytes 131104 | tf_op jit(solution)/shard_map/ppermute | solution.py:431
  69.8 0.2 collective-permute-start.23
  70.0 0.6 collective-permute-done.24.refs_1_
  70.7 1.7 %collective-permute-start.27 = (bf16[64,1024]{1,0:T(8,128)(2,1)S(1)}, bf16[64,1024]{1,0:T(8,128)(2,1)S(1)}, u32[]{:S(2)}, u32[]{:S(2)}) collective-permute-start(bf16[64,1024]{1,0:T(8,128)(2,1)S(1)} %get-tuple-element.95), channel_id=1, source_target_pairs={{4,0},{8,4},{12,8},{14,12},{10,14},{6,10},{2,6},{0,2},{5,1},{9,5},... | collective-permute-start | bytes 393224 | tf_op jit(solution)/shard_map/ppermute | solution.py:373
  72.4 0.4 collective-permute-start.28
  72.8 0.7 shard_map.126
  73.5 0.8 collective-permute-done.22.refs_1_
  74.2 1.3 %collective-permute-done.23.refs_2_ = bf16[64,1024]{1,0:T(8,128)(2,1)S(1)} collective-permute-done((bf16[64,1024]{1,0:T(8,128)(2,1)S(1)}, bf16[64,1024]{1,0:T(8,128)(2,1)S(1)}, u32[]{:S(2)}, u32[]{:S(2)}) %collective-permute-start.23) | collective-permute-done | bytes 131104 | tf_op jit(solution)/shard_map/ppermute | solution.py:373
  75.6 1.1 %collective-permute-done.27.refs_3_ = bf16[64,1024]{1,0:T(8,128)(2,1)S(1)} collective-permute-done((bf16[64,1024]{1,0:T(8,128)(2,1)S(1)}, bf16[64,1024]{1,0:T(8,128)(2,1)S(1)}, u32[]{:S(2)}, u32[]{:S(2)}) %collective-permute-start.27) | collective-permute-done | bytes 131104 | tf_op jit(solution)/shard_map/ppermute | solution.py:373
  76.7 0.7 collective-permute-done.28.refs_4_
  77.4 0.8 %shard_map.124 = bf16[64,2048]{1,0:T(8,128)(2,1)} custom-call(f32[192,2048]{1,0:T(8,128)S(1)} %get-tuple-element.57.refs_0_, bf16[64,1024]{1,0:T(8,128)(2,1)S(1)} %collective-permute-done.22.refs_1_, bf16[64,1024]{1,0:T(8,128)(2,1)S(1)} %collective-permute-done.23.refs_2_, bf16[64,1024]{1,0:T(8,128)(2,1)S(1)} %collective-permute-done.27.refs_3_, ...), custom_call_target="tpu_custom_call" | custom-call | tf_op jit(solution)/shard_map/pallas_call | solution.py:450
  (32 shorter events, 0.5 us)
Async XLA Ops:
  0.6 27.4 %copy-start = (bf16[2,16,2048]{2,1,0:T(8,128)(2,1)S(1)}, bf16[2,16,2048]{2,1,0:T(8,128)(2,1)}, u32[]{:S(2)}) copy-start(bf16[2,16,2048]{2,1,0:T(8,128)(2,1)} %param.17) | copy-start | bytes 393220
  4.1 23.9 %collective-permute-start.4 = (bf16[1024,2304]{1,0:T(8,128)(2,1)S(1)}, bf16[1024,2304]{1,0:T(8,128)(2,1)S(1)}, u32[]{:S(2)}, u32[]{:S(2)}) collective-permute-start(bf16[1024,2304]{1,0:T(8,128)(2,1)S(1)} %get-tuple-element.56.refs_8_.refs_6_.refs_0_), channel_id=1, source_target_pairs={{0,1},{1,0},{2,3},{3,2},{4,5},{5,4},{6,7},{7,6},{8,9},{9,8},{10,11... | collective-permute-start | bytes 14155784 | tf_op jit(solution)/shard_map/ppermute | solution.py:354
  4.6 9.7 %collective-permute-start.2 = (bf16[64,2048]{1,0:T(8,128)(2,1)S(1)}, bf16[64,2048]{1,0:T(8,128)(2,1)S(1)}, u32[]{:S(2)}, u32[]{:S(2)}) collective-permute-start(bf16[64,2048]{1,0:T(8,128)(2,1)S(1)} %get-tuple-element.54.refs_5_), channel_id=1, source_target_pairs={{0,4},{4,8},{8,12},{12,14},{14,10},{10,6},{6,2},{2,0},{1,5},{5,9},... | collective-permute-start | bytes 786440 | tf_op jit(solution)/shard_map/ppermute | solution.py:393
  7.2 9.1 %collective-permute-start.3 = (bf16[64,2048]{1,0:T(8,128)(2,1)S(1)}, bf16[64,2048]{1,0:T(8,128)(2,1)S(1)}, u32[]{:S(2)}, u32[]{:S(2)}) collective-permute-start(bf16[64,2048]{1,0:T(8,128)(2,1)S(1)} %get-tuple-element.54.refs_5_), channel_id=1, source_target_pairs={{4,0},{8,4},{12,8},{14,12},{10,14},{6,10},{2,6},{0,2},{5,1},{9,5},... | collective-permute-start | bytes 786440 | tf_op jit(solution)/shard_map/ppermute | solution.py:394
  7.2 13.0 %collective-permute-start = (bf16[64,2176]{1,0:T(8,128)(2,1)S(1)}, bf16[64,2176]{1,0:T(8,128)(2,1)S(1)}, u32[]{:S(2)}, u32[]{:S(2)}) collective-permute-start(bf16[64,2176]{1,0:T(8,128)(2,1)S(1)} %get-tuple-element.53.refs_2_), channel_id=1, source_target_pairs={{0,4},{4,8},{8,12},{12,14},{14,10},{10,6},{6,2},{2,0},{1,5},{5,9},... | collective-permute-start | bytes 835592 | tf_op jit(solution)/shard_map/ppermute | solution.py:393
  9.3 13.1 %collective-permute-start.1 = (bf16[64,2176]{1,0:T(8,128)(2,1)S(1)}, bf16[64,2176]{1,0:T(8,128)(2,1)S(1)}, u32[]{:S(2)}, u32[]{:S(2)}) collective-permute-start(bf16[64,2176]{1,0:T(8,128)(2,1)S(1)} %get-tuple-element.53.refs_2_), channel_id=1, source_target_pairs={{4,0},{8,4},{12,8},{14,12},{10,14},{6,10},{2,6},{0,2},{5,1},{9,5},... | collective-permute-start | bytes 835592 | tf_op jit(solution)/shard_map/ppermute | solution.py:394
  14.3 11.6 %collective-permute-start.7 = (bf16[64,2048]{1,0:T(8,128)(2,1)S(1)}, bf16[64,2048]{1,0:T(8,128)(2,1)S(1)}, u32[]{:S(2)}, u32[]{:S(2)}) collective-permute-start(bf16[64,2048]{1,0:T(8,128)(2,1)S(1)} %collective-permute-done.2.refs_3_), channel_id=1, source_target_pairs={{0,4},{4,8},{8,12},{12,14},{14,10},{10,6},{6,2},{2,0},{1,5},{5,9},... | collective-permute-start | bytes 786440 | tf_op jit(solution)/shard_map/ppermute | solution.py:393
  16.4 11.6 %collective-permute-start.8 = (bf16[64,2048]{1,0:T(8,128)(2,1)S(1)}, bf16[64,2048]{1,0:T(8,128)(2,1)S(1)}, u32[]{:S(2)}, u32[]{:S(2)}) collective-permute-start(bf16[64,2048]{1,0:T(8,128)(2,1)S(1)} %collective-permute-done.3.refs_4_), channel_id=1, source_target_pairs={{4,0},{8,4},{12,8},{14,12},{10,14},{6,10},{2,6},{0,2},{5,1},{9,5},... | collective-permute-start | bytes 786440 | tf_op jit(solution)/shard_map/ppermute | solution.py:394
  20.3 12.3 %collective-permute-start.5 = (bf16[64,2176]{1,0:T(8,128)(2,1)S(1)}, bf16[64,2176]{1,0:T(8,128)(2,1)S(1)}, u32[]{:S(2)}, u32[]{:S(2)}) collective-permute-start(bf16[64,2176]{1,0:T(8,128)(2,1)S(1)} %collective-permute-done.refs_0_), channel_id=1, source_target_pairs={{0,4},{4,8},{8,12},{12,14},{14,10},{10,6},{6,2},{2,0},{1,5},{5,9},... | collective-permute-start | bytes 835592 | tf_op jit(solution)/shard_map/ppermute | solution.py:393
  22.4 12.3 %collective-permute-start.6 = (bf16[64,2176]{1,0:T(8,128)(2,1)S(1)}, bf16[64,2176]{1,0:T(8,128)(2,1)S(1)}, u32[]{:S(2)}, u32[]{:S(2)}) collective-permute-start(bf16[64,2176]{1,0:T(8,128)(2,1)S(1)} %collective-permute-done.1.refs_1_), channel_id=1, source_target_pairs={{4,0},{8,4},{12,8},{14,12},{10,14},{6,10},{2,6},{0,2},{5,1},{9,5},... | collective-permute-start | bytes 835592 | tf_op jit(solution)/shard_map/ppermute | solution.py:394
  25.9 11.6 %collective-permute-start.11 = (bf16[64,2048]{1,0:T(8,128)(2,1)S(1)}, bf16[64,2048]{1,0:T(8,128)(2,1)S(1)}, u32[]{:S(2)}, u32[]{:S(2)}) collective-permute-start(bf16[64,2048]{1,0:T(8,128)(2,1)S(1)} %collective-permute-done.7.refs_2_), channel_id=1, source_target_pairs={{0,4},{4,8},{8,12},{12,14},{14,10},{10,6},{6,2},{2,0},{1,5},{5,9},... | collective-permute-start | bytes 786440 | tf_op jit(solution)/shard_map/ppermute | solution.py:393
  28.0 11.6 %collective-permute-start.12 = (bf16[64,2048]{1,0:T(8,128)(2,1)S(1)}, bf16[64,2048]{1,0:T(8,128)(2,1)S(1)}, u32[]{:S(2)}, u32[]{:S(2)}) collective-permute-start(bf16[64,2048]{1,0:T(8,128)(2,1)S(1)} %collective-permute-done.8.refs_3_), channel_id=1, source_target_pairs={{4,0},{8,4},{12,8},{14,12},{10,14},{6,10},{2,6},{0,2},{5,1},{9,5},... | collective-permute-start | bytes 786440 | tf_op jit(solution)/shard_map/ppermute | solution.py:394
  32.6 12.5 %collective-permute-start.9 = (bf16[64,2176]{1,0:T(8,128)(2,1)S(1)}, bf16[64,2176]{1,0:T(8,128)(2,1)S(1)}, u32[]{:S(2)}, u32[]{:S(2)}) collective-permute-start(bf16[64,2176]{1,0:T(8,128)(2,1)S(1)} %collective-permute-done.5.refs_0_), channel_id=1, source_target_pairs={{0,4},{4,8},{8,12},{12,14},{14,10},{10,6},{6,2},{2,0},{1,5},{5,9},... | collective-permute-start | bytes 835592 | tf_op jit(solution)/shard_map/ppermute | solution.py:393
  34.7 10.8 %collective-permute-start.10 = (bf16[64,2176]{1,0:T(8,128)(2,1)S(1)}, bf16[64,2176]{1,0:T(8,128)(2,1)S(1)}, u32[]{:S(2)}, u32[]{:S(2)}) collective-permute-start(bf16[64,2176]{1,0:T(8,128)(2,1)S(1)} %collective-permute-done.6.refs_1_), channel_id=1, source_target_pairs={{4,0},{8,4},{12,8},{14,12},{10,14},{6,10},{2,6},{0,2},{5,1},{9,5},... | collective-permute-start | bytes 835592 | tf_op jit(solution)/shard_map/ppermute | solution.py:394
  39.6 11.0 %collective-permute-start.19 = (bf16[32,2048]{1,0:T(8,128)(2,1)S(1)}, bf16[32,2048]{1,0:T(8,128)(2,1)S(1)}, u32[]{:S(2)}, u32[]{:S(2)}) collective-permute-start(bf16[32,2048]{1,0:T(8,128)(2,1)S(1)} %get-tuple-element.85), channel_id=1, source_target_pairs={{0,4},{4,8},{8,12},{12,14},{14,10},{10,6},{6,2},{2,0},{1,5},{5,9},... | collective-permute-start | bytes 393224 | tf_op jit(solution)/shard_map/ppermute | solution.py:412
  41.2 11.2 %collective-permute-start.20 = (bf16[32,2048]{1,0:T(8,128)(2,1)S(1)}, bf16[32,2048]{1,0:T(8,128)(2,1)S(1)}, u32[]{:S(2)}, u32[]{:S(2)}) collective-permute-start(bf16[32,2048]{1,0:T(8,128)(2,1)S(1)} %get-tuple-element.86), channel_id=1, source_target_pairs={{4,0},{8,4},{12,8},{14,12},{10,14},{6,10},{2,6},{0,2},{5,1},{9,5},... | collective-permute-start | bytes 393224 | tf_op jit(solution)/shard_map/ppermute | solution.py:413
  45.6 6.9 %collective-permute-start.17 = (bf16[32,2176]{1,0:T(8,128)(2,1)S(1)}, bf16[32,2176]{1,0:T(8,128)(2,1)S(1)}, u32[]{:S(2)}, u32[]{:S(2)}) collective-permute-start(bf16[32,2176]{1,0:T(8,128)(2,1)S(1)} %get-tuple-element.81), channel_id=1, source_target_pairs={{0,4},{4,8},{8,12},{12,14},{14,10},{10,6},{6,2},{2,0},{1,5},{5,9},... | collective-permute-start | bytes 417800 | tf_op jit(solution)/shard_map/ppermute | solution.py:412
  47.2 6.3 %collective-permute-start.18 = (bf16[32,2176]{1,0:T(8,128)(2,1)S(1)}, bf16[32,2176]{1,0:T(8,128)(2,1)S(1)}, u32[]{:S(2)}, u32[]{:S(2)}) collective-permute-start(bf16[32,2176]{1,0:T(8,128)(2,1)S(1)} %get-tuple-element.82), channel_id=1, source_target_pairs={{4,0},{8,4},{12,8},{14,12},{10,14},{6,10},{2,6},{0,2},{5,1},{9,5},... | collective-permute-start | bytes 417800 | tf_op jit(solution)/shard_map/ppermute | solution.py:413
  50.4 8.8 %collective-permute-start.13 = (bf16[64,2048]{1,0:T(8,128)(2,1)S(1)}, bf16[64,2048]{1,0:T(8,128)(2,1)S(1)}, u32[]{:S(2)}, u32[]{:S(2)}) collective-permute-start(bf16[64,2048]{1,0:T(8,128)(2,1)S(1)} %get-tuple-element.75), channel_id=1, source_target_pairs={{4,0},{8,4},{12,8},{14,12},{10,14},{6,10},{2,6},{0,2},{5,1},{9,5},... | collective-permute-start | bytes 786440 | tf_op jit(solution)/shard_map/ppermute | solution.py:373
  50.6 8.6 %collective-permute-start.14 = (bf16[64,2048]{1,0:T(8,128)(2,1)S(1)}, bf16[64,2048]{1,0:T(8,128)(2,1)S(1)}, u32[]{:S(2)}, u32[]{:S(2)}) collective-permute-start(bf16[64,2048]{1,0:T(8,128)(2,1)S(1)} %get-tuple-element.76), channel_id=1, source_target_pairs={{0,4},{4,8},{8,12},{12,14},{14,10},{10,6},{6,2},{2,0},{1,5},{5,9},... | collective-permute-start | bytes 786440 | tf_op jit(solution)/shard_map/ppermute | solution.py:373
  56.6 8.4 %collective-permute-start.21 = (bf16[64,1024]{1,0:T(8,128)(2,1)S(1)}, bf16[64,1024]{1,0:T(8,128)(2,1)S(1)}, u32[]{:S(2)}, u32[]{:S(2)}) collective-permute-start(bf16[64,1024]{1,0:T(8,128)(2,1)S(1)} %get-tuple-element.89), channel_id=1, source_target_pairs={{0,12},{4,6},{8,10},{12,0},{14,2},{10,8},{6,4},{2,14},{1,13},{5,7}... | collective-permute-start | bytes 393224 | tf_op jit(solution)/shard_map/ppermute | solution.py:431
  59.2 8.5 %collective-permute-start.15 = (bf16[64,1024]{1,0:T(8,128)(2,1)S(1)}, bf16[64,1024]{1,0:T(8,128)(2,1)S(1)}, u32[]{:S(2)}, u32[]{:S(2)}) collective-permute-start(bf16[64,1024]{1,0:T(8,128)(2,1)S(1)} %get-tuple-element.77), channel_id=1, source_target_pairs={{4,0},{8,4},{12,8},{14,12},{10,14},{6,10},{2,6},{0,2},{5,1},{9,5},... | collective-permute-start | bytes 393224 | tf_op jit(solution)/shard_map/ppermute | solution.py:373
  59.7 8.0 %collective-permute-start.16 = (bf16[64,1024]{1,0:T(8,128)(2,1)S(1)}, bf16[64,1024]{1,0:T(8,128)(2,1)S(1)}, u32[]{:S(2)}, u32[]{:S(2)}) collective-permute-start(bf16[64,1024]{1,0:T(8,128)(2,1)S(1)} %get-tuple-element.78), channel_id=1, source_target_pairs={{0,4},{4,8},{8,12},{12,14},{14,10},{10,6},{6,2},{2,0},{1,5},{5,9},... | collective-permute-start | bytes 393224 | tf_op jit(solution)/shard_map/ppermute | solution.py:373
  61.4 8.5 %collective-permute-start.26 = (bf16[64,1024]{1,0:T(8,128)(2,1)S(1)}, bf16[64,1024]{1,0:T(8,128)(2,1)S(1)}, u32[]{:S(2)}, u32[]{:S(2)}) collective-permute-start(bf16[64,1024]{1,0:T(8,128)(2,1)S(1)} %get-tuple-element.94), channel_id=1, source_target_pairs={{0,12},{4,6},{8,10},{12,0},{14,2},{10,8},{6,4},{2,14},{1,13},{5,7}... | collective-permute-start | bytes 393224 | tf_op jit(solution)/shard_map/ppermute | solution.py:431
  63.8 6.8 %collective-permute-start.24 = (bf16[64,1024]{1,0:T(8,128)(2,1)S(1)}, bf16[64,1024]{1,0:T(8,128)(2,1)S(1)}, u32[]{:S(2)}, u32[]{:S(2)}) collective-permute-start(bf16[64,1024]{1,0:T(8,128)(2,1)S(1)} %get-tuple-element.92), channel_id=1, source_target_pairs={{4,0},{8,4},{12,8},{14,12},{10,14},{6,10},{2,6},{0,2},{5,1},{9,5},... | collective-permute-start | bytes 393224 | tf_op jit(solution)/shard_map/ppermute | solution.py:373
  65.0 5.6 %collective-permute-start.25 = (bf16[64,1024]{1,0:T(8,128)(2,1)S(1)}, bf16[64,1024]{1,0:T(8,128)(2,1)S(1)}, u32[]{:S(2)}, u32[]{:S(2)}) collective-permute-start(bf16[64,1024]{1,0:T(8,128)(2,1)S(1)} %get-tuple-element.93), channel_id=1, source_target_pairs={{0,4},{4,8},{8,12},{12,14},{14,10},{10,6},{6,2},{2,0},{1,5},{5,9},... | collective-permute-start | bytes 393224 | tf_op jit(solution)/shard_map/ppermute | solution.py:373
  67.8 5.0 %collective-permute-start.29 = (f32[32,1216]{1,0:T(8,128)S(1)}, f32[32,1216]{1,0:T(8,128)S(1)}, u32[]{:S(2)}, u32[]{:S(2)}) collective-permute-start(f32[32,1216]{1,0:T(8,128)S(1)} %get-tuple-element.100), channel_id=1, source_target_pairs={{0,1},{1,0},{2,3},{3,2},{4,5},{5,4},{6,7},{7,6},{8,9},{9,8},{10,11... | collective-permute-start | bytes 466952 | tf_op jit(solution)/shard_map/ppermute | solution.py:464
  67.9 6.3 %collective-permute-start.22 = (bf16[64,1024]{1,0:T(8,128)(2,1)S(1)}, bf16[64,1024]{1,0:T(8,128)(2,1)S(1)}, u32[]{:S(2)}, u32[]{:S(2)}) collective-permute-start(bf16[64,1024]{1,0:T(8,128)(2,1)S(1)} %get-tuple-element.90), channel_id=1, source_target_pairs={{4,0},{8,4},{12,8},{14,12},{10,14},{6,10},{2,6},{0,2},{5,1},{9,5},... | collective-permute-start | bytes 393224 | tf_op jit(solution)/shard_map/ppermute | solution.py:373
  69.8 5.7 %collective-permute-start.23 = (bf16[64,1024]{1,0:T(8,128)(2,1)S(1)}, bf16[64,1024]{1,0:T(8,128)(2,1)S(1)}, u32[]{:S(2)}, u32[]{:S(2)}) collective-permute-start(bf16[64,1024]{1,0:T(8,128)(2,1)S(1)} %get-tuple-element.91), channel_id=1, source_target_pairs={{0,4},{4,8},{8,12},{12,14},{14,10},{10,6},{6,2},{2,0},{1,5},{5,9},... | collective-permute-start | bytes 393224 | tf_op jit(solution)/shard_map/ppermute | solution.py:373
  70.7 6.0 %collective-permute-start.27 = (bf16[64,1024]{1,0:T(8,128)(2,1)S(1)}, bf16[64,1024]{1,0:T(8,128)(2,1)S(1)}, u32[]{:S(2)}, u32[]{:S(2)}) collective-permute-start(bf16[64,1024]{1,0:T(8,128)(2,1)S(1)} %get-tuple-element.95), channel_id=1, source_target_pairs={{4,0},{8,4},{12,8},{14,12},{10,14},{6,10},{2,6},{0,2},{5,1},{9,5},... | collective-permute-start | bytes 393224 | tf_op jit(solution)/shard_map/ppermute | solution.py:373
  72.4 5.0 %collective-permute-start.28 = (bf16[64,1024]{1,0:T(8,128)(2,1)S(1)}, bf16[64,1024]{1,0:T(8,128)(2,1)S(1)}, u32[]{:S(2)}, u32[]{:S(2)}) collective-permute-start(bf16[64,1024]{1,0:T(8,128)(2,1)S(1)} %get-tuple-element.96), channel_id=1, source_target_pairs={{0,4},{4,8},{8,12},{12,14},{14,10},{10,6},{6,2},{2,0},{1,5},{5,9},... | collective-permute-start | bytes 393224 | tf_op jit(solution)/shard_map/ppermute | solution.py:373

commit v16 on v15

--- a/solution.py
+++ b/solution.py
@@ -145,14 +145,9 @@
 
 
 def prepare_kernel(plan, *refs):
-    raw_refs, refs = refs[:3], refs[3:]
-    out_grad_ref, ids_ref, route_ref, factor_ref = refs[:4]
-    tokens_ref, refs = refs[4], refs[5:]
-    packed_ref, grads_ref, tokens_held_ref, factor_in_ref, ids_held, sems = refs
+    raw_refs, factor_ref, packed_ref, factor_in_ref, sems = refs[:3], *refs[3:]
     width, rank, cuts = plan.hidden_width, plan.rank, plan.cuts
-    pairs = [(ids_ref, ids_held)]
-    pairs.append((out_grad_ref, grads_ref))
-    pairs.append((tokens_ref, tokens_held_ref.at[:, : plan.model_width]))
+    pairs = []
     for kind in range(3):
         for expert in range(plan.experts):
             at = kind * plan.wide + expert * width
@@ -177,17 +172,21 @@
                 factor_in_ref[
                     expert * rank : (expert + 1) * rank, other * width : (other + 1) * width
                 ] = jnp.zeros((rank, width), bf16)
-    copies[0].wait()
-    rows, lanes = grads_ref.shape[0], tokens_held_ref.shape[1] - plan.model_width
+    for copy in copies:
+        copy.wait()
+
+
+def tokens_kernel(plan, tokens_ref, ids_ref, route_ref, held_ref, sem):
+    copy = pltpu.make_async_copy(tokens_ref, held_ref.at[:, : plan.model_width], sem)
+    copy.start()
+    rows, lanes = held_ref.shape[0], held_ref.shape[1] - plan.model_width
     expert_at = lax.broadcasted_iota(jnp.int32, (lanes, rows), 0)
-    ids, route = ids_held[...], route_ref[...]
+    ids, route = ids_ref[...], route_ref[...].astype(f32)
     dense = jnp.zeros((lanes, rows), f32)
     for k in range(ids.shape[0]):
         dense = jnp.where(ids[k : k + 1, :] == expert_at, route[k : k + 1, :], dense)
-    dense = dense.T.astype(bf16)
-    tokens_held_ref[:, plan.model_width :] = dense
-    for copy in copies[1:]:
-        copy.wait()
+    held_ref[:, plan.model_width :] = dense.T.astype(bf16)
+    copy.wait()
 
 
 def add_kernel(blocks, skip, *refs):
@@ -328,28 +327,30 @@
     wide, ranks = plan.wide, plan.ranks
 
     lanes = -(-expert_total // lane_count) * lane_count
-    mine, grads, tokens_held, factor_in = pl.pallas_call(
+    mine, factor_in = pl.pallas_call(
         functools.partial(prepare_kernel, plan),
         out_shape=(
             jax.ShapeDtypeStruct((depth, 3 * wide), bf16),
-            jax.ShapeDtypeStruct((token_count, model_width), bf16),
-            jax.ShapeDtypeStruct((token_count, model_width + lanes), bf16),
             jax.ShapeDtypeStruct((ranks, wide), bf16),
         ),
-        in_specs=[pl.BlockSpec(memory_space=pltpu.HBM)] * 5
-        + [pl.BlockSpec(memory_space=pltpu.VMEM)]
-        + [pl.BlockSpec(memory_space=pltpu.HBM)] * 2,
-        out_specs=(pl.BlockSpec(memory_space=pltpu.VMEM),) * 4,
-        scratch_shapes=[
-            pltpu.VMEM(expert_ids.shape[::-1], jnp.int32),
-            pltpu.SemaphoreType.DMA((3 + (3 * plan.cuts + 1) * local_count,)),
+        in_specs=[pl.BlockSpec(memory_space=pltpu.HBM)] * 4,
+        out_specs=(pl.BlockSpec(memory_space=pltpu.VMEM),) * 2,
+        scratch_shapes=[pltpu.SemaphoreType.DMA(((3 * plan.cuts + 1) * local_count,))],
+        compiler_params=pltpu.CompilerParams(vmem_limit_bytes=16 * 1024 * 1024),
+    )(*in_hbm(gate_weight, up_weight, down_weight, adapter_in))
+    tokens_held = pl.pallas_call(
+        functools.partial(tokens_kernel, plan),
+        out_shape=jax.ShapeDtypeStruct((token_count, model_width + lanes), bf16),
+        in_specs=[
+            pl.BlockSpec(memory_space=pltpu.HBM),
+            pl.BlockSpec(memory_space=pltpu.VMEM),
+            pl.BlockSpec(memory_space=pltpu.VMEM),
         ],
+        out_specs=pl.BlockSpec(memory_space=pltpu.VMEM),
+        scratch_shapes=[pltpu.SemaphoreType.DMA],
         compiler_params=pltpu.CompilerParams(vmem_limit_bytes=16 * 1024 * 1024),
-    )(
-        *in_hbm(gate_weight, up_weight, down_weight, out_grad, expert_ids.T),
-        route_weight.T.astype(f32),
-        *in_hbm(adapter_in, tokens),
-    )
+    )(*in_hbm(tokens), expert_ids.T, route_weight.T)
+    grads = out_grad
     if parts == 2:
         weights = [mine, lax.ppermute(mine, "dp", swap)]
     else:

time: 78.3 us -> 77.6 us (level)
  waiting for transfers between devices: 24.4 us -> 23.3 us
  Pallas kernels: 20.4 us -> 21.3 us
    ppermute x8, waiting for transfers between devices: 13.5 us -> 12.4 us  [per_device(): lax.ppermute(x, 'expert', forward)]
    pallas_call x0 -> x1, Pallas kernels: none -> 0.96 us  [per_device(): pl.pallas_call(functools.partial(tokens_kernel, plan), out_shape=jax.Shap...]
  transfers between devices with their start and end apart: 30 -> 30, of which waited for: 15 -> 15; matrix products, arithmetic and copies ran while one was open for 0% -> 0% of each run, Pallas kernels for 22% -> 23%
where the time goes in v16:
time: 77.6 us; the launch traced here: 77.4 us
  starting transfers between devices  32 us (41%)
  waiting for transfers between devices  23.3 us (30%)
  Pallas kernels  21.3 us (27%)
  between operations  0.79 us (1%)
    ppermute x8, starting transfers between devices, per_device(): lax.ppermute(x, 'expert', forward)  16.2 us
    pallas_call x4, Pallas kernels, expert_call(): pl.pallas_call(functools.partial(whole_kernel, plan, len(pieces), blocks,...  13.9 us
    ppermute x8, waiting for transfers between devices, per_device(): lax.ppermute(x, 'expert', forward)  12.4 us
    ppermute x10, starting transfers between devices, send(): return lax.ppermute(value, 'expert', ways[way][1])  9.35 us
    ppermute x10, waiting for transfers between devices, send(): return lax.ppermute(value, 'expert', ways[way][1])  6.25 us
    ppermute x2, starting transfers between devices, per_device(): skipped = [lax.ppermute(value, 'expert', pairs) for value in outs[2:]]  4.99 us
    pallas_call x1, Pallas kernels, per_device(): pl.pallas_call(functools.partial(prepare_kernel, plan), out_shape=(jax.Sh...  2.67 us
    pallas_call x5, Pallas kernels, simple_call(): pl.pallas_call(kernel, out_shape=tuple((jax.ShapeDtypeStruct(shape, dtype...  2.64 us
  transfers between devices with their start and end apart: 30, of which 15 were waited for; matrix products, arithmetic and copies ran while one was open for 0% of the time, Pallas kernels for 23%

profile of v16, /device:TPU:0, one launch (start us, length us, event | category | flops | bytes accessed | tf_op | source)
XLA Modules:
  0.0 77.4 jit_solution(13357626544532338222)
XLA Ops:
  0.7 2.7 %shard_map.113 = (bf16[1024,2304]{1,0:T(8,128)(2,1)S(1)}, bf16[32,768]{1,0:T(8,128)(2,1)S(1)}) custom-call(bf16[2,1024,384]{2,1,0:T(8,128)(2,1)} %refs_0_.1, bf16[2,1024,384]{2,1,0:T(8,128)(2,1)} %refs_1_.1, bf16[2,1024,384]{2,1,0:T(8,128)(2,1)} %refs_2_.1, bf16[2,16,384]{2,1,0:T(8,128)(2,1)} %refs_3_.1), custom_call_target="tpu_custom_call" | custom-call | tf_op jit(solution)/shard_map/pallas_call | solution.py:330
  3.4 0.5 collective-permute-start.4
  3.9 2.6 %collective-permute-start.2 = (bf16[64,2048]{1,0:T(8,128)(2,1)S(1)}, bf16[64,2048]{1,0:T(8,128)(2,1)S(1)}, u32[]{:S(2)}, u32[]{:S(2)}) collective-permute-start(bf16[64,2048]{1,0:T(8,128)(2,1)S(1)} %copy-done.1), channel_id=1, source_target_pairs={{0,4},{4,8},{8,12},{12,14},{14,10},{10,6},{6,2},{2,0},{1,5},{5,9},... | collective-permute-start | bytes 786440 | tf_op jit(solution)/shard_map/ppermute | solution.py:394
  6.5 1.0 %shard_map.112.refs_2_ = bf16[64,2176]{1,0:T(8,128)(2,1)S(1)} custom-call(bf16[64,2048]{1,0:T(8,128)(2,1)} %tokens_ref.1, s32[8,64]{1,0:T(8,128)S(1)} %bitcast.7, bf16[8,64]{1,0:T(8,128)(2,1)S(1)} %bitcast.8), custom_call_target="tpu_custom_call" | custom-call | tf_op jit(solution)/shard_map/pallas_call | solution.py:341
  7.5 2.1 %collective-permute-start = (bf16[64,2176]{1,0:T(8,128)(2,1)S(1)}, bf16[64,2176]{1,0:T(8,128)(2,1)S(1)}, u32[]{:S(2)}, u32[]{:S(2)}) collective-permute-start(bf16[64,2176]{1,0:T(8,128)(2,1)S(1)} %shard_map.112.refs_2_), channel_id=1, source_target_pairs={{0,4},{4,8},{8,12},{12,14},{14,10},{10,6},{6,2},{2,0},{1,5},{5,9},... | collective-permute-start | bytes 835592 | tf_op jit(solution)/shard_map/ppermute | solution.py:394
  9.6 4.0 %collective-permute-done.2.refs_3_ = bf16[64,2048]{1,0:T(8,128)(2,1)S(1)} collective-permute-done((bf16[64,2048]{1,0:T(8,128)(2,1)S(1)}, bf16[64,2048]{1,0:T(8,128)(2,1)S(1)}, u32[]{:S(2)}, u32[]{:S(2)}) %collective-permute-start.2) | collective-permute-done | bytes 262176 | tf_op jit(solution)/shard_map/ppermute | solution.py:394
  13.6 2.0 %collective-permute-start.7 = (bf16[64,2048]{1,0:T(8,128)(2,1)S(1)}, bf16[64,2048]{1,0:T(8,128)(2,1)S(1)}, u32[]{:S(2)}, u32[]{:S(2)}) collective-permute-start(bf16[64,2048]{1,0:T(8,128)(2,1)S(1)} %collective-permute-done.2.refs_3_), channel_id=1, source_target_pairs={{0,4},{4,8},{8,12},{12,14},{14,10},{10,6},{6,2},{2,0},{1,5},{5,9},... | collective-permute-start | bytes 786440 | tf_op jit(solution)/shard_map/ppermute | solution.py:394
  15.7 3.9 %collective-permute-done.refs_0_ = bf16[64,2176]{1,0:T(8,128)(2,1)S(1)} collective-permute-done((bf16[64,2176]{1,0:T(8,128)(2,1)S(1)}, bf16[64,2176]{1,0:T(8,128)(2,1)S(1)}, u32[]{:S(2)}, u32[]{:S(2)}) %collective-permute-start) | collective-permute-done | bytes 278560 | tf_op jit(solution)/shard_map/ppermute | solution.py:394
  19.6 2.0 %collective-permute-start.5 = (bf16[64,2176]{1,0:T(8,128)(2,1)S(1)}, bf16[64,2176]{1,0:T(8,128)(2,1)S(1)}, u32[]{:S(2)}, u32[]{:S(2)}) collective-permute-start(bf16[64,2176]{1,0:T(8,128)(2,1)S(1)} %collective-permute-done.refs_0_), channel_id=1, source_target_pairs={{0,4},{4,8},{8,12},{12,14},{14,10},{10,6},{6,2},{2,0},{1,5},{5,9},... | collective-permute-start | bytes 835592 | tf_op jit(solution)/shard_map/ppermute | solution.py:394
  21.6 3.5 %collective-permute-done.7.refs_2_ = bf16[64,2048]{1,0:T(8,128)(2,1)S(1)} collective-permute-done((bf16[64,2048]{1,0:T(8,128)(2,1)S(1)}, bf16[64,2048]{1,0:T(8,128)(2,1)S(1)}, u32[]{:S(2)}, u32[]{:S(2)}) %collective-permute-start.7) | collective-permute-done | bytes 262176 | tf_op jit(solution)/shard_map/ppermute | solution.py:394
  25.2 2.0 %collective-permute-start.11 = (bf16[64,2048]{1,0:T(8,128)(2,1)S(1)}, bf16[64,2048]{1,0:T(8,128)(2,1)S(1)}, u32[]{:S(2)}, u32[]{:S(2)}) collective-permute-start(bf16[64,2048]{1,0:T(8,128)(2,1)S(1)} %collective-permute-done.7.refs_2_), channel_id=1, source_target_pairs={{0,4},{4,8},{8,12},{12,14},{14,10},{10,6},{6,2},{2,0},{1,5},{5,9},... | collective-permute-start | bytes 786440 | tf_op jit(solution)/shard_map/ppermute | solution.py:394
  27.3 4.6 %shard_map.114 = (f32[192,2048]{1,0:T(8,128)S(1)}, f32[32,768]{1,0:T(8,128)S(1)}, f32[32,2048]{1,0:T(8,128)S(1)}) custom-call(bf16[64,2176]{1,0:T(8,128)(2,1)S(1)} %collective-permute-done.refs_0_, bf16[64,2176]{1,0:T(8,128)(2,1)S(1)} %collective-permute-done.1.refs_1_, bf16[64,2176]{1,0:T(8,128)(2,1)S(1)} %shard_map.112.refs_2_, ...), custom_call_target="tpu_custom_call" | custom-call | flops 3019898880 | bytes 11599872 | tf_op jit(solution)/shard_map/pallas_call | solution.py:284
  31.9 2.1 %collective-permute-start.9 = (bf16[64,2176]{1,0:T(8,128)(2,1)S(1)}, bf16[64,2176]{1,0:T(8,128)(2,1)S(1)}, u32[]{:S(2)}, u32[]{:S(2)}) collective-permute-start(bf16[64,2176]{1,0:T(8,128)(2,1)S(1)} %collective-permute-done.5.refs_0_), channel_id=1, source_target_pairs={{0,4},{4,8},{8,12},{12,14},{14,10},{10,6},{6,2},{2,0},{1,5},{5,9},... | collective-permute-start | bytes 835592 | tf_op jit(solution)/shard_map/ppermute | solution.py:394
  34.0 1.8 %shard_map.116 = (bf16[1536,1024]{1,0:T(8,128)(2,1)S(1)}, bf16[1536,1024]{1,0:T(8,128)(2,1)S(1)}) custom-call(bf16[1024,2304]{1,0:T(8,128)(2,1)S(1)} %get-tuple-element.52.refs_8_.refs_6_.refs_0_, bf16[1024,2304]{1,0:T(8,128)(2,1)S(1)} %collective-permute-done.4.refs_9_.refs_7_.refs_1_), custom_call_target="tpu_custom_call" | custom-call | tf_op jit(solution)/shard_map/pallas_call | solution.py:268
  35.8 1.0 %collective-permute-done.11.refs_2_.first_ref = bf16[64,2048]{1,0:T(8,128)(2,1)S(1)} collective-permute-done((bf16[64,2048]{1,0:T(8,128)(2,1)S(1)}, bf16[64,2048]{1,0:T(8,128)(2,1)S(1)}, u32[]{:S(2)}, u32[]{:S(2)}) %collective-permute-start.11) | collective-permute-done | bytes 262176 | tf_op jit(solution)/shard_map/ppermute | solution.py:394
  36.8 2.1 %collective-permute-done.12.refs_3_.second_ref = bf16[64,2048]{1,0:T(8,128)(2,1)S(1)} collective-permute-done((bf16[64,2048]{1,0:T(8,128)(2,1)S(1)}, bf16[64,2048]{1,0:T(8,128)(2,1)S(1)}, u32[]{:S(2)}, u32[]{:S(2)}) %collective-permute-start.12) | collective-permute-done | bytes 262176 | tf_op jit(solution)/shard_map/ppermute | solution.py:395
  38.9 1.6 %collective-permute-start.19 = (bf16[32,2048]{1,0:T(8,128)(2,1)S(1)}, bf16[32,2048]{1,0:T(8,128)(2,1)S(1)}, u32[]{:S(2)}, u32[]{:S(2)}) collective-permute-start(bf16[32,2048]{1,0:T(8,128)(2,1)S(1)} %get-tuple-element.81), channel_id=1, source_target_pairs={{0,4},{4,8},{8,12},{12,14},{14,10},{10,6},{6,2},{2,0},{1,5},{5,9},... | collective-permute-start | bytes 393224 | tf_op jit(solution)/shard_map/ppermute | solution.py:413
  40.5 0.4 collective-permute-start.20
  40.9 3.5 %shard_map.115 = (f32[128,2048]{1,0:T(8,128)S(1)}, f32[32,768]{1,0:T(8,128)S(1)}, f32[32,2048]{1,0:T(8,128)S(1)}) custom-call(bf16[64,2176]{1,0:T(8,128)(2,1)S(1)} %collective-permute-done.5.refs_0_, bf16[64,2176]{1,0:T(8,128)(2,1)S(1)} %collective-permute-done.6.refs_1_, bf16[64,2048]{1,0:T(8,128)(2,1)S(1)} %collective-permute-done.7.refs_2_, ...), custom_call_target="tpu_custom_call" | custom-call | flops 2013265920 | bytes 11059200 | tf_op jit(solution)/shard_map/pallas_call | solution.py:284
  44.4 0.4 collective-permute-done.10.refs_1_.second_ref
  44.8 1.6 %collective-permute-start.17 = (bf16[32,2176]{1,0:T(8,128)(2,1)S(1)}, bf16[32,2176]{1,0:T(8,128)(2,1)S(1)}, u32[]{:S(2)}, u32[]{:S(2)}) collective-permute-start(bf16[32,2176]{1,0:T(8,128)(2,1)S(1)} %get-tuple-element.77), channel_id=1, source_target_pairs={{0,4},{4,8},{8,12},{12,14},{14,10},{10,6},{6,2},{2,0},{1,5},{5,9},... | collective-permute-start | bytes 417800 | tf_op jit(solution)/shard_map/ppermute | solution.py:413
  46.5 0.5 collective-permute-start.18
  46.9 2.7 %shard_map.117 = (f32[32,768]{1,0:T(8,128)S(1)}, f32[32,2048]{1,0:T(8,128)S(1)}, bf16[64,2048]{1,0:T(8,128)(2,1)S(1)}, bf16[64,2048]{1,0:T(8,128)(2,1)S(1)}) custom-call(bf16[64,2176]{1,0:T(8,128)(2,1)S(1)} %collective-permute-done.9.refs_0_.first_ref, bf16[64,2176]{1,0:T(8,128)(2,1)S(1)} %collective-permute-done.10.refs_1_.second_ref, ...), custom_call_target="tpu_custom_call" | custom-call | flops 2013265920 | bytes 17350656 | tf_op jit(solution)/shard_map/pallas_call | solution.py:284
  49.7 0.2 collective-permute-start.13
  49.9 1.9 %collective-permute-start.14 = (bf16[64,2048]{1,0:T(8,128)(2,1)S(1)}, bf16[64,2048]{1,0:T(8,128)(2,1)S(1)}, u32[]{:S(2)}, u32[]{:S(2)}) collective-permute-start(bf16[64,2048]{1,0:T(8,128)(2,1)S(1)} %get-tuple-element.72), channel_id=1, source_target_pairs={{0,4},{4,8},{8,12},{12,14},{14,10},{10,6},{6,2},{2,0},{1,5},{5,9},... | collective-permute-start | bytes 786440 | tf_op jit(solution)/shard_map/ppermute | solution.py:374
  51.7 1.0 %collective-permute-done.18.refs_1_ = bf16[32,2176]{1,0:T(8,128)(2,1)S(1)} collective-permute-done((bf16[32,2176]{1,0:T(8,128)(2,1)S(1)}, bf16[32,2176]{1,0:T(8,128)(2,1)S(1)}, u32[]{:S(2)}, u32[]{:S(2)}) %collective-permute-start.18) | collective-permute-done | bytes 139296 | tf_op jit(solution)/shard_map/ppermute | solution.py:414
  52.8 3.1 %shard_map.121 = (f32[32,768]{1,0:T(8,128)S(1)}, f32[32,2048]{1,0:T(8,128)S(1)}, bf16[64,1024]{1,0:T(8,128)(2,1)S(1)}, bf16[64,1024]{1,0:T(8,128)(2,1)S(1)}) custom-call(bf16[32,2176]{1,0:T(8,128)(2,1)S(1)} %collective-permute-done.17.refs_0_, bf16[32,2176]{1,0:T(8,128)(2,1)S(1)} %collective-permute-done.18.refs_1_, ...), custom_call_target="tpu_custom_call" | custom-call | flops 1006632960 | bytes 16809984 | tf_op jit(solution)/shard_map/pallas_call | solution.py:284
  55.9 2.6 %collective-permute-start.21 = (bf16[64,1024]{1,0:T(8,128)(2,1)S(1)}, bf16[64,1024]{1,0:T(8,128)(2,1)S(1)}, u32[]{:S(2)}, u32[]{:S(2)}) collective-permute-start(bf16[64,1024]{1,0:T(8,128)(2,1)S(1)} %get-tuple-element.85), channel_id=1, source_target_pairs={{0,12},{4,6},{8,10},{12,0},{14,2},{10,8},{6,4},{2,14},{1,13},{5,7}... | collective-permute-start | bytes 393224 | tf_op jit(solution)/shard_map/ppermute | solution.py:432
  58.5 0.5 collective-permute-start.15
  59.0 1.6 %collective-permute-start.16 = (bf16[64,1024]{1,0:T(8,128)(2,1)S(1)}, bf16[64,1024]{1,0:T(8,128)(2,1)S(1)}, u32[]{:S(2)}, u32[]{:S(2)}) collective-permute-start(bf16[64,1024]{1,0:T(8,128)(2,1)S(1)} %get-tuple-element.74), channel_id=1, source_target_pairs={{0,4},{4,8},{8,12},{12,14},{14,10},{10,6},{6,2},{2,0},{1,5},{5,9},... | collective-permute-start | bytes 393224 | tf_op jit(solution)/shard_map/ppermute | solution.py:374
  60.6 2.4 %collective-permute-start.26 = (bf16[64,1024]{1,0:T(8,128)(2,1)S(1)}, bf16[64,1024]{1,0:T(8,128)(2,1)S(1)}, u32[]{:S(2)}, u32[]{:S(2)}) collective-permute-start(bf16[64,1024]{1,0:T(8,128)(2,1)S(1)} %get-tuple-element.90), channel_id=1, source_target_pairs={{0,12},{4,6},{8,10},{12,0},{14,2},{10,8},{6,4},{2,14},{1,13},{5,7}... | collective-permute-start | bytes 393224 | tf_op jit(solution)/shard_map/ppermute | solution.py:432
  63.1 1.2 %collective-permute-start.24 = (bf16[64,1024]{1,0:T(8,128)(2,1)S(1)}, bf16[64,1024]{1,0:T(8,128)(2,1)S(1)}, u32[]{:S(2)}, u32[]{:S(2)}) collective-permute-start(bf16[64,1024]{1,0:T(8,128)(2,1)S(1)} %get-tuple-element.88), channel_id=1, source_target_pairs={{4,0},{8,4},{12,8},{14,12},{10,14},{6,10},{2,6},{0,2},{5,1},{9,5},... | collective-permute-start | bytes 393224 | tf_op jit(solution)/shard_map/ppermute | solution.py:374
  64.3 0.8 %collective-permute-start.25 = (bf16[64,1024]{1,0:T(8,128)(2,1)S(1)}, bf16[64,1024]{1,0:T(8,128)(2,1)S(1)}, u32[]{:S(2)}, u32[]{:S(2)}) collective-permute-start(bf16[64,1024]{1,0:T(8,128)(2,1)S(1)} %get-tuple-element.89), channel_id=1, source_target_pairs={{0,4},{4,8},{8,12},{12,14},{14,10},{10,6},{6,2},{2,0},{1,5},{5,9},... | collective-permute-start | bytes 393224 | tf_op jit(solution)/shard_map/ppermute | solution.py:374
  65.2 0.1 shard_map.126
  65.3 1.8 %collective-permute-done.15.refs_1_ = bf16[64,1024]{1,0:T(8,128)(2,1)S(1)} collective-permute-done((bf16[64,1024]{1,0:T(8,128)(2,1)S(1)}, bf16[64,1024]{1,0:T(8,128)(2,1)S(1)}, u32[]{:S(2)}, u32[]{:S(2)}) %collective-permute-start.15) | collective-permute-done | bytes 131104 | tf_op jit(solution)/shard_map/ppermute | solution.py:374
  67.1 0.1 shard_map.122
  67.2 0.9 %collective-permute-start.22 = (bf16[64,1024]{1,0:T(8,128)(2,1)S(1)}, bf16[64,1024]{1,0:T(8,128)(2,1)S(1)}, u32[]{:S(2)}, u32[]{:S(2)}) collective-permute-start(bf16[64,1024]{1,0:T(8,128)(2,1)S(1)} %get-tuple-element.86), channel_id=1, source_target_pairs={{4,0},{8,4},{12,8},{14,12},{10,14},{6,10},{2,6},{0,2},{5,1},{9,5},... | collective-permute-start | bytes 393224 | tf_op jit(solution)/shard_map/ppermute | solution.py:374
  68.1 1.0 %collective-permute-done.26.refs_3_ = bf16[64,1024]{1,0:T(8,128)(2,1)S(1)} collective-permute-done((bf16[64,1024]{1,0:T(8,128)(2,1)S(1)}, bf16[64,1024]{1,0:T(8,128)(2,1)S(1)}, u32[]{:S(2)}, u32[]{:S(2)}) %collective-permute-start.26) | collective-permute-done | bytes 131104 | tf_op jit(solution)/shard_map/ppermute | solution.py:432
  69.1 0.2 collective-permute-start.23
  69.3 0.6 collective-permute-done.24.refs_1_
  70.0 1.7 %collective-permute-start.27 = (bf16[64,1024]{1,0:T(8,128)(2,1)S(1)}, bf16[64,1024]{1,0:T(8,128)(2,1)S(1)}, u32[]{:S(2)}, u32[]{:S(2)}) collective-permute-start(bf16[64,1024]{1,0:T(8,128)(2,1)S(1)} %get-tuple-element.91), channel_id=1, source_target_pairs={{4,0},{8,4},{12,8},{14,12},{10,14},{6,10},{2,6},{0,2},{5,1},{9,5},... | collective-permute-start | bytes 393224 | tf_op jit(solution)/shard_map/ppermute | solution.py:374
  71.7 0.4 collective-permute-start.28
  72.1 0.7 shard_map.127
  72.8 0.8 %collective-permute-done.22.refs_1_ = bf16[64,1024]{1,0:T(8,128)(2,1)S(1)} collective-permute-done((bf16[64,1024]{1,0:T(8,128)(2,1)S(1)}, bf16[64,1024]{1,0:T(8,128)(2,1)S(1)}, u32[]{:S(2)}, u32[]{:S(2)}) %collective-permute-start.22) | collective-permute-done | bytes 131104 | tf_op jit(solution)/shard_map/ppermute | solution.py:374
  73.5 1.3 %collective-permute-done.23.refs_2_ = bf16[64,1024]{1,0:T(8,128)(2,1)S(1)} collective-permute-done((bf16[64,1024]{1,0:T(8,128)(2,1)S(1)}, bf16[64,1024]{1,0:T(8,128)(2,1)S(1)}, u32[]{:S(2)}, u32[]{:S(2)}) %collective-permute-start.23) | collective-permute-done | bytes 131104 | tf_op jit(solution)/shard_map/ppermute | solution.py:374
  74.9 1.1 %collective-permute-done.27.refs_3_ = bf16[64,1024]{1,0:T(8,128)(2,1)S(1)} collective-permute-done((bf16[64,1024]{1,0:T(8,128)(2,1)S(1)}, bf16[64,1024]{1,0:T(8,128)(2,1)S(1)}, u32[]{:S(2)}, u32[]{:S(2)}) %collective-permute-start.27) | collective-permute-done | bytes 131104 | tf_op jit(solution)/shard_map/ppermute | solution.py:374
  76.0 0.7 collective-permute-done.28.refs_4_
  76.6 0.8 %shard_map.125 = bf16[64,2048]{1,0:T(8,128)(2,1)} custom-call(f32[192,2048]{1,0:T(8,128)S(1)} %get-tuple-element.53.refs_0_, bf16[64,1024]{1,0:T(8,128)(2,1)S(1)} %collective-permute-done.22.refs_1_, bf16[64,1024]{1,0:T(8,128)(2,1)S(1)} %collective-permute-done.23.refs_2_, bf16[64,1024]{1,0:T(8,128)(2,1)S(1)} %collective-permute-done.27.refs_3_, ...), custom_call_target="tpu_custom_call" | custom-call | tf_op jit(solution)/shard_map/pallas_call | solution.py:451
  (38 shorter events, 0.5 us)
Async XLA Ops:
  0.6 3.2 %copy-start.1 = (bf16[64,2048]{1,0:T(8,128)(2,1)S(1)}, bf16[64,2048]{1,0:T(8,128)(2,1)}, u32[]{:S(2)}) copy-start(bf16[64,2048]{1,0:T(8,128)(2,1)} %refs_5_.1) | copy-start | bytes 786436
  0.6 5.9 %copy-start.2 = (s32[64,8]{0,1:T(8,128)S(1)}, s32[64,8]{0,1:T(8,128)}, u32[]{:S(2)}) copy-start(s32[64,8]{0,1:T(8,128)} %param.11) | copy-start | bytes 6148
  0.7 5.9 %copy-start.3 = (bf16[64,8]{0,1:T(8,128)(2,1)S(1)}, bf16[64,8]{0,1:T(8,128)(2,1)}, u32[]{:S(2)}) copy-start(bf16[64,8]{0,1:T(8,128)(2,1)} %param.12) | copy-start | bytes 3076
  0.7 26.6 %copy-start = (bf16[2,16,2048]{2,1,0:T(8,128)(2,1)S(1)}, bf16[2,16,2048]{2,1,0:T(8,128)(2,1)}, u32[]{:S(2)}) copy-start(bf16[2,16,2048]{2,1,0:T(8,128)(2,1)} %param.17) | copy-start | bytes 393220
  3.4 23.9 %collective-permute-start.4 = (bf16[1024,2304]{1,0:T(8,128)(2,1)S(1)}, bf16[1024,2304]{1,0:T(8,128)(2,1)S(1)}, u32[]{:S(2)}, u32[]{:S(2)}) collective-permute-start(bf16[1024,2304]{1,0:T(8,128)(2,1)S(1)} %get-tuple-element.52.refs_8_.refs_6_.refs_0_), channel_id=1, source_target_pairs={{0,1},{1,0},{2,3},{3,2},{4,5},{5,4},{6,7},{7,6},{8,9},{9,8},{10,11... | collective-permute-start | bytes 14155784 | tf_op jit(solution)/shard_map/ppermute | solution.py:355
  3.9 9.7 %collective-permute-start.2 = (bf16[64,2048]{1,0:T(8,128)(2,1)S(1)}, bf16[64,2048]{1,0:T(8,128)(2,1)S(1)}, u32[]{:S(2)}, u32[]{:S(2)}) collective-permute-start(bf16[64,2048]{1,0:T(8,128)(2,1)S(1)} %copy-done.1), channel_id=1, source_target_pairs={{0,4},{4,8},{8,12},{12,14},{14,10},{10,6},{6,2},{2,0},{1,5},{5,9},... | collective-permute-start | bytes 786440 | tf_op jit(solution)/shard_map/ppermute | solution.py:394
  6.5 9.2 %collective-permute-start.3 = (bf16[64,2048]{1,0:T(8,128)(2,1)S(1)}, bf16[64,2048]{1,0:T(8,128)(2,1)S(1)}, u32[]{:S(2)}, u32[]{:S(2)}) collective-permute-start(bf16[64,2048]{1,0:T(8,128)(2,1)S(1)} %copy-done.1), channel_id=1, source_target_pairs={{4,0},{8,4},{12,8},{14,12},{10,14},{6,10},{2,6},{0,2},{5,1},{9,5},... | collective-permute-start | bytes 786440 | tf_op jit(solution)/shard_map/ppermute | solution.py:395
  7.5 12.1 %collective-permute-start = (bf16[64,2176]{1,0:T(8,128)(2,1)S(1)}, bf16[64,2176]{1,0:T(8,128)(2,1)S(1)}, u32[]{:S(2)}, u32[]{:S(2)}) collective-permute-start(bf16[64,2176]{1,0:T(8,128)(2,1)S(1)} %shard_map.112.refs_2_), channel_id=1, source_target_pairs={{0,4},{4,8},{8,12},{12,14},{14,10},{10,6},{6,2},{2,0},{1,5},{5,9},... | collective-permute-start | bytes 835592 | tf_op jit(solution)/shard_map/ppermute | solution.py:394
  9.6 12.1 %collective-permute-start.1 = (bf16[64,2176]{1,0:T(8,128)(2,1)S(1)}, bf16[64,2176]{1,0:T(8,128)(2,1)S(1)}, u32[]{:S(2)}, u32[]{:S(2)}) collective-permute-start(bf16[64,2176]{1,0:T(8,128)(2,1)S(1)} %shard_map.112.refs_2_), channel_id=1, source_target_pairs={{4,0},{8,4},{12,8},{14,12},{10,14},{6,10},{2,6},{0,2},{5,1},{9,5},... | collective-permute-start | bytes 835592 | tf_op jit(solution)/shard_map/ppermute | solution.py:395
  13.6 11.6 %collective-permute-start.7 = (bf16[64,2048]{1,0:T(8,128)(2,1)S(1)}, bf16[64,2048]{1,0:T(8,128)(2,1)S(1)}, u32[]{:S(2)}, u32[]{:S(2)}) collective-permute-start(bf16[64,2048]{1,0:T(8,128)(2,1)S(1)} %collective-permute-done.2.refs_3_), channel_id=1, source_target_pairs={{0,4},{4,8},{8,12},{12,14},{14,10},{10,6},{6,2},{2,0},{1,5},{5,9},... | collective-permute-start | bytes 786440 | tf_op jit(solution)/shard_map/ppermute | solution.py:394
  15.7 11.6 %collective-permute-start.8 = (bf16[64,2048]{1,0:T(8,128)(2,1)S(1)}, bf16[64,2048]{1,0:T(8,128)(2,1)S(1)}, u32[]{:S(2)}, u32[]{:S(2)}) collective-permute-start(bf16[64,2048]{1,0:T(8,128)(2,1)S(1)} %collective-permute-done.3.refs_4_), channel_id=1, source_target_pairs={{4,0},{8,4},{12,8},{14,12},{10,14},{6,10},{2,6},{0,2},{5,1},{9,5},... | collective-permute-start | bytes 786440 | tf_op jit(solution)/shard_map/ppermute | solution.py:395
  19.6 12.3 %collective-permute-start.5 = (bf16[64,2176]{1,0:T(8,128)(2,1)S(1)}, bf16[64,2176]{1,0:T(8,128)(2,1)S(1)}, u32[]{:S(2)}, u32[]{:S(2)}) collective-permute-start(bf16[64,2176]{1,0:T(8,128)(2,1)S(1)} %collective-permute-done.refs_0_), channel_id=1, source_target_pairs={{0,4},{4,8},{8,12},{12,14},{14,10},{10,6},{6,2},{2,0},{1,5},{5,9},... | collective-permute-start | bytes 835592 | tf_op jit(solution)/shard_map/ppermute | solution.py:394
  21.6 12.3 %collective-permute-start.6 = (bf16[64,2176]{1,0:T(8,128)(2,1)S(1)}, bf16[64,2176]{1,0:T(8,128)(2,1)S(1)}, u32[]{:S(2)}, u32[]{:S(2)}) collective-permute-start(bf16[64,2176]{1,0:T(8,128)(2,1)S(1)} %collective-permute-done.1.refs_1_), channel_id=1, source_target_pairs={{4,0},{8,4},{12,8},{14,12},{10,14},{6,10},{2,6},{0,2},{5,1},{9,5},... | collective-permute-start | bytes 835592 | tf_op jit(solution)/shard_map/ppermute | solution.py:395
  25.2 11.6 %collective-permute-start.11 = (bf16[64,2048]{1,0:T(8,128)(2,1)S(1)}, bf16[64,2048]{1,0:T(8,128)(2,1)S(1)}, u32[]{:S(2)}, u32[]{:S(2)}) collective-permute-start(bf16[64,2048]{1,0:T(8,128)(2,1)S(1)} %collective-permute-done.7.refs_2_), channel_id=1, source_target_pairs={{0,4},{4,8},{8,12},{12,14},{14,10},{10,6},{6,2},{2,0},{1,5},{5,9},... | collective-permute-start | bytes 786440 | tf_op jit(solution)/shard_map/ppermute | solution.py:394
  27.3 11.6 %collective-permute-start.12 = (bf16[64,2048]{1,0:T(8,128)(2,1)S(1)}, bf16[64,2048]{1,0:T(8,128)(2,1)S(1)}, u32[]{:S(2)}, u32[]{:S(2)}) collective-permute-start(bf16[64,2048]{1,0:T(8,128)(2,1)S(1)} %collective-permute-done.8.refs_3_), channel_id=1, source_target_pairs={{4,0},{8,4},{12,8},{14,12},{10,14},{6,10},{2,6},{0,2},{5,1},{9,5},... | collective-permute-start | bytes 786440 | tf_op jit(solution)/shard_map/ppermute | solution.py:395
  31.9 12.5 %collective-permute-start.9 = (bf16[64,2176]{1,0:T(8,128)(2,1)S(1)}, bf16[64,2176]{1,0:T(8,128)(2,1)S(1)}, u32[]{:S(2)}, u32[]{:S(2)}) collective-permute-start(bf16[64,2176]{1,0:T(8,128)(2,1)S(1)} %collective-permute-done.5.refs_0_), channel_id=1, source_target_pairs={{0,4},{4,8},{8,12},{12,14},{14,10},{10,6},{6,2},{2,0},{1,5},{5,9},... | collective-permute-start | bytes 835592 | tf_op jit(solution)/shard_map/ppermute | solution.py:394
  34.0 10.8 %collective-permute-start.10 = (bf16[64,2176]{1,0:T(8,128)(2,1)S(1)}, bf16[64,2176]{1,0:T(8,128)(2,1)S(1)}, u32[]{:S(2)}, u32[]{:S(2)}) collective-permute-start(bf16[64,2176]{1,0:T(8,128)(2,1)S(1)} %collective-permute-done.6.refs_1_), channel_id=1, source_target_pairs={{4,0},{8,4},{12,8},{14,12},{10,14},{6,10},{2,6},{0,2},{5,1},{9,5},... | collective-permute-start | bytes 835592 | tf_op jit(solution)/shard_map/ppermute | solution.py:395
  38.9 11.0 %collective-permute-start.19 = (bf16[32,2048]{1,0:T(8,128)(2,1)S(1)}, bf16[32,2048]{1,0:T(8,128)(2,1)S(1)}, u32[]{:S(2)}, u32[]{:S(2)}) collective-permute-start(bf16[32,2048]{1,0:T(8,128)(2,1)S(1)} %get-tuple-element.81), channel_id=1, source_target_pairs={{0,4},{4,8},{8,12},{12,14},{14,10},{10,6},{6,2},{2,0},{1,5},{5,9},... | collective-permute-start | bytes 393224 | tf_op jit(solution)/shard_map/ppermute | solution.py:413
  40.5 11.2 %collective-permute-start.20 = (bf16[32,2048]{1,0:T(8,128)(2,1)S(1)}, bf16[32,2048]{1,0:T(8,128)(2,1)S(1)}, u32[]{:S(2)}, u32[]{:S(2)}) collective-permute-start(bf16[32,2048]{1,0:T(8,128)(2,1)S(1)} %get-tuple-element.82), channel_id=1, source_target_pairs={{4,0},{8,4},{12,8},{14,12},{10,14},{6,10},{2,6},{0,2},{5,1},{9,5},... | collective-permute-start | bytes 393224 | tf_op jit(solution)/shard_map/ppermute | solution.py:414
  44.8 6.9 %collective-permute-start.17 = (bf16[32,2176]{1,0:T(8,128)(2,1)S(1)}, bf16[32,2176]{1,0:T(8,128)(2,1)S(1)}, u32[]{:S(2)}, u32[]{:S(2)}) collective-permute-start(bf16[32,2176]{1,0:T(8,128)(2,1)S(1)} %get-tuple-element.77), channel_id=1, source_target_pairs={{0,4},{4,8},{8,12},{12,14},{14,10},{10,6},{6,2},{2,0},{1,5},{5,9},... | collective-permute-start | bytes 417800 | tf_op jit(solution)/shard_map/ppermute | solution.py:413
  46.5 6.3 %collective-permute-start.18 = (bf16[32,2176]{1,0:T(8,128)(2,1)S(1)}, bf16[32,2176]{1,0:T(8,128)(2,1)S(1)}, u32[]{:S(2)}, u32[]{:S(2)}) collective-permute-start(bf16[32,2176]{1,0:T(8,128)(2,1)S(1)} %get-tuple-element.78), channel_id=1, source_target_pairs={{4,0},{8,4},{12,8},{14,12},{10,14},{6,10},{2,6},{0,2},{5,1},{9,5},... | collective-permute-start | bytes 417800 | tf_op jit(solution)/shard_map/ppermute | solution.py:414
  49.7 8.8 %collective-permute-start.13 = (bf16[64,2048]{1,0:T(8,128)(2,1)S(1)}, bf16[64,2048]{1,0:T(8,128)(2,1)S(1)}, u32[]{:S(2)}, u32[]{:S(2)}) collective-permute-start(bf16[64,2048]{1,0:T(8,128)(2,1)S(1)} %get-tuple-element.71), channel_id=1, source_target_pairs={{4,0},{8,4},{12,8},{14,12},{10,14},{6,10},{2,6},{0,2},{5,1},{9,5},... | collective-permute-start | bytes 786440 | tf_op jit(solution)/shard_map/ppermute | solution.py:374
  49.9 8.6 %collective-permute-start.14 = (bf16[64,2048]{1,0:T(8,128)(2,1)S(1)}, bf16[64,2048]{1,0:T(8,128)(2,1)S(1)}, u32[]{:S(2)}, u32[]{:S(2)}) collective-permute-start(bf16[64,2048]{1,0:T(8,128)(2,1)S(1)} %get-tuple-element.72), channel_id=1, source_target_pairs={{0,4},{4,8},{8,12},{12,14},{14,10},{10,6},{6,2},{2,0},{1,5},{5,9},... | collective-permute-start | bytes 786440 | tf_op jit(solution)/shard_map/ppermute | solution.py:374
  55.9 8.4 %collective-permute-start.21 = (bf16[64,1024]{1,0:T(8,128)(2,1)S(1)}, bf16[64,1024]{1,0:T(8,128)(2,1)S(1)}, u32[]{:S(2)}, u32[]{:S(2)}) collective-permute-start(bf16[64,1024]{1,0:T(8,128)(2,1)S(1)} %get-tuple-element.85), channel_id=1, source_target_pairs={{0,12},{4,6},{8,10},{12,0},{14,2},{10,8},{6,4},{2,14},{1,13},{5,7}... | collective-permute-start | bytes 393224 | tf_op jit(solution)/shard_map/ppermute | solution.py:432
  58.5 8.5 %collective-permute-start.15 = (bf16[64,1024]{1,0:T(8,128)(2,1)S(1)}, bf16[64,1024]{1,0:T(8,128)(2,1)S(1)}, u32[]{:S(2)}, u32[]{:S(2)}) collective-permute-start(bf16[64,1024]{1,0:T(8,128)(2,1)S(1)} %get-tuple-element.73), channel_id=1, source_target_pairs={{4,0},{8,4},{12,8},{14,12},{10,14},{6,10},{2,6},{0,2},{5,1},{9,5},... | collective-permute-start | bytes 393224 | tf_op jit(solution)/shard_map/ppermute | solution.py:374
  59.0 8.1 %collective-permute-start.16 = (bf16[64,1024]{1,0:T(8,128)(2,1)S(1)}, bf16[64,1024]{1,0:T(8,128)(2,1)S(1)}, u32[]{:S(2)}, u32[]{:S(2)}) collective-permute-start(bf16[64,1024]{1,0:T(8,128)(2,1)S(1)} %get-tuple-element.74), channel_id=1, source_target_pairs={{0,4},{4,8},{8,12},{12,14},{14,10},{10,6},{6,2},{2,0},{1,5},{5,9},... | collective-permute-start | bytes 393224 | tf_op jit(solution)/shard_map/ppermute | solution.py:374
  60.6 8.5 %collective-permute-start.26 = (bf16[64,1024]{1,0:T(8,128)(2,1)S(1)}, bf16[64,1024]{1,0:T(8,128)(2,1)S(1)}, u32[]{:S(2)}, u32[]{:S(2)}) collective-permute-start(bf16[64,1024]{1,0:T(8,128)(2,1)S(1)} %get-tuple-element.90), channel_id=1, source_target_pairs={{0,12},{4,6},{8,10},{12,0},{14,2},{10,8},{6,4},{2,14},{1,13},{5,7}... | collective-permute-start | bytes 393224 | tf_op jit(solution)/shard_map/ppermute | solution.py:432
  63.1 6.8 %collective-permute-start.24 = (bf16[64,1024]{1,0:T(8,128)(2,1)S(1)}, bf16[64,1024]{1,0:T(8,128)(2,1)S(1)}, u32[]{:S(2)}, u32[]{:S(2)}) collective-permute-start(bf16[64,1024]{1,0:T(8,128)(2,1)S(1)} %get-tuple-element.88), channel_id=1, source_target_pairs={{4,0},{8,4},{12,8},{14,12},{10,14},{6,10},{2,6},{0,2},{5,1},{9,5},... | collective-permute-start | bytes 393224 | tf_op jit(solution)/shard_map/ppermute | solution.py:374
  64.3 5.6 %collective-permute-start.25 = (bf16[64,1024]{1,0:T(8,128)(2,1)S(1)}, bf16[64,1024]{1,0:T(8,128)(2,1)S(1)}, u32[]{:S(2)}, u32[]{:S(2)}) collective-permute-start(bf16[64,1024]{1,0:T(8,128)(2,1)S(1)} %get-tuple-element.89), channel_id=1, source_target_pairs={{0,4},{4,8},{8,12},{12,14},{14,10},{10,6},{6,2},{2,0},{1,5},{5,9},... | collective-permute-start | bytes 393224 | tf_op jit(solution)/shard_map/ppermute | solution.py:374
  67.1 5.0 %collective-permute-start.29 = (f32[32,1216]{1,0:T(8,128)S(1)}, f32[32,1216]{1,0:T(8,128)S(1)}, u32[]{:S(2)}, u32[]{:S(2)}) collective-permute-start(f32[32,1216]{1,0:T(8,128)S(1)} %get-tuple-element.96), channel_id=1, source_target_pairs={{0,1},{1,0},{2,3},{3,2},{4,5},{5,4},{6,7},{7,6},{8,9},{9,8},{10,11... | collective-permute-start | bytes 466952 | tf_op jit(solution)/shard_map/ppermute | solution.py:465
  67.2 6.3 %collective-permute-start.22 = (bf16[64,1024]{1,0:T(8,128)(2,1)S(1)}, bf16[64,1024]{1,0:T(8,128)(2,1)S(1)}, u32[]{:S(2)}, u32[]{:S(2)}) collective-permute-start(bf16[64,1024]{1,0:T(8,128)(2,1)S(1)} %get-tuple-element.86), channel_id=1, source_target_pairs={{4,0},{8,4},{12,8},{14,12},{10,14},{6,10},{2,6},{0,2},{5,1},{9,5},... | collective-permute-start | bytes 393224 | tf_op jit(solution)/shard_map/ppermute | solution.py:374
  69.1 5.8 %collective-permute-start.23 = (bf16[64,1024]{1,0:T(8,128)(2,1)S(1)}, bf16[64,1024]{1,0:T(8,128)(2,1)S(1)}, u32[]{:S(2)}, u32[]{:S(2)}) collective-permute-start(bf16[64,1024]{1,0:T(8,128)(2,1)S(1)} %get-tuple-element.87), channel_id=1, source_target_pairs={{0,4},{4,8},{8,12},{12,14},{14,10},{10,6},{6,2},{2,0},{1,5},{5,9},... | collective-permute-start | bytes 393224 | tf_op jit(solution)/shard_map/ppermute | solution.py:374
  70.0 6.0 %collective-permute-start.27 = (bf16[64,1024]{1,0:T(8,128)(2,1)S(1)}, bf16[64,1024]{1,0:T(8,128)(2,1)S(1)}, u32[]{:S(2)}, u32[]{:S(2)}) collective-permute-start(bf16[64,1024]{1,0:T(8,128)(2,1)S(1)} %get-tuple-element.91), channel_id=1, source_target_pairs={{4,0},{8,4},{12,8},{14,12},{10,14},{6,10},{2,6},{0,2},{5,1},{9,5},... | collective-permute-start | bytes 393224 | tf_op jit(solution)/shard_map/ppermute | solution.py:374
  71.7 5.0 %collective-permute-start.28 = (bf16[64,1024]{1,0:T(8,128)(2,1)S(1)}, bf16[64,1024]{1,0:T(8,128)(2,1)S(1)}, u32[]{:S(2)}, u32[]{:S(2)}) collective-permute-start(bf16[64,1024]{1,0:T(8,128)(2,1)S(1)} %get-tuple-element.92), channel_id=1, source_target_pairs={{0,4},{4,8},{8,12},{12,14},{14,10},{10,6},{6,2},{2,0},{1,5},{5,9},... | collective-permute-start | bytes 393224 | tf_op jit(solution)/shard_map/ppermute | solution.py:374

commit v17 on v16

--- a/solution.py
+++ b/solution.py
@@ -386,6 +386,11 @@
             held.append(x)
         return value, held
 
+    turned = simple_call(
+        functools.partial(turn_kernel, plan),
+        weights,
+        [((2 * wide, w.shape[0]), bf16) for w in weights],
+    )
     for d in range(full):
         if d > 1:
             totals, (tokens_b, tokens_a) = after(totals, behind[d][0], ahead[d][0])
@@ -394,14 +399,9 @@
         behind.append(tuple(lax.ppermute(x, "expert", forward) for x in behind[d]))
         ahead.append(tuple(lax.ppermute(x, "expert", backward) for x in ahead[d]))
         if d > 0:
-            pieces = [behind[d], ahead[d]] + ([behind[0]] if d == 1 else [])
-            rows_d, *totals = run(pieces, [], totals)
+            pieces = [behind[d], ahead[d]] + ([behind[0]] if d == full - 1 else [])
+            rows_d, *totals = run(pieces, [], totals, turned=turned if d == full - 1 else ())
             rows_at.append(rows_d)
-    turned = simple_call(
-        functools.partial(turn_kernel, plan),
-        weights,
-        [((2 * wide, w.shape[0]), bf16) for w in weights],
-    )
     if split:
         half = token_count // 2
         totals, (tokens_b, tokens_a) = after(totals, behind[full][0], ahead[full][0])
@@ -454,7 +454,7 @@
         in_specs=[pl.BlockSpec(memory_space=pltpu.VMEM)] * 5,
         out_specs=pl.BlockSpec(memory_space=pltpu.VMEM),
         compiler_params=pltpu.CompilerParams(vmem_limit_bytes=16 * 1024 * 1024),
-    )(rows_at[1], *(moving[side, way] for side in columns for way in ways))
+    )(rows_at[full - 1], *(moving[side, way] for side in columns for way in ways))
 
     narrow = hidden_width // dp_count
     if dp_count == 2:

time: 77.6 us -> 77.6 us (level)
  waiting for transfers between devices: 23.3 us -> 24.1 us
    ppermute x6, waiting for transfers between devices: 2.57 us -> 3.99 us  [per_device(): ahead.append(tuple((lax.ppermute(x, 'expert', backward) for x in ahead[d])))]
  transfers between devices with their start and end apart: 30 -> 30, of which waited for: 15 -> 15; matrix products, arithmetic and copies ran while one was open for 0% -> 0% of each run, Pallas kernels for 23% -> 22%
where the time goes in v17:
time: 77.6 us; the launch traced here: 77.4 us
  starting transfers between devices  31.9 us (41%)
  waiting for transfers between devices  24.1 us (31%)
  Pallas kernels  20.6 us (27%)
  between operations  0.79 us (1%)
    ppermute x8, starting transfers between devices, per_device(): lax.ppermute(x, 'expert', forward)  15.7 us
    pallas_call x4, Pallas kernels, expert_call(): pl.pallas_call(functools.partial(whole_kernel, plan, len(pieces), blocks,...  13.2 us
    ppermute x8, waiting for transfers between devices, per_device(): lax.ppermute(x, 'expert', forward)  11.8 us
    ppermute x10, starting transfers between devices, send(): return lax.ppermute(value, 'expert', ways[way][1])  9.37 us
    ppermute x10, waiting for transfers between devices, send(): return lax.ppermute(value, 'expert', ways[way][1])  6.26 us
    ppermute x2, starting transfers between devices, per_device(): skipped = [lax.ppermute(value, 'expert', pairs) for value in outs[2:]]  4.99 us
    ppermute x6, waiting for transfers between devices, per_device(): ahead.append(tuple((lax.ppermute(x, 'expert', backward) for x in ahead[d])))  3.99 us
    pallas_call x1, Pallas kernels, per_device(): pl.pallas_call(functools.partial(prepare_kernel, plan), out_shape=(jax.Sh...  2.67 us
  transfers between devices with their start and end apart: 30, of which 15 were waited for; matrix products, arithmetic and copies ran while one was open for 0% of the time, Pallas kernels for 22%

profile of v17, /device:TPU:0, one launch (start us, length us, event | category | flops | bytes accessed | tf_op | source)
XLA Modules:
  0.0 77.4 jit_solution(7535756039661896942)
XLA Ops:
  0.7 2.7 %shard_map.113 = (bf16[1024,2304]{1,0:T(8,128)(2,1)S(1)}, bf16[32,768]{1,0:T(8,128)(2,1)S(1)}) custom-call(bf16[2,1024,384]{2,1,0:T(8,128)(2,1)} %refs_0_.1, bf16[2,1024,384]{2,1,0:T(8,128)(2,1)} %refs_1_.1, bf16[2,1024,384]{2,1,0:T(8,128)(2,1)} %refs_2_.1, bf16[2,16,384]{2,1,0:T(8,128)(2,1)} %refs_3_.1), custom_call_target="tpu_custom_call" | custom-call | tf_op jit(solution)/shard_map/pallas_call | solution.py:330
  3.4 0.5 collective-permute-start.5
  3.9 2.6 %collective-permute-start.3 = (bf16[64,2048]{1,0:T(8,128)(2,1)S(1)}, bf16[64,2048]{1,0:T(8,128)(2,1)S(1)}, u32[]{:S(2)}, u32[]{:S(2)}) collective-permute-start(bf16[64,2048]{1,0:T(8,128)(2,1)S(1)} %copy-done.1), channel_id=1, source_target_pairs={{0,4},{4,8},{8,12},{12,14},{14,10},{10,6},{6,2},{2,0},{1,5},{5,9},... | collective-permute-start | bytes 786440 | tf_op jit(solution)/shard_map/ppermute | solution.py:399
  6.5 1.0 %shard_map.112.refs_2_ = bf16[64,2176]{1,0:T(8,128)(2,1)S(1)} custom-call(bf16[64,2048]{1,0:T(8,128)(2,1)} %tokens_ref.1, s32[8,64]{1,0:T(8,128)S(1)} %bitcast.7, bf16[8,64]{1,0:T(8,128)(2,1)S(1)} %bitcast.8), custom_call_target="tpu_custom_call" | custom-call | tf_op jit(solution)/shard_map/pallas_call | solution.py:341
  7.5 2.1 %collective-permute-start = (bf16[64,2176]{1,0:T(8,128)(2,1)S(1)}, bf16[64,2176]{1,0:T(8,128)(2,1)S(1)}, u32[]{:S(2)}, u32[]{:S(2)}) collective-permute-start(bf16[64,2176]{1,0:T(8,128)(2,1)S(1)} %shard_map.112.refs_2_), channel_id=1, source_target_pairs={{0,4},{4,8},{8,12},{12,14},{14,10},{10,6},{6,2},{2,0},{1,5},{5,9},... | collective-permute-start | bytes 835592 | tf_op jit(solution)/shard_map/ppermute | solution.py:399
  9.6 4.0 %collective-permute-done.3.refs_2_ = bf16[64,2048]{1,0:T(8,128)(2,1)S(1)} collective-permute-done((bf16[64,2048]{1,0:T(8,128)(2,1)S(1)}, bf16[64,2048]{1,0:T(8,128)(2,1)S(1)}, u32[]{:S(2)}, u32[]{:S(2)}) %collective-permute-start.3) | collective-permute-done | bytes 262176 | tf_op jit(solution)/shard_map/ppermute | solution.py:399
  13.6 2.0 %collective-permute-start.7 = (bf16[64,2048]{1,0:T(8,128)(2,1)S(1)}, bf16[64,2048]{1,0:T(8,128)(2,1)S(1)}, u32[]{:S(2)}, u32[]{:S(2)}) collective-permute-start(bf16[64,2048]{1,0:T(8,128)(2,1)S(1)} %collective-permute-done.3.refs_2_), channel_id=1, source_target_pairs={{0,4},{4,8},{8,12},{12,14},{14,10},{10,6},{6,2},{2,0},{1,5},{5,9},... | collective-permute-start | bytes 786440 | tf_op jit(solution)/shard_map/ppermute | solution.py:399
  15.7 3.9 %collective-permute-done.refs_0_ = bf16[64,2176]{1,0:T(8,128)(2,1)S(1)} collective-permute-done((bf16[64,2176]{1,0:T(8,128)(2,1)S(1)}, bf16[64,2176]{1,0:T(8,128)(2,1)S(1)}, u32[]{:S(2)}, u32[]{:S(2)}) %collective-permute-start) | collective-permute-done | bytes 278560 | tf_op jit(solution)/shard_map/ppermute | solution.py:399
  19.6 2.0 %collective-permute-start.1 = (bf16[64,2176]{1,0:T(8,128)(2,1)S(1)}, bf16[64,2176]{1,0:T(8,128)(2,1)S(1)}, u32[]{:S(2)}, u32[]{:S(2)}) collective-permute-start(bf16[64,2176]{1,0:T(8,128)(2,1)S(1)} %collective-permute-done.refs_0_), channel_id=1, source_target_pairs={{0,4},{4,8},{8,12},{12,14},{14,10},{10,6},{6,2},{2,0},{1,5},{5,9},... | collective-permute-start | bytes 835592 | tf_op jit(solution)/shard_map/ppermute | solution.py:399
  21.6 3.5 %collective-permute-done.7.refs_3_ = bf16[64,2048]{1,0:T(8,128)(2,1)S(1)} collective-permute-done((bf16[64,2048]{1,0:T(8,128)(2,1)S(1)}, bf16[64,2048]{1,0:T(8,128)(2,1)S(1)}, u32[]{:S(2)}, u32[]{:S(2)}) %collective-permute-start.7) | collective-permute-done | bytes 262176 | tf_op jit(solution)/shard_map/ppermute | solution.py:399
  25.2 2.0 %collective-permute-start.11 = (bf16[64,2048]{1,0:T(8,128)(2,1)S(1)}, bf16[64,2048]{1,0:T(8,128)(2,1)S(1)}, u32[]{:S(2)}, u32[]{:S(2)}) collective-permute-start(bf16[64,2048]{1,0:T(8,128)(2,1)S(1)} %collective-permute-done.7.refs_3_), channel_id=1, source_target_pairs={{0,4},{4,8},{8,12},{12,14},{14,10},{10,6},{6,2},{2,0},{1,5},{5,9},... | collective-permute-start | bytes 786440 | tf_op jit(solution)/shard_map/ppermute | solution.py:399
  27.3 3.5 %shard_map.114 = (f32[128,2048]{1,0:T(8,128)S(1)}, f32[32,768]{1,0:T(8,128)S(1)}, f32[32,2048]{1,0:T(8,128)S(1)}) custom-call(bf16[64,2176]{1,0:T(8,128)(2,1)S(1)} %collective-permute-done.refs_0_, bf16[64,2176]{1,0:T(8,128)(2,1)S(1)} %collective-permute-done.2.refs_1_, bf16[64,2048]{1,0:T(8,128)(2,1)S(1)} %collective-permute-done.3.refs_2_, ...), custom_call_target="tpu_custom_call" | custom-call | flops 2013265920 | bytes 11059200 | tf_op jit(solution)/shard_map/pallas_call | solution.py:284
  30.8 0.3 collective-permute-done.1.refs_0_
  31.1 2.1 %collective-permute-done.6.refs_1_ = bf16[64,2176]{1,0:T(8,128)(2,1)S(1)} collective-permute-done((bf16[64,2176]{1,0:T(8,128)(2,1)S(1)}, bf16[64,2176]{1,0:T(8,128)(2,1)S(1)}, u32[]{:S(2)}, u32[]{:S(2)}) %collective-permute-start.6) | collective-permute-done | bytes 278560 | tf_op jit(solution)/shard_map/ppermute | solution.py:400
  33.2 1.6 %collective-permute-start.9 = (bf16[64,2176]{1,0:T(8,128)(2,1)S(1)}, bf16[64,2176]{1,0:T(8,128)(2,1)S(1)}, u32[]{:S(2)}, u32[]{:S(2)}) collective-permute-start(bf16[64,2176]{1,0:T(8,128)(2,1)S(1)} %collective-permute-done.1.refs_0_), channel_id=1, source_target_pairs={{0,4},{4,8},{8,12},{12,14},{14,10},{10,6},{6,2},{2,0},{1,5},{5,9},... | collective-permute-start | bytes 835592 | tf_op jit(solution)/shard_map/ppermute | solution.py:399
  34.8 0.4 collective-permute-start.10
  35.3 1.8 %shard_map.115 = (bf16[1536,1024]{1,0:T(8,128)(2,1)S(1)}, bf16[1536,1024]{1,0:T(8,128)(2,1)S(1)}) custom-call(bf16[1024,2304]{1,0:T(8,128)(2,1)S(1)} %get-tuple-element.52.refs_6_.refs_0_.refs_8_, bf16[1024,2304]{1,0:T(8,128)(2,1)S(1)} %collective-permute-done.5.refs_7_.refs_1_.refs_9_), custom_call_target="tpu_custom_call" | custom-call | tf_op jit(solution)/shard_map/pallas_call | solution.py:268
  37.1 1.8 %collective-permute-done.12.refs_3_.second_ref = bf16[64,2048]{1,0:T(8,128)(2,1)S(1)} collective-permute-done((bf16[64,2048]{1,0:T(8,128)(2,1)S(1)}, bf16[64,2048]{1,0:T(8,128)(2,1)S(1)}, u32[]{:S(2)}, u32[]{:S(2)}) %collective-permute-start.12) | collective-permute-done | bytes 262176 | tf_op jit(solution)/shard_map/ppermute | solution.py:400
  38.9 1.6 %collective-permute-start.19 = (bf16[32,2048]{1,0:T(8,128)(2,1)S(1)}, bf16[32,2048]{1,0:T(8,128)(2,1)S(1)}, u32[]{:S(2)}, u32[]{:S(2)}) collective-permute-start(bf16[32,2048]{1,0:T(8,128)(2,1)S(1)} %get-tuple-element.81), channel_id=1, source_target_pairs={{0,4},{4,8},{8,12},{12,14},{14,10},{10,6},{6,2},{2,0},{1,5},{5,9},... | collective-permute-start | bytes 393224 | tf_op jit(solution)/shard_map/ppermute | solution.py:413
  40.5 0.4 collective-permute-start.20
  40.9 3.8 %shard_map.116 = (f32[192,2048]{1,0:T(8,128)S(1)}, f32[32,768]{1,0:T(8,128)S(1)}, f32[32,2048]{1,0:T(8,128)S(1)}) custom-call(bf16[64,2176]{1,0:T(8,128)(2,1)S(1)} %collective-permute-done.1.refs_0_, bf16[64,2176]{1,0:T(8,128)(2,1)S(1)} %collective-permute-done.6.refs_1_, bf16[64,2176]{1,0:T(8,128)(2,1)S(1)} %shard_map.112.refs_2_, ...), custom_call_target="tpu_custom_call" | custom-call | flops 3019898880 | bytes 17891328 | tf_op jit(solution)/shard_map/pallas_call | solution.py:284
  44.8 1.6 %collective-permute-start.17 = (bf16[32,2176]{1,0:T(8,128)(2,1)S(1)}, bf16[32,2176]{1,0:T(8,128)(2,1)S(1)}, u32[]{:S(2)}, u32[]{:S(2)}) collective-permute-start(bf16[32,2176]{1,0:T(8,128)(2,1)S(1)} %get-tuple-element.77), channel_id=1, source_target_pairs={{0,4},{4,8},{8,12},{12,14},{14,10},{10,6},{6,2},{2,0},{1,5},{5,9},... | collective-permute-start | bytes 417800 | tf_op jit(solution)/shard_map/ppermute | solution.py:413
  46.5 0.4 collective-permute-start.18
  46.9 2.7 %shard_map.117 = (f32[32,768]{1,0:T(8,128)S(1)}, f32[32,2048]{1,0:T(8,128)S(1)}, bf16[64,2048]{1,0:T(8,128)(2,1)S(1)}, bf16[64,2048]{1,0:T(8,128)(2,1)S(1)}) custom-call(bf16[64,2176]{1,0:T(8,128)(2,1)S(1)} %collective-permute-done.9.refs_0_.first_ref, bf16[64,2176]{1,0:T(8,128)(2,1)S(1)} %collective-permute-done.10.refs_1_.second_ref, ...), custom_call_target="tpu_custom_call" | custom-call | flops 2013265920 | bytes 17350656 | tf_op jit(solution)/shard_map/pallas_call | solution.py:284
  49.7 0.2 collective-permute-start.13
  49.9 1.9 %collective-permute-start.14 = (bf16[64,2048]{1,0:T(8,128)(2,1)S(1)}, bf16[64,2048]{1,0:T(8,128)(2,1)S(1)}, u32[]{:S(2)}, u32[]{:S(2)}) collective-permute-start(bf16[64,2048]{1,0:T(8,128)(2,1)S(1)} %get-tuple-element.72), channel_id=1, source_target_pairs={{0,4},{4,8},{8,12},{12,14},{14,10},{10,6},{6,2},{2,0},{1,5},{5,9},... | collective-permute-start | bytes 786440 | tf_op jit(solution)/shard_map/ppermute | solution.py:374
  51.8 1.0 %collective-permute-done.18.refs_1_ = bf16[32,2176]{1,0:T(8,128)(2,1)S(1)} collective-permute-done((bf16[32,2176]{1,0:T(8,128)(2,1)S(1)}, bf16[32,2176]{1,0:T(8,128)(2,1)S(1)}, u32[]{:S(2)}, u32[]{:S(2)}) %collective-permute-start.18) | collective-permute-done | bytes 139296 | tf_op jit(solution)/shard_map/ppermute | solution.py:414
  52.8 3.1 %shard_map.121 = (f32[32,768]{1,0:T(8,128)S(1)}, f32[32,2048]{1,0:T(8,128)S(1)}, bf16[64,1024]{1,0:T(8,128)(2,1)S(1)}, bf16[64,1024]{1,0:T(8,128)(2,1)S(1)}) custom-call(bf16[32,2176]{1,0:T(8,128)(2,1)S(1)} %collective-permute-done.17.refs_0_, bf16[32,2176]{1,0:T(8,128)(2,1)S(1)} %collective-permute-done.18.refs_1_, ...), custom_call_target="tpu_custom_call" | custom-call | flops 1006632960 | bytes 16809984 | tf_op jit(solution)/shard_map/pallas_call | solution.py:284
  55.9 2.6 %collective-permute-start.21 = (bf16[64,1024]{1,0:T(8,128)(2,1)S(1)}, bf16[64,1024]{1,0:T(8,128)(2,1)S(1)}, u32[]{:S(2)}, u32[]{:S(2)}) collective-permute-start(bf16[64,1024]{1,0:T(8,128)(2,1)S(1)} %get-tuple-element.85), channel_id=1, source_target_pairs={{0,12},{4,6},{8,10},{12,0},{14,2},{10,8},{6,4},{2,14},{1,13},{5,7}... | collective-permute-start | bytes 393224 | tf_op jit(solution)/shard_map/ppermute | solution.py:432
  58.5 0.5 collective-permute-start.15
  59.0 1.6 %collective-permute-start.16 = (bf16[64,1024]{1,0:T(8,128)(2,1)S(1)}, bf16[64,1024]{1,0:T(8,128)(2,1)S(1)}, u32[]{:S(2)}, u32[]{:S(2)}) collective-permute-start(bf16[64,1024]{1,0:T(8,128)(2,1)S(1)} %get-tuple-element.74), channel_id=1, source_target_pairs={{0,4},{4,8},{8,12},{12,14},{14,10},{10,6},{6,2},{2,0},{1,5},{5,9},... | collective-permute-start | bytes 393224 | tf_op jit(solution)/shard_map/ppermute | solution.py:374
  60.6 2.4 %collective-permute-start.26 = (bf16[64,1024]{1,0:T(8,128)(2,1)S(1)}, bf16[64,1024]{1,0:T(8,128)(2,1)S(1)}, u32[]{:S(2)}, u32[]{:S(2)}) collective-permute-start(bf16[64,1024]{1,0:T(8,128)(2,1)S(1)} %get-tuple-element.90), channel_id=1, source_target_pairs={{0,12},{4,6},{8,10},{12,0},{14,2},{10,8},{6,4},{2,14},{1,13},{5,7}... | collective-permute-start | bytes 393224 | tf_op jit(solution)/shard_map/ppermute | solution.py:432
  63.1 1.2 %collective-permute-start.24 = (bf16[64,1024]{1,0:T(8,128)(2,1)S(1)}, bf16[64,1024]{1,0:T(8,128)(2,1)S(1)}, u32[]{:S(2)}, u32[]{:S(2)}) collective-permute-start(bf16[64,1024]{1,0:T(8,128)(2,1)S(1)} %get-tuple-element.88), channel_id=1, source_target_pairs={{4,0},{8,4},{12,8},{14,12},{10,14},{6,10},{2,6},{0,2},{5,1},{9,5},... | collective-permute-start | bytes 393224 | tf_op jit(solution)/shard_map/ppermute | solution.py:374
  64.3 0.9 %collective-permute-start.25 = (bf16[64,1024]{1,0:T(8,128)(2,1)S(1)}, bf16[64,1024]{1,0:T(8,128)(2,1)S(1)}, u32[]{:S(2)}, u32[]{:S(2)}) collective-permute-start(bf16[64,1024]{1,0:T(8,128)(2,1)S(1)} %get-tuple-element.89), channel_id=1, source_target_pairs={{0,4},{4,8},{8,12},{12,14},{14,10},{10,6},{6,2},{2,0},{1,5},{5,9},... | collective-permute-start | bytes 393224 | tf_op jit(solution)/shard_map/ppermute | solution.py:374
  65.2 0.1 shard_map.126
  65.3 1.8 %collective-permute-done.15.refs_1_ = bf16[64,1024]{1,0:T(8,128)(2,1)S(1)} collective-permute-done((bf16[64,1024]{1,0:T(8,128)(2,1)S(1)}, bf16[64,1024]{1,0:T(8,128)(2,1)S(1)}, u32[]{:S(2)}, u32[]{:S(2)}) %collective-permute-start.15) | collective-permute-done | bytes 131104 | tf_op jit(solution)/shard_map/ppermute | solution.py:374
  67.2 0.9 %collective-permute-start.22 = (bf16[64,1024]{1,0:T(8,128)(2,1)S(1)}, bf16[64,1024]{1,0:T(8,128)(2,1)S(1)}, u32[]{:S(2)}, u32[]{:S(2)}) collective-permute-start(bf16[64,1024]{1,0:T(8,128)(2,1)S(1)} %get-tuple-element.86), channel_id=1, source_target_pairs={{4,0},{8,4},{12,8},{14,12},{10,14},{6,10},{2,6},{0,2},{5,1},{9,5},... | collective-permute-start | bytes 393224 | tf_op jit(solution)/shard_map/ppermute | solution.py:374
  68.1 1.0 %collective-permute-done.26.refs_3_ = bf16[64,1024]{1,0:T(8,128)(2,1)S(1)} collective-permute-done((bf16[64,1024]{1,0:T(8,128)(2,1)S(1)}, bf16[64,1024]{1,0:T(8,128)(2,1)S(1)}, u32[]{:S(2)}, u32[]{:S(2)}) %collective-permute-start.26) | collective-permute-done | bytes 131104 | tf_op jit(solution)/shard_map/ppermute | solution.py:432
  69.1 0.2 collective-permute-start.23
  69.3 0.6 collective-permute-done.24.refs_1_
  70.0 1.7 %collective-permute-start.27 = (bf16[64,1024]{1,0:T(8,128)(2,1)S(1)}, bf16[64,1024]{1,0:T(8,128)(2,1)S(1)}, u32[]{:S(2)}, u32[]{:S(2)}) collective-permute-start(bf16[64,1024]{1,0:T(8,128)(2,1)S(1)} %get-tuple-element.91), channel_id=1, source_target_pairs={{4,0},{8,4},{12,8},{14,12},{10,14},{6,10},{2,6},{0,2},{5,1},{9,5},... | collective-permute-start | bytes 393224 | tf_op jit(solution)/shard_map/ppermute | solution.py:374
  71.7 0.4 collective-permute-start.28
  72.1 0.7 shard_map.127
  72.8 0.8 %collective-permute-done.22.refs_1_ = bf16[64,1024]{1,0:T(8,128)(2,1)S(1)} collective-permute-done((bf16[64,1024]{1,0:T(8,128)(2,1)S(1)}, bf16[64,1024]{1,0:T(8,128)(2,1)S(1)}, u32[]{:S(2)}, u32[]{:S(2)}) %collective-permute-start.22) | collective-permute-done | bytes 131104 | tf_op jit(solution)/shard_map/ppermute | solution.py:374
  73.6 1.3 %collective-permute-done.23.refs_2_ = bf16[64,1024]{1,0:T(8,128)(2,1)S(1)} collective-permute-done((bf16[64,1024]{1,0:T(8,128)(2,1)S(1)}, bf16[64,1024]{1,0:T(8,128)(2,1)S(1)}, u32[]{:S(2)}, u32[]{:S(2)}) %collective-permute-start.23) | collective-permute-done | bytes 131104 | tf_op jit(solution)/shard_map/ppermute | solution.py:374
  74.9 1.1 %collective-permute-done.27.refs_3_ = bf16[64,1024]{1,0:T(8,128)(2,1)S(1)} collective-permute-done((bf16[64,1024]{1,0:T(8,128)(2,1)S(1)}, bf16[64,1024]{1,0:T(8,128)(2,1)S(1)}, u32[]{:S(2)}, u32[]{:S(2)}) %collective-permute-start.27) | collective-permute-done | bytes 131104 | tf_op jit(solution)/shard_map/ppermute | solution.py:374
  76.0 0.7 collective-permute-done.28.refs_4_
  76.7 0.8 %shard_map.125 = bf16[64,2048]{1,0:T(8,128)(2,1)} custom-call(f32[192,2048]{1,0:T(8,128)S(1)} %get-tuple-element.63.refs_0_, bf16[64,1024]{1,0:T(8,128)(2,1)S(1)} %collective-permute-done.22.refs_1_, bf16[64,1024]{1,0:T(8,128)(2,1)S(1)} %collective-permute-done.23.refs_2_, bf16[64,1024]{1,0:T(8,128)(2,1)S(1)} %collective-permute-done.27.refs_3_, ...), custom_call_target="tpu_custom_call" | custom-call | tf_op jit(solution)/shard_map/pallas_call | solution.py:451
  (38 shorter events, 0.6 us)
Async XLA Ops:
  0.6 3.2 %copy-start.1 = (bf16[64,2048]{1,0:T(8,128)(2,1)S(1)}, bf16[64,2048]{1,0:T(8,128)(2,1)}, u32[]{:S(2)}) copy-start(bf16[64,2048]{1,0:T(8,128)(2,1)} %refs_5_.1) | copy-start | bytes 786436
  0.6 5.9 %copy-start.2 = (s32[64,8]{0,1:T(8,128)S(1)}, s32[64,8]{0,1:T(8,128)}, u32[]{:S(2)}) copy-start(s32[64,8]{0,1:T(8,128)} %param.11) | copy-start | bytes 6148
  0.7 5.9 %copy-start.3 = (bf16[64,8]{0,1:T(8,128)(2,1)S(1)}, bf16[64,8]{0,1:T(8,128)(2,1)}, u32[]{:S(2)}) copy-start(bf16[64,8]{0,1:T(8,128)(2,1)} %param.12) | copy-start | bytes 3076
  0.7 26.6 %copy-start = (bf16[2,16,2048]{2,1,0:T(8,128)(2,1)S(1)}, bf16[2,16,2048]{2,1,0:T(8,128)(2,1)}, u32[]{:S(2)}) copy-start(bf16[2,16,2048]{2,1,0:T(8,128)(2,1)} %param.17) | copy-start | bytes 393220
  3.4 23.9 %collective-permute-start.5 = (bf16[1024,2304]{1,0:T(8,128)(2,1)S(1)}, bf16[1024,2304]{1,0:T(8,128)(2,1)S(1)}, u32[]{:S(2)}, u32[]{:S(2)}) collective-permute-start(bf16[1024,2304]{1,0:T(8,128)(2,1)S(1)} %get-tuple-element.52.refs_6_.refs_0_.refs_8_), channel_id=1, source_target_pairs={{0,1},{1,0},{2,3},{3,2},{4,5},{5,4},{6,7},{7,6},{8,9},{9,8},{10,11... | collective-permute-start | bytes 14155784 | tf_op jit(solution)/shard_map/ppermute | solution.py:355
  3.9 9.7 %collective-permute-start.3 = (bf16[64,2048]{1,0:T(8,128)(2,1)S(1)}, bf16[64,2048]{1,0:T(8,128)(2,1)S(1)}, u32[]{:S(2)}, u32[]{:S(2)}) collective-permute-start(bf16[64,2048]{1,0:T(8,128)(2,1)S(1)} %copy-done.1), channel_id=1, source_target_pairs={{0,4},{4,8},{8,12},{12,14},{14,10},{10,6},{6,2},{2,0},{1,5},{5,9},... | collective-permute-start | bytes 786440 | tf_op jit(solution)/shard_map/ppermute | solution.py:399
  6.5 9.2 %collective-permute-start.4 = (bf16[64,2048]{1,0:T(8,128)(2,1)S(1)}, bf16[64,2048]{1,0:T(8,128)(2,1)S(1)}, u32[]{:S(2)}, u32[]{:S(2)}) collective-permute-start(bf16[64,2048]{1,0:T(8,128)(2,1)S(1)} %copy-done.1), channel_id=1, source_target_pairs={{4,0},{8,4},{12,8},{14,12},{10,14},{6,10},{2,6},{0,2},{5,1},{9,5},... | collective-permute-start | bytes 786440 | tf_op jit(solution)/shard_map/ppermute | solution.py:400
  7.5 12.1 %collective-permute-start = (bf16[64,2176]{1,0:T(8,128)(2,1)S(1)}, bf16[64,2176]{1,0:T(8,128)(2,1)S(1)}, u32[]{:S(2)}, u32[]{:S(2)}) collective-permute-start(bf16[64,2176]{1,0:T(8,128)(2,1)S(1)} %shard_map.112.refs_2_), channel_id=1, source_target_pairs={{0,4},{4,8},{8,12},{12,14},{14,10},{10,6},{6,2},{2,0},{1,5},{5,9},... | collective-permute-start | bytes 835592 | tf_op jit(solution)/shard_map/ppermute | solution.py:399
  9.6 12.1 %collective-permute-start.2 = (bf16[64,2176]{1,0:T(8,128)(2,1)S(1)}, bf16[64,2176]{1,0:T(8,128)(2,1)S(1)}, u32[]{:S(2)}, u32[]{:S(2)}) collective-permute-start(bf16[64,2176]{1,0:T(8,128)(2,1)S(1)} %shard_map.112.refs_2_), channel_id=1, source_target_pairs={{4,0},{8,4},{12,8},{14,12},{10,14},{6,10},{2,6},{0,2},{5,1},{9,5},... | collective-permute-start | bytes 835592 | tf_op jit(solution)/shard_map/ppermute | solution.py:400
  13.6 11.6 %collective-permute-start.7 = (bf16[64,2048]{1,0:T(8,128)(2,1)S(1)}, bf16[64,2048]{1,0:T(8,128)(2,1)S(1)}, u32[]{:S(2)}, u32[]{:S(2)}) collective-permute-start(bf16[64,2048]{1,0:T(8,128)(2,1)S(1)} %collective-permute-done.3.refs_2_), channel_id=1, source_target_pairs={{0,4},{4,8},{8,12},{12,14},{14,10},{10,6},{6,2},{2,0},{1,5},{5,9},... | collective-permute-start | bytes 786440 | tf_op jit(solution)/shard_map/ppermute | solution.py:399
  15.7 11.6 %collective-permute-start.8 = (bf16[64,2048]{1,0:T(8,128)(2,1)S(1)}, bf16[64,2048]{1,0:T(8,128)(2,1)S(1)}, u32[]{:S(2)}, u32[]{:S(2)}) collective-permute-start(bf16[64,2048]{1,0:T(8,128)(2,1)S(1)} %collective-permute-done.4.refs_3_), channel_id=1, source_target_pairs={{4,0},{8,4},{12,8},{14,12},{10,14},{6,10},{2,6},{0,2},{5,1},{9,5},... | collective-permute-start | bytes 786440 | tf_op jit(solution)/shard_map/ppermute | solution.py:400
  19.6 11.6 %collective-permute-start.1 = (bf16[64,2176]{1,0:T(8,128)(2,1)S(1)}, bf16[64,2176]{1,0:T(8,128)(2,1)S(1)}, u32[]{:S(2)}, u32[]{:S(2)}) collective-permute-start(bf16[64,2176]{1,0:T(8,128)(2,1)S(1)} %collective-permute-done.refs_0_), channel_id=1, source_target_pairs={{0,4},{4,8},{8,12},{12,14},{14,10},{10,6},{6,2},{2,0},{1,5},{5,9},... | collective-permute-start | bytes 835592 | tf_op jit(solution)/shard_map/ppermute | solution.py:399
  21.6 11.6 %collective-permute-start.6 = (bf16[64,2176]{1,0:T(8,128)(2,1)S(1)}, bf16[64,2176]{1,0:T(8,128)(2,1)S(1)}, u32[]{:S(2)}, u32[]{:S(2)}) collective-permute-start(bf16[64,2176]{1,0:T(8,128)(2,1)S(1)} %collective-permute-done.2.refs_1_), channel_id=1, source_target_pairs={{4,0},{8,4},{12,8},{14,12},{10,14},{6,10},{2,6},{0,2},{5,1},{9,5},... | collective-permute-start | bytes 835592 | tf_op jit(solution)/shard_map/ppermute | solution.py:400
  25.2 11.9 %collective-permute-start.11 = (bf16[64,2048]{1,0:T(8,128)(2,1)S(1)}, bf16[64,2048]{1,0:T(8,128)(2,1)S(1)}, u32[]{:S(2)}, u32[]{:S(2)}) collective-permute-start(bf16[64,2048]{1,0:T(8,128)(2,1)S(1)} %collective-permute-done.7.refs_3_), channel_id=1, source_target_pairs={{0,4},{4,8},{8,12},{12,14},{14,10},{10,6},{6,2},{2,0},{1,5},{5,9},... | collective-permute-start | bytes 786440 | tf_op jit(solution)/shard_map/ppermute | solution.py:399
  27.3 11.6 %collective-permute-start.12 = (bf16[64,2048]{1,0:T(8,128)(2,1)S(1)}, bf16[64,2048]{1,0:T(8,128)(2,1)S(1)}, u32[]{:S(2)}, u32[]{:S(2)}) collective-permute-start(bf16[64,2048]{1,0:T(8,128)(2,1)S(1)} %collective-permute-done.8.refs_4_), channel_id=1, source_target_pairs={{4,0},{8,4},{12,8},{14,12},{10,14},{6,10},{2,6},{0,2},{5,1},{9,5},... | collective-permute-start | bytes 786440 | tf_op jit(solution)/shard_map/ppermute | solution.py:400
  33.2 11.6 %collective-permute-start.9 = (bf16[64,2176]{1,0:T(8,128)(2,1)S(1)}, bf16[64,2176]{1,0:T(8,128)(2,1)S(1)}, u32[]{:S(2)}, u32[]{:S(2)}) collective-permute-start(bf16[64,2176]{1,0:T(8,128)(2,1)S(1)} %collective-permute-done.1.refs_0_), channel_id=1, source_target_pairs={{0,4},{4,8},{8,12},{12,14},{14,10},{10,6},{6,2},{2,0},{1,5},{5,9},... | collective-permute-start | bytes 835592 | tf_op jit(solution)/shard_map/ppermute | solution.py:399
  34.8 10.0 %collective-permute-start.10 = (bf16[64,2176]{1,0:T(8,128)(2,1)S(1)}, bf16[64,2176]{1,0:T(8,128)(2,1)S(1)}, u32[]{:S(2)}, u32[]{:S(2)}) collective-permute-start(bf16[64,2176]{1,0:T(8,128)(2,1)S(1)} %collective-permute-done.6.refs_1_), channel_id=1, source_target_pairs={{4,0},{8,4},{12,8},{14,12},{10,14},{6,10},{2,6},{0,2},{5,1},{9,5},... | collective-permute-start | bytes 835592 | tf_op jit(solution)/shard_map/ppermute | solution.py:400
  38.9 11.0 %collective-permute-start.19 = (bf16[32,2048]{1,0:T(8,128)(2,1)S(1)}, bf16[32,2048]{1,0:T(8,128)(2,1)S(1)}, u32[]{:S(2)}, u32[]{:S(2)}) collective-permute-start(bf16[32,2048]{1,0:T(8,128)(2,1)S(1)} %get-tuple-element.81), channel_id=1, source_target_pairs={{0,4},{4,8},{8,12},{12,14},{14,10},{10,6},{6,2},{2,0},{1,5},{5,9},... | collective-permute-start | bytes 393224 | tf_op jit(solution)/shard_map/ppermute | solution.py:413
  40.5 11.3 %collective-permute-start.20 = (bf16[32,2048]{1,0:T(8,128)(2,1)S(1)}, bf16[32,2048]{1,0:T(8,128)(2,1)S(1)}, u32[]{:S(2)}, u32[]{:S(2)}) collective-permute-start(bf16[32,2048]{1,0:T(8,128)(2,1)S(1)} %get-tuple-element.82), channel_id=1, source_target_pairs={{4,0},{8,4},{12,8},{14,12},{10,14},{6,10},{2,6},{0,2},{5,1},{9,5},... | collective-permute-start | bytes 393224 | tf_op jit(solution)/shard_map/ppermute | solution.py:414
  44.8 6.9 %collective-permute-start.17 = (bf16[32,2176]{1,0:T(8,128)(2,1)S(1)}, bf16[32,2176]{1,0:T(8,128)(2,1)S(1)}, u32[]{:S(2)}, u32[]{:S(2)}) collective-permute-start(bf16[32,2176]{1,0:T(8,128)(2,1)S(1)} %get-tuple-element.77), channel_id=1, source_target_pairs={{0,4},{4,8},{8,12},{12,14},{14,10},{10,6},{6,2},{2,0},{1,5},{5,9},... | collective-permute-start | bytes 417800 | tf_op jit(solution)/shard_map/ppermute | solution.py:413
  46.5 6.3 %collective-permute-start.18 = (bf16[32,2176]{1,0:T(8,128)(2,1)S(1)}, bf16[32,2176]{1,0:T(8,128)(2,1)S(1)}, u32[]{:S(2)}, u32[]{:S(2)}) collective-permute-start(bf16[32,2176]{1,0:T(8,128)(2,1)S(1)} %get-tuple-element.78), channel_id=1, source_target_pairs={{4,0},{8,4},{12,8},{14,12},{10,14},{6,10},{2,6},{0,2},{5,1},{9,5},... | collective-permute-start | bytes 417800 | tf_op jit(solution)/shard_map/ppermute | solution.py:414
  49.7 8.8 %collective-permute-start.13 = (bf16[64,2048]{1,0:T(8,128)(2,1)S(1)}, bf16[64,2048]{1,0:T(8,128)(2,1)S(1)}, u32[]{:S(2)}, u32[]{:S(2)}) collective-permute-start(bf16[64,2048]{1,0:T(8,128)(2,1)S(1)} %get-tuple-element.71), channel_id=1, source_target_pairs={{4,0},{8,4},{12,8},{14,12},{10,14},{6,10},{2,6},{0,2},{5,1},{9,5},... | collective-permute-start | bytes 786440 | tf_op jit(solution)/shard_map/ppermute | solution.py:374
  49.9 8.6 %collective-permute-start.14 = (bf16[64,2048]{1,0:T(8,128)(2,1)S(1)}, bf16[64,2048]{1,0:T(8,128)(2,1)S(1)}, u32[]{:S(2)}, u32[]{:S(2)}) collective-permute-start(bf16[64,2048]{1,0:T(8,128)(2,1)S(1)} %get-tuple-element.72), channel_id=1, source_target_pairs={{0,4},{4,8},{8,12},{12,14},{14,10},{10,6},{6,2},{2,0},{1,5},{5,9},... | collective-permute-start | bytes 786440 | tf_op jit(solution)/shard_map/ppermute | solution.py:374
  55.9 8.4 %collective-permute-start.21 = (bf16[64,1024]{1,0:T(8,128)(2,1)S(1)}, bf16[64,1024]{1,0:T(8,128)(2,1)S(1)}, u32[]{:S(2)}, u32[]{:S(2)}) collective-permute-start(bf16[64,1024]{1,0:T(8,128)(2,1)S(1)} %get-tuple-element.85), channel_id=1, source_target_pairs={{0,12},{4,6},{8,10},{12,0},{14,2},{10,8},{6,4},{2,14},{1,13},{5,7}... | collective-permute-start | bytes 393224 | tf_op jit(solution)/shard_map/ppermute | solution.py:432
  58.5 8.6 %collective-permute-start.15 = (bf16[64,1024]{1,0:T(8,128)(2,1)S(1)}, bf16[64,1024]{1,0:T(8,128)(2,1)S(1)}, u32[]{:S(2)}, u32[]{:S(2)}) collective-permute-start(bf16[64,1024]{1,0:T(8,128)(2,1)S(1)} %get-tuple-element.73), channel_id=1, source_target_pairs={{4,0},{8,4},{12,8},{14,12},{10,14},{6,10},{2,6},{0,2},{5,1},{9,5},... | collective-permute-start | bytes 393224 | tf_op jit(solution)/shard_map/ppermute | solution.py:374
  59.0 8.1 %collective-permute-start.16 = (bf16[64,1024]{1,0:T(8,128)(2,1)S(1)}, bf16[64,1024]{1,0:T(8,128)(2,1)S(1)}, u32[]{:S(2)}, u32[]{:S(2)}) collective-permute-start(bf16[64,1024]{1,0:T(8,128)(2,1)S(1)} %get-tuple-element.74), channel_id=1, source_target_pairs={{0,4},{4,8},{8,12},{12,14},{14,10},{10,6},{6,2},{2,0},{1,5},{5,9},... | collective-permute-start | bytes 393224 | tf_op jit(solution)/shard_map/ppermute | solution.py:374
  60.6 8.5 %collective-permute-start.26 = (bf16[64,1024]{1,0:T(8,128)(2,1)S(1)}, bf16[64,1024]{1,0:T(8,128)(2,1)S(1)}, u32[]{:S(2)}, u32[]{:S(2)}) collective-permute-start(bf16[64,1024]{1,0:T(8,128)(2,1)S(1)} %get-tuple-element.90), channel_id=1, source_target_pairs={{0,12},{4,6},{8,10},{12,0},{14,2},{10,8},{6,4},{2,14},{1,13},{5,7}... | collective-permute-start | bytes 393224 | tf_op jit(solution)/shard_map/ppermute | solution.py:432
  63.1 6.8 %collective-permute-start.24 = (bf16[64,1024]{1,0:T(8,128)(2,1)S(1)}, bf16[64,1024]{1,0:T(8,128)(2,1)S(1)}, u32[]{:S(2)}, u32[]{:S(2)}) collective-permute-start(bf16[64,1024]{1,0:T(8,128)(2,1)S(1)} %get-tuple-element.88), channel_id=1, source_target_pairs={{4,0},{8,4},{12,8},{14,12},{10,14},{6,10},{2,6},{0,2},{5,1},{9,5},... | collective-permute-start | bytes 393224 | tf_op jit(solution)/shard_map/ppermute | solution.py:374
  64.3 5.6 %collective-permute-start.25 = (bf16[64,1024]{1,0:T(8,128)(2,1)S(1)}, bf16[64,1024]{1,0:T(8,128)(2,1)S(1)}, u32[]{:S(2)}, u32[]{:S(2)}) collective-permute-start(bf16[64,1024]{1,0:T(8,128)(2,1)S(1)} %get-tuple-element.89), channel_id=1, source_target_pairs={{0,4},{4,8},{8,12},{12,14},{14,10},{10,6},{6,2},{2,0},{1,5},{5,9},... | collective-permute-start | bytes 393224 | tf_op jit(solution)/shard_map/ppermute | solution.py:374
  67.1 5.0 %collective-permute-start.29 = (f32[32,1216]{1,0:T(8,128)S(1)}, f32[32,1216]{1,0:T(8,128)S(1)}, u32[]{:S(2)}, u32[]{:S(2)}) collective-permute-start(f32[32,1216]{1,0:T(8,128)S(1)} %get-tuple-element.96), channel_id=1, source_target_pairs={{0,1},{1,0},{2,3},{3,2},{4,5},{5,4},{6,7},{7,6},{8,9},{9,8},{10,11... | collective-permute-start | bytes 466952 | tf_op jit(solution)/shard_map/ppermute | solution.py:465
  67.2 6.3 %collective-permute-start.22 = (bf16[64,1024]{1,0:T(8,128)(2,1)S(1)}, bf16[64,1024]{1,0:T(8,128)(2,1)S(1)}, u32[]{:S(2)}, u32[]{:S(2)}) collective-permute-start(bf16[64,1024]{1,0:T(8,128)(2,1)S(1)} %get-tuple-element.86), channel_id=1, source_target_pairs={{4,0},{8,4},{12,8},{14,12},{10,14},{6,10},{2,6},{0,2},{5,1},{9,5},... | collective-permute-start | bytes 393224 | tf_op jit(solution)/shard_map/ppermute | solution.py:374
  69.1 5.8 %collective-permute-start.23 = (bf16[64,1024]{1,0:T(8,128)(2,1)S(1)}, bf16[64,1024]{1,0:T(8,128)(2,1)S(1)}, u32[]{:S(2)}, u32[]{:S(2)}) collective-permute-start(bf16[64,1024]{1,0:T(8,128)(2,1)S(1)} %get-tuple-element.87), channel_id=1, source_target_pairs={{0,4},{4,8},{8,12},{12,14},{14,10},{10,6},{6,2},{2,0},{1,5},{5,9},... | collective-permute-start | bytes 393224 | tf_op jit(solution)/shard_map/ppermute | solution.py:374
  70.0 6.0 %collective-permute-start.27 = (bf16[64,1024]{1,0:T(8,128)(2,1)S(1)}, bf16[64,1024]{1,0:T(8,128)(2,1)S(1)}, u32[]{:S(2)}, u32[]{:S(2)}) collective-permute-start(bf16[64,1024]{1,0:T(8,128)(2,1)S(1)} %get-tuple-element.91), channel_id=1, source_target_pairs={{4,0},{8,4},{12,8},{14,12},{10,14},{6,10},{2,6},{0,2},{5,1},{9,5},... | collective-permute-start | bytes 393224 | tf_op jit(solution)/shard_map/ppermute | solution.py:374
  71.7 5.0 %collective-permute-start.28 = (bf16[64,1024]{1,0:T(8,128)(2,1)S(1)}, bf16[64,1024]{1,0:T(8,128)(2,1)S(1)}, u32[]{:S(2)}, u32[]{:S(2)}) collective-permute-start(bf16[64,1024]{1,0:T(8,128)(2,1)S(1)} %get-tuple-element.92), channel_id=1, source_target_pairs={{0,4},{4,8},{8,12},{12,14},{14,10},{10,6},{6,2},{2,0},{1,5},{5,9},... | collective-permute-start | bytes 393224 | tf_op jit(solution)/shard_map/ppermute | solution.py:374
